TPU v7x, 32 devices: a whole 2x2x4 slice. The times are simulated.
32 devices in a mesh: parts: 2 (over y), lon: 4 (over z), ch: 2 (over x), sub: 2 (over core).
Axes of the slice: x: 2, y: 2, z: 4, core: 2. Of those that a mesh axis runs over, the one named last changes fastest.
Arguments:
- features: bfloat16 [512, 8192], P('ch', ('parts', 'lon', 'sub')), parts along dimension 1, may hold values from -6 to 6
- cotangent: bfloat16 [512, 8192], P('ch', ('parts', 'lon', 'sub')), parts along dimension 1, may hold values from -6 to 6
- senders: int32 [12, 8192], P(None, ('parts', 'lon', 'sub')), parts along dimension 1, may hold values from 0 to 2047, as said below
- in_degree: int32 [8192], P(('parts', 'lon', 'sub')), parts along dimension 0, may hold values from 1 to 12
- tile_count: int32 [16], P(('parts', 'lon', 'sub')), parts along dimension 0, may hold values from 2 to 4, as said below
- send_tiles: int32 [16, 6, 2], P(('parts', 'lon', 'sub')), parts along dimension 0, may hold values from 0 to 3, as said below
- w_send: bfloat16 [512, 512], replicated, may hold values from -0.25 to 0.25
- w_recv: bfloat16 [512, 512], replicated, may hold values from -0.25 to 0.25
- bias_edge: float32 [512], replicated, may hold values from -4 to 4
- w_msg: bfloat16 [512, 512], replicated, may hold values from -0.25 to 0.25
- w_node_v: bfloat16 [512, 512], replicated, may hold values from -0.1875 to 0.1875
- w_node_a: bfloat16 [512, 512], replicated, may hold values from -0.1875 to 0.1875
- bias_node: float32 [512], replicated, may hold values from -4 to 4
- w_out: bfloat16 [512, 512], replicated, may hold values from -0.25 to 0.25
Outputs:
- updated: bfloat16 [512, 8192], P('ch', ('parts', 'lon', 'sub')), parts along dimension 1
- grad_features: bfloat16 [512, 8192], P('ch', ('parts', 'lon', 'sub')), parts along dimension 1
- grad_w_send: float32 [1024, 512], P(('parts', 'ch'), ('lon', 'sub')), parts along dimension 0
There are 2 independent parts, one for each index of `parts`. A program takes and returns all parts, laid end to end along the dimension named above; an argument that names none is the same for every part. Nothing has to cross between parts.
Inputs may be any that keep to these rules, and one draw needn't show every extreme that they name: `tile_count`: some shard has all 4 tiles active. send_tiles[s, j, :] are active tiles of shard s; for j < 3 they lie in the upper half of its active tiles, else in the lower half; repeats may occur. `senders`: positions below 512 name active nodes of the receiver's own shard.
All inputs are finite; a program needn't handle non-finite values.
Results may differ from a plain program's by a relative error of at most 0.015.
Values may be sent and summed in bfloat16 or wider, within the bound.
No kernel may reach another device: no remote copies, remote signals or barrier semaphores. Data moves between devices by JAX's collectives and lax.ppermute only.
A program may use at most 64 MiB of HBM per device.

v0:
```python
import math

import jax
import jax.numpy as jnp
from jax import lax
from jax.sharding import PartitionSpec as P

TILE = 128


def shifted(block, axis, distance):
    devices = range(lax.axis_size(axis))
    route = [((i - distance) % len(devices), i) for i in devices]
    return lax.ppermute(block, axis, route)


def swish_grad(pre_value):
    sigmoid_v = jax.nn.sigmoid(pre_value)
    return sigmoid_v * (1.0 + pre_value * (1.0 - sigmoid_v))


def left_dot(left, right):
    return lax.dot_general(
        left, right, (((0,), (0,)), ((), ())), preferred_element_type=jnp.float32
    )


def shards(
    features,
    cotangent,
    senders,
    in_degree,
    tile_count,
    send_tiles,
    w_send,
    w_recv,
    bias_edge,
    w_msg,
    w_node_v,
    w_node_a,
    bias_node,
    w_out,
):
    node_rows = features.shape[1]
    chan_count = lax.axis_size("ch")
    chan_index = lax.axis_index("ch")
    hidden_all = w_send.shape[0]
    hid_dev = hidden_all // chan_count
    part_nodes = node_rows // chan_count
    hid_start = chan_index * hid_dev
    node_start = chan_index * part_nodes
    total_nodes = node_rows * lax.axis_size(("lon", "sub"))
    tile_rows = node_rows // TILE
    hop_count = send_tiles.shape[1] // 2
    offsets = [number + 1 for number in range(hop_count)] + [
        -(number + 1) for number in range(hop_count)
    ]
    band_tiles = tile_count[0]
    active = jnp.arange(node_rows) // TILE < band_tiles
    node_active = ((node_start + jnp.arange(part_nodes)) // TILE < band_tiles).astype(jnp.float32)
    my_send = lax.dynamic_slice_in_dim(w_send, hid_start, hid_dev, 0)
    my_recv = lax.dynamic_slice_in_dim(w_recv, hid_start, hid_dev, 0)
    piece = lax.all_gather(features, "ch", axis=0, tiled=True)
    acc_send = jnp.dot(my_send, piece, preferred_element_type=jnp.float32)
    acc_recv = jnp.dot(my_recv, piece, preferred_element_type=jnp.float32)
    own_cols = lax.dynamic_slice_in_dim(piece, node_start, part_nodes, 1)
    acc_send, acc_recv, node_feats = (acc_send, acc_recv, own_cols)
    proj_send = acc_send.astype(jnp.bfloat16)
    proj_recv = acc_recv.astype(jnp.bfloat16)
    node_cot = lax.all_to_all(cotangent, "ch", split_axis=1, concat_axis=0, tiled=True)
    my_bias = lax.dynamic_slice_in_dim(bias_edge, hid_start, hid_dev, 0)
    tile_ids = send_tiles[0].reshape(-1)
    tile_pick = tile_ids[:, None] == jnp.arange(tile_rows)[None, :]
    proj_tiles = proj_send.reshape(hid_dev, tile_rows, TILE)
    parcels = (
        jnp.einsum(
            "st,htl->hsl",
            tile_pick.astype(jnp.bfloat16),
            proj_tiles,
            preferred_element_type=jnp.float32,
        )
        .astype(jnp.bfloat16)
        .reshape(hid_dev, 2 * hop_count, -1)
    )
    arrivals = [
        shifted(parcels[:, slot_idx], ("lon", "sub"), offsets[slot_idx])
        for slot_idx in range(2 * hop_count)
    ]
    extended = jnp.concatenate([proj_send] + arrivals, axis=1)
    ext_len = extended.shape[1]
    positions = jnp.arange(ext_len, dtype=jnp.int32)[:, None]
    edge_valid = (jnp.arange(senders.shape[0])[:, None] < in_degree[None, :]) & active[None, :]
    degree_f = in_degree.astype(jnp.float32)
    recv_base = proj_recv.astype(jnp.float32) + my_bias[:, None]

    def forward_edge(summed, inputs):
        row_ids, valid_row = inputs
        picker = (positions == row_ids[None, :]).astype(jnp.bfloat16)
        pre_row = jnp.dot(extended, picker, preferred_element_type=jnp.float32) + recv_base
        summed = summed + jnp.where(valid_row[None], jax.nn.silu(pre_row), 0.0)
        return (summed, pre_row)

    summed, edge_pre = lax.scan(
        forward_edge, jnp.zeros((hid_dev, node_rows), jnp.float32), (senders, edge_valid)
    )
    message = (summed / degree_f[None, :]).astype(jnp.bfloat16)
    node_msg = lax.all_to_all(message, "ch", split_axis=1, concat_axis=0, tiled=True)
    aggregate = jnp.dot(w_msg, node_msg, preferred_element_type=jnp.float32).astype(jnp.bfloat16)
    node_pre = (
        jnp.dot(w_node_v, node_feats, preferred_element_type=jnp.float32)
        + jnp.dot(w_node_a, aggregate, preferred_element_type=jnp.float32)
        + bias_node[:, None]
    )
    node_hidden = jax.nn.silu(node_pre).astype(jnp.bfloat16)
    node_out = jnp.dot(w_out, node_hidden, preferred_element_type=jnp.float32)
    node_new = (node_feats.astype(jnp.float32) + node_active[None, :] * node_out).astype(
        jnp.bfloat16
    )
    updated = lax.all_to_all(node_new, "ch", split_axis=0, concat_axis=1, tiled=True)
    masked_cot = node_cot * node_active.astype(jnp.bfloat16)[None, :]
    grad_hidden = left_dot(w_out, masked_cot)
    grad_pre = (grad_hidden * swish_grad(node_pre)).astype(jnp.bfloat16)
    grad_agg = left_dot(w_node_a, grad_pre).astype(jnp.bfloat16)
    grad_msg_node = left_dot(w_msg, grad_agg).astype(jnp.bfloat16)
    grad_direct = left_dot(w_node_v, grad_pre)
    grad_msg = lax.all_to_all(grad_msg_node, "ch", split_axis=0, concat_axis=1, tiled=True)
    edge_scale = grad_msg.astype(jnp.float32) / degree_f[None, :]
    spread_dims = (((1,), (1,)), ((), ()))

    def backward_edge(carry, inputs):
        grad_ext, grad_recv = carry
        row_ids, valid_row, pre_row = inputs
        grad_row = jnp.where(valid_row[None], edge_scale * swish_grad(pre_row), 0.0)
        high_part = grad_row.astype(jnp.bfloat16)
        low_part = (grad_row - high_part.astype(jnp.float32)).astype(jnp.bfloat16)
        picker = (positions == row_ids[None, :]).astype(jnp.bfloat16)
        spread = lax.dot_general(
            high_part, picker, spread_dims, preferred_element_type=jnp.float32
        ) + lax.dot_general(low_part, picker, spread_dims, preferred_element_type=jnp.float32)
        return ((grad_ext + spread, grad_recv + grad_row), None)

    start_back = (
        jnp.zeros((hid_dev, ext_len), jnp.float32),
        jnp.zeros((hid_dev, node_rows), jnp.float32),
    )
    (grad_ext, grad_recv), unused_out = lax.scan(
        backward_edge, start_back, (senders, edge_valid, edge_pre)
    )
    grad_own = grad_ext[:, :node_rows]
    grad_far = grad_ext[:, node_rows:].reshape(hid_dev, 2 * hop_count, -1)
    returned = [
        shifted(grad_far[:, slot_idx], ("lon", "sub"), -offsets[slot_idx])
        for slot_idx in range(2 * hop_count)
    ]
    back_blocks = jnp.stack(returned, axis=1).reshape(hid_dev, tile_ids.shape[0], TILE)
    back_tiles = jnp.einsum(
        "st,hsl->htl",
        tile_pick.astype(jnp.float32),
        back_blocks,
        precision=lax.Precision.HIGHEST,
        preferred_element_type=jnp.float32,
    )
    grad_send = (grad_own.reshape(hid_dev, tile_rows, TILE) + back_tiles).reshape(
        hid_dev, node_rows
    )
    grad_send_low = grad_send.astype(jnp.bfloat16)
    grad_pair = jnp.stack([grad_send_low, grad_recv.astype(jnp.bfloat16)])
    node_pair = lax.all_to_all(grad_pair, "ch", split_axis=2, concat_axis=1, tiled=True)
    grad_node = (
        node_cot.astype(jnp.float32)
        + grad_direct
        + left_dot(w_send, node_pair[0])
        + left_dot(w_recv, node_pair[1])
    )
    grad_features = lax.all_to_all(
        grad_node.astype(jnp.bfloat16), "ch", split_axis=0, concat_axis=1, tiled=True
    )
    inv_root = 1.0 / math.sqrt(total_nodes)
    weight_terms = (
        lax.dot_general(
            node_pair[0], node_feats, (((1,), (1,)), ((), ())), preferred_element_type=jnp.float32
        )
        * inv_root
    )
    banded = lax.psum_scatter(weight_terms, ("lon", "sub"), scatter_dimension=1, tiled=True)
    grad_w_send = lax.psum_scatter(banded, "ch", scatter_dimension=0, tiled=True)
    return (updated, grad_features, grad_w_send)


def solution(mesh):
    placed = (
        P("ch", ("parts", "lon", "sub")),
        P("ch", ("parts", "lon", "sub")),
        P(None, ("parts", "lon", "sub")),
        P(("parts", "lon", "sub")),
        P(("parts", "lon", "sub")),
        P(("parts", "lon", "sub"), None, None),
        P(),
        P(),
        P(),
        P(),
        P(),
        P(),
        P(),
        P(),
    )
    return jax.shard_map(
        shards,
        mesh=mesh,
        in_specs=placed,
        out_specs=(
            P("ch", ("parts", "lon", "sub")),
            P("ch", ("parts", "lon", "sub")),
            P(("parts", "ch"), ("lon", "sub")),
        ),
        check_vma=False,
    )
```

profile of v0, /device:TPU:0, one launch (start us, length us, event | category | flops | bytes accessed | tf_op | source)
XLA Modules:
  0.0 341.5 jit_solution(11039431786216963997)
XLA Ops:
  8.3 9.9 %all_gather.3 = bf16[512,512]{0,1:T(8,128)(2,1)S(1)} all-gather(bf16[256,512]{0,1:T(8,128)(2,1)S(1)} %copy.100), channel_id=1, replica_groups=mesh['parts'=2,'lon'=4,'ch'=2,'sub'=2] {'ch'}, dimensions={0}, use_global_device_ids=true | all-gather | bytes 786432 | tf_op jit(solution)/shard_map/all_gather | solution.py:63
  24.5 2.6 collective-permute-start.2
  30.5 3.4 %all-to-all-start.2 = ((bf16[256,2,256]{0,2,1:T(8,128)(2,1)}), bf16[256,2,256]{0,2,1:T(8,128)(2,1)S(1)}, u32[]{:S(2)}, u32[]{:S(2)}) async-start(bf16[256,2,256]{0,2,1:T(8,128)(2,1)} %bitcast.17), calls=%async_computation.2 | async-start | bytes 524288 | tf_op jit(solution)/shard_map/all_to_all | solution.py:70
  41.5 55.2 %while.26 = (s32[]{:T(128)}, f32[256,512]{0,1:T(8,128)}, f32[12,256,512]{1,2,0:T(8,128)}, pred[12,512]{1,0:T(8,128)(4,1)S(1)}, s32[12,512]{1,0:T(8,128)}, /*inde...) while((s32[]{:T(128)}, f32[256,512]{0,1:T(8,128)}, ...), condition=%wide.region_1.2_spmd.clone, body=%wide.region_0.1_spmd.clone.sunk | while | flops 540016640 | bytes 4202607 | solution.py:103
  42.3 2.9 select_add_fusion.4
  46.7 3.0 select_add_fusion.4
  51.3 3.0 select_add_fusion.4
  56.0 3.0 select_add_fusion.4
  60.6 3.0 select_add_fusion.4
  65.2 3.0 select_add_fusion.4
  69.7 3.0 select_add_fusion.4
  74.3 3.0 select_add_fusion.4
  78.9 3.0 select_add_fusion.4
  83.6 3.0 select_add_fusion.4
  88.2 3.0 select_add_fusion.4
  92.8 3.0 select_add_fusion.4
  98.6 4.1 %all-to-all-start = ((bf16[256,2,256]{0,2,1:T(8,128)(2,1)}), bf16[256,2,256]{0,2,1:T(8,128)(2,1)}, u32[]{:S(2)}, u32[]{:S(2)}) async-start(bf16[256,2,256]{0,2,1:T(8,128)(2,1)} %bitcast.10), calls=%async_computation | async-start | bytes 524288 | tf_op jit(solution)/shard_map/all_to_all | solution.py:107
  104.1 4.0 %all-to-all-done = bf16[256,2,256]{0,2,1:T(8,128)(2,1)} async-done(((bf16[256,2,256]{0,2,1:T(8,128)(2,1)}), bf16[256,2,256]{0,2,1:T(8,128)(2,1)}, u32[]{:S(2)}, u32[]{:S(2)}) %all-to-all-start) | async-done | bytes 262176 | tf_op jit(solution)/shard_map/all_to_all | solution.py:107
  112.6 4.1 %all-to-all-start.3 = ((bf16[2,256,256]{1,2,0:T(8,128)(2,1)}), bf16[2,256,256]{1,2,0:T(8,128)(2,1)}, u32[]{:S(2)}, u32[]{:S(2)}) async-start(bf16[2,256,256]{1,2,0:T(8,128)(2,1)} %bitcast.158), calls=%async_computation.3 | async-start | bytes 524288 | tf_op jit(solution)/shard_map/all_to_all | solution.py:126
  116.8 5.5 %all-to-all-done.3 = bf16[2,256,256]{1,2,0:T(8,128)(2,1)} async-done(((bf16[2,256,256]{1,2,0:T(8,128)(2,1)}), bf16[2,256,256]{1,2,0:T(8,128)(2,1)}, u32[]{:S(2)}, u32[]{:S(2)}) %all-to-all-start.3) | async-done | bytes 262176 | tf_op jit(solution)/shard_map/all_to_all | solution.py:126
  124.4 103.2 %while.27 = (s32[]{:T(128)}, f32[256,2048]{1,0:T(8,128)S(1)}, f32[256,512]{1,0:T(8,128)}, pred[12,512]{1,0:T(8,128)(4,1)S(1)}, f32[12,256,512]{1,2,0:T(8,128)}, ...) while((s32[]{:T(128)}, f32[256,2048]{1,0:T(8,128)S(1)}, ...), condition=%wide.region_3.4_spmd.clone, body=%wide.region_2.3_spmd.clone.sunk | while | flops 1079508992 | bytes 14165620 | solution.py:146
  153.2 2.3 select_add_fusion.5
  234.2 4.3 %collective-permute-start.7 = (f32[256,256]{0,1:T(8,128)}, f32[256,256]{0,1:T(8,128)}, u32[]{:S(2)}, u32[]{:S(2)}) collective-permute-start(f32[256,256]{0,1:T(8,128)} %get-tuple-element.257), channel_id=1, source_target_pairs={{4,0},{5,1},{8,4},{9,5},{12,8},{13,9},{0,12},{1,13},{6,2},{7,3},{1... | collective-permute-start | bytes 786440 | tf_op jit(solution)/shard_map/ppermute | solution.py:14
  244.2 7.9 %collective-permute-done.7 = f32[256,256]{0,1:T(8,128)} collective-permute-done((f32[256,256]{0,1:T(8,128)}, f32[256,256]{0,1:T(8,128)}, u32[]{:S(2)}, u32[]{:S(2)}) %collective-permute-start.7) | collective-permute-done | bytes 262176 | tf_op jit(solution)/shard_map/ppermute | solution.py:14
  254.1 2.7 collective-permute-done.9
  257.8 5.0 %collective-permute-done.10 = f32[256,256]{0,1:T(8,128)} collective-permute-done((f32[256,256]{0,1:T(8,128)}, f32[256,256]{0,1:T(8,128)}, u32[]{:S(2)}, u32[]{:S(2)}) %collective-permute-start.10) | collective-permute-done | bytes 262176 | tf_op jit(solution)/shard_map/ppermute | solution.py:14
  263.8 7.4 %collective-permute-done.11 = f32[256,256]{0,1:T(8,128)S(1)} collective-permute-done((f32[256,256]{0,1:T(8,128)}, f32[256,256]{0,1:T(8,128)S(1)}, u32[]{:S(2)}, u32[]{:S(2)}) %collective-permute-start.11) | collective-permute-done | bytes 262176 | tf_op jit(solution)/shard_map/ppermute | solution.py:14
  278.7 11.5 %all_to_all.104 = bf16[2,256,512]{1,0,2:T(2,128)(2,1)S(1)} all-to-all(bf16[2,256,512]{1,0,2:T(2,128)(2,1)S(1)} %copy.119), channel_id=1, replica_groups=mesh['parts'=2,'lon'=4,'ch'=2,'sub'=2] {'ch'}, dimensions={2} | all-to-all | bytes 1048576 | tf_op jit(solution)/shard_map/all_to_all | solution.py:168
  293.0 4.1 %all-to-all-start.1 = ((bf16[2,256,256]{1,2,0:T(8,128)(2,1)}), bf16[2,256,256]{1,2,0:T(8,128)(2,1)}, u32[]{:S(2)}, u32[]{:S(2)}) async-start(bf16[2,256,256]{1,2,0:T(8,128)(2,1)} %bitcast.159), calls=%async_computation.1 | async-start | bytes 524288 | tf_op jit(solution)/shard_map/all_to_all | solution.py:119
  297.9 23.9 %reduce-scatter.3.cloned.1.call-done = f32[512,64]{0,1:T(8,128)} async-done(((f32[512,512]{0,1:T(8,128)}), f32[512,64]{0,1:T(8,128)}) %reduce-scatter.3.cloned.1.call-update) | async-done | bytes 131088 | tf_op jit(solution)/shard_map/reduce_scatter | solution.py:185
  323.9 3.4 %all-to-all-start.5 = ((bf16[2,256,256]{1,2,0:T(8,128)(2,1)}), bf16[2,256,256]{1,2,0:T(8,128)(2,1)S(1)}, u32[]{:S(2)}, u32[]{:S(2)}) async-start(bf16[2,256,256]{1,2,0:T(8,128)(2,1)} %bitcast.157), calls=%async_computation.5 | async-start | bytes 524288 | tf_op jit(solution)/shard_map/all_to_all | solution.py:175
  329.2 4.6 %all-to-all-done.5 = bf16[2,256,256]{1,2,0:T(8,128)(2,1)S(1)} async-done(((bf16[2,256,256]{1,2,0:T(8,128)(2,1)}), bf16[2,256,256]{1,2,0:T(8,128)(2,1)S(1)}, u32[]{:S(2)}, u32[]{:S(2)}) %all-to-all-start.5) | async-done | bytes 262176 | tf_op jit(solution)/shard_map/all_to_all | solution.py:175
  (266 shorter events, 178.7 us)
Async XLA Ops:
  7.2 11.1 %copy-start = (bf16[512,512]{1,0:T(8,128)(2,1)S(1)}, bf16[512,512]{1,0:T(8,128)(2,1)}, u32[]{:S(2)}) copy-start(bf16[512,512]{1,0:T(8,128)(2,1)} %param.24) | copy-start | bytes 1572868
  7.2 12.2 %copy-start.21 = (s32[1,6,2]{1,2,0:T(2,128)S(1)}, s32[1,6,2]{1,2,0:T(2,128)}, u32[]{:S(2)}) copy-start(s32[1,6,2]{1,2,0:T(2,128)} %param.23) | copy-start | bytes 148
  18.2 84.5 %copy-start.2 = (bf16[512,512]{0,1:T(8,128)(2,1)}, bf16[512,512]{0,1:T(8,128)(2,1)S(1)}, u32[]{:S(2)}) copy-start(bf16[512,512]{0,1:T(8,128)(2,1)S(1)} %all_gather.3) | copy-start | bytes 1572868
  21.5 12.5 %copy-start.22 = (f32[512]{0:T(512)S(1)}, f32[512]{0:T(512)}, u32[]{:S(2)}) copy-start(f32[512]{0:T(512)} %param.26) | copy-start | bytes 6148
  21.5 13.2 %copy-start.10 = (bf16[512,512]{1,0:T(8,128)(2,1)S(1)}, bf16[512,512]{1,0:T(8,128)(2,1)}, u32[]{:S(2)}) copy-start(bf16[512,512]{1,0:T(8,128)(2,1)} %param.25) | copy-start | bytes 1572868
  21.6 13.5 %copy-start.17 = (s32[512]{0:T(512)S(1)}, s32[512]{0:T(512)}, u32[]{:S(2)}) copy-start(s32[512]{0:T(512)} %param.21) | copy-start | bytes 6148
  22.4 13.8 %collective-permute-start = (bf16[256,256]{1,0:T(8,128)(2,1)}, bf16[256,256]{1,0:T(8,128)(2,1)S(1)}, u32[]{:S(2)}, u32[]{:S(2)}) collective-permute-start(bf16[256,256]{1,0:T(8,128)(2,1)} %bitcast.4), channel_id=1, source_target_pairs={{13,0},{0,1},{1,4},{4,5},{5,8},{8,9},{9,12},{12,13},{15,2},{2,3},{... | collective-permute-start | bytes 393224 | tf_op jit(solution)/shard_map/ppermute | solution.py:14
  22.5 14.4 %collective-permute-start.1 = (bf16[256,256]{1,0:T(8,128)(2,1)S(1)}, bf16[256,256]{1,0:T(8,128)(2,1)}, u32[]{:S(2)}, u32[]{:S(2)}) collective-permute-start(bf16[256,256]{1,0:T(8,128)(2,1)S(1)} %bitcast.191), channel_id=1, source_target_pairs={{12,0},{13,1},{0,4},{1,5},{4,8},{5,9},{8,12},{9,13},{14,2},{15,3},... | collective-permute-start | bytes 393224 | tf_op jit(solution)/shard_map/ppermute | solution.py:14
  24.5 14.0 %collective-permute-start.2 = (bf16[256,256]{1,0:T(8,128)(2,1)S(1)}, bf16[256,256]{1,0:T(8,128)(2,1)S(1)}, u32[]{:S(2)}, u32[]{:S(2)}) collective-permute-start(bf16[256,256]{1,0:T(8,128)(2,1)S(1)} %bitcast.190), channel_id=1, source_target_pairs={{9,0},{12,1},{13,4},{0,5},{1,8},{4,9},{5,12},{8,13},{11,2},{14,3},... | collective-permute-start | bytes 393224 | tf_op jit(solution)/shard_map/ppermute | solution.py:14
  27.2 11.9 %collective-permute-start.3 = (bf16[256,256]{1,0:T(8,128)(2,1)S(1)}, bf16[256,256]{1,0:T(8,128)(2,1)S(1)}, u32[]{:S(2)}, u32[]{:S(2)}) collective-permute-start(bf16[256,256]{1,0:T(8,128)(2,1)S(1)} %bitcast.189), channel_id=1, source_target_pairs={{1,0},{4,1},{5,4},{8,5},{9,8},{12,9},{13,12},{0,13},{3,2},{6,3},{7... | collective-permute-start | bytes 393224 | tf_op jit(solution)/shard_map/ppermute | solution.py:14
  28.4 11.4 %collective-permute-start.4 = (bf16[256,256]{1,0:T(8,128)(2,1)S(1)}, bf16[256,256]{1,0:T(8,128)(2,1)S(1)}, u32[]{:S(2)}, u32[]{:S(2)}) collective-permute-start(bf16[256,256]{1,0:T(8,128)(2,1)S(1)} %bitcast.188), channel_id=1, source_target_pairs={{4,0},{5,1},{8,4},{9,5},{12,8},{13,9},{0,12},{1,13},{6,2},{7,3},{1... | collective-permute-start | bytes 393224 | tf_op jit(solution)/shard_map/ppermute | solution.py:14
  30.5 68.1 %all-to-all-start.2 = ((bf16[256,2,256]{0,2,1:T(8,128)(2,1)}), bf16[256,2,256]{0,2,1:T(8,128)(2,1)S(1)}, u32[]{:S(2)}, u32[]{:S(2)}) async-start(bf16[256,2,256]{0,2,1:T(8,128)(2,1)} %bitcast.17), calls=%async_computation.2 | async-start | bytes 524288 | tf_op jit(solution)/shard_map/all_to_all | solution.py:70
  36.1 4.7 %collective-permute-start.5 = (bf16[256,256]{1,0:T(8,128)(2,1)}, bf16[256,256]{1,0:T(8,128)(2,1)S(1)}, u32[]{:S(2)}, u32[]{:S(2)}) collective-permute-start(bf16[256,256]{1,0:T(8,128)(2,1)} %bitcast.192), channel_id=1, source_target_pairs={{5,0},{8,1},{9,4},{12,5},{13,8},{0,9},{1,12},{4,13},{7,2},{10,3},{... | collective-permute-start | bytes 393224 | tf_op jit(solution)/shard_map/ppermute | solution.py:14
  41.5 61.3 %copy-start.7 = (bf16[512,512]{1,0:T(8,128)(2,1)S(1)}, bf16[512,512]{1,0:T(8,128)(2,1)}, u32[]{:S(2)}) copy-start(bf16[512,512]{1,0:T(8,128)(2,1)} %param.28) | copy-start | bytes 1572868
  96.6 12.5 %copy-start.5 = (bf16[512,512]{1,0:T(8,128)(2,1)S(1)}, bf16[512,512]{1,0:T(8,128)(2,1)}, u32[]{:S(2)}) copy-start(bf16[512,512]{1,0:T(8,128)(2,1)} %param.29) | copy-start | bytes 1572868
  96.6 12.5 %copy-start.6 = (bf16[512,512]{1,0:T(8,128)(2,1)S(1)}, bf16[512,512]{1,0:T(8,128)(2,1)}, u32[]{:S(2)}) copy-start(bf16[512,512]{1,0:T(8,128)(2,1)} %param.27) | copy-start | bytes 1572868
  96.6 12.5 %copy-start.20 = (f32[512]{0:T(512)S(1)}, f32[512]{0:T(512)}, u32[]{:S(2)}) copy-start(f32[512]{0:T(512)} %param.30) | copy-start | bytes 6148
  98.6 9.4 %all-to-all-start = ((bf16[256,2,256]{0,2,1:T(8,128)(2,1)}), bf16[256,2,256]{0,2,1:T(8,128)(2,1)}, u32[]{:S(2)}, u32[]{:S(2)}) async-start(bf16[256,2,256]{0,2,1:T(8,128)(2,1)} %bitcast.10), calls=%async_computation | async-start | bytes 524288 | tf_op jit(solution)/shard_map/all_to_all | solution.py:107
  112.6 9.6 %all-to-all-start.3 = ((bf16[2,256,256]{1,2,0:T(8,128)(2,1)}), bf16[2,256,256]{1,2,0:T(8,128)(2,1)}, u32[]{:S(2)}, u32[]{:S(2)}) async-start(bf16[2,256,256]{1,2,0:T(8,128)(2,1)} %bitcast.158), calls=%async_computation.3 | async-start | bytes 524288 | tf_op jit(solution)/shard_map/all_to_all | solution.py:126
  116.7 205.1 %reduce-scatter.3.cloned.1.call-start = ((), (), s32[]{:S(2)}) async-start(), calls=%async_computation.8 | async-start | bytes 1179648 | tf_op jit(solution)/shard_map/reduce_scatter | solution.py:185
  229.4 11.1 %copy-start.1 = (f32[256,512]{1,0:T(8,128)S(1)}, f32[256,512]{1,0:T(8,128)}, u32[]{:S(2)}) copy-start(f32[256,512]{1,0:T(8,128)} %get-tuple-element.92) | copy-start | bytes 1572868
  232.0 10.3 %collective-permute-start.6 = (f32[256,256]{0,1:T(8,128)}, f32[256,256]{0,1:T(8,128)}, u32[]{:S(2)}, u32[]{:S(2)}) collective-permute-start(f32[256,256]{0,1:T(8,128)} %get-tuple-element.258), channel_id=1, source_target_pairs={{1,0},{4,1},{5,4},{8,5},{9,8},{12,9},{13,12},{0,13},{3,2},{6,3},{7... | collective-permute-start | bytes 786440 | tf_op jit(solution)/shard_map/ppermute | solution.py:14
  234.2 18.0 %collective-permute-start.7 = (f32[256,256]{0,1:T(8,128)}, f32[256,256]{0,1:T(8,128)}, u32[]{:S(2)}, u32[]{:S(2)}) collective-permute-start(f32[256,256]{0,1:T(8,128)} %get-tuple-element.257), channel_id=1, source_target_pairs={{4,0},{5,1},{8,4},{9,5},{12,8},{13,9},{0,12},{1,13},{6,2},{7,3},{1... | collective-permute-start | bytes 786440 | tf_op jit(solution)/shard_map/ppermute | solution.py:14
  238.4 14.7 %collective-permute-start.8 = (f32[256,256]{0,1:T(8,128)}, f32[256,256]{0,1:T(8,128)}, u32[]{:S(2)}, u32[]{:S(2)}) collective-permute-start(f32[256,256]{0,1:T(8,128)} %get-tuple-element.256), channel_id=1, source_target_pairs={{5,0},{8,1},{9,4},{12,5},{13,8},{0,9},{1,12},{4,13},{7,2},{10,3},{... | collective-permute-start | bytes 786440 | tf_op jit(solution)/shard_map/ppermute | solution.py:14
  238.4 18.4 %collective-permute-start.9 = (f32[256,256]{0,1:T(8,128)}, f32[256,256]{0,1:T(8,128)}, u32[]{:S(2)}, u32[]{:S(2)}) collective-permute-start(f32[256,256]{0,1:T(8,128)} %get-tuple-element.255), channel_id=1, source_target_pairs={{13,0},{0,1},{1,4},{4,5},{5,8},{8,9},{9,12},{12,13},{15,2},{2,3},{... | collective-permute-start | bytes 786440 | tf_op jit(solution)/shard_map/ppermute | solution.py:14
  238.7 24.1 %collective-permute-start.10 = (f32[256,256]{0,1:T(8,128)}, f32[256,256]{0,1:T(8,128)}, u32[]{:S(2)}, u32[]{:S(2)}) collective-permute-start(f32[256,256]{0,1:T(8,128)} %get-tuple-element.254), channel_id=1, source_target_pairs={{12,0},{13,1},{0,4},{1,5},{4,8},{5,9},{8,12},{9,13},{14,2},{15,3},... | collective-permute-start | bytes 786440 | tf_op jit(solution)/shard_map/ppermute | solution.py:14
  242.3 28.8 %collective-permute-start.11 = (f32[256,256]{0,1:T(8,128)}, f32[256,256]{0,1:T(8,128)S(1)}, u32[]{:S(2)}, u32[]{:S(2)}) collective-permute-start(f32[256,256]{0,1:T(8,128)} %get-tuple-element.253), channel_id=1, source_target_pairs={{9,0},{12,1},{13,4},{0,5},{1,8},{4,9},{5,12},{8,13},{11,2},{14,3},... | collective-permute-start | bytes 786440 | tf_op jit(solution)/shard_map/ppermute | solution.py:14
  278.7 11.8 %copy-start.3 = (bf16[512,512]{0,1:T(8,128)(2,1)S(1)}, bf16[512,512]{0,1:T(8,128)(2,1)}, u32[]{:S(2)}) copy-start(bf16[512,512]{0,1:T(8,128)(2,1)} %copy-done.2) | copy-start | bytes 1572868
  292.2 29.7 %copy-start.8 = (bf16[512,512]{1,0:T(8,128)(2,1)S(1)}, bf16[512,512]{1,0:T(8,128)(2,1)}, u32[]{:S(2)}) copy-start(bf16[512,512]{1,0:T(8,128)(2,1)} %param.28) | copy-start | bytes 1572868
  293.0 30.9 %all-to-all-start.1 = ((bf16[2,256,256]{1,2,0:T(8,128)(2,1)}), bf16[2,256,256]{1,2,0:T(8,128)(2,1)}, u32[]{:S(2)}, u32[]{:S(2)}) async-start(bf16[2,256,256]{1,2,0:T(8,128)(2,1)} %bitcast.159), calls=%async_computation.1 | async-start | bytes 524288 | tf_op jit(solution)/shard_map/all_to_all | solution.py:119
  297.1 37.6 %reduce-scatter.5.cloned.1.call-start = ((), (), s32[]{:S(2)}) async-start(), calls=%async_computation.9 | async-start | bytes 196608 | tf_op jit(solution)/shard_map/reduce_scatter | solution.py:186
  323.9 9.9 %all-to-all-start.5 = ((bf16[2,256,256]{1,2,0:T(8,128)(2,1)}), bf16[2,256,256]{1,2,0:T(8,128)(2,1)S(1)}, u32[]{:S(2)}, u32[]{:S(2)}) async-start(bf16[2,256,256]{1,2,0:T(8,128)(2,1)} %bitcast.157), calls=%async_computation.5 | async-start | bytes 524288 | tf_op jit(solution)/shard_map/all_to_all | solution.py:175
  (12 other events, 54.4 us)
Sparse Core Ops, SparseCore 0:
  291.9 29.8 reduce-scatter.2
  324.7 9.2 reduce-scatter.4
where the time goes:
time: 345 us; the launch traced here: 341 us
  local copies, waits for them, and re-layouts  99.9 us (29%)
  matrix products  75.2 us (22%)
  waiting for transfers between devices  61.4 us (18%)
  starting transfers between devices  35.7 us (10%)
  other arithmetic  31.9 us (9%)
  blocking collectives  21.4 us (6%)
  between operations  15.4 us (4%)
    dynamic_slice x24, local copies, waits for them, and re-layouts, shards(): lax.scan(backward_edge, start_back, (senders, edge_valid, edge_pre))  37.5 us
    dot_general x12, matrix products, forward_edge(): jnp.dot(extended, picker, preferred_element_type=jnp.float32) + recv_base  36 us
    add x12, other arithmetic, backward_edge(): return ((grad_ext + spread, grad_recv + grad_row), None)  27.1 us
    reduce_scatter x1, waiting for transfers between devices, shards(): lax.psum_scatter(weight_terms, ('lon', 'sub'), scatter_dimension=1, tiled...  23.9 us
    ppermute x12, waiting for transfers between devices, shifted(): return lax.ppermute(block, axis, route)  23.3 us
    unnamed x71, local copies, waits for them, and re-layouts  18.8 us
    dynamic_slice x48, local copies, waits for them, and re-layouts, shards(): lax.scan(forward_edge, jnp.zeros((hid_dev, node_rows), jnp.float32), (sen...  18.1 us
    dot_general x12, matrix products, backward_edge(): lax.dot_general(high_part, picker, spread_dims, preferred_element_type=jn...  16.5 us
  transfers between devices with their start and end apart: 19, of which 9 were waited for; matrix products, arithmetic and copies ran while one was open for 23% of the time, Pallas kernels for 0%

commit v1 on v0

v1 whole, which is shorter than its diff:
```python
import functools
import math

import jax
import jax.numpy as jnp
from jax import lax
from jax.experimental import pallas as pl
from jax.experimental.pallas import tpu as pltpu
from jax.sharding import PartitionSpec as P

TILE = 128
CHUNK = 256
LANES = 128
PACK = 16
MIB = 1 << 20


def shifted(block, axis, distance):
    size = lax.axis_size(axis)
    route = [((i - distance) % size, i) for i in range(size)]
    return lax.ppermute(block, axis, route)


def gathered(block, axis):
    return [block] + [shifted(block, axis, k) for k in range(1, lax.axis_size(axis))]


def dot(left, right):
    return jnp.dot(left, right, preferred_element_type=jnp.float32)


def dot_nt(left, right):
    return lax.dot_general(
        left, right, (((1,), (1,)), ((), ())), preferred_element_type=jnp.float32
    )


def sigmoid(value):
    return 0.5 * jnp.tanh(0.5 * value) + 0.5


def call(kernel, out_shape, operands, flops, scratch=(), scalars=1, limit=32):
    vmem = pl.BlockSpec(memory_space=pltpu.VMEM)
    smem = pl.BlockSpec(memory_space=pltpu.SMEM)
    moved = sum(math.prod(x.shape) * x.dtype.itemsize for x in operands)
    return pl.pallas_call(
        kernel,
        out_shape=out_shape,
        in_specs=[smem] * scalars + [vmem] * (len(operands) - scalars),
        out_specs=jax.tree.map(lambda _: vmem, out_shape),
        scratch_shapes=scratch,
        compiler_params=pltpu.CompilerParams(vmem_limit_bytes=limit * MIB),
        cost_estimate=pl.CostEstimate(flops=flops, bytes_accessed=moved, transcendentals=0),
    )(*operands)


def assemble(whole_ref, blocks, first):
    count = len(blocks)
    rows = blocks[0].shape[0]
    for k, block in enumerate(blocks):
        place = lax.rem(first - k + count, count) * rows
        whole_ref[pl.ds(pl.multiple_of(place, rows), rows), :] = block[...]


def project_kernel(count, info, *refs):
    blocks = refs[:count]
    w_send, w_recv, bias, feats, proj, base, parcels = refs[count:]
    assemble(feats, blocks, info[0])
    whole = feats[...]
    proj[...] = dot(w_send[...], whole).T.astype(jnp.bfloat16)
    base[...] = (dot(w_recv[...], whole).astype(jnp.bfloat16).astype(jnp.float32) + bias[...]).T
    slots, rows, _ = parcels.shape
    per_slot = rows // TILE
    for slot in range(slots):
        for place in range(per_slot):
            tile = info[2 + slot * per_slot + place]
            parcels[slot, place * TILE : (place + 1) * TILE, :] = proj[
                pl.ds(pl.multiple_of(tile * TILE, TILE), TILE), :
            ]


def prepare_kernel(count, info, *refs):
    blocks = refs[:count]
    feats, w_node_v, bias, w_out_t, cots, pre, grad_hidden = refs[count:]
    assemble(cots, blocks, info[0])
    pre[...] = dot(w_node_v[...], feats[...]) + bias[...]
    lane = lax.broadcasted_iota(jnp.int32, (1, cots.shape[1]), 1)
    active = (lane < info[1] * TILE).astype(jnp.bfloat16)
    grad_hidden[...] = dot(w_out_t[...], cots[...] * active)


def forward_kernel(slots, low, high, base, inv_deg, proj, *refs):
    arrivals = refs[:slots]
    message, slope, ext, total = refs[slots:]
    own = proj.shape[0]
    rows = arrivals[0].shape[0]
    ext[:own, :] = proj[...]
    for slot in range(slots):
        ext[own + slot * rows : own + (slot + 1) * rows, :] = arrivals[slot][...]
    chunks = ext.shape[0] // CHUNK
    halves = CHUNK // LANES
    total[...] = jnp.zeros_like(total)
    lane = lax.broadcasted_iota(jnp.int32, (own, LANES), 1)

    def step(m, carry):
        low_m, high_m = low[m], high[m]
        one = jnp.bfloat16(1.0)
        zero = jnp.bfloat16(0.0)
        marks = [
            jnp.where(low_m == (lane + half * LANES).astype(jnp.bfloat16), one, zero)
            for half in range(halves)
        ]
        picker = jnp.concatenate(
            [
                jnp.where(high_m == jnp.bfloat16(chunk), mark, zero)
                for chunk in range(chunks)
                for mark in marks
            ],
            axis=1,
        )
        pre = dot(picker, ext[...]) + base[...]
        valid = high_m[:, :1].astype(jnp.float32) < chunks
        sig = sigmoid(pre)
        act = pre * sig
        total[...] += jnp.where(valid, act, 0.0)
        slope[m] = jnp.where(valid, sig + act * (1.0 - sig), 0.0).astype(jnp.bfloat16)
        return carry

    lax.fori_loop(0, low.shape[0], step, 0)
    message[...] = (total[...] * inv_deg[...]).astype(jnp.bfloat16)


def node_kernel(count, inv_deg, *refs):
    blocks = refs[:count]
    w_msg, w_node_a, w_node_a_t, w_msg_t, pre, grad_hidden, hidden, grad_pre, scale = refs[count:]
    agg = dot_nt(w_msg[0], blocks[0][...])
    for k in range(1, count):
        agg += dot_nt(w_msg[k], blocks[k][...])
    node_pre = pre[...] + dot(w_node_a[...], agg.astype(jnp.bfloat16))
    sig = sigmoid(node_pre)
    act = node_pre * sig
    hidden[...] = act.astype(jnp.bfloat16)
    low_grad = (grad_hidden[...] * (sig + act * (1.0 - sig))).astype(jnp.bfloat16)
    grad_pre[...] = low_grad
    grad_agg = dot(w_node_a_t[...], low_grad).astype(jnp.bfloat16)
    grad_msg = dot(w_msg_t[...], grad_agg)
    scale[...] = (grad_msg.astype(jnp.bfloat16).astype(jnp.float32) * inv_deg[...]).T


def far_kernel(low, high, slope, scale, *refs):
    outs, (grads, recv, total, recv_total) = refs[:-4], refs[-4:]
    slots = len(outs)
    rows = outs[0].shape[0]
    nodes = scale.shape[0]
    first = nodes // CHUNK
    chunks = slots * rows // CHUNK
    total[...] = jnp.zeros_like(total)
    recv_total[...] = jnp.zeros_like(recv_total)
    groups = CHUNK // PACK
    place = lax.broadcasted_iota(jnp.int32, (groups, PACK, nodes), 0) * PACK
    place = place + lax.broadcasted_iota(jnp.int32, (groups, PACK, nodes), 1)

    def step(m, carry):
        grad = slope[m].astype(jnp.float32) * scale[...]
        recv_total[...] += grad
        grad_low = grad.astype(jnp.bfloat16)
        grads[m] = grad_low
        one = jnp.bfloat16(1.0)
        zero = jnp.bfloat16(0.0)
        mark = jnp.where(low[m][None] == place.astype(jnp.bfloat16), one, zero)
        picker = jnp.concatenate(
            [
                jnp.where(high[m][None] == jnp.bfloat16(first + chunk), mark, zero)
                for chunk in range(chunks)
            ],
            axis=0,
        ).reshape(chunks * CHUNK, nodes)
        total[...] += dot(picker, grad_low)
        return carry

    lax.fori_loop(0, slope.shape[0], step, 0)
    for slot in range(slots):
        outs[slot][...] = total[slot * rows : (slot + 1) * rows, :].astype(jnp.bfloat16)
    recv[...] = recv_total[...].astype(jnp.bfloat16)


def own_kernel(low, high, grads, total):
    nodes = total.shape[0]
    chunks = nodes // CHUNK
    groups = CHUNK // PACK
    total[...] = jnp.zeros_like(total)
    place = lax.broadcasted_iota(jnp.int32, (groups, PACK, nodes), 0) * PACK
    place = place + lax.broadcasted_iota(jnp.int32, (groups, PACK, nodes), 1)

    def step(m, carry):
        one = jnp.bfloat16(1.0)
        zero = jnp.bfloat16(0.0)
        mark = jnp.where(low[m][None] == place.astype(jnp.bfloat16), one, zero)
        picker = jnp.concatenate(
            [
                jnp.where(high[m][None] == jnp.bfloat16(chunk), mark, zero)
                for chunk in range(chunks)
            ],
            axis=0,
        ).reshape(chunks * CHUNK, nodes)
        total[...] += dot(picker, grads[m])
        return carry

    lax.fori_loop(0, grads.shape[0], step, 0)


def output_kernel(info, feats, cots, hidden, grad_pre, w_out, w_node_v_t, updated, direct):
    lane = lax.broadcasted_iota(jnp.int32, (1, feats.shape[1]), 1)
    active = (lane < info[1] * TILE).astype(jnp.float32)
    updated[...] = (
        feats[...].astype(jnp.float32) + active * dot(w_out[...], hidden[...])
    ).astype(jnp.bfloat16)
    direct[...] = cots[...].astype(jnp.float32) + dot(w_node_v_t[...], grad_pre[...])


def final_kernel(inv_root, info, own, recv, direct, feats, w_send_t, w_recv_t, *refs):
    returned, (kept, sent, weight, total) = refs[:-4], refs[-4:]
    total[...] = own[...]
    per_slot = returned[0].shape[0] // TILE
    for slot, block in enumerate(returned):
        for place in range(per_slot):
            tile = info[2 + slot * per_slot + place]
            rows = pl.ds(pl.multiple_of(tile * TILE, TILE), TILE)
            total[rows, :] += block[place * TILE : (place + 1) * TILE, :].astype(jnp.float32)
    grad_send = total[...].T.astype(jnp.bfloat16)
    grad_recv = recv[...].astype(jnp.float32).T.astype(jnp.bfloat16)
    chans = direct.shape[0]
    terms = dot(w_send_t[...], grad_send) + dot(w_recv_t[...], grad_recv)
    kept[...] = direct[...] + terms[:chans]
    for k in range(sent.shape[0]):
        sent[k] = terms[(k + 1) * chans : (k + 2) * chans].astype(jnp.bfloat16)
    weight[...] = (dot_nt(grad_send, feats[...]) * inv_root).astype(jnp.bfloat16)


def shards(
    features,
    cotangent,
    senders,
    in_degree,
    tile_count,
    send_tiles,
    w_send,
    w_recv,
    bias_edge,
    w_msg,
    w_node_v,
    w_node_a,
    bias_node,
    w_out,
):
    chans, nodes = features.shape
    count = lax.axis_size("ch")
    mine = lax.axis_index("ch")
    hidden_all, chans_all = w_send.shape
    hid = hidden_all // count
    hid_start = mine * hid
    chan_start = mine * chans
    cycle = ("lon", "sub")
    shard_count = lax.axis_size(cycle)
    total_nodes = nodes * shard_count
    degree = senders.shape[0]
    hop_count = send_tiles.shape[1] // 2
    slots = 2 * hop_count
    slot_rows = send_tiles.shape[2] * TILE
    offsets = [number + 1 for number in range(hop_count)] + [
        -(number + 1) for number in range(hop_count)
    ]
    ext_len = nodes + slots * slot_rows
    chunks = ext_len // CHUNK
    bf16, f32 = jnp.bfloat16, jnp.float32
    shape = jax.ShapeDtypeStruct

    info = jnp.concatenate(
        [mine.reshape(1).astype(jnp.int32), tile_count, send_tiles.reshape(-1)]
    )
    feat_blocks = gathered(features, "ch")
    cot_blocks = gathered(cotangent, "ch")

    rows_of = lambda w, k: lax.dynamic_slice_in_dim(w, (mine + k) % count * hid, hid, 0)
    cols_of = lambda w, k: lax.dynamic_slice_in_dim(w, (mine + k) % count * hid, hid, 1)
    w_send_my, w_recv_my = rows_of(w_send, 0), rows_of(w_recv, 0)
    bias_my = lax.dynamic_slice_in_dim(bias_edge, hid_start, hid, 0)[:, None]
    roll = lambda w: jnp.concatenate(
        [
            lax.dynamic_slice_in_dim(w, (mine + k) % count * chans, chans, 0)
            for k in range(count)
        ],
        axis=0,
    )
    w_send_t, w_recv_t = roll(w_send_my.T), roll(w_recv_my.T)
    w_msg_rolled = jnp.stack([cols_of(w_msg, (count - k) % count) for k in range(count)])
    w_msg_t = cols_of(w_msg, 0).T
    w_out_my = lax.dynamic_slice_in_dim(w_out, chan_start, chans, 0)
    w_node_v_t = lax.dynamic_slice_in_dim(w_node_v, chan_start, chans, 1).T

    active = jnp.arange(nodes) < tile_count[0] * TILE
    valid = (jnp.arange(degree)[:, None] < in_degree[None, :]) & active[None, :]
    low = (senders % CHUNK).astype(bf16)
    high = jnp.where(valid, senders // CHUNK, chunks).astype(bf16)
    low_cols = jnp.broadcast_to(low[:, :, None], (degree, nodes, LANES))
    high_cols = jnp.broadcast_to(high[:, :, None], (degree, nodes, LANES))
    low_rows = jnp.broadcast_to(low[:, None, :], (degree, PACK, nodes))
    high_rows = jnp.broadcast_to(high[:, None, :], (degree, PACK, nodes))
    inv_deg = 1.0 / in_degree.astype(f32)

    feats, proj, base, parcels = call(
        functools.partial(project_kernel, count),
        (
            shape((chans_all, nodes), bf16),
            shape((nodes, hid), bf16),
            shape((nodes, hid), f32),
            shape((slots, slot_rows, hid), bf16),
        ),
        [info] + feat_blocks + [w_send_my, w_recv_my, bias_my],
        flops=4 * hid * chans_all * nodes,
    )
    arrivals = [shifted(parcels[slot], cycle, offsets[slot]) for slot in range(slots)]

    cots, pre, grad_hidden = call(
        functools.partial(prepare_kernel, count),
        (
            shape((chans_all, nodes), bf16),
            shape((hidden_all, nodes), f32),
            shape((hidden_all, nodes), f32),
        ),
        [info] + cot_blocks + [feats, w_node_v, bias_node[:, None], w_out.T],
        flops=4 * hidden_all * chans_all * nodes,
    )

    message, slope = call(
        functools.partial(forward_kernel, slots),
        (shape((nodes, hid), bf16), shape((degree, nodes, hid), bf16)),
        [low_cols, high_cols, base, inv_deg[:, None], proj] + arrivals,
        flops=2 * degree * nodes * ext_len * hid,
        scratch=[pltpu.VMEM((ext_len, hid), bf16), pltpu.VMEM((nodes, hid), f32)],
        scalars=0,
    )
    messages = gathered(message, "ch")

    hidden, grad_pre, scale = call(
        functools.partial(node_kernel, count),
        (
            shape((hidden_all, nodes), bf16),
            shape((hidden_all, nodes), bf16),
            shape((nodes, hid), f32),
        ),
        [inv_deg[None, :]]
        + messages
        + [w_msg_rolled, w_node_a, w_node_a.T, w_msg_t, pre, grad_hidden],
        flops=6 * hidden_all * chans_all * nodes,
        scalars=0,
    )

    *far, grads, grad_recv = call(
        far_kernel,
        (
            *[shape((slot_rows, hid), bf16)] * slots,
            shape((degree, nodes, hid), bf16),
            shape((nodes, hid), bf16),
        ),
        [low_rows, high_rows, slope, scale],
        flops=2 * degree * nodes * (ext_len - nodes) * hid,
        scratch=[pltpu.VMEM((ext_len - nodes, hid), f32), pltpu.VMEM((nodes, hid), f32)],
        scalars=0,
    )
    returned = [shifted(far[slot], cycle, -offsets[slot]) for slot in range(slots)]

    own = call(
        own_kernel,
        shape((nodes, hid), f32),
        [low_rows, high_rows, grads],
        flops=2 * degree * nodes * nodes * hid,
        scalars=0,
    )
    updated, direct = call(
        output_kernel,
        (shape((chans, nodes), bf16), shape((chans, nodes), f32)),
        [info, features, cotangent, hidden, grad_pre, w_out_my, w_node_v_t],
        flops=4 * hidden_all * chans * nodes,
    )

    kept, sent, weight = call(
        functools.partial(final_kernel, 1.0 / math.sqrt(total_nodes)),
        (
            shape((chans, nodes), f32),
            shape((count - 1, chans, nodes), bf16),
            shape((hid, chans_all), bf16),
        ),
        [info, own, grad_recv, direct, feats, w_send_t, w_recv_t] + returned,
        flops=6 * hid * chans_all * nodes,
        scratch=[pltpu.VMEM((nodes, hid), f32)],
    )
    for k in range(1, count):
        kept = kept + shifted(sent[k - 1], "ch", k).astype(f32)
    grad_features = kept.astype(bf16)

    columns = chans_all // shard_count
    weight_terms = jnp.moveaxis(weight.reshape(hid, shard_count, columns), 1, 0)
    weight_terms = lax.all_to_all(weight_terms, cycle, split_axis=0, concat_axis=0)
    grad_w_send = jnp.sum(weight_terms.astype(f32), axis=0)
    return (updated, grad_features, grad_w_send)


def solution(mesh):
    nodes_last = P("ch", ("parts", "lon", "sub"))
    spread = ("parts", "lon", "sub")
    placed = (nodes_last, nodes_last, P(None, spread), P(spread), P(spread), P(spread, None, None))
    return jax.shard_map(
        shards,
        mesh=mesh,
        in_specs=placed + (P(),) * 8,
        out_specs=(nodes_last, nodes_last, P(("parts", "ch"), ("lon", "sub"))),
        check_vma=False,
    )
```

time: 345 us -> 110 us (0.32)
  matrix products: 75.2 us -> 0 us
  local copies, waits for them, and re-layouts: 99.9 us -> 25 us
  waiting for transfers between devices: 61.4 us -> 26 us
  Pallas kernels: 0 us -> 30.6 us
  other arithmetic: 31.9 us -> 3.71 us
  blocking collectives: 21.4 us -> 0 us
  between operations: 15.4 us -> 1.71 us
  starting transfers between devices: 35.7 us -> 22.3 us
    dot_general x49 -> x0, matrix products: 75.2 us -> none  [the longest x12 36 us: forward_edge(): jnp.dot(extended, picker, preferred_element_type=jnp.float32) + recv_base]
    dynamic_slice x73 -> x5, local copies, waits for them, and re-layouts: 55.6 us -> 4.43 us  [the longest x1 1.07 us: shards(): lax.dynamic_slice_in_dim(w, (mine + k) % count * hid, hid, 0)]
    pallas_call x0 -> x8, Pallas kernels: none -> 30.6 us  [call(): pl.pallas_call(kernel, out_shape=out_shape, in_specs=[smem] * scalars + [...]
    add x12 -> x0, other arithmetic: 27.1 us -> none  [backward_edge(): return ((grad_ext + spread, grad_recv + grad_row), None)]
    reduce_scatter x2 -> x0, waiting for transfers between devices: 24 us -> none  [the longest x1 23.9 us: shards(): lax.psum_scatter(weight_terms, ('lon', 'sub'), scatter_dimension=1, tiled...]
    all_to_all x5 -> x1, starting transfers between devices: 19.2 us -> 4.79 us  [shards(): lax.all_to_all(weight_terms, cycle, split_axis=0, concat_axis=0)]
    all_to_all x1 -> x0, blocking collectives: 11.5 us -> none  [shards(): lax.all_to_all(grad_pair, 'ch', split_axis=2, concat_axis=1, tiled=True)]
    dynamic_update_slice x12 -> x0, local copies, waits for them, and re-layouts: 10.1 us -> none  [shards(): lax.scan(forward_edge, jnp.zeros((hid_dev, node_rows), jnp.float32), (sen...]
  transfers between devices with their start and end apart: 19 -> 17, of which waited for: 9 -> 7; matrix products, arithmetic and copies ran while one was open for 23% -> 24% of each run, Pallas kernels for 0% -> 17%
where the time goes in v1:
time: 110 us; the launch traced here: 109 us
  Pallas kernels  30.6 us (28%)
  waiting for transfers between devices  26 us (24%)
  local copies, waits for them, and re-layouts  25 us (23%)
  starting transfers between devices  22.3 us (20%)
  other arithmetic  3.71 us (3%)
  between operations  1.71 us (2%)
    pallas_call x8, Pallas kernels, call(): pl.pallas_call(kernel, out_shape=out_shape, in_specs=[smem] * scalars + [...  30.6 us
    ppermute x16, waiting for transfers between devices, shifted(): return lax.ppermute(block, axis, route)  19.6 us
    ppermute x16, starting transfers between devices, shifted(): return lax.ppermute(block, axis, route)  17.6 us
    unnamed x53, local copies, waits for them, and re-layouts  11.3 us
    all_to_all x1, waiting for transfers between devices, shards(): lax.all_to_all(weight_terms, cycle, split_axis=0, concat_axis=0)  6.42 us
    all_to_all x1, starting transfers between devices, shards(): lax.all_to_all(weight_terms, cycle, split_axis=0, concat_axis=0)  4.79 us
    another operation x1, local copies, waits for them, and re-layouts  2.32 us
  transfers between devices with their start and end apart: 17, of which 7 were waited for; matrix products, arithmetic and copies ran while one was open for 24% of the time, Pallas kernels for 17%

profile of v1, /device:TPU:0, one launch (start us, length us, event | category | flops | bytes accessed | tf_op | source)
XLA Modules:
  0.0 109.5 jit_solution(17473816249208628154)
XLA Ops:
  0.7 3.0 %collective-permute-start = (bf16[256,512]{1,0:T(8,128)(2,1)}, bf16[256,512]{1,0:T(8,128)(2,1)S(1)}, u32[]{:S(2)}, u32[]{:S(2)}) collective-permute-start(bf16[256,512]{1,0:T(8,128)(2,1)} %feats.1), channel_id=1, source_target_pairs={{2,0},{0,2},{3,1},{1,3},{6,4},{4,6},{7,5},{5,7},{10,8},{8,10},{11,... | collective-permute-start | bytes 786440 | tf_op jit(solution)/shard_map/ppermute | solution.py:21
  8.0 1.4 %fusion.2 = (bf16[12,512]{1,0:T(8,128)(2,1)}, bf16[12,512]{1,0:T(8,128)(2,1)}) fusion(s32[12,512]{1,0:T(8,128)} %param.16, s32[512]{0:T(512)} %param.17, pred[512]{0:T(512)(128)(4,1)S(1)} %iota_compare_fusion.1), kind=kLoop, calls=%fused_computation.19 | loop fusion | flops 147456 | bytes 51712 | tf_op jit(solution)/shard_map/convert_element_type | solution.py:304
  11.1 1.2 %shard_map.157 = (bf16[512,512]{1,0:T(8,128)(2,1)S(1)}, bf16[512,256]{1,0:T(8,128)(2,1)S(1)}, f32[512,256]{1,0:T(8,128)S(1)}, bf16[6,256,256]{2,1,0:T(8,128)(2,1)S(1)}) custom-call(s32[14]{0:T(128)S(1)} %pad_add_fusion.info, bf16[256,512]{1,0:T(8,128)(2,1)S(1)} %copy-done.4, bf16[256,512]{1,0:T(8,128)(2,1)S(1)} %collective-permute-done.refs_1_, ...), custom_call_target="tpu_custom_call" | custom-call | flops 268435456 | bytes 1049656 | tf_op jit(solution)/shard_map/pallas_call | solution.py:46
  14.1 2.3 %fusion.6 = (bf16[256,256]{1,0:T(8,128)(2,1)}, bf16[256,256]{1,0:T(8,128)(2,1)}, bf16[256,256]{1,0:T(8,128)(2,1)}, bf16[256,256]{1,0:T(8,128)(2,1)}) fusion(bf16[512,512]{1,0:T(8,128)(2,1)} %param.21, s32[]{:T(128)S(6)} %select_n.70, s32[]{:T(128)S(6)} %select_n.71, bf16[512,512]{1,0:T(8,128)(2,1)} %param.20), kind=kLoop, calls=%fused_computation.33 | loop fusion | bytes 1048584 | tf_op jit(solution)/shard_map/dynamic-slice.2
  16.4 1.8 %collective-permute-start.2 = (bf16[256,256]{1,0:T(8,128)(2,1)}, bf16[256,256]{1,0:T(8,128)(2,1)}, u32[]{:S(2)}, u32[]{:S(2)}) collective-permute-start(bf16[256,256]{1,0:T(8,128)(2,1)} %get-tuple-element.55), channel_id=1, source_target_pairs={{12,0},{13,1},{0,4},{1,5},{4,8},{5,9},{8,12},{9,13},{14,2},{15,3},... | collective-permute-start | bytes 393224 | tf_op jit(solution)/shard_map/ppermute | solution.py:21
  18.2 2.6 %collective-permute-start.3 = (bf16[256,256]{1,0:T(8,128)(2,1)}, bf16[256,256]{1,0:T(8,128)(2,1)}, u32[]{:S(2)}, u32[]{:S(2)}) collective-permute-start(bf16[256,256]{1,0:T(8,128)(2,1)} %get-tuple-element.54), channel_id=1, source_target_pairs={{9,0},{12,1},{13,4},{0,5},{1,8},{4,9},{5,12},{8,13},{11,2},{14,3},... | collective-permute-start | bytes 393224 | tf_op jit(solution)/shard_map/ppermute | solution.py:21
  21.9 1.2 %collective-permute-start.5 = (bf16[256,256]{1,0:T(8,128)(2,1)}, bf16[256,256]{1,0:T(8,128)(2,1)}, u32[]{:S(2)}, u32[]{:S(2)}) collective-permute-start(bf16[256,256]{1,0:T(8,128)(2,1)} %get-tuple-element.52), channel_id=1, source_target_pairs={{4,0},{5,1},{8,4},{9,5},{12,8},{13,9},{0,12},{1,13},{6,2},{7,3},{1... | collective-permute-start | bytes 393224 | tf_op jit(solution)/shard_map/ppermute | solution.py:21
  25.9 1.3 %copy.32 = bf16[512,512]{0,1:T(8,128)(2,1)S(1)} copy(bf16[512,512]{1,0:T(8,128)(2,1)} %param.27) | data formatting | bytes 1048576 | tf_op args[13]
  27.2 1.1 copy.41
  28.3 1.6 %copy.43 = bf16[256,256]{0,1:T(8,128)(2,1)} copy(bf16[256,256]{1,0:T(8,128)(2,1)} %get-tuple-element.67) | data formatting | bytes 262144
  29.9 1.7 %copy.42 = bf16[256,256]{0,1:T(8,128)(2,1)} copy(bf16[256,256]{1,0:T(8,128)(2,1)} %get-tuple-element.68) | data formatting | bytes 262144
  31.6 1.7 %copy.45 = bf16[256,256]{0,1:T(8,128)(2,1)} copy(bf16[256,256]{1,0:T(8,128)(2,1)} %get-tuple-element.58) | data formatting | bytes 262144
  33.3 1.7 %copy.44 = bf16[256,256]{0,1:T(8,128)(2,1)} copy(bf16[256,256]{1,0:T(8,128)(2,1)} %get-tuple-element.57) | data formatting | bytes 262144
  36.0 1.6 %collective-permute-start.8 = (bf16[256,512]{1,0:T(8,128)(2,1)S(1)}, bf16[256,512]{1,0:T(8,128)(2,1)S(1)}, u32[]{:S(2)}, u32[]{:S(2)}) collective-permute-start(bf16[256,512]{1,0:T(8,128)(2,1)S(1)} %copy-done.2), channel_id=1, source_target_pairs={{2,0},{0,2},{3,1},{1,3},{6,4},{4,6},{7,5},{5,7},{10,8},{8,10},{11,... | collective-permute-start | bytes 786440 | tf_op jit(solution)/shard_map/ppermute | solution.py:21
  37.6 1.7 %broadcast_in_dim.19.low = bf16[12,512,128]{2,1,0:T(8,128)(2,1)S(1)} broadcast(bf16[12,512]{1,0:T(8,128)(2,1)} %get-tuple-element.64), dimensions={0,1} | broadcast | bytes 1585152 | tf_op jit(solution)/shard_map/broadcast_in_dim | solution.py:305
  39.3 1.7 %broadcast_in_dim.20.high = bf16[12,512,128]{2,1,0:T(8,128)(2,1)S(1)} broadcast(bf16[12,512]{1,0:T(8,128)(2,1)} %get-tuple-element.63), dimensions={0,1} | broadcast | bytes 1585152 | tf_op jit(solution)/shard_map/broadcast_in_dim | solution.py:306
  41.0 11.7 %shard_map.158 = (bf16[512,256]{1,0:T(8,128)(2,1)S(1)}, bf16[12,512,256]{2,1,0:T(8,128)(2,1)S(1)}) custom-call(bf16[12,512,128]{2,1,0:T(8,128)(2,1)S(1)} %broadcast_in_dim.19.low, bf16[12,512,128]{2,1,0:T(8,128)(2,1)S(1)} %broadcast_in_dim.20.high, f32[512,256]{1,0:T(8,128)S(1)} %copy-done.8, f32[512,1]{1,0:T(8,128)S(1)} %copy-done.6, ...), custom_call_target="tpu_custom_call" | custom-call | flops 6442450944 | bytes 4720640 | tf_op jit(solution)/shard_map/pallas_call | solution.py:46
  53.5 1.6 %shard_map.159 = (bf16[512,512]{1,0:T(8,128)(2,1)}, f32[512,512]{1,0:T(8,128)S(1)}, f32[512,512]{1,0:T(8,128)S(1)}) custom-call(s32[14]{0:T(128)S(1)} %pad_add_fusion.info, bf16[256,512]{1,0:T(8,128)(2,1)S(1)} %copy-done.2, bf16[256,512]{1,0:T(8,128)(2,1)S(1)} %collective-permute-done.8.refs_1_, bf16[512,512]{1,0:T(8,128)(2,1)S(1)} %get-tuple-element.31.refs_2_.feats, ...), custom_call_target="tpu_custom_call" | custom-call | flops 536870912 | bytes 2099256 | tf_op jit(solution)/shard_map/pallas_call | solution.py:46
  55.1 6.4 %collective-permute-done.7.refs_1_ = bf16[512,256]{1,0:T(8,128)(2,1)S(1)} collective-permute-done((bf16[512,256]{1,0:T(8,128)(2,1)S(1)}, bf16[512,256]{1,0:T(8,128)(2,1)S(1)}, u32[]{:S(2)}, u32[]{:S(2)}) %collective-permute-start.7) | collective-permute-done | bytes 262176 | tf_op jit(solution)/shard_map/ppermute | solution.py:21
  61.6 1.7 %shard_map.160 = (bf16[512,512]{1,0:T(8,128)(2,1)S(1)}, bf16[512,512]{1,0:T(8,128)(2,1)S(1)}, f32[512,256]{1,0:T(8,128)S(1)}) custom-call(f32[1,512]{1,0:T(1,128)S(1)} %bitcast.38, bf16[512,256]{1,0:T(8,128)(2,1)S(1)} %get-tuple-element.30.refs_0_, bf16[512,256]{1,0:T(8,128)(2,1)S(1)} %collective-permute-done.7.refs_1_, ...), custom_call_target="tpu_custom_call" | custom-call | flops 805306368 | bytes 4458496 | tf_op jit(solution)/shard_map/pallas_call | solution.py:46
  63.4 7.8 %shard_map.162 = (bf16[256,256]{1,0:T(8,128)(2,1)S(1)}, bf16[256,256]{1,0:T(8,128)(2,1)S(1)}, bf16[256,256]{1,0:T(8,128)(2,1)S(1)}, bf16[256,256]{1,0:T(8,128)(2...) custom-call(bf16[12,16,512]{2,1,0:T(8,128)(2,1)S(1)} %broadcast_in_d, ...), custom_call_target="tpu_custom_call" | custom-call | flops 4831838208 | bytes 4063232 | tf_op jit(solution)/shard_map/pallas_call | solution.py:46
  73.8 1.5 %collective-permute-start.12 = (bf16[256,256]{1,0:T(8,128)(2,1)S(1)}, bf16[256,256]{1,0:T(8,128)(2,1)S(1)}, u32[]{:S(2)}, u32[]{:S(2)}) collective-permute-start(bf16[256,256]{1,0:T(8,128)(2,1)S(1)} %get-tuple-element.45), channel_id=1, source_target_pairs={{13,0},{0,1},{1,4},{4,5},{5,8},{8,9},{9,12},{12,13},{15,2},{2,3},{... | collective-permute-start | bytes 393224 | tf_op jit(solution)/shard_map/ppermute | solution.py:21
  75.3 1.5 %shard_map.161 = (bf16[256,512]{1,0:T(8,128)(2,1)}, f32[256,512]{1,0:T(8,128)S(1)}) custom-call(s32[14]{0:T(128)S(1)} %pad_add_fusion.info, bf16[256,512]{1,0:T(8,128)(2,1)S(1)} %copy-done.5, bf16[256,512]{1,0:T(8,128)(2,1)S(1)} %copy-done.2, bf16[512,512]{1,0:T(8,128)(2,1)S(1)} %get-tuple-element.34.hidden, ...), custom_call_target="tpu_custom_call" | custom-call | flops 268435456 | bytes 2097208 | tf_op jit(solution)/shard_map/pallas_call | solution.py:46
  76.9 1.4 %collective-permute-start.14 = (bf16[256,256]{1,0:T(8,128)(2,1)S(1)}, bf16[256,256]{1,0:T(8,128)(2,1)S(1)}, u32[]{:S(2)}, u32[]{:S(2)}) collective-permute-start(bf16[256,256]{1,0:T(8,128)(2,1)S(1)} %get-tuple-element.47), channel_id=1, source_target_pairs={{9,0},{12,1},{13,4},{0,5},{1,8},{4,9},{5,12},{8,13},{11,2},{14,3},... | collective-permute-start | bytes 393224 | tf_op jit(solution)/shard_map/ppermute | solution.py:21
  78.3 3.7 %shard_map.163.own = f32[512,256]{1,0:T(8,128)S(1)} custom-call(bf16[12,16,512]{2,1,0:T(8,128)(2,1)S(1)} %broadcast_in_dim.24.low, bf16[12,16,512]{2,1,0:T(8,128)(2,1)S(1)} %broadcast_in_dim.48.high, bf16[12,512,256]{2,1,0:T(8,128)(2,1)S(1)} %get-tuple-element.39.grads), custom_call_target="tpu_custom_call" | custom-call | flops 1610612736 | bytes 3538944 | tf_op jit(solution)/shard_map/pallas_call | solution.py:46
  82.0 1.7 %collective-permute-done.12.refs_3_ = bf16[256,256]{1,0:T(8,128)(2,1)S(1)} collective-permute-done((bf16[256,256]{1,0:T(8,128)(2,1)S(1)}, bf16[256,256]{1,0:T(8,128)(2,1)S(1)}, u32[]{:S(2)}, u32[]{:S(2)}) %collective-permute-start.12) | collective-permute-done | bytes 131104 | tf_op jit(solution)/shard_map/ppermute | solution.py:21
  83.7 1.6 %collective-permute-done.13.refs_4_ = bf16[256,256]{1,0:T(8,128)(2,1)S(1)} collective-permute-done((bf16[256,256]{1,0:T(8,128)(2,1)S(1)}, bf16[256,256]{1,0:T(8,128)(2,1)S(1)}, u32[]{:S(2)}, u32[]{:S(2)}) %collective-permute-start.13) | collective-permute-done | bytes 131104 | tf_op jit(solution)/shard_map/ppermute | solution.py:21
  85.3 6.6 %collective-permute-done.14.refs_5_ = bf16[256,256]{1,0:T(8,128)(2,1)S(1)} collective-permute-done((bf16[256,256]{1,0:T(8,128)(2,1)S(1)}, bf16[256,256]{1,0:T(8,128)(2,1)S(1)}, u32[]{:S(2)}, u32[]{:S(2)}) %collective-permute-start.14) | collective-permute-done | bytes 131104 | tf_op jit(solution)/shard_map/ppermute | solution.py:21
  91.8 1.3 %shard_map.164 = (f32[256,512]{1,0:T(8,128)S(1)}, bf16[1,256,512]{2,1,0:T(8,128)(2,1)S(1)}, bf16[256,512]{1,0:T(8,128)(2,1)S(1)}) custom-call(s32[14]{0:T(128)S(1)} %pad_add_fusion.info, f32[512,256]{1,0:T(8,128)S(1)} %shard_map.163.own, bf16[512,256]{1,0:T(8,128)(2,1)S(1)} %get-tuple-element.40.recv, f32[256,512]{1,0:T(8,128)S(1)} %get-tuple-element.41.direct, ...), custom_call_target="tpu_custom_call" | custom-call | flops 402653184 | bytes 3145784 | tf_op jit(solution)/shard_map/pallas_call | solution.py:46
  94.3 4.8 %all-to-all-start = ((bf16[8,256,64]{1,2,0:T(8,128)(2,1)}), bf16[8,256,64]{1,2,0:T(8,128)(2,1)S(1)}, u32[]{:S(2)}, u32[]{:S(2)}) async-start(bf16[8,256,64]{1,2,0:T(8,128)(2,1)} %bitcast.24), calls=%async_computation | async-start | bytes 524288 | tf_op jit(solution)/shard_map/all_to_all | solution.py:404
  99.0 2.5 %collective-permute-done.15 = bf16[256,512]{1,0:T(8,128)(2,1)S(1)} collective-permute-done((bf16[256,512]{1,0:T(8,128)(2,1)S(1)}, bf16[256,512]{1,0:T(8,128)(2,1)S(1)}, u32[]{:S(2)}, u32[]{:S(2)}) %collective-permute-start.15) | collective-permute-done | bytes 262176 | tf_op jit(solution)/shard_map/ppermute | solution.py:21
  102.4 6.4 %all-to-all-done = bf16[8,256,64]{1,2,0:T(8,128)(2,1)S(1)} async-done(((bf16[8,256,64]{1,2,0:T(8,128)(2,1)}), bf16[8,256,64]{1,2,0:T(8,128)(2,1)S(1)}, u32[]{:S(2)}, u32[]{:S(2)}) %all-to-all-start) | async-done | bytes 262176 | tf_op jit(solution)/shard_map/all_to_all | solution.py:404
  (88 shorter events, 18.0 us)
Async XLA Ops:
  0.6 12.7 %copy-start.14 = (bf16[512,512]{1,0:T(8,128)(2,1)S(1)}, bf16[512,512]{1,0:T(8,128)(2,1)}, u32[]{:S(2)}) copy-start(bf16[512,512]{1,0:T(8,128)(2,1)} %param.23) | copy-start | bytes 1572868
  0.6 22.4 %copy-start.1 = (bf16[512,512]{1,0:T(8,128)(2,1)S(1)}, bf16[512,512]{1,0:T(8,128)(2,1)}, u32[]{:S(2)}) copy-start(bf16[512,512]{1,0:T(8,128)(2,1)} %refs_3_.2) | copy-start | bytes 1572868
  0.7 9.5 %collective-permute-start = (bf16[256,512]{1,0:T(8,128)(2,1)}, bf16[256,512]{1,0:T(8,128)(2,1)S(1)}, u32[]{:S(2)}, u32[]{:S(2)}) collective-permute-start(bf16[256,512]{1,0:T(8,128)(2,1)} %feats.1), channel_id=1, source_target_pairs={{2,0},{0,2},{3,1},{1,3},{6,4},{4,6},{7,5},{5,7},{10,8},{8,10},{11,... | collective-permute-start | bytes 786440 | tf_op jit(solution)/shard_map/ppermute | solution.py:21
  6.9 17.8 %copy-start = (bf16[512,512]{1,0:T(8,128)(2,1)S(1)}, bf16[512,512]{1,0:T(8,128)(2,1)}, u32[]{:S(2)}) copy-start(bf16[512,512]{1,0:T(8,128)(2,1)} %refs_3_.3) | copy-start | bytes 1572868
  12.3 12.7 %copy-start.21 = (f32[512]{0:T(512)S(1)}, f32[512]{0:T(512)}, u32[]{:S(2)}) copy-start(f32[512]{0:T(512)} %param.26) | copy-start | bytes 6148
  13.3 9.8 %collective-permute-start.1 = (bf16[256,256]{1,0:T(8,128)(2,1)S(1)}, bf16[256,256]{1,0:T(8,128)(2,1)S(1)}, u32[]{:S(2)}, u32[]{:S(2)}) collective-permute-start(bf16[256,256]{1,0:T(8,128)(2,1)S(1)} %get-tuple-element.56), channel_id=1, source_target_pairs={{13,0},{0,1},{1,4},{4,5},{5,8},{8,9},{9,12},{12,13},{15,2},{2,3},{... | collective-permute-start | bytes 393224 | tf_op jit(solution)/shard_map/ppermute | solution.py:21
  14.1 11.9 %copy-start.11 = (bf16[512,256]{1,0:T(8,128)(2,1)}, bf16[512,256]{1,0:T(8,128)(2,1)S(1)}, u32[]{:S(2)}) copy-start(bf16[512,256]{1,0:T(8,128)(2,1)S(1)} %get-tuple-element.61) | copy-start | bytes 786436
  16.4 19.6 %copy-start.2 = (bf16[256,512]{1,0:T(8,128)(2,1)S(1)}, bf16[256,512]{1,0:T(8,128)(2,1)}, u32[]{:S(2)}) copy-start(bf16[256,512]{1,0:T(8,128)(2,1)} %cots.1) | copy-start | bytes 786436
  16.4 19.6 %collective-permute-start.2 = (bf16[256,256]{1,0:T(8,128)(2,1)}, bf16[256,256]{1,0:T(8,128)(2,1)}, u32[]{:S(2)}, u32[]{:S(2)}) collective-permute-start(bf16[256,256]{1,0:T(8,128)(2,1)} %get-tuple-element.55), channel_id=1, source_target_pairs={{12,0},{13,1},{0,4},{1,5},{4,8},{5,9},{8,12},{9,13},{14,2},{15,3},... | collective-permute-start | bytes 393224 | tf_op jit(solution)/shard_map/ppermute | solution.py:21
  18.2 19.3 %collective-permute-start.3 = (bf16[256,256]{1,0:T(8,128)(2,1)}, bf16[256,256]{1,0:T(8,128)(2,1)}, u32[]{:S(2)}, u32[]{:S(2)}) collective-permute-start(bf16[256,256]{1,0:T(8,128)(2,1)} %get-tuple-element.54), channel_id=1, source_target_pairs={{9,0},{12,1},{13,4},{0,5},{1,8},{4,9},{5,12},{8,13},{11,2},{14,3},... | collective-permute-start | bytes 393224 | tf_op jit(solution)/shard_map/ppermute | solution.py:21
  20.8 16.7 %collective-permute-start.4 = (bf16[256,256]{1,0:T(8,128)(2,1)}, bf16[256,256]{1,0:T(8,128)(2,1)}, u32[]{:S(2)}, u32[]{:S(2)}) collective-permute-start(bf16[256,256]{1,0:T(8,128)(2,1)} %get-tuple-element.53), channel_id=1, source_target_pairs={{1,0},{4,1},{5,4},{8,5},{9,8},{12,9},{13,12},{0,13},{3,2},{6,3},{7... | collective-permute-start | bytes 393224 | tf_op jit(solution)/shard_map/ppermute | solution.py:21
  21.9 15.7 %collective-permute-start.5 = (bf16[256,256]{1,0:T(8,128)(2,1)}, bf16[256,256]{1,0:T(8,128)(2,1)}, u32[]{:S(2)}, u32[]{:S(2)}) collective-permute-start(bf16[256,256]{1,0:T(8,128)(2,1)} %get-tuple-element.52), channel_id=1, source_target_pairs={{4,0},{5,1},{8,4},{9,5},{12,8},{13,9},{0,12},{1,13},{6,2},{7,3},{1... | collective-permute-start | bytes 393224 | tf_op jit(solution)/shard_map/ppermute | solution.py:21
  23.1 14.5 %collective-permute-start.6 = (bf16[256,256]{1,0:T(8,128)(2,1)}, bf16[256,256]{1,0:T(8,128)(2,1)}, u32[]{:S(2)}, u32[]{:S(2)}) collective-permute-start(bf16[256,256]{1,0:T(8,128)(2,1)} %get-tuple-element.51), channel_id=1, source_target_pairs={{5,0},{8,1},{9,4},{12,5},{13,8},{0,9},{1,12},{4,13},{7,2},{10,3},{... | collective-permute-start | bytes 393224 | tf_op jit(solution)/shard_map/ppermute | solution.py:21
  36.0 17.5 %collective-permute-start.8 = (bf16[256,512]{1,0:T(8,128)(2,1)S(1)}, bf16[256,512]{1,0:T(8,128)(2,1)S(1)}, u32[]{:S(2)}, u32[]{:S(2)}) collective-permute-start(bf16[256,512]{1,0:T(8,128)(2,1)S(1)} %copy-done.2), channel_id=1, source_target_pairs={{2,0},{0,2},{3,1},{1,3},{6,4},{4,6},{7,5},{5,7},{10,8},{8,10},{11,... | collective-permute-start | bytes 786440 | tf_op jit(solution)/shard_map/ppermute | solution.py:21
  41.0 12.4 %copy-start.17 = (bf16[256,256]{0,1:T(8,128)(2,1)S(1)}, bf16[256,256]{0,1:T(8,128)(2,1)}, u32[]{:S(2)}) copy-start(bf16[256,256]{0,1:T(8,128)(2,1)} %copy.43) | copy-start | bytes 393220
  41.0 12.4 %copy-start.18 = (bf16[256,256]{0,1:T(8,128)(2,1)S(1)}, bf16[256,256]{0,1:T(8,128)(2,1)}, u32[]{:S(2)}) copy-start(bf16[256,256]{0,1:T(8,128)(2,1)} %copy.42) | copy-start | bytes 393220
  41.0 12.4 %copy-start.12 = (bf16[512,256]{1,0:T(8,128)(2,1)S(1)}, bf16[512,256]{1,0:T(8,128)(2,1)}, u32[]{:S(2)}) copy-start(bf16[512,256]{1,0:T(8,128)(2,1)} %copy-done.11) | copy-start | bytes 786436
  41.0 12.4 %copy-start.13 = (bf16[1,512,256]{2,1,0:T(8,128)(2,1)S(1)}, bf16[1,512,256]{2,1,0:T(8,128)(2,1)}, u32[]{:S(2)}) copy-start(bf16[1,512,256]{2,1,0:T(8,128)(2,1)} %get-tuple-element.62) | copy-start | bytes 786436
  41.0 12.5 %copy-start.3 = (f32[512,1]{1,0:T(8,128)S(1)}, f32[512,1]{1,0:T(8,128)}, u32[]{:S(2)}) copy-start(f32[512,1]{1,0:T(8,128)} %copy.33.refs_4_) | copy-start | bytes 6148
  52.7 8.8 %collective-permute-start.7 = (bf16[512,256]{1,0:T(8,128)(2,1)S(1)}, bf16[512,256]{1,0:T(8,128)(2,1)S(1)}, u32[]{:S(2)}, u32[]{:S(2)}) collective-permute-start(bf16[512,256]{1,0:T(8,128)(2,1)S(1)} %get-tuple-element.30.refs_0_), channel_id=1, source_target_pairs={{2,0},{0,2},{3,1},{1,3},{6,4},{4,6},{7,5},{5,7},{10,8},{8,10},{11,... | collective-permute-start | bytes 786440 | tf_op jit(solution)/shard_map/ppermute | solution.py:21
  53.5 9.8 %copy-start.20 = (bf16[12,512]{1,0:T(8,128)(2,1)S(1)}, bf16[12,512]{1,0:T(8,128)(2,1)}, u32[]{:S(2)}) copy-start(bf16[12,512]{1,0:T(8,128)(2,1)} %get-tuple-element.64) | copy-start | bytes 36868
  53.5 9.8 %copy-start.19 = (bf16[12,512]{1,0:T(8,128)(2,1)S(1)}, bf16[12,512]{1,0:T(8,128)(2,1)}, u32[]{:S(2)}) copy-start(bf16[12,512]{1,0:T(8,128)(2,1)} %get-tuple-element.63) | copy-start | bytes 36868
  63.4 8.7 %copy-start.15 = (bf16[256,256]{0,1:T(8,128)(2,1)S(1)}, bf16[256,256]{0,1:T(8,128)(2,1)}, u32[]{:S(2)}) copy-start(bf16[256,256]{0,1:T(8,128)(2,1)} %copy.45) | copy-start | bytes 393220
  63.4 11.9 %copy-start.5 = (bf16[256,512]{1,0:T(8,128)(2,1)S(1)}, bf16[256,512]{1,0:T(8,128)(2,1)}, u32[]{:S(2)}) copy-start(bf16[256,512]{1,0:T(8,128)(2,1)} %feats.1) | copy-start | bytes 786436
  71.2 5.6 %collective-permute-start.9 = (bf16[256,256]{1,0:T(8,128)(2,1)S(1)}, bf16[256,256]{1,0:T(8,128)(2,1)S(1)}, u32[]{:S(2)}, u32[]{:S(2)}) collective-permute-start(bf16[256,256]{1,0:T(8,128)(2,1)S(1)} %get-tuple-element.42), channel_id=1, source_target_pairs={{1,0},{4,1},{5,4},{8,5},{9,8},{12,9},{13,12},{0,13},{3,2},{6,3},{7... | collective-permute-start | bytes 393224 | tf_op jit(solution)/shard_map/ppermute | solution.py:21
  72.1 9.9 %collective-permute-start.10 = (bf16[256,256]{1,0:T(8,128)(2,1)S(1)}, bf16[256,256]{1,0:T(8,128)(2,1)S(1)}, u32[]{:S(2)}, u32[]{:S(2)}) collective-permute-start(bf16[256,256]{1,0:T(8,128)(2,1)S(1)} %get-tuple-element.43), channel_id=1, source_target_pairs={{4,0},{5,1},{8,4},{9,5},{12,8},{13,9},{0,12},{1,13},{6,2},{7,3},{1... | collective-permute-start | bytes 393224 | tf_op jit(solution)/shard_map/ppermute | solution.py:21
  73.1 8.9 %collective-permute-start.11 = (bf16[256,256]{1,0:T(8,128)(2,1)S(1)}, bf16[256,256]{1,0:T(8,128)(2,1)S(1)}, u32[]{:S(2)}, u32[]{:S(2)}) collective-permute-start(bf16[256,256]{1,0:T(8,128)(2,1)S(1)} %get-tuple-element.44), channel_id=1, source_target_pairs={{5,0},{8,1},{9,4},{12,5},{13,8},{0,9},{1,12},{4,13},{7,2},{10,3},{... | collective-permute-start | bytes 393224 | tf_op jit(solution)/shard_map/ppermute | solution.py:21
  73.8 9.9 %collective-permute-start.12 = (bf16[256,256]{1,0:T(8,128)(2,1)S(1)}, bf16[256,256]{1,0:T(8,128)(2,1)S(1)}, u32[]{:S(2)}, u32[]{:S(2)}) collective-permute-start(bf16[256,256]{1,0:T(8,128)(2,1)S(1)} %get-tuple-element.45), channel_id=1, source_target_pairs={{13,0},{0,1},{1,4},{4,5},{5,8},{8,9},{9,12},{12,13},{15,2},{2,3},{... | collective-permute-start | bytes 393224 | tf_op jit(solution)/shard_map/ppermute | solution.py:21
  75.3 10.0 %collective-permute-start.13 = (bf16[256,256]{1,0:T(8,128)(2,1)S(1)}, bf16[256,256]{1,0:T(8,128)(2,1)S(1)}, u32[]{:S(2)}, u32[]{:S(2)}) collective-permute-start(bf16[256,256]{1,0:T(8,128)(2,1)S(1)} %get-tuple-element.46), channel_id=1, source_target_pairs={{12,0},{13,1},{0,4},{1,5},{4,8},{5,9},{8,12},{9,13},{14,2},{15,3},... | collective-permute-start | bytes 393224 | tf_op jit(solution)/shard_map/ppermute | solution.py:21
  76.9 15.0 %collective-permute-start.14 = (bf16[256,256]{1,0:T(8,128)(2,1)S(1)}, bf16[256,256]{1,0:T(8,128)(2,1)S(1)}, u32[]{:S(2)}, u32[]{:S(2)}) collective-permute-start(bf16[256,256]{1,0:T(8,128)(2,1)S(1)} %get-tuple-element.47), channel_id=1, source_target_pairs={{9,0},{12,1},{13,4},{0,5},{1,8},{4,9},{5,12},{8,13},{11,2},{14,3},... | collective-permute-start | bytes 393224 | tf_op jit(solution)/shard_map/ppermute | solution.py:21
  93.2 8.4 %collective-permute-start.15 = (bf16[256,512]{1,0:T(8,128)(2,1)S(1)}, bf16[256,512]{1,0:T(8,128)(2,1)S(1)}, u32[]{:S(2)}, u32[]{:S(2)}) collective-permute-start(bf16[256,512]{1,0:T(8,128)(2,1)S(1)} %bitcast.39), channel_id=1, source_target_pairs={{2,0},{0,2},{3,1},{1,3},{6,4},{4,6},{7,5},{5,7},{10,8},{8,10},{11,... | collective-permute-start | bytes 786440 | tf_op jit(solution)/shard_map/ppermute | solution.py:21
  94.3 14.5 %all-to-all-start = ((bf16[8,256,64]{1,2,0:T(8,128)(2,1)}), bf16[8,256,64]{1,2,0:T(8,128)(2,1)S(1)}, u32[]{:S(2)}, u32[]{:S(2)}) async-start(bf16[8,256,64]{1,2,0:T(8,128)(2,1)} %bitcast.24), calls=%async_computation | async-start | bytes 524288 | tf_op jit(solution)/shard_map/all_to_all | solution.py:404
  (7 other events, 30.6 us)

commit v2 on v1

v2 whole, which is shorter than its diff:
```python
import functools
import math

import jax
import jax.numpy as jnp
from jax import lax
from jax.experimental import pallas as pl
from jax.experimental.pallas import tpu as pltpu
from jax.sharding import PartitionSpec as P

TILE = 128
CHUNK = 256
LANES = 128
PACK = 16
MIB = 1 << 20
NO_CHUNK = 64
CH, TILES, SUB, FIRST, LON, PLACES, PICKS = 0, 1, 2, 3, 4, 5, 11


def shifted(block, axis, distance):
    size = lax.axis_size(axis)
    route = [((i - distance) % size, i) for i in range(size)]
    return lax.ppermute(block, axis, route)


def gathered(block, axis):
    return [block] + [shifted(block, axis, k) for k in range(1, lax.axis_size(axis))]


def dot(left, right):
    return jnp.dot(left, right, preferred_element_type=jnp.float32)


def dot_nt(left, right):
    return lax.dot_general(
        left, right, (((1,), (1,)), ((), ())), preferred_element_type=jnp.float32
    )


def sigmoid(value):
    return 0.5 * jnp.tanh(0.5 * value) + 0.5


def call(kernel, out_shape, operands, flops, scratch=(), scalars=1, limit=32):
    vmem = pl.BlockSpec(memory_space=pltpu.VMEM)
    smem = pl.BlockSpec(memory_space=pltpu.SMEM)
    moved = sum(math.prod(x.shape) * x.dtype.itemsize for x in operands)
    return pl.pallas_call(
        kernel,
        out_shape=out_shape,
        in_specs=[smem] * scalars + [vmem] * (len(operands) - scalars),
        out_specs=jax.tree.map(lambda _: vmem, out_shape),
        scratch_shapes=scratch,
        compiler_params=pltpu.CompilerParams(vmem_limit_bytes=limit * MIB),
        cost_estimate=pl.CostEstimate(flops=flops, bytes_accessed=moved, transcendentals=0),
    )(*operands)


def assemble(whole_ref, blocks, first):
    count = len(blocks)
    rows = blocks[0].shape[0]
    for k, block in enumerate(blocks):
        place = lax.rem(first - k + count, count) * rows
        whole_ref[pl.ds(pl.multiple_of(place, rows), rows), :] = block[...]


def mine_of(ref, index, rows):
    return ref[pl.ds(pl.multiple_of(index * rows, rows), rows), :]


def weights_kernel(
    info,
    senders,
    in_degree,
    w_send,
    w_recv,
    w_msg,
    w_node_v,
    w_node_a,
    w_out,
    w_send_t,
    w_recv_t,
    w_msg_t,
    w_node_v_t,
    w_node_a_t,
    w_out_t,
    low_cols,
    high_cols,
    low_rows,
    high_rows,
    turned,
):
    mine, tiles = info[CH], info[TILES]
    hid = w_send_t.shape[1]
    w_send_t[...] = mine_of(w_send, mine, hid).T
    w_recv_t[...] = mine_of(w_recv, mine, hid).T
    w_out_t[...] = w_out[...].T
    w_node_a_t[...] = w_node_a[...].T
    turned[...] = w_msg[...].T
    w_msg_t[...] = mine_of(turned, mine, hid)
    turned[...] = w_node_v[...].T
    w_node_v_t[...] = mine_of(turned, mine, w_node_v_t.shape[0])

    degree, nodes = senders.shape
    lane = lax.broadcasted_iota(jnp.int32, (degree, nodes), 1)
    row = lax.broadcasted_iota(jnp.int32, (degree, nodes), 0)
    valid = (row < in_degree[...]) & (lane < tiles * TILE)
    ids = senders[...]
    low = (ids & (CHUNK - 1)).astype(jnp.float32)
    high = jnp.where(valid, ids // CHUNK, NO_CHUNK).astype(jnp.float32)
    for m in range(degree):
        shape = (PACK, nodes)
        low_rows[m] = jnp.broadcast_to(low[m : m + 1], shape).astype(jnp.bfloat16)
        high_rows[m] = jnp.broadcast_to(high[m : m + 1], shape).astype(jnp.bfloat16)
    fill = jnp.zeros((PACK - degree, nodes), jnp.float32)
    depth = 2 * PACK
    both = jnp.concatenate([low, fill, high, fill], axis=0).T.astype(jnp.bfloat16)
    width = degree * LANES
    spot = lax.broadcasted_iota(jnp.int32, (depth, width), 0)
    group = lax.broadcasted_iota(jnp.int32, (depth, width), 1) // LANES
    for first, out in ((0, low_cols), (PACK, high_cols)):
        pick = (spot == group + first).astype(jnp.bfloat16)
        spread = dot(both, pick).astype(jnp.bfloat16)
        for m in range(degree):
            out[m] = spread[:, m * LANES : (m + 1) * LANES]


def project_kernel(count, info, bias, *refs):
    blocks = refs[:count]
    w_send, w_recv, feats, proj, base, upper, lower, cross, beside = refs[count:]
    mine, sub, first = info[CH], info[SUB], info[FIRST]
    assemble(feats, blocks, mine)
    whole = feats[...]
    hid = proj.shape[1]
    proj[...] = dot(mine_of(w_send, mine, hid), whole).T.astype(jnp.bfloat16)
    my_bias = jnp.zeros((1, hid), jnp.float32)
    for k in range(count):
        my_bias += jnp.where(mine == k, bias[:, k * hid : (k + 1) * hid], 0.0)
    recv = dot(mine_of(w_recv, mine, hid), whole).T
    base[...] = recv.astype(jnp.bfloat16).astype(jnp.float32) + my_bias
    rows = upper.shape[0] - PACK
    upper[:rows, :] = proj[pl.ds(pl.multiple_of(first * TILE, TILE), rows), :]
    lower[:rows, :] = proj[:rows, :]
    spot = lax.broadcasted_iota(jnp.int32, (PACK, hid), 0)
    half = info.shape[0] - PICKS
    half = half // 2
    for start, out in ((0, upper), (half, lower)):
        marks = jnp.zeros((PACK, hid), jnp.float32)
        for k in range(half):
            rel = info[PICKS + start + k]
            marks = jnp.where(spot == k, rel.astype(jnp.float32), marks)
        out[rows:, :] = marks.astype(jnp.bfloat16)

    @pl.when(sub == 0)
    def _():
        cross[...] = lower[...]
        beside[...] = upper[...]

    @pl.when(sub != 0)
    def _():
        cross[...] = upper[...]
        beside[...] = lower[...]


def prepare_kernel(count, info, *refs):
    blocks = refs[:count]
    feats, w_node_v, bias, w_out_t, cots, pre, grad_hidden = refs[count:]
    assemble(cots, blocks, info[CH])
    column = jnp.broadcast_to(bias[...], (8, bias.shape[1])).T[:, :1]
    pre[...] = dot(w_node_v[...], feats[...]) + column
    lane = lax.broadcasted_iota(jnp.int32, (1, cots.shape[1]), 1)
    active = (lane < info[TILES] * TILE).astype(jnp.bfloat16)
    grad_hidden[...] = dot(w_out_t[...], cots[...] * active)


def forward_kernel(info, low, high, base, in_degree, proj, *refs):
    arrivals = refs[:6]
    message, slope, rels, ext, total, held = refs[6:]
    own = proj.shape[0]
    rows = held.shape[1] - PACK
    per_slot = rows // TILE
    slots = len(arrivals)
    ext[:own, :] = proj[...]
    for place, block in enumerate(arrivals):
        held[place] = block[...]
    rels[...] = jnp.zeros_like(rels)
    for slot in range(slots):
        place = info[PLACES + slot]
        group = slot % (slots // 2)
        for t in range(per_slot):
            index = group * per_slot + t
            rel = held[place, rows : rows + PACK, :][index : index + 1, :].astype(jnp.float32)
            number = slot * per_slot + t
            rels[number : number + 1, :] = rel
            start = own + number * TILE
            ext[start : start + TILE, :] = jnp.where(
                rel > 0.5, held[place, TILE : 2 * TILE, :], held[place, :TILE, :]
            )
    chunks = ext.shape[0] // CHUNK
    halves = CHUNK // LANES
    total[...] = jnp.zeros_like(total)
    lane = lax.broadcasted_iota(jnp.int32, (own, LANES), 1)

    def step(m, carry):
        low_m, high_m = low[m], high[m]
        one = jnp.bfloat16(1.0)
        zero = jnp.bfloat16(0.0)
        marks = [
            jnp.where(low_m == (lane + half * LANES).astype(jnp.bfloat16), one, zero)
            for half in range(halves)
        ]
        picker = jnp.concatenate(
            [
                jnp.where(high_m == jnp.bfloat16(chunk), mark, zero)
                for chunk in range(chunks)
                for mark in marks
            ],
            axis=1,
        )
        pre = dot(picker, ext[...]) + base[...]
        valid = high_m[:, :1].astype(jnp.float32) < chunks
        sig = sigmoid(pre)
        act = pre * sig
        total[...] += jnp.where(valid, act, 0.0)
        slope[m] = jnp.where(valid, sig + act * (1.0 - sig), 0.0).astype(jnp.bfloat16)
        return carry

    lax.fori_loop(0, low.shape[0], step, 0)
    degree = in_degree[...].astype(jnp.float32)
    message[...] = (total[...].T / degree).astype(jnp.bfloat16)


def node_kernel(count, info, in_degree, *refs):
    blocks = refs[:count]
    w_msg, w_node_a, w_node_a_t, w_msg_t, pre, grad_hidden = refs[count : count + 6]
    hidden, grad_pre, scale, messages = refs[count + 6 :]
    assemble(messages, blocks, info[CH])
    agg = dot(w_msg[...], messages[...])
    node_pre = pre[...] + dot(w_node_a[...], agg.astype(jnp.bfloat16))
    sig = sigmoid(node_pre)
    act = node_pre * sig
    hidden[...] = act.astype(jnp.bfloat16)
    low_grad = (grad_hidden[...] * (sig + act * (1.0 - sig))).astype(jnp.bfloat16)
    grad_pre[...] = low_grad
    grad_agg = dot(w_node_a_t[...], low_grad).astype(jnp.bfloat16)
    grad_msg = dot(w_msg_t[...], grad_agg).astype(jnp.bfloat16).astype(jnp.float32)
    scale[...] = (grad_msg / in_degree[...].astype(jnp.float32)).T


def far_kernel(info, low, high, slope, scale, rels, *refs):
    to_west, to_east, to_cross, to_beside, grads, recv, total, recv_total, held = refs
    slots = held.shape[0]
    rows = held.shape[1]
    per_slot = rows // TILE
    nodes = scale.shape[0]
    first = nodes // CHUNK
    chunks = slots * rows // CHUNK
    total[...] = jnp.zeros_like(total)
    recv_total[...] = jnp.zeros_like(recv_total)
    groups = CHUNK // PACK
    place = lax.broadcasted_iota(jnp.int32, (groups, PACK, nodes), 0) * PACK
    place = place + lax.broadcasted_iota(jnp.int32, (groups, PACK, nodes), 1)

    def step(m, carry):
        grad = slope[m].astype(jnp.float32) * scale[...]
        recv_total[...] += grad
        grad_low = grad.astype(jnp.bfloat16)
        grads[m] = grad_low
        one = jnp.bfloat16(1.0)
        zero = jnp.bfloat16(0.0)
        mark = jnp.where(low[m][None] == place.astype(jnp.bfloat16), one, zero)
        picker = jnp.concatenate(
            [
                jnp.where(high[m][None] == jnp.bfloat16(first + chunk), mark, zero)
                for chunk in range(chunks)
            ],
            axis=0,
        ).reshape(chunks * CHUNK, nodes)
        total[...] += dot(picker, grad_low)
        return carry

    lax.fori_loop(0, slope.shape[0], step, 0)
    for slot in range(slots):
        spot = info[PLACES + slot]
        for half in range(per_slot):
            terms = jnp.zeros((TILE, scale.shape[1]), jnp.float32)
            for t in range(per_slot):
                number = slot * per_slot + t
                hit = jnp.abs(rels[number : number + 1, :] - half) < 0.5
                tile = total[number * TILE : (number + 1) * TILE, :]
                terms += jnp.where(hit, tile, 0.0)
            held[spot, half * TILE : (half + 1) * TILE, :] = terms.astype(jnp.bfloat16)
    to_west[...] = held[1]
    to_east[...] = held[2]
    to_cross[...] = held[3]
    to_beside[0] = held[0]
    to_beside[1] = held[4]
    to_beside[2] = held[5]
    recv[...] = recv_total[...].astype(jnp.bfloat16)


def own_kernel(low, high, grads, total):
    nodes = total.shape[0]
    chunks = nodes // CHUNK
    groups = CHUNK // PACK
    total[...] = jnp.zeros_like(total)
    place = lax.broadcasted_iota(jnp.int32, (groups, PACK, nodes), 0) * PACK
    place = place + lax.broadcasted_iota(jnp.int32, (groups, PACK, nodes), 1)

    def step(m, carry):
        one = jnp.bfloat16(1.0)
        zero = jnp.bfloat16(0.0)
        mark = jnp.where(low[m][None] == place.astype(jnp.bfloat16), one, zero)
        picker = jnp.concatenate(
            [
                jnp.where(high[m][None] == jnp.bfloat16(chunk), mark, zero)
                for chunk in range(chunks)
            ],
            axis=0,
        ).reshape(chunks * CHUNK, nodes)
        total[...] += dot(picker, grads[m])
        return carry

    lax.fori_loop(0, grads.shape[0], step, 0)


def output_kernel(info, feats, cots, hidden, grad_pre, w_out, w_node_v_t, updated, direct):
    chans = feats.shape[0]
    lane = lax.broadcasted_iota(jnp.int32, (1, feats.shape[1]), 1)
    active = (lane < info[TILES] * TILE).astype(jnp.float32)
    node_out = dot(mine_of(w_out, info[CH], chans), hidden[...])
    updated[...] = (feats[...].astype(jnp.float32) + active * node_out).astype(jnp.bfloat16)
    direct[...] = cots[...].astype(jnp.float32) + dot(w_node_v_t[...], grad_pre[...])


def add_kernel(left, more, right, west, east):
    west[...] = (left[...].astype(jnp.float32) + more[1].astype(jnp.float32)).astype(jnp.bfloat16)
    east[...] = (right[...].astype(jnp.float32) + more[2].astype(jnp.float32)).astype(jnp.bfloat16)


def final_kernel(
    inv_root,
    info,
    own,
    recv,
    direct,
    feats,
    w_send_t,
    w_recv_t,
    upper,
    lower,
    across,
    beside,
    kept,
    sent,
    w_mine,
    w_beside,
    total,
    terms,
):
    rows = upper.shape[0]
    mine, sub, lon = info[CH], info[SUB], info[LON]
    start = info[FIRST] * TILE
    total[...] = own[...]

    def put(offset, block):
        spot = pl.ds(pl.multiple_of(offset, TILE), rows)
        total[spot, :] += block.astype(jnp.float32)

    put(start, upper[...])
    put(0, lower[...])
    put(jnp.where(sub == 0, 0, start), across[...])
    put(jnp.where(sub == 0, start, 0), beside[0])
    grad_send = total[...].astype(jnp.bfloat16)
    grad_send_t = total[...].T.astype(jnp.bfloat16)
    grad_recv_t = recv[...].astype(jnp.float32).T.astype(jnp.bfloat16)
    chans = direct.shape[0]
    terms[...] = dot(w_send_t[...], grad_send_t) + dot(w_recv_t[...], grad_recv_t)
    kept[...] = direct[...] + mine_of(terms, mine, chans)
    count = sent.shape[0] + 1
    for k in range(1, count):
        sent[k - 1] = mine_of(terms, lax.rem(mine + k, count), chans).astype(jnp.bfloat16)
    weight = dot(feats[...], grad_send) * inv_root
    terms[:, : weight.shape[1]] = weight
    lons, columns, hid = w_mine.shape
    for k in range(lons):
        band = lax.rem(lon + k, lons) * 2
        for out, core in ((w_mine, sub), (w_beside, 1 - sub)):
            spot = pl.multiple_of((band + core) * columns, columns)
            out[k] = terms[pl.ds(spot, columns), :hid].astype(out.dtype)


def sum_kernel(w_mine, w_beside, near, sent):
    near[...] = w_mine[0] + w_beside[0].astype(jnp.float32)
    for k in range(sent.shape[0]):
        sent[k] = (w_mine[k + 1] + w_beside[k + 1].astype(jnp.float32)).astype(jnp.bfloat16)


def weight_kernel(near, *refs):
    out = refs[-1]
    total = near[...]
    for ref in refs[:-1]:
        total += ref[...].astype(jnp.float32)
    out[...] = total.T


def shards(
    features,
    cotangent,
    senders,
    in_degree,
    tile_count,
    send_tiles,
    w_send,
    w_recv,
    bias_edge,
    w_msg,
    w_node_v,
    w_node_a,
    bias_node,
    w_out,
):
    chans, nodes = features.shape
    count = lax.axis_size("ch")
    mine = lax.axis_index("ch")
    sub = lax.axis_index("sub")
    lons = lax.axis_size("lon")
    hidden_all, chans_all = w_send.shape
    hid = hidden_all // count
    cycle = ("lon", "sub")
    shard_count = lax.axis_size(cycle)
    total_nodes = nodes * shard_count
    degree = senders.shape[0]
    slots = send_tiles.shape[1]
    slot_rows = send_tiles.shape[2] * TILE
    ext_len = nodes + slots * slot_rows
    bf16, f32 = jnp.bfloat16, jnp.float32
    shape = jax.ShapeDtypeStruct

    first_tile = tile_count[0] // 2
    places = jnp.where(sub == 0, jnp.array([4, 1, 3, 0, 2, 5]), jnp.array([0, 1, 4, 5, 2, 3]))
    lift = jnp.where(jnp.arange(slots) < slots // 2, first_tile, 0)[:, None]
    scalars = jnp.stack([mine, tile_count[0], sub, first_tile, lax.axis_index("lon")])
    info = jnp.concatenate([scalars, places, (send_tiles[0] - lift).reshape(-1)]).astype(jnp.int32)
    across_route = [(i, (i + (3 if i % 2 else -3)) % shard_count) for i in range(shard_count)]
    across = lambda block: lax.ppermute(block, cycle, across_route)
    degrees = in_degree[None, :]

    feat_blocks = gathered(features, "ch")
    cot_blocks = gathered(cotangent, "ch")

    (
        w_send_t,
        w_recv_t,
        w_msg_t,
        w_node_v_t,
        w_node_a_t,
        w_out_t,
        low_cols,
        high_cols,
        low_rows,
        high_rows,
    ) = call(
        weights_kernel,
        (
            shape((chans_all, hid), bf16),
            shape((chans_all, hid), bf16),
            shape((hid, chans_all), bf16),
            shape((chans, hidden_all), bf16),
            shape((chans_all, hidden_all), bf16),
            shape((hidden_all, chans_all), bf16),
            shape((degree, nodes, LANES), bf16),
            shape((degree, nodes, LANES), bf16),
            shape((degree, PACK, nodes), bf16),
            shape((degree, PACK, nodes), bf16),
        ),
        [info, senders, degrees, w_send, w_recv, w_msg, w_node_v, w_node_a, w_out],
        flops=4 * hidden_all * chans_all * nodes,
        scratch=[pltpu.VMEM((chans_all, hidden_all), bf16)],
    )

    block = shape((slot_rows + PACK, hid), bf16)
    feats, proj, base, upper, lower, cross, beside = call(
        functools.partial(project_kernel, count),
        (
            shape((chans_all, nodes), bf16),
            shape((nodes, hid), bf16),
            shape((nodes, hid), f32),
            block,
            block,
            block,
            block,
        ),
        [info, bias_edge[None, :]] + feat_blocks + [w_send, w_recv],
        flops=4 * hid * chans_all * nodes,
    )
    west = shifted(upper, "lon", 1)
    east = shifted(lower, "lon", -1)
    beside = shifted(beside, "sub", 1)
    cross = across(cross)
    west_too = shifted(west, "sub", 1)
    east_too = shifted(east, "sub", 1)
    arrivals = [beside, west, east, cross, west_too, east_too]

    cots, pre, grad_hidden = call(
        functools.partial(prepare_kernel, count),
        (
            shape((chans_all, nodes), bf16),
            shape((hidden_all, nodes), f32),
            shape((hidden_all, nodes), f32),
        ),
        [info] + cot_blocks + [feats, w_node_v, bias_node[None, :], w_out_t],
        flops=4 * hidden_all * chans_all * nodes,
    )

    message, slope, rels = call(
        forward_kernel,
        (
            shape((hid, nodes), bf16),
            shape((degree, nodes, hid), bf16),
            shape((PACK, hid), f32),
        ),
        [info, low_cols, high_cols, base, degrees, proj] + arrivals,
        flops=2 * degree * nodes * ext_len * hid,
        scratch=[
            pltpu.VMEM((ext_len, hid), bf16),
            pltpu.VMEM((nodes, hid), f32),
            pltpu.VMEM((slots, slot_rows + PACK, hid), bf16),
        ],
    )
    messages = gathered(message, "ch")

    hidden, grad_pre, scale = call(
        functools.partial(node_kernel, count),
        (
            shape((hidden_all, nodes), bf16),
            shape((hidden_all, nodes), bf16),
            shape((nodes, hid), f32),
        ),
        [info, degrees] + messages + [w_msg, w_node_a, w_node_a_t, w_msg_t, pre, grad_hidden],
        flops=6 * hidden_all * chans_all * nodes,
        scratch=[pltpu.VMEM((hidden_all, nodes), bf16)],
    )

    block = shape((slot_rows, hid), bf16)
    to_west, to_east, to_cross, to_beside, grads, grad_recv = call(
        far_kernel,
        (
            block,
            block,
            block,
            shape((3, slot_rows, hid), bf16),
            shape((degree, nodes, hid), bf16),
            shape((nodes, hid), bf16),
        ),
        [info, low_rows, high_rows, slope, scale, rels],
        flops=2 * degree * nodes * (ext_len - nodes) * hid,
        scratch=[
            pltpu.VMEM((ext_len - nodes, hid), f32),
            pltpu.VMEM((nodes, hid), f32),
            pltpu.VMEM((slots, slot_rows, hid), bf16),
        ],
    )
    from_beside = shifted(to_beside, "sub", 1)
    from_cross = across(to_cross)
    to_west, to_east = call(
        add_kernel, (block, block), [to_west, from_beside, to_east], flops=0, scalars=0
    )
    from_upper = shifted(to_west, "lon", -1)
    from_lower = shifted(to_east, "lon", 1)

    own = call(
        own_kernel,
        shape((nodes, hid), f32),
        [low_rows, high_rows, grads],
        flops=2 * degree * nodes * nodes * hid,
        scalars=0,
    )
    updated, direct = call(
        output_kernel,
        (shape((chans, nodes), bf16), shape((chans, nodes), f32)),
        [info, features, cotangent, hidden, grad_pre, w_out, w_node_v_t],
        flops=4 * hidden_all * chans * nodes,
    )

    columns = chans_all // shard_count
    kept, sent, w_mine, w_beside = call(
        functools.partial(final_kernel, 1.0 / math.sqrt(total_nodes)),
        (
            shape((chans, nodes), f32),
            shape((count - 1, chans, nodes), bf16),
            shape((lons, columns, hid), f32),
            shape((lons, columns, hid), bf16),
        ),
        [info, own, grad_recv, direct, feats, w_send_t, w_recv_t]
        + [from_upper, from_lower, from_cross, from_beside],
        flops=6 * hid * chans_all * nodes,
        scratch=[pltpu.VMEM((nodes, hid), f32), pltpu.VMEM((chans_all, nodes), f32)],
    )
    w_beside = shifted(w_beside, "sub", 1)
    for k in range(1, count):
        kept = kept + shifted(sent[k - 1], "ch", k).astype(f32)
    grad_features = kept.astype(bf16)

    near, w_sent = call(
        sum_kernel,
        (shape((columns, hid), f32), shape((lons - 1, columns, hid), bf16)),
        [w_mine, w_beside],
        flops=0,
        scalars=0,
    )
    w_terms = [shifted(w_sent[k - 1], "lon", k) for k in range(1, lons)]
    grad_w_send = call(
        weight_kernel, shape((hid, columns), f32), [near] + w_terms, flops=0, scalars=0
    )
    return (updated, grad_features, grad_w_send)


def solution(mesh):
    nodes_last = P("ch", ("parts", "lon", "sub"))
    spread = ("parts", "lon", "sub")
    placed = (nodes_last, nodes_last, P(None, spread), P(spread), P(spread), P(spread, None, None))
    return jax.shard_map(
        shards,
        mesh=mesh,
        in_specs=placed + (P(),) * 8,
        out_specs=(nodes_last, nodes_last, P(("parts", "ch"), ("lon", "sub"))),
        check_vma=False,
    )
```

time: 110 us -> 95.4 us (0.87)
  local copies, waits for them, and re-layouts: 25 us -> 13.2 us
  waiting for transfers between devices: 26 us -> 21.4 us
  Pallas kernels: 30.6 us -> 33.7 us
  other arithmetic: 3.71 us -> 1.44 us
    all_to_all x1 -> x0, waiting for transfers between devices: 6.42 us -> none  [shards(): lax.all_to_all(weight_terms, cycle, split_axis=0, concat_axis=0)]
    ppermute x0 -> x2, starting transfers between devices: none -> 6.15 us  [shards(): across = lambda block: lax.ppermute(block, cycle, across_route)]
    broadcast_in_dim x7 -> x0, local copies, waits for them, and re-layouts: 5.25 us -> none  [the longest x1 1.68 us: shards(): low_cols = jnp.broadcast_to(low[:, :, None], (degree, nodes, LANES))]
    all_to_all x1 -> x0, starting transfers between devices: 4.79 us -> none  [shards(): lax.all_to_all(weight_terms, cycle, split_axis=0, concat_axis=0)]
    dynamic_slice x5 -> x0, local copies, waits for them, and re-layouts: 4.43 us -> none  [the longest x1 1.07 us: shards(): lax.dynamic_slice_in_dim(w, (mine + k) % count * hid, hid, 0)]
    pallas_call x8 -> x12, Pallas kernels: 30.6 us -> 33.7 us  [call(): pl.pallas_call(kernel, out_shape=out_shape, in_specs=[smem] * scalars + [...]
    another operation x1 -> x0, local copies, waits for them, and re-layouts: 2.32 us -> none
    ppermute x16, waiting for transfers between devices: 19.6 us -> 21.4 us  [shifted(): return lax.ppermute(block, axis, route)]
  transfers between devices with their start and end apart: 17 -> 18, of which waited for: 7 -> 9; matrix products, arithmetic and copies ran while one was open for 24% -> 3% of each run, Pallas kernels for 17% -> 21%
where the time goes in v2:
time: 95.4 us; the launch traced here: 94.8 us
  Pallas kernels  33.7 us (35%)
  starting transfers between devices  23.4 us (25%)
  waiting for transfers between devices  21.4 us (22%)
  local copies, waits for them, and re-layouts  13.2 us (14%)
  between operations  1.54 us (2%)
  other arithmetic  1.44 us (2%)
    pallas_call x12, Pallas kernels, call(): pl.pallas_call(kernel, out_shape=out_shape, in_specs=[smem] * scalars + [...  33.7 us
    ppermute x16, waiting for transfers between devices, shifted(): return lax.ppermute(block, axis, route)  21.4 us
    ppermute x16, starting transfers between devices, shifted(): return lax.ppermute(block, axis, route)  17.3 us
    unnamed x40, local copies, waits for them, and re-layouts  12.9 us
    ppermute x2, starting transfers between devices, shards(): across = lambda block: lax.ppermute(block, cycle, across_route)  6.15 us
  transfers between devices with their start and end apart: 18, of which 9 were waited for; matrix products, arithmetic and copies ran while one was open for 3% of the time, Pallas kernels for 21%

profile of v2, /device:TPU:0, one launch (start us, length us, event | category | flops | bytes accessed | tf_op | source)
XLA Modules:
  0.0 94.8 jit_solution(15876437591519935727)
XLA Ops:
  0.6 3.0 %collective-permute-start = (bf16[256,512]{1,0:T(8,128)(2,1)}, bf16[256,512]{1,0:T(8,128)(2,1)S(1)}, u32[]{:S(2)}, u32[]{:S(2)}) collective-permute-start(bf16[256,512]{1,0:T(8,128)(2,1)} %feats.1), channel_id=1, source_target_pairs={{2,0},{0,2},{3,1},{1,3},{6,4},{4,6},{7,5},{5,7},{10,8},{8,10},{11,... | collective-permute-start | bytes 786440 | tf_op jit(solution)/shard_map/ppermute | solution.py:23
  6.1 4.1 %collective-permute-done.refs_1_ = bf16[256,512]{1,0:T(8,128)(2,1)S(1)} collective-permute-done((bf16[256,512]{1,0:T(8,128)(2,1)}, bf16[256,512]{1,0:T(8,128)(2,1)S(1)}, u32[]{:S(2)}, u32[]{:S(2)}) %collective-permute-start) | collective-permute-done | bytes 262176 | tf_op jit(solution)/shard_map/ppermute | solution.py:23
  10.2 1.0 %copy-done = bf16[512,512]{1,0:T(8,128)(2,1)S(1)} copy-done((bf16[512,512]{1,0:T(8,128)(2,1)S(1)}, bf16[512,512]{1,0:T(8,128)(2,1)}, u32[]{:S(2)}) %copy-start) | copy-done | bytes 524312
  11.2 1.0 %copy-done.2 = bf16[512,512]{1,0:T(8,128)(2,1)S(1)} copy-done((bf16[512,512]{1,0:T(8,128)(2,1)S(1)}, bf16[512,512]{1,0:T(8,128)(2,1)}, u32[]{:S(2)}) %copy-start.2) | copy-done | bytes 524312
  13.9 1.1 %shard_map.176 = (bf16[512,512]{1,0:T(8,128)(2,1)S(1)}, bf16[512,256]{1,0:T(8,128)(2,1)S(1)}, f32[512,256]{1,0:T(8,128)S(1)}, bf16[272,256]{1,0:T(8,128)(2,1)S(1...) custom-call(s32[23]{0:T(128)S(1)} %concatenate.3.info, ...), custom_call_target="tpu_custom_call" | custom-call | flops 268435456 | bytes 1575004 | tf_op jit(solution)/shard_map/pallas_call | solution.py:48
  15.0 1.9 %collective-permute-start.2 = (bf16[272,256]{1,0:T(8,128)(2,1)S(1)}, bf16[272,256]{1,0:T(8,128)(2,1)S(1)}, u32[]{:S(2)}, u32[]{:S(2)}) collective-permute-start(bf16[272,256]{1,0:T(8,128)(2,1)S(1)} %get-tuple-element.49), channel_id=1, source_target_pairs={{12,0},{0,4},{4,8},{8,12},{13,1},{1,5},{5,9},{9,13},{14,2},{2,6},{... | collective-permute-start | bytes 417800 | tf_op jit(solution)/shard_map/ppermute | solution.py:23
  16.9 2.1 %collective-permute-start.3 = (bf16[272,256]{1,0:T(8,128)(2,1)S(1)}, bf16[272,256]{1,0:T(8,128)(2,1)S(1)}, u32[]{:S(2)}, u32[]{:S(2)}) collective-permute-start(bf16[272,256]{1,0:T(8,128)(2,1)S(1)} %get-tuple-element.50), channel_id=1, source_target_pairs={{4,0},{8,4},{12,8},{0,12},{5,1},{9,5},{13,9},{1,13},{6,2},{10,6},{... | collective-permute-start | bytes 417800 | tf_op jit(solution)/shard_map/ppermute | solution.py:23
  19.0 1.1 %collective-permute-start.4 = (bf16[272,256]{1,0:T(8,128)(2,1)S(1)}, bf16[272,256]{1,0:T(8,128)(2,1)S(1)}, u32[]{:S(2)}, u32[]{:S(2)}) collective-permute-start(bf16[272,256]{1,0:T(8,128)(2,1)S(1)} %get-tuple-element.51), channel_id=1, source_target_pairs={{0,9},{1,8},{4,13},{5,12},{8,1},{9,0},{12,5},{13,4},{2,11},{3,10},... | collective-permute-start | bytes 417800 | tf_op jit(solution)/shard_map/ppermute | solution.py:446
  20.0 3.5 %collective-permute-done.2.refs_1_ = bf16[272,256]{1,0:T(8,128)(2,1)S(1)} collective-permute-done((bf16[272,256]{1,0:T(8,128)(2,1)S(1)}, bf16[272,256]{1,0:T(8,128)(2,1)S(1)}, u32[]{:S(2)}, u32[]{:S(2)}) %collective-permute-start.2) | collective-permute-done | bytes 139296 | tf_op jit(solution)/shard_map/ppermute | solution.py:23
  24.1 1.6 %collective-permute-start.8 = (bf16[256,512]{1,0:T(8,128)(2,1)}, bf16[256,512]{1,0:T(8,128)(2,1)S(1)}, u32[]{:S(2)}, u32[]{:S(2)}) collective-permute-start(bf16[256,512]{1,0:T(8,128)(2,1)} %cots.1), channel_id=1, source_target_pairs={{2,0},{0,2},{3,1},{1,3},{6,4},{4,6},{7,5},{5,7},{10,8},{8,10},{11,... | collective-permute-start | bytes 786440 | tf_op jit(solution)/shard_map/ppermute | solution.py:23
  25.8 1.0 %copy-done.1 = bf16[512,512]{1,0:T(8,128)(2,1)S(1)} copy-done((bf16[512,512]{1,0:T(8,128)(2,1)S(1)}, bf16[512,512]{1,0:T(8,128)(2,1)}, u32[]{:S(2)}) %copy-start.1) | copy-done | bytes 524312
  26.8 1.0 %copy-done.3 = bf16[512,512]{1,0:T(8,128)(2,1)S(1)} copy-done((bf16[512,512]{1,0:T(8,128)(2,1)S(1)}, bf16[512,512]{1,0:T(8,128)(2,1)}, u32[]{:S(2)}) %copy-start.3) | copy-done | bytes 524312
  27.9 1.0 %copy-done.4 = bf16[512,512]{1,0:T(8,128)(2,1)S(1)} copy-done((bf16[512,512]{1,0:T(8,128)(2,1)S(1)}, bf16[512,512]{1,0:T(8,128)(2,1)}, u32[]{:S(2)}) %copy-start.4) | copy-done | bytes 524312
  28.9 1.0 %copy-done.6 = bf16[512,512]{1,0:T(8,128)(2,1)S(1)} copy-done((bf16[512,512]{1,0:T(8,128)(2,1)S(1)}, bf16[512,512]{1,0:T(8,128)(2,1)}, u32[]{:S(2)}) %copy-start.6) | copy-done | bytes 524312
  29.9 1.0 %copy-done.8 = bf16[512,512]{1,0:T(8,128)(2,1)S(1)} copy-done((bf16[512,512]{1,0:T(8,128)(2,1)S(1)}, bf16[512,512]{1,0:T(8,128)(2,1)}, u32[]{:S(2)}) %copy-start.8) | copy-done | bytes 524312
  31.0 1.0 %copy-done.10 = bf16[512,512]{1,0:T(8,128)(2,1)S(1)} copy-done((bf16[512,512]{1,0:T(8,128)(2,1)S(1)}, bf16[512,512]{1,0:T(8,128)(2,1)}, u32[]{:S(2)}) %copy-start.10) | copy-done | bytes 524312
  33.5 1.6 %shard_map.175 = (bf16[512,256]{1,0:T(8,128)(2,1)S(1)}, bf16[512,256]{1,0:T(8,128)(2,1)S(1)}, bf16[256,512]{1,0:T(8,128)(2,1)S(1)}, bf16[256,512]{1,0:T(8,128)(2...) custom-call(s32[23]{0:T(128)S(1)} %concatenate.3.info, ...), custom_call_target="tpu_custom_call" | custom-call | flops 536870912 | bytes 3172444 | tf_op jit(solution)/shard_map/pallas_call | solution.py:48
  35.2 11.2 %shard_map.177 = (bf16[256,512]{1,0:T(8,128)(2,1)S(1)}, bf16[12,512,256]{2,1,0:T(8,128)(2,1)S(1)}, f32[16,256]{1,0:T(8,128)S(1)}) custom-call(s32[23]{0:T(128)S(1)} %concatenate.3.info, bf16[12,512,128]{2,1,0:T(8,128)(2,1)S(1)} %get-tuple-element.44.low, bf16[12,512,128]{2,1,0:T(8,128)(2,1)S(1)} %get-tuple-element.45.high, ...), custom_call_target="tpu_custom_call" | custom-call | flops 6442450944 | bytes 4769884 | tf_op jit(solution)/shard_map/pallas_call | solution.py:48
  46.8 1.7 %shard_map.178 = (bf16[512,512]{1,0:T(8,128)(2,1)}, f32[512,512]{1,0:T(8,128)S(1)}, f32[512,512]{1,0:T(8,128)S(1)}) custom-call(s32[23]{0:T(128)S(1)} %concatenate.3.info, bf16[256,512]{1,0:T(8,128)(2,1)S(1)} %copy-done.14, bf16[256,512]{1,0:T(8,128)(2,1)S(1)} %collective-permute-done.8.refs_1_, bf16[512,512]{1,0:T(8,128)(2,1)S(1)} %get-tuple-element.55.refs_2_.feats, ...), custom_call_target="tpu_custom_call" | custom-call | flops 536870912 | bytes 2099292 | tf_op jit(solution)/shard_map/pallas_call | solution.py:48
  48.5 6.2 %collective-permute-done.7.refs_1_ = bf16[256,512]{1,0:T(8,128)(2,1)S(1)} collective-permute-done((bf16[256,512]{1,0:T(8,128)(2,1)S(1)}, bf16[256,512]{1,0:T(8,128)(2,1)S(1)}, u32[]{:S(2)}, u32[]{:S(2)}) %collective-permute-start.7) | collective-permute-done | bytes 262176 | tf_op jit(solution)/shard_map/ppermute | solution.py:23
  54.7 2.3 %shard_map.179 = (bf16[512,512]{1,0:T(8,128)(2,1)S(1)}, bf16[512,512]{1,0:T(8,128)(2,1)S(1)}, f32[512,256]{1,0:T(8,128)S(1)}) custom-call(s32[23]{0:T(128)S(1)} %concatenate.3.info, s32[1,512]{1,0:T(1,128)S(1)} %bitcast.21, bf16[256,512]{1,0:T(8,128)(2,1)S(1)} %get-tuple-element.52.refs_0_, bf16[256,512]{1,0:T(8,128)(2,1)S(1)} %collective-permute-done.7.refs_1_, ...), custom_call_target="tpu_custom_call" | custom-call | flops 805306368 | bytes 4458588 | tf_op jit(solution)/shard_map/pallas_call | solution.py:48
  57.0 8.8 %shard_map.181 = (bf16[256,256]{1,0:T(8,128)(2,1)S(1)}, bf16[256,256]{1,0:T(8,128)(2,1)S(1)}, bf16[256,256]{1,0:T(8,128)(2,1)S(1)}, bf16[3,256,256]{2,1,0:T(8,12...) custom-call(s32[23]{0:T(128)S(1)} %concatenate.3.info, ...), custom_call_target="tpu_custom_call" | custom-call | flops 4831838208 | bytes 4079708 | tf_op jit(solution)/shard_map/pallas_call | solution.py:48
  65.9 5.1 %collective-permute-start.12 = (bf16[256,256]{1,0:T(8,128)(2,1)S(1)}, bf16[256,256]{1,0:T(8,128)(2,1)S(1)}, u32[]{:S(2)}, u32[]{:S(2)}) collective-permute-start(bf16[256,256]{1,0:T(8,128)(2,1)S(1)} %get-tuple-element.78), channel_id=1, source_target_pairs={{0,9},{1,8},{4,13},{5,12},{8,1},{9,0},{12,5},{13,4},{2,11},{3,10},... | collective-permute-start | bytes 393224 | tf_op jit(solution)/shard_map/ppermute | solution.py:446
  71.0 1.5 %shard_map.180 = (bf16[256,512]{1,0:T(8,128)(2,1)}, f32[256,512]{1,0:T(8,128)S(1)}) custom-call(s32[23]{0:T(128)S(1)} %concatenate.3.info, bf16[256,512]{1,0:T(8,128)(2,1)S(1)} %copy-done.13, bf16[256,512]{1,0:T(8,128)(2,1)S(1)} %copy-done.14, bf16[512,512]{1,0:T(8,128)(2,1)S(1)} %get-tuple-element.59.hidden, ...), custom_call_target="tpu_custom_call" | custom-call | flops 268435456 | bytes 2359388 | tf_op jit(solution)/shard_map/pallas_call | solution.py:48
  72.6 2.5 %collective-permute-start.10 = (bf16[256,256]{1,0:T(8,128)(2,1)S(1)}, bf16[256,256]{1,0:T(8,128)(2,1)S(1)}, u32[]{:S(2)}, u32[]{:S(2)}) collective-permute-start(bf16[256,256]{1,0:T(8,128)(2,1)S(1)} %get-tuple-element.76), channel_id=1, source_target_pairs={{4,0},{8,4},{12,8},{0,12},{5,1},{9,5},{13,9},{1,13},{6,2},{10,6},{... | collective-permute-start | bytes 393224 | tf_op jit(solution)/shard_map/ppermute | solution.py:23
  75.1 3.7 %shard_map.182.own = f32[512,256]{1,0:T(8,128)S(1)} custom-call(bf16[12,16,512]{2,1,0:T(8,128)(2,1)S(1)} %get-tuple-element.63.low, bf16[12,16,512]{2,1,0:T(8,128)(2,1)S(1)} %get-tuple-element.64.high, bf16[12,512,256]{2,1,0:T(8,128)(2,1)S(1)} %get-tuple-element.68.grads), custom_call_target="tpu_custom_call" | custom-call | flops 1610612736 | bytes 3538944 | tf_op jit(solution)/shard_map/pallas_call | solution.py:48
  79.1 3.9 %collective-permute-done.11.lower = bf16[256,256]{1,0:T(8,128)(2,1)S(1)} collective-permute-done((bf16[256,256]{1,0:T(8,128)(2,1)S(1)}, bf16[256,256]{1,0:T(8,128)(2,1)S(1)}, u32[]{:S(2)}, u32[]{:S(2)}) %collective-permute-start.11) | collective-permute-done | bytes 131104 | tf_op jit(solution)/shard_map/ppermute | solution.py:23
  82.9 1.6 %shard_map.184 = (f32[256,512]{1,0:T(8,128)S(1)}, bf16[1,256,512]{2,1,0:T(8,128)(2,1)S(1)}, f32[4,64,256]{2,1,0:T(8,128)S(1)}, bf16[4,64,256]{2,1,0:T(8,128)(2,1)S(1)}) custom-call(s32[23]{0:T(128)S(1)} %concatenate.3.info, f32[512,256]{1,0:T(8,128)S(1)} %shard_map.182.own, bf16[512,256]{1,0:T(8,128)(2,1)S(1)} %get-tuple-element.69.recv, ...), custom_call_target="tpu_custom_call" | custom-call | flops 402653184 | bytes 3145820 | tf_op jit(solution)/shard_map/pallas_call | solution.py:48
  86.0 1.2 %collective-permute-start.15 = (bf16[64,256]{1,0:T(8,128)(2,1)S(1)}, bf16[64,256]{1,0:T(8,128)(2,1)S(1)}, u32[]{:S(2)}, u32[]{:S(2)}) collective-permute-start(bf16[64,256]{1,0:T(8,128)(2,1)S(1)} %get-tuple-element.93), channel_id=1, source_target_pairs={{12,0},{0,4},{4,8},{8,12},{13,1},{1,5},{5,9},{9,13},{14,2},{2,6},{... | collective-permute-start | bytes 98312 | tf_op jit(solution)/shard_map/ppermute | solution.py:23
  87.2 1.6 %collective-permute-start.16 = (bf16[64,256]{1,0:T(8,128)(2,1)S(1)}, bf16[64,256]{1,0:T(8,128)(2,1)S(1)}, u32[]{:S(2)}, u32[]{:S(2)}) collective-permute-start(bf16[64,256]{1,0:T(8,128)(2,1)S(1)} %get-tuple-element.92), channel_id=1, source_target_pairs={{8,0},{12,4},{0,8},{4,12},{9,1},{13,5},{1,9},{5,13},{10,2},{14,6},... | collective-permute-start | bytes 98312 | tf_op jit(solution)/shard_map/ppermute | solution.py:23
  88.8 2.3 %collective-permute-start.17 = (bf16[64,256]{1,0:T(8,128)(2,1)S(1)}, bf16[64,256]{1,0:T(8,128)(2,1)S(1)}, u32[]{:S(2)}, u32[]{:S(2)}) collective-permute-start(bf16[64,256]{1,0:T(8,128)(2,1)S(1)} %get-tuple-element.91), channel_id=1, source_target_pairs={{4,0},{8,4},{12,8},{0,12},{5,1},{9,5},{13,9},{1,13},{6,2},{10,6},{... | collective-permute-start | bytes 98312 | tf_op jit(solution)/shard_map/ppermute | solution.py:23
  92.0 1.2 %collective-permute-done.16.refs_1_ = bf16[64,256]{1,0:T(8,128)(2,1)S(1)} collective-permute-done((bf16[64,256]{1,0:T(8,128)(2,1)S(1)}, bf16[64,256]{1,0:T(8,128)(2,1)S(1)}, u32[]{:S(2)}, u32[]{:S(2)}) %collective-permute-start.16) | collective-permute-done | bytes 32800 | tf_op jit(solution)/shard_map/ppermute | solution.py:23
  (65 shorter events, 10.2 us)
Async XLA Ops:
  0.6 9.5 %collective-permute-start = (bf16[256,512]{1,0:T(8,128)(2,1)}, bf16[256,512]{1,0:T(8,128)(2,1)S(1)}, u32[]{:S(2)}, u32[]{:S(2)}) collective-permute-start(bf16[256,512]{1,0:T(8,128)(2,1)} %feats.1), channel_id=1, source_target_pairs={{2,0},{0,2},{3,1},{1,3},{6,4},{4,6},{7,5},{5,7},{10,8},{8,10},{11,... | collective-permute-start | bytes 786440 | tf_op jit(solution)/shard_map/ppermute | solution.py:23
  10.2 1.0 %copy-start = (bf16[512,512]{1,0:T(8,128)(2,1)S(1)}, bf16[512,512]{1,0:T(8,128)(2,1)}, u32[]{:S(2)}) copy-start(bf16[512,512]{1,0:T(8,128)(2,1)} %refs_2_.2) | copy-start | bytes 1572868
  11.2 1.0 %copy-start.2 = (bf16[512,512]{1,0:T(8,128)(2,1)S(1)}, bf16[512,512]{1,0:T(8,128)(2,1)}, u32[]{:S(2)}) copy-start(bf16[512,512]{1,0:T(8,128)(2,1)} %refs_3_.3) | copy-start | bytes 1572868
  15.0 8.6 %collective-permute-start.2 = (bf16[272,256]{1,0:T(8,128)(2,1)S(1)}, bf16[272,256]{1,0:T(8,128)(2,1)S(1)}, u32[]{:S(2)}, u32[]{:S(2)}) collective-permute-start(bf16[272,256]{1,0:T(8,128)(2,1)S(1)} %get-tuple-element.49), channel_id=1, source_target_pairs={{12,0},{0,4},{4,8},{8,12},{13,1},{1,5},{5,9},{9,13},{14,2},{2,6},{... | collective-permute-start | bytes 417800 | tf_op jit(solution)/shard_map/ppermute | solution.py:23
  16.9 7.2 %collective-permute-start.3 = (bf16[272,256]{1,0:T(8,128)(2,1)S(1)}, bf16[272,256]{1,0:T(8,128)(2,1)S(1)}, u32[]{:S(2)}, u32[]{:S(2)}) collective-permute-start(bf16[272,256]{1,0:T(8,128)(2,1)S(1)} %get-tuple-element.50), channel_id=1, source_target_pairs={{4,0},{8,4},{12,8},{0,12},{5,1},{9,5},{13,9},{1,13},{6,2},{10,6},{... | collective-permute-start | bytes 417800 | tf_op jit(solution)/shard_map/ppermute | solution.py:23
  19.0 16.1 %collective-permute-start.1 = (bf16[272,256]{1,0:T(8,128)(2,1)S(1)}, bf16[272,256]{1,0:T(8,128)(2,1)S(1)}, u32[]{:S(2)}, u32[]{:S(2)}) collective-permute-start(bf16[272,256]{1,0:T(8,128)(2,1)S(1)} %get-tuple-element.48), channel_id=1, source_target_pairs={{1,0},{0,1},{3,2},{2,3},{5,4},{4,5},{7,6},{6,7},{9,8},{8,9},{11,10... | collective-permute-start | bytes 417800 | tf_op jit(solution)/shard_map/ppermute | solution.py:23
  19.0 16.1 %collective-permute-start.4 = (bf16[272,256]{1,0:T(8,128)(2,1)S(1)}, bf16[272,256]{1,0:T(8,128)(2,1)S(1)}, u32[]{:S(2)}, u32[]{:S(2)}) collective-permute-start(bf16[272,256]{1,0:T(8,128)(2,1)S(1)} %get-tuple-element.51), channel_id=1, source_target_pairs={{0,9},{1,8},{4,13},{5,12},{8,1},{9,0},{12,5},{13,4},{2,11},{3,10},... | collective-permute-start | bytes 417800 | tf_op jit(solution)/shard_map/ppermute | solution.py:446
  23.5 11.5 %collective-permute-start.5 = (bf16[272,256]{1,0:T(8,128)(2,1)S(1)}, bf16[272,256]{1,0:T(8,128)(2,1)S(1)}, u32[]{:S(2)}, u32[]{:S(2)}) collective-permute-start(bf16[272,256]{1,0:T(8,128)(2,1)S(1)} %collective-permute-done.2.refs_1_), channel_id=1, source_target_pairs={{1,0},{0,1},{3,2},{2,3},{5,4},{4,5},{7,6},{6,7},{9,8},{8,9},{11,10... | collective-permute-start | bytes 417800 | tf_op jit(solution)/shard_map/ppermute | solution.py:23
  24.1 11.0 %collective-permute-start.6 = (bf16[272,256]{1,0:T(8,128)(2,1)S(1)}, bf16[272,256]{1,0:T(8,128)(2,1)S(1)}, u32[]{:S(2)}, u32[]{:S(2)}) collective-permute-start(bf16[272,256]{1,0:T(8,128)(2,1)S(1)} %collective-permute-done.3.refs_2_), channel_id=1, source_target_pairs={{1,0},{0,1},{3,2},{2,3},{5,4},{4,5},{7,6},{6,7},{9,8},{8,9},{11,10... | collective-permute-start | bytes 417800 | tf_op jit(solution)/shard_map/ppermute | solution.py:23
  24.1 22.7 %collective-permute-start.8 = (bf16[256,512]{1,0:T(8,128)(2,1)}, bf16[256,512]{1,0:T(8,128)(2,1)S(1)}, u32[]{:S(2)}, u32[]{:S(2)}) collective-permute-start(bf16[256,512]{1,0:T(8,128)(2,1)} %cots.1), channel_id=1, source_target_pairs={{2,0},{0,2},{3,1},{1,3},{6,4},{4,6},{7,5},{5,7},{10,8},{8,10},{11,... | collective-permute-start | bytes 786440 | tf_op jit(solution)/shard_map/ppermute | solution.py:23
  25.8 1.0 %copy-start.1 = (bf16[512,512]{1,0:T(8,128)(2,1)S(1)}, bf16[512,512]{1,0:T(8,128)(2,1)}, u32[]{:S(2)}) copy-start(bf16[512,512]{1,0:T(8,128)(2,1)} %refs_2_.2) | copy-start | bytes 1572868
  26.8 1.0 %copy-start.3 = (bf16[512,512]{1,0:T(8,128)(2,1)S(1)}, bf16[512,512]{1,0:T(8,128)(2,1)}, u32[]{:S(2)}) copy-start(bf16[512,512]{1,0:T(8,128)(2,1)} %refs_3_.3) | copy-start | bytes 1572868
  27.9 1.0 %copy-start.4 = (bf16[512,512]{1,0:T(8,128)(2,1)S(1)}, bf16[512,512]{1,0:T(8,128)(2,1)}, u32[]{:S(2)}) copy-start(bf16[512,512]{1,0:T(8,128)(2,1)} %refs_2_.3) | copy-start | bytes 1572868
  28.9 1.0 %copy-start.6 = (bf16[512,512]{1,0:T(8,128)(2,1)S(1)}, bf16[512,512]{1,0:T(8,128)(2,1)}, u32[]{:S(2)}) copy-start(bf16[512,512]{1,0:T(8,128)(2,1)} %refs_3_.5) | copy-start | bytes 1572868
  29.9 1.0 %copy-start.8 = (bf16[512,512]{1,0:T(8,128)(2,1)S(1)}, bf16[512,512]{1,0:T(8,128)(2,1)}, u32[]{:S(2)}) copy-start(bf16[512,512]{1,0:T(8,128)(2,1)} %w_out.3) | copy-start | bytes 1572868
  35.1 11.7 %copy-start.11 = (bf16[512,512]{1,0:T(8,128)(2,1)S(1)}, bf16[512,512]{1,0:T(8,128)(2,1)}, u32[]{:S(2)}) copy-start(bf16[512,512]{1,0:T(8,128)(2,1)} %refs_3_.4) | copy-start | bytes 1572868
  35.1 11.7 %copy-start.14 = (bf16[256,512]{1,0:T(8,128)(2,1)S(1)}, bf16[256,512]{1,0:T(8,128)(2,1)}, u32[]{:S(2)}) copy-start(bf16[256,512]{1,0:T(8,128)(2,1)} %cots.1) | copy-start | bytes 786436
  35.1 11.7 %copy-start.18 = (f32[512]{0:T(512)S(1)}, f32[512]{0:T(512)}, u32[]{:S(2)}) copy-start(f32[512]{0:T(512)} %param.28) | copy-start | bytes 6148
  35.1 19.5 %copy-start.5 = (bf16[512,512]{1,0:T(8,128)(2,1)S(1)}, bf16[512,512]{1,0:T(8,128)(2,1)}, u32[]{:S(2)}) copy-start(bf16[512,512]{1,0:T(8,128)(2,1)} %refs_2_.3) | copy-start | bytes 1572868
  35.2 19.5 %copy-start.7 = (bf16[512,512]{1,0:T(8,128)(2,1)S(1)}, bf16[512,512]{1,0:T(8,128)(2,1)}, u32[]{:S(2)}) copy-start(bf16[512,512]{1,0:T(8,128)(2,1)} %refs_3_.5) | copy-start | bytes 1572868
  46.3 8.3 %collective-permute-start.7 = (bf16[256,512]{1,0:T(8,128)(2,1)S(1)}, bf16[256,512]{1,0:T(8,128)(2,1)S(1)}, u32[]{:S(2)}, u32[]{:S(2)}) collective-permute-start(bf16[256,512]{1,0:T(8,128)(2,1)S(1)} %get-tuple-element.52.refs_0_), channel_id=1, source_target_pairs={{2,0},{0,2},{3,1},{1,3},{6,4},{4,6},{7,5},{5,7},{10,8},{8,10},{11,... | collective-permute-start | bytes 786440 | tf_op jit(solution)/shard_map/ppermute | solution.py:23
  57.0 14.0 %copy-start.9 = (bf16[512,512]{1,0:T(8,128)(2,1)S(1)}, bf16[512,512]{1,0:T(8,128)(2,1)}, u32[]{:S(2)}) copy-start(bf16[512,512]{1,0:T(8,128)(2,1)} %w_out.3) | copy-start | bytes 1572868
  57.0 14.0 %copy-start.13 = (bf16[256,512]{1,0:T(8,128)(2,1)S(1)}, bf16[256,512]{1,0:T(8,128)(2,1)}, u32[]{:S(2)}) copy-start(bf16[256,512]{1,0:T(8,128)(2,1)} %feats.1) | copy-start | bytes 786436
  65.8 6.7 %collective-permute-start.9 = (bf16[3,256,256]{2,1,0:T(8,128)(2,1)S(1)}, bf16[3,256,256]{2,1,0:T(8,128)(2,1)S(1)}, u32[]{:S(2)}, u32[]{:S(2)}) collective-permute-start(bf16[3,256,256]{2,1,0:T(8,128)(2,1)S(1)} %get-tuple-element.74), channel_id=1, source_target_pairs={{1,0},{0,1},{3,2},{2,3},{5,4},{4,5},{7,6},{6,7},{9,8},{8,9},{11,10... | collective-permute-start | bytes 1179656 | tf_op jit(solution)/shard_map/ppermute | solution.py:23
  65.9 12.9 %collective-permute-start.12 = (bf16[256,256]{1,0:T(8,128)(2,1)S(1)}, bf16[256,256]{1,0:T(8,128)(2,1)S(1)}, u32[]{:S(2)}, u32[]{:S(2)}) collective-permute-start(bf16[256,256]{1,0:T(8,128)(2,1)S(1)} %get-tuple-element.78), channel_id=1, source_target_pairs={{0,9},{1,8},{4,13},{5,12},{8,1},{9,0},{12,5},{13,4},{2,11},{3,10},... | collective-permute-start | bytes 393224 | tf_op jit(solution)/shard_map/ppermute | solution.py:446
  72.6 6.5 %collective-permute-start.10 = (bf16[256,256]{1,0:T(8,128)(2,1)S(1)}, bf16[256,256]{1,0:T(8,128)(2,1)S(1)}, u32[]{:S(2)}, u32[]{:S(2)}) collective-permute-start(bf16[256,256]{1,0:T(8,128)(2,1)S(1)} %get-tuple-element.76), channel_id=1, source_target_pairs={{4,0},{8,4},{12,8},{0,12},{5,1},{9,5},{13,9},{1,13},{6,2},{10,6},{... | collective-permute-start | bytes 393224 | tf_op jit(solution)/shard_map/ppermute | solution.py:23
  75.1 7.8 %collective-permute-start.11 = (bf16[256,256]{1,0:T(8,128)(2,1)S(1)}, bf16[256,256]{1,0:T(8,128)(2,1)S(1)}, u32[]{:S(2)}, u32[]{:S(2)}) collective-permute-start(bf16[256,256]{1,0:T(8,128)(2,1)S(1)} %get-tuple-element.77), channel_id=1, source_target_pairs={{12,0},{0,4},{4,8},{8,12},{13,1},{1,5},{5,9},{9,13},{14,2},{2,6},{... | collective-permute-start | bytes 393224 | tf_op jit(solution)/shard_map/ppermute | solution.py:23
  84.5 1.4 %collective-permute-start.14 = (bf16[4,64,256]{2,1,0:T(8,128)(2,1)S(1)}, bf16[4,64,256]{2,1,0:T(8,128)(2,1)S(1)}, u32[]{:S(2)}, u32[]{:S(2)}) collective-permute-start(bf16[4,64,256]{2,1,0:T(8,128)(2,1)S(1)} %get-tuple-element.82), channel_id=1, source_target_pairs={{1,0},{0,1},{3,2},{2,3},{5,4},{4,5},{7,6},{6,7},{9,8},{8,9},{11,10... | collective-permute-start | bytes 393224 | tf_op jit(solution)/shard_map/ppermute | solution.py:23
  84.6 9.4 %collective-permute-start.13 = (bf16[256,512]{1,0:T(8,128)(2,1)S(1)}, bf16[256,512]{1,0:T(8,128)(2,1)S(1)}, u32[]{:S(2)}, u32[]{:S(2)}) collective-permute-start(bf16[256,512]{1,0:T(8,128)(2,1)S(1)} %bitcast.24), channel_id=1, source_target_pairs={{2,0},{0,2},{3,1},{1,3},{6,4},{4,6},{7,5},{5,7},{10,8},{8,10},{11,... | collective-permute-start | bytes 786440 | tf_op jit(solution)/shard_map/ppermute | solution.py:23
  86.0 6.0 %collective-permute-start.15 = (bf16[64,256]{1,0:T(8,128)(2,1)S(1)}, bf16[64,256]{1,0:T(8,128)(2,1)S(1)}, u32[]{:S(2)}, u32[]{:S(2)}) collective-permute-start(bf16[64,256]{1,0:T(8,128)(2,1)S(1)} %get-tuple-element.93), channel_id=1, source_target_pairs={{12,0},{0,4},{4,8},{8,12},{13,1},{1,5},{5,9},{9,13},{14,2},{2,6},{... | collective-permute-start | bytes 98312 | tf_op jit(solution)/shard_map/ppermute | solution.py:23
  87.2 6.0 %collective-permute-start.16 = (bf16[64,256]{1,0:T(8,128)(2,1)S(1)}, bf16[64,256]{1,0:T(8,128)(2,1)S(1)}, u32[]{:S(2)}, u32[]{:S(2)}) collective-permute-start(bf16[64,256]{1,0:T(8,128)(2,1)S(1)} %get-tuple-element.92), channel_id=1, source_target_pairs={{8,0},{12,4},{0,8},{4,12},{9,1},{13,5},{1,9},{5,13},{10,2},{14,6},... | collective-permute-start | bytes 98312 | tf_op jit(solution)/shard_map/ppermute | solution.py:23
  88.8 4.4 %collective-permute-start.17 = (bf16[64,256]{1,0:T(8,128)(2,1)S(1)}, bf16[64,256]{1,0:T(8,128)(2,1)S(1)}, u32[]{:S(2)}, u32[]{:S(2)}) collective-permute-start(bf16[64,256]{1,0:T(8,128)(2,1)S(1)} %get-tuple-element.91), channel_id=1, source_target_pairs={{4,0},{8,4},{12,8},{0,12},{5,1},{9,5},{13,9},{1,13},{6,2},{10,6},{... | collective-permute-start | bytes 98312 | tf_op jit(solution)/shard_map/ppermute | solution.py:23
  (5 other events, 4.1 us)

commit v3 on v2

--- a/solution.py
+++ b/solution.py
@@ -14,7 +14,7 @@
 PACK = 16
 MIB = 1 << 20
 NO_CHUNK = 64
-CH, TILES, SUB, FIRST, LON, PLACES, PICKS = 0, 1, 2, 3, 4, 5, 11
+EARLY, LATE = (0, 2, 3, 5), (1, 4)
 
 
 def shifted(block, axis, distance):
@@ -41,19 +41,27 @@
     return 0.5 * jnp.tanh(0.5 * value) + 0.5
 
 
-def call(kernel, out_shape, operands, flops, scratch=(), scalars=1, limit=32):
+def call(kernel, out_shape, operands, flops, scratch=(), scalars=2, away=0, limit=24):
     vmem = pl.BlockSpec(memory_space=pltpu.VMEM)
     smem = pl.BlockSpec(memory_space=pltpu.SMEM)
+    anywhere = pl.BlockSpec(memory_space=pl.ANY)
     moved = sum(math.prod(x.shape) * x.dtype.itemsize for x in operands)
     return pl.pallas_call(
         kernel,
         out_shape=out_shape,
-        in_specs=[smem] * scalars + [vmem] * (len(operands) - scalars),
+        in_specs=[smem] * scalars
+        + [anywhere] * away
+        + [vmem] * (len(operands) - scalars - away),
         out_specs=jax.tree.map(lambda _: vmem, out_shape),
         scratch_shapes=scratch,
         compiler_params=pltpu.CompilerParams(vmem_limit_bytes=limit * MIB),
         cost_estimate=pl.CostEstimate(flops=flops, bytes_accessed=moved, transcendentals=0),
     )(*operands)
+
+
+def place_of(slot, slots):
+    sub = lax.axis_index("sub")
+    return jnp.where(sub == 0, (4, 1, 3, 0, 2, 5)[slot], (0, 1, 4, 5, 2, 3)[slot])
 
 
 def assemble(whole_ref, blocks, first):
@@ -68,43 +76,30 @@
     return ref[pl.ds(pl.multiple_of(index * rows, rows), rows), :]
 
 
-def weights_kernel(
-    info,
-    senders,
-    in_degree,
-    w_send,
-    w_recv,
-    w_msg,
-    w_node_v,
-    w_node_a,
-    w_out,
-    w_send_t,
-    w_recv_t,
-    w_msg_t,
-    w_node_v_t,
-    w_node_a_t,
-    w_out_t,
-    low_cols,
-    high_cols,
-    low_rows,
-    high_rows,
-    turned,
-):
-    mine, tiles = info[CH], info[TILES]
-    hid = w_send_t.shape[1]
-    w_send_t[...] = mine_of(w_send, mine, hid).T
-    w_recv_t[...] = mine_of(w_recv, mine, hid).T
-    w_out_t[...] = w_out[...].T
-    w_node_a_t[...] = w_node_a[...].T
-    turned[...] = w_msg[...].T
-    w_msg_t[...] = mine_of(turned, mine, hid)
-    turned[...] = w_node_v[...].T
-    w_node_v_t[...] = mine_of(turned, mine, w_node_v_t.shape[0])
-
+def weights_kernel(tiles, picks, *refs):
+    sources, refs = refs[:12], refs[12:]
+    held, refs = refs[:12], refs[12:]
+    w_send_t, w_recv_t, w_msg_t, w_node_v_t, w_node_a_t, w_out_t, *refs = refs
+    low_cols, high_cols, low_rows, high_rows, turned, w_out_all, sems = refs
+    w_send, w_recv, w_msg, w_node_v, w_node_a, w_out, senders, in_degree = held[:8]
+    mine = lax.axis_index("ch")
+    hid = w_send.shape[0]
+    copies = []
+    for k, (source, target) in enumerate(zip(sources, held)):
+        if k in (0, 1):
+            source = source.at[pl.ds(pl.multiple_of(mine * hid, hid), hid), :]
+        target = w_out_all if k == 5 else target
+        copies.append(pltpu.make_async_copy(source, target, sems.at[k]))
+    order = (6, 7, 0, 1, 2, 3, 4, 5, 8, 9, 10, 11)
+    for k in order:
+        copies[k].start()
+
+    copies[6].wait()
+    copies[7].wait()
     degree, nodes = senders.shape
     lane = lax.broadcasted_iota(jnp.int32, (degree, nodes), 1)
     row = lax.broadcasted_iota(jnp.int32, (degree, nodes), 0)
-    valid = (row < in_degree[...]) & (lane < tiles * TILE)
+    valid = (row < in_degree[...]) & (lane < tiles[0] * TILE)
     ids = senders[...]
     low = (ids & (CHUNK - 1)).astype(jnp.float32)
     high = jnp.where(valid, ids // CHUNK, NO_CHUNK).astype(jnp.float32)
@@ -124,30 +119,38 @@
         for m in range(degree):
             out[m] = spread[:, m * LANES : (m + 1) * LANES]
 
-
-def project_kernel(count, info, bias, *refs):
+    for k in order[2:]:
+        copies[k].wait()
+    w_send_t[...] = w_send[...].T
+    w_recv_t[...] = w_recv[...].T
+    w_node_a_t[...] = w_node_a[...].T
+    w_out_t[...] = w_out_all[...].T
+    w_out[...] = mine_of(w_out_all, mine, w_out.shape[0])
+    turned[...] = w_msg[...].T
+    w_msg_t[...] = mine_of(turned, mine, hid)
+    turned[...] = w_node_v[...].T
+    w_node_v_t[...] = mine_of(turned, mine, w_node_v_t.shape[0])
+
+
+def project_kernel(count, tiles, picks, bias, *refs):
     blocks = refs[:count]
     w_send, w_recv, feats, proj, base, upper, lower, cross, beside = refs[count:]
-    mine, sub, first = info[CH], info[SUB], info[FIRST]
+    mine, sub = lax.axis_index("ch"), lax.axis_index("sub")
+    first = tiles[0] // 2
     assemble(feats, blocks, mine)
     whole = feats[...]
     hid = proj.shape[1]
-    proj[...] = dot(mine_of(w_send, mine, hid), whole).T.astype(jnp.bfloat16)
-    my_bias = jnp.zeros((1, hid), jnp.float32)
-    for k in range(count):
-        my_bias += jnp.where(mine == k, bias[:, k * hid : (k + 1) * hid], 0.0)
-    recv = dot(mine_of(w_recv, mine, hid), whole).T
-    base[...] = recv.astype(jnp.bfloat16).astype(jnp.float32) + my_bias
+    proj[...] = dot(w_send[...], whole).T.astype(jnp.bfloat16)
     rows = upper.shape[0] - PACK
     upper[:rows, :] = proj[pl.ds(pl.multiple_of(first * TILE, TILE), rows), :]
     lower[:rows, :] = proj[:rows, :]
     spot = lax.broadcasted_iota(jnp.int32, (PACK, hid), 0)
-    half = info.shape[0] - PICKS
-    half = half // 2
-    for start, out in ((0, upper), (half, lower)):
+    _, slots, per_slot = picks.shape
+    half = slots // 2
+    for start, out, lift in ((0, upper, first), (half, lower, 0)):
         marks = jnp.zeros((PACK, hid), jnp.float32)
-        for k in range(half):
-            rel = info[PICKS + start + k]
+        for k in range(half * per_slot):
+            rel = picks[0, start + k // per_slot, k % per_slot] - lift
             marks = jnp.where(spot == k, rel.astype(jnp.float32), marks)
         out[rows:, :] = marks.astype(jnp.bfloat16)
 
@@ -161,19 +164,25 @@
         cross[...] = upper[...]
         beside[...] = lower[...]
 
-
-def prepare_kernel(count, info, *refs):
+    my_bias = jnp.zeros((1, hid), jnp.float32)
+    for k in range(count):
+        my_bias += jnp.where(mine == k, bias[:, k * hid : (k + 1) * hid], 0.0)
+    recv = dot(w_recv[...], whole).T
+    base[...] = recv.astype(jnp.bfloat16).astype(jnp.float32) + my_bias
+
+
+def prepare_kernel(count, tiles, *refs):
     blocks = refs[:count]
     feats, w_node_v, bias, w_out_t, cots, pre, grad_hidden = refs[count:]
-    assemble(cots, blocks, info[CH])
+    assemble(cots, blocks, lax.axis_index("ch"))
     column = jnp.broadcast_to(bias[...], (8, bias.shape[1])).T[:, :1]
     pre[...] = dot(w_node_v[...], feats[...]) + column
     lane = lax.broadcasted_iota(jnp.int32, (1, cots.shape[1]), 1)
-    active = (lane < info[TILES] * TILE).astype(jnp.bfloat16)
+    active = (lane < tiles[0] * TILE).astype(jnp.bfloat16)
     grad_hidden[...] = dot(w_out_t[...], cots[...] * active)
 
 
-def forward_kernel(info, low, high, base, in_degree, proj, *refs):
+def forward_kernel(low, high, base, in_degree, proj, *refs):
     arrivals = refs[:6]
     message, slope, rels, ext, total, held = refs[6:]
     own = proj.shape[0]
@@ -185,7 +194,7 @@
         held[place] = block[...]
     rels[...] = jnp.zeros_like(rels)
     for slot in range(slots):
-        place = info[PLACES + slot]
+        place = place_of(slot, slots)
         group = slot % (slots // 2)
         for t in range(per_slot):
             index = group * per_slot + t
@@ -225,16 +234,16 @@
         slope[m] = jnp.where(valid, sig + act * (1.0 - sig), 0.0).astype(jnp.bfloat16)
         return carry
 
-    lax.fori_loop(0, low.shape[0], step, 0)
+    lax.fori_loop(0, low.shape[0], step, 0, unroll=True)
     degree = in_degree[...].astype(jnp.float32)
     message[...] = (total[...].T / degree).astype(jnp.bfloat16)
 
 
-def node_kernel(count, info, in_degree, *refs):
+def node_kernel(count, in_degree, *refs):
     blocks = refs[:count]
     w_msg, w_node_a, w_node_a_t, w_msg_t, pre, grad_hidden = refs[count : count + 6]
     hidden, grad_pre, scale, messages = refs[count + 6 :]
-    assemble(messages, blocks, info[CH])
+    assemble(messages, blocks, lax.axis_index("ch"))
     agg = dot(w_msg[...], messages[...])
     node_pre = pre[...] + dot(w_node_a[...], agg.astype(jnp.bfloat16))
     sig = sigmoid(node_pre)
@@ -247,88 +256,81 @@
     scale[...] = (grad_msg / in_degree[...].astype(jnp.float32)).T
 
 
-def far_kernel(info, low, high, slope, scale, rels, *refs):
-    to_west, to_east, to_cross, to_beside, grads, recv, total, recv_total, held = refs
-    slots = held.shape[0]
-    rows = held.shape[1]
-    per_slot = rows // TILE
-    nodes = scale.shape[0]
-    first = nodes // CHUNK
-    chunks = slots * rows // CHUNK
-    total[...] = jnp.zeros_like(total)
-    recv_total[...] = jnp.zeros_like(recv_total)
+def scatter(low, high, grad_of, chunks, total):
+    nodes = low.shape[2]
     groups = CHUNK // PACK
     place = lax.broadcasted_iota(jnp.int32, (groups, PACK, nodes), 0) * PACK
     place = place + lax.broadcasted_iota(jnp.int32, (groups, PACK, nodes), 1)
-
-    def step(m, carry):
-        grad = slope[m].astype(jnp.float32) * scale[...]
-        recv_total[...] += grad
-        grad_low = grad.astype(jnp.bfloat16)
-        grads[m] = grad_low
-        one = jnp.bfloat16(1.0)
-        zero = jnp.bfloat16(0.0)
-        mark = jnp.where(low[m][None] == place.astype(jnp.bfloat16), one, zero)
-        picker = jnp.concatenate(
-            [
-                jnp.where(high[m][None] == jnp.bfloat16(first + chunk), mark, zero)
-                for chunk in range(chunks)
-            ],
-            axis=0,
-        ).reshape(chunks * CHUNK, nodes)
-        total[...] += dot(picker, grad_low)
-        return carry
-
-    lax.fori_loop(0, slope.shape[0], step, 0)
-    for slot in range(slots):
-        spot = info[PLACES + slot]
-        for half in range(per_slot):
-            terms = jnp.zeros((TILE, scale.shape[1]), jnp.float32)
-            for t in range(per_slot):
-                number = slot * per_slot + t
-                hit = jnp.abs(rels[number : number + 1, :] - half) < 0.5
-                tile = total[number * TILE : (number + 1) * TILE, :]
-                terms += jnp.where(hit, tile, 0.0)
-            held[spot, half * TILE : (half + 1) * TILE, :] = terms.astype(jnp.bfloat16)
-    to_west[...] = held[1]
-    to_east[...] = held[2]
-    to_cross[...] = held[3]
-    to_beside[0] = held[0]
-    to_beside[1] = held[4]
-    to_beside[2] = held[5]
-    recv[...] = recv_total[...].astype(jnp.bfloat16)
-
-
-def own_kernel(low, high, grads, total):
-    nodes = total.shape[0]
-    chunks = nodes // CHUNK
-    groups = CHUNK // PACK
     total[...] = jnp.zeros_like(total)
-    place = lax.broadcasted_iota(jnp.int32, (groups, PACK, nodes), 0) * PACK
-    place = place + lax.broadcasted_iota(jnp.int32, (groups, PACK, nodes), 1)
 
     def step(m, carry):
         one = jnp.bfloat16(1.0)
         zero = jnp.bfloat16(0.0)
         mark = jnp.where(low[m][None] == place.astype(jnp.bfloat16), one, zero)
         picker = jnp.concatenate(
-            [
-                jnp.where(high[m][None] == jnp.bfloat16(chunk), mark, zero)
-                for chunk in range(chunks)
-            ],
+            [jnp.where(high[m][None] == jnp.bfloat16(chunk), mark, zero) for chunk in chunks],
             axis=0,
-        ).reshape(chunks * CHUNK, nodes)
-        total[...] += dot(picker, grads[m])
+        ).reshape(len(chunks) * CHUNK, nodes)
+        total[...] += dot(picker, grad_of(m))
         return carry
 
+    lax.fori_loop(0, low.shape[0], step, 0, unroll=True)
+
+
+def fold(slots, index, rels, total):
+    rows = CHUNK // TILE
+    halves = []
+    for half in range(rows):
+        terms = 0.0
+        for t in range(rows):
+            number = slots[index] * rows + t
+            hit = jnp.abs(rels[number : number + 1, :] - half) < 0.5
+            tile = total[(index * rows + t) * TILE : (index * rows + t + 1) * TILE, :]
+            terms += jnp.where(hit, tile, 0.0)
+        halves.append(terms)
+    return jnp.concatenate(halves, axis=0).astype(jnp.bfloat16)
+
+
+def early_kernel(low, high, slope, scale, rels, to_cross, to_beside, grads, total, held):
+    first = scale.shape[0] // CHUNK
+
+    def grad_of(m):
+        grads[m] = (slope[m].astype(jnp.float32) * scale[...]).astype(jnp.bfloat16)
+        return grads[m]
+
+    scatter(low, high, grad_of, [first + slot for slot in EARLY], total)
+    for index, slot in enumerate(EARLY):
+        held[place_of(slot, 6)] = fold(EARLY, index, rels, total)
+    to_cross[...] = held[3]
+    to_beside[0] = held[0]
+    to_beside[1] = held[4]
+    to_beside[2] = held[5]
+
+
+def late_kernel(low, high, grads, rels, to_west, to_east, total):
+    first = low.shape[2] // CHUNK
+    scatter(low, high, lambda m: grads[m], [first + slot for slot in LATE], total)
+    to_west[...] = fold(LATE, 0, rels, total)
+    to_east[...] = fold(LATE, 1, rels, total)
+
+
+def own_kernel(low, high, grads, total, recv, recv_total):
+    chunks = list(range(total.shape[0] // CHUNK))
+    scatter(low, high, lambda m: grads[m], chunks, total)
+    recv_total[...] = jnp.zeros_like(recv_total)
+
+    def step(m, carry):
+        recv_total[...] += grads[m].astype(jnp.float32)
+        return carry
+
     lax.fori_loop(0, grads.shape[0], step, 0)
-
-
-def output_kernel(info, feats, cots, hidden, grad_pre, w_out, w_node_v_t, updated, direct):
-    chans = feats.shape[0]
+    recv[...] = recv_total[...].T.astype(jnp.bfloat16)
+
+
+def output_kernel(tiles, feats, cots, hidden, grad_pre, w_out, w_node_v_t, updated, direct):
     lane = lax.broadcasted_iota(jnp.int32, (1, feats.shape[1]), 1)
-    active = (lane < info[TILES] * TILE).astype(jnp.float32)
-    node_out = dot(mine_of(w_out, info[CH], chans), hidden[...])
+    active = (lane < tiles[0] * TILE).astype(jnp.float32)
+    node_out = dot(w_out[...], hidden[...])
     updated[...] = (feats[...].astype(jnp.float32) + active * node_out).astype(jnp.bfloat16)
     direct[...] = cots[...].astype(jnp.float32) + dot(w_node_v_t[...], grad_pre[...])
 
@@ -340,7 +342,7 @@
 
 def final_kernel(
     inv_root,
-    info,
+    tiles,
     own,
     recv,
     direct,
@@ -359,8 +361,8 @@
     terms,
 ):
     rows = upper.shape[0]
-    mine, sub, lon = info[CH], info[SUB], info[LON]
-    start = info[FIRST] * TILE
+    mine, sub, lon = lax.axis_index("ch"), lax.axis_index("sub"), lax.axis_index("lon")
+    start = tiles[0] // 2 * TILE
     total[...] = own[...]
 
     def put(offset, block):
@@ -373,9 +375,8 @@
     put(jnp.where(sub == 0, start, 0), beside[0])
     grad_send = total[...].astype(jnp.bfloat16)
     grad_send_t = total[...].T.astype(jnp.bfloat16)
-    grad_recv_t = recv[...].astype(jnp.float32).T.astype(jnp.bfloat16)
     chans = direct.shape[0]
-    terms[...] = dot(w_send_t[...], grad_send_t) + dot(w_recv_t[...], grad_recv_t)
+    terms[...] = dot(w_send_t[...], grad_send_t) + dot(w_recv_t[...], recv[...])
     kept[...] = direct[...] + mine_of(terms, mine, chans)
     count = sent.shape[0] + 1
     for k in range(1, count):
@@ -422,8 +423,6 @@
 ):
     chans, nodes = features.shape
     count = lax.axis_size("ch")
-    mine = lax.axis_index("ch")
-    sub = lax.axis_index("sub")
     lons = lax.axis_size("lon")
     hidden_all, chans_all = w_send.shape
     hid = hidden_all // count
@@ -437,11 +436,6 @@
     bf16, f32 = jnp.bfloat16, jnp.float32
     shape = jax.ShapeDtypeStruct
 
-    first_tile = tile_count[0] // 2
-    places = jnp.where(sub == 0, jnp.array([4, 1, 3, 0, 2, 5]), jnp.array([0, 1, 4, 5, 2, 3]))
-    lift = jnp.where(jnp.arange(slots) < slots // 2, first_tile, 0)[:, None]
-    scalars = jnp.stack([mine, tile_count[0], sub, first_tile, lax.axis_index("lon")])
-    info = jnp.concatenate([scalars, places, (send_tiles[0] - lift).reshape(-1)]).astype(jnp.int32)
     across_route = [(i, (i + (3 if i % 2 else -3)) % shard_count) for i in range(shard_count)]
     across = lambda block: lax.ppermute(block, cycle, across_route)
     degrees = in_degree[None, :]
@@ -449,20 +443,17 @@
     feat_blocks = gathered(features, "ch")
     cot_blocks = gathered(cotangent, "ch")
 
-    (
-        w_send_t,
-        w_recv_t,
-        w_msg_t,
-        w_node_v_t,
-        w_node_a_t,
-        w_out_t,
-        low_cols,
-        high_cols,
-        low_rows,
-        high_rows,
-    ) = call(
+    fixed = (
+        [shape((hid, chans_all), bf16)] * 2
+        + [shape((chans_all, hidden_all), bf16), shape((hidden_all, chans_all), bf16)]
+        + [shape((hidden_all, chans_all), bf16), shape((chans, hidden_all), bf16)]
+    )
+    inputs = [senders, degrees, features, cotangent, bias_edge[None, :], bias_node[None, :]]
+    held = call(
         weights_kernel,
         (
+            *fixed,
+            *[shape(x.shape, x.dtype) for x in inputs],
             shape((chans_all, hid), bf16),
             shape((chans_all, hid), bf16),
             shape((hid, chans_all), bf16),
@@ -474,10 +465,20 @@
             shape((degree, PACK, nodes), bf16),
             shape((degree, PACK, nodes), bf16),
         ),
-        [info, senders, degrees, w_send, w_recv, w_msg, w_node_v, w_node_a, w_out],
+        [tile_count, send_tiles, w_send, w_recv, w_msg, w_node_v, w_node_a, w_out] + inputs,
         flops=4 * hidden_all * chans_all * nodes,
-        scratch=[pltpu.VMEM((chans_all, hidden_all), bf16)],
-    )
+        away=12,
+        scratch=[
+            pltpu.VMEM((chans_all, hidden_all), bf16),
+            pltpu.VMEM((chans_all, hidden_all), bf16),
+            pltpu.SemaphoreType.DMA((12,)),
+        ],
+    )
+    w_send_my, w_recv_my, w_msg, w_node_v, w_node_a, w_out_my, _, degrees = held[:8]
+    features_held, cotangent_held, bias_edge, bias_node = held[8:12]
+    w_send_t, w_recv_t, w_msg_t, w_node_v_t, w_node_a_t, w_out_t = held[12:18]
+    low_cols, high_cols, low_rows, high_rows = held[18:]
+    feat_blocks[0], cot_blocks[0] = features_held, cotangent_held
 
     block = shape((slot_rows + PACK, hid), bf16)
     feats, proj, base, upper, lower, cross, beside = call(
@@ -491,7 +492,7 @@
             block,
             block,
         ),
-        [info, bias_edge[None, :]] + feat_blocks + [w_send, w_recv],
+        [tile_count, send_tiles, bias_edge] + feat_blocks + [w_send_my, w_recv_my],
         flops=4 * hid * chans_all * nodes,
     )
     west = shifted(upper, "lon", 1)
@@ -509,8 +510,9 @@
             shape((hidden_all, nodes), f32),
             shape((hidden_all, nodes), f32),
         ),
-        [info] + cot_blocks + [feats, w_node_v, bias_node[None, :], w_out_t],
+        [tile_count] + cot_blocks + [feats, w_node_v, bias_node, w_out_t],
         flops=4 * hidden_all * chans_all * nodes,
+        scalars=1,
     )
 
     message, slope, rels = call(
@@ -520,13 +522,14 @@
             shape((degree, nodes, hid), bf16),
             shape((PACK, hid), f32),
         ),
-        [info, low_cols, high_cols, base, degrees, proj] + arrivals,
+        [low_cols, high_cols, base, degrees, proj] + arrivals,
         flops=2 * degree * nodes * ext_len * hid,
         scratch=[
             pltpu.VMEM((ext_len, hid), bf16),
             pltpu.VMEM((nodes, hid), f32),
             pltpu.VMEM((slots, slot_rows + PACK, hid), bf16),
         ],
+        scalars=0,
     )
     messages = gathered(message, "ch")
 
@@ -537,50 +540,54 @@
             shape((hidden_all, nodes), bf16),
             shape((nodes, hid), f32),
         ),
-        [info, degrees] + messages + [w_msg, w_node_a, w_node_a_t, w_msg_t, pre, grad_hidden],
+        [degrees] + messages + [w_msg, w_node_a, w_node_a_t, w_msg_t, pre, grad_hidden],
         flops=6 * hidden_all * chans_all * nodes,
         scratch=[pltpu.VMEM((hidden_all, nodes), bf16)],
+        scalars=0,
     )
 
     block = shape((slot_rows, hid), bf16)
-    to_west, to_east, to_cross, to_beside, grads, grad_recv = call(
-        far_kernel,
-        (
-            block,
-            block,
-            block,
-            shape((3, slot_rows, hid), bf16),
-            shape((degree, nodes, hid), bf16),
-            shape((nodes, hid), bf16),
-        ),
-        [info, low_rows, high_rows, slope, scale, rels],
-        flops=2 * degree * nodes * (ext_len - nodes) * hid,
+    to_cross, to_beside, grads = call(
+        early_kernel,
+        (block, shape((3, slot_rows, hid), bf16), shape((degree, nodes, hid), bf16)),
+        [low_rows, high_rows, slope, scale, rels],
+        flops=2 * degree * nodes * len(EARLY) * slot_rows * hid,
         scratch=[
-            pltpu.VMEM((ext_len - nodes, hid), f32),
-            pltpu.VMEM((nodes, hid), f32),
+            pltpu.VMEM((len(EARLY) * slot_rows, hid), f32),
             pltpu.VMEM((slots, slot_rows, hid), bf16),
         ],
+        scalars=0,
     )
     from_beside = shifted(to_beside, "sub", 1)
     from_cross = across(to_cross)
     to_west, to_east = call(
+        late_kernel,
+        (block, block),
+        [low_rows, high_rows, grads, rels],
+        flops=2 * degree * nodes * len(LATE) * slot_rows * hid,
+        scratch=[pltpu.VMEM((len(LATE) * slot_rows, hid), f32)],
+        scalars=0,
+    )
+    to_west, to_east = call(
         add_kernel, (block, block), [to_west, from_beside, to_east], flops=0, scalars=0
     )
     from_upper = shifted(to_west, "lon", -1)
     from_lower = shifted(to_east, "lon", 1)
 
-    own = call(
+    own, grad_recv = call(
         own_kernel,
-        shape((nodes, hid), f32),
+        (shape((nodes, hid), f32), shape((hid, nodes), bf16)),
         [low_rows, high_rows, grads],
         flops=2 * degree * nodes * nodes * hid,
+        scratch=[pltpu.VMEM((nodes, hid), f32)],
         scalars=0,
     )
     updated, direct = call(
         output_kernel,
         (shape((chans, nodes), bf16), shape((chans, nodes), f32)),
-        [info, features, cotangent, hidden, grad_pre, w_out, w_node_v_t],
+        [tile_count, features_held, cotangent_held, hidden, grad_pre, w_out_my, w_node_v_t],
         flops=4 * hidden_all * chans * nodes,
+        scalars=1,
     )
 
     columns = chans_all // shard_count
@@ -592,10 +599,11 @@
             shape((lons, columns, hid), f32),
             shape((lons, columns, hid), bf16),
         ),
-        [info, own, grad_recv, direct, feats, w_send_t, w_recv_t]
+        [tile_count, own, grad_recv, direct, feats, w_send_t, w_recv_t]
         + [from_upper, from_lower, from_cross, from_beside],
         flops=6 * hid * chans_all * nodes,
         scratch=[pltpu.VMEM((nodes, hid), f32), pltpu.VMEM((chans_all, nodes), f32)],
+        scalars=1,
     )
     w_beside = shifted(w_beside, "sub", 1)
     for k in range(1, count):

time: 95.4 us -> 84.8 us (0.89)
  starting transfers between devices: 23.4 us -> 16.6 us
  Pallas kernels: 33.7 us -> 27.7 us
  waiting for transfers between devices: 21.4 us -> 26.3 us
  local copies, waits for them, and re-layouts: 13.2 us -> 11.5 us
    ppermute x2, waiting for transfers between devices: 0.01 us -> 6.2 us  [shards(): across = lambda block: lax.ppermute(block, cycle, across_route)]
    pallas_call x12 -> x13, Pallas kernels: 33.7 us -> 27.7 us  [call(): pl.pallas_call(kernel, out_shape=out_shape, in_specs=[smem] * scalars + [...]
    ppermute x2, starting transfers between devices: 6.15 us -> 0.95 us  [shards(): across = lambda block: lax.ppermute(block, cycle, across_route)]
    ppermute x16, starting transfers between devices: 17.3 us -> 15.6 us  [shifted(): return lax.ppermute(block, axis, route)]
    unnamed x40 -> x24, local copies, waits for them, and re-layouts: 12.9 us -> 11.5 us
    ppermute x16, waiting for transfers between devices: 21.4 us -> 20.1 us  [shifted(): return lax.ppermute(block, axis, route)]
  transfers between devices with their start and end apart: 18 -> 18, of which waited for: 9 -> 10; matrix products, arithmetic and copies ran while one was open for 3% -> 2% of each run, Pallas kernels for 21% -> 23%
where the time goes in v3:
time: 84.8 us; the launch traced here: 84.2 us
  Pallas kernels  27.7 us (33%)
  waiting for transfers between devices  26.3 us (31%)
  starting transfers between devices  16.6 us (20%)
  local copies, waits for them, and re-layouts  11.5 us (14%)
  between operations  1.42 us (2%)
    pallas_call x13, Pallas kernels, call(): pl.pallas_call(kernel, out_shape=out_shape, in_specs=[smem] * scalars + [...  27.7 us
    ppermute x16, waiting for transfers between devices, shifted(): return lax.ppermute(block, axis, route)  20.1 us
    ppermute x16, starting transfers between devices, shifted(): return lax.ppermute(block, axis, route)  15.6 us
    unnamed x24, local copies, waits for them, and re-layouts  11.5 us
    ppermute x2, waiting for transfers between devices, shards(): across = lambda block: lax.ppermute(block, cycle, across_route)  6.2 us
  transfers between devices with their start and end apart: 18, of which 10 were waited for; matrix products, arithmetic and copies ran while one was open for 2% of the time, Pallas kernels for 23%

profile of v3, /device:TPU:0, one launch (start us, length us, event | category | flops | bytes accessed | tf_op | source)
XLA Modules:
  0.0 84.2 jit_solution(14768470242666791702)
XLA Ops:
  0.6 3.0 %collective-permute-start = (bf16[256,512]{1,0:T(8,128)(2,1)}, bf16[256,512]{1,0:T(8,128)(2,1)S(1)}, u32[]{:S(2)}, u32[]{:S(2)}) collective-permute-start(bf16[256,512]{1,0:T(8,128)(2,1)} %refs_8_.1), channel_id=1, source_target_pairs={{2,0},{0,2},{3,1},{1,3},{6,4},{4,6},{7,5},{5,7},{10,8},{8,10},{11,... | collective-permute-start | bytes 786440 | tf_op jit(solution)/shard_map/ppermute | solution.py:23
  4.3 0.8 copy.17.picks
  5.1 1.0 %copy-done = bf16[512,512]{1,0:T(8,128)(2,1)S(1)} copy-done((bf16[512,512]{1,0:T(8,128)(2,1)S(1)}, bf16[512,512]{1,0:T(8,128)(2,1)}, u32[]{:S(2)}) %copy-start) | copy-done | bytes 524312
  6.1 1.0 %copy-done.1 = bf16[512,512]{1,0:T(8,128)(2,1)S(1)} copy-done((bf16[512,512]{1,0:T(8,128)(2,1)S(1)}, bf16[512,512]{1,0:T(8,128)(2,1)}, u32[]{:S(2)}) %copy-start.1) | copy-done | bytes 524312
  7.1 1.0 %copy-done.2 = bf16[512,512]{1,0:T(8,128)(2,1)S(1)} copy-done((bf16[512,512]{1,0:T(8,128)(2,1)S(1)}, bf16[512,512]{1,0:T(8,128)(2,1)}, u32[]{:S(2)}) %copy-start.2) | copy-done | bytes 524312
  8.2 1.0 %copy-done.3 = bf16[512,512]{1,0:T(8,128)(2,1)S(1)} copy-done((bf16[512,512]{1,0:T(8,128)(2,1)S(1)}, bf16[512,512]{1,0:T(8,128)(2,1)}, u32[]{:S(2)}) %copy-start.3) | copy-done | bytes 524312
  9.2 1.0 %copy-done.4 = bf16[512,512]{1,0:T(8,128)(2,1)S(1)} copy-done((bf16[512,512]{1,0:T(8,128)(2,1)S(1)}, bf16[512,512]{1,0:T(8,128)(2,1)}, u32[]{:S(2)}) %copy-start.4) | copy-done | bytes 524312
  10.3 1.0 %copy-done.5 = bf16[512,512]{1,0:T(8,128)(2,1)S(1)} copy-done((bf16[512,512]{1,0:T(8,128)(2,1)S(1)}, bf16[512,512]{1,0:T(8,128)(2,1)}, u32[]{:S(2)}) %copy-start.5) | copy-done | bytes 524312
  11.3 0.9 %copy-done.6 = bf16[256,512]{1,0:T(8,128)(2,1)S(1)} copy-done((bf16[256,512]{1,0:T(8,128)(2,1)S(1)}, bf16[256,512]{1,0:T(8,128)(2,1)}, u32[]{:S(2)}) %copy-start.6) | copy-done | bytes 262168
  15.1 2.8 %shard_map.157 = (bf16[256,512]{1,0:T(8,128)(2,1)S(1)}, bf16[256,512]{1,0:T(8,128)(2,1)S(1)}, bf16[512,512]{1,0:T(8,128)(2,1)S(1)}, bf16[512,512]{1,0:T(8,128)(2...) custom-call(s32[1]{0:T(128)S(6)} %copy.20.tiles, ...), custom_call_target="tpu_custom_call" | custom-call | flops 536870912 | bytes 3700788 | tf_op jit(solution)/shard_map/pallas_call | solution.py:49
  17.9 1.4 %shard_map.158 = (bf16[512,512]{1,0:T(8,128)(2,1)S(1)}, bf16[512,256]{1,0:T(8,128)(2,1)S(1)}, f32[512,256]{1,0:T(8,128)S(1)}, bf16[272,256]{1,0:T(8,128)(2,1)S(1...) custom-call(s32[1]{0:T(128)S(6)} %copy.20.tiles, ...), custom_call_target="tpu_custom_call" | custom-call | flops 268435456 | bytes 1050676 | tf_op jit(solution)/shard_map/pallas_call | solution.py:49
  19.3 1.6 %collective-permute-start.2 = (bf16[272,256]{1,0:T(8,128)(2,1)S(1)}, bf16[272,256]{1,0:T(8,128)(2,1)S(1)}, u32[]{:S(2)}, u32[]{:S(2)}) collective-permute-start(bf16[272,256]{1,0:T(8,128)(2,1)S(1)} %get-tuple-element.67), channel_id=1, source_target_pairs={{12,0},{0,4},{4,8},{8,12},{13,1},{1,5},{5,9},{9,13},{14,2},{2,6},{... | collective-permute-start | bytes 417800 | tf_op jit(solution)/shard_map/ppermute | solution.py:23
  20.9 2.3 %collective-permute-start.3 = (bf16[272,256]{1,0:T(8,128)(2,1)S(1)}, bf16[272,256]{1,0:T(8,128)(2,1)S(1)}, u32[]{:S(2)}, u32[]{:S(2)}) collective-permute-start(bf16[272,256]{1,0:T(8,128)(2,1)S(1)} %get-tuple-element.68), channel_id=1, source_target_pairs={{4,0},{8,4},{12,8},{0,12},{5,1},{9,5},{13,9},{1,13},{6,2},{10,6},{... | collective-permute-start | bytes 417800 | tf_op jit(solution)/shard_map/ppermute | solution.py:23
  23.2 0.9 %collective-permute-start.4 = (bf16[272,256]{1,0:T(8,128)(2,1)S(1)}, bf16[272,256]{1,0:T(8,128)(2,1)S(1)}, u32[]{:S(2)}, u32[]{:S(2)}) collective-permute-start(bf16[272,256]{1,0:T(8,128)(2,1)S(1)} %get-tuple-element.69), channel_id=1, source_target_pairs={{0,9},{1,8},{4,13},{5,12},{8,1},{9,0},{12,5},{13,4},{2,11},{3,10},... | collective-permute-start | bytes 417800 | tf_op jit(solution)/shard_map/ppermute | solution.py:440
  24.1 3.7 %collective-permute-done.2.refs_1_ = bf16[272,256]{1,0:T(8,128)(2,1)S(1)} collective-permute-done((bf16[272,256]{1,0:T(8,128)(2,1)S(1)}, bf16[272,256]{1,0:T(8,128)(2,1)S(1)}, u32[]{:S(2)}, u32[]{:S(2)}) %collective-permute-start.2) | collective-permute-done | bytes 139296 | tf_op jit(solution)/shard_map/ppermute | solution.py:23
  27.8 1.0 %collective-permute-done.3.refs_2_ = bf16[272,256]{1,0:T(8,128)(2,1)S(1)} collective-permute-done((bf16[272,256]{1,0:T(8,128)(2,1)S(1)}, bf16[272,256]{1,0:T(8,128)(2,1)S(1)}, u32[]{:S(2)}, u32[]{:S(2)}) %collective-permute-start.3) | collective-permute-done | bytes 139296 | tf_op jit(solution)/shard_map/ppermute | solution.py:23
  29.3 5.7 %collective-permute-done.4.refs_3_ = bf16[272,256]{1,0:T(8,128)(2,1)S(1)} collective-permute-done((bf16[272,256]{1,0:T(8,128)(2,1)S(1)}, bf16[272,256]{1,0:T(8,128)(2,1)S(1)}, u32[]{:S(2)}, u32[]{:S(2)}) %collective-permute-start.4) | collective-permute-done | bytes 139296 | tf_op jit(solution)/shard_map/ppermute | solution.py:440
  35.0 10.1 %shard_map.159 = (bf16[256,512]{1,0:T(8,128)(2,1)S(1)}, bf16[12,512,256]{2,1,0:T(8,128)(2,1)S(1)}, f32[16,256]{1,0:T(8,128)S(1)}) custom-call(bf16[12,512,128]{2,1,0:T(8,128)(2,1)S(1)} %get-tuple-element.59.low, bf16[12,512,128]{2,1,0:T(8,128)(2,1)S(1)} %get-tuple-element.60.high, f32[512,256]{1,0:T(8,128)S(1)} %get-tuple-element.64.base, ...), custom_call_target="tpu_custom_call" | custom-call | flops 6442450944 | bytes 4769792 | tf_op jit(solution)/shard_map/pallas_call | solution.py:49
  45.9 1.0 %shard_map.160 = (bf16[512,512]{1,0:T(8,128)(2,1)}, f32[512,512]{1,0:T(8,128)S(1)}, f32[512,512]{1,0:T(8,128)S(1)}) custom-call(s32[1]{0:T(128)S(6)} %copy.20.tiles, bf16[256,512]{1,0:T(8,128)(2,1)S(1)} %get-tuple-element.57.refs_0_.cots, bf16[256,512]{1,0:T(8,128)(2,1)S(1)} %collective-permute-done.8.refs_1_, ...), custom_call_target="tpu_custom_call" | custom-call | flops 536870912 | bytes 2099204 | tf_op jit(solution)/shard_map/pallas_call | solution.py:49
  46.9 6.6 %collective-permute-done.7.refs_1_ = bf16[256,512]{1,0:T(8,128)(2,1)S(1)} collective-permute-done((bf16[256,512]{1,0:T(8,128)(2,1)S(1)}, bf16[256,512]{1,0:T(8,128)(2,1)S(1)}, u32[]{:S(2)}, u32[]{:S(2)}) %collective-permute-start.7) | collective-permute-done | bytes 262176 | tf_op jit(solution)/shard_map/ppermute | solution.py:23
  53.5 1.8 %shard_map.161 = (bf16[512,512]{1,0:T(8,128)(2,1)S(1)}, bf16[512,512]{1,0:T(8,128)(2,1)S(1)}, f32[512,256]{1,0:T(8,128)S(1)}) custom-call(s32[1,512]{1,0:T(1,128)S(1)} %get-tuple-element.58.in_degree, bf16[256,512]{1,0:T(8,128)(2,1)S(1)} %get-tuple-element.70.refs_0_, bf16[256,512]{1,0:T(8,128)(2,1)S(1)} %collective-permute-done.7.refs_1_, ...), custom_call_target="tpu_custom_call" | custom-call | flops 805306368 | bytes 4458496 | tf_op jit(solution)/shard_map/pallas_call | solution.py:49
  55.3 3.8 %shard_map.163 = (bf16[256,256]{1,0:T(8,128)(2,1)S(1)}, bf16[3,256,256]{2,1,0:T(8,128)(2,1)S(1)}, bf16[12,512,256]{2,1,0:T(8,128)(2,1)S(1)}) custom-call(bf16[12,16,512]{2,1,0:T(8,128)(2,1)S(1)} %get-tuple-element.86.low, bf16[12,16,512]{2,1,0:T(8,128)(2,1)S(1)} %get-tuple-element.87.high, bf16[12,512,256]{2,1,0:T(8,128)(2,1)S(1)} %get-tuple-element.88.slope, ...), custom_call_target="tpu_custom_call" | custom-call | flops 3221225472 | bytes 4079616 | tf_op jit(solution)/shard_map/pallas_call | solution.py:49
  59.2 1.0 %shard_map.162 = (bf16[256,512]{1,0:T(8,128)(2,1)}, f32[256,512]{1,0:T(8,128)S(1)}) custom-call(s32[1]{0:T(128)S(6)} %copy.20.tiles, bf16[256,512]{1,0:T(8,128)(2,1)S(1)} %get-tuple-element.56.refs_0_.feats, bf16[256,512]{1,0:T(8,128)(2,1)S(1)} %get-tuple-element.57.refs_0_.cots, bf16[512,512]{1,0:T(8,128)(2,1)S(1)} %get-tuple-element.81.hidden, ...), custom_call_target="tpu_custom_call" | custom-call | flops 268435456 | bytes 2097156 | tf_op jit(solution)/shard_map/pallas_call | solution.py:49
  60.2 1.8 %shard_map.165 = (bf16[256,256]{1,0:T(8,128)(2,1)S(1)}, bf16[256,256]{1,0:T(8,128)(2,1)S(1)}) custom-call(bf16[12,16,512]{2,1,0:T(8,128)(2,1)S(1)} %get-tuple-element.86.low, bf16[12,16,512]{2,1,0:T(8,128)(2,1)S(1)} %get-tuple-element.87.high, bf16[12,512,256]{2,1,0:T(8,128)(2,1)S(1)} %get-tuple-element.91.grads, f32[16,256]{1,0:T(8,128)S(1)} %get-tuple-element.90.rels), custom_call_target="tpu_custom_call" | custom-call | flops 1610612736 | bytes 3555328 | tf_op jit(solution)/shard_map/pallas_call | solution.py:49
  62.1 2.0 %collective-permute-start.10 = (bf16[256,256]{1,0:T(8,128)(2,1)S(1)}, bf16[256,256]{1,0:T(8,128)(2,1)S(1)}, u32[]{:S(2)}, u32[]{:S(2)}) collective-permute-start(bf16[256,256]{1,0:T(8,128)(2,1)S(1)} %get-tuple-element.100), channel_id=1, source_target_pairs={{4,0},{8,4},{12,8},{0,12},{5,1},{9,5},{13,9},{1,13},{6,2},{10,6},{... | collective-permute-start | bytes 393224 | tf_op jit(solution)/shard_map/ppermute | solution.py:23
  64.7 2.8 %shard_map.164 = (f32[512,256]{1,0:T(8,128)S(1)}, bf16[256,512]{1,0:T(8,128)(2,1)S(1)}) custom-call(bf16[12,16,512]{2,1,0:T(8,128)(2,1)S(1)} %get-tuple-element.86.low, bf16[12,16,512]{2,1,0:T(8,128)(2,1)S(1)} %get-tuple-element.87.high, bf16[12,512,256]{2,1,0:T(8,128)(2,1)S(1)} %get-tuple-element.91.grads), custom_call_target="tpu_custom_call" | custom-call | flops 1610612736 | bytes 3538944 | tf_op jit(solution)/shard_map/pallas_call | solution.py:49
  68.0 5.6 %collective-permute-done.10.upper = bf16[256,256]{1,0:T(8,128)(2,1)S(1)} collective-permute-done((bf16[256,256]{1,0:T(8,128)(2,1)S(1)}, bf16[256,256]{1,0:T(8,128)(2,1)S(1)}, u32[]{:S(2)}, u32[]{:S(2)}) %collective-permute-start.10) | collective-permute-done | bytes 131104 | tf_op jit(solution)/shard_map/ppermute | solution.py:23
  73.6 1.0 %shard_map.167 = (f32[256,512]{1,0:T(8,128)S(1)}, bf16[1,256,512]{2,1,0:T(8,128)(2,1)S(1)}, f32[4,64,256]{2,1,0:T(8,128)S(1)}, bf16[4,64,256]{2,1,0:T(8,128)(2,1)S(1)}) custom-call(s32[1]{0:T(128)S(6)} %copy.20.tiles, f32[512,256]{1,0:T(8,128)S(1)} %get-tuple-element.92.own, bf16[256,512]{1,0:T(8,128)(2,1)S(1)} %get-tuple-element.93.recv, ...), custom_call_target="tpu_custom_call" | custom-call | flops 402653184 | bytes 3145732 | tf_op jit(solution)/shard_map/pallas_call | solution.py:49
  76.7 1.9 %collective-permute-start.16 = (bf16[64,256]{1,0:T(8,128)(2,1)S(1)}, bf16[64,256]{1,0:T(8,128)(2,1)S(1)}, u32[]{:S(2)}, u32[]{:S(2)}) collective-permute-start(bf16[64,256]{1,0:T(8,128)(2,1)S(1)} %get-tuple-element.113), channel_id=1, source_target_pairs={{8,0},{12,4},{0,8},{4,12},{9,1},{13,5},{1,9},{5,13},{10,2},{14,6},... | collective-permute-start | bytes 98312 | tf_op jit(solution)/shard_map/ppermute | solution.py:23
  78.6 1.5 %collective-permute-start.17 = (bf16[64,256]{1,0:T(8,128)(2,1)S(1)}, bf16[64,256]{1,0:T(8,128)(2,1)S(1)}, u32[]{:S(2)}, u32[]{:S(2)}) collective-permute-start(bf16[64,256]{1,0:T(8,128)(2,1)S(1)} %get-tuple-element.112), channel_id=1, source_target_pairs={{4,0},{8,4},{12,8},{0,12},{5,1},{9,5},{13,9},{1,13},{6,2},{10,6},{... | collective-permute-start | bytes 98312 | tf_op jit(solution)/shard_map/ppermute | solution.py:23
  80.1 1.9 %collective-permute-done.15.refs_0_ = bf16[64,256]{1,0:T(8,128)(2,1)S(1)} collective-permute-done((bf16[64,256]{1,0:T(8,128)(2,1)S(1)}, bf16[64,256]{1,0:T(8,128)(2,1)S(1)}, u32[]{:S(2)}, u32[]{:S(2)}) %collective-permute-start.15) | collective-permute-done | bytes 32800 | tf_op jit(solution)/shard_map/ppermute | solution.py:23
  83.4 0.8 add_convert_fusion
  (43 shorter events, 8.9 us)
Async XLA Ops:
  0.6 17.2 %collective-permute-start = (bf16[256,512]{1,0:T(8,128)(2,1)}, bf16[256,512]{1,0:T(8,128)(2,1)S(1)}, u32[]{:S(2)}, u32[]{:S(2)}) collective-permute-start(bf16[256,512]{1,0:T(8,128)(2,1)} %refs_8_.1), channel_id=1, source_target_pairs={{2,0},{0,2},{3,1},{1,3},{6,4},{4,6},{7,5},{5,7},{10,8},{8,10},{11,... | collective-permute-start | bytes 786440 | tf_op jit(solution)/shard_map/ppermute | solution.py:23
  5.1 1.0 %copy-start = (bf16[512,512]{1,0:T(8,128)(2,1)S(1)}, bf16[512,512]{1,0:T(8,128)(2,1)}, u32[]{:S(2)}) copy-start(bf16[512,512]{1,0:T(8,128)(2,1)} %refs_0_.1) | copy-start | bytes 1572868
  6.1 1.0 %copy-start.1 = (bf16[512,512]{1,0:T(8,128)(2,1)S(1)}, bf16[512,512]{1,0:T(8,128)(2,1)}, u32[]{:S(2)}) copy-start(bf16[512,512]{1,0:T(8,128)(2,1)} %refs_1_.1) | copy-start | bytes 1572868
  7.1 1.0 %copy-start.2 = (bf16[512,512]{1,0:T(8,128)(2,1)S(1)}, bf16[512,512]{1,0:T(8,128)(2,1)}, u32[]{:S(2)}) copy-start(bf16[512,512]{1,0:T(8,128)(2,1)} %refs_2_.1) | copy-start | bytes 1572868
  8.2 1.0 %copy-start.3 = (bf16[512,512]{1,0:T(8,128)(2,1)S(1)}, bf16[512,512]{1,0:T(8,128)(2,1)}, u32[]{:S(2)}) copy-start(bf16[512,512]{1,0:T(8,128)(2,1)} %refs_3_.1) | copy-start | bytes 1572868
  9.2 1.0 %copy-start.4 = (bf16[512,512]{1,0:T(8,128)(2,1)S(1)}, bf16[512,512]{1,0:T(8,128)(2,1)}, u32[]{:S(2)}) copy-start(bf16[512,512]{1,0:T(8,128)(2,1)} %refs_4_.1) | copy-start | bytes 1572868
  10.3 1.0 %copy-start.5 = (bf16[512,512]{1,0:T(8,128)(2,1)S(1)}, bf16[512,512]{1,0:T(8,128)(2,1)}, u32[]{:S(2)}) copy-start(bf16[512,512]{1,0:T(8,128)(2,1)} %refs_5_.1) | copy-start | bytes 1572868
  11.3 0.9 %copy-start.6 = (bf16[256,512]{1,0:T(8,128)(2,1)S(1)}, bf16[256,512]{1,0:T(8,128)(2,1)}, u32[]{:S(2)}) copy-start(bf16[256,512]{1,0:T(8,128)(2,1)} %refs_8_.1) | copy-start | bytes 786436
  12.3 0.8 copy-start.7
  13.0 0.7 copy-start.8
  13.7 0.7 copy-start.9
  14.4 0.7 copy-start.10
  19.3 8.4 %collective-permute-start.2 = (bf16[272,256]{1,0:T(8,128)(2,1)S(1)}, bf16[272,256]{1,0:T(8,128)(2,1)S(1)}, u32[]{:S(2)}, u32[]{:S(2)}) collective-permute-start(bf16[272,256]{1,0:T(8,128)(2,1)S(1)} %get-tuple-element.67), channel_id=1, source_target_pairs={{12,0},{0,4},{4,8},{8,12},{13,1},{1,5},{5,9},{9,13},{14,2},{2,6},{... | collective-permute-start | bytes 417800 | tf_op jit(solution)/shard_map/ppermute | solution.py:23
  20.9 7.8 %collective-permute-start.3 = (bf16[272,256]{1,0:T(8,128)(2,1)S(1)}, bf16[272,256]{1,0:T(8,128)(2,1)S(1)}, u32[]{:S(2)}, u32[]{:S(2)}) collective-permute-start(bf16[272,256]{1,0:T(8,128)(2,1)S(1)} %get-tuple-element.68), channel_id=1, source_target_pairs={{4,0},{8,4},{12,8},{0,12},{5,1},{9,5},{13,9},{1,13},{6,2},{10,6},{... | collective-permute-start | bytes 417800 | tf_op jit(solution)/shard_map/ppermute | solution.py:23
  23.2 6.1 %collective-permute-start.1 = (bf16[272,256]{1,0:T(8,128)(2,1)S(1)}, bf16[272,256]{1,0:T(8,128)(2,1)S(1)}, u32[]{:S(2)}, u32[]{:S(2)}) collective-permute-start(bf16[272,256]{1,0:T(8,128)(2,1)S(1)} %get-tuple-element.66), channel_id=1, source_target_pairs={{1,0},{0,1},{3,2},{2,3},{5,4},{4,5},{7,6},{6,7},{9,8},{8,9},{11,10... | collective-permute-start | bytes 417800 | tf_op jit(solution)/shard_map/ppermute | solution.py:23
  23.2 11.8 %collective-permute-start.4 = (bf16[272,256]{1,0:T(8,128)(2,1)S(1)}, bf16[272,256]{1,0:T(8,128)(2,1)S(1)}, u32[]{:S(2)}, u32[]{:S(2)}) collective-permute-start(bf16[272,256]{1,0:T(8,128)(2,1)S(1)} %get-tuple-element.69), channel_id=1, source_target_pairs={{0,9},{1,8},{4,13},{5,12},{8,1},{9,0},{12,5},{13,4},{2,11},{3,10},... | collective-permute-start | bytes 417800 | tf_op jit(solution)/shard_map/ppermute | solution.py:440
  27.8 7.3 %collective-permute-start.5 = (bf16[272,256]{1,0:T(8,128)(2,1)S(1)}, bf16[272,256]{1,0:T(8,128)(2,1)S(1)}, u32[]{:S(2)}, u32[]{:S(2)}) collective-permute-start(bf16[272,256]{1,0:T(8,128)(2,1)S(1)} %collective-permute-done.2.refs_1_), channel_id=1, source_target_pairs={{1,0},{0,1},{3,2},{2,3},{5,4},{4,5},{7,6},{6,7},{9,8},{8,9},{11,10... | collective-permute-start | bytes 417800 | tf_op jit(solution)/shard_map/ppermute | solution.py:23
  28.8 6.3 %collective-permute-start.6 = (bf16[272,256]{1,0:T(8,128)(2,1)S(1)}, bf16[272,256]{1,0:T(8,128)(2,1)S(1)}, u32[]{:S(2)}, u32[]{:S(2)}) collective-permute-start(bf16[272,256]{1,0:T(8,128)(2,1)S(1)} %collective-permute-done.3.refs_2_), channel_id=1, source_target_pairs={{1,0},{0,1},{3,2},{2,3},{5,4},{4,5},{7,6},{6,7},{9,8},{8,9},{11,10... | collective-permute-start | bytes 417800 | tf_op jit(solution)/shard_map/ppermute | solution.py:23
  28.8 17.1 %collective-permute-start.8 = (bf16[256,512]{1,0:T(8,128)(2,1)}, bf16[256,512]{1,0:T(8,128)(2,1)S(1)}, u32[]{:S(2)}, u32[]{:S(2)}) collective-permute-start(bf16[256,512]{1,0:T(8,128)(2,1)} %refs_9_.1), channel_id=1, source_target_pairs={{2,0},{0,2},{3,1},{1,3},{6,4},{4,6},{7,5},{5,7},{10,8},{8,10},{11,... | collective-permute-start | bytes 786440 | tf_op jit(solution)/shard_map/ppermute | solution.py:23
  45.1 8.4 %collective-permute-start.7 = (bf16[256,512]{1,0:T(8,128)(2,1)S(1)}, bf16[256,512]{1,0:T(8,128)(2,1)S(1)}, u32[]{:S(2)}, u32[]{:S(2)}) collective-permute-start(bf16[256,512]{1,0:T(8,128)(2,1)S(1)} %get-tuple-element.70.refs_0_), channel_id=1, source_target_pairs={{2,0},{0,2},{3,1},{1,3},{6,4},{4,6},{7,5},{5,7},{10,8},{8,10},{11,... | collective-permute-start | bytes 786440 | tf_op jit(solution)/shard_map/ppermute | solution.py:23
  59.1 3.0 %collective-permute-start.9 = (bf16[3,256,256]{2,1,0:T(8,128)(2,1)S(1)}, bf16[3,256,256]{2,1,0:T(8,128)(2,1)S(1)}, u32[]{:S(2)}, u32[]{:S(2)}) collective-permute-start(bf16[3,256,256]{2,1,0:T(8,128)(2,1)S(1)} %get-tuple-element.98), channel_id=1, source_target_pairs={{1,0},{0,1},{3,2},{2,3},{5,4},{4,5},{7,6},{6,7},{9,8},{8,9},{11,10... | collective-permute-start | bytes 1179656 | tf_op jit(solution)/shard_map/ppermute | solution.py:23
  59.1 8.9 %collective-permute-start.12 = (bf16[256,256]{1,0:T(8,128)(2,1)S(1)}, bf16[256,256]{1,0:T(8,128)(2,1)S(1)}, u32[]{:S(2)}, u32[]{:S(2)}) collective-permute-start(bf16[256,256]{1,0:T(8,128)(2,1)S(1)} %get-tuple-element.102), channel_id=1, source_target_pairs={{0,9},{1,8},{4,13},{5,12},{8,1},{9,0},{12,5},{13,4},{2,11},{3,10},... | collective-permute-start | bytes 393224 | tf_op jit(solution)/shard_map/ppermute | solution.py:440
  62.1 11.5 %collective-permute-start.10 = (bf16[256,256]{1,0:T(8,128)(2,1)S(1)}, bf16[256,256]{1,0:T(8,128)(2,1)S(1)}, u32[]{:S(2)}, u32[]{:S(2)}) collective-permute-start(bf16[256,256]{1,0:T(8,128)(2,1)S(1)} %get-tuple-element.100), channel_id=1, source_target_pairs={{4,0},{8,4},{12,8},{0,12},{5,1},{9,5},{13,9},{1,13},{6,2},{10,6},{... | collective-permute-start | bytes 393224 | tf_op jit(solution)/shard_map/ppermute | solution.py:23
  64.1 9.5 %collective-permute-start.11 = (bf16[256,256]{1,0:T(8,128)(2,1)S(1)}, bf16[256,256]{1,0:T(8,128)(2,1)S(1)}, u32[]{:S(2)}, u32[]{:S(2)}) collective-permute-start(bf16[256,256]{1,0:T(8,128)(2,1)S(1)} %get-tuple-element.101), channel_id=1, source_target_pairs={{12,0},{0,4},{4,8},{8,12},{13,1},{1,5},{5,9},{9,13},{14,2},{2,6},{... | collective-permute-start | bytes 393224 | tf_op jit(solution)/shard_map/ppermute | solution.py:23
  74.6 1.4 %collective-permute-start.14 = (bf16[4,64,256]{2,1,0:T(8,128)(2,1)S(1)}, bf16[4,64,256]{2,1,0:T(8,128)(2,1)S(1)}, u32[]{:S(2)}, u32[]{:S(2)}) collective-permute-start(bf16[4,64,256]{2,1,0:T(8,128)(2,1)S(1)} %get-tuple-element.106), channel_id=1, source_target_pairs={{1,0},{0,1},{3,2},{2,3},{5,4},{4,5},{7,6},{6,7},{9,8},{8,9},{11,10... | collective-permute-start | bytes 393224 | tf_op jit(solution)/shard_map/ppermute | solution.py:23
  74.7 8.7 %collective-permute-start.13 = (bf16[256,512]{1,0:T(8,128)(2,1)S(1)}, bf16[256,512]{1,0:T(8,128)(2,1)S(1)}, u32[]{:S(2)}, u32[]{:S(2)}) collective-permute-start(bf16[256,512]{1,0:T(8,128)(2,1)S(1)} %bitcast.13), channel_id=1, source_target_pairs={{2,0},{0,2},{3,1},{1,3},{6,4},{4,6},{7,5},{5,7},{10,8},{8,10},{11,... | collective-permute-start | bytes 786440 | tf_op jit(solution)/shard_map/ppermute | solution.py:23
  76.1 6.0 %collective-permute-start.15 = (bf16[64,256]{1,0:T(8,128)(2,1)S(1)}, bf16[64,256]{1,0:T(8,128)(2,1)S(1)}, u32[]{:S(2)}, u32[]{:S(2)}) collective-permute-start(bf16[64,256]{1,0:T(8,128)(2,1)S(1)} %get-tuple-element.114), channel_id=1, source_target_pairs={{12,0},{0,4},{4,8},{8,12},{13,1},{1,5},{5,9},{9,13},{14,2},{2,6},{... | collective-permute-start | bytes 98312 | tf_op jit(solution)/shard_map/ppermute | solution.py:23
  76.7 5.3 %collective-permute-start.16 = (bf16[64,256]{1,0:T(8,128)(2,1)S(1)}, bf16[64,256]{1,0:T(8,128)(2,1)S(1)}, u32[]{:S(2)}, u32[]{:S(2)}) collective-permute-start(bf16[64,256]{1,0:T(8,128)(2,1)S(1)} %get-tuple-element.113), channel_id=1, source_target_pairs={{8,0},{12,4},{0,8},{4,12},{9,1},{13,5},{1,9},{5,13},{10,2},{14,6},... | collective-permute-start | bytes 98312 | tf_op jit(solution)/shard_map/ppermute | solution.py:23
  78.6 3.9 %collective-permute-start.17 = (bf16[64,256]{1,0:T(8,128)(2,1)S(1)}, bf16[64,256]{1,0:T(8,128)(2,1)S(1)}, u32[]{:S(2)}, u32[]{:S(2)}) collective-permute-start(bf16[64,256]{1,0:T(8,128)(2,1)S(1)} %get-tuple-element.112), channel_id=1, source_target_pairs={{4,0},{8,4},{12,8},{0,12},{5,1},{9,5},{13,9},{1,13},{6,2},{10,6},{... | collective-permute-start | bytes 98312 | tf_op jit(solution)/shard_map/ppermute | solution.py:23

commit v4 on v3

--- a/solution.py
+++ b/solution.py
@@ -14,7 +14,9 @@
 PACK = 16
 MIB = 1 << 20
 NO_CHUNK = 64
-EARLY, LATE = (0, 2, 3, 5), (1, 4)
+SLOT_OF = ((3, 0), (1, 1), (4, 4), (2, 5), (0, 2), (5, 3))
+EARLY, LATE = (0, 3, 4, 5), (1, 2)
+OFF = -1e4
 
 
 def shifted(block, axis, distance):
@@ -44,7 +46,7 @@
 def call(kernel, out_shape, operands, flops, scratch=(), scalars=2, away=0, limit=24):
     vmem = pl.BlockSpec(memory_space=pltpu.VMEM)
     smem = pl.BlockSpec(memory_space=pltpu.SMEM)
-    anywhere = pl.BlockSpec(memory_space=pl.ANY)
+    anywhere = pl.BlockSpec(memory_space=pltpu.HBM)
     moved = sum(math.prod(x.shape) * x.dtype.itemsize for x in operands)
     return pl.pallas_call(
         kernel,
@@ -57,11 +59,6 @@
         compiler_params=pltpu.CompilerParams(vmem_limit_bytes=limit * MIB),
         cost_estimate=pl.CostEstimate(flops=flops, bytes_accessed=moved, transcendentals=0),
     )(*operands)
-
-
-def place_of(slot, slots):
-    sub = lax.axis_index("sub")
-    return jnp.where(sub == 0, (4, 1, 3, 0, 2, 5)[slot], (0, 1, 4, 5, 2, 3)[slot])
 
 
 def assemble(whole_ref, blocks, first):
@@ -140,7 +137,7 @@
     assemble(feats, blocks, mine)
     whole = feats[...]
     hid = proj.shape[1]
-    proj[...] = dot(w_send[...], whole).T.astype(jnp.bfloat16)
+    proj[...] = (0.5 * dot(w_send[...], whole).T).astype(jnp.bfloat16)
     rows = upper.shape[0] - PACK
     upper[:rows, :] = proj[pl.ds(pl.multiple_of(first * TILE, TILE), rows), :]
     lower[:rows, :] = proj[:rows, :]
@@ -168,7 +165,7 @@
     for k in range(count):
         my_bias += jnp.where(mine == k, bias[:, k * hid : (k + 1) * hid], 0.0)
     recv = dot(w_recv[...], whole).T
-    base[...] = recv.astype(jnp.bfloat16).astype(jnp.float32) + my_bias
+    base[...] = 0.5 * (recv.astype(jnp.bfloat16).astype(jnp.float32) + my_bias)
 
 
 def prepare_kernel(count, tiles, *refs):
@@ -182,157 +179,250 @@
     grad_hidden[...] = dot(w_out_t[...], cots[...] * active)
 
 
-def forward_kernel(low, high, base, in_degree, proj, *refs):
-    arrivals = refs[:6]
-    message, slope, rels, ext, total, held = refs[6:]
+def chunk_of(place, first, shape):
+    on_zero, on_one = (float(first + slot) for slot in SLOT_OF[place])
+    chunk = jnp.where(lax.axis_index("sub") == 0, on_zero, on_one)
+    return jnp.full(shape, chunk, jnp.float32).astype(jnp.bfloat16)
+
+
+def picks_of(block, place):
+    marks = block[CHUNK : CHUNK + PACK, :].astype(jnp.float32)
+    per_slot = CHUNK // TILE
+    half = len(SLOT_OF) // 2
+    starts = [slot % half * per_slot for slot in SLOT_OF[place]]
+    sub = lax.axis_index("sub")
+    return [
+        jnp.where(
+            sub == 0,
+            marks[starts[0] + t : starts[0] + t + 1],
+            marks[starts[1] + t : starts[1] + t + 1],
+        )
+        for t in range(per_slot)
+    ]
+
+
+def fill(ext, start, block, place):
+    for t, pick in enumerate(picks_of(block, place)):
+        ext[start + t * TILE : start + (t + 1) * TILE, :] = jnp.where(
+            pick > 0.5, block[TILE : 2 * TILE, :], block[:TILE, :]
+        )
+
+
+def pick_rows(low, high, chunks, ext):
+    one = jnp.bfloat16(1.0)
+    zero = jnp.bfloat16(0.0)
+    lane = lax.broadcasted_iota(jnp.int32, low.shape, 1)
+    marks = [
+        jnp.where(low == (lane + half * LANES).astype(jnp.bfloat16), one, zero)
+        for half in range(CHUNK // LANES)
+    ]
+    picker = jnp.concatenate(
+        [jnp.where(high == chunk, mark, zero) for chunk in chunks for mark in marks], axis=1
+    )
+    return dot(picker, ext[...])
+
+
+def near_kernel(low, high, proj, beside, part, ext):
     own = proj.shape[0]
-    rows = held.shape[1] - PACK
-    per_slot = rows // TILE
-    slots = len(arrivals)
     ext[:own, :] = proj[...]
-    for place, block in enumerate(arrivals):
-        held[place] = block[...]
-    rels[...] = jnp.zeros_like(rels)
-    for slot in range(slots):
-        place = place_of(slot, slots)
-        group = slot % (slots // 2)
-        for t in range(per_slot):
-            index = group * per_slot + t
-            rel = held[place, rows : rows + PACK, :][index : index + 1, :].astype(jnp.float32)
-            number = slot * per_slot + t
-            rels[number : number + 1, :] = rel
-            start = own + number * TILE
-            ext[start : start + TILE, :] = jnp.where(
-                rel > 0.5, held[place, TILE : 2 * TILE, :], held[place, :TILE, :]
-            )
-    chunks = ext.shape[0] // CHUNK
-    halves = CHUNK // LANES
+    fill(ext, own, beside, 0)
+    first = own // CHUNK
+    chunks = [jnp.bfloat16(chunk) for chunk in range(first)]
+    chunks.append(chunk_of(0, first, low.shape[1:]))
+
+    def step(m, carry):
+        part[m] = pick_rows(low[m], high[m], chunks, ext).astype(jnp.bfloat16)
+        return carry
+
+    lax.fori_loop(0, low.shape[0], step, 0, unroll=True)
+
+
+def line_kernel(low, high, before, west, east, part, ext):
+    first = low.shape[1] // CHUNK
+    chunks = []
+    for index, (place, block) in enumerate(((1, west), (2, east))):
+        fill(ext, index * CHUNK, block, place)
+        chunks.append(jnp.bfloat16(first + SLOT_OF[place][0]))
+
+    def step(m, carry):
+        more = pick_rows(low[m], high[m], chunks, ext)
+        part[m] = (before[m].astype(jnp.float32) + more).astype(jnp.bfloat16)
+        return carry
+
+    lax.fori_loop(0, low.shape[0], step, 0, unroll=True)
+
+
+def message_kernel(
+    start, low, high, base, in_degree, part, cross, west, east, message, slope, ext, total
+):
+    nodes = low.shape[1]
+    degree, rows, hid = slope.shape
+    first = nodes // CHUNK
+    together = nodes // rows
+    span = slice(start, start + rows)
+    chunks = []
+    for index, (place, block) in enumerate(((3, cross), (4, west), (5, east))):
+        fill(ext, index * CHUNK, block, place)
+        chunks.append(chunk_of(place, first, (nodes, LANES)))
     total[...] = jnp.zeros_like(total)
-    lane = lax.broadcasted_iota(jnp.int32, (own, LANES), 1)
-
-    def step(m, carry):
-        low_m, high_m = low[m], high[m]
-        one = jnp.bfloat16(1.0)
-        zero = jnp.bfloat16(0.0)
-        marks = [
-            jnp.where(low_m == (lane + half * LANES).astype(jnp.bfloat16), one, zero)
-            for half in range(halves)
-        ]
-        picker = jnp.concatenate(
-            [
-                jnp.where(high_m == jnp.bfloat16(chunk), mark, zero)
-                for chunk in range(chunks)
-                for mark in marks
-            ],
-            axis=1,
-        )
-        pre = dot(picker, ext[...]) + base[...]
-        valid = high_m[:, :1].astype(jnp.float32) < chunks
-        sig = sigmoid(pre)
-        act = pre * sig
-        total[...] += jnp.where(valid, act, 0.0)
-        slope[m] = jnp.where(valid, sig + act * (1.0 - sig), 0.0).astype(jnp.bfloat16)
+
+    def rows_of(ref, k):
+        return jnp.concatenate([ref[k * together + i, span, :] for i in range(together)], axis=0)
+
+    def step(k, carry):
+        low_k, high_k = rows_of(low, k), rows_of(high, k)
+        half = pick_rows(low_k, high_k, chunks, ext) + rows_of(part, k).astype(jnp.float32)
+        half += jnp.concatenate([base[span, :]] * together, axis=0)
+        wide = jnp.concatenate([high_k] * pl.cdiv(hid, LANES), axis=1)[:, :hid]
+        half = jnp.where(wide.astype(jnp.float32) < NO_CHUNK, half, OFF)
+        twice = jnp.tanh(half) + 1.0
+        act = half * twice
+        grad = (twice + act * (2.0 - twice)).astype(jnp.bfloat16)
+        terms = 0.0
+        for i in range(together):
+            terms += act[i * rows : (i + 1) * rows]
+            slope[k * together + i] = grad[i * rows : (i + 1) * rows]
+        total[...] += terms
         return carry
 
-    lax.fori_loop(0, low.shape[0], step, 0, unroll=True)
-    degree = in_degree[...].astype(jnp.float32)
-    message[...] = (total[...].T / degree).astype(jnp.bfloat16)
-
-
-def node_kernel(count, in_degree, *refs):
+    lax.fori_loop(0, degree // together, step, 0, unroll=True)
+    count = in_degree[:, span].astype(jnp.float32)
+    message[...] = (total[...].T / count).astype(jnp.bfloat16)
+
+
+def node_kernel(count, start, in_degree, *refs):
     blocks = refs[:count]
     w_msg, w_node_a, w_node_a_t, w_msg_t, pre, grad_hidden = refs[count : count + 6]
     hidden, grad_pre, scale, messages = refs[count + 6 :]
     assemble(messages, blocks, lax.axis_index("ch"))
+    span = slice(start, start + hidden.shape[1])
     agg = dot(w_msg[...], messages[...])
-    node_pre = pre[...] + dot(w_node_a[...], agg.astype(jnp.bfloat16))
-    sig = sigmoid(node_pre)
-    act = node_pre * sig
+    half = 0.5 * (pre[:, span] + dot(w_node_a[...], agg.astype(jnp.bfloat16)))
+    twice = jnp.tanh(half) + 1.0
+    act = half * twice
     hidden[...] = act.astype(jnp.bfloat16)
-    low_grad = (grad_hidden[...] * (sig + act * (1.0 - sig))).astype(jnp.bfloat16)
+    slope = 0.5 * (twice + act * (2.0 - twice))
+    low_grad = (grad_hidden[:, span] * slope).astype(jnp.bfloat16)
     grad_pre[...] = low_grad
     grad_agg = dot(w_node_a_t[...], low_grad).astype(jnp.bfloat16)
     grad_msg = dot(w_msg_t[...], grad_agg).astype(jnp.bfloat16).astype(jnp.float32)
-    scale[...] = (grad_msg / in_degree[...].astype(jnp.float32)).T
-
-
-def scatter(low, high, grad_of, chunks, total):
-    nodes = low.shape[2]
+    scale[...] = (grad_msg * (0.5 / in_degree[:, span].astype(jnp.float32))).T
+
+
+def scatter(low, high, edges, chunks, total):
+    one = jnp.bfloat16(1.0)
+    zero = jnp.bfloat16(0.0)
     groups = CHUNK // PACK
-    place = lax.broadcasted_iota(jnp.int32, (groups, PACK, nodes), 0) * PACK
-    place = place + lax.broadcasted_iota(jnp.int32, (groups, PACK, nodes), 1)
-    total[...] = jnp.zeros_like(total)
-
-    def step(m, carry):
-        one = jnp.bfloat16(1.0)
-        zero = jnp.bfloat16(0.0)
-        mark = jnp.where(low[m][None] == place.astype(jnp.bfloat16), one, zero)
+    for step in edges:
+        width = sum(rows for _, _, rows, _ in step)
+        place = lax.broadcasted_iota(jnp.int32, (groups, PACK, width), 0) * PACK
+        place = place + lax.broadcasted_iota(jnp.int32, (groups, PACK, width), 1)
+        low_k = jnp.concatenate([low[m, :, s : s + r] for m, s, r, _ in step], axis=1)
+        high_k = jnp.concatenate([high[m, :, s : s + r] for m, s, r, _ in step], axis=1)
+        grads = jnp.concatenate([grad() for _, _, _, grad in step], axis=0)
+        mark = jnp.where(low_k[None] == place.astype(jnp.bfloat16), one, zero)
         picker = jnp.concatenate(
-            [jnp.where(high[m][None] == jnp.bfloat16(chunk), mark, zero) for chunk in chunks],
-            axis=0,
-        ).reshape(len(chunks) * CHUNK, nodes)
-        total[...] += dot(picker, grad_of(m))
-        return carry
-
-    lax.fori_loop(0, low.shape[0], step, 0, unroll=True)
-
-
-def fold(slots, index, rels, total):
-    rows = CHUNK // TILE
+            [jnp.where(high_k[None] == chunk, mark, zero) for chunk in chunks], axis=0
+        ).reshape(len(chunks) * CHUNK, width)
+        total[...] += dot(picker, grads)
+
+
+def pairs(start, ref, nodes, grad_of):
+    degree, rows, _ = ref.shape
+    together = nodes // rows
+    return [
+        [
+            (m, start, rows, functools.partial(grad_of, ref, m))
+            for m in range(k * together, (k + 1) * together)
+        ]
+        for k in range(degree // together)
+    ]
+
+
+def fold(block, place, index, total):
+    picks = picks_of(block, place)
     halves = []
-    for half in range(rows):
+    for half in range(len(picks)):
         terms = 0.0
-        for t in range(rows):
-            number = slots[index] * rows + t
-            hit = jnp.abs(rels[number : number + 1, :] - half) < 0.5
-            tile = total[(index * rows + t) * TILE : (index * rows + t + 1) * TILE, :]
-            terms += jnp.where(hit, tile, 0.0)
+        for t, pick in enumerate(picks):
+            start = index * CHUNK + t * TILE
+            hit = jnp.abs(pick - half) < 0.5
+            terms += jnp.where(hit, total[start : start + TILE, :], 0.0)
         halves.append(terms)
     return jnp.concatenate(halves, axis=0).astype(jnp.bfloat16)
 
 
-def early_kernel(low, high, slope, scale, rels, to_cross, to_beside, grads, total, held):
-    first = scale.shape[0] // CHUNK
-
-    def grad_of(m):
-        grads[m] = (slope[m].astype(jnp.float32) * scale[...]).astype(jnp.bfloat16)
+def early_kernel(start, low, high, slope, scale, *refs):
+    if start:
+        before, beside, cross, west, east, to_cross, to_beside, grads, total = refs
+        total[...] = before[...]
+    else:
+        grads, total = refs
+        total[...] = jnp.zeros_like(total)
+    nodes = low.shape[2]
+    first = nodes // CHUNK
+
+    def grad_of(ref, m):
+        grads[m] = (ref[m].astype(jnp.float32) * scale[...]).astype(jnp.bfloat16)
         return grads[m]
 
-    scatter(low, high, grad_of, [first + slot for slot in EARLY], total)
-    for index, slot in enumerate(EARLY):
-        held[place_of(slot, 6)] = fold(EARLY, index, rels, total)
-    to_cross[...] = held[3]
-    to_beside[0] = held[0]
-    to_beside[1] = held[4]
-    to_beside[2] = held[5]
-
-
-def late_kernel(low, high, grads, rels, to_west, to_east, total):
-    first = low.shape[2] // CHUNK
-    scatter(low, high, lambda m: grads[m], [first + slot for slot in LATE], total)
-    to_west[...] = fold(LATE, 0, rels, total)
-    to_east[...] = fold(LATE, 1, rels, total)
-
-
-def own_kernel(low, high, grads, total, recv, recv_total):
-    chunks = list(range(total.shape[0] // CHUNK))
-    scatter(low, high, lambda m: grads[m], chunks, total)
-    recv_total[...] = jnp.zeros_like(recv_total)
-
-    def step(m, carry):
-        recv_total[...] += grads[m].astype(jnp.float32)
-        return carry
-
-    lax.fori_loop(0, grads.shape[0], step, 0)
-    recv[...] = recv_total[...].T.astype(jnp.bfloat16)
-
-
-def output_kernel(tiles, feats, cots, hidden, grad_pre, w_out, w_node_v_t, updated, direct):
-    lane = lax.broadcasted_iota(jnp.int32, (1, feats.shape[1]), 1)
-    active = (lane < tiles[0] * TILE).astype(jnp.float32)
-    node_out = dot(w_out[...], hidden[...])
-    updated[...] = (feats[...].astype(jnp.float32) + active * node_out).astype(jnp.bfloat16)
-    direct[...] = cots[...].astype(jnp.float32) + dot(w_node_v_t[...], grad_pre[...])
+    chunks = [chunk_of(place, first, (1, PACK, nodes)) for place in EARLY]
+    scatter(low, high, pairs(start, slope, nodes, grad_of), chunks, total)
+    if start:
+        to_beside[0] = fold(beside, 0, 0, total)
+        to_cross[...] = fold(cross, 3, 1, total)
+        to_beside[1] = fold(west, 4, 2, total)
+        to_beside[2] = fold(east, 5, 3, total)
+
+
+def all_pairs(parts, nodes):
+    start, steps = 0, []
+    for part in parts:
+        steps += pairs(start, part, nodes, lambda ref, m: ref[m])
+        start += part.shape[1]
+    return steps
+
+
+def late_kernel(low, high, *refs):
+    *parts, west, east, to_west, to_east, total = refs
+    nodes = low.shape[2]
+    first = nodes // CHUNK
+    chunks = [jnp.bfloat16(first + SLOT_OF[place][0]) for place in LATE]
+    total[...] = jnp.zeros_like(total)
+    scatter(low, high, all_pairs(parts, nodes), chunks, total)
+    to_west[...] = fold(west, 1, 0, total)
+    to_east[...] = fold(east, 2, 1, total)
+
+
+def own_kernel(low, high, *refs):
+    *parts, total, recv = refs
+    nodes = low.shape[2]
+    chunks = [jnp.bfloat16(chunk) for chunk in range(nodes // CHUNK)]
+    total[...] = jnp.zeros_like(total)
+    scatter(low, high, all_pairs(parts, nodes), chunks, total)
+    start = 0
+    for part in parts:
+        degree, rows, _ = part.shape
+        terms = 0.0
+        for m in range(degree):
+            terms += part[m].astype(jnp.float32)
+        recv[:, start : start + rows] = terms.T.astype(jnp.bfloat16)
+        start += rows
+
+
+def output_kernel(tiles, feats, cots, w_out, w_node_v_t, *refs):
+    *parts, updated, direct = refs
+    count = len(parts) // 2
+    rows = parts[0].shape[1]
+    for k in range(count):
+        hidden, grad_pre = parts[k], parts[count + k]
+        span = slice(k * rows, (k + 1) * rows)
+        lane = lax.broadcasted_iota(jnp.int32, (1, rows), 1) + k * rows
+        active = (lane < tiles[0] * TILE).astype(jnp.float32)
+        node_out = dot(w_out[...], hidden[...])
+        new = feats[:, span].astype(jnp.float32) + active * node_out
+        updated[:, span] = new.astype(jnp.bfloat16)
+        direct[:, span] = cots[:, span].astype(jnp.float32) + dot(w_node_v_t[...], grad_pre[...])
 
 
 def add_kernel(left, more, right, west, east):
@@ -501,8 +591,6 @@
     cross = across(cross)
     west_too = shifted(west, "sub", 1)
     east_too = shifted(east, "sub", 1)
-    arrivals = [beside, west, east, cross, west_too, east_too]
-
     cots, pre, grad_hidden = call(
         functools.partial(prepare_kernel, count),
         (
@@ -515,55 +603,78 @@
         scalars=1,
     )
 
-    message, slope, rels = call(
-        forward_kernel,
-        (
-            shape((hid, nodes), bf16),
-            shape((degree, nodes, hid), bf16),
-            shape((PACK, hid), f32),
-        ),
-        [low_cols, high_cols, base, degrees, proj] + arrivals,
-        flops=2 * degree * nodes * ext_len * hid,
-        scratch=[
-            pltpu.VMEM((ext_len, hid), bf16),
-            pltpu.VMEM((nodes, hid), f32),
-            pltpu.VMEM((slots, slot_rows + PACK, hid), bf16),
-        ],
+    part_shape = shape((degree, nodes, hid), bf16)
+    part = call(
+        near_kernel,
+        part_shape,
+        [low_cols, high_cols, proj, beside],
+        flops=2 * degree * nodes * (nodes + slot_rows) * hid,
+        scratch=[pltpu.VMEM((nodes + slot_rows, hid), bf16)],
         scalars=0,
     )
-    messages = gathered(message, "ch")
-
-    hidden, grad_pre, scale = call(
-        functools.partial(node_kernel, count),
-        (
-            shape((hidden_all, nodes), bf16),
-            shape((hidden_all, nodes), bf16),
-            shape((nodes, hid), f32),
-        ),
-        [degrees] + messages + [w_msg, w_node_a, w_node_a_t, w_msg_t, pre, grad_hidden],
-        flops=6 * hidden_all * chans_all * nodes,
-        scratch=[pltpu.VMEM((hidden_all, nodes), bf16)],
+    part = call(
+        line_kernel,
+        part_shape,
+        [low_cols, high_cols, part, west, east],
+        flops=2 * degree * nodes * 2 * slot_rows * hid,
+        scratch=[pltpu.VMEM((2 * slot_rows, hid), bf16)],
         scalars=0,
     )
+    halves = 2
+    rows = nodes // halves
+    slopes, messages, hiddens, grad_pres, grads = [], [], [], [], []
+    for k in range(halves):
+        message, slope = call(
+            functools.partial(message_kernel, k * rows),
+            (shape((hid, rows), bf16), shape((degree, rows, hid), bf16)),
+            [low_cols, high_cols, base, degrees, part, cross, west_too, east_too],
+            flops=2 * degree * rows * 3 * slot_rows * hid,
+            scratch=[pltpu.VMEM((3 * slot_rows, hid), bf16), pltpu.VMEM((rows, hid), f32)],
+            scalars=0,
+        )
+        slopes.append(slope)
+        messages.append(gathered(message, "ch"))
 
     block = shape((slot_rows, hid), bf16)
-    to_cross, to_beside, grads = call(
-        early_kernel,
-        (block, shape((3, slot_rows, hid), bf16), shape((degree, nodes, hid), bf16)),
-        [low_rows, high_rows, slope, scale, rels],
-        flops=2 * degree * nodes * len(EARLY) * slot_rows * hid,
-        scratch=[
-            pltpu.VMEM((len(EARLY) * slot_rows, hid), f32),
-            pltpu.VMEM((slots, slot_rows, hid), bf16),
-        ],
-        scalars=0,
-    )
+    sums = shape((len(EARLY) * slot_rows, hid), f32)
+    grad_shape = shape((degree, rows, hid), bf16)
+    for k in range(halves):
+        hidden, grad_pre, scale = call(
+            functools.partial(node_kernel, count, k * rows),
+            (
+                shape((hidden_all, rows), bf16),
+                shape((hidden_all, rows), bf16),
+                shape((rows, hid), f32),
+            ),
+            [degrees] + messages[k] + [w_msg, w_node_a, w_node_a_t, w_msg_t, pre, grad_hidden],
+            flops=6 * hidden_all * chans_all * rows,
+            scratch=[pltpu.VMEM((hidden_all, rows), bf16)],
+            scalars=0,
+        )
+        hiddens.append(hidden)
+        grad_pres.append(grad_pre)
+        operands = [low_rows, high_rows, slopes[k], scale]
+        flops = 2 * degree * rows * len(EARLY) * slot_rows * hid
+        kernel = functools.partial(early_kernel, k * rows)
+        if k == 0:
+            grad, before = call(kernel, (grad_shape, sums), operands, flops=flops, scalars=0)
+        else:
+            to_cross, to_beside, grad = call(
+                kernel,
+                (block, shape((3, slot_rows, hid), bf16), grad_shape),
+                operands + [before, beside, cross, west_too, east_too],
+                flops=flops,
+                scratch=[pltpu.VMEM(sums.shape, f32)],
+                scalars=0,
+            )
+        grads.append(grad)
+
     from_beside = shifted(to_beside, "sub", 1)
     from_cross = across(to_cross)
     to_west, to_east = call(
         late_kernel,
         (block, block),
-        [low_rows, high_rows, grads, rels],
+        [low_rows, high_rows] + grads + [west, east],
         flops=2 * degree * nodes * len(LATE) * slot_rows * hid,
         scratch=[pltpu.VMEM((len(LATE) * slot_rows, hid), f32)],
         scalars=0,
@@ -577,15 +688,14 @@
     own, grad_recv = call(
         own_kernel,
         (shape((nodes, hid), f32), shape((hid, nodes), bf16)),
-        [low_rows, high_rows, grads],
+        [low_rows, high_rows] + grads,
         flops=2 * degree * nodes * nodes * hid,
-        scratch=[pltpu.VMEM((nodes, hid), f32)],
         scalars=0,
     )
     updated, direct = call(
         output_kernel,
         (shape((chans, nodes), bf16), shape((chans, nodes), f32)),
-        [tile_count, features_held, cotangent_held, hidden, grad_pre, w_out_my, w_node_v_t],
+        [tile_count, features_held, cotangent_held, w_out_my, w_node_v_t] + hiddens + grad_pres,
         flops=4 * hidden_all * chans * nodes,
         scalars=1,
     )

time: 84.8 us -> 81.3 us (0.959)
  waiting for transfers between devices: 26.3 us -> 15.7 us
  starting transfers between devices: 16.6 us -> 21.7 us
  local copies, waits for them, and re-layouts: 11.5 us -> 12.4 us
    ppermute x2, waiting for transfers between devices: 6.2 us -> 0.88 us  [shards(): across = lambda block: lax.ppermute(block, cycle, across_route)]
    ppermute x16 -> x17, waiting for transfers between devices: 20.1 us -> 14.8 us  [shifted(): return lax.ppermute(block, axis, route)]
    ppermute x2, starting transfers between devices: 0.95 us -> 4.42 us  [shards(): across = lambda block: lax.ppermute(block, cycle, across_route)]
    ppermute x16 -> x17, starting transfers between devices: 15.6 us -> 17.3 us  [shifted(): return lax.ppermute(block, axis, route)]
    unnamed x24 -> x28, local copies, waits for them, and re-layouts: 11.5 us -> 12.4 us
    pallas_call x13 -> x18, Pallas kernels: 27.7 us -> 28.5 us  [call(): pl.pallas_call(kernel, out_shape=out_shape, in_specs=[smem] * scalars + [...]
  transfers between devices with their start and end apart: 18 -> 19, of which waited for: 10 -> 9; matrix products, arithmetic and copies ran while one was open for 2% -> 2% of each run, Pallas kernels for 23% -> 28%
where the time goes in v4:
time: 81.3 us; the launch traced here: 80.6 us
  Pallas kernels  28.5 us (35%)
  starting transfers between devices  21.7 us (27%)
  waiting for transfers between devices  15.7 us (19%)
  local copies, waits for them, and re-layouts  12.4 us (15%)
  between operations  1.47 us (2%)
    pallas_call x18, Pallas kernels, call(): pl.pallas_call(kernel, out_shape=out_shape, in_specs=[smem] * scalars + [...  28.5 us
    ppermute x17, starting transfers between devices, shifted(): return lax.ppermute(block, axis, route)  17.3 us
    ppermute x17, waiting for transfers between devices, shifted(): return lax.ppermute(block, axis, route)  14.8 us
    unnamed x28, local copies, waits for them, and re-layouts  12.4 us
    ppermute x2, starting transfers between devices, shards(): across = lambda block: lax.ppermute(block, cycle, across_route)  4.42 us
  transfers between devices with their start and end apart: 19, of which 9 were waited for; matrix products, arithmetic and copies ran while one was open for 2% of the time, Pallas kernels for 28%

profile of v4, /device:TPU:0, one launch (start us, length us, event | category | flops | bytes accessed | tf_op | source)
XLA Modules:
  0.0 80.6 jit_solution(13322029595536546847)
XLA Ops:
  0.6 3.0 %collective-permute-start = (bf16[256,512]{1,0:T(8,128)(2,1)}, bf16[256,512]{1,0:T(8,128)(2,1)S(1)}, u32[]{:S(2)}, u32[]{:S(2)}) collective-permute-start(bf16[256,512]{1,0:T(8,128)(2,1)} %refs_8_.1), channel_id=1, source_target_pairs={{2,0},{0,2},{3,1},{1,3},{6,4},{4,6},{7,5},{5,7},{10,8},{8,10},{11,... | collective-permute-start | bytes 786440 | tf_op jit(solution)/shard_map/ppermute | solution.py:25
  5.1 1.0 %copy-done = bf16[512,512]{1,0:T(8,128)(2,1)S(1)} copy-done((bf16[512,512]{1,0:T(8,128)(2,1)S(1)}, bf16[512,512]{1,0:T(8,128)(2,1)}, u32[]{:S(2)}) %copy-start) | copy-done | bytes 524312
  6.1 1.0 %copy-done.1 = bf16[512,512]{1,0:T(8,128)(2,1)S(1)} copy-done((bf16[512,512]{1,0:T(8,128)(2,1)S(1)}, bf16[512,512]{1,0:T(8,128)(2,1)}, u32[]{:S(2)}) %copy-start.1) | copy-done | bytes 524312
  7.1 1.0 %copy-done.2 = bf16[512,512]{1,0:T(8,128)(2,1)S(1)} copy-done((bf16[512,512]{1,0:T(8,128)(2,1)S(1)}, bf16[512,512]{1,0:T(8,128)(2,1)}, u32[]{:S(2)}) %copy-start.2) | copy-done | bytes 524312
  8.2 1.0 %copy-done.3 = bf16[512,512]{1,0:T(8,128)(2,1)S(1)} copy-done((bf16[512,512]{1,0:T(8,128)(2,1)S(1)}, bf16[512,512]{1,0:T(8,128)(2,1)}, u32[]{:S(2)}) %copy-start.3) | copy-done | bytes 524312
  9.2 1.0 %copy-done.4 = bf16[512,512]{1,0:T(8,128)(2,1)S(1)} copy-done((bf16[512,512]{1,0:T(8,128)(2,1)S(1)}, bf16[512,512]{1,0:T(8,128)(2,1)}, u32[]{:S(2)}) %copy-start.4) | copy-done | bytes 524312
  10.3 1.0 %copy-done.5 = bf16[512,512]{1,0:T(8,128)(2,1)S(1)} copy-done((bf16[512,512]{1,0:T(8,128)(2,1)S(1)}, bf16[512,512]{1,0:T(8,128)(2,1)}, u32[]{:S(2)}) %copy-start.5) | copy-done | bytes 524312
  16.0 2.8 %shard_map.157 = (bf16[256,512]{1,0:T(8,128)(2,1)S(1)}, bf16[256,512]{1,0:T(8,128)(2,1)S(1)}, bf16[512,512]{1,0:T(8,128)(2,1)S(1)}, bf16[512,512]{1,0:T(8,128)(2...) custom-call(s32[1]{0:T(128)S(6)} %copy.20.tiles, ...), custom_call_target="tpu_custom_call" | custom-call | flops 536870912 | bytes 3700788 | tf_op jit(solution)/shard_map/pallas_call | solution.py:51
  18.8 1.5 %shard_map.158 = (bf16[512,512]{1,0:T(8,128)(2,1)S(1)}, bf16[512,256]{1,0:T(8,128)(2,1)S(1)}, f32[512,256]{1,0:T(8,128)S(1)}, bf16[272,256]{1,0:T(8,128)(2,1)S(1...) custom-call(s32[1]{0:T(128)S(6)} %copy.20.tiles, ...), custom_call_target="tpu_custom_call" | custom-call | flops 268435456 | bytes 1050676 | tf_op jit(solution)/shard_map/pallas_call | solution.py:51
  20.3 1.6 %collective-permute-start.2 = (bf16[272,256]{1,0:T(8,128)(2,1)S(1)}, bf16[272,256]{1,0:T(8,128)(2,1)S(1)}, u32[]{:S(2)}, u32[]{:S(2)}) collective-permute-start(bf16[272,256]{1,0:T(8,128)(2,1)S(1)} %get-tuple-element.75), channel_id=1, source_target_pairs={{12,0},{0,4},{4,8},{8,12},{13,1},{1,5},{5,9},{9,13},{14,2},{2,6},{... | collective-permute-start | bytes 417800 | tf_op jit(solution)/shard_map/ppermute | solution.py:25
  22.0 2.3 %collective-permute-start.3 = (bf16[272,256]{1,0:T(8,128)(2,1)S(1)}, bf16[272,256]{1,0:T(8,128)(2,1)S(1)}, u32[]{:S(2)}, u32[]{:S(2)}) collective-permute-start(bf16[272,256]{1,0:T(8,128)(2,1)S(1)} %get-tuple-element.76), channel_id=1, source_target_pairs={{4,0},{8,4},{12,8},{0,12},{5,1},{9,5},{13,9},{1,13},{6,2},{10,6},{... | collective-permute-start | bytes 417800 | tf_op jit(solution)/shard_map/ppermute | solution.py:25
  25.4 3.4 %collective-permute-done.2.west.refs_2_ = bf16[272,256]{1,0:T(8,128)(2,1)S(1)} collective-permute-done((bf16[272,256]{1,0:T(8,128)(2,1)S(1)}, bf16[272,256]{1,0:T(8,128)(2,1)S(1)}, u32[]{:S(2)}, u32[]{:S(2)}) %collective-permute-start.2) | collective-permute-done | bytes 139296 | tf_op jit(solution)/shard_map/ppermute | solution.py:25
  29.8 2.8 %shard_map.159.before = bf16[12,512,256]{2,1,0:T(8,128)(2,1)S(1)} custom-call(bf16[12,512,128]{2,1,0:T(8,128)(2,1)S(1)} %get-tuple-element.67.low, bf16[12,512,128]{2,1,0:T(8,128)(2,1)S(1)} %get-tuple-element.68.high, bf16[512,256]{1,0:T(8,128)(2,1)S(1)} %get-tuple-element.73.proj, bf16[272,256]{1,0:T(8,128)(2,1)S(1)} %collective-permute-done.1.beside.refs_1_), custom_call_target="tpu_custom_call" | custom-call | flops 2415919104 | bytes 3547136 | tf_op jit(solution)/shard_map/pallas_call | solution.py:51
  32.7 2.5 %shard_map.160.part = bf16[12,512,256]{2,1,0:T(8,128)(2,1)S(1)} custom-call(bf16[12,512,128]{2,1,0:T(8,128)(2,1)S(1)} %get-tuple-element.67.low, bf16[12,512,128]{2,1,0:T(8,128)(2,1)S(1)} %get-tuple-element.68.high, bf16[12,512,256]{2,1,0:T(8,128)(2,1)S(1)} %shard_map.159.before, bf16[272,256]{1,0:T(8,128)(2,1)S(1)} %collective-permute-done.2.west.refs_2_, ...), custom_call_target="tpu_custom_call" | custom-call | flops 1610612736 | bytes 6569984 | tf_op jit(solution)/shard_map/pallas_call | solution.py:51
  36.1 2.5 %shard_map.161 = (bf16[256,256]{1,0:T(8,128)(2,1)S(1)}, bf16[12,256,256]{2,1,0:T(8,128)(2,1)S(1)}) custom-call(bf16[12,512,128]{2,1,0:T(8,128)(2,1)S(1)} %get-tuple-element.67.low, bf16[12,512,128]{2,1,0:T(8,128)(2,1)S(1)} %get-tuple-element.68.high, f32[512,256]{1,0:T(8,128)S(1)} %get-tuple-element.72.base, s32[1,512]{1,0:T(1,128)S(1)} %get-tuple-element.66.in_degree, ...), custom_call_target="tpu_custom_call" | custom-call | flops 1207959552 | bytes 7235584 | tf_op jit(solution)/shard_map/pallas_call | solution.py:51
  39.3 1.1 %shard_map.162 = (bf16[512,512]{1,0:T(8,128)(2,1)}, f32[512,512]{1,0:T(8,128)S(1)}, f32[512,512]{1,0:T(8,128)S(1)}) custom-call(s32[1]{0:T(128)S(6)} %copy.20.tiles, bf16[256,512]{1,0:T(8,128)(2,1)S(1)} %get-tuple-element.63.refs_0_.cots, bf16[256,512]{1,0:T(8,128)(2,1)S(1)} %collective-permute-done.8.refs_1_, ...), custom_call_target="tpu_custom_call" | custom-call | flops 536870912 | bytes 2099204 | tf_op jit(solution)/shard_map/pallas_call | solution.py:51
  40.4 2.5 %shard_map.164 = (bf16[256,256]{1,0:T(8,128)(2,1)S(1)}, bf16[12,256,256]{2,1,0:T(8,128)(2,1)S(1)}) custom-call(bf16[12,512,128]{2,1,0:T(8,128)(2,1)S(1)} %get-tuple-element.67.low, bf16[12,512,128]{2,1,0:T(8,128)(2,1)S(1)} %get-tuple-element.68.high, f32[512,256]{1,0:T(8,128)S(1)} %get-tuple-element.72.base, s32[1,512]{1,0:T(1,128)S(1)} %get-tuple-element.66.in_degree, ...), custom_call_target="tpu_custom_call" | custom-call | flops 1207959552 | bytes 7235584 | tf_op jit(solution)/shard_map/pallas_call | solution.py:51
  42.9 1.4 %collective-permute-start.9 = (bf16[256,256]{1,0:T(8,128)(2,1)S(1)}, bf16[256,256]{1,0:T(8,128)(2,1)S(1)}, u32[]{:S(2)}, u32[]{:S(2)}) collective-permute-start(bf16[256,256]{1,0:T(8,128)(2,1)S(1)} %get-tuple-element.90.refs_0_), channel_id=1, source_target_pairs={{2,0},{0,2},{3,1},{1,3},{6,4},{4,6},{7,5},{5,7},{10,8},{8,10},{11,... | collective-permute-start | bytes 393224 | tf_op jit(solution)/shard_map/ppermute | solution.py:25
  44.3 1.3 %shard_map.163 = (bf16[512,256]{1,0:T(8,128)(2,1)S(1)}, bf16[512,256]{1,0:T(8,128)(2,1)S(1)}, f32[256,256]{1,0:T(8,128)S(1)}) custom-call(s32[1,512]{1,0:T(1,128)S(1)} %get-tuple-element.66.in_degree, bf16[256,256]{1,0:T(8,128)(2,1)S(1)} %get-tuple-element.78.refs_0_, bf16[256,256]{1,0:T(8,128)(2,1)S(1)} %collective-permute-done.7.refs_1_, ...), custom_call_target="tpu_custom_call" | custom-call | flops 402653184 | bytes 4196352 | tf_op jit(solution)/shard_map/pallas_call | solution.py:51
  45.7 2.1 %shard_map.167 = (bf16[12,256,256]{2,1,0:T(8,128)(2,1)S(1)}, f32[1024,256]{1,0:T(8,128)S(1)}) custom-call(bf16[12,16,512]{2,1,0:T(8,128)(2,1)S(1)} %get-tuple-element.95.low, bf16[12,16,512]{2,1,0:T(8,128)(2,1)S(1)} %get-tuple-element.96.high, bf16[12,256,256]{2,1,0:T(8,128)(2,1)S(1)} %get-tuple-element.97.slope, f32[256,256]{1,0:T(8,128)S(1)} %get-tuple-element.98.scale), custom_call_target="tpu_custom_call" | custom-call | flops 1610612736 | bytes 2228224 | tf_op jit(solution)/shard_map/pallas_call | solution.py:51
  48.2 1.3 %shard_map.165 = (bf16[512,256]{1,0:T(8,128)(2,1)S(1)}, bf16[512,256]{1,0:T(8,128)(2,1)S(1)}, f32[256,256]{1,0:T(8,128)S(1)}) custom-call(s32[1,512]{1,0:T(1,128)S(1)} %get-tuple-element.66.in_degree, bf16[256,256]{1,0:T(8,128)(2,1)S(1)} %get-tuple-element.90.refs_0_, bf16[256,256]{1,0:T(8,128)(2,1)S(1)} %collective-permute-done.9.refs_1_, ...), custom_call_target="tpu_custom_call" | custom-call | flops 402653184 | bytes 4196352 | tf_op jit(solution)/shard_map/pallas_call | solution.py:51
  49.5 1.9 %shard_map.168 = (bf16[256,256]{1,0:T(8,128)(2,1)S(1)}, bf16[3,256,256]{2,1,0:T(8,128)(2,1)S(1)}, bf16[12,256,256]{2,1,0:T(8,128)(2,1)S(1)}) custom-call(bf16[12,16,512]{2,1,0:T(8,128)(2,1)S(1)} %get-tuple-element.95.low, bf16[12,16,512]{2,1,0:T(8,128)(2,1)S(1)} %get-tuple-element.96.high, bf16[12,256,256]{2,1,0:T(8,128)(2,1)S(1)} %get-tuple-element.100.slope, ...), custom_call_target="tpu_custom_call" | custom-call | flops 1610612736 | bytes 3833856 | tf_op jit(solution)/shard_map/pallas_call | solution.py:51
  51.5 3.8 %collective-permute-start.13 = (bf16[256,256]{1,0:T(8,128)(2,1)S(1)}, bf16[256,256]{1,0:T(8,128)(2,1)S(1)}, u32[]{:S(2)}, u32[]{:S(2)}) collective-permute-start(bf16[256,256]{1,0:T(8,128)(2,1)S(1)} %get-tuple-element.114), channel_id=1, source_target_pairs={{0,9},{1,8},{4,13},{5,12},{8,1},{9,0},{12,5},{13,4},{2,11},{3,10},... | collective-permute-start | bytes 393224 | tf_op jit(solution)/shard_map/ppermute | solution.py:530
  55.3 1.2 %shard_map.166 = (bf16[256,512]{1,0:T(8,128)(2,1)}, f32[256,512]{1,0:T(8,128)S(1)}) custom-call(s32[1]{0:T(128)S(6)} %copy.20.tiles, bf16[256,512]{1,0:T(8,128)(2,1)S(1)} %get-tuple-element.62.refs_0_.feats, bf16[256,512]{1,0:T(8,128)(2,1)S(1)} %get-tuple-element.63.refs_0_.cots, bf16[256,512]{1,0:T(8,128)(2,1)S(1)} %get-tuple-element.64.w_out, ...), custom_call_target="tpu_custom_call" | custom-call | flops 268435456 | bytes 2097156 | tf_op jit(solution)/shard_map/pallas_call | solution.py:51
  56.4 1.8 %shard_map.170 = (bf16[256,256]{1,0:T(8,128)(2,1)S(1)}, bf16[256,256]{1,0:T(8,128)(2,1)S(1)}) custom-call(bf16[12,16,512]{2,1,0:T(8,128)(2,1)S(1)} %get-tuple-element.95.low, bf16[12,16,512]{2,1,0:T(8,128)(2,1)S(1)} %get-tuple-element.96.high, bf16[12,256,256]{2,1,0:T(8,128)(2,1)S(1)} %get-tuple-element.99.refs_0_, ...), custom_call_target="tpu_custom_call" | custom-call | flops 1610612736 | bytes 3817472 | tf_op jit(solution)/shard_map/pallas_call | solution.py:51
  58.3 2.4 %collective-permute-start.11 = (bf16[256,256]{1,0:T(8,128)(2,1)S(1)}, bf16[256,256]{1,0:T(8,128)(2,1)S(1)}, u32[]{:S(2)}, u32[]{:S(2)}) collective-permute-start(bf16[256,256]{1,0:T(8,128)(2,1)S(1)} %get-tuple-element.112), channel_id=1, source_target_pairs={{4,0},{8,4},{12,8},{0,12},{5,1},{9,5},{13,9},{1,13},{6,2},{10,6},{... | collective-permute-start | bytes 393224 | tf_op jit(solution)/shard_map/ppermute | solution.py:25
  60.7 2.1 %shard_map.169 = (f32[512,256]{1,0:T(8,128)S(1)}, bf16[256,512]{1,0:T(8,128)(2,1)S(1)}) custom-call(bf16[12,16,512]{2,1,0:T(8,128)(2,1)S(1)} %get-tuple-element.95.low, bf16[12,16,512]{2,1,0:T(8,128)(2,1)S(1)} %get-tuple-element.96.high, bf16[12,256,256]{2,1,0:T(8,128)(2,1)S(1)} %get-tuple-element.99.refs_0_, ...), custom_call_target="tpu_custom_call" | custom-call | flops 1610612736 | bytes 3538944 | tf_op jit(solution)/shard_map/pallas_call | solution.py:51
  62.8 1.8 %collective-permute-done.11.upper = bf16[256,256]{1,0:T(8,128)(2,1)S(1)} collective-permute-done((bf16[256,256]{1,0:T(8,128)(2,1)S(1)}, bf16[256,256]{1,0:T(8,128)(2,1)S(1)}, u32[]{:S(2)}, u32[]{:S(2)}) %collective-permute-start.11) | collective-permute-done | bytes 131104 | tf_op jit(solution)/shard_map/ppermute | solution.py:25
  64.6 3.1 %collective-permute-done.12.lower = bf16[256,256]{1,0:T(8,128)(2,1)S(1)} collective-permute-done((bf16[256,256]{1,0:T(8,128)(2,1)S(1)}, bf16[256,256]{1,0:T(8,128)(2,1)S(1)}, u32[]{:S(2)}, u32[]{:S(2)}) %collective-permute-start.12) | collective-permute-done | bytes 131104 | tf_op jit(solution)/shard_map/ppermute | solution.py:25
  68.8 1.6 %collective-permute-start.14 = (bf16[256,512]{1,0:T(8,128)(2,1)S(1)}, bf16[256,512]{1,0:T(8,128)(2,1)S(1)}, u32[]{:S(2)}, u32[]{:S(2)}) collective-permute-start(bf16[256,512]{1,0:T(8,128)(2,1)S(1)} %bitcast.13), channel_id=1, source_target_pairs={{2,0},{0,2},{3,1},{1,3},{6,4},{4,6},{7,5},{5,7},{10,8},{8,10},{11,... | collective-permute-start | bytes 786440 | tf_op jit(solution)/shard_map/ppermute | solution.py:25
  70.5 2.5 %collective-permute-start.18 = (bf16[64,256]{1,0:T(8,128)(2,1)S(1)}, bf16[64,256]{1,0:T(8,128)(2,1)S(1)}, u32[]{:S(2)}, u32[]{:S(2)}) collective-permute-start(bf16[64,256]{1,0:T(8,128)(2,1)S(1)} %get-tuple-element.124), channel_id=1, source_target_pairs={{4,0},{8,4},{12,8},{0,12},{5,1},{9,5},{13,9},{1,13},{6,2},{10,6},{... | collective-permute-start | bytes 98312 | tf_op jit(solution)/shard_map/ppermute | solution.py:25
  74.6 3.4 %collective-permute-done.17.refs_1_ = bf16[64,256]{1,0:T(8,128)(2,1)S(1)} collective-permute-done((bf16[64,256]{1,0:T(8,128)(2,1)S(1)}, bf16[64,256]{1,0:T(8,128)(2,1)S(1)}, u32[]{:S(2)}, u32[]{:S(2)}) %collective-permute-start.17) | collective-permute-done | bytes 32800 | tf_op jit(solution)/shard_map/ppermute | solution.py:25
  (54 shorter events, 15.2 us)
Async XLA Ops:
  0.6 18.2 %collective-permute-start = (bf16[256,512]{1,0:T(8,128)(2,1)}, bf16[256,512]{1,0:T(8,128)(2,1)S(1)}, u32[]{:S(2)}, u32[]{:S(2)}) collective-permute-start(bf16[256,512]{1,0:T(8,128)(2,1)} %refs_8_.1), channel_id=1, source_target_pairs={{2,0},{0,2},{3,1},{1,3},{6,4},{4,6},{7,5},{5,7},{10,8},{8,10},{11,... | collective-permute-start | bytes 786440 | tf_op jit(solution)/shard_map/ppermute | solution.py:25
  5.1 1.0 %copy-start = (bf16[512,512]{1,0:T(8,128)(2,1)S(1)}, bf16[512,512]{1,0:T(8,128)(2,1)}, u32[]{:S(2)}) copy-start(bf16[512,512]{1,0:T(8,128)(2,1)} %refs_0_.1) | copy-start | bytes 1572868
  6.1 1.0 %copy-start.1 = (bf16[512,512]{1,0:T(8,128)(2,1)S(1)}, bf16[512,512]{1,0:T(8,128)(2,1)}, u32[]{:S(2)}) copy-start(bf16[512,512]{1,0:T(8,128)(2,1)} %refs_1_.1) | copy-start | bytes 1572868
  7.1 1.0 %copy-start.2 = (bf16[512,512]{1,0:T(8,128)(2,1)S(1)}, bf16[512,512]{1,0:T(8,128)(2,1)}, u32[]{:S(2)}) copy-start(bf16[512,512]{1,0:T(8,128)(2,1)} %refs_2_.1) | copy-start | bytes 1572868
  8.2 1.0 %copy-start.3 = (bf16[512,512]{1,0:T(8,128)(2,1)S(1)}, bf16[512,512]{1,0:T(8,128)(2,1)}, u32[]{:S(2)}) copy-start(bf16[512,512]{1,0:T(8,128)(2,1)} %refs_3_.1) | copy-start | bytes 1572868
  9.2 1.0 %copy-start.4 = (bf16[512,512]{1,0:T(8,128)(2,1)S(1)}, bf16[512,512]{1,0:T(8,128)(2,1)}, u32[]{:S(2)}) copy-start(bf16[512,512]{1,0:T(8,128)(2,1)} %refs_4_.1) | copy-start | bytes 1572868
  10.3 1.0 %copy-start.5 = (bf16[512,512]{1,0:T(8,128)(2,1)S(1)}, bf16[512,512]{1,0:T(8,128)(2,1)}, u32[]{:S(2)}) copy-start(bf16[512,512]{1,0:T(8,128)(2,1)} %refs_5_.1) | copy-start | bytes 1572868
  11.3 0.9 %copy-start.6 = (bf16[256,512]{1,0:T(8,128)(2,1)S(1)}, bf16[256,512]{1,0:T(8,128)(2,1)}, u32[]{:S(2)}) copy-start(bf16[256,512]{1,0:T(8,128)(2,1)} %refs_8_.1) | copy-start | bytes 786436
  12.3 0.9 %copy-start.7 = (bf16[256,512]{1,0:T(8,128)(2,1)S(1)}, bf16[256,512]{1,0:T(8,128)(2,1)}, u32[]{:S(2)}) copy-start(bf16[256,512]{1,0:T(8,128)(2,1)} %refs_9_.1) | copy-start | bytes 786436
  13.2 0.8 copy-start.9
  14.0 0.7 copy-start.10
  14.6 0.7 copy-start.11
  15.3 0.7 copy-start.12
  16.0 8.2 %copy-start.8 = (bf16[256,512]{1,0:T(8,128)(2,1)S(1)}, bf16[256,512]{1,0:T(8,128)(2,1)}, u32[]{:S(2)}) copy-start(bf16[256,512]{1,0:T(8,128)(2,1)} %refs_9_.1) | copy-start | bytes 786436
  20.3 8.4 %collective-permute-start.2 = (bf16[272,256]{1,0:T(8,128)(2,1)S(1)}, bf16[272,256]{1,0:T(8,128)(2,1)S(1)}, u32[]{:S(2)}, u32[]{:S(2)}) collective-permute-start(bf16[272,256]{1,0:T(8,128)(2,1)S(1)} %get-tuple-element.75), channel_id=1, source_target_pairs={{12,0},{0,4},{4,8},{8,12},{13,1},{1,5},{5,9},{9,13},{14,2},{2,6},{... | collective-permute-start | bytes 417800 | tf_op jit(solution)/shard_map/ppermute | solution.py:25
  22.0 7.8 %collective-permute-start.3 = (bf16[272,256]{1,0:T(8,128)(2,1)S(1)}, bf16[272,256]{1,0:T(8,128)(2,1)S(1)}, u32[]{:S(2)}, u32[]{:S(2)}) collective-permute-start(bf16[272,256]{1,0:T(8,128)(2,1)S(1)} %get-tuple-element.76), channel_id=1, source_target_pairs={{4,0},{8,4},{12,8},{0,12},{5,1},{9,5},{13,9},{1,13},{6,2},{10,6},{... | collective-permute-start | bytes 417800 | tf_op jit(solution)/shard_map/ppermute | solution.py:25
  24.2 5.6 %collective-permute-start.1 = (bf16[272,256]{1,0:T(8,128)(2,1)S(1)}, bf16[272,256]{1,0:T(8,128)(2,1)S(1)}, u32[]{:S(2)}, u32[]{:S(2)}) collective-permute-start(bf16[272,256]{1,0:T(8,128)(2,1)S(1)} %get-tuple-element.74), channel_id=1, source_target_pairs={{1,0},{0,1},{3,2},{2,3},{5,4},{4,5},{7,6},{6,7},{9,8},{8,9},{11,10... | collective-permute-start | bytes 417800 | tf_op jit(solution)/shard_map/ppermute | solution.py:25
  24.2 15.1 %collective-permute-start.8 = (bf16[256,512]{1,0:T(8,128)(2,1)S(1)}, bf16[256,512]{1,0:T(8,128)(2,1)S(1)}, u32[]{:S(2)}, u32[]{:S(2)}) collective-permute-start(bf16[256,512]{1,0:T(8,128)(2,1)S(1)} %copy-done.8), channel_id=1, source_target_pairs={{2,0},{0,2},{3,1},{1,3},{6,4},{4,6},{7,5},{5,7},{10,8},{8,10},{11,... | collective-permute-start | bytes 786440 | tf_op jit(solution)/shard_map/ppermute | solution.py:25
  24.8 11.3 %collective-permute-start.4 = (bf16[272,256]{1,0:T(8,128)(2,1)S(1)}, bf16[272,256]{1,0:T(8,128)(2,1)S(1)}, u32[]{:S(2)}, u32[]{:S(2)}) collective-permute-start(bf16[272,256]{1,0:T(8,128)(2,1)S(1)} %get-tuple-element.77), channel_id=1, source_target_pairs={{0,9},{1,8},{4,13},{5,12},{8,1},{9,0},{12,5},{13,4},{2,11},{3,10},... | collective-permute-start | bytes 417800 | tf_op jit(solution)/shard_map/ppermute | solution.py:530
  28.8 7.3 %collective-permute-start.5 = (bf16[272,256]{1,0:T(8,128)(2,1)S(1)}, bf16[272,256]{1,0:T(8,128)(2,1)S(1)}, u32[]{:S(2)}, u32[]{:S(2)}) collective-permute-start(bf16[272,256]{1,0:T(8,128)(2,1)S(1)} %collective-permute-done.2.west.refs_2_), channel_id=1, source_target_pairs={{1,0},{0,1},{3,2},{2,3},{5,4},{4,5},{7,6},{6,7},{9,8},{8,9},{11,10... | collective-permute-start | bytes 417800 | tf_op jit(solution)/shard_map/ppermute | solution.py:25
  29.8 6.3 %collective-permute-start.6 = (bf16[272,256]{1,0:T(8,128)(2,1)S(1)}, bf16[272,256]{1,0:T(8,128)(2,1)S(1)}, u32[]{:S(2)}, u32[]{:S(2)}) collective-permute-start(bf16[272,256]{1,0:T(8,128)(2,1)S(1)} %collective-permute-done.3.east.refs_3_), channel_id=1, source_target_pairs={{1,0},{0,1},{3,2},{2,3},{5,4},{4,5},{7,6},{6,7},{9,8},{8,9},{11,10... | collective-permute-start | bytes 417800 | tf_op jit(solution)/shard_map/ppermute | solution.py:25
  38.6 5.7 %collective-permute-start.7 = (bf16[256,256]{1,0:T(8,128)(2,1)S(1)}, bf16[256,256]{1,0:T(8,128)(2,1)S(1)}, u32[]{:S(2)}, u32[]{:S(2)}) collective-permute-start(bf16[256,256]{1,0:T(8,128)(2,1)S(1)} %get-tuple-element.78.refs_0_), channel_id=1, source_target_pairs={{2,0},{0,2},{3,1},{1,3},{6,4},{4,6},{7,5},{5,7},{10,8},{8,10},{11,... | collective-permute-start | bytes 393224 | tf_op jit(solution)/shard_map/ppermute | solution.py:25
  42.9 5.3 %collective-permute-start.9 = (bf16[256,256]{1,0:T(8,128)(2,1)S(1)}, bf16[256,256]{1,0:T(8,128)(2,1)S(1)}, u32[]{:S(2)}, u32[]{:S(2)}) collective-permute-start(bf16[256,256]{1,0:T(8,128)(2,1)S(1)} %get-tuple-element.90.refs_0_), channel_id=1, source_target_pairs={{2,0},{0,2},{3,1},{1,3},{6,4},{4,6},{7,5},{5,7},{10,8},{8,10},{11,... | collective-permute-start | bytes 393224 | tf_op jit(solution)/shard_map/ppermute | solution.py:25
  51.4 6.9 %collective-permute-start.10 = (bf16[3,256,256]{2,1,0:T(8,128)(2,1)S(1)}, bf16[3,256,256]{2,1,0:T(8,128)(2,1)S(1)}, u32[]{:S(2)}, u32[]{:S(2)}) collective-permute-start(bf16[3,256,256]{2,1,0:T(8,128)(2,1)S(1)} %get-tuple-element.110), channel_id=1, source_target_pairs={{1,0},{0,1},{3,2},{2,3},{5,4},{4,5},{7,6},{6,7},{9,8},{8,9},{11,10... | collective-permute-start | bytes 1179656 | tf_op jit(solution)/shard_map/ppermute | solution.py:25
  51.5 11.3 %collective-permute-start.13 = (bf16[256,256]{1,0:T(8,128)(2,1)S(1)}, bf16[256,256]{1,0:T(8,128)(2,1)S(1)}, u32[]{:S(2)}, u32[]{:S(2)}) collective-permute-start(bf16[256,256]{1,0:T(8,128)(2,1)S(1)} %get-tuple-element.114), channel_id=1, source_target_pairs={{0,9},{1,8},{4,13},{5,12},{8,1},{9,0},{12,5},{13,4},{2,11},{3,10},... | collective-permute-start | bytes 393224 | tf_op jit(solution)/shard_map/ppermute | solution.py:530
  58.3 6.3 %collective-permute-start.11 = (bf16[256,256]{1,0:T(8,128)(2,1)S(1)}, bf16[256,256]{1,0:T(8,128)(2,1)S(1)}, u32[]{:S(2)}, u32[]{:S(2)}) collective-permute-start(bf16[256,256]{1,0:T(8,128)(2,1)S(1)} %get-tuple-element.112), channel_id=1, source_target_pairs={{4,0},{8,4},{12,8},{0,12},{5,1},{9,5},{13,9},{1,13},{6,2},{10,6},{... | collective-permute-start | bytes 393224 | tf_op jit(solution)/shard_map/ppermute | solution.py:25
  60.7 7.1 %collective-permute-start.12 = (bf16[256,256]{1,0:T(8,128)(2,1)S(1)}, bf16[256,256]{1,0:T(8,128)(2,1)S(1)}, u32[]{:S(2)}, u32[]{:S(2)}) collective-permute-start(bf16[256,256]{1,0:T(8,128)(2,1)S(1)} %get-tuple-element.113), channel_id=1, source_target_pairs={{12,0},{0,4},{4,8},{8,12},{13,1},{1,5},{5,9},{9,13},{14,2},{2,6},{... | collective-permute-start | bytes 393224 | tf_op jit(solution)/shard_map/ppermute | solution.py:25
  68.7 1.7 %collective-permute-start.15 = (bf16[4,64,256]{2,1,0:T(8,128)(2,1)S(1)}, bf16[4,64,256]{2,1,0:T(8,128)(2,1)S(1)}, u32[]{:S(2)}, u32[]{:S(2)}) collective-permute-start(bf16[4,64,256]{2,1,0:T(8,128)(2,1)S(1)} %get-tuple-element.118), channel_id=1, source_target_pairs={{1,0},{0,1},{3,2},{2,3},{5,4},{4,5},{7,6},{6,7},{9,8},{8,9},{11,10... | collective-permute-start | bytes 393224 | tf_op jit(solution)/shard_map/ppermute | solution.py:25
  68.8 11.0 %collective-permute-start.14 = (bf16[256,512]{1,0:T(8,128)(2,1)S(1)}, bf16[256,512]{1,0:T(8,128)(2,1)S(1)}, u32[]{:S(2)}, u32[]{:S(2)}) collective-permute-start(bf16[256,512]{1,0:T(8,128)(2,1)S(1)} %bitcast.13), channel_id=1, source_target_pairs={{2,0},{0,2},{3,1},{1,3},{6,4},{4,6},{7,5},{5,7},{10,8},{8,10},{11,... | collective-permute-start | bytes 786440 | tf_op jit(solution)/shard_map/ppermute | solution.py:25
  70.5 4.1 %collective-permute-start.18 = (bf16[64,256]{1,0:T(8,128)(2,1)S(1)}, bf16[64,256]{1,0:T(8,128)(2,1)S(1)}, u32[]{:S(2)}, u32[]{:S(2)}) collective-permute-start(bf16[64,256]{1,0:T(8,128)(2,1)S(1)} %get-tuple-element.124), channel_id=1, source_target_pairs={{4,0},{8,4},{12,8},{0,12},{5,1},{9,5},{13,9},{1,13},{6,2},{10,6},{... | collective-permute-start | bytes 98312 | tf_op jit(solution)/shard_map/ppermute | solution.py:25
  72.9 5.1 %collective-permute-start.17 = (bf16[64,256]{1,0:T(8,128)(2,1)S(1)}, bf16[64,256]{1,0:T(8,128)(2,1)S(1)}, u32[]{:S(2)}, u32[]{:S(2)}) collective-permute-start(bf16[64,256]{1,0:T(8,128)(2,1)S(1)} %get-tuple-element.125), channel_id=1, source_target_pairs={{8,0},{12,4},{0,8},{4,12},{9,1},{13,5},{1,9},{5,13},{10,2},{14,6},... | collective-permute-start | bytes 98312 | tf_op jit(solution)/shard_map/ppermute | solution.py:25
  73.3 5.7 %collective-permute-start.16 = (bf16[64,256]{1,0:T(8,128)(2,1)S(1)}, bf16[64,256]{1,0:T(8,128)(2,1)S(1)}, u32[]{:S(2)}, u32[]{:S(2)}) collective-permute-start(bf16[64,256]{1,0:T(8,128)(2,1)S(1)} %get-tuple-element.126), channel_id=1, source_target_pairs={{12,0},{0,4},{4,8},{8,12},{13,1},{1,5},{5,9},{9,13},{14,2},{2,6},{... | collective-permute-start | bytes 98312 | tf_op jit(solution)/shard_map/ppermute | solution.py:25

commit v5 on v4

--- a/solution.py
+++ b/solution.py
@@ -13,6 +13,7 @@
 LANES = 128
 PACK = 16
 MIB = 1 << 20
+WEIGHTS_LIMIT = 52
 NO_CHUNK = 64
 SLOT_OF = ((3, 0), (1, 1), (4, 4), (2, 5), (0, 2), (5, 3))
 EARLY, LATE = (0, 3, 4, 5), (1, 2)
@@ -73,26 +74,34 @@
     return ref[pl.ds(pl.multiple_of(index * rows, rows), rows), :]
 
 
-def weights_kernel(tiles, picks, *refs):
-    sources, refs = refs[:12], refs[12:]
-    held, refs = refs[:12], refs[12:]
-    w_send_t, w_recv_t, w_msg_t, w_node_v_t, w_node_a_t, w_out_t, *refs = refs
-    low_cols, high_cols, low_rows, high_rows, turned, w_out_all, sems = refs
-    w_send, w_recv, w_msg, w_node_v, w_node_a, w_out, senders, in_degree = held[:8]
+def weights_kernel(*refs):
+    sources, refs = refs[:7], refs[7:]
+    w_send, w_recv, w_out, feats, w_send_t, w_recv_t, w_msg_t, w_node_v_t, w_node_a_t, w_out_t = refs[:10]
+    w_msg, w_node_v, w_node_a, w_out_all, turned, sems = refs[10:]
     mine = lax.axis_index("ch")
     hid = w_send.shape[0]
+    targets = (feats, w_send, w_recv, w_msg, w_node_v, w_node_a, w_out_all)
     copies = []
-    for k, (source, target) in enumerate(zip(sources, held)):
-        if k in (0, 1):
+    for k, (source, target) in enumerate(zip(sources, targets)):
+        if k in (1, 2):
             source = source.at[pl.ds(pl.multiple_of(mine * hid, hid), hid), :]
-        target = w_out_all if k == 5 else target
         copies.append(pltpu.make_async_copy(source, target, sems.at[k]))
-    order = (6, 7, 0, 1, 2, 3, 4, 5, 8, 9, 10, 11)
-    for k in order:
-        copies[k].start()
-
-    copies[6].wait()
-    copies[7].wait()
+    for copy in copies:
+        copy.start()
+    for copy in copies:
+        copy.wait()
+    w_send_t[...] = w_send[...].T
+    w_recv_t[...] = w_recv[...].T
+    turned[...] = w_msg[...].T
+    w_msg_t[...] = mine_of(turned, mine, hid)
+    turned[...] = w_node_v[...].T
+    w_node_v_t[...] = mine_of(turned, mine, w_node_v_t.shape[0])
+    w_node_a_t[...] = w_node_a[...].T
+    w_out_t[...] = w_out_all[...].T
+    w_out[...] = mine_of(w_out_all, mine, w_out.shape[0])
+
+
+def edges_kernel(tiles, senders, in_degree, low_cols, high_cols, low_rows, high_rows):
     degree, nodes = senders.shape
     lane = lax.broadcasted_iota(jnp.int32, (degree, nodes), 1)
     row = lax.broadcasted_iota(jnp.int32, (degree, nodes), 0)
@@ -116,22 +125,10 @@
         for m in range(degree):
             out[m] = spread[:, m * LANES : (m + 1) * LANES]
 
-    for k in order[2:]:
-        copies[k].wait()
-    w_send_t[...] = w_send[...].T
-    w_recv_t[...] = w_recv[...].T
-    w_node_a_t[...] = w_node_a[...].T
-    w_out_t[...] = w_out_all[...].T
-    w_out[...] = mine_of(w_out_all, mine, w_out.shape[0])
-    turned[...] = w_msg[...].T
-    w_msg_t[...] = mine_of(turned, mine, hid)
-    turned[...] = w_node_v[...].T
-    w_node_v_t[...] = mine_of(turned, mine, w_node_v_t.shape[0])
-
 
 def project_kernel(count, tiles, picks, bias, *refs):
     blocks = refs[:count]
-    w_send, w_recv, feats, proj, base, upper, lower, cross, beside = refs[count:]
+    w_send, w_recv, feats, proj, base, upper, lower, beside = refs[count:]
     mine, sub = lax.axis_index("ch"), lax.axis_index("sub")
     first = tiles[0] // 2
     assemble(feats, blocks, mine)
@@ -142,23 +139,21 @@
     upper[:rows, :] = proj[pl.ds(pl.multiple_of(first * TILE, TILE), rows), :]
     lower[:rows, :] = proj[:rows, :]
     spot = lax.broadcasted_iota(jnp.int32, (PACK, hid), 0)
-    _, slots, per_slot = picks.shape
+    _, per_slot, slots = picks.shape
     half = slots // 2
     for start, out, lift in ((0, upper, first), (half, lower, 0)):
         marks = jnp.zeros((PACK, hid), jnp.float32)
         for k in range(half * per_slot):
-            rel = picks[0, start + k // per_slot, k % per_slot] - lift
+            rel = picks[0, k % per_slot, start + k // per_slot] - lift
             marks = jnp.where(spot == k, rel.astype(jnp.float32), marks)
         out[rows:, :] = marks.astype(jnp.bfloat16)
 
     @pl.when(sub == 0)
     def _():
-        cross[...] = lower[...]
         beside[...] = upper[...]
 
     @pl.when(sub != 0)
     def _():
-        cross[...] = upper[...]
         beside[...] = lower[...]
 
     my_bias = jnp.zeros((1, hid), jnp.float32)
@@ -425,60 +420,67 @@
         direct[:, span] = cots[:, span].astype(jnp.float32) + dot(w_node_v_t[...], grad_pre[...])
 
 
-def add_kernel(left, more, right, west, east):
-    west[...] = (left[...].astype(jnp.float32) + more[1].astype(jnp.float32)).astype(jnp.bfloat16)
-    east[...] = (right[...].astype(jnp.float32) + more[2].astype(jnp.float32)).astype(jnp.bfloat16)
-
-
-def final_kernel(
-    inv_root,
-    tiles,
-    own,
-    recv,
-    direct,
-    feats,
-    w_send_t,
-    w_recv_t,
-    upper,
-    lower,
-    across,
-    beside,
-    kept,
-    sent,
-    w_mine,
-    w_beside,
-    total,
-    terms,
-):
-    rows = upper.shape[0]
-    mine, sub, lon = lax.axis_index("ch"), lax.axis_index("sub"), lax.axis_index("lon")
-    start = tiles[0] // 2 * TILE
+def add_kernel(left, more, right, across, west, east):
+    sub = lax.axis_index("sub")
+    other = across[...].astype(jnp.float32)
+    to_west = left[...].astype(jnp.float32) + more[1].astype(jnp.float32)
+    to_east = right[...].astype(jnp.float32) + more[2].astype(jnp.float32)
+    west[...] = (to_west + jnp.where(sub == 0, 0.0, other)).astype(jnp.bfloat16)
+    east[...] = (to_east + jnp.where(sub == 0, other, 0.0)).astype(jnp.bfloat16)
+
+
+def back_kernel(start, inv_root, tiles, own, beside, feats, upper, *refs):
+    *refs, total = refs
+    sub = lax.axis_index("sub")
+    offset = pl.multiple_of(tiles[0] // 2 * TILE, TILE)
     total[...] = own[...]
-
-    def put(offset, block):
-        spot = pl.ds(pl.multiple_of(offset, TILE), rows)
-        total[spot, :] += block.astype(jnp.float32)
-
-    put(start, upper[...])
-    put(0, lower[...])
-    put(jnp.where(sub == 0, 0, start), across[...])
-    put(jnp.where(sub == 0, start, 0), beside[0])
-    grad_send = total[...].astype(jnp.bfloat16)
-    grad_send_t = total[...].T.astype(jnp.bfloat16)
-    chans = direct.shape[0]
-    terms[...] = dot(w_send_t[...], grad_send_t) + dot(w_recv_t[...], recv[...])
-    kept[...] = direct[...] + mine_of(terms, mine, chans)
-    count = sent.shape[0] + 1
-    for k in range(1, count):
-        sent[k - 1] = mine_of(terms, lax.rem(mine + k, count), chans).astype(jnp.bfloat16)
-    weight = dot(feats[...], grad_send) * inv_root
-    terms[:, : weight.shape[1]] = weight
-    lons, columns, hid = w_mine.shape
+    near = beside[0].astype(jnp.float32)
+    block = upper[...].astype(jnp.float32) + jnp.where(sub == 0, near, 0.0)
+    total[pl.ds(offset, block.shape[0]), :] += block
+    if start:
+        grad_send, weight = refs
+    else:
+        lower, before, grad_send, w_mine, w_beside, weight = refs
+        block = lower[...].astype(jnp.float32) + jnp.where(sub == 0, 0.0, near)
+        total[: block.shape[0], :] += block
+    rows = grad_send.shape[0]
+    grad_send[...] = total[start : start + rows, :].astype(jnp.bfloat16)
+    terms = dot(feats[:, start : start + rows], grad_send[...])
+    if start:
+        weight[...] = terms
+        return
+    weight[...] = (before[...] + terms) * inv_root
+    lon = lax.axis_index("lon")
+    lons, columns, _ = w_mine.shape
     for k in range(lons):
         band = lax.rem(lon + k, lons) * 2
         for out, core in ((w_mine, sub), (w_beside, 1 - sub)):
             spot = pl.multiple_of((band + core) * columns, columns)
-            out[k] = terms[pl.ds(spot, columns), :hid].astype(out.dtype)
+            out[k] = weight[pl.ds(spot, columns), :].astype(out.dtype)
+
+
+def terms_kernel(start, grad_send, recv, direct, w_send_t, w_recv_t, kept, sent, terms):
+    span = slice(start, start + grad_send.shape[0])
+    mine = lax.axis_index("ch")
+    chans = kept.shape[0]
+    grad_send_t = grad_send[...].astype(jnp.float32).T.astype(jnp.bfloat16)
+    terms[...] = dot(w_send_t[...], grad_send_t) + dot(w_recv_t[...], recv[:, span])
+    kept[...] = direct[:, span] + mine_of(terms, mine, chans)
+    count = sent.shape[0] + 1
+    for k in range(1, count):
+        sent[k - 1] = mine_of(terms, lax.rem(mine + k, count), chans).astype(jnp.bfloat16)
+
+
+def finish_kernel(*refs):
+    *parts, out = refs
+    rows = out.shape[1] // 2
+    count = len(parts) // 2
+    for k in range(2):
+        kept, *others = parts[k * count : (k + 1) * count]
+        total = kept[...]
+        for other in others:
+            total += other[...].astype(jnp.float32)
+        out[:, k * rows : (k + 1) * rows] = total.astype(jnp.bfloat16)
 
 
 def sum_kernel(w_mine, w_beside, near, sent):
@@ -492,7 +494,7 @@
     total = near[...]
     for ref in refs[:-1]:
         total += ref[...].astype(jnp.float32)
-    out[...] = total.T
+    out[...] = total
 
 
 def shards(
@@ -526,52 +528,64 @@
     bf16, f32 = jnp.bfloat16, jnp.float32
     shape = jax.ShapeDtypeStruct
 
-    across_route = [(i, (i + (3 if i % 2 else -3)) % shard_count) for i in range(shard_count)]
+    across_route = [(i, (i + (1 if i % 2 else -1)) % shard_count) for i in range(shard_count)]
     across = lambda block: lax.ppermute(block, cycle, across_route)
     degrees = in_degree[None, :]
+    picks = jnp.transpose(send_tiles, (0, 2, 1))
+    sub = lax.axis_index("sub")
 
     feat_blocks = gathered(features, "ch")
     cot_blocks = gathered(cotangent, "ch")
 
-    fixed = (
-        [shape((hid, chans_all), bf16)] * 2
-        + [shape((chans_all, hidden_all), bf16), shape((hidden_all, chans_all), bf16)]
-        + [shape((hidden_all, chans_all), bf16), shape((chans, hidden_all), bf16)]
-    )
-    inputs = [senders, degrees, features, cotangent, bias_edge[None, :], bias_node[None, :]]
-    held = call(
+    whole_w = pltpu.VMEM((chans_all, hidden_all), bf16)
+    (
+        w_send_my,
+        w_recv_my,
+        w_out_my,
+        features_held,
+        w_send_t,
+        w_recv_t,
+        w_msg_t,
+        w_node_v_t,
+        w_node_a_t,
+        w_out_t,
+    ) = call(
         weights_kernel,
         (
-            *fixed,
-            *[shape(x.shape, x.dtype) for x in inputs],
+            shape((hid, chans_all), bf16),
+            shape((hid, chans_all), bf16),
+            shape((chans, hidden_all), bf16),
+            shape((chans, nodes), bf16),
             shape((chans_all, hid), bf16),
             shape((chans_all, hid), bf16),
             shape((hid, chans_all), bf16),
             shape((chans, hidden_all), bf16),
             shape((chans_all, hidden_all), bf16),
             shape((hidden_all, chans_all), bf16),
+        ),
+        [features, w_send, w_recv, w_msg, w_node_v, w_node_a, w_out],
+        flops=4 * hidden_all * chans_all * nodes,
+        away=7,
+        scalars=0,
+        scratch=[whole_w] * 5 + [pltpu.SemaphoreType.DMA((7,))],
+        limit=WEIGHTS_LIMIT,
+    )
+    feat_blocks[0] = features_held
+    low_cols, high_cols, low_rows, high_rows = call(
+        edges_kernel,
+        (
             shape((degree, nodes, LANES), bf16),
             shape((degree, nodes, LANES), bf16),
             shape((degree, PACK, nodes), bf16),
             shape((degree, PACK, nodes), bf16),
         ),
-        [tile_count, send_tiles, w_send, w_recv, w_msg, w_node_v, w_node_a, w_out] + inputs,
-        flops=4 * hidden_all * chans_all * nodes,
-        away=12,
-        scratch=[
-            pltpu.VMEM((chans_all, hidden_all), bf16),
-            pltpu.VMEM((chans_all, hidden_all), bf16),
-            pltpu.SemaphoreType.DMA((12,)),
-        ],
-    )
-    w_send_my, w_recv_my, w_msg, w_node_v, w_node_a, w_out_my, _, degrees = held[:8]
-    features_held, cotangent_held, bias_edge, bias_node = held[8:12]
-    w_send_t, w_recv_t, w_msg_t, w_node_v_t, w_node_a_t, w_out_t = held[12:18]
-    low_cols, high_cols, low_rows, high_rows = held[18:]
-    feat_blocks[0], cot_blocks[0] = features_held, cotangent_held
+        [tile_count, senders, degrees],
+        flops=2 * hidden_all * chans_all * nodes,
+        scalars=1,
+    )
 
     block = shape((slot_rows + PACK, hid), bf16)
-    feats, proj, base, upper, lower, cross, beside = call(
+    feats, proj, base, upper, lower, beside = call(
         functools.partial(project_kernel, count),
         (
             shape((chans_all, nodes), bf16),
@@ -580,17 +594,13 @@
             block,
             block,
             block,
-            block,
         ),
-        [tile_count, send_tiles, bias_edge] + feat_blocks + [w_send_my, w_recv_my],
+        [tile_count, picks, bias_edge[None, :]] + feat_blocks + [w_send_my, w_recv_my],
         flops=4 * hid * chans_all * nodes,
     )
     west = shifted(upper, "lon", 1)
     east = shifted(lower, "lon", -1)
     beside = shifted(beside, "sub", 1)
-    cross = across(cross)
-    west_too = shifted(west, "sub", 1)
-    east_too = shifted(east, "sub", 1)
     cots, pre, grad_hidden = call(
         functools.partial(prepare_kernel, count),
         (
@@ -598,7 +608,7 @@
             shape((hidden_all, nodes), f32),
             shape((hidden_all, nodes), f32),
         ),
-        [tile_count] + cot_blocks + [feats, w_node_v, bias_node, w_out_t],
+        [tile_count] + cot_blocks + [feats, w_node_v, bias_node[None, :], w_out_t],
         flops=4 * hidden_all * chans_all * nodes,
         scalars=1,
     )
@@ -612,6 +622,11 @@
         scratch=[pltpu.VMEM((nodes + slot_rows, hid), bf16)],
         scalars=0,
     )
+    west, east, part = lax.optimization_barrier((west, east, part))
+    west_too = shifted(west, "sub", 1)
+    east_too = shifted(east, "sub", 1)
+    cross = across(jnp.where(sub == 0, east, west))
+    part, pre = lax.optimization_barrier((part, pre))
     part = call(
         line_kernel,
         part_shape,
@@ -680,7 +695,11 @@
         scalars=0,
     )
     to_west, to_east = call(
-        add_kernel, (block, block), [to_west, from_beside, to_east], flops=0, scalars=0
+        add_kernel,
+        (block, block),
+        [to_west, from_beside, to_east, from_cross],
+        flops=0,
+        scalars=0,
     )
     from_upper = shifted(to_west, "lon", -1)
     from_lower = shifted(to_east, "lon", 1)
@@ -695,30 +714,55 @@
     updated, direct = call(
         output_kernel,
         (shape((chans, nodes), bf16), shape((chans, nodes), f32)),
-        [tile_count, features_held, cotangent_held, w_out_my, w_node_v_t] + hiddens + grad_pres,
+        [tile_count, features_held, cotangent, w_out_my, w_node_v_t] + hiddens + grad_pres,
         flops=4 * hidden_all * chans * nodes,
         scalars=1,
     )
 
     columns = chans_all // shard_count
-    kept, sent, w_mine, w_beside = call(
-        functools.partial(final_kernel, 1.0 / math.sqrt(total_nodes)),
-        (
-            shape((chans, nodes), f32),
-            shape((count - 1, chans, nodes), bf16),
-            shape((lons, columns, hid), f32),
-            shape((lons, columns, hid), bf16),
-        ),
-        [tile_count, own, grad_recv, direct, feats, w_send_t, w_recv_t]
-        + [from_upper, from_lower, from_cross, from_beside],
-        flops=6 * hid * chans_all * nodes,
-        scratch=[pltpu.VMEM((nodes, hid), f32), pltpu.VMEM((chans_all, nodes), f32)],
-        scalars=1,
-    )
-    w_beside = shifted(w_beside, "sub", 1)
-    for k in range(1, count):
-        kept = kept + shifted(sent[k - 1], "ch", k).astype(f32)
-    grad_features = kept.astype(bf16)
+    inv_root = 1.0 / math.sqrt(total_nodes)
+    inputs = [tile_count, own, from_beside, feats, from_upper]
+    weight_shape = shape((chans_all, hid), f32)
+    grad_shape = shape((rows, hid), bf16)
+    finals = [None] * halves
+    for k in reversed(range(halves)):
+        kernel = functools.partial(back_kernel, k * rows, inv_root)
+        flops = 2 * hid * chans_all * rows
+        if k:
+            grad_send, weight = call(
+                kernel,
+                (grad_shape, weight_shape),
+                inputs,
+                flops=flops,
+                scratch=[pltpu.VMEM((nodes, hid), f32)],
+                scalars=1,
+            )
+        else:
+            grad_send, w_mine, w_beside = call(
+                kernel,
+                (
+                    grad_shape,
+                    shape((lons, columns, hid), f32),
+                    shape((lons, columns, hid), bf16),
+                ),
+                inputs + [from_lower, weight],
+                flops=flops,
+                scratch=[pltpu.VMEM(weight_shape.shape, f32), pltpu.VMEM((nodes, hid), f32)],
+                scalars=1,
+            )
+            w_beside = shifted(w_beside, "sub", 1)
+        kept, sent = call(
+            functools.partial(terms_kernel, k * rows),
+            (shape((chans, rows), f32), shape((count - 1, chans, rows), bf16)),
+            [grad_send, grad_recv, direct, w_send_t, w_recv_t],
+            flops=4 * hid * chans_all * rows,
+            scratch=[pltpu.VMEM((chans_all, rows), f32)],
+            scalars=0,
+        )
+        finals[k] = [kept] + [shifted(sent[i - 1], "ch", i) for i in range(1, count)]
+    grad_features = call(
+        finish_kernel, shape((chans, nodes), bf16), sum(finals, []), flops=0, scalars=0
+    )
 
     near, w_sent = call(
         sum_kernel,
@@ -729,9 +773,9 @@
     )
     w_terms = [shifted(w_sent[k - 1], "lon", k) for k in range(1, lons)]
     grad_w_send = call(
-        weight_kernel, shape((hid, columns), f32), [near] + w_terms, flops=0, scalars=0
-    )
-    return (updated, grad_features, grad_w_send)
+        weight_kernel, shape((columns, hid), f32), [near] + w_terms, flops=0, scalars=0
+    )
+    return (updated, grad_features, grad_w_send.T)
 
 
 def solution(mesh):

time: 81.3 us -> 79.1 us (0.973)
  local copies, waits for them, and re-layouts: 12.4 us -> 3.57 us
  Pallas kernels: 28.5 us -> 33.2 us
  waiting for transfers between devices: 15.7 us -> 20.1 us
  starting transfers between devices: 21.7 us -> 20.5 us
    unnamed x28 -> x36, local copies, waits for them, and re-layouts: 12.4 us -> 3.56 us
    ppermute x2, waiting for transfers between devices: 0.88 us -> 6.86 us  [shards(): across = lambda block: lax.ppermute(block, cycle, across_route)]
    pallas_call x18 -> x23, Pallas kernels: 28.5 us -> 33.2 us  [call(): pl.pallas_call(kernel, out_shape=out_shape, in_specs=[smem] * scalars + [...]
    ppermute x2, starting transfers between devices: 4.42 us -> 2.22 us  [shards(): across = lambda block: lax.ppermute(block, cycle, across_route)]
    ppermute x17 -> x18, waiting for transfers between devices: 14.8 us -> 13.2 us  [shifted(): return lax.ppermute(block, axis, route)]
    ppermute x17 -> x18, starting transfers between devices: 17.3 us -> 18.3 us  [shifted(): return lax.ppermute(block, axis, route)]
  transfers between devices with their start and end apart: 19 -> 20, of which waited for: 9 -> 11; matrix products, arithmetic and copies ran while one was open for 2% -> 0% of each run, Pallas kernels for 28% -> 33%
where the time goes in v5:
time: 79.1 us; the launch traced here: 78.9 us
  Pallas kernels  33.2 us (42%)
  starting transfers between devices  20.5 us (26%)
  waiting for transfers between devices  20.1 us (25%)
  local copies, waits for them, and re-layouts  3.57 us (5%)
  between operations  1.56 us (2%)
    pallas_call x23, Pallas kernels, call(): pl.pallas_call(kernel, out_shape=out_shape, in_specs=[smem] * scalars + [...  33.2 us
    ppermute x18, starting transfers between devices, shifted(): return lax.ppermute(block, axis, route)  18.3 us
    ppermute x18, waiting for transfers between devices, shifted(): return lax.ppermute(block, axis, route)  13.2 us
    ppermute x2, waiting for transfers between devices, shards(): across = lambda block: lax.ppermute(block, cycle, across_route)  6.86 us
    unnamed x36, local copies, waits for them, and re-layouts  3.56 us
    ppermute x2, starting transfers between devices, shards(): across = lambda block: lax.ppermute(block, cycle, across_route)  2.22 us
  transfers between devices with their start and end apart: 20, of which 11 were waited for; matrix products, arithmetic and copies ran while one was open for 0% of the time, Pallas kernels for 33%

profile of v5, /device:TPU:0, one launch (start us, length us, event | category | flops | bytes accessed | tf_op | source)
XLA Modules:
  0.0 78.9 jit_solution(9579735379524292718)
XLA Ops:
  0.6 3.0 %collective-permute-start = (bf16[256,512]{1,0:T(8,128)(2,1)}, bf16[256,512]{1,0:T(8,128)(2,1)S(1)}, u32[]{:S(2)}, u32[]{:S(2)}) collective-permute-start(bf16[256,512]{1,0:T(8,128)(2,1)} %refs_0_.2), channel_id=1, source_target_pairs={{2,0},{0,2},{3,1},{1,3},{6,4},{4,6},{7,5},{5,7},{10,8},{8,10},{11,... | collective-permute-start | bytes 786440 | tf_op jit(solution)/shard_map/ppermute | solution.py:26
  4.4 3.4 %shard_map.157 = (bf16[256,512]{1,0:T(8,128)(2,1)S(1)}, bf16[256,512]{1,0:T(8,128)(2,1)S(1)}, bf16[256,512]{1,0:T(8,128)(2,1)S(1)}, bf16[256,512]{1,0:T(8,128)(2...) custom-call(bf16[256,512]{1,0:T(8,128)(2,1)} %refs_0_.2, ...), custom_call_target="tpu_custom_call" | custom-call | flops 536870912 | bytes 3407872 | tf_op jit(solution)/shard_map/pallas_call | solution.py:52
  8.6 2.4 %collective-permute-done.refs_1_ = bf16[256,512]{1,0:T(8,128)(2,1)S(1)} collective-permute-done((bf16[256,512]{1,0:T(8,128)(2,1)}, bf16[256,512]{1,0:T(8,128)(2,1)S(1)}, u32[]{:S(2)}, u32[]{:S(2)}) %collective-permute-start) | collective-permute-done | bytes 262176 | tf_op jit(solution)/shard_map/ppermute | solution.py:26
  11.0 1.7 %shard_map.159 = (bf16[512,512]{1,0:T(8,128)(2,1)S(1)}, bf16[512,256]{1,0:T(8,128)(2,1)S(1)}, f32[512,256]{1,0:T(8,128)S(1)}, bf16[272,256]{1,0:T(8,128)(2,1)S(1...) custom-call(s32[1]{0:T(128)S(6)} %copy.17.tiles, s32[1,2,6]{2,1,0:T(2,128)S(1)} %bitcast.20, ...), custom_call_target="tpu_custom_call" | custom-call | flops 268435456 | bytes 1050676 | tf_op jit(solution)/shard_map/pallas_call | solution.py:52
  16.6 2.2 %collective-permute-start.1 = (bf16[272,256]{1,0:T(8,128)(2,1)}, bf16[272,256]{1,0:T(8,128)(2,1)S(1)}, u32[]{:S(2)}, u32[]{:S(2)}) collective-permute-start(bf16[272,256]{1,0:T(8,128)(2,1)} %copy-done.16), channel_id=1, source_target_pairs={{12,0},{0,4},{4,8},{8,12},{13,1},{1,5},{5,9},{9,13},{14,2},{2,6},{... | collective-permute-start | bytes 417800 | tf_op jit(solution)/shard_map/ppermute | solution.py:26
  18.8 2.3 %collective-permute-start.2 = (bf16[272,256]{1,0:T(8,128)(2,1)}, bf16[272,256]{1,0:T(8,128)(2,1)S(1)}, u32[]{:S(2)}, u32[]{:S(2)}) collective-permute-start(bf16[272,256]{1,0:T(8,128)(2,1)} %copy-done.15), channel_id=1, source_target_pairs={{4,0},{8,4},{12,8},{0,12},{5,1},{9,5},{13,9},{1,13},{6,2},{10,6},{... | collective-permute-start | bytes 417800 | tf_op jit(solution)/shard_map/ppermute | solution.py:26
  21.1 2.1 %shard_map.161 = (bf16[512,512]{1,0:T(8,128)(2,1)}, f32[512,512]{1,0:T(8,128)S(1)}, f32[512,512]{1,0:T(8,128)S(1)}) custom-call(s32[1]{0:T(128)S(6)} %copy.17.tiles, bf16[256,512]{1,0:T(8,128)(2,1)S(1)} %copy-done.4, bf16[256,512]{1,0:T(8,128)(2,1)} %collective-permute-done.4.refs_1_, bf16[512,512]{1,0:T(8,128)(2,1)S(1)} %get-tuple-element.77.refs_2_.feats, ...), custom_call_target="tpu_custom_call" | custom-call | flops 536870912 | bytes 2099204 | tf_op jit(solution)/shard_map/pallas_call | solution.py:52
  23.2 2.7 %shard_map.160.before = bf16[12,512,256]{2,1,0:T(8,128)(2,1)S(1)} custom-call(bf16[12,512,128]{2,1,0:T(8,128)(2,1)S(1)} %get-tuple-element.67.low, bf16[12,512,128]{2,1,0:T(8,128)(2,1)S(1)} %get-tuple-element.68.high, bf16[512,256]{1,0:T(8,128)(2,1)S(1)} %copy-done.14, bf16[272,256]{1,0:T(8,128)(2,1)S(1)} %collective-permute-done.3.beside.refs_1_), custom_call_target="tpu_custom_call" | custom-call | flops 2415919104 | bytes 3547136 | tf_op jit(solution)/shard_map/pallas_call | solution.py:52
  26.0 1.8 %collective-permute-done.2.east.refs_3_ = bf16[272,256]{1,0:T(8,128)(2,1)S(1)} collective-permute-done((bf16[272,256]{1,0:T(8,128)(2,1)}, bf16[272,256]{1,0:T(8,128)(2,1)S(1)}, u32[]{:S(2)}, u32[]{:S(2)}) %collective-permute-start.2) | collective-permute-done | bytes 139296 | tf_op jit(solution)/shard_map/ppermute | solution.py:26
  28.3 2.0 %collective-permute-start.5 = (bf16[272,256]{1,0:T(8,128)(2,1)S(1)}, bf16[272,256]{1,0:T(8,128)(2,1)S(1)}, u32[]{:S(2)}, u32[]{:S(2)}) collective-permute-start(bf16[272,256]{1,0:T(8,128)(2,1)S(1)} %broadcast_select_fusion), channel_id=1, source_target_pairs={{0,13},{1,4},{4,1},{5,8},{8,5},{9,12},{12,9},{13,0},{2,15},{3,6},{... | collective-permute-start | bytes 417800 | tf_op jit(solution)/shard_map/ppermute | solution.py:532
  30.3 2.4 %shard_map.162.part = bf16[12,512,256]{2,1,0:T(8,128)(2,1)S(1)} custom-call(bf16[12,512,128]{2,1,0:T(8,128)(2,1)S(1)} %get-tuple-element.67.low, bf16[12,512,128]{2,1,0:T(8,128)(2,1)S(1)} %get-tuple-element.68.high, bf16[12,512,256]{2,1,0:T(8,128)(2,1)S(1)} %shard_map.160.before, bf16[272,256]{1,0:T(8,128)(2,1)S(1)} %collective-permute-done.1.west.refs_2_, ...), custom_call_target="tpu_custom_call" | custom-call | flops 1610612736 | bytes 6569984 | tf_op jit(solution)/shard_map/pallas_call | solution.py:52
  32.7 2.5 %collective-permute-done.5.cross.refs_2_ = bf16[272,256]{1,0:T(8,128)(2,1)S(1)} collective-permute-done((bf16[272,256]{1,0:T(8,128)(2,1)S(1)}, bf16[272,256]{1,0:T(8,128)(2,1)S(1)}, u32[]{:S(2)}, u32[]{:S(2)}) %collective-permute-start.5) | collective-permute-done | bytes 139296 | tf_op jit(solution)/shard_map/ppermute | solution.py:532
  35.3 2.5 %shard_map.163 = (bf16[256,256]{1,0:T(8,128)(2,1)S(1)}, bf16[12,256,256]{2,1,0:T(8,128)(2,1)S(1)}) custom-call(bf16[12,512,128]{2,1,0:T(8,128)(2,1)S(1)} %get-tuple-element.67.low, bf16[12,512,128]{2,1,0:T(8,128)(2,1)S(1)} %get-tuple-element.68.high, f32[512,256]{1,0:T(8,128)S(1)} %get-tuple-element.71.base, s32[1,512]{1,0:T(1,128)S(1)} %bitcast.14, ...), custom_call_target="tpu_custom_call" | custom-call | flops 1207959552 | bytes 7235584 | tf_op jit(solution)/shard_map/pallas_call | solution.py:52
  37.8 1.6 %collective-permute-start.8 = (bf16[256,256]{1,0:T(8,128)(2,1)S(1)}, bf16[256,256]{1,0:T(8,128)(2,1)S(1)}, u32[]{:S(2)}, u32[]{:S(2)}) collective-permute-start(bf16[256,256]{1,0:T(8,128)(2,1)S(1)} %get-tuple-element.83.refs_0_), channel_id=1, source_target_pairs={{2,0},{0,2},{3,1},{1,3},{6,4},{4,6},{7,5},{5,7},{10,8},{8,10},{11,... | collective-permute-start | bytes 393224 | tf_op jit(solution)/shard_map/ppermute | solution.py:26
  39.4 2.5 %shard_map.165 = (bf16[256,256]{1,0:T(8,128)(2,1)S(1)}, bf16[12,256,256]{2,1,0:T(8,128)(2,1)S(1)}) custom-call(bf16[12,512,128]{2,1,0:T(8,128)(2,1)S(1)} %get-tuple-element.67.low, bf16[12,512,128]{2,1,0:T(8,128)(2,1)S(1)} %get-tuple-element.68.high, f32[512,256]{1,0:T(8,128)S(1)} %get-tuple-element.71.base, s32[1,512]{1,0:T(1,128)S(1)} %bitcast.15, ...), custom_call_target="tpu_custom_call" | custom-call | flops 1207959552 | bytes 7235584 | tf_op jit(solution)/shard_map/pallas_call | solution.py:52
  42.4 1.5 %collective-permute-done.8.refs_1_ = bf16[256,256]{1,0:T(8,128)(2,1)S(1)} collective-permute-done((bf16[256,256]{1,0:T(8,128)(2,1)S(1)}, bf16[256,256]{1,0:T(8,128)(2,1)S(1)}, u32[]{:S(2)}, u32[]{:S(2)}) %collective-permute-start.8) | collective-permute-done | bytes 131104 | tf_op jit(solution)/shard_map/ppermute | solution.py:26
  43.9 1.3 %shard_map.164 = (bf16[512,256]{1,0:T(8,128)(2,1)S(1)}, bf16[512,256]{1,0:T(8,128)(2,1)S(1)}, f32[256,256]{1,0:T(8,128)S(1)}) custom-call(s32[1,512]{1,0:T(1,128)S(1)} %bitcast.16, bf16[256,256]{1,0:T(8,128)(2,1)S(1)} %get-tuple-element.83.refs_0_, bf16[256,256]{1,0:T(8,128)(2,1)S(1)} %collective-permute-done.8.refs_1_, bf16[512,512]{1,0:T(8,128)(2,1)S(1)} %copy-done, ...), custom_call_target="tpu_custom_call" | custom-call | flops 402653184 | bytes 4196352 | tf_op jit(solution)/shard_map/pallas_call | solution.py:52
  45.3 2.1 %shard_map.168 = (bf16[12,256,256]{2,1,0:T(8,128)(2,1)S(1)}, f32[1024,256]{1,0:T(8,128)S(1)}) custom-call(bf16[12,16,512]{2,1,0:T(8,128)(2,1)S(1)} %get-tuple-element.94.low, bf16[12,16,512]{2,1,0:T(8,128)(2,1)S(1)} %get-tuple-element.95.high, bf16[12,256,256]{2,1,0:T(8,128)(2,1)S(1)} %get-tuple-element.96.slope, f32[256,256]{1,0:T(8,128)S(1)} %get-tuple-element.97.scale), custom_call_target="tpu_custom_call" | custom-call | flops 1610612736 | bytes 2228224 | tf_op jit(solution)/shard_map/pallas_call | solution.py:52
  47.4 1.3 %shard_map.166 = (bf16[512,256]{1,0:T(8,128)(2,1)S(1)}, bf16[512,256]{1,0:T(8,128)(2,1)S(1)}, f32[256,256]{1,0:T(8,128)S(1)}) custom-call(s32[1,512]{1,0:T(1,128)S(1)} %bitcast.17, bf16[256,256]{1,0:T(8,128)(2,1)S(1)} %get-tuple-element.89.refs_0_, bf16[256,256]{1,0:T(8,128)(2,1)S(1)} %collective-permute-done.9.refs_1_, bf16[512,512]{1,0:T(8,128)(2,1)S(1)} %copy-done, ...), custom_call_target="tpu_custom_call" | custom-call | flops 402653184 | bytes 4196352 | tf_op jit(solution)/shard_map/pallas_call | solution.py:52
  48.7 1.9 %shard_map.169 = (bf16[256,256]{1,0:T(8,128)(2,1)S(1)}, bf16[3,256,256]{2,1,0:T(8,128)(2,1)S(1)}, bf16[12,256,256]{2,1,0:T(8,128)(2,1)S(1)}) custom-call(bf16[12,16,512]{2,1,0:T(8,128)(2,1)S(1)} %get-tuple-element.94.low, bf16[12,16,512]{2,1,0:T(8,128)(2,1)S(1)} %get-tuple-element.95.high, bf16[12,256,256]{2,1,0:T(8,128)(2,1)S(1)} %get-tuple-element.99.slope, ...), custom_call_target="tpu_custom_call" | custom-call | flops 1610612736 | bytes 3833856 | tf_op jit(solution)/shard_map/pallas_call | solution.py:52
  50.9 1.8 %shard_map.171 = (bf16[256,256]{1,0:T(8,128)(2,1)S(1)}, bf16[256,256]{1,0:T(8,128)(2,1)S(1)}) custom-call(bf16[12,16,512]{2,1,0:T(8,128)(2,1)S(1)} %get-tuple-element.94.low, bf16[12,16,512]{2,1,0:T(8,128)(2,1)S(1)} %get-tuple-element.95.high, bf16[12,256,256]{2,1,0:T(8,128)(2,1)S(1)} %get-tuple-element.98.refs_0_, ...), custom_call_target="tpu_custom_call" | custom-call | flops 1610612736 | bytes 3817472 | tf_op jit(solution)/shard_map/pallas_call | solution.py:52
  52.7 4.3 %collective-permute-done.11.across = bf16[256,256]{1,0:T(8,128)(2,1)S(1)} collective-permute-done((bf16[256,256]{1,0:T(8,128)(2,1)S(1)}, bf16[256,256]{1,0:T(8,128)(2,1)S(1)}, u32[]{:S(2)}, u32[]{:S(2)}) %collective-permute-start.11) | collective-permute-done | bytes 131104 | tf_op jit(solution)/shard_map/ppermute | solution.py:532
  57.2 2.0 %collective-permute-start.13 = (bf16[256,256]{1,0:T(8,128)(2,1)S(1)}, bf16[256,256]{1,0:T(8,128)(2,1)S(1)}, u32[]{:S(2)}, u32[]{:S(2)}) collective-permute-start(bf16[256,256]{1,0:T(8,128)(2,1)S(1)} %get-tuple-element.109), channel_id=1, source_target_pairs={{12,0},{0,4},{4,8},{8,12},{13,1},{1,5},{5,9},{9,13},{14,2},{2,6},{... | collective-permute-start | bytes 393224 | tf_op jit(solution)/shard_map/ppermute | solution.py:26
  59.2 2.1 %shard_map.170 = (f32[512,256]{1,0:T(8,128)S(1)}, bf16[256,512]{1,0:T(8,128)(2,1)S(1)}) custom-call(bf16[12,16,512]{2,1,0:T(8,128)(2,1)S(1)} %get-tuple-element.94.low, bf16[12,16,512]{2,1,0:T(8,128)(2,1)S(1)} %get-tuple-element.95.high, bf16[12,256,256]{2,1,0:T(8,128)(2,1)S(1)} %get-tuple-element.98.refs_0_, ...), custom_call_target="tpu_custom_call" | custom-call | flops 1610612736 | bytes 3538944 | tf_op jit(solution)/shard_map/pallas_call | solution.py:52
  61.3 1.3 %collective-permute-done.12.upper = bf16[256,256]{1,0:T(8,128)(2,1)S(1)} collective-permute-done((bf16[256,256]{1,0:T(8,128)(2,1)S(1)}, bf16[256,256]{1,0:T(8,128)(2,1)S(1)}, u32[]{:S(2)}, u32[]{:S(2)}) %collective-permute-start.12) | collective-permute-done | bytes 131104 | tf_op jit(solution)/shard_map/ppermute | solution.py:26
  62.9 2.4 %collective-permute-done.13.refs_0_ = bf16[256,256]{1,0:T(8,128)(2,1)S(1)} collective-permute-done((bf16[256,256]{1,0:T(8,128)(2,1)S(1)}, bf16[256,256]{1,0:T(8,128)(2,1)S(1)}, u32[]{:S(2)}, u32[]{:S(2)}) %collective-permute-start.13) | collective-permute-done | bytes 131104 | tf_op jit(solution)/shard_map/ppermute | solution.py:26
  65.9 1.1 %shard_map.167 = (bf16[256,512]{1,0:T(8,128)(2,1)}, f32[256,512]{1,0:T(8,128)S(1)}) custom-call(s32[1]{0:T(128)S(6)} %copy.17.tiles, bf16[256,512]{1,0:T(8,128)(2,1)S(1)} %get-tuple-element.64.refs_0_.feats, bf16[256,512]{1,0:T(8,128)(2,1)S(1)} %copy-done.4, bf16[256,512]{1,0:T(8,128)(2,1)S(1)} %copy-done.7, bf16[256,512]{1,0:T(8,128)(2,1)S(1)} %copy-done.8, ...), custom_call_target="tpu_custom_call" | custom-call | flops 268435456 | bytes 2097156 | tf_op jit(solution)/shard_map/pallas_call | solution.py:52
  67.5 1.3 %collective-permute-start.14 = (bf16[256,256]{1,0:T(8,128)(2,1)S(1)}, bf16[256,256]{1,0:T(8,128)(2,1)S(1)}, u32[]{:S(2)}, u32[]{:S(2)}) collective-permute-start(bf16[256,256]{1,0:T(8,128)(2,1)S(1)} %bitcast.21), channel_id=1, source_target_pairs={{2,0},{0,2},{3,1},{1,3},{6,4},{4,6},{7,5},{5,7},{10,8},{8,10},{11,... | collective-permute-start | bytes 393224 | tf_op jit(solution)/shard_map/ppermute | solution.py:26
  70.2 1.3 %collective-permute-start.19 = (bf16[64,256]{1,0:T(8,128)(2,1)S(1)}, bf16[64,256]{1,0:T(8,128)(2,1)S(1)}, u32[]{:S(2)}, u32[]{:S(2)}) collective-permute-start(bf16[64,256]{1,0:T(8,128)(2,1)S(1)} %get-tuple-element.125), channel_id=1, source_target_pairs={{4,0},{8,4},{12,8},{0,12},{5,1},{9,5},{13,9},{1,13},{6,2},{10,6},{... | collective-permute-start | bytes 98312 | tf_op jit(solution)/shard_map/ppermute | solution.py:26
  72.5 1.2 %collective-permute-start.17 = (bf16[64,256]{1,0:T(8,128)(2,1)S(1)}, bf16[64,256]{1,0:T(8,128)(2,1)S(1)}, u32[]{:S(2)}, u32[]{:S(2)}) collective-permute-start(bf16[64,256]{1,0:T(8,128)(2,1)S(1)} %get-tuple-element.127), channel_id=1, source_target_pairs={{12,0},{0,4},{4,8},{8,12},{13,1},{1,5},{5,9},{9,13},{14,2},{2,6},{... | collective-permute-start | bytes 98312 | tf_op jit(solution)/shard_map/ppermute | solution.py:26
  73.9 2.3 %collective-permute-done.15.refs_3_ = bf16[256,256]{1,0:T(8,128)(2,1)S(1)} collective-permute-done((bf16[256,256]{1,0:T(8,128)(2,1)S(1)}, bf16[256,256]{1,0:T(8,128)(2,1)S(1)}, u32[]{:S(2)}, u32[]{:S(2)}) %collective-permute-start.15) | collective-permute-done | bytes 131104 | tf_op jit(solution)/shard_map/ppermute | solution.py:26
  77.0 1.2 %collective-permute-done.17.refs_0_ = bf16[64,256]{1,0:T(8,128)(2,1)S(1)} collective-permute-done((bf16[64,256]{1,0:T(8,128)(2,1)S(1)}, bf16[64,256]{1,0:T(8,128)(2,1)S(1)}, u32[]{:S(2)}, u32[]{:S(2)}) %collective-permute-start.17) | collective-permute-done | bytes 32800 | tf_op jit(solution)/shard_map/ppermute | solution.py:26
  (69 shorter events, 11.7 us)
Async XLA Ops:
  0.6 10.3 %collective-permute-start = (bf16[256,512]{1,0:T(8,128)(2,1)}, bf16[256,512]{1,0:T(8,128)(2,1)S(1)}, u32[]{:S(2)}, u32[]{:S(2)}) collective-permute-start(bf16[256,512]{1,0:T(8,128)(2,1)} %refs_0_.2), channel_id=1, source_target_pairs={{2,0},{0,2},{3,1},{1,3},{6,4},{4,6},{7,5},{5,7},{10,8},{8,10},{11,... | collective-permute-start | bytes 786440 | tf_op jit(solution)/shard_map/ppermute | solution.py:26
  3.6 17.4 %collective-permute-start.4 = (bf16[256,512]{1,0:T(8,128)(2,1)}, bf16[256,512]{1,0:T(8,128)(2,1)}, u32[]{:S(2)}, u32[]{:S(2)}) collective-permute-start(bf16[256,512]{1,0:T(8,128)(2,1)} %cots.1), channel_id=1, source_target_pairs={{2,0},{0,2},{3,1},{1,3},{6,4},{4,6},{7,5},{5,7},{10,8},{8,10},{11,... | collective-permute-start | bytes 786440 | tf_op jit(solution)/shard_map/ppermute | solution.py:26
  4.4 6.6 %copy-start.10 = (f32[512]{0:T(512)S(1)}, f32[512]{0:T(512)}, u32[]{:S(2)}) copy-start(f32[512]{0:T(512)} %param.22) | copy-start | bytes 6148
  4.4 6.6 %copy-start.12 = (s32[1,6,2]{1,2,0:T(2,128)S(1)}, s32[1,6,2]{1,2,0:T(2,128)}, u32[]{:S(2)}) copy-start(s32[1,6,2]{1,2,0:T(2,128)} %param.19) | copy-start | bytes 148
  4.4 10.3 %copy-start.9 = (s32[512]{0:T(512)S(1)}, s32[512]{0:T(512)}, u32[]{:S(2)}) copy-start(s32[512]{0:T(512)} %param.17) | copy-start | bytes 6148
  8.5 12.5 %copy-start.2 = (bf16[512,512]{1,0:T(8,128)(2,1)S(1)}, bf16[512,512]{1,0:T(8,128)(2,1)}, u32[]{:S(2)}) copy-start(bf16[512,512]{1,0:T(8,128)(2,1)} %refs_3_.5) | copy-start | bytes 1572868
  8.5 12.5 %copy-start.4 = (bf16[256,512]{1,0:T(8,128)(2,1)S(1)}, bf16[256,512]{1,0:T(8,128)(2,1)}, u32[]{:S(2)}) copy-start(bf16[256,512]{1,0:T(8,128)(2,1)} %cots.1) | copy-start | bytes 786436
  8.5 12.5 %copy-start.5 = (bf16[512,512]{1,0:T(8,128)(2,1)S(1)}, bf16[512,512]{1,0:T(8,128)(2,1)}, u32[]{:S(2)}) copy-start(bf16[512,512]{1,0:T(8,128)(2,1)} %get-tuple-element.78.refs_5_) | copy-start | bytes 1572868
  8.5 12.5 %copy-start.11 = (f32[512]{0:T(512)S(1)}, f32[512]{0:T(512)}, u32[]{:S(2)}) copy-start(f32[512]{0:T(512)} %param.26) | copy-start | bytes 6148
  14.7 8.5 %collective-permute-start.3 = (bf16[272,256]{1,0:T(8,128)(2,1)}, bf16[272,256]{1,0:T(8,128)(2,1)S(1)}, u32[]{:S(2)}, u32[]{:S(2)}) collective-permute-start(bf16[272,256]{1,0:T(8,128)(2,1)} %get-tuple-element.75), channel_id=1, source_target_pairs={{1,0},{0,1},{3,2},{2,3},{5,4},{4,5},{7,6},{6,7},{9,8},{8,9},{11,10... | collective-permute-start | bytes 417800 | tf_op jit(solution)/shard_map/ppermute | solution.py:26
  14.7 8.5 %copy-start.14 = (bf16[512,256]{1,0:T(8,128)(2,1)S(1)}, bf16[512,256]{1,0:T(8,128)(2,1)}, u32[]{:S(2)}) copy-start(bf16[512,256]{1,0:T(8,128)(2,1)} %copy-done.13) | copy-start | bytes 786436
  16.6 9.4 %collective-permute-start.1 = (bf16[272,256]{1,0:T(8,128)(2,1)}, bf16[272,256]{1,0:T(8,128)(2,1)S(1)}, u32[]{:S(2)}, u32[]{:S(2)}) collective-permute-start(bf16[272,256]{1,0:T(8,128)(2,1)} %copy-done.16), channel_id=1, source_target_pairs={{12,0},{0,4},{4,8},{8,12},{13,1},{1,5},{5,9},{9,13},{14,2},{2,6},{... | collective-permute-start | bytes 417800 | tf_op jit(solution)/shard_map/ppermute | solution.py:26
  18.8 9.0 %collective-permute-start.2 = (bf16[272,256]{1,0:T(8,128)(2,1)}, bf16[272,256]{1,0:T(8,128)(2,1)S(1)}, u32[]{:S(2)}, u32[]{:S(2)}) collective-permute-start(bf16[272,256]{1,0:T(8,128)(2,1)} %copy-done.15), channel_id=1, source_target_pairs={{4,0},{8,4},{12,8},{0,12},{5,1},{9,5},{13,9},{1,13},{6,2},{10,6},{... | collective-permute-start | bytes 417800 | tf_op jit(solution)/shard_map/ppermute | solution.py:26
  27.8 7.5 %collective-permute-start.6 = (bf16[272,256]{1,0:T(8,128)(2,1)S(1)}, bf16[272,256]{1,0:T(8,128)(2,1)S(1)}, u32[]{:S(2)}, u32[]{:S(2)}) collective-permute-start(bf16[272,256]{1,0:T(8,128)(2,1)S(1)} %collective-permute-done.1.west.refs_2_), channel_id=1, source_target_pairs={{1,0},{0,1},{3,2},{2,3},{5,4},{4,5},{7,6},{6,7},{9,8},{8,9},{11,10... | collective-permute-start | bytes 417800 | tf_op jit(solution)/shard_map/ppermute | solution.py:26
  27.8 7.5 %collective-permute-start.7 = (bf16[272,256]{1,0:T(8,128)(2,1)S(1)}, bf16[272,256]{1,0:T(8,128)(2,1)S(1)}, u32[]{:S(2)}, u32[]{:S(2)}) collective-permute-start(bf16[272,256]{1,0:T(8,128)(2,1)S(1)} %collective-permute-done.2.east.refs_3_), channel_id=1, source_target_pairs={{1,0},{0,1},{3,2},{2,3},{5,4},{4,5},{7,6},{6,7},{9,8},{8,9},{11,10... | collective-permute-start | bytes 417800 | tf_op jit(solution)/shard_map/ppermute | solution.py:26
  28.3 7.0 %collective-permute-start.5 = (bf16[272,256]{1,0:T(8,128)(2,1)S(1)}, bf16[272,256]{1,0:T(8,128)(2,1)S(1)}, u32[]{:S(2)}, u32[]{:S(2)}) collective-permute-start(bf16[272,256]{1,0:T(8,128)(2,1)S(1)} %broadcast_select_fusion), channel_id=1, source_target_pairs={{0,13},{1,4},{4,1},{5,8},{8,5},{9,12},{12,9},{13,0},{2,15},{3,6},{... | collective-permute-start | bytes 417800 | tf_op jit(solution)/shard_map/ppermute | solution.py:532
  37.7 6.2 %copy-start = (bf16[512,512]{1,0:T(8,128)(2,1)S(1)}, bf16[512,512]{1,0:T(8,128)(2,1)}, u32[]{:S(2)}) copy-start(bf16[512,512]{1,0:T(8,128)(2,1)} %refs_2_.5) | copy-start | bytes 1572868
  37.7 6.2 %copy-start.1 = (bf16[512,512]{1,0:T(8,128)(2,1)S(1)}, bf16[512,512]{1,0:T(8,128)(2,1)}, u32[]{:S(2)}) copy-start(bf16[512,512]{1,0:T(8,128)(2,1)} %refs_3_.7) | copy-start | bytes 1572868
  37.8 6.2 %copy-start.3 = (bf16[512,512]{1,0:T(8,128)(2,1)S(1)}, bf16[512,512]{1,0:T(8,128)(2,1)}, u32[]{:S(2)}) copy-start(bf16[512,512]{1,0:T(8,128)(2,1)} %get-tuple-element.84.refs_4_) | copy-start | bytes 1572868
  37.8 6.2 %collective-permute-start.8 = (bf16[256,256]{1,0:T(8,128)(2,1)S(1)}, bf16[256,256]{1,0:T(8,128)(2,1)S(1)}, u32[]{:S(2)}, u32[]{:S(2)}) collective-permute-start(bf16[256,256]{1,0:T(8,128)(2,1)S(1)} %get-tuple-element.83.refs_0_), channel_id=1, source_target_pairs={{2,0},{0,2},{3,1},{1,3},{6,4},{4,6},{7,5},{5,7},{10,8},{8,10},{11,... | collective-permute-start | bytes 393224 | tf_op jit(solution)/shard_map/ppermute | solution.py:26
  41.8 5.5 %collective-permute-start.9 = (bf16[256,256]{1,0:T(8,128)(2,1)S(1)}, bf16[256,256]{1,0:T(8,128)(2,1)S(1)}, u32[]{:S(2)}, u32[]{:S(2)}) collective-permute-start(bf16[256,256]{1,0:T(8,128)(2,1)S(1)} %get-tuple-element.89.refs_0_), channel_id=1, source_target_pairs={{2,0},{0,2},{3,1},{1,3},{6,4},{4,6},{7,5},{5,7},{10,8},{8,10},{11,... | collective-permute-start | bytes 393224 | tf_op jit(solution)/shard_map/ppermute | solution.py:26
  50.6 6.4 %collective-permute-start.10 = (bf16[3,256,256]{2,1,0:T(8,128)(2,1)S(1)}, bf16[3,256,256]{2,1,0:T(8,128)(2,1)S(1)}, u32[]{:S(2)}, u32[]{:S(2)}) collective-permute-start(bf16[3,256,256]{2,1,0:T(8,128)(2,1)S(1)} %get-tuple-element.104), channel_id=1, source_target_pairs={{1,0},{0,1},{3,2},{2,3},{5,4},{4,5},{7,6},{6,7},{9,8},{8,9},{11,10... | collective-permute-start | bytes 1179656 | tf_op jit(solution)/shard_map/ppermute | solution.py:26
  50.7 6.4 %collective-permute-start.11 = (bf16[256,256]{1,0:T(8,128)(2,1)S(1)}, bf16[256,256]{1,0:T(8,128)(2,1)S(1)}, u32[]{:S(2)}, u32[]{:S(2)}) collective-permute-start(bf16[256,256]{1,0:T(8,128)(2,1)S(1)} %get-tuple-element.107), channel_id=1, source_target_pairs={{0,13},{1,4},{4,1},{5,8},{8,5},{9,12},{12,9},{13,0},{2,15},{3,6},{... | collective-permute-start | bytes 393224 | tf_op jit(solution)/shard_map/ppermute | solution.py:532
  57.2 5.5 %collective-permute-start.12 = (bf16[256,256]{1,0:T(8,128)(2,1)S(1)}, bf16[256,256]{1,0:T(8,128)(2,1)S(1)}, u32[]{:S(2)}, u32[]{:S(2)}) collective-permute-start(bf16[256,256]{1,0:T(8,128)(2,1)S(1)} %get-tuple-element.108), channel_id=1, source_target_pairs={{4,0},{8,4},{12,8},{0,12},{5,1},{9,5},{13,9},{1,13},{6,2},{10,6},{... | collective-permute-start | bytes 393224 | tf_op jit(solution)/shard_map/ppermute | solution.py:26
  57.2 8.1 %collective-permute-start.13 = (bf16[256,256]{1,0:T(8,128)(2,1)S(1)}, bf16[256,256]{1,0:T(8,128)(2,1)S(1)}, u32[]{:S(2)}, u32[]{:S(2)}) collective-permute-start(bf16[256,256]{1,0:T(8,128)(2,1)S(1)} %get-tuple-element.109), channel_id=1, source_target_pairs={{12,0},{0,4},{4,8},{8,12},{13,1},{1,5},{5,9},{9,13},{14,2},{2,6},{... | collective-permute-start | bytes 393224 | tf_op jit(solution)/shard_map/ppermute | solution.py:26
  62.6 3.3 %copy-start.8 = (bf16[256,512]{1,0:T(8,128)(2,1)S(1)}, bf16[256,512]{1,0:T(8,128)(2,1)}, u32[]{:S(2)}) copy-start(bf16[256,512]{1,0:T(8,128)(2,1)} %get-tuple-element.66.w_node_v_t) | copy-start | bytes 786436
  65.7 4.4 %collective-permute-start.16 = (bf16[4,64,256]{2,1,0:T(8,128)(2,1)S(1)}, bf16[4,64,256]{2,1,0:T(8,128)(2,1)S(1)}, u32[]{:S(2)}, u32[]{:S(2)}) collective-permute-start(bf16[4,64,256]{2,1,0:T(8,128)(2,1)S(1)} %get-tuple-element.122), channel_id=1, source_target_pairs={{1,0},{0,1},{3,2},{2,3},{5,4},{4,5},{7,6},{6,7},{9,8},{8,9},{11,10... | collective-permute-start | bytes 393224 | tf_op jit(solution)/shard_map/ppermute | solution.py:26
  67.5 6.4 %collective-permute-start.14 = (bf16[256,256]{1,0:T(8,128)(2,1)S(1)}, bf16[256,256]{1,0:T(8,128)(2,1)S(1)}, u32[]{:S(2)}, u32[]{:S(2)}) collective-permute-start(bf16[256,256]{1,0:T(8,128)(2,1)S(1)} %bitcast.21), channel_id=1, source_target_pairs={{2,0},{0,2},{3,1},{1,3},{6,4},{4,6},{7,5},{5,7},{10,8},{8,10},{11,... | collective-permute-start | bytes 393224 | tf_op jit(solution)/shard_map/ppermute | solution.py:26
  69.2 7.0 %collective-permute-start.15 = (bf16[256,256]{1,0:T(8,128)(2,1)S(1)}, bf16[256,256]{1,0:T(8,128)(2,1)S(1)}, u32[]{:S(2)}, u32[]{:S(2)}) collective-permute-start(bf16[256,256]{1,0:T(8,128)(2,1)S(1)} %bitcast.22), channel_id=1, source_target_pairs={{2,0},{0,2},{3,1},{1,3},{6,4},{4,6},{7,5},{5,7},{10,8},{8,10},{11,... | collective-permute-start | bytes 393224 | tf_op jit(solution)/shard_map/ppermute | solution.py:26
  70.2 6.7 %collective-permute-start.19 = (bf16[64,256]{1,0:T(8,128)(2,1)S(1)}, bf16[64,256]{1,0:T(8,128)(2,1)S(1)}, u32[]{:S(2)}, u32[]{:S(2)}) collective-permute-start(bf16[64,256]{1,0:T(8,128)(2,1)S(1)} %get-tuple-element.125), channel_id=1, source_target_pairs={{4,0},{8,4},{12,8},{0,12},{5,1},{9,5},{13,9},{1,13},{6,2},{10,6},{... | collective-permute-start | bytes 98312 | tf_op jit(solution)/shard_map/ppermute | solution.py:26
  71.5 5.5 %collective-permute-start.18 = (bf16[64,256]{1,0:T(8,128)(2,1)S(1)}, bf16[64,256]{1,0:T(8,128)(2,1)S(1)}, u32[]{:S(2)}, u32[]{:S(2)}) collective-permute-start(bf16[64,256]{1,0:T(8,128)(2,1)S(1)} %get-tuple-element.126), channel_id=1, source_target_pairs={{8,0},{12,4},{0,8},{4,12},{9,1},{13,5},{1,9},{5,13},{10,2},{14,6},... | collective-permute-start | bytes 98312 | tf_op jit(solution)/shard_map/ppermute | solution.py:26
  72.5 5.7 %collective-permute-start.17 = (bf16[64,256]{1,0:T(8,128)(2,1)S(1)}, bf16[64,256]{1,0:T(8,128)(2,1)S(1)}, u32[]{:S(2)}, u32[]{:S(2)}) collective-permute-start(bf16[64,256]{1,0:T(8,128)(2,1)S(1)} %get-tuple-element.127), channel_id=1, source_target_pairs={{12,0},{0,4},{4,8},{8,12},{13,1},{1,5},{5,9},{9,13},{14,2},{2,6},{... | collective-permute-start | bytes 98312 | tf_op jit(solution)/shard_map/ppermute | solution.py:26
  (6 other events, 6.8 us)

commit v6 on v5

--- a/solution.py
+++ b/solution.py
@@ -126,9 +126,9 @@
             out[m] = spread[:, m * LANES : (m + 1) * LANES]
 
 
-def project_kernel(count, tiles, picks, bias, *refs):
+def project_kernel(count, tiles, picks, *refs):
     blocks = refs[:count]
-    w_send, w_recv, feats, proj, base, upper, lower, beside = refs[count:]
+    w_send, feats, proj, upper, lower, beside, cross = refs[count:]
     mine, sub = lax.axis_index("ch"), lax.axis_index("sub")
     first = tiles[0] // 2
     assemble(feats, blocks, mine)
@@ -151,15 +151,21 @@
     @pl.when(sub == 0)
     def _():
         beside[...] = upper[...]
+        cross[...] = lower[...]
 
     @pl.when(sub != 0)
     def _():
         beside[...] = lower[...]
-
+        cross[...] = upper[...]
+
+
+def receive_kernel(bias, feats, w_recv, base):
+    hid = base.shape[1]
+    mine = lax.axis_index("ch")
     my_bias = jnp.zeros((1, hid), jnp.float32)
-    for k in range(count):
+    for k in range(bias.shape[1] // hid):
         my_bias += jnp.where(mine == k, bias[:, k * hid : (k + 1) * hid], 0.0)
-    recv = dot(w_recv[...], whole).T
+    recv = dot(w_recv[...], feats[...]).T
     base[...] = 0.5 * (recv.astype(jnp.bfloat16).astype(jnp.float32) + my_bias)
 
 
@@ -528,6 +534,7 @@
     bf16, f32 = jnp.bfloat16, jnp.float32
     shape = jax.ShapeDtypeStruct
 
+    far_route = [(i, (i + (3 if i % 2 else -3)) % shard_count) for i in range(shard_count)]
     across_route = [(i, (i + (1 if i % 2 else -1)) % shard_count) for i in range(shard_count)]
     across = lambda block: lax.ppermute(block, cycle, across_route)
     degrees = in_degree[None, :]
@@ -535,7 +542,8 @@
     sub = lax.axis_index("sub")
 
     feat_blocks = gathered(features, "ch")
-    cot_blocks = gathered(cotangent, "ch")
+    cot_later, feat_blocks[-1] = lax.optimization_barrier((cotangent, feat_blocks[-1]))
+    cot_blocks = gathered(cot_later, "ch")
 
     whole_w = pltpu.VMEM((chans_all, hidden_all), bf16)
     (
@@ -570,7 +578,6 @@
         scratch=[whole_w] * 5 + [pltpu.SemaphoreType.DMA((7,))],
         limit=WEIGHTS_LIMIT,
     )
-    feat_blocks[0] = features_held
     low_cols, high_cols, low_rows, high_rows = call(
         edges_kernel,
         (
@@ -583,24 +590,35 @@
         flops=2 * hidden_all * chans_all * nodes,
         scalars=1,
     )
+    feat_blocks[0], low_cols, high_cols, low_rows, high_rows = lax.optimization_barrier(
+        (features_held, low_cols, high_cols, low_rows, high_rows)
+    )
 
     block = shape((slot_rows + PACK, hid), bf16)
-    feats, proj, base, upper, lower, beside = call(
+    feats, proj, upper, lower, beside, cross = call(
         functools.partial(project_kernel, count),
         (
             shape((chans_all, nodes), bf16),
             shape((nodes, hid), bf16),
-            shape((nodes, hid), f32),
+            block,
             block,
             block,
             block,
         ),
-        [tile_count, picks, bias_edge[None, :]] + feat_blocks + [w_send_my, w_recv_my],
-        flops=4 * hid * chans_all * nodes,
+        [tile_count, picks] + feat_blocks + [w_send_my],
+        flops=2 * hid * chans_all * nodes,
+    )
+    base = call(
+        receive_kernel,
+        shape((nodes, hid), f32),
+        [bias_edge[None, :], feats, w_recv_my],
+        flops=2 * hid * chans_all * nodes,
+        scalars=0,
     )
     west = shifted(upper, "lon", 1)
     east = shifted(lower, "lon", -1)
     beside = shifted(beside, "sub", 1)
+    cross = lax.ppermute(cross, cycle, far_route)
     cots, pre, grad_hidden = call(
         functools.partial(prepare_kernel, count),
         (
@@ -625,7 +643,6 @@
     west, east, part = lax.optimization_barrier((west, east, part))
     west_too = shifted(west, "sub", 1)
     east_too = shifted(east, "sub", 1)
-    cross = across(jnp.where(sub == 0, east, west))
     part, pre = lax.optimization_barrier((part, pre))
     part = call(
         line_kernel,
@@ -694,6 +711,14 @@
         scratch=[pltpu.VMEM((len(LATE) * slot_rows, hid), f32)],
         scalars=0,
     )
+    updated, direct = call(
+        output_kernel,
+        (shape((chans, nodes), bf16), shape((chans, nodes), f32)),
+        [tile_count, features_held, cotangent, w_out_my, w_node_v_t] + hiddens + grad_pres,
+        flops=4 * hidden_all * chans * nodes,
+        scalars=1,
+    )
+    to_west, direct = lax.optimization_barrier((to_west, direct))
     to_west, to_east = call(
         add_kernel,
         (block, block),
@@ -711,14 +736,6 @@
         flops=2 * degree * nodes * nodes * hid,
         scalars=0,
     )
-    updated, direct = call(
-        output_kernel,
-        (shape((chans, nodes), bf16), shape((chans, nodes), f32)),
-        [tile_count, features_held, cotangent, w_out_my, w_node_v_t] + hiddens + grad_pres,
-        flops=4 * hidden_all * chans * nodes,
-        scalars=1,
-    )
-
     columns = chans_all // shard_count
     inv_root = 1.0 / math.sqrt(total_nodes)
     inputs = [tile_count, own, from_beside, feats, from_upper]

time: 79.1 us -> 72.8 us (0.920)
  waiting for transfers between devices: 20.1 us -> 17.8 us
  local copies, waits for them, and re-layouts: 3.57 us -> 1.51 us
  Pallas kernels: 33.2 us -> 31.8 us
    ppermute x2 -> x1, waiting for transfers between devices: 6.86 us -> 2.83 us  [shards(): across = lambda block: lax.ppermute(block, cycle, across_route)]
    ppermute x0 -> x1, waiting for transfers between devices: none -> 2.37 us  [shards(): cross = lax.ppermute(cross, cycle, far_route)]
    unnamed x36 -> x26, local copies, waits for them, and re-layouts: 3.56 us -> 1.5 us
    pallas_call x23 -> x24, Pallas kernels: 33.2 us -> 31.8 us  [call(): pl.pallas_call(kernel, out_shape=out_shape, in_specs=[smem] * scalars + [...]
    ppermute x2 -> x1, starting transfers between devices: 2.22 us -> 1.59 us  [shards(): across = lambda block: lax.ppermute(block, cycle, across_route)]
where the time goes in v6:
time: 72.8 us; the launch traced here: 72.6 us
  Pallas kernels  31.8 us (44%)
  starting transfers between devices  19.9 us (27%)
  waiting for transfers between devices  17.8 us (24%)
  between operations  1.62 us (2%)
  local copies, waits for them, and re-layouts  1.51 us (2%)
    pallas_call x24, Pallas kernels, call(): pl.pallas_call(kernel, out_shape=out_shape, in_specs=[smem] * scalars + [...  31.8 us
    ppermute x18, starting transfers between devices, shifted(): return lax.ppermute(block, axis, route)  18.3 us
    ppermute x18, waiting for transfers between devices, shifted(): return lax.ppermute(block, axis, route)  12.6 us
    ppermute x1, waiting for transfers between devices, shards(): across = lambda block: lax.ppermute(block, cycle, across_route)  2.83 us
    ppermute x1, waiting for transfers between devices, shards(): cross = lax.ppermute(cross, cycle, far_route)  2.37 us
    ppermute x1, starting transfers between devices, shards(): across = lambda block: lax.ppermute(block, cycle, across_route)  1.59 us
    unnamed x26, local copies, waits for them, and re-layouts  1.5 us
  transfers between devices with their start and end apart: 20, of which 11 were waited for; matrix products, arithmetic and copies ran while one was open for 0% of the time, Pallas kernels for 33%

profile of v6, /device:TPU:0, one launch (start us, length us, event | category | flops | bytes accessed | tf_op | source)
XLA Modules:
  0.0 72.6 jit_solution(2474076245138448015)
XLA Ops:
  0.6 3.0 %collective-permute-start = (bf16[256,512]{1,0:T(8,128)(2,1)}, bf16[256,512]{1,0:T(8,128)(2,1)S(1)}, u32[]{:S(2)}, u32[]{:S(2)}) collective-permute-start(bf16[256,512]{1,0:T(8,128)(2,1)} %refs_0_.1), channel_id=1, source_target_pairs={{2,0},{0,2},{3,1},{1,3},{6,4},{4,6},{7,5},{5,7},{10,8},{8,10},{11,... | collective-permute-start | bytes 786440 | tf_op jit(solution)/shard_map/ppermute | solution.py:26
  5.7 1.0 %shard_map.158 = (bf16[12,512,128]{2,1,0:T(8,128)(2,1)S(1)}, bf16[12,512,128]{2,1,0:T(8,128)(2,1)S(1)}, bf16[12,16,512]{2,1,0:T(8,128)(2,1)S(1)}, bf16[12,16,512]{2,1,0:T(8,128)(2,1)S(1)}) custom-call(s32[1]{0:T(128)S(6)} %copy.17.tiles, s32[12,512]{1,0:T(8,128)S(1)} %copy-done.12, s32[1,512]{1,0:T(1,128)S(1)} %bitcast.13), custom_call_target="tpu_custom_call" | custom-call | flops 268435456 | bytes 26628 | tf_op jit(solution)/shard_map/pallas_call | solution.py:52
  6.8 3.5 %shard_map.157 = (bf16[256,512]{1,0:T(8,128)(2,1)S(1)}, bf16[256,512]{1,0:T(8,128)(2,1)S(1)}, bf16[256,512]{1,0:T(8,128)(2,1)S(1)}, bf16[256,512]{1,0:T(8,128)(2...) custom-call(bf16[256,512]{1,0:T(8,128)(2,1)} %refs_0_.1, ...), custom_call_target="tpu_custom_call" | custom-call | flops 536870912 | bytes 3407872 | tf_op jit(solution)/shard_map/pallas_call | solution.py:52
  10.3 1.1 %shard_map.159 = (bf16[512,512]{1,0:T(8,128)(2,1)S(1)}, bf16[512,256]{1,0:T(8,128)(2,1)S(1)}, bf16[272,256]{1,0:T(8,128)(2,1)S(1)}, bf16[272,256]{1,0:T(8,128)(2...) custom-call(s32[1]{0:T(128)S(6)} %copy.17.tiles, s32[1,2,6]{2,1,0:T(2,128)S(1)} %bitcast.20, ...), custom_call_target="tpu_custom_call" | custom-call | flops 134217728 | bytes 786484 | tf_op jit(solution)/shard_map/pallas_call | solution.py:52
  11.5 1.7 %collective-permute-start.4 = (bf16[256,512]{1,0:T(8,128)(2,1)S(1)}, bf16[256,512]{1,0:T(8,128)(2,1)S(1)}, u32[]{:S(2)}, u32[]{:S(2)}) collective-permute-start(bf16[256,512]{1,0:T(8,128)(2,1)S(1)} %copy-done.4), channel_id=1, source_target_pairs={{2,0},{0,2},{3,1},{1,3},{6,4},{4,6},{7,5},{5,7},{10,8},{8,10},{11,... | collective-permute-start | bytes 786440 | tf_op jit(solution)/shard_map/ppermute | solution.py:26
  13.1 1.6 %collective-permute-start.1 = (bf16[272,256]{1,0:T(8,128)(2,1)S(1)}, bf16[272,256]{1,0:T(8,128)(2,1)S(1)}, u32[]{:S(2)}, u32[]{:S(2)}) collective-permute-start(bf16[272,256]{1,0:T(8,128)(2,1)S(1)} %get-tuple-element.87), channel_id=1, source_target_pairs={{12,0},{0,4},{4,8},{8,12},{13,1},{1,5},{5,9},{9,13},{14,2},{2,6},{... | collective-permute-start | bytes 417800 | tf_op jit(solution)/shard_map/ppermute | solution.py:26
  14.7 2.2 %collective-permute-start.2 = (bf16[272,256]{1,0:T(8,128)(2,1)S(1)}, bf16[272,256]{1,0:T(8,128)(2,1)S(1)}, u32[]{:S(2)}, u32[]{:S(2)}) collective-permute-start(bf16[272,256]{1,0:T(8,128)(2,1)S(1)} %get-tuple-element.88), channel_id=1, source_target_pairs={{4,0},{8,4},{12,8},{0,12},{5,1},{9,5},{13,9},{1,13},{6,2},{10,6},{... | collective-permute-start | bytes 417800 | tf_op jit(solution)/shard_map/ppermute | solution.py:26
  17.4 2.8 %shard_map.161.before = bf16[12,512,256]{2,1,0:T(8,128)(2,1)S(1)} custom-call(bf16[12,512,128]{2,1,0:T(8,128)(2,1)S(1)} %get-tuple-element.80.low, bf16[12,512,128]{2,1,0:T(8,128)(2,1)S(1)} %get-tuple-element.81.high, bf16[512,256]{1,0:T(8,128)(2,1)S(1)} %get-tuple-element.89.proj, bf16[272,256]{1,0:T(8,128)(2,1)S(1)} %collective-permute-done.3.beside.refs_1_), custom_call_target="tpu_custom_call" | custom-call | flops 2415919104 | bytes 3547136 | tf_op jit(solution)/shard_map/pallas_call | solution.py:52
  20.2 1.3 %collective-permute-done.1.west.refs_2_ = bf16[272,256]{1,0:T(8,128)(2,1)S(1)} collective-permute-done((bf16[272,256]{1,0:T(8,128)(2,1)S(1)}, bf16[272,256]{1,0:T(8,128)(2,1)S(1)}, u32[]{:S(2)}, u32[]{:S(2)}) %collective-permute-start.1) | collective-permute-done | bytes 139296 | tf_op jit(solution)/shard_map/ppermute | solution.py:26
  21.5 1.7 %collective-permute-done.2.east.refs_3_ = bf16[272,256]{1,0:T(8,128)(2,1)S(1)} collective-permute-done((bf16[272,256]{1,0:T(8,128)(2,1)S(1)}, bf16[272,256]{1,0:T(8,128)(2,1)S(1)}, u32[]{:S(2)}, u32[]{:S(2)}) %collective-permute-start.2) | collective-permute-done | bytes 139296 | tf_op jit(solution)/shard_map/ppermute | solution.py:26
  23.7 1.1 %shard_map.162 = (bf16[512,512]{1,0:T(8,128)(2,1)}, f32[512,512]{1,0:T(8,128)S(1)}, f32[512,512]{1,0:T(8,128)S(1)}) custom-call(s32[1]{0:T(128)S(6)} %copy.17.tiles, bf16[256,512]{1,0:T(8,128)(2,1)S(1)} %copy-done.4, bf16[256,512]{1,0:T(8,128)(2,1)S(1)} %collective-permute-done.4.refs_1_, bf16[512,512]{1,0:T(8,128)(2,1)S(1)} %get-tuple-element.85.feats.refs_2_, ...), custom_call_target="tpu_custom_call" | custom-call | flops 536870912 | bytes 2099204 | tf_op jit(solution)/shard_map/pallas_call | solution.py:52
  24.8 2.4 %shard_map.163.part = bf16[12,512,256]{2,1,0:T(8,128)(2,1)S(1)} custom-call(bf16[12,512,128]{2,1,0:T(8,128)(2,1)S(1)} %get-tuple-element.80.low, bf16[12,512,128]{2,1,0:T(8,128)(2,1)S(1)} %get-tuple-element.81.high, bf16[12,512,256]{2,1,0:T(8,128)(2,1)S(1)} %shard_map.161.before, bf16[272,256]{1,0:T(8,128)(2,1)S(1)} %collective-permute-done.1.west.refs_2_, ...), custom_call_target="tpu_custom_call" | custom-call | flops 1610612736 | bytes 6569984 | tf_op jit(solution)/shard_map/pallas_call | solution.py:52
  27.2 2.4 %collective-permute-done.5.cross.refs_2_ = bf16[272,256]{1,0:T(8,128)(2,1)S(1)} collective-permute-done((bf16[272,256]{1,0:T(8,128)(2,1)S(1)}, bf16[272,256]{1,0:T(8,128)(2,1)S(1)}, u32[]{:S(2)}, u32[]{:S(2)}) %collective-permute-start.5) | collective-permute-done | bytes 139296 | tf_op jit(solution)/shard_map/ppermute | solution.py:621
  29.6 2.4 %shard_map.164 = (bf16[256,256]{1,0:T(8,128)(2,1)S(1)}, bf16[12,256,256]{2,1,0:T(8,128)(2,1)S(1)}) custom-call(bf16[12,512,128]{2,1,0:T(8,128)(2,1)S(1)} %get-tuple-element.80.low, bf16[12,512,128]{2,1,0:T(8,128)(2,1)S(1)} %get-tuple-element.81.high, f32[512,256]{1,0:T(8,128)S(1)} %shard_map.160.base, s32[1,512]{1,0:T(1,128)S(1)} %bitcast.14, ...), custom_call_target="tpu_custom_call" | custom-call | flops 1207959552 | bytes 7235584 | tf_op jit(solution)/shard_map/pallas_call | solution.py:52
  32.6 2.4 %shard_map.166 = (bf16[256,256]{1,0:T(8,128)(2,1)S(1)}, bf16[12,256,256]{2,1,0:T(8,128)(2,1)S(1)}) custom-call(bf16[12,512,128]{2,1,0:T(8,128)(2,1)S(1)} %get-tuple-element.80.low, bf16[12,512,128]{2,1,0:T(8,128)(2,1)S(1)} %get-tuple-element.81.high, f32[512,256]{1,0:T(8,128)S(1)} %shard_map.160.base, s32[1,512]{1,0:T(1,128)S(1)} %bitcast.15, ...), custom_call_target="tpu_custom_call" | custom-call | flops 1207959552 | bytes 7235584 | tf_op jit(solution)/shard_map/pallas_call | solution.py:52
  35.1 1.6 %collective-permute-start.9 = (bf16[256,256]{1,0:T(8,128)(2,1)S(1)}, bf16[256,256]{1,0:T(8,128)(2,1)S(1)}, u32[]{:S(2)}, u32[]{:S(2)}) collective-permute-start(bf16[256,256]{1,0:T(8,128)(2,1)S(1)} %get-tuple-element.105.refs_0_), channel_id=1, source_target_pairs={{2,0},{0,2},{3,1},{1,3},{6,4},{4,6},{7,5},{5,7},{10,8},{8,10},{11,... | collective-permute-start | bytes 393224 | tf_op jit(solution)/shard_map/ppermute | solution.py:26
  36.6 1.0 %collective-permute-done.8.refs_1_ = bf16[256,256]{1,0:T(8,128)(2,1)S(1)} collective-permute-done((bf16[256,256]{1,0:T(8,128)(2,1)S(1)}, bf16[256,256]{1,0:T(8,128)(2,1)S(1)}, u32[]{:S(2)}, u32[]{:S(2)}) %collective-permute-start.8) | collective-permute-done | bytes 131104 | tf_op jit(solution)/shard_map/ppermute | solution.py:26
  37.6 1.3 %shard_map.165 = (bf16[512,256]{1,0:T(8,128)(2,1)S(1)}, bf16[512,256]{1,0:T(8,128)(2,1)S(1)}, f32[256,256]{1,0:T(8,128)S(1)}) custom-call(s32[1,512]{1,0:T(1,128)S(1)} %bitcast.16, bf16[256,256]{1,0:T(8,128)(2,1)S(1)} %get-tuple-element.99.refs_0_, bf16[256,256]{1,0:T(8,128)(2,1)S(1)} %collective-permute-done.8.refs_1_, bf16[512,512]{1,0:T(8,128)(2,1)S(1)} %copy-done, ...), custom_call_target="tpu_custom_call" | custom-call | flops 402653184 | bytes 4196352 | tf_op jit(solution)/shard_map/pallas_call | solution.py:52
  39.0 2.1 %shard_map.169 = (bf16[12,256,256]{2,1,0:T(8,128)(2,1)S(1)}, f32[1024,256]{1,0:T(8,128)S(1)}) custom-call(bf16[12,16,512]{2,1,0:T(8,128)(2,1)S(1)} %get-tuple-element.110.low, bf16[12,16,512]{2,1,0:T(8,128)(2,1)S(1)} %get-tuple-element.111.high, bf16[12,256,256]{2,1,0:T(8,128)(2,1)S(1)} %get-tuple-element.112.slope, f32[256,256]{1,0:T(8,128)S(1)} %get-tuple-element.113.scale), custom_call_target="tpu_custom_call" | custom-call | flops 1610612736 | bytes 2228224 | tf_op jit(solution)/shard_map/pallas_call | solution.py:52
  41.1 1.3 %shard_map.167 = (bf16[512,256]{1,0:T(8,128)(2,1)S(1)}, bf16[512,256]{1,0:T(8,128)(2,1)S(1)}, f32[256,256]{1,0:T(8,128)S(1)}) custom-call(s32[1,512]{1,0:T(1,128)S(1)} %bitcast.17, bf16[256,256]{1,0:T(8,128)(2,1)S(1)} %get-tuple-element.105.refs_0_, bf16[256,256]{1,0:T(8,128)(2,1)S(1)} %collective-permute-done.9.refs_1_, bf16[512,512]{1,0:T(8,128)(2,1)S(1)} %copy-done, ...), custom_call_target="tpu_custom_call" | custom-call | flops 402653184 | bytes 4196352 | tf_op jit(solution)/shard_map/pallas_call | solution.py:52
  42.4 1.9 %shard_map.170 = (bf16[256,256]{1,0:T(8,128)(2,1)S(1)}, bf16[3,256,256]{2,1,0:T(8,128)(2,1)S(1)}, bf16[12,256,256]{2,1,0:T(8,128)(2,1)S(1)}) custom-call(bf16[12,16,512]{2,1,0:T(8,128)(2,1)S(1)} %get-tuple-element.110.low, bf16[12,16,512]{2,1,0:T(8,128)(2,1)S(1)} %get-tuple-element.111.high, bf16[12,256,256]{2,1,0:T(8,128)(2,1)S(1)} %get-tuple-element.115.slope, ...), custom_call_target="tpu_custom_call" | custom-call | flops 1610612736 | bytes 3833856 | tf_op jit(solution)/shard_map/pallas_call | solution.py:52
  44.4 1.6 %collective-permute-start.11 = (bf16[256,256]{1,0:T(8,128)(2,1)S(1)}, bf16[256,256]{1,0:T(8,128)(2,1)S(1)}, u32[]{:S(2)}, u32[]{:S(2)}) collective-permute-start(bf16[256,256]{1,0:T(8,128)(2,1)S(1)} %get-tuple-element.125), channel_id=1, source_target_pairs={{0,13},{1,4},{4,1},{5,8},{8,5},{9,12},{12,9},{13,0},{2,15},{3,6},{... | collective-permute-start | bytes 393224 | tf_op jit(solution)/shard_map/ppermute | solution.py:539
  46.0 1.1 %shard_map.168 = (bf16[256,512]{1,0:T(8,128)(2,1)}, f32[256,512]{1,0:T(8,128)S(1)}) custom-call(s32[1]{0:T(128)S(6)} %copy.17.tiles, bf16[256,512]{1,0:T(8,128)(2,1)S(1)} %get-tuple-element.82.refs_0_.feats, bf16[256,512]{1,0:T(8,128)(2,1)S(1)} %copy-done.4, bf16[256,512]{1,0:T(8,128)(2,1)S(1)} %get-tuple-element.74.w_out, bf16[256,512]{1,0:T(8,128)(2,1)S(1)} %copy-done.6, ...), custom_call_target="tpu_custom_call" | custom-call | flops 268435456 | bytes 2097156 | tf_op jit(solution)/shard_map/pallas_call | solution.py:52
  47.1 1.8 %shard_map.172 = (bf16[256,256]{1,0:T(8,128)(2,1)S(1)}, bf16[256,256]{1,0:T(8,128)(2,1)S(1)}) custom-call(bf16[12,16,512]{2,1,0:T(8,128)(2,1)S(1)} %get-tuple-element.110.low, bf16[12,16,512]{2,1,0:T(8,128)(2,1)S(1)} %get-tuple-element.111.high, bf16[12,256,256]{2,1,0:T(8,128)(2,1)S(1)} %get-tuple-element.114.refs_0_, ...), custom_call_target="tpu_custom_call" | custom-call | flops 1610612736 | bytes 3817472 | tf_op jit(solution)/shard_map/pallas_call | solution.py:52
  48.9 2.8 %collective-permute-done.11.across = bf16[256,256]{1,0:T(8,128)(2,1)S(1)} collective-permute-done((bf16[256,256]{1,0:T(8,128)(2,1)S(1)}, bf16[256,256]{1,0:T(8,128)(2,1)S(1)}, u32[]{:S(2)}, u32[]{:S(2)}) %collective-permute-start.11) | collective-permute-done | bytes 131104 | tf_op jit(solution)/shard_map/ppermute | solution.py:539
  51.9 2.0 %collective-permute-start.13 = (bf16[256,256]{1,0:T(8,128)(2,1)S(1)}, bf16[256,256]{1,0:T(8,128)(2,1)S(1)}, u32[]{:S(2)}, u32[]{:S(2)}) collective-permute-start(bf16[256,256]{1,0:T(8,128)(2,1)S(1)} %get-tuple-element.127), channel_id=1, source_target_pairs={{12,0},{0,4},{4,8},{8,12},{13,1},{1,5},{5,9},{9,13},{14,2},{2,6},{... | collective-permute-start | bytes 393224 | tf_op jit(solution)/shard_map/ppermute | solution.py:26
  53.9 2.1 %shard_map.171 = (f32[512,256]{1,0:T(8,128)S(1)}, bf16[256,512]{1,0:T(8,128)(2,1)S(1)}) custom-call(bf16[12,16,512]{2,1,0:T(8,128)(2,1)S(1)} %get-tuple-element.110.low, bf16[12,16,512]{2,1,0:T(8,128)(2,1)S(1)} %get-tuple-element.111.high, bf16[12,256,256]{2,1,0:T(8,128)(2,1)S(1)} %get-tuple-element.114.refs_0_, ...), custom_call_target="tpu_custom_call" | custom-call | flops 1610612736 | bytes 3538944 | tf_op jit(solution)/shard_map/pallas_call | solution.py:52
  57.2 3.0 %collective-permute-done.13.refs_0_ = bf16[256,256]{1,0:T(8,128)(2,1)S(1)} collective-permute-done((bf16[256,256]{1,0:T(8,128)(2,1)S(1)}, bf16[256,256]{1,0:T(8,128)(2,1)S(1)}, u32[]{:S(2)}, u32[]{:S(2)}) %collective-permute-start.13) | collective-permute-done | bytes 131104 | tf_op jit(solution)/shard_map/ppermute | solution.py:26
  62.5 1.3 %collective-permute-start.15 = (bf16[256,256]{1,0:T(8,128)(2,1)S(1)}, bf16[256,256]{1,0:T(8,128)(2,1)S(1)}, u32[]{:S(2)}, u32[]{:S(2)}) collective-permute-start(bf16[256,256]{1,0:T(8,128)(2,1)S(1)} %bitcast.22), channel_id=1, source_target_pairs={{2,0},{0,2},{3,1},{1,3},{6,4},{4,6},{7,5},{5,7},{10,8},{8,10},{11,... | collective-permute-start | bytes 393224 | tf_op jit(solution)/shard_map/ppermute | solution.py:26
  63.8 1.8 %collective-permute-start.19 = (bf16[64,256]{1,0:T(8,128)(2,1)S(1)}, bf16[64,256]{1,0:T(8,128)(2,1)S(1)}, u32[]{:S(2)}, u32[]{:S(2)}) collective-permute-start(bf16[64,256]{1,0:T(8,128)(2,1)S(1)} %get-tuple-element.143), channel_id=1, source_target_pairs={{4,0},{8,4},{12,8},{0,12},{5,1},{9,5},{13,9},{1,13},{6,2},{10,6},{... | collective-permute-start | bytes 98312 | tf_op jit(solution)/shard_map/ppermute | solution.py:26
  67.5 2.4 %collective-permute-done.15.refs_3_ = bf16[256,256]{1,0:T(8,128)(2,1)S(1)} collective-permute-done((bf16[256,256]{1,0:T(8,128)(2,1)S(1)}, bf16[256,256]{1,0:T(8,128)(2,1)S(1)}, u32[]{:S(2)}, u32[]{:S(2)}) %collective-permute-start.15) | collective-permute-done | bytes 131104 | tf_op jit(solution)/shard_map/ppermute | solution.py:26
  70.9 1.1 %collective-permute-done.17.refs_0_ = bf16[64,256]{1,0:T(8,128)(2,1)S(1)} collective-permute-done((bf16[64,256]{1,0:T(8,128)(2,1)S(1)}, bf16[64,256]{1,0:T(8,128)(2,1)S(1)}, u32[]{:S(2)}, u32[]{:S(2)}) %collective-permute-start.17) | collective-permute-done | bytes 32800 | tf_op jit(solution)/shard_map/ppermute | solution.py:26
  (59 shorter events, 10.2 us)
Async XLA Ops:
  0.6 9.7 %collective-permute-start = (bf16[256,512]{1,0:T(8,128)(2,1)}, bf16[256,512]{1,0:T(8,128)(2,1)S(1)}, u32[]{:S(2)}, u32[]{:S(2)}) collective-permute-start(bf16[256,512]{1,0:T(8,128)(2,1)} %refs_0_.1), channel_id=1, source_target_pairs={{2,0},{0,2},{3,1},{1,3},{6,4},{4,6},{7,5},{5,7},{10,8},{8,10},{11,... | collective-permute-start | bytes 786440 | tf_op jit(solution)/shard_map/ppermute | solution.py:26
  5.0 0.8 %copy-start.12 = (s32[12,512]{1,0:T(8,128)S(1)}, s32[12,512]{1,0:T(8,128)}, u32[]{:S(2)}) copy-start(s32[12,512]{1,0:T(8,128)} %senders.1) | copy-start | bytes 73732
  6.8 3.5 %copy-start.11 = (s32[1,6,2]{1,2,0:T(2,128)S(1)}, s32[1,6,2]{1,2,0:T(2,128)}, u32[]{:S(2)}) copy-start(s32[1,6,2]{1,2,0:T(2,128)} %param.19) | copy-start | bytes 148
  6.8 4.7 %copy-start.4 = (bf16[256,512]{1,0:T(8,128)(2,1)S(1)}, bf16[256,512]{1,0:T(8,128)(2,1)}, u32[]{:S(2)}) copy-start(bf16[256,512]{1,0:T(8,128)(2,1)} %cots.1) | copy-start | bytes 786436
  6.8 10.2 %copy-start.9 = (f32[512]{0:T(512)S(1)}, f32[512]{0:T(512)}, u32[]{:S(2)}) copy-start(f32[512]{0:T(512)} %param.22) | copy-start | bytes 6148
  11.4 6.0 %collective-permute-start.3 = (bf16[272,256]{1,0:T(8,128)(2,1)S(1)}, bf16[272,256]{1,0:T(8,128)(2,1)S(1)}, u32[]{:S(2)}, u32[]{:S(2)}) collective-permute-start(bf16[272,256]{1,0:T(8,128)(2,1)S(1)} %get-tuple-element.90), channel_id=1, source_target_pairs={{1,0},{0,1},{3,2},{2,3},{5,4},{4,5},{7,6},{6,7},{9,8},{8,9},{11,10... | collective-permute-start | bytes 417800 | tf_op jit(solution)/shard_map/ppermute | solution.py:26
  11.5 12.2 %collective-permute-start.4 = (bf16[256,512]{1,0:T(8,128)(2,1)S(1)}, bf16[256,512]{1,0:T(8,128)(2,1)S(1)}, u32[]{:S(2)}, u32[]{:S(2)}) collective-permute-start(bf16[256,512]{1,0:T(8,128)(2,1)S(1)} %copy-done.4), channel_id=1, source_target_pairs={{2,0},{0,2},{3,1},{1,3},{6,4},{4,6},{7,5},{5,7},{10,8},{8,10},{11,... | collective-permute-start | bytes 786440 | tf_op jit(solution)/shard_map/ppermute | solution.py:26
  13.1 8.3 %collective-permute-start.1 = (bf16[272,256]{1,0:T(8,128)(2,1)S(1)}, bf16[272,256]{1,0:T(8,128)(2,1)S(1)}, u32[]{:S(2)}, u32[]{:S(2)}) collective-permute-start(bf16[272,256]{1,0:T(8,128)(2,1)S(1)} %get-tuple-element.87), channel_id=1, source_target_pairs={{12,0},{0,4},{4,8},{8,12},{13,1},{1,5},{5,9},{9,13},{14,2},{2,6},{... | collective-permute-start | bytes 417800 | tf_op jit(solution)/shard_map/ppermute | solution.py:26
  14.7 8.4 %collective-permute-start.2 = (bf16[272,256]{1,0:T(8,128)(2,1)S(1)}, bf16[272,256]{1,0:T(8,128)(2,1)S(1)}, u32[]{:S(2)}, u32[]{:S(2)}) collective-permute-start(bf16[272,256]{1,0:T(8,128)(2,1)S(1)} %get-tuple-element.88), channel_id=1, source_target_pairs={{4,0},{8,4},{12,8},{0,12},{5,1},{9,5},{13,9},{1,13},{6,2},{10,6},{... | collective-permute-start | bytes 417800 | tf_op jit(solution)/shard_map/ppermute | solution.py:26
  17.0 12.6 %collective-permute-start.5 = (bf16[272,256]{1,0:T(8,128)(2,1)S(1)}, bf16[272,256]{1,0:T(8,128)(2,1)S(1)}, u32[]{:S(2)}, u32[]{:S(2)}) collective-permute-start(bf16[272,256]{1,0:T(8,128)(2,1)S(1)} %get-tuple-element.98), channel_id=1, source_target_pairs={{0,9},{1,8},{4,13},{5,12},{8,1},{9,0},{12,5},{13,4},{2,11},{3,10},... | collective-permute-start | bytes 417800 | tf_op jit(solution)/shard_map/ppermute | solution.py:621
  17.4 6.3 %copy-start.2 = (bf16[512,512]{1,0:T(8,128)(2,1)S(1)}, bf16[512,512]{1,0:T(8,128)(2,1)}, u32[]{:S(2)}) copy-start(bf16[512,512]{1,0:T(8,128)(2,1)} %refs_3_.5) | copy-start | bytes 1572868
  17.4 6.3 %copy-start.5 = (bf16[512,512]{1,0:T(8,128)(2,1)S(1)}, bf16[512,512]{1,0:T(8,128)(2,1)}, u32[]{:S(2)}) copy-start(bf16[512,512]{1,0:T(8,128)(2,1)} %get-tuple-element.93.refs_5_) | copy-start | bytes 1572868
  17.4 6.3 %copy-start.10 = (f32[512]{0:T(512)S(1)}, f32[512]{0:T(512)}, u32[]{:S(2)}) copy-start(f32[512]{0:T(512)} %param.26) | copy-start | bytes 6148
  23.1 6.4 %collective-permute-start.6 = (bf16[272,256]{1,0:T(8,128)(2,1)S(1)}, bf16[272,256]{1,0:T(8,128)(2,1)S(1)}, u32[]{:S(2)}, u32[]{:S(2)}) collective-permute-start(bf16[272,256]{1,0:T(8,128)(2,1)S(1)} %collective-permute-done.1.west.refs_2_), channel_id=1, source_target_pairs={{1,0},{0,1},{3,2},{2,3},{5,4},{4,5},{7,6},{6,7},{9,8},{8,9},{11,10... | collective-permute-start | bytes 417800 | tf_op jit(solution)/shard_map/ppermute | solution.py:26
  23.1 6.4 %collective-permute-start.7 = (bf16[272,256]{1,0:T(8,128)(2,1)S(1)}, bf16[272,256]{1,0:T(8,128)(2,1)S(1)}, u32[]{:S(2)}, u32[]{:S(2)}) collective-permute-start(bf16[272,256]{1,0:T(8,128)(2,1)S(1)} %collective-permute-done.2.east.refs_3_), channel_id=1, source_target_pairs={{1,0},{0,1},{3,2},{2,3},{5,4},{4,5},{7,6},{6,7},{9,8},{8,9},{11,10... | collective-permute-start | bytes 417800 | tf_op jit(solution)/shard_map/ppermute | solution.py:26
  24.8 4.8 %copy-start.8 = (s32[512]{0:T(512)S(1)}, s32[512]{0:T(512)}, u32[]{:S(2)}) copy-start(s32[512]{0:T(512)} %param.17) | copy-start | bytes 6148
  32.0 5.6 %copy-start = (bf16[512,512]{1,0:T(8,128)(2,1)S(1)}, bf16[512,512]{1,0:T(8,128)(2,1)}, u32[]{:S(2)}) copy-start(bf16[512,512]{1,0:T(8,128)(2,1)} %refs_2_.5) | copy-start | bytes 1572868
  32.0 5.6 %copy-start.1 = (bf16[512,512]{1,0:T(8,128)(2,1)S(1)}, bf16[512,512]{1,0:T(8,128)(2,1)}, u32[]{:S(2)}) copy-start(bf16[512,512]{1,0:T(8,128)(2,1)} %refs_3_.7) | copy-start | bytes 1572868
  32.0 5.6 %copy-start.3 = (bf16[512,512]{1,0:T(8,128)(2,1)S(1)}, bf16[512,512]{1,0:T(8,128)(2,1)}, u32[]{:S(2)}) copy-start(bf16[512,512]{1,0:T(8,128)(2,1)} %get-tuple-element.100.refs_4_) | copy-start | bytes 1572868
  32.0 5.6 %collective-permute-start.8 = (bf16[256,256]{1,0:T(8,128)(2,1)S(1)}, bf16[256,256]{1,0:T(8,128)(2,1)S(1)}, u32[]{:S(2)}, u32[]{:S(2)}) collective-permute-start(bf16[256,256]{1,0:T(8,128)(2,1)S(1)} %get-tuple-element.99.refs_0_), channel_id=1, source_target_pairs={{2,0},{0,2},{3,1},{1,3},{6,4},{4,6},{7,5},{5,7},{10,8},{8,10},{11,... | collective-permute-start | bytes 393224 | tf_op jit(solution)/shard_map/ppermute | solution.py:26
  35.1 6.0 %collective-permute-start.9 = (bf16[256,256]{1,0:T(8,128)(2,1)S(1)}, bf16[256,256]{1,0:T(8,128)(2,1)S(1)}, u32[]{:S(2)}, u32[]{:S(2)}) collective-permute-start(bf16[256,256]{1,0:T(8,128)(2,1)S(1)} %get-tuple-element.105.refs_0_), channel_id=1, source_target_pairs={{2,0},{0,2},{3,1},{1,3},{6,4},{4,6},{7,5},{5,7},{10,8},{8,10},{11,... | collective-permute-start | bytes 393224 | tf_op jit(solution)/shard_map/ppermute | solution.py:26
  42.4 3.5 %copy-start.6 = (bf16[256,512]{1,0:T(8,128)(2,1)S(1)}, bf16[256,512]{1,0:T(8,128)(2,1)}, u32[]{:S(2)}) copy-start(bf16[256,512]{1,0:T(8,128)(2,1)} %get-tuple-element.75.w_node_v_t) | copy-start | bytes 786436
  44.3 7.4 %collective-permute-start.10 = (bf16[3,256,256]{2,1,0:T(8,128)(2,1)S(1)}, bf16[3,256,256]{2,1,0:T(8,128)(2,1)S(1)}, u32[]{:S(2)}, u32[]{:S(2)}) collective-permute-start(bf16[3,256,256]{2,1,0:T(8,128)(2,1)S(1)} %get-tuple-element.120), channel_id=1, source_target_pairs={{1,0},{0,1},{3,2},{2,3},{5,4},{4,5},{7,6},{6,7},{9,8},{8,9},{11,10... | collective-permute-start | bytes 1179656 | tf_op jit(solution)/shard_map/ppermute | solution.py:26
  44.4 7.4 %collective-permute-start.11 = (bf16[256,256]{1,0:T(8,128)(2,1)S(1)}, bf16[256,256]{1,0:T(8,128)(2,1)S(1)}, u32[]{:S(2)}, u32[]{:S(2)}) collective-permute-start(bf16[256,256]{1,0:T(8,128)(2,1)S(1)} %get-tuple-element.125), channel_id=1, source_target_pairs={{0,13},{1,4},{4,1},{5,8},{8,5},{9,12},{12,9},{13,0},{2,15},{3,6},{... | collective-permute-start | bytes 393224 | tf_op jit(solution)/shard_map/ppermute | solution.py:539
  51.9 5.0 %collective-permute-start.12 = (bf16[256,256]{1,0:T(8,128)(2,1)S(1)}, bf16[256,256]{1,0:T(8,128)(2,1)S(1)}, u32[]{:S(2)}, u32[]{:S(2)}) collective-permute-start(bf16[256,256]{1,0:T(8,128)(2,1)S(1)} %get-tuple-element.126), channel_id=1, source_target_pairs={{4,0},{8,4},{12,8},{0,12},{5,1},{9,5},{13,9},{1,13},{6,2},{10,6},{... | collective-permute-start | bytes 393224 | tf_op jit(solution)/shard_map/ppermute | solution.py:26
  51.9 8.3 %collective-permute-start.13 = (bf16[256,256]{1,0:T(8,128)(2,1)S(1)}, bf16[256,256]{1,0:T(8,128)(2,1)S(1)}, u32[]{:S(2)}, u32[]{:S(2)}) collective-permute-start(bf16[256,256]{1,0:T(8,128)(2,1)S(1)} %get-tuple-element.127), channel_id=1, source_target_pairs={{12,0},{0,4},{4,8},{8,12},{13,1},{1,5},{5,9},{9,13},{14,2},{2,6},{... | collective-permute-start | bytes 393224 | tf_op jit(solution)/shard_map/ppermute | solution.py:26
  60.6 3.2 %collective-permute-start.16 = (bf16[4,64,256]{2,1,0:T(8,128)(2,1)S(1)}, bf16[4,64,256]{2,1,0:T(8,128)(2,1)S(1)}, u32[]{:S(2)}, u32[]{:S(2)}) collective-permute-start(bf16[4,64,256]{2,1,0:T(8,128)(2,1)S(1)} %get-tuple-element.140), channel_id=1, source_target_pairs={{1,0},{0,1},{3,2},{2,3},{5,4},{4,5},{7,6},{6,7},{9,8},{8,9},{11,10... | collective-permute-start | bytes 393224 | tf_op jit(solution)/shard_map/ppermute | solution.py:26
  61.2 6.4 %collective-permute-start.14 = (bf16[256,256]{1,0:T(8,128)(2,1)S(1)}, bf16[256,256]{1,0:T(8,128)(2,1)S(1)}, u32[]{:S(2)}, u32[]{:S(2)}) collective-permute-start(bf16[256,256]{1,0:T(8,128)(2,1)S(1)} %bitcast.21), channel_id=1, source_target_pairs={{2,0},{0,2},{3,1},{1,3},{6,4},{4,6},{7,5},{5,7},{10,8},{8,10},{11,... | collective-permute-start | bytes 393224 | tf_op jit(solution)/shard_map/ppermute | solution.py:26
  62.5 7.5 %collective-permute-start.15 = (bf16[256,256]{1,0:T(8,128)(2,1)S(1)}, bf16[256,256]{1,0:T(8,128)(2,1)S(1)}, u32[]{:S(2)}, u32[]{:S(2)}) collective-permute-start(bf16[256,256]{1,0:T(8,128)(2,1)S(1)} %bitcast.22), channel_id=1, source_target_pairs={{2,0},{0,2},{3,1},{1,3},{6,4},{4,6},{7,5},{5,7},{10,8},{8,10},{11,... | collective-permute-start | bytes 393224 | tf_op jit(solution)/shard_map/ppermute | solution.py:26
  63.8 6.9 %collective-permute-start.19 = (bf16[64,256]{1,0:T(8,128)(2,1)S(1)}, bf16[64,256]{1,0:T(8,128)(2,1)S(1)}, u32[]{:S(2)}, u32[]{:S(2)}) collective-permute-start(bf16[64,256]{1,0:T(8,128)(2,1)S(1)} %get-tuple-element.143), channel_id=1, source_target_pairs={{4,0},{8,4},{12,8},{0,12},{5,1},{9,5},{13,9},{1,13},{6,2},{10,6},{... | collective-permute-start | bytes 98312 | tf_op jit(solution)/shard_map/ppermute | solution.py:26
  65.6 5.2 %collective-permute-start.18 = (bf16[64,256]{1,0:T(8,128)(2,1)S(1)}, bf16[64,256]{1,0:T(8,128)(2,1)S(1)}, u32[]{:S(2)}, u32[]{:S(2)}) collective-permute-start(bf16[64,256]{1,0:T(8,128)(2,1)S(1)} %get-tuple-element.144), channel_id=1, source_target_pairs={{8,0},{12,4},{0,8},{4,12},{9,1},{13,5},{1,9},{5,13},{10,2},{14,6},... | collective-permute-start | bytes 98312 | tf_op jit(solution)/shard_map/ppermute | solution.py:26
  66.2 5.7 %collective-permute-start.17 = (bf16[64,256]{1,0:T(8,128)(2,1)S(1)}, bf16[64,256]{1,0:T(8,128)(2,1)S(1)}, u32[]{:S(2)}, u32[]{:S(2)}) collective-permute-start(bf16[64,256]{1,0:T(8,128)(2,1)S(1)} %get-tuple-element.145), channel_id=1, source_target_pairs={{12,0},{0,4},{4,8},{8,12},{13,1},{1,5},{5,9},{9,13},{14,2},{2,6},{... | collective-permute-start | bytes 98312 | tf_op jit(solution)/shard_map/ppermute | solution.py:26
  (1 other events, 0.7 us)

commit v7 on v6

--- a/solution.py
+++ b/solution.py
@@ -16,7 +16,7 @@
 WEIGHTS_LIMIT = 52
 NO_CHUNK = 64
 SLOT_OF = ((3, 0), (1, 1), (4, 4), (2, 5), (0, 2), (5, 3))
-EARLY, LATE = (0, 3, 4, 5), (1, 2)
+EARLY, LATE = (3, 4, 5), (1, 2, 0)
 OFF = -1e4
 
 
@@ -44,11 +44,10 @@
     return 0.5 * jnp.tanh(0.5 * value) + 0.5
 
 
-def call(kernel, out_shape, operands, flops, scratch=(), scalars=2, away=0, limit=24):
+def call(kernel, out_shape, operands, scratch=(), scalars=2, away=0, limit=24):
     vmem = pl.BlockSpec(memory_space=pltpu.VMEM)
     smem = pl.BlockSpec(memory_space=pltpu.SMEM)
     anywhere = pl.BlockSpec(memory_space=pltpu.HBM)
-    moved = sum(math.prod(x.shape) * x.dtype.itemsize for x in operands)
     return pl.pallas_call(
         kernel,
         out_shape=out_shape,
@@ -58,7 +57,7 @@
         out_specs=jax.tree.map(lambda _: vmem, out_shape),
         scratch_shapes=scratch,
         compiler_params=pltpu.CompilerParams(vmem_limit_bytes=limit * MIB),
-        cost_estimate=pl.CostEstimate(flops=flops, bytes_accessed=moved, transcendentals=0),
+        cost_estimate=pl.CostEstimate(flops=1024, bytes_accessed=1024, transcendentals=0),
     )(*operands)
 
 
@@ -76,27 +75,29 @@
 
 def weights_kernel(*refs):
     sources, refs = refs[:7], refs[7:]
-    w_send, w_recv, w_out, feats, w_send_t, w_recv_t, w_msg_t, w_node_v_t, w_node_a_t, w_out_t = refs[:10]
+    w_send, w_recv, w_out, feats, w_send_t, w_recv_t, w_both_t, w_node_v_t, w_both, w_out_t = refs[:10]
     w_msg, w_node_v, w_node_a, w_out_all, turned, sems = refs[10:]
     mine = lax.axis_index("ch")
     hid = w_send.shape[0]
-    targets = (feats, w_send, w_recv, w_msg, w_node_v, w_node_a, w_out_all)
+    targets = (w_msg, w_node_a, feats, w_send, w_recv, w_node_v, w_out_all)
     copies = []
     for k, (source, target) in enumerate(zip(sources, targets)):
-        if k in (1, 2):
+        if k in (3, 4):
             source = source.at[pl.ds(pl.multiple_of(mine * hid, hid), hid), :]
         copies.append(pltpu.make_async_copy(source, target, sems.at[k]))
     for copy in copies:
         copy.start()
-    for copy in copies:
+    for copy in copies[:2]:
+        copy.wait()
+    w_both[...] = dot(w_node_a[...], w_msg[...]).astype(jnp.bfloat16)
+    turned[...] = w_both[...].T
+    w_both_t[...] = mine_of(turned, mine, hid)
+    for copy in copies[2:]:
         copy.wait()
     w_send_t[...] = w_send[...].T
     w_recv_t[...] = w_recv[...].T
-    turned[...] = w_msg[...].T
-    w_msg_t[...] = mine_of(turned, mine, hid)
     turned[...] = w_node_v[...].T
     w_node_v_t[...] = mine_of(turned, mine, w_node_v_t.shape[0])
-    w_node_a_t[...] = w_node_a[...].T
     w_out_t[...] = w_out_all[...].T
     w_out[...] = mine_of(w_out_all, mine, w_out.shape[0])
 
@@ -293,20 +294,18 @@
 
 def node_kernel(count, start, in_degree, *refs):
     blocks = refs[:count]
-    w_msg, w_node_a, w_node_a_t, w_msg_t, pre, grad_hidden = refs[count : count + 6]
-    hidden, grad_pre, scale, messages = refs[count + 6 :]
+    w_both, w_both_t, pre, grad_hidden = refs[count : count + 4]
+    hidden, grad_pre, scale, messages = refs[count + 4 :]
     assemble(messages, blocks, lax.axis_index("ch"))
     span = slice(start, start + hidden.shape[1])
-    agg = dot(w_msg[...], messages[...])
-    half = 0.5 * (pre[:, span] + dot(w_node_a[...], agg.astype(jnp.bfloat16)))
+    half = 0.5 * (pre[:, span] + dot(w_both[...], messages[...]))
     twice = jnp.tanh(half) + 1.0
     act = half * twice
     hidden[...] = act.astype(jnp.bfloat16)
     slope = 0.5 * (twice + act * (2.0 - twice))
     low_grad = (grad_hidden[:, span] * slope).astype(jnp.bfloat16)
     grad_pre[...] = low_grad
-    grad_agg = dot(w_node_a_t[...], low_grad).astype(jnp.bfloat16)
-    grad_msg = dot(w_msg_t[...], grad_agg).astype(jnp.bfloat16).astype(jnp.float32)
+    grad_msg = dot(w_both_t[...], low_grad).astype(jnp.bfloat16).astype(jnp.float32)
     scale[...] = (grad_msg * (0.5 / in_degree[:, span].astype(jnp.float32))).T
 
 
@@ -355,7 +354,7 @@
 
 def early_kernel(start, low, high, slope, scale, *refs):
     if start:
-        before, beside, cross, west, east, to_cross, to_beside, grads, total = refs
+        before, cross, west, east, to_cross, to_other, grads, total = refs
         total[...] = before[...]
     else:
         grads, total = refs
@@ -370,10 +369,9 @@
     chunks = [chunk_of(place, first, (1, PACK, nodes)) for place in EARLY]
     scatter(low, high, pairs(start, slope, nodes, grad_of), chunks, total)
     if start:
-        to_beside[0] = fold(beside, 0, 0, total)
-        to_cross[...] = fold(cross, 3, 1, total)
-        to_beside[1] = fold(west, 4, 2, total)
-        to_beside[2] = fold(east, 5, 3, total)
+        to_cross[...] = fold(cross, 3, 0, total)
+        to_other[0] = fold(west, 4, 1, total)
+        to_other[1] = fold(east, 5, 2, total)
 
 
 def all_pairs(parts, nodes):
@@ -385,14 +383,15 @@
 
 
 def late_kernel(low, high, *refs):
-    *parts, west, east, to_west, to_east, total = refs
+    *parts, west, east, beside, to_west, to_east, to_beside, total = refs
     nodes = low.shape[2]
     first = nodes // CHUNK
-    chunks = [jnp.bfloat16(first + SLOT_OF[place][0]) for place in LATE]
+    chunks = [chunk_of(place, first, (1, PACK, nodes)) for place in LATE]
     total[...] = jnp.zeros_like(total)
     scatter(low, high, all_pairs(parts, nodes), chunks, total)
     to_west[...] = fold(west, 1, 0, total)
     to_east[...] = fold(east, 2, 1, total)
+    to_beside[...] = fold(beside, 0, 2, total)
 
 
 def own_kernel(low, high, *refs):
@@ -429,8 +428,8 @@
 def add_kernel(left, more, right, across, west, east):
     sub = lax.axis_index("sub")
     other = across[...].astype(jnp.float32)
-    to_west = left[...].astype(jnp.float32) + more[1].astype(jnp.float32)
-    to_east = right[...].astype(jnp.float32) + more[2].astype(jnp.float32)
+    to_west = left[...].astype(jnp.float32) + more[0].astype(jnp.float32)
+    to_east = right[...].astype(jnp.float32) + more[1].astype(jnp.float32)
     west[...] = (to_west + jnp.where(sub == 0, 0.0, other)).astype(jnp.bfloat16)
     east[...] = (to_east + jnp.where(sub == 0, other, 0.0)).astype(jnp.bfloat16)
 
@@ -440,7 +439,7 @@
     sub = lax.axis_index("sub")
     offset = pl.multiple_of(tiles[0] // 2 * TILE, TILE)
     total[...] = own[...]
-    near = beside[0].astype(jnp.float32)
+    near = beside[...].astype(jnp.float32)
     block = upper[...].astype(jnp.float32) + jnp.where(sub == 0, near, 0.0)
     total[pl.ds(offset, block.shape[0]), :] += block
     if start:
@@ -477,16 +476,17 @@
         sent[k - 1] = mine_of(terms, lax.rem(mine + k, count), chans).astype(jnp.bfloat16)
 
 
-def finish_kernel(*refs):
-    *parts, out = refs
-    rows = out.shape[1] // 2
-    count = len(parts) // 2
-    for k in range(2):
-        kept, *others = parts[k * count : (k + 1) * count]
-        total = kept[...]
-        for other in others:
-            total += other[...].astype(jnp.float32)
-        out[:, k * rows : (k + 1) * rows] = total.astype(jnp.bfloat16)
+def finish_kernel(count, *refs):
+    kept, *others = refs[: count]
+    *done, out = refs[count:]
+    total = kept[...]
+    for other in others:
+        total += other[...].astype(jnp.float32)
+    out[:, : kept.shape[1]] = total.astype(jnp.bfloat16)
+    start = kept.shape[1]
+    for part in done:
+        out[:, start : start + part.shape[1]] = part[...]
+        start += part.shape[1]
 
 
 def sum_kernel(w_mine, w_beside, near, sent):
@@ -542,8 +542,6 @@
     sub = lax.axis_index("sub")
 
     feat_blocks = gathered(features, "ch")
-    cot_later, feat_blocks[-1] = lax.optimization_barrier((cotangent, feat_blocks[-1]))
-    cot_blocks = gathered(cot_later, "ch")
 
     whole_w = pltpu.VMEM((chans_all, hidden_all), bf16)
     (
@@ -553,9 +551,9 @@
         features_held,
         w_send_t,
         w_recv_t,
-        w_msg_t,
+        w_both_t,
         w_node_v_t,
-        w_node_a_t,
+        w_both,
         w_out_t,
     ) = call(
         weights_kernel,
@@ -566,33 +564,18 @@
             shape((chans, nodes), bf16),
             shape((chans_all, hid), bf16),
             shape((chans_all, hid), bf16),
-            shape((hid, chans_all), bf16),
+            shape((hid, hidden_all), bf16),
             shape((chans, hidden_all), bf16),
-            shape((chans_all, hidden_all), bf16),
+            shape((hidden_all, hidden_all), bf16),
             shape((hidden_all, chans_all), bf16),
         ),
-        [features, w_send, w_recv, w_msg, w_node_v, w_node_a, w_out],
-        flops=4 * hidden_all * chans_all * nodes,
+        [w_msg, w_node_a, features, w_send, w_recv, w_node_v, w_out],
         away=7,
         scalars=0,
         scratch=[whole_w] * 5 + [pltpu.SemaphoreType.DMA((7,))],
         limit=WEIGHTS_LIMIT,
     )
-    low_cols, high_cols, low_rows, high_rows = call(
-        edges_kernel,
-        (
-            shape((degree, nodes, LANES), bf16),
-            shape((degree, nodes, LANES), bf16),
-            shape((degree, PACK, nodes), bf16),
-            shape((degree, PACK, nodes), bf16),
-        ),
-        [tile_count, senders, degrees],
-        flops=2 * hidden_all * chans_all * nodes,
-        scalars=1,
-    )
-    feat_blocks[0], low_cols, high_cols, low_rows, high_rows = lax.optimization_barrier(
-        (features_held, low_cols, high_cols, low_rows, high_rows)
-    )
+    feat_blocks[0] = features_held
 
     block = shape((slot_rows + PACK, hid), bf16)
     feats, proj, upper, lower, beside, cross = call(
@@ -606,19 +589,30 @@
             block,
         ),
         [tile_count, picks] + feat_blocks + [w_send_my],
-        flops=2 * hid * chans_all * nodes,
-    )
+    )
+    west = shifted(upper, "lon", 1)
+    east = shifted(lower, "lon", -1)
+    cross = lax.ppermute(cross, cycle, far_route)
     base = call(
         receive_kernel,
         shape((nodes, hid), f32),
         [bias_edge[None, :], feats, w_recv_my],
-        flops=2 * hid * chans_all * nodes,
         scalars=0,
     )
-    west = shifted(upper, "lon", 1)
-    east = shifted(lower, "lon", -1)
+    base, senders, cotangent_late = lax.optimization_barrier((base, senders, cotangent))
     beside = shifted(beside, "sub", 1)
-    cross = lax.ppermute(cross, cycle, far_route)
+    cot_blocks = gathered(cotangent_late, "ch")
+    low_cols, high_cols, low_rows, high_rows = call(
+        edges_kernel,
+        (
+            shape((degree, nodes, LANES), bf16),
+            shape((degree, nodes, LANES), bf16),
+            shape((degree, PACK, nodes), bf16),
+            shape((degree, PACK, nodes), bf16),
+        ),
+        [tile_count, senders, degrees],
+        scalars=1,
+    )
     cots, pre, grad_hidden = call(
         functools.partial(prepare_kernel, count),
         (
@@ -627,7 +621,6 @@
             shape((hidden_all, nodes), f32),
         ),
         [tile_count] + cot_blocks + [feats, w_node_v, bias_node[None, :], w_out_t],
-        flops=4 * hidden_all * chans_all * nodes,
         scalars=1,
     )
 
@@ -636,7 +629,6 @@
         near_kernel,
         part_shape,
         [low_cols, high_cols, proj, beside],
-        flops=2 * degree * nodes * (nodes + slot_rows) * hid,
         scratch=[pltpu.VMEM((nodes + slot_rows, hid), bf16)],
         scalars=0,
     )
@@ -648,7 +640,6 @@
         line_kernel,
         part_shape,
         [low_cols, high_cols, part, west, east],
-        flops=2 * degree * nodes * 2 * slot_rows * hid,
         scratch=[pltpu.VMEM((2 * slot_rows, hid), bf16)],
         scalars=0,
     )
@@ -660,7 +651,6 @@
             functools.partial(message_kernel, k * rows),
             (shape((hid, rows), bf16), shape((degree, rows, hid), bf16)),
             [low_cols, high_cols, base, degrees, part, cross, west_too, east_too],
-            flops=2 * degree * rows * 3 * slot_rows * hid,
             scratch=[pltpu.VMEM((3 * slot_rows, hid), bf16), pltpu.VMEM((rows, hid), f32)],
             scalars=0,
         )
@@ -678,36 +668,32 @@
                 shape((hidden_all, rows), bf16),
                 shape((rows, hid), f32),
             ),
-            [degrees] + messages[k] + [w_msg, w_node_a, w_node_a_t, w_msg_t, pre, grad_hidden],
-            flops=6 * hidden_all * chans_all * rows,
+            [degrees] + messages[k] + [w_both, w_both_t, pre, grad_hidden],
             scratch=[pltpu.VMEM((hidden_all, rows), bf16)],
             scalars=0,
         )
         hiddens.append(hidden)
         grad_pres.append(grad_pre)
         operands = [low_rows, high_rows, slopes[k], scale]
-        flops = 2 * degree * rows * len(EARLY) * slot_rows * hid
         kernel = functools.partial(early_kernel, k * rows)
         if k == 0:
-            grad, before = call(kernel, (grad_shape, sums), operands, flops=flops, scalars=0)
+            grad, before = call(kernel, (grad_shape, sums), operands, scalars=0)
         else:
-            to_cross, to_beside, grad = call(
+            to_cross, to_other, grad = call(
                 kernel,
-                (block, shape((3, slot_rows, hid), bf16), grad_shape),
-                operands + [before, beside, cross, west_too, east_too],
-                flops=flops,
+                (block, shape((2, slot_rows, hid), bf16), grad_shape),
+                operands + [before, cross, west_too, east_too],
                 scratch=[pltpu.VMEM(sums.shape, f32)],
                 scalars=0,
             )
         grads.append(grad)
 
-    from_beside = shifted(to_beside, "sub", 1)
+    from_other = shifted(to_other, "sub", 1)
     from_cross = across(to_cross)
-    to_west, to_east = call(
+    to_west, to_east, to_beside = call(
         late_kernel,
-        (block, block),
-        [low_rows, high_rows] + grads + [west, east],
-        flops=2 * degree * nodes * len(LATE) * slot_rows * hid,
+        (block, block, block),
+        [low_rows, high_rows] + grads + [west, east, beside],
         scratch=[pltpu.VMEM((len(LATE) * slot_rows, hid), f32)],
         scalars=0,
     )
@@ -715,25 +701,23 @@
         output_kernel,
         (shape((chans, nodes), bf16), shape((chans, nodes), f32)),
         [tile_count, features_held, cotangent, w_out_my, w_node_v_t] + hiddens + grad_pres,
-        flops=4 * hidden_all * chans * nodes,
         scalars=1,
     )
     to_west, direct = lax.optimization_barrier((to_west, direct))
     to_west, to_east = call(
         add_kernel,
         (block, block),
-        [to_west, from_beside, to_east, from_cross],
-        flops=0,
+        [to_west, from_other, to_east, from_cross],
         scalars=0,
     )
     from_upper = shifted(to_west, "lon", -1)
     from_lower = shifted(to_east, "lon", 1)
+    from_beside = shifted(to_beside, "sub", 1)
 
     own, grad_recv = call(
         own_kernel,
         (shape((nodes, hid), f32), shape((hid, nodes), bf16)),
         [low_rows, high_rows] + grads,
-        flops=2 * degree * nodes * nodes * hid,
         scalars=0,
     )
     columns = chans_all // shard_count
@@ -741,16 +725,14 @@
     inputs = [tile_count, own, from_beside, feats, from_upper]
     weight_shape = shape((chans_all, hid), f32)
     grad_shape = shape((rows, hid), bf16)
-    finals = [None] * halves
+    finals = []
     for k in reversed(range(halves)):
         kernel = functools.partial(back_kernel, k * rows, inv_root)
-        flops = 2 * hid * chans_all * rows
         if k:
             grad_send, weight = call(
                 kernel,
                 (grad_shape, weight_shape),
                 inputs,
-                flops=flops,
                 scratch=[pltpu.VMEM((nodes, hid), f32)],
                 scalars=1,
             )
@@ -763,34 +745,38 @@
                     shape((lons, columns, hid), bf16),
                 ),
                 inputs + [from_lower, weight],
-                flops=flops,
                 scratch=[pltpu.VMEM(weight_shape.shape, f32), pltpu.VMEM((nodes, hid), f32)],
                 scalars=1,
             )
             w_beside = shifted(w_beside, "sub", 1)
+            w_beside, *finals = lax.optimization_barrier((w_beside, *finals))
         kept, sent = call(
             functools.partial(terms_kernel, k * rows),
             (shape((chans, rows), f32), shape((count - 1, chans, rows), bf16)),
             [grad_send, grad_recv, direct, w_send_t, w_recv_t],
-            flops=4 * hid * chans_all * rows,
             scratch=[pltpu.VMEM((chans_all, rows), f32)],
             scalars=0,
         )
-        finals[k] = [kept] + [shifted(sent[i - 1], "ch", i) for i in range(1, count)]
-    grad_features = call(
-        finish_kernel, shape((chans, nodes), bf16), sum(finals, []), flops=0, scalars=0
-    )
+        if k:
+            weight, kept = lax.optimization_barrier((weight, kept))
+        parts = [kept] + [shifted(sent[i - 1], "ch", i) for i in range(1, count)]
+        grad_features = call(
+            functools.partial(finish_kernel, count),
+            shape((chans, nodes - k * rows), bf16),
+            parts + finals,
+            scalars=0,
+        )
+        finals = [grad_features]
 
     near, w_sent = call(
         sum_kernel,
         (shape((columns, hid), f32), shape((lons - 1, columns, hid), bf16)),
         [w_mine, w_beside],
-        flops=0,
         scalars=0,
     )
     w_terms = [shifted(w_sent[k - 1], "lon", k) for k in range(1, lons)]
     grad_w_send = call(
-        weight_kernel, shape((columns, hid), f32), [near] + w_terms, flops=0, scalars=0
+        weight_kernel, shape((columns, hid), f32), [near] + w_terms, scalars=0
     )
     return (updated, grad_features, grad_w_send.T)
 

time: 72.8 us -> 71.4 us (0.981)
  local copies, waits for them, and re-layouts: 1.51 us -> 0.06 us
  starting transfers between devices: 19.9 us -> 21.2 us
  Pallas kernels: 31.8 us -> 30.7 us
    ppermute x18 -> x19, waiting for transfers between devices: 12.6 us -> 15.1 us  [shifted(): return lax.ppermute(block, axis, route)]
    ppermute x1, waiting for transfers between devices: 2.37 us -> 0.63 us  [shards(): cross = lax.ppermute(cross, cycle, far_route)]
    unnamed x26 -> x20, local copies, waits for them, and re-layouts: 1.5 us -> 0.05 us
    ppermute x18 -> x19, starting transfers between devices: 18.3 us -> 19.4 us  [shifted(): return lax.ppermute(block, axis, route)]
    pallas_call x24 -> x25, Pallas kernels: 31.8 us -> 30.7 us  [call(): pl.pallas_call(kernel, out_shape=out_shape, in_specs=[smem] * scalars + [...]
    ppermute x1, waiting for transfers between devices: 2.83 us -> 1.86 us  [shards(): across = lambda block: lax.ppermute(block, cycle, across_route)]
  transfers between devices with their start and end apart: 20 -> 21, of which waited for: 11 -> 13; matrix products, arithmetic and copies ran while one was open for 0% -> 0% of each run, Pallas kernels for 33% -> 34%
where the time goes in v7:
time: 71.4 us; the launch traced here: 71.2 us
  Pallas kernels  30.7 us (43%)
  starting transfers between devices  21.2 us (30%)
  waiting for transfers between devices  17.6 us (25%)
  between operations  1.65 us (2%)
    pallas_call x25, Pallas kernels, call(): pl.pallas_call(kernel, out_shape=out_shape, in_specs=[smem] * scalars + [...  30.7 us
    ppermute x19, starting transfers between devices, shifted(): return lax.ppermute(block, axis, route)  19.4 us
    ppermute x19, waiting for transfers between devices, shifted(): return lax.ppermute(block, axis, route)  15.1 us
    ppermute x1, waiting for transfers between devices, shards(): across = lambda block: lax.ppermute(block, cycle, across_route)  1.86 us
    ppermute x1, starting transfers between devices, shards(): across = lambda block: lax.ppermute(block, cycle, across_route)  1.75 us
  transfers between devices with their start and end apart: 21, of which 13 were waited for; matrix products, arithmetic and copies ran while one was open for 0% of the time, Pallas kernels for 34%

profile of v7, /device:TPU:0, one launch (start us, length us, event | category | flops | bytes accessed | tf_op | source)
XLA Modules:
  0.0 71.2 jit_solution(4281853276758417820)
XLA Ops:
  0.7 3.0 %collective-permute-start = (bf16[256,512]{1,0:T(8,128)(2,1)}, bf16[256,512]{1,0:T(8,128)(2,1)S(1)}, u32[]{:S(2)}, u32[]{:S(2)}) collective-permute-start(bf16[256,512]{1,0:T(8,128)(2,1)} %refs_2_.1), channel_id=1, source_target_pairs={{2,0},{0,2},{3,1},{1,3},{6,4},{4,6},{7,5},{5,7},{10,8},{8,10},{11,... | collective-permute-start | bytes 786440 | tf_op jit(solution)/shard_map/ppermute | solution.py:26
  3.7 3.3 %shard_map.157 = (bf16[256,512]{1,0:T(8,128)(2,1)S(1)}, bf16[256,512]{1,0:T(8,128)(2,1)S(1)}, bf16[256,512]{1,0:T(8,128)(2,1)S(1)}, bf16[256,512]{1,0:T(8,128)(2...) custom-call(bf16[512,512]{1,0:T(8,128)(2,1)} %refs_0_.1, ...), custom_call_target="tpu_custom_call" | custom-call | flops 1024 | bytes 1024 | tf_op jit(solution)/shard_map/pallas_call | solution.py:51
  7.7 2.5 %collective-permute-done.refs_1_ = bf16[256,512]{1,0:T(8,128)(2,1)S(1)} collective-permute-done((bf16[256,512]{1,0:T(8,128)(2,1)}, bf16[256,512]{1,0:T(8,128)(2,1)S(1)}, u32[]{:S(2)}, u32[]{:S(2)}) %collective-permute-start) | collective-permute-done | bytes 262176 | tf_op jit(solution)/shard_map/ppermute | solution.py:26
  10.2 1.1 %shard_map.158 = (bf16[512,512]{1,0:T(8,128)(2,1)S(1)}, bf16[512,256]{1,0:T(8,128)(2,1)S(1)}, bf16[272,256]{1,0:T(8,128)(2,1)S(1)}, bf16[272,256]{1,0:T(8,128)(2...) custom-call(s32[1]{0:T(128)S(6)} %copy.17.tiles, s32[1,2,6]{2,1,0:T(2,128)S(1)} %bitcast.20, ...), custom_call_target="tpu_custom_call" | custom-call | flops 1024 | bytes 1024 | tf_op jit(solution)/shard_map/pallas_call | solution.py:51
  11.3 1.9 %collective-permute-start.1 = (bf16[272,256]{1,0:T(8,128)(2,1)S(1)}, bf16[272,256]{1,0:T(8,128)(2,1)S(1)}, u32[]{:S(2)}, u32[]{:S(2)}) collective-permute-start(bf16[272,256]{1,0:T(8,128)(2,1)S(1)} %get-tuple-element.84), channel_id=1, source_target_pairs={{12,0},{0,4},{4,8},{8,12},{13,1},{1,5},{5,9},{9,13},{14,2},{2,6},{... | collective-permute-start | bytes 417800 | tf_op jit(solution)/shard_map/ppermute | solution.py:26
  13.2 2.1 %collective-permute-start.2 = (bf16[272,256]{1,0:T(8,128)(2,1)S(1)}, bf16[272,256]{1,0:T(8,128)(2,1)S(1)}, u32[]{:S(2)}, u32[]{:S(2)}) collective-permute-start(bf16[272,256]{1,0:T(8,128)(2,1)S(1)} %get-tuple-element.85), channel_id=1, source_target_pairs={{4,0},{8,4},{12,8},{0,12},{5,1},{9,5},{13,9},{1,13},{6,2},{10,6},{... | collective-permute-start | bytes 417800 | tf_op jit(solution)/shard_map/ppermute | solution.py:26
  15.7 1.7 %collective-permute-start.4 = (bf16[256,512]{1,0:T(8,128)(2,1)S(1)}, bf16[256,512]{1,0:T(8,128)(2,1)S(1)}, u32[]{:S(2)}, u32[]{:S(2)}) collective-permute-start(bf16[256,512]{1,0:T(8,128)(2,1)S(1)} %copy-done.2), channel_id=1, source_target_pairs={{2,0},{0,2},{3,1},{1,3},{6,4},{4,6},{7,5},{5,7},{10,8},{8,10},{11,... | collective-permute-start | bytes 786440 | tf_op jit(solution)/shard_map/ppermute | solution.py:26
  17.4 1.0 %shard_map.160 = (bf16[12,512,128]{2,1,0:T(8,128)(2,1)S(1)}, bf16[12,512,128]{2,1,0:T(8,128)(2,1)S(1)}, bf16[12,16,512]{2,1,0:T(8,128)(2,1)S(1)}, bf16[12,16,512]{2,1,0:T(8,128)(2,1)S(1)}) custom-call(s32[1]{0:T(128)S(6)} %copy.17.tiles, s32[12,512]{1,0:T(8,128)S(1)} %copy-done.6, s32[1,512]{1,0:T(1,128)S(1)} %bitcast.13), custom_call_target="tpu_custom_call" | custom-call | flops 1024 | bytes 1024 | tf_op jit(solution)/shard_map/pallas_call | solution.py:51
  18.5 2.9 %shard_map.161.before = bf16[12,512,256]{2,1,0:T(8,128)(2,1)S(1)} custom-call(bf16[12,512,128]{2,1,0:T(8,128)(2,1)S(1)} %get-tuple-element.81.low, bf16[12,512,128]{2,1,0:T(8,128)(2,1)S(1)} %get-tuple-element.82.high, bf16[512,256]{1,0:T(8,128)(2,1)S(1)} %get-tuple-element.86.proj, bf16[272,256]{1,0:T(8,128)(2,1)S(1)} %collective-permute-done.3.beside.refs_4_), custom_call_target="tpu_custom_call" | custom-call | flops 1024 | bytes 1024 | tf_op jit(solution)/shard_map/pallas_call | solution.py:51
  22.4 1.6 %collective-permute-done.4.refs_1_ = bf16[256,512]{1,0:T(8,128)(2,1)S(1)} collective-permute-done((bf16[256,512]{1,0:T(8,128)(2,1)S(1)}, bf16[256,512]{1,0:T(8,128)(2,1)S(1)}, u32[]{:S(2)}, u32[]{:S(2)}) %collective-permute-start.4) | collective-permute-done | bytes 262176 | tf_op jit(solution)/shard_map/ppermute | solution.py:26
  24.1 1.1 %shard_map.162 = (bf16[512,512]{1,0:T(8,128)(2,1)}, f32[512,512]{1,0:T(8,128)S(1)}, f32[512,512]{1,0:T(8,128)S(1)}) custom-call(s32[1]{0:T(128)S(6)} %copy.17.tiles, bf16[256,512]{1,0:T(8,128)(2,1)S(1)} %copy-done.2, bf16[256,512]{1,0:T(8,128)(2,1)S(1)} %collective-permute-done.4.refs_1_, bf16[512,512]{1,0:T(8,128)(2,1)S(1)} %get-tuple-element.78.feats.refs_2_, ...), custom_call_target="tpu_custom_call" | custom-call | flops 1024 | bytes 1024 | tf_op jit(solution)/shard_map/pallas_call | solution.py:51
  25.2 2.6 %shard_map.163.part = bf16[12,512,256]{2,1,0:T(8,128)(2,1)S(1)} custom-call(bf16[12,512,128]{2,1,0:T(8,128)(2,1)S(1)} %get-tuple-element.81.low, bf16[12,512,128]{2,1,0:T(8,128)(2,1)S(1)} %get-tuple-element.82.high, bf16[12,512,256]{2,1,0:T(8,128)(2,1)S(1)} %shard_map.161.before, bf16[272,256]{1,0:T(8,128)(2,1)S(1)} %collective-permute-done.1.west.refs_2_, ...), custom_call_target="tpu_custom_call" | custom-call | flops 1024 | bytes 1024 | tf_op jit(solution)/shard_map/pallas_call | solution.py:51
  28.4 2.5 %shard_map.164 = (bf16[256,256]{1,0:T(8,128)(2,1)S(1)}, bf16[12,256,256]{2,1,0:T(8,128)(2,1)S(1)}) custom-call(bf16[12,512,128]{2,1,0:T(8,128)(2,1)S(1)} %get-tuple-element.81.low, bf16[12,512,128]{2,1,0:T(8,128)(2,1)S(1)} %get-tuple-element.82.high, f32[512,256]{1,0:T(8,128)S(1)} %shard_map.159.base, s32[1,512]{1,0:T(1,128)S(1)} %bitcast.14, ...), custom_call_target="tpu_custom_call" | custom-call | flops 1024 | bytes 1024 | tf_op jit(solution)/shard_map/pallas_call | solution.py:51
  30.9 1.6 %collective-permute-start.8 = (bf16[256,256]{1,0:T(8,128)(2,1)S(1)}, bf16[256,256]{1,0:T(8,128)(2,1)S(1)}, u32[]{:S(2)}, u32[]{:S(2)}) collective-permute-start(bf16[256,256]{1,0:T(8,128)(2,1)S(1)} %get-tuple-element.96.refs_0_), channel_id=1, source_target_pairs={{2,0},{0,2},{3,1},{1,3},{6,4},{4,6},{7,5},{5,7},{10,8},{8,10},{11,... | collective-permute-start | bytes 393224 | tf_op jit(solution)/shard_map/ppermute | solution.py:26
  32.4 2.5 %shard_map.166 = (bf16[256,256]{1,0:T(8,128)(2,1)S(1)}, bf16[12,256,256]{2,1,0:T(8,128)(2,1)S(1)}) custom-call(bf16[12,512,128]{2,1,0:T(8,128)(2,1)S(1)} %get-tuple-element.81.low, bf16[12,512,128]{2,1,0:T(8,128)(2,1)S(1)} %get-tuple-element.82.high, f32[512,256]{1,0:T(8,128)S(1)} %shard_map.159.base, s32[1,512]{1,0:T(1,128)S(1)} %bitcast.15, ...), custom_call_target="tpu_custom_call" | custom-call | flops 1024 | bytes 1024 | tf_op jit(solution)/shard_map/pallas_call | solution.py:51
  35.5 0.9 %collective-permute-done.8.refs_1_ = bf16[256,256]{1,0:T(8,128)(2,1)S(1)} collective-permute-done((bf16[256,256]{1,0:T(8,128)(2,1)S(1)}, bf16[256,256]{1,0:T(8,128)(2,1)S(1)}, u32[]{:S(2)}, u32[]{:S(2)}) %collective-permute-start.8) | collective-permute-done | bytes 131104 | tf_op jit(solution)/shard_map/ppermute | solution.py:26
  36.5 0.9 %shard_map.165 = (bf16[512,256]{1,0:T(8,128)(2,1)S(1)}, bf16[512,256]{1,0:T(8,128)(2,1)S(1)}, f32[256,256]{1,0:T(8,128)S(1)}) custom-call(s32[1,512]{1,0:T(1,128)S(1)} %bitcast.16, bf16[256,256]{1,0:T(8,128)(2,1)S(1)} %get-tuple-element.96.refs_0_, bf16[256,256]{1,0:T(8,128)(2,1)S(1)} %collective-permute-done.8.refs_1_, bf16[512,512]{1,0:T(8,128)(2,1)S(1)} %copy-done.1, ...), custom_call_target="tpu_custom_call" | custom-call | flops 1024 | bytes 1024 | tf_op jit(solution)/shard_map/pallas_call | solution.py:51
  37.4 1.4 %shard_map.169 = (bf16[12,256,256]{2,1,0:T(8,128)(2,1)S(1)}, f32[768,256]{1,0:T(8,128)S(1)}) custom-call(bf16[12,16,512]{2,1,0:T(8,128)(2,1)S(1)} %get-tuple-element.107.low, bf16[12,16,512]{2,1,0:T(8,128)(2,1)S(1)} %get-tuple-element.108.high, bf16[12,256,256]{2,1,0:T(8,128)(2,1)S(1)} %get-tuple-element.109.slope, f32[256,256]{1,0:T(8,128)S(1)} %get-tuple-element.110.scale), custom_call_target="tpu_custom_call" | custom-call | flops 1024 | bytes 1024 | tf_op jit(solution)/shard_map/pallas_call | solution.py:51
  38.8 1.4 %collective-permute-done.9.refs_1_ = bf16[256,256]{1,0:T(8,128)(2,1)S(1)} collective-permute-done((bf16[256,256]{1,0:T(8,128)(2,1)S(1)}, bf16[256,256]{1,0:T(8,128)(2,1)S(1)}, u32[]{:S(2)}, u32[]{:S(2)}) %collective-permute-start.9) | collective-permute-done | bytes 131104 | tf_op jit(solution)/shard_map/ppermute | solution.py:26
  41.0 1.5 %shard_map.170 = (bf16[256,256]{1,0:T(8,128)(2,1)S(1)}, bf16[2,256,256]{2,1,0:T(8,128)(2,1)S(1)}, bf16[12,256,256]{2,1,0:T(8,128)(2,1)S(1)}) custom-call(bf16[12,16,512]{2,1,0:T(8,128)(2,1)S(1)} %get-tuple-element.107.low, bf16[12,16,512]{2,1,0:T(8,128)(2,1)S(1)} %get-tuple-element.108.high, bf16[12,256,256]{2,1,0:T(8,128)(2,1)S(1)} %get-tuple-element.112.slope, ...), custom_call_target="tpu_custom_call" | custom-call | flops 1024 | bytes 1024 | tf_op jit(solution)/shard_map/pallas_call | solution.py:51
  42.5 1.8 %collective-permute-start.12 = (bf16[256,256]{1,0:T(8,128)(2,1)S(1)}, bf16[256,256]{1,0:T(8,128)(2,1)S(1)}, u32[]{:S(2)}, u32[]{:S(2)}) collective-permute-start(bf16[256,256]{1,0:T(8,128)(2,1)S(1)} %get-tuple-element.123), channel_id=1, source_target_pairs={{0,13},{1,4},{4,1},{5,8},{8,5},{9,12},{12,9},{13,0},{2,15},{3,6},{... | collective-permute-start | bytes 393224 | tf_op jit(solution)/shard_map/ppermute | solution.py:539
  44.3 1.2 %shard_map.168 = (bf16[256,512]{1,0:T(8,128)(2,1)}, f32[256,512]{1,0:T(8,128)S(1)}) custom-call(s32[1]{0:T(128)S(6)} %copy.17.tiles, bf16[256,512]{1,0:T(8,128)(2,1)S(1)} %get-tuple-element.74.refs_0_.feats, bf16[256,512]{1,0:T(8,128)(2,1)S(1)} %copy-done.2, bf16[256,512]{1,0:T(8,128)(2,1)S(1)} %get-tuple-element.75.w_out, bf16[256,512]{1,0:T(8,128)(2,1)S(1)} %copy-done.4, ...), custom_call_target="tpu_custom_call" | custom-call | flops 1024 | bytes 1024 | tf_op jit(solution)/shard_map/pallas_call | solution.py:51
  45.4 2.6 %shard_map.172 = (bf16[256,256]{1,0:T(8,128)(2,1)S(1)}, bf16[256,256]{1,0:T(8,128)(2,1)S(1)}, bf16[256,256]{1,0:T(8,128)(2,1)S(1)}) custom-call(bf16[12,16,512]{2,1,0:T(8,128)(2,1)S(1)} %get-tuple-element.107.low, bf16[12,16,512]{2,1,0:T(8,128)(2,1)S(1)} %get-tuple-element.108.high, bf16[12,256,256]{2,1,0:T(8,128)(2,1)S(1)} %get-tuple-element.111.refs_0_, ...), custom_call_target="tpu_custom_call" | custom-call | flops 1024 | bytes 1024 | tf_op jit(solution)/shard_map/pallas_call | solution.py:51
  48.1 1.9 %collective-permute-done.12.across = bf16[256,256]{1,0:T(8,128)(2,1)S(1)} collective-permute-done((bf16[256,256]{1,0:T(8,128)(2,1)S(1)}, bf16[256,256]{1,0:T(8,128)(2,1)S(1)}, u32[]{:S(2)}, u32[]{:S(2)}) %collective-permute-start.12) | collective-permute-done | bytes 131104 | tf_op jit(solution)/shard_map/ppermute | solution.py:539
  50.5 1.6 %collective-permute-start.14 = (bf16[256,256]{1,0:T(8,128)(2,1)S(1)}, bf16[256,256]{1,0:T(8,128)(2,1)S(1)}, u32[]{:S(2)}, u32[]{:S(2)}) collective-permute-start(bf16[256,256]{1,0:T(8,128)(2,1)S(1)} %get-tuple-element.125), channel_id=1, source_target_pairs={{12,0},{0,4},{4,8},{8,12},{13,1},{1,5},{5,9},{9,13},{14,2},{2,6},{... | collective-permute-start | bytes 393224 | tf_op jit(solution)/shard_map/ppermute | solution.py:26
  52.2 2.1 %shard_map.171 = (f32[512,256]{1,0:T(8,128)S(1)}, bf16[256,512]{1,0:T(8,128)(2,1)S(1)}) custom-call(bf16[12,16,512]{2,1,0:T(8,128)(2,1)S(1)} %get-tuple-element.107.low, bf16[12,16,512]{2,1,0:T(8,128)(2,1)S(1)} %get-tuple-element.108.high, bf16[12,256,256]{2,1,0:T(8,128)(2,1)S(1)} %get-tuple-element.111.refs_0_, ...), custom_call_target="tpu_custom_call" | custom-call | flops 1024 | bytes 1024 | tf_op jit(solution)/shard_map/pallas_call | solution.py:51
  54.3 0.9 %collective-permute-done.13.upper = bf16[256,256]{1,0:T(8,128)(2,1)S(1)} collective-permute-done((bf16[256,256]{1,0:T(8,128)(2,1)S(1)}, bf16[256,256]{1,0:T(8,128)(2,1)S(1)}, u32[]{:S(2)}, u32[]{:S(2)}) %collective-permute-start.13) | collective-permute-done | bytes 131104 | tf_op jit(solution)/shard_map/ppermute | solution.py:26
  56.5 1.9 %collective-permute-done.14.refs_0_ = bf16[256,256]{1,0:T(8,128)(2,1)S(1)} collective-permute-done((bf16[256,256]{1,0:T(8,128)(2,1)S(1)}, bf16[256,256]{1,0:T(8,128)(2,1)S(1)}, u32[]{:S(2)}, u32[]{:S(2)}) %collective-permute-start.14) | collective-permute-done | bytes 131104 | tf_op jit(solution)/shard_map/ppermute | solution.py:26
  59.9 1.0 %collective-permute-done.17.refs_1_ = bf16[256,256]{1,0:T(8,128)(2,1)S(1)} collective-permute-done((bf16[256,256]{1,0:T(8,128)(2,1)S(1)}, bf16[256,256]{1,0:T(8,128)(2,1)S(1)}, u32[]{:S(2)}, u32[]{:S(2)}) %collective-permute-start.17) | collective-permute-done | bytes 131104 | tf_op jit(solution)/shard_map/ppermute | solution.py:26
  61.0 3.8 %collective-permute-start.20 = (bf16[64,256]{1,0:T(8,128)(2,1)S(1)}, bf16[64,256]{1,0:T(8,128)(2,1)S(1)}, u32[]{:S(2)}, u32[]{:S(2)}) collective-permute-start(bf16[64,256]{1,0:T(8,128)(2,1)S(1)} %get-tuple-element.145), channel_id=1, source_target_pairs={{4,0},{8,4},{12,8},{0,12},{5,1},{9,5},{13,9},{1,13},{6,2},{10,6},{... | collective-permute-start | bytes 98312 | tf_op jit(solution)/shard_map/ppermute | solution.py:26
  66.5 3.2 %collective-permute-done.19.refs_1_ = bf16[64,256]{1,0:T(8,128)(2,1)S(1)} collective-permute-done((bf16[64,256]{1,0:T(8,128)(2,1)S(1)}, bf16[64,256]{1,0:T(8,128)(2,1)S(1)}, u32[]{:S(2)}, u32[]{:S(2)}) %collective-permute-start.19) | collective-permute-done | bytes 32800 | tf_op jit(solution)/shard_map/ppermute | solution.py:26
  69.7 0.9 %collective-permute-done.18.refs_0_ = bf16[64,256]{1,0:T(8,128)(2,1)S(1)} collective-permute-done((bf16[64,256]{1,0:T(8,128)(2,1)S(1)}, bf16[64,256]{1,0:T(8,128)(2,1)S(1)}, u32[]{:S(2)}, u32[]{:S(2)}) %collective-permute-start.18) | collective-permute-done | bytes 32800 | tf_op jit(solution)/shard_map/ppermute | solution.py:26
  (56 shorter events, 9.5 us)
Async XLA Ops:
  0.6 9.5 %copy-start.9 = (s32[1,6,2]{1,2,0:T(2,128)S(1)}, s32[1,6,2]{1,2,0:T(2,128)}, u32[]{:S(2)}) copy-start(s32[1,6,2]{1,2,0:T(2,128)} %param.19) | copy-start | bytes 148
  0.6 14.7 %copy-start.7 = (f32[512]{0:T(512)S(1)}, f32[512]{0:T(512)}, u32[]{:S(2)}) copy-start(f32[512]{0:T(512)} %param.22) | copy-start | bytes 6148
  0.7 9.5 %collective-permute-start = (bf16[256,512]{1,0:T(8,128)(2,1)}, bf16[256,512]{1,0:T(8,128)(2,1)S(1)}, u32[]{:S(2)}, u32[]{:S(2)}) collective-permute-start(bf16[256,512]{1,0:T(8,128)(2,1)} %refs_2_.1), channel_id=1, source_target_pairs={{2,0},{0,2},{3,1},{1,3},{6,4},{4,6},{7,5},{5,7},{10,8},{8,10},{11,... | collective-permute-start | bytes 786440 | tf_op jit(solution)/shard_map/ppermute | solution.py:26
  6.9 8.8 %copy-start.2 = (bf16[256,512]{1,0:T(8,128)(2,1)S(1)}, bf16[256,512]{1,0:T(8,128)(2,1)}, u32[]{:S(2)}) copy-start(bf16[256,512]{1,0:T(8,128)(2,1)} %cots.1) | copy-start | bytes 786436
  6.9 10.5 %copy-start.5 = (s32[512]{0:T(512)S(1)}, s32[512]{0:T(512)}, u32[]{:S(2)}) copy-start(s32[512]{0:T(512)} %param.17) | copy-start | bytes 6148
  7.0 10.5 %copy-start.6 = (s32[12,512]{1,0:T(8,128)S(1)}, s32[12,512]{1,0:T(8,128)}, u32[]{:S(2)}) copy-start(s32[12,512]{1,0:T(8,128)} %senders) | copy-start | bytes 73732
  11.3 7.2 %collective-permute-start.3 = (bf16[272,256]{1,0:T(8,128)(2,1)S(1)}, bf16[272,256]{1,0:T(8,128)(2,1)S(1)}, u32[]{:S(2)}, u32[]{:S(2)}) collective-permute-start(bf16[272,256]{1,0:T(8,128)(2,1)S(1)} %get-tuple-element.87), channel_id=1, source_target_pairs={{1,0},{0,1},{3,2},{2,3},{5,4},{4,5},{7,6},{6,7},{9,8},{8,9},{11,10... | collective-permute-start | bytes 417800 | tf_op jit(solution)/shard_map/ppermute | solution.py:26
  11.3 10.1 %collective-permute-start.1 = (bf16[272,256]{1,0:T(8,128)(2,1)S(1)}, bf16[272,256]{1,0:T(8,128)(2,1)S(1)}, u32[]{:S(2)}, u32[]{:S(2)}) collective-permute-start(bf16[272,256]{1,0:T(8,128)(2,1)S(1)} %get-tuple-element.84), channel_id=1, source_target_pairs={{12,0},{0,4},{4,8},{8,12},{13,1},{1,5},{5,9},{9,13},{14,2},{2,6},{... | collective-permute-start | bytes 417800 | tf_op jit(solution)/shard_map/ppermute | solution.py:26
  13.2 8.7 %collective-permute-start.2 = (bf16[272,256]{1,0:T(8,128)(2,1)S(1)}, bf16[272,256]{1,0:T(8,128)(2,1)S(1)}, u32[]{:S(2)}, u32[]{:S(2)}) collective-permute-start(bf16[272,256]{1,0:T(8,128)(2,1)S(1)} %get-tuple-element.85), channel_id=1, source_target_pairs={{4,0},{8,4},{12,8},{0,12},{5,1},{9,5},{13,9},{1,13},{6,2},{10,6},{... | collective-permute-start | bytes 417800 | tf_op jit(solution)/shard_map/ppermute | solution.py:26
  15.7 8.4 %collective-permute-start.4 = (bf16[256,512]{1,0:T(8,128)(2,1)S(1)}, bf16[256,512]{1,0:T(8,128)(2,1)S(1)}, u32[]{:S(2)}, u32[]{:S(2)}) collective-permute-start(bf16[256,512]{1,0:T(8,128)(2,1)S(1)} %copy-done.2), channel_id=1, source_target_pairs={{2,0},{0,2},{3,1},{1,3},{6,4},{4,6},{7,5},{5,7},{10,8},{8,10},{11,... | collective-permute-start | bytes 786440 | tf_op jit(solution)/shard_map/ppermute | solution.py:26
  17.4 11.0 %collective-permute-start.5 = (bf16[272,256]{1,0:T(8,128)(2,1)S(1)}, bf16[272,256]{1,0:T(8,128)(2,1)S(1)}, u32[]{:S(2)}, u32[]{:S(2)}) collective-permute-start(bf16[272,256]{1,0:T(8,128)(2,1)S(1)} %get-tuple-element.95), channel_id=1, source_target_pairs={{0,9},{1,8},{4,13},{5,12},{8,1},{9,0},{12,5},{13,4},{2,11},{3,10},... | collective-permute-start | bytes 417800 | tf_op jit(solution)/shard_map/ppermute | solution.py:595
  18.5 5.6 %copy-start = (bf16[512,512]{1,0:T(8,128)(2,1)S(1)}, bf16[512,512]{1,0:T(8,128)(2,1)}, u32[]{:S(2)}) copy-start(bf16[512,512]{1,0:T(8,128)(2,1)} %refs_3_.3) | copy-start | bytes 1572868
  18.5 5.6 %copy-start.3 = (bf16[512,512]{1,0:T(8,128)(2,1)S(1)}, bf16[512,512]{1,0:T(8,128)(2,1)}, u32[]{:S(2)}) copy-start(bf16[512,512]{1,0:T(8,128)(2,1)} %get-tuple-element.90.refs_5_) | copy-start | bytes 1572868
  18.5 5.6 %copy-start.8 = (f32[512]{0:T(512)S(1)}, f32[512]{0:T(512)}, u32[]{:S(2)}) copy-start(f32[512]{0:T(512)} %param.26) | copy-start | bytes 6148
  21.9 6.5 %collective-permute-start.6 = (bf16[272,256]{1,0:T(8,128)(2,1)S(1)}, bf16[272,256]{1,0:T(8,128)(2,1)S(1)}, u32[]{:S(2)}, u32[]{:S(2)}) collective-permute-start(bf16[272,256]{1,0:T(8,128)(2,1)S(1)} %collective-permute-done.1.west.refs_2_), channel_id=1, source_target_pairs={{1,0},{0,1},{3,2},{2,3},{5,4},{4,5},{7,6},{6,7},{9,8},{8,9},{11,10... | collective-permute-start | bytes 417800 | tf_op jit(solution)/shard_map/ppermute | solution.py:26
  22.4 6.0 %collective-permute-start.7 = (bf16[272,256]{1,0:T(8,128)(2,1)S(1)}, bf16[272,256]{1,0:T(8,128)(2,1)S(1)}, u32[]{:S(2)}, u32[]{:S(2)}) collective-permute-start(bf16[272,256]{1,0:T(8,128)(2,1)S(1)} %collective-permute-done.2.east.refs_3_), channel_id=1, source_target_pairs={{1,0},{0,1},{3,2},{2,3},{5,4},{4,5},{7,6},{6,7},{9,8},{8,9},{11,10... | collective-permute-start | bytes 417800 | tf_op jit(solution)/shard_map/ppermute | solution.py:26
  30.9 5.6 %copy-start.1 = (bf16[512,512]{1,0:T(8,128)(2,1)S(1)}, bf16[512,512]{1,0:T(8,128)(2,1)}, u32[]{:S(2)}) copy-start(bf16[512,512]{1,0:T(8,128)(2,1)} %get-tuple-element.97.refs_2_) | copy-start | bytes 1572868
  30.9 5.6 %collective-permute-start.8 = (bf16[256,256]{1,0:T(8,128)(2,1)S(1)}, bf16[256,256]{1,0:T(8,128)(2,1)S(1)}, u32[]{:S(2)}, u32[]{:S(2)}) collective-permute-start(bf16[256,256]{1,0:T(8,128)(2,1)S(1)} %get-tuple-element.96.refs_0_), channel_id=1, source_target_pairs={{2,0},{0,2},{3,1},{1,3},{6,4},{4,6},{7,5},{5,7},{10,8},{8,10},{11,... | collective-permute-start | bytes 393224 | tf_op jit(solution)/shard_map/ppermute | solution.py:26
  34.9 5.3 %collective-permute-start.9 = (bf16[256,256]{1,0:T(8,128)(2,1)S(1)}, bf16[256,256]{1,0:T(8,128)(2,1)S(1)}, u32[]{:S(2)}, u32[]{:S(2)}) collective-permute-start(bf16[256,256]{1,0:T(8,128)(2,1)S(1)} %get-tuple-element.102.refs_0_), channel_id=1, source_target_pairs={{2,0},{0,2},{3,1},{1,3},{6,4},{4,6},{7,5},{5,7},{10,8},{8,10},{11,... | collective-permute-start | bytes 393224 | tf_op jit(solution)/shard_map/ppermute | solution.py:26
  41.0 3.3 %copy-start.4 = (bf16[256,512]{1,0:T(8,128)(2,1)S(1)}, bf16[256,512]{1,0:T(8,128)(2,1)}, u32[]{:S(2)}) copy-start(bf16[256,512]{1,0:T(8,128)(2,1)} %get-tuple-element.76.w_node_v_t) | copy-start | bytes 786436
  42.4 7.5 %collective-permute-start.11 = (bf16[2,256,256]{2,1,0:T(8,128)(2,1)S(1)}, bf16[2,256,256]{2,1,0:T(8,128)(2,1)S(1)}, u32[]{:S(2)}, u32[]{:S(2)}) collective-permute-start(bf16[2,256,256]{2,1,0:T(8,128)(2,1)S(1)} %get-tuple-element.121), channel_id=1, source_target_pairs={{1,0},{0,1},{3,2},{2,3},{5,4},{4,5},{7,6},{6,7},{9,8},{8,9},{11,10... | collective-permute-start | bytes 786440 | tf_op jit(solution)/shard_map/ppermute | solution.py:26
  42.5 7.5 %collective-permute-start.12 = (bf16[256,256]{1,0:T(8,128)(2,1)S(1)}, bf16[256,256]{1,0:T(8,128)(2,1)S(1)}, u32[]{:S(2)}, u32[]{:S(2)}) collective-permute-start(bf16[256,256]{1,0:T(8,128)(2,1)S(1)} %get-tuple-element.123), channel_id=1, source_target_pairs={{0,13},{1,4},{4,1},{5,8},{8,5},{9,12},{12,9},{13,0},{2,15},{3,6},{... | collective-permute-start | bytes 393224 | tf_op jit(solution)/shard_map/ppermute | solution.py:539
  48.0 6.2 %collective-permute-start.10 = (bf16[256,256]{1,0:T(8,128)(2,1)S(1)}, bf16[256,256]{1,0:T(8,128)(2,1)S(1)}, u32[]{:S(2)}, u32[]{:S(2)}) collective-permute-start(bf16[256,256]{1,0:T(8,128)(2,1)S(1)} %get-tuple-element.117), channel_id=1, source_target_pairs={{1,0},{0,1},{3,2},{2,3},{5,4},{4,5},{7,6},{6,7},{9,8},{8,9},{11,10... | collective-permute-start | bytes 393224 | tf_op jit(solution)/shard_map/ppermute | solution.py:26
  50.1 5.0 %collective-permute-start.13 = (bf16[256,256]{1,0:T(8,128)(2,1)S(1)}, bf16[256,256]{1,0:T(8,128)(2,1)S(1)}, u32[]{:S(2)}, u32[]{:S(2)}) collective-permute-start(bf16[256,256]{1,0:T(8,128)(2,1)S(1)} %get-tuple-element.124), channel_id=1, source_target_pairs={{4,0},{8,4},{12,8},{0,12},{5,1},{9,5},{13,9},{1,13},{6,2},{10,6},{... | collective-permute-start | bytes 393224 | tf_op jit(solution)/shard_map/ppermute | solution.py:26
  50.5 7.9 %collective-permute-start.14 = (bf16[256,256]{1,0:T(8,128)(2,1)S(1)}, bf16[256,256]{1,0:T(8,128)(2,1)S(1)}, u32[]{:S(2)}, u32[]{:S(2)}) collective-permute-start(bf16[256,256]{1,0:T(8,128)(2,1)S(1)} %get-tuple-element.125), channel_id=1, source_target_pairs={{12,0},{0,4},{4,8},{8,12},{13,1},{1,5},{5,9},{9,13},{14,2},{2,6},{... | collective-permute-start | bytes 393224 | tf_op jit(solution)/shard_map/ppermute | solution.py:26
  55.9 5.0 %collective-permute-start.17 = (bf16[256,256]{1,0:T(8,128)(2,1)S(1)}, bf16[256,256]{1,0:T(8,128)(2,1)S(1)}, u32[]{:S(2)}, u32[]{:S(2)}) collective-permute-start(bf16[256,256]{1,0:T(8,128)(2,1)S(1)} %bitcast.22), channel_id=1, source_target_pairs={{2,0},{0,2},{3,1},{1,3},{6,4},{4,6},{7,5},{5,7},{10,8},{8,10},{11,... | collective-permute-start | bytes 393224 | tf_op jit(solution)/shard_map/ppermute | solution.py:26
  58.8 2.2 %collective-permute-start.16 = (bf16[4,64,256]{2,1,0:T(8,128)(2,1)S(1)}, bf16[4,64,256]{2,1,0:T(8,128)(2,1)S(1)}, u32[]{:S(2)}, u32[]{:S(2)}) collective-permute-start(bf16[4,64,256]{2,1,0:T(8,128)(2,1)S(1)} %get-tuple-element.137), channel_id=1, source_target_pairs={{1,0},{0,1},{3,2},{2,3},{5,4},{4,5},{7,6},{6,7},{9,8},{8,9},{11,10... | collective-permute-start | bytes 393224 | tf_op jit(solution)/shard_map/ppermute | solution.py:26
  59.3 6.2 %collective-permute-start.15 = (bf16[256,256]{1,0:T(8,128)(2,1)S(1)}, bf16[256,256]{1,0:T(8,128)(2,1)S(1)}, u32[]{:S(2)}, u32[]{:S(2)}) collective-permute-start(bf16[256,256]{1,0:T(8,128)(2,1)S(1)} %bitcast.21), channel_id=1, source_target_pairs={{2,0},{0,2},{3,1},{1,3},{6,4},{4,6},{7,5},{5,7},{10,8},{8,10},{11,... | collective-permute-start | bytes 393224 | tf_op jit(solution)/shard_map/ppermute | solution.py:26
  61.0 5.4 %collective-permute-start.20 = (bf16[64,256]{1,0:T(8,128)(2,1)S(1)}, bf16[64,256]{1,0:T(8,128)(2,1)S(1)}, u32[]{:S(2)}, u32[]{:S(2)}) collective-permute-start(bf16[64,256]{1,0:T(8,128)(2,1)S(1)} %get-tuple-element.145), channel_id=1, source_target_pairs={{4,0},{8,4},{12,8},{0,12},{5,1},{9,5},{13,9},{1,13},{6,2},{10,6},{... | collective-permute-start | bytes 98312 | tf_op jit(solution)/shard_map/ppermute | solution.py:26
  64.9 4.8 %collective-permute-start.19 = (bf16[64,256]{1,0:T(8,128)(2,1)S(1)}, bf16[64,256]{1,0:T(8,128)(2,1)S(1)}, u32[]{:S(2)}, u32[]{:S(2)}) collective-permute-start(bf16[64,256]{1,0:T(8,128)(2,1)S(1)} %get-tuple-element.146), channel_id=1, source_target_pairs={{8,0},{12,4},{0,8},{4,12},{9,1},{13,5},{1,9},{5,13},{10,2},{14,6},... | collective-permute-start | bytes 98312 | tf_op jit(solution)/shard_map/ppermute | solution.py:26
  64.9 5.7 %collective-permute-start.18 = (bf16[64,256]{1,0:T(8,128)(2,1)S(1)}, bf16[64,256]{1,0:T(8,128)(2,1)S(1)}, u32[]{:S(2)}, u32[]{:S(2)}) collective-permute-start(bf16[64,256]{1,0:T(8,128)(2,1)S(1)} %get-tuple-element.147), channel_id=1, source_target_pairs={{12,0},{0,4},{4,8},{8,12},{13,1},{1,5},{5,9},{9,13},{14,2},{2,6},{... | collective-permute-start | bytes 98312 | tf_op jit(solution)/shard_map/ppermute | solution.py:26

commit v8 on v7

--- a/solution.py
+++ b/solution.py
@@ -44,7 +44,7 @@
     return 0.5 * jnp.tanh(0.5 * value) + 0.5
 
 
-def call(kernel, out_shape, operands, scratch=(), scalars=2, away=0, limit=24):
+def call(kernel, out_shape, operands, scratch=(), scalars=2, away=0, limit=24, flops=1024):
     vmem = pl.BlockSpec(memory_space=pltpu.VMEM)
     smem = pl.BlockSpec(memory_space=pltpu.SMEM)
     anywhere = pl.BlockSpec(memory_space=pltpu.HBM)
@@ -57,7 +57,7 @@
         out_specs=jax.tree.map(lambda _: vmem, out_shape),
         scratch_shapes=scratch,
         compiler_params=pltpu.CompilerParams(vmem_limit_bytes=limit * MIB),
-        cost_estimate=pl.CostEstimate(flops=1024, bytes_accessed=1024, transcendentals=0),
+        cost_estimate=pl.CostEstimate(flops=flops, bytes_accessed=1024, transcendentals=0),
     )(*operands)
 
 
@@ -254,6 +254,10 @@
     lax.fori_loop(0, low.shape[0], step, 0, unroll=True)
 
 
+def cross_rows_kernel(block, rows):
+    fill(rows, 0, block, 3)
+
+
 def message_kernel(
     start, low, high, base, in_degree, part, cross, west, east, message, slope, ext, total
 ):
@@ -263,8 +267,10 @@
     together = nodes // rows
     span = slice(start, start + rows)
     chunks = []
-    for index, (place, block) in enumerate(((3, cross), (4, west), (5, east))):
-        fill(ext, index * CHUNK, block, place)
+    ext[:CHUNK, :] = cross[...]
+    for index, (place, block) in enumerate(((4, west), (5, east))):
+        fill(ext, (index + 1) * CHUNK, block, place)
+    for place in (3, 4, 5):
         chunks.append(chunk_of(place, first, (nodes, LANES)))
     total[...] = jnp.zeros_like(total)
 
@@ -352,26 +358,38 @@
     return jnp.concatenate(halves, axis=0).astype(jnp.bfloat16)
 
 
-def early_kernel(start, low, high, slope, scale, *refs):
-    if start:
-        before, cross, west, east, to_cross, to_other, grads, total = refs
-        total[...] = before[...]
-    else:
-        grads, total = refs
-        total[...] = jnp.zeros_like(total)
+def early_kernel(low, high, slope, scale, grads, total):
     nodes = low.shape[2]
-    first = nodes // CHUNK
 
     def grad_of(ref, m):
         grads[m] = (ref[m].astype(jnp.float32) * scale[...]).astype(jnp.bfloat16)
         return grads[m]
 
-    chunks = [chunk_of(place, first, (1, PACK, nodes)) for place in EARLY]
+    chunks = [chunk_of(place, nodes // CHUNK, (1, PACK, nodes)) for place in EARLY]
+    total[...] = jnp.zeros_like(total)
+    scatter(low, high, pairs(0, slope, nodes, grad_of), chunks, total)
+
+
+def cross_kernel(start, low, high, slope, scale, before, cross, to_cross, grads, total):
+    nodes = low.shape[2]
+
+    def grad_of(ref, m):
+        grads[m] = (ref[m].astype(jnp.float32) * scale[...]).astype(jnp.bfloat16)
+        return grads[m]
+
+    chunks = [chunk_of(EARLY[0], nodes // CHUNK, (1, PACK, nodes))]
+    total[...] = before[:CHUNK, :]
     scatter(low, high, pairs(start, slope, nodes, grad_of), chunks, total)
-    if start:
-        to_cross[...] = fold(cross, 3, 0, total)
-        to_other[0] = fold(west, 4, 1, total)
-        to_other[1] = fold(east, 5, 2, total)
+    to_cross[...] = fold(cross, EARLY[0], 0, total)
+
+
+def other_kernel(start, low, high, grads, before, west, east, to_other, total):
+    nodes = low.shape[2]
+    chunks = [chunk_of(place, nodes // CHUNK, (1, PACK, nodes)) for place in EARLY[1:]]
+    total[...] = before[CHUNK:, :]
+    scatter(low, high, pairs(start, grads, nodes, lambda ref, m: ref[m]), chunks, total)
+    to_other[0] = fold(west, EARLY[1], 0, total)
+    to_other[1] = fold(east, EARLY[2], 1, total)
 
 
 def all_pairs(parts, nodes):
@@ -425,13 +443,18 @@
         direct[:, span] = cots[:, span].astype(jnp.float32) + dot(w_node_v_t[...], grad_pre[...])
 
 
-def add_kernel(left, more, right, across, west, east):
+def across_kernel(left, right, across, west, east):
     sub = lax.axis_index("sub")
     other = across[...].astype(jnp.float32)
-    to_west = left[...].astype(jnp.float32) + more[0].astype(jnp.float32)
-    to_east = right[...].astype(jnp.float32) + more[1].astype(jnp.float32)
-    west[...] = (to_west + jnp.where(sub == 0, 0.0, other)).astype(jnp.bfloat16)
-    east[...] = (to_east + jnp.where(sub == 0, other, 0.0)).astype(jnp.bfloat16)
+    to_west = left[...].astype(jnp.float32) + jnp.where(sub == 0, 0.0, other)
+    to_east = right[...].astype(jnp.float32) + jnp.where(sub == 0, other, 0.0)
+    west[...] = to_west.astype(west.dtype)
+    east[...] = to_east.astype(east.dtype)
+
+
+def add_kernel(left, right, more, west, east):
+    west[...] = (left[...] + more[0].astype(jnp.float32)).astype(jnp.bfloat16)
+    east[...] = (right[...] + more[1].astype(jnp.float32)).astype(jnp.bfloat16)
 
 
 def back_kernel(start, inv_root, tiles, own, beside, feats, upper, *refs):
@@ -643,6 +666,10 @@
         scratch=[pltpu.VMEM((2 * slot_rows, hid), bf16)],
         scalars=0,
     )
+    part, cross = lax.optimization_barrier((part, cross))
+    cross_rows = call(
+        cross_rows_kernel, shape((slot_rows, hid), bf16), [cross], scalars=0
+    )
     halves = 2
     rows = nodes // halves
     slopes, messages, hiddens, grad_pres, grads = [], [], [], [], []
@@ -650,7 +677,7 @@
         message, slope = call(
             functools.partial(message_kernel, k * rows),
             (shape((hid, rows), bf16), shape((degree, rows, hid), bf16)),
-            [low_cols, high_cols, base, degrees, part, cross, west_too, east_too],
+            [low_cols, high_cols, base, degrees, part, cross_rows, west_too, east_too],
             scratch=[pltpu.VMEM((3 * slot_rows, hid), bf16), pltpu.VMEM((rows, hid), f32)],
             scalars=0,
         )
@@ -675,19 +702,26 @@
         hiddens.append(hidden)
         grad_pres.append(grad_pre)
         operands = [low_rows, high_rows, slopes[k], scale]
-        kernel = functools.partial(early_kernel, k * rows)
         if k == 0:
-            grad, before = call(kernel, (grad_shape, sums), operands, scalars=0)
+            grad, before = call(early_kernel, (grad_shape, sums), operands, scalars=0)
         else:
-            to_cross, to_other, grad = call(
-                kernel,
-                (block, shape((2, slot_rows, hid), bf16), grad_shape),
-                operands + [before, cross, west_too, east_too],
-                scratch=[pltpu.VMEM(sums.shape, f32)],
+            to_cross, grad = call(
+                functools.partial(cross_kernel, k * rows),
+                (block, grad_shape),
+                operands + [before, cross],
+                scratch=[pltpu.VMEM((slot_rows, hid), f32)],
+                scalars=0,
+            )
+            to_other = call(
+                functools.partial(other_kernel, k * rows),
+                shape((2, slot_rows, hid), bf16),
+                [low_rows, high_rows, grad, before, west_too, east_too],
+                scratch=[pltpu.VMEM((2 * slot_rows, hid), f32)],
                 scalars=0,
             )
         grads.append(grad)
 
+    grads[0], to_other = lax.optimization_barrier((grads[0], to_other))
     from_other = shifted(to_other, "sub", 1)
     from_cross = across(to_cross)
     to_west, to_east, to_beside = call(
@@ -697,28 +731,28 @@
         scratch=[pltpu.VMEM((len(LATE) * slot_rows, hid), f32)],
         scalars=0,
     )
+    wide = shape((slot_rows, hid), f32)
+    to_west, to_east = call(
+        across_kernel, (wide, wide), [to_west, to_east, from_cross], scalars=0, flops=15 * 10**8
+    )
+    to_west, to_east = call(add_kernel, (block, block), [to_west, to_east, from_other], scalars=0)
+    from_upper = shifted(to_west, "lon", -1)
+    from_lower = shifted(to_east, "lon", 1)
+    from_beside = shifted(to_beside, "sub", 1)
+    to_west, grads[0] = lax.optimization_barrier((to_west, grads[0]))
+
+    own, grad_recv = call(
+        own_kernel,
+        (shape((nodes, hid), f32), shape((hid, nodes), bf16)),
+        [low_rows, high_rows] + grads,
+        scalars=0,
+    )
+    own, hiddens[0] = lax.optimization_barrier((own, hiddens[0]))
     updated, direct = call(
         output_kernel,
         (shape((chans, nodes), bf16), shape((chans, nodes), f32)),
         [tile_count, features_held, cotangent, w_out_my, w_node_v_t] + hiddens + grad_pres,
         scalars=1,
-    )
-    to_west, direct = lax.optimization_barrier((to_west, direct))
-    to_west, to_east = call(
-        add_kernel,
-        (block, block),
-        [to_west, from_other, to_east, from_cross],
-        scalars=0,
-    )
-    from_upper = shifted(to_west, "lon", -1)
-    from_lower = shifted(to_east, "lon", 1)
-    from_beside = shifted(to_beside, "sub", 1)
-
-    own, grad_recv = call(
-        own_kernel,
-        (shape((nodes, hid), f32), shape((hid, nodes), bf16)),
-        [low_rows, high_rows] + grads,
-        scalars=0,
     )
     columns = chans_all // shard_count
     inv_root = 1.0 / math.sqrt(total_nodes)

time: 71.4 us -> 70.6 us (0.989)
  waiting for transfers between devices: 17.6 us -> 16.8 us
    ppermute x1, starting transfers between devices: 1.75 us -> 0.22 us  [shards(): across = lambda block: lax.ppermute(block, cycle, across_route)]
    ppermute x19, starting transfers between devices: 19.4 us -> 20.7 us  [shifted(): return lax.ppermute(block, axis, route)]
    ppermute x19, waiting for transfers between devices: 15.1 us -> 14.3 us  [shifted(): return lax.ppermute(block, axis, route)]
    pallas_call x25 -> x28, Pallas kernels: 30.7 us -> 31 us  [call(): pl.pallas_call(kernel, out_shape=out_shape, in_specs=[smem] * scalars + [...]
  transfers between devices with their start and end apart: 21 -> 21, of which waited for: 13 -> 12; matrix products, arithmetic and copies ran while one was open for 0% -> 0% of each run, Pallas kernels for 34% -> 36%
where the time goes in v8:
time: 70.6 us; the launch traced here: 70.4 us
  Pallas kernels  31 us (44%)
  starting transfers between devices  20.9 us (30%)
  waiting for transfers between devices  16.8 us (24%)
  between operations  1.67 us (2%)
    pallas_call x28, Pallas kernels, call(): pl.pallas_call(kernel, out_shape=out_shape, in_specs=[smem] * scalars + [...  31 us
    ppermute x19, starting transfers between devices, shifted(): return lax.ppermute(block, axis, route)  20.7 us
    ppermute x19, waiting for transfers between devices, shifted(): return lax.ppermute(block, axis, route)  14.3 us
    ppermute x1, waiting for transfers between devices, shards(): across = lambda block: lax.ppermute(block, cycle, across_route)  1.85 us
  transfers between devices with their start and end apart: 21, of which 12 were waited for; matrix products, arithmetic and copies ran while one was open for 0% of the time, Pallas kernels for 36%

profile of v8, /device:TPU:0, one launch (start us, length us, event | category | flops | bytes accessed | tf_op | source)
XLA Modules:
  0.0 70.4 jit_solution(1408126064421210299)
XLA Ops:
  0.7 3.0 %collective-permute-start = (bf16[256,512]{1,0:T(8,128)(2,1)}, bf16[256,512]{1,0:T(8,128)(2,1)S(1)}, u32[]{:S(2)}, u32[]{:S(2)}) collective-permute-start(bf16[256,512]{1,0:T(8,128)(2,1)} %refs_2_.1), channel_id=1, source_target_pairs={{2,0},{0,2},{3,1},{1,3},{6,4},{4,6},{7,5},{5,7},{10,8},{8,10},{11,... | collective-permute-start | bytes 786440 | tf_op jit(solution)/shard_map/ppermute | solution.py:26
  3.7 3.3 %shard_map.157 = (bf16[256,512]{1,0:T(8,128)(2,1)S(1)}, bf16[256,512]{1,0:T(8,128)(2,1)S(1)}, bf16[256,512]{1,0:T(8,128)(2,1)S(1)}, bf16[256,512]{1,0:T(8,128)(2...) custom-call(bf16[512,512]{1,0:T(8,128)(2,1)} %refs_0_.1, ...), custom_call_target="tpu_custom_call" | custom-call | flops 1024 | bytes 1024 | tf_op jit(solution)/shard_map/pallas_call | solution.py:51
  7.6 2.5 %collective-permute-done.refs_1_ = bf16[256,512]{1,0:T(8,128)(2,1)S(1)} collective-permute-done((bf16[256,512]{1,0:T(8,128)(2,1)}, bf16[256,512]{1,0:T(8,128)(2,1)S(1)}, u32[]{:S(2)}, u32[]{:S(2)}) %collective-permute-start) | collective-permute-done | bytes 262176 | tf_op jit(solution)/shard_map/ppermute | solution.py:26
  10.2 1.1 %shard_map.158 = (bf16[512,512]{1,0:T(8,128)(2,1)S(1)}, bf16[512,256]{1,0:T(8,128)(2,1)S(1)}, bf16[272,256]{1,0:T(8,128)(2,1)S(1)}, bf16[272,256]{1,0:T(8,128)(2...) custom-call(s32[1]{0:T(128)S(6)} %copy.17.tiles, s32[1,2,6]{2,1,0:T(2,128)S(1)} %bitcast.20, ...), custom_call_target="tpu_custom_call" | custom-call | flops 1024 | bytes 1024 | tf_op jit(solution)/shard_map/pallas_call | solution.py:51
  11.3 1.9 %collective-permute-start.1 = (bf16[272,256]{1,0:T(8,128)(2,1)S(1)}, bf16[272,256]{1,0:T(8,128)(2,1)S(1)}, u32[]{:S(2)}, u32[]{:S(2)}) collective-permute-start(bf16[272,256]{1,0:T(8,128)(2,1)S(1)} %get-tuple-element.92), channel_id=1, source_target_pairs={{12,0},{0,4},{4,8},{8,12},{13,1},{1,5},{5,9},{9,13},{14,2},{2,6},{... | collective-permute-start | bytes 417800 | tf_op jit(solution)/shard_map/ppermute | solution.py:26
  13.2 2.1 %collective-permute-start.2 = (bf16[272,256]{1,0:T(8,128)(2,1)S(1)}, bf16[272,256]{1,0:T(8,128)(2,1)S(1)}, u32[]{:S(2)}, u32[]{:S(2)}) collective-permute-start(bf16[272,256]{1,0:T(8,128)(2,1)S(1)} %get-tuple-element.93), channel_id=1, source_target_pairs={{4,0},{8,4},{12,8},{0,12},{5,1},{9,5},{13,9},{1,13},{6,2},{10,6},{... | collective-permute-start | bytes 417800 | tf_op jit(solution)/shard_map/ppermute | solution.py:26
  15.7 1.7 %collective-permute-start.4 = (bf16[256,512]{1,0:T(8,128)(2,1)S(1)}, bf16[256,512]{1,0:T(8,128)(2,1)S(1)}, u32[]{:S(2)}, u32[]{:S(2)}) collective-permute-start(bf16[256,512]{1,0:T(8,128)(2,1)S(1)} %copy-done.2), channel_id=1, source_target_pairs={{2,0},{0,2},{3,1},{1,3},{6,4},{4,6},{7,5},{5,7},{10,8},{8,10},{11,... | collective-permute-start | bytes 786440 | tf_op jit(solution)/shard_map/ppermute | solution.py:26
  17.4 1.0 %shard_map.160 = (bf16[12,512,128]{2,1,0:T(8,128)(2,1)S(1)}, bf16[12,512,128]{2,1,0:T(8,128)(2,1)S(1)}, bf16[12,16,512]{2,1,0:T(8,128)(2,1)S(1)}, bf16[12,16,512]{2,1,0:T(8,128)(2,1)S(1)}) custom-call(s32[1]{0:T(128)S(6)} %copy.17.tiles, s32[12,512]{1,0:T(8,128)S(1)} %copy-done.6, s32[1,512]{1,0:T(1,128)S(1)} %bitcast.13), custom_call_target="tpu_custom_call" | custom-call | flops 1024 | bytes 1024 | tf_op jit(solution)/shard_map/pallas_call | solution.py:51
  18.5 2.9 %shard_map.161.before = bf16[12,512,256]{2,1,0:T(8,128)(2,1)S(1)} custom-call(bf16[12,512,128]{2,1,0:T(8,128)(2,1)S(1)} %get-tuple-element.89.low, bf16[12,512,128]{2,1,0:T(8,128)(2,1)S(1)} %get-tuple-element.90.high, bf16[512,256]{1,0:T(8,128)(2,1)S(1)} %get-tuple-element.94.proj, bf16[272,256]{1,0:T(8,128)(2,1)S(1)} %collective-permute-done.3.beside.refs_4_), custom_call_target="tpu_custom_call" | custom-call | flops 1024 | bytes 1024 | tf_op jit(solution)/shard_map/pallas_call | solution.py:51
  22.4 1.6 %collective-permute-done.4.refs_1_ = bf16[256,512]{1,0:T(8,128)(2,1)S(1)} collective-permute-done((bf16[256,512]{1,0:T(8,128)(2,1)S(1)}, bf16[256,512]{1,0:T(8,128)(2,1)S(1)}, u32[]{:S(2)}, u32[]{:S(2)}) %collective-permute-start.4) | collective-permute-done | bytes 262176 | tf_op jit(solution)/shard_map/ppermute | solution.py:26
  24.1 1.1 %shard_map.162 = (bf16[512,512]{1,0:T(8,128)(2,1)}, f32[512,512]{1,0:T(8,128)S(1)}, f32[512,512]{1,0:T(8,128)S(1)}) custom-call(s32[1]{0:T(128)S(6)} %copy.17.tiles, bf16[256,512]{1,0:T(8,128)(2,1)S(1)} %copy-done.2, bf16[256,512]{1,0:T(8,128)(2,1)S(1)} %collective-permute-done.4.refs_1_, bf16[512,512]{1,0:T(8,128)(2,1)S(1)} %get-tuple-element.84.feats.refs_2_, ...), custom_call_target="tpu_custom_call" | custom-call | flops 1024 | bytes 1024 | tf_op jit(solution)/shard_map/pallas_call | solution.py:51
  25.2 2.5 %shard_map.163.part = bf16[12,512,256]{2,1,0:T(8,128)(2,1)S(1)} custom-call(bf16[12,512,128]{2,1,0:T(8,128)(2,1)S(1)} %get-tuple-element.89.low, bf16[12,512,128]{2,1,0:T(8,128)(2,1)S(1)} %get-tuple-element.90.high, bf16[12,512,256]{2,1,0:T(8,128)(2,1)S(1)} %shard_map.161.before, bf16[272,256]{1,0:T(8,128)(2,1)S(1)} %collective-permute-done.1.west.refs_2_, ...), custom_call_target="tpu_custom_call" | custom-call | flops 1024 | bytes 1024 | tf_op jit(solution)/shard_map/pallas_call | solution.py:51
  28.4 2.5 %shard_map.165 = (bf16[256,256]{1,0:T(8,128)(2,1)S(1)}, bf16[12,256,256]{2,1,0:T(8,128)(2,1)S(1)}) custom-call(bf16[12,512,128]{2,1,0:T(8,128)(2,1)S(1)} %get-tuple-element.89.low, bf16[12,512,128]{2,1,0:T(8,128)(2,1)S(1)} %get-tuple-element.90.high, f32[512,256]{1,0:T(8,128)S(1)} %shard_map.159.base, s32[1,512]{1,0:T(1,128)S(1)} %bitcast.14, ...), custom_call_target="tpu_custom_call" | custom-call | flops 1024 | bytes 1024 | tf_op jit(solution)/shard_map/pallas_call | solution.py:51
  30.9 1.6 %collective-permute-start.8 = (bf16[256,256]{1,0:T(8,128)(2,1)S(1)}, bf16[256,256]{1,0:T(8,128)(2,1)S(1)}, u32[]{:S(2)}, u32[]{:S(2)}) collective-permute-start(bf16[256,256]{1,0:T(8,128)(2,1)S(1)} %get-tuple-element.107.refs_0_), channel_id=1, source_target_pairs={{2,0},{0,2},{3,1},{1,3},{6,4},{4,6},{7,5},{5,7},{10,8},{8,10},{11,... | collective-permute-start | bytes 393224 | tf_op jit(solution)/shard_map/ppermute | solution.py:26
  32.5 2.5 %shard_map.168 = (bf16[256,256]{1,0:T(8,128)(2,1)S(1)}, bf16[12,256,256]{2,1,0:T(8,128)(2,1)S(1)}) custom-call(bf16[12,512,128]{2,1,0:T(8,128)(2,1)S(1)} %get-tuple-element.89.low, bf16[12,512,128]{2,1,0:T(8,128)(2,1)S(1)} %get-tuple-element.90.high, f32[512,256]{1,0:T(8,128)S(1)} %shard_map.159.base, s32[1,512]{1,0:T(1,128)S(1)} %bitcast.15, ...), custom_call_target="tpu_custom_call" | custom-call | flops 1024 | bytes 1024 | tf_op jit(solution)/shard_map/pallas_call | solution.py:51
  35.5 1.0 %collective-permute-done.8.refs_1_ = bf16[256,256]{1,0:T(8,128)(2,1)S(1)} collective-permute-done((bf16[256,256]{1,0:T(8,128)(2,1)S(1)}, bf16[256,256]{1,0:T(8,128)(2,1)S(1)}, u32[]{:S(2)}, u32[]{:S(2)}) %collective-permute-start.8) | collective-permute-done | bytes 131104 | tf_op jit(solution)/shard_map/ppermute | solution.py:26
  36.5 0.9 %shard_map.166 = (bf16[512,256]{1,0:T(8,128)(2,1)S(1)}, bf16[512,256]{1,0:T(8,128)(2,1)S(1)}, f32[256,256]{1,0:T(8,128)S(1)}) custom-call(s32[1,512]{1,0:T(1,128)S(1)} %bitcast.16, bf16[256,256]{1,0:T(8,128)(2,1)S(1)} %get-tuple-element.107.refs_0_, bf16[256,256]{1,0:T(8,128)(2,1)S(1)} %collective-permute-done.8.refs_1_, bf16[512,512]{1,0:T(8,128)(2,1)S(1)} %copy-done.1, ...), custom_call_target="tpu_custom_call" | custom-call | flops 1024 | bytes 1024 | tf_op jit(solution)/shard_map/pallas_call | solution.py:51
  37.4 1.4 %shard_map.167 = (bf16[12,256,256]{2,1,0:T(8,128)(2,1)S(1)}, f32[768,256]{1,0:T(8,128)S(1)}) custom-call(bf16[12,16,512]{2,1,0:T(8,128)(2,1)S(1)} %get-tuple-element.87.low, bf16[12,16,512]{2,1,0:T(8,128)(2,1)S(1)} %get-tuple-element.88.high, bf16[12,256,256]{2,1,0:T(8,128)(2,1)S(1)} %get-tuple-element.106.slope, f32[256,256]{1,0:T(8,128)S(1)} %get-tuple-element.112.scale), custom_call_target="tpu_custom_call" | custom-call | flops 1024 | bytes 1024 | tf_op jit(solution)/shard_map/pallas_call | solution.py:51
  38.9 1.4 %collective-permute-done.9.refs_1_ = bf16[256,256]{1,0:T(8,128)(2,1)S(1)} collective-permute-done((bf16[256,256]{1,0:T(8,128)(2,1)S(1)}, bf16[256,256]{1,0:T(8,128)(2,1)S(1)}, u32[]{:S(2)}, u32[]{:S(2)}) %collective-permute-start.9) | collective-permute-done | bytes 131104 | tf_op jit(solution)/shard_map/ppermute | solution.py:26
  40.3 0.8 %shard_map.169 = (bf16[512,256]{1,0:T(8,128)(2,1)S(1)}, bf16[512,256]{1,0:T(8,128)(2,1)S(1)}, f32[256,256]{1,0:T(8,128)S(1)}) custom-call(s32[1,512]{1,0:T(1,128)S(1)} %bitcast.17, bf16[256,256]{1,0:T(8,128)(2,1)S(1)} %get-tuple-element.115.refs_0_, bf16[256,256]{1,0:T(8,128)(2,1)S(1)} %collective-permute-done.9.refs_1_, bf16[512,512]{1,0:T(8,128)(2,1)S(1)} %copy-done.1, ...), custom_call_target="tpu_custom_call" | custom-call | flops 1024 | bytes 1024 | tf_op jit(solution)/shard_map/pallas_call | solution.py:51
  41.9 1.0 %shard_map.171 = bf16[2,256,256]{2,1,0:T(8,128)(2,1)S(1)} custom-call(bf16[12,16,512]{2,1,0:T(8,128)(2,1)S(1)} %get-tuple-element.87.low, bf16[12,16,512]{2,1,0:T(8,128)(2,1)S(1)} %get-tuple-element.88.high, bf16[12,256,256]{2,1,0:T(8,128)(2,1)S(1)} %get-tuple-element.118.grads.refs_1_, f32[768,256]{1,0:T(8,128)S(1)} %get-tuple-element.117.before, ...), custom_call_target="tpu_custom_call" | custom-call | flops 1024 | bytes 1024 | tf_op jit(solution)/shard_map/pallas_call | solution.py:51
  43.0 2.6 %shard_map.172 = (bf16[256,256]{1,0:T(8,128)(2,1)S(1)}, bf16[256,256]{1,0:T(8,128)(2,1)S(1)}, bf16[256,256]{1,0:T(8,128)(2,1)S(1)}) custom-call(bf16[12,16,512]{2,1,0:T(8,128)(2,1)S(1)} %get-tuple-element.87.low, bf16[12,16,512]{2,1,0:T(8,128)(2,1)S(1)} %get-tuple-element.88.high, bf16[12,256,256]{2,1,0:T(8,128)(2,1)S(1)} %get-tuple-element.127.refs_0_, ...), custom_call_target="tpu_custom_call" | custom-call | flops 1024 | bytes 1024 | tf_op jit(solution)/shard_map/pallas_call | solution.py:51
  46.2 1.8 %collective-permute-done.10.across = bf16[256,256]{1,0:T(8,128)(2,1)S(1)} collective-permute-done((bf16[256,256]{1,0:T(8,128)(2,1)S(1)}, bf16[256,256]{1,0:T(8,128)(2,1)S(1)}, u32[]{:S(2)}, u32[]{:S(2)}) %collective-permute-start.10) | collective-permute-done | bytes 131104 | tf_op jit(solution)/shard_map/ppermute | solution.py:562
  48.2 1.5 %collective-permute-start.13 = (bf16[256,256]{1,0:T(8,128)(2,1)S(1)}, bf16[256,256]{1,0:T(8,128)(2,1)S(1)}, u32[]{:S(2)}, u32[]{:S(2)}) collective-permute-start(bf16[256,256]{1,0:T(8,128)(2,1)S(1)} %get-tuple-element.126), channel_id=1, source_target_pairs={{4,0},{8,4},{12,8},{0,12},{5,1},{9,5},{13,9},{1,13},{6,2},{10,6},{... | collective-permute-start | bytes 393224 | tf_op jit(solution)/shard_map/ppermute | solution.py:26
  50.3 2.1 %shard_map.175 = (f32[512,256]{1,0:T(8,128)S(1)}, bf16[256,512]{1,0:T(8,128)(2,1)S(1)}) custom-call(bf16[12,16,512]{2,1,0:T(8,128)(2,1)S(1)} %get-tuple-element.87.low, bf16[12,16,512]{2,1,0:T(8,128)(2,1)S(1)} %get-tuple-element.88.high, bf16[12,256,256]{2,1,0:T(8,128)(2,1)S(1)} %get-tuple-element.127.refs_0_, ...), custom_call_target="tpu_custom_call" | custom-call | flops 1024 | bytes 1024 | tf_op jit(solution)/shard_map/pallas_call | solution.py:51
  52.3 1.2 %shard_map.176 = (bf16[256,512]{1,0:T(8,128)(2,1)}, f32[256,512]{1,0:T(8,128)S(1)}) custom-call(s32[1]{0:T(128)S(6)} %copy.17.tiles, bf16[256,512]{1,0:T(8,128)(2,1)S(1)} %get-tuple-element.80.refs_0_.feats, bf16[256,512]{1,0:T(8,128)(2,1)S(1)} %copy-done.2, bf16[256,512]{1,0:T(8,128)(2,1)S(1)} %get-tuple-element.81.w_out, bf16[256,512]{1,0:T(8,128)(2,1)S(1)} %copy-done.4, ...), custom_call_target="tpu_custom_call" | custom-call | flops 1024 | bytes 1024 | tf_op jit(solution)/shard_map/pallas_call | solution.py:51
  55.0 2.1 %collective-permute-done.14.refs_0_ = bf16[256,256]{1,0:T(8,128)(2,1)S(1)} collective-permute-done((bf16[256,256]{1,0:T(8,128)(2,1)S(1)}, bf16[256,256]{1,0:T(8,128)(2,1)S(1)}, u32[]{:S(2)}, u32[]{:S(2)}) %collective-permute-start.14) | collective-permute-done | bytes 131104 | tf_op jit(solution)/shard_map/ppermute | solution.py:26
  58.7 0.7 %collective-permute-done.17.refs_1_ = bf16[256,256]{1,0:T(8,128)(2,1)S(1)} collective-permute-done((bf16[256,256]{1,0:T(8,128)(2,1)S(1)}, bf16[256,256]{1,0:T(8,128)(2,1)S(1)}, u32[]{:S(2)}, u32[]{:S(2)}) %collective-permute-start.17) | collective-permute-done | bytes 131104 | tf_op jit(solution)/shard_map/ppermute | solution.py:26
  59.5 4.6 %collective-permute-start.20 = (bf16[64,256]{1,0:T(8,128)(2,1)S(1)}, bf16[64,256]{1,0:T(8,128)(2,1)S(1)}, u32[]{:S(2)}, u32[]{:S(2)}) collective-permute-start(bf16[64,256]{1,0:T(8,128)(2,1)S(1)} %get-tuple-element.157), channel_id=1, source_target_pairs={{4,0},{8,4},{12,8},{0,12},{5,1},{9,5},{13,9},{1,13},{6,2},{10,6},{... | collective-permute-start | bytes 98312 | tf_op jit(solution)/shard_map/ppermute | solution.py:26
  64.7 0.7 %shard_map.182 = bf16[256,512]{1,0:T(8,128)(2,1)} custom-call(f32[256,256]{1,0:T(8,128)S(1)} %get-tuple-element.147.refs_0_, bf16[256,256]{1,0:T(8,128)(2,1)S(1)} %collective-permute-done.15.refs_1_, bf16[256,256]{1,0:T(8,128)(2,1)S(1)} %shard_map.181.refs_2_), custom_call_target="tpu_custom_call" | custom-call | flops 1024 | bytes 1024 | tf_op jit(solution)/shard_map/pallas_call | solution.py:51
  65.6 3.2 %collective-permute-done.19.refs_1_ = bf16[64,256]{1,0:T(8,128)(2,1)S(1)} collective-permute-done((bf16[64,256]{1,0:T(8,128)(2,1)S(1)}, bf16[64,256]{1,0:T(8,128)(2,1)S(1)}, u32[]{:S(2)}, u32[]{:S(2)}) %collective-permute-start.19) | collective-permute-done | bytes 32800 | tf_op jit(solution)/shard_map/ppermute | solution.py:26
  68.9 0.9 %collective-permute-done.18.refs_0_ = bf16[64,256]{1,0:T(8,128)(2,1)S(1)} collective-permute-done((bf16[64,256]{1,0:T(8,128)(2,1)S(1)}, bf16[64,256]{1,0:T(8,128)(2,1)S(1)}, u32[]{:S(2)}, u32[]{:S(2)}) %collective-permute-start.18) | collective-permute-done | bytes 32800 | tf_op jit(solution)/shard_map/ppermute | solution.py:26
  (59 shorter events, 9.7 us)
Async XLA Ops:
  0.6 9.5 %copy-start.9 = (s32[1,6,2]{1,2,0:T(2,128)S(1)}, s32[1,6,2]{1,2,0:T(2,128)}, u32[]{:S(2)}) copy-start(s32[1,6,2]{1,2,0:T(2,128)} %param.19) | copy-start | bytes 148
  0.6 14.7 %copy-start.7 = (f32[512]{0:T(512)S(1)}, f32[512]{0:T(512)}, u32[]{:S(2)}) copy-start(f32[512]{0:T(512)} %param.22) | copy-start | bytes 6148
  0.7 9.5 %collective-permute-start = (bf16[256,512]{1,0:T(8,128)(2,1)}, bf16[256,512]{1,0:T(8,128)(2,1)S(1)}, u32[]{:S(2)}, u32[]{:S(2)}) collective-permute-start(bf16[256,512]{1,0:T(8,128)(2,1)} %refs_2_.1), channel_id=1, source_target_pairs={{2,0},{0,2},{3,1},{1,3},{6,4},{4,6},{7,5},{5,7},{10,8},{8,10},{11,... | collective-permute-start | bytes 786440 | tf_op jit(solution)/shard_map/ppermute | solution.py:26
  6.9 8.8 %copy-start.2 = (bf16[256,512]{1,0:T(8,128)(2,1)S(1)}, bf16[256,512]{1,0:T(8,128)(2,1)}, u32[]{:S(2)}) copy-start(bf16[256,512]{1,0:T(8,128)(2,1)} %cots.1) | copy-start | bytes 786436
  6.9 10.5 %copy-start.5 = (s32[512]{0:T(512)S(1)}, s32[512]{0:T(512)}, u32[]{:S(2)}) copy-start(s32[512]{0:T(512)} %param.17) | copy-start | bytes 6148
  7.0 10.5 %copy-start.6 = (s32[12,512]{1,0:T(8,128)S(1)}, s32[12,512]{1,0:T(8,128)}, u32[]{:S(2)}) copy-start(s32[12,512]{1,0:T(8,128)} %senders) | copy-start | bytes 73732
  11.3 7.2 %collective-permute-start.3 = (bf16[272,256]{1,0:T(8,128)(2,1)S(1)}, bf16[272,256]{1,0:T(8,128)(2,1)S(1)}, u32[]{:S(2)}, u32[]{:S(2)}) collective-permute-start(bf16[272,256]{1,0:T(8,128)(2,1)S(1)} %get-tuple-element.95), channel_id=1, source_target_pairs={{1,0},{0,1},{3,2},{2,3},{5,4},{4,5},{7,6},{6,7},{9,8},{8,9},{11,10... | collective-permute-start | bytes 417800 | tf_op jit(solution)/shard_map/ppermute | solution.py:26
  11.3 10.1 %collective-permute-start.1 = (bf16[272,256]{1,0:T(8,128)(2,1)S(1)}, bf16[272,256]{1,0:T(8,128)(2,1)S(1)}, u32[]{:S(2)}, u32[]{:S(2)}) collective-permute-start(bf16[272,256]{1,0:T(8,128)(2,1)S(1)} %get-tuple-element.92), channel_id=1, source_target_pairs={{12,0},{0,4},{4,8},{8,12},{13,1},{1,5},{5,9},{9,13},{14,2},{2,6},{... | collective-permute-start | bytes 417800 | tf_op jit(solution)/shard_map/ppermute | solution.py:26
  13.2 8.7 %collective-permute-start.2 = (bf16[272,256]{1,0:T(8,128)(2,1)S(1)}, bf16[272,256]{1,0:T(8,128)(2,1)S(1)}, u32[]{:S(2)}, u32[]{:S(2)}) collective-permute-start(bf16[272,256]{1,0:T(8,128)(2,1)S(1)} %get-tuple-element.93), channel_id=1, source_target_pairs={{4,0},{8,4},{12,8},{0,12},{5,1},{9,5},{13,9},{1,13},{6,2},{10,6},{... | collective-permute-start | bytes 417800 | tf_op jit(solution)/shard_map/ppermute | solution.py:26
  15.7 8.4 %collective-permute-start.4 = (bf16[256,512]{1,0:T(8,128)(2,1)S(1)}, bf16[256,512]{1,0:T(8,128)(2,1)S(1)}, u32[]{:S(2)}, u32[]{:S(2)}) collective-permute-start(bf16[256,512]{1,0:T(8,128)(2,1)S(1)} %copy-done.2), channel_id=1, source_target_pairs={{2,0},{0,2},{3,1},{1,3},{6,4},{4,6},{7,5},{5,7},{10,8},{8,10},{11,... | collective-permute-start | bytes 786440 | tf_op jit(solution)/shard_map/ppermute | solution.py:26
  17.4 11.0 %collective-permute-start.5 = (bf16[272,256]{1,0:T(8,128)(2,1)S(1)}, bf16[272,256]{1,0:T(8,128)(2,1)S(1)}, u32[]{:S(2)}, u32[]{:S(2)}) collective-permute-start(bf16[272,256]{1,0:T(8,128)(2,1)S(1)} %get-tuple-element.103), channel_id=1, source_target_pairs={{0,9},{1,8},{4,13},{5,12},{8,1},{9,0},{12,5},{13,4},{2,11},{3,10},... | collective-permute-start | bytes 417800 | tf_op jit(solution)/shard_map/ppermute | solution.py:618
  18.5 5.6 %copy-start = (bf16[512,512]{1,0:T(8,128)(2,1)S(1)}, bf16[512,512]{1,0:T(8,128)(2,1)}, u32[]{:S(2)}) copy-start(bf16[512,512]{1,0:T(8,128)(2,1)} %refs_3_.3) | copy-start | bytes 1572868
  18.5 5.6 %copy-start.3 = (bf16[512,512]{1,0:T(8,128)(2,1)S(1)}, bf16[512,512]{1,0:T(8,128)(2,1)}, u32[]{:S(2)}) copy-start(bf16[512,512]{1,0:T(8,128)(2,1)} %get-tuple-element.98.refs_5_) | copy-start | bytes 1572868
  18.5 5.6 %copy-start.8 = (f32[512]{0:T(512)S(1)}, f32[512]{0:T(512)}, u32[]{:S(2)}) copy-start(f32[512]{0:T(512)} %param.26) | copy-start | bytes 6148
  21.9 6.5 %collective-permute-start.6 = (bf16[272,256]{1,0:T(8,128)(2,1)S(1)}, bf16[272,256]{1,0:T(8,128)(2,1)S(1)}, u32[]{:S(2)}, u32[]{:S(2)}) collective-permute-start(bf16[272,256]{1,0:T(8,128)(2,1)S(1)} %collective-permute-done.1.west.refs_2_), channel_id=1, source_target_pairs={{1,0},{0,1},{3,2},{2,3},{5,4},{4,5},{7,6},{6,7},{9,8},{8,9},{11,10... | collective-permute-start | bytes 417800 | tf_op jit(solution)/shard_map/ppermute | solution.py:26
  22.4 6.1 %collective-permute-start.7 = (bf16[272,256]{1,0:T(8,128)(2,1)S(1)}, bf16[272,256]{1,0:T(8,128)(2,1)S(1)}, u32[]{:S(2)}, u32[]{:S(2)}) collective-permute-start(bf16[272,256]{1,0:T(8,128)(2,1)S(1)} %collective-permute-done.2.east.refs_3_), channel_id=1, source_target_pairs={{1,0},{0,1},{3,2},{2,3},{5,4},{4,5},{7,6},{6,7},{9,8},{8,9},{11,10... | collective-permute-start | bytes 417800 | tf_op jit(solution)/shard_map/ppermute | solution.py:26
  30.9 5.6 %copy-start.1 = (bf16[512,512]{1,0:T(8,128)(2,1)S(1)}, bf16[512,512]{1,0:T(8,128)(2,1)}, u32[]{:S(2)}) copy-start(bf16[512,512]{1,0:T(8,128)(2,1)} %get-tuple-element.108.refs_2_) | copy-start | bytes 1572868
  30.9 5.6 %collective-permute-start.8 = (bf16[256,256]{1,0:T(8,128)(2,1)S(1)}, bf16[256,256]{1,0:T(8,128)(2,1)S(1)}, u32[]{:S(2)}, u32[]{:S(2)}) collective-permute-start(bf16[256,256]{1,0:T(8,128)(2,1)S(1)} %get-tuple-element.107.refs_0_), channel_id=1, source_target_pairs={{2,0},{0,2},{3,1},{1,3},{6,4},{4,6},{7,5},{5,7},{10,8},{8,10},{11,... | collective-permute-start | bytes 393224 | tf_op jit(solution)/shard_map/ppermute | solution.py:26
  34.9 5.3 %collective-permute-start.9 = (bf16[256,256]{1,0:T(8,128)(2,1)S(1)}, bf16[256,256]{1,0:T(8,128)(2,1)S(1)}, u32[]{:S(2)}, u32[]{:S(2)}) collective-permute-start(bf16[256,256]{1,0:T(8,128)(2,1)S(1)} %get-tuple-element.115.refs_0_), channel_id=1, source_target_pairs={{2,0},{0,2},{3,1},{1,3},{6,4},{4,6},{7,5},{5,7},{10,8},{8,10},{11,... | collective-permute-start | bytes 393224 | tf_op jit(solution)/shard_map/ppermute | solution.py:26
  41.7 6.3 %collective-permute-start.10 = (bf16[256,256]{1,0:T(8,128)(2,1)S(1)}, bf16[256,256]{1,0:T(8,128)(2,1)S(1)}, u32[]{:S(2)}, u32[]{:S(2)}) collective-permute-start(bf16[256,256]{1,0:T(8,128)(2,1)S(1)} %get-tuple-element.122), channel_id=1, source_target_pairs={{0,13},{1,4},{4,1},{5,8},{8,5},{9,12},{12,9},{13,0},{2,15},{3,6},{... | collective-permute-start | bytes 393224 | tf_op jit(solution)/shard_map/ppermute | solution.py:562
  42.9 5.2 %collective-permute-start.11 = (bf16[2,256,256]{2,1,0:T(8,128)(2,1)S(1)}, bf16[2,256,256]{2,1,0:T(8,128)(2,1)S(1)}, u32[]{:S(2)}, u32[]{:S(2)}) collective-permute-start(bf16[2,256,256]{2,1,0:T(8,128)(2,1)S(1)} %shard_map.171), channel_id=1, source_target_pairs={{1,0},{0,1},{3,2},{2,3},{5,4},{4,5},{7,6},{6,7},{9,8},{8,9},{11,10... | collective-permute-start | bytes 786440 | tf_op jit(solution)/shard_map/ppermute | solution.py:26
  45.6 7.9 %collective-permute-start.12 = (bf16[256,256]{1,0:T(8,128)(2,1)S(1)}, bf16[256,256]{1,0:T(8,128)(2,1)S(1)}, u32[]{:S(2)}, u32[]{:S(2)}) collective-permute-start(bf16[256,256]{1,0:T(8,128)(2,1)S(1)} %get-tuple-element.136), channel_id=1, source_target_pairs={{1,0},{0,1},{3,2},{2,3},{5,4},{4,5},{7,6},{6,7},{9,8},{8,9},{11,10... | collective-permute-start | bytes 393224 | tf_op jit(solution)/shard_map/ppermute | solution.py:26
  48.2 5.4 %collective-permute-start.13 = (bf16[256,256]{1,0:T(8,128)(2,1)S(1)}, bf16[256,256]{1,0:T(8,128)(2,1)S(1)}, u32[]{:S(2)}, u32[]{:S(2)}) collective-permute-start(bf16[256,256]{1,0:T(8,128)(2,1)S(1)} %get-tuple-element.126), channel_id=1, source_target_pairs={{4,0},{8,4},{12,8},{0,12},{5,1},{9,5},{13,9},{1,13},{6,2},{10,6},{... | collective-permute-start | bytes 393224 | tf_op jit(solution)/shard_map/ppermute | solution.py:26
  49.7 2.6 %copy-start.4 = (bf16[256,512]{1,0:T(8,128)(2,1)S(1)}, bf16[256,512]{1,0:T(8,128)(2,1)}, u32[]{:S(2)}) copy-start(bf16[256,512]{1,0:T(8,128)(2,1)} %get-tuple-element.82.w_node_v_t) | copy-start | bytes 786436
  49.7 7.4 %collective-permute-start.14 = (bf16[256,256]{1,0:T(8,128)(2,1)S(1)}, bf16[256,256]{1,0:T(8,128)(2,1)S(1)}, u32[]{:S(2)}, u32[]{:S(2)}) collective-permute-start(bf16[256,256]{1,0:T(8,128)(2,1)S(1)} %get-tuple-element.137), channel_id=1, source_target_pairs={{12,0},{0,4},{4,8},{8,12},{13,1},{1,5},{5,9},{9,13},{14,2},{2,6},{... | collective-permute-start | bytes 393224 | tf_op jit(solution)/shard_map/ppermute | solution.py:26
  54.3 5.1 %collective-permute-start.17 = (bf16[256,256]{1,0:T(8,128)(2,1)S(1)}, bf16[256,256]{1,0:T(8,128)(2,1)S(1)}, u32[]{:S(2)}, u32[]{:S(2)}) collective-permute-start(bf16[256,256]{1,0:T(8,128)(2,1)S(1)} %bitcast.22), channel_id=1, source_target_pairs={{2,0},{0,2},{3,1},{1,3},{6,4},{4,6},{7,5},{5,7},{10,8},{8,10},{11,... | collective-permute-start | bytes 393224 | tf_op jit(solution)/shard_map/ppermute | solution.py:26
  57.5 1.9 %collective-permute-start.16 = (bf16[4,64,256]{2,1,0:T(8,128)(2,1)S(1)}, bf16[4,64,256]{2,1,0:T(8,128)(2,1)S(1)}, u32[]{:S(2)}, u32[]{:S(2)}) collective-permute-start(bf16[4,64,256]{2,1,0:T(8,128)(2,1)S(1)} %get-tuple-element.149), channel_id=1, source_target_pairs={{1,0},{0,1},{3,2},{2,3},{5,4},{4,5},{7,6},{6,7},{9,8},{8,9},{11,10... | collective-permute-start | bytes 393224 | tf_op jit(solution)/shard_map/ppermute | solution.py:26
  58.0 6.7 %collective-permute-start.15 = (bf16[256,256]{1,0:T(8,128)(2,1)S(1)}, bf16[256,256]{1,0:T(8,128)(2,1)S(1)}, u32[]{:S(2)}, u32[]{:S(2)}) collective-permute-start(bf16[256,256]{1,0:T(8,128)(2,1)S(1)} %bitcast.21), channel_id=1, source_target_pairs={{2,0},{0,2},{3,1},{1,3},{6,4},{4,6},{7,5},{5,7},{10,8},{8,10},{11,... | collective-permute-start | bytes 393224 | tf_op jit(solution)/shard_map/ppermute | solution.py:26
  59.5 6.2 %collective-permute-start.20 = (bf16[64,256]{1,0:T(8,128)(2,1)S(1)}, bf16[64,256]{1,0:T(8,128)(2,1)S(1)}, u32[]{:S(2)}, u32[]{:S(2)}) collective-permute-start(bf16[64,256]{1,0:T(8,128)(2,1)S(1)} %get-tuple-element.157), channel_id=1, source_target_pairs={{4,0},{8,4},{12,8},{0,12},{5,1},{9,5},{13,9},{1,13},{6,2},{10,6},{... | collective-permute-start | bytes 98312 | tf_op jit(solution)/shard_map/ppermute | solution.py:26
  64.0 4.8 %collective-permute-start.19 = (bf16[64,256]{1,0:T(8,128)(2,1)S(1)}, bf16[64,256]{1,0:T(8,128)(2,1)S(1)}, u32[]{:S(2)}, u32[]{:S(2)}) collective-permute-start(bf16[64,256]{1,0:T(8,128)(2,1)S(1)} %get-tuple-element.158), channel_id=1, source_target_pairs={{8,0},{12,4},{0,8},{4,12},{9,1},{13,5},{1,9},{5,13},{10,2},{14,6},... | collective-permute-start | bytes 98312 | tf_op jit(solution)/shard_map/ppermute | solution.py:26
  64.0 5.7 %collective-permute-start.18 = (bf16[64,256]{1,0:T(8,128)(2,1)S(1)}, bf16[64,256]{1,0:T(8,128)(2,1)S(1)}, u32[]{:S(2)}, u32[]{:S(2)}) collective-permute-start(bf16[64,256]{1,0:T(8,128)(2,1)S(1)} %get-tuple-element.159), channel_id=1, source_target_pairs={{12,0},{0,4},{4,8},{8,12},{13,1},{1,5},{5,9},{9,13},{14,2},{2,6},{... | collective-permute-start | bytes 98312 | tf_op jit(solution)/shard_map/ppermute | solution.py:26

commit v9 on v8

--- a/solution.py
+++ b/solution.py
@@ -481,7 +481,7 @@
     lon = lax.axis_index("lon")
     lons, columns, _ = w_mine.shape
     for k in range(lons):
-        band = lax.rem(lon + k, lons) * 2
+        band = (lon ^ k) * 2
         for out, core in ((w_mine, sub), (w_beside, 1 - sub)):
             spot = pl.multiple_of((band + core) * columns, columns)
             out[k] = weight[pl.ds(spot, columns), :].astype(out.dtype)
@@ -512,18 +512,14 @@
         start += part.shape[1]
 
 
-def sum_kernel(w_mine, w_beside, near, sent):
-    near[...] = w_mine[0] + w_beside[0].astype(jnp.float32)
-    for k in range(sent.shape[0]):
-        sent[k] = (w_mine[k + 1] + w_beside[k + 1].astype(jnp.float32)).astype(jnp.bfloat16)
-
-
-def weight_kernel(near, *refs):
-    out = refs[-1]
-    total = near[...]
-    for ref in refs[:-1]:
-        total += ref[...].astype(jnp.float32)
-    out[...] = total
+def sum_kernel(held, received, near, sent):
+    half = near.shape[0]
+    near[...] = held[:half] + received[:half].astype(jnp.float32)
+    sent[...] = (held[half:] + received[half:].astype(jnp.float32)).astype(jnp.bfloat16)
+
+
+def weight_kernel(held, received, out):
+    out[...] = held[0] + received[0].astype(jnp.float32)
 
 
 def shards(
@@ -802,15 +798,18 @@
         )
         finals = [grad_features]
 
-    near, w_sent = call(
-        sum_kernel,
-        (shape((columns, hid), f32), shape((lons - 1, columns, hid), bf16)),
-        [w_mine, w_beside],
-        scalars=0,
-    )
-    w_terms = [shifted(w_sent[k - 1], "lon", k) for k in range(1, lons)]
+    span = lons
+    while span > 1:
+        span //= 2
+        w_mine, w_sent = call(
+            sum_kernel,
+            (shape((span, columns, hid), f32), shape((span, columns, hid), bf16)),
+            [w_mine, w_beside],
+            scalars=0,
+        )
+        w_beside = lax.ppermute(w_sent, "lon", [(i, i ^ span) for i in range(lons)])
     grad_w_send = call(
-        weight_kernel, shape((columns, hid), f32), [near] + w_terms, scalars=0
+        weight_kernel, shape((columns, hid), f32), [w_mine, w_beside], scalars=0
     )
     return (updated, grad_features, grad_w_send.T)
 

time: 70.6 us -> 69.6 us (0.986)
  starting transfers between devices: 20.9 us -> 19 us
  waiting for transfers between devices: 16.8 us -> 17.7 us
    ppermute x0 -> x2, waiting for transfers between devices: none -> 5.32 us  [shards(): w_beside = lax.ppermute(w_sent, 'lon', [(i, i ^ span) for i in range(lons)])]
    ppermute x19 -> x16, starting transfers between devices: 20.7 us -> 15.5 us  [shifted(): return lax.ppermute(block, axis, route)]
    ppermute x19 -> x16, waiting for transfers between devices: 14.3 us -> 9.91 us  [shifted(): return lax.ppermute(block, axis, route)]
    ppermute x0 -> x2, starting transfers between devices: none -> 3.29 us  [shards(): w_beside = lax.ppermute(w_sent, 'lon', [(i, i ^ span) for i in range(lons)])]
    pallas_call x28 -> x29, Pallas kernels: 31 us -> 31 us  [call(): pl.pallas_call(kernel, out_shape=out_shape, in_specs=[smem] * scalars + [...]
  transfers between devices with their start and end apart: 21 -> 20, of which waited for: 12 -> 11; matrix products, arithmetic and copies ran while one was open for 0% -> 0% of each run, Pallas kernels for 36% -> 36%
where the time goes in v9:
time: 69.6 us; the launch traced here: 69.5 us
  Pallas kernels  31 us (45%)
  starting transfers between devices  19 us (27%)
  waiting for transfers between devices  17.7 us (25%)
  between operations  1.67 us (2%)
    pallas_call x29, Pallas kernels, call(): pl.pallas_call(kernel, out_shape=out_shape, in_specs=[smem] * scalars + [...  31 us
    ppermute x16, starting transfers between devices, shifted(): return lax.ppermute(block, axis, route)  15.5 us
    ppermute x16, waiting for transfers between devices, shifted(): return lax.ppermute(block, axis, route)  9.91 us
    ppermute x2, waiting for transfers between devices, shards(): w_beside = lax.ppermute(w_sent, 'lon', [(i, i ^ span) for i in range(lons)])  5.32 us
    ppermute x2, starting transfers between devices, shards(): w_beside = lax.ppermute(w_sent, 'lon', [(i, i ^ span) for i in range(lons)])  3.29 us
    ppermute x1, waiting for transfers between devices, shards(): across = lambda block: lax.ppermute(block, cycle, across_route)  1.86 us
  transfers between devices with their start and end apart: 20, of which 11 were waited for; matrix products, arithmetic and copies ran while one was open for 0% of the time, Pallas kernels for 36%

profile of v9, /device:TPU:0, one launch (start us, length us, event | category | flops | bytes accessed | tf_op | source)
XLA Modules:
  0.0 69.5 jit_solution(9851544157723347693)
XLA Ops:
  0.7 3.0 %collective-permute-start = (bf16[256,512]{1,0:T(8,128)(2,1)}, bf16[256,512]{1,0:T(8,128)(2,1)S(1)}, u32[]{:S(2)}, u32[]{:S(2)}) collective-permute-start(bf16[256,512]{1,0:T(8,128)(2,1)} %refs_2_.1), channel_id=1, source_target_pairs={{2,0},{0,2},{3,1},{1,3},{6,4},{4,6},{7,5},{5,7},{10,8},{8,10},{11,... | collective-permute-start | bytes 786440 | tf_op jit(solution)/shard_map/ppermute | solution.py:26
  3.7 3.3 %shard_map.157 = (bf16[256,512]{1,0:T(8,128)(2,1)S(1)}, bf16[256,512]{1,0:T(8,128)(2,1)S(1)}, bf16[256,512]{1,0:T(8,128)(2,1)S(1)}, bf16[256,512]{1,0:T(8,128)(2...) custom-call(bf16[512,512]{1,0:T(8,128)(2,1)} %refs_0_.1, ...), custom_call_target="tpu_custom_call" | custom-call | flops 1024 | bytes 1024 | tf_op jit(solution)/shard_map/pallas_call | solution.py:51
  7.7 2.5 %collective-permute-done.refs_1_ = bf16[256,512]{1,0:T(8,128)(2,1)S(1)} collective-permute-done((bf16[256,512]{1,0:T(8,128)(2,1)}, bf16[256,512]{1,0:T(8,128)(2,1)S(1)}, u32[]{:S(2)}, u32[]{:S(2)}) %collective-permute-start) | collective-permute-done | bytes 262176 | tf_op jit(solution)/shard_map/ppermute | solution.py:26
  10.2 1.1 %shard_map.158 = (bf16[512,512]{1,0:T(8,128)(2,1)S(1)}, bf16[512,256]{1,0:T(8,128)(2,1)S(1)}, bf16[272,256]{1,0:T(8,128)(2,1)S(1)}, bf16[272,256]{1,0:T(8,128)(2...) custom-call(s32[1]{0:T(128)S(6)} %copy.17.tiles, s32[1,2,6]{2,1,0:T(2,128)S(1)} %bitcast.14, ...), custom_call_target="tpu_custom_call" | custom-call | flops 1024 | bytes 1024 | tf_op jit(solution)/shard_map/pallas_call | solution.py:51
  11.3 1.9 %collective-permute-start.1 = (bf16[272,256]{1,0:T(8,128)(2,1)S(1)}, bf16[272,256]{1,0:T(8,128)(2,1)S(1)}, u32[]{:S(2)}, u32[]{:S(2)}) collective-permute-start(bf16[272,256]{1,0:T(8,128)(2,1)S(1)} %get-tuple-element.94), channel_id=1, source_target_pairs={{12,0},{0,4},{4,8},{8,12},{13,1},{1,5},{5,9},{9,13},{14,2},{2,6},{... | collective-permute-start | bytes 417800 | tf_op jit(solution)/shard_map/ppermute | solution.py:26
  13.2 2.1 %collective-permute-start.2 = (bf16[272,256]{1,0:T(8,128)(2,1)S(1)}, bf16[272,256]{1,0:T(8,128)(2,1)S(1)}, u32[]{:S(2)}, u32[]{:S(2)}) collective-permute-start(bf16[272,256]{1,0:T(8,128)(2,1)S(1)} %get-tuple-element.95), channel_id=1, source_target_pairs={{4,0},{8,4},{12,8},{0,12},{5,1},{9,5},{13,9},{1,13},{6,2},{10,6},{... | collective-permute-start | bytes 417800 | tf_op jit(solution)/shard_map/ppermute | solution.py:26
  15.7 1.7 %collective-permute-start.4 = (bf16[256,512]{1,0:T(8,128)(2,1)S(1)}, bf16[256,512]{1,0:T(8,128)(2,1)S(1)}, u32[]{:S(2)}, u32[]{:S(2)}) collective-permute-start(bf16[256,512]{1,0:T(8,128)(2,1)S(1)} %copy-done.2), channel_id=1, source_target_pairs={{2,0},{0,2},{3,1},{1,3},{6,4},{4,6},{7,5},{5,7},{10,8},{8,10},{11,... | collective-permute-start | bytes 786440 | tf_op jit(solution)/shard_map/ppermute | solution.py:26
  17.4 1.0 %shard_map.160 = (bf16[12,512,128]{2,1,0:T(8,128)(2,1)S(1)}, bf16[12,512,128]{2,1,0:T(8,128)(2,1)S(1)}, bf16[12,16,512]{2,1,0:T(8,128)(2,1)S(1)}, bf16[12,16,512]{2,1,0:T(8,128)(2,1)S(1)}) custom-call(s32[1]{0:T(128)S(6)} %copy.17.tiles, s32[12,512]{1,0:T(8,128)S(1)} %copy-done.6, s32[1,512]{1,0:T(1,128)S(1)} %bitcast.7), custom_call_target="tpu_custom_call" | custom-call | flops 1024 | bytes 1024 | tf_op jit(solution)/shard_map/pallas_call | solution.py:51
  18.5 2.9 %shard_map.161.before = bf16[12,512,256]{2,1,0:T(8,128)(2,1)S(1)} custom-call(bf16[12,512,128]{2,1,0:T(8,128)(2,1)S(1)} %get-tuple-element.91.low, bf16[12,512,128]{2,1,0:T(8,128)(2,1)S(1)} %get-tuple-element.92.high, bf16[512,256]{1,0:T(8,128)(2,1)S(1)} %get-tuple-element.96.proj, bf16[272,256]{1,0:T(8,128)(2,1)S(1)} %collective-permute-done.3.beside.refs_4_), custom_call_target="tpu_custom_call" | custom-call | flops 1024 | bytes 1024 | tf_op jit(solution)/shard_map/pallas_call | solution.py:51
  22.4 1.6 %collective-permute-done.4.refs_1_ = bf16[256,512]{1,0:T(8,128)(2,1)S(1)} collective-permute-done((bf16[256,512]{1,0:T(8,128)(2,1)S(1)}, bf16[256,512]{1,0:T(8,128)(2,1)S(1)}, u32[]{:S(2)}, u32[]{:S(2)}) %collective-permute-start.4) | collective-permute-done | bytes 262176 | tf_op jit(solution)/shard_map/ppermute | solution.py:26
  24.1 1.1 %shard_map.162 = (bf16[512,512]{1,0:T(8,128)(2,1)}, f32[512,512]{1,0:T(8,128)S(1)}, f32[512,512]{1,0:T(8,128)S(1)}) custom-call(s32[1]{0:T(128)S(6)} %copy.17.tiles, bf16[256,512]{1,0:T(8,128)(2,1)S(1)} %copy-done.2, bf16[256,512]{1,0:T(8,128)(2,1)S(1)} %collective-permute-done.4.refs_1_, bf16[512,512]{1,0:T(8,128)(2,1)S(1)} %get-tuple-element.86.feats.refs_2_, ...), custom_call_target="tpu_custom_call" | custom-call | flops 1024 | bytes 1024 | tf_op jit(solution)/shard_map/pallas_call | solution.py:51
  25.2 2.5 %shard_map.163.part = bf16[12,512,256]{2,1,0:T(8,128)(2,1)S(1)} custom-call(bf16[12,512,128]{2,1,0:T(8,128)(2,1)S(1)} %get-tuple-element.91.low, bf16[12,512,128]{2,1,0:T(8,128)(2,1)S(1)} %get-tuple-element.92.high, bf16[12,512,256]{2,1,0:T(8,128)(2,1)S(1)} %shard_map.161.before, bf16[272,256]{1,0:T(8,128)(2,1)S(1)} %collective-permute-done.1.west.refs_2_, ...), custom_call_target="tpu_custom_call" | custom-call | flops 1024 | bytes 1024 | tf_op jit(solution)/shard_map/pallas_call | solution.py:51
  28.4 2.5 %shard_map.165 = (bf16[256,256]{1,0:T(8,128)(2,1)S(1)}, bf16[12,256,256]{2,1,0:T(8,128)(2,1)S(1)}) custom-call(bf16[12,512,128]{2,1,0:T(8,128)(2,1)S(1)} %get-tuple-element.91.low, bf16[12,512,128]{2,1,0:T(8,128)(2,1)S(1)} %get-tuple-element.92.high, f32[512,256]{1,0:T(8,128)S(1)} %shard_map.159.base, s32[1,512]{1,0:T(1,128)S(1)} %bitcast.8, ...), custom_call_target="tpu_custom_call" | custom-call | flops 1024 | bytes 1024 | tf_op jit(solution)/shard_map/pallas_call | solution.py:51
  30.9 1.6 %collective-permute-start.8 = (bf16[256,256]{1,0:T(8,128)(2,1)S(1)}, bf16[256,256]{1,0:T(8,128)(2,1)S(1)}, u32[]{:S(2)}, u32[]{:S(2)}) collective-permute-start(bf16[256,256]{1,0:T(8,128)(2,1)S(1)} %get-tuple-element.109.refs_0_), channel_id=1, source_target_pairs={{2,0},{0,2},{3,1},{1,3},{6,4},{4,6},{7,5},{5,7},{10,8},{8,10},{11,... | collective-permute-start | bytes 393224 | tf_op jit(solution)/shard_map/ppermute | solution.py:26
  32.5 2.5 %shard_map.168 = (bf16[256,256]{1,0:T(8,128)(2,1)S(1)}, bf16[12,256,256]{2,1,0:T(8,128)(2,1)S(1)}) custom-call(bf16[12,512,128]{2,1,0:T(8,128)(2,1)S(1)} %get-tuple-element.91.low, bf16[12,512,128]{2,1,0:T(8,128)(2,1)S(1)} %get-tuple-element.92.high, f32[512,256]{1,0:T(8,128)S(1)} %shard_map.159.base, s32[1,512]{1,0:T(1,128)S(1)} %bitcast.9, ...), custom_call_target="tpu_custom_call" | custom-call | flops 1024 | bytes 1024 | tf_op jit(solution)/shard_map/pallas_call | solution.py:51
  35.5 1.0 %collective-permute-done.8.refs_1_ = bf16[256,256]{1,0:T(8,128)(2,1)S(1)} collective-permute-done((bf16[256,256]{1,0:T(8,128)(2,1)S(1)}, bf16[256,256]{1,0:T(8,128)(2,1)S(1)}, u32[]{:S(2)}, u32[]{:S(2)}) %collective-permute-start.8) | collective-permute-done | bytes 131104 | tf_op jit(solution)/shard_map/ppermute | solution.py:26
  36.5 0.9 %shard_map.166 = (bf16[512,256]{1,0:T(8,128)(2,1)S(1)}, bf16[512,256]{1,0:T(8,128)(2,1)S(1)}, f32[256,256]{1,0:T(8,128)S(1)}) custom-call(s32[1,512]{1,0:T(1,128)S(1)} %bitcast.10, bf16[256,256]{1,0:T(8,128)(2,1)S(1)} %get-tuple-element.109.refs_0_, bf16[256,256]{1,0:T(8,128)(2,1)S(1)} %collective-permute-done.8.refs_1_, bf16[512,512]{1,0:T(8,128)(2,1)S(1)} %copy-done.1, ...), custom_call_target="tpu_custom_call" | custom-call | flops 1024 | bytes 1024 | tf_op jit(solution)/shard_map/pallas_call | solution.py:51
  37.4 1.4 %shard_map.167 = (bf16[12,256,256]{2,1,0:T(8,128)(2,1)S(1)}, f32[768,256]{1,0:T(8,128)S(1)}) custom-call(bf16[12,16,512]{2,1,0:T(8,128)(2,1)S(1)} %get-tuple-element.89.low, bf16[12,16,512]{2,1,0:T(8,128)(2,1)S(1)} %get-tuple-element.90.high, bf16[12,256,256]{2,1,0:T(8,128)(2,1)S(1)} %get-tuple-element.108.slope, f32[256,256]{1,0:T(8,128)S(1)} %get-tuple-element.114.scale), custom_call_target="tpu_custom_call" | custom-call | flops 1024 | bytes 1024 | tf_op jit(solution)/shard_map/pallas_call | solution.py:51
  38.9 1.4 %collective-permute-done.9.refs_1_ = bf16[256,256]{1,0:T(8,128)(2,1)S(1)} collective-permute-done((bf16[256,256]{1,0:T(8,128)(2,1)S(1)}, bf16[256,256]{1,0:T(8,128)(2,1)S(1)}, u32[]{:S(2)}, u32[]{:S(2)}) %collective-permute-start.9) | collective-permute-done | bytes 131104 | tf_op jit(solution)/shard_map/ppermute | solution.py:26
  40.3 0.8 %shard_map.169 = (bf16[512,256]{1,0:T(8,128)(2,1)S(1)}, bf16[512,256]{1,0:T(8,128)(2,1)S(1)}, f32[256,256]{1,0:T(8,128)S(1)}) custom-call(s32[1,512]{1,0:T(1,128)S(1)} %bitcast.11, bf16[256,256]{1,0:T(8,128)(2,1)S(1)} %get-tuple-element.117.refs_0_, bf16[256,256]{1,0:T(8,128)(2,1)S(1)} %collective-permute-done.9.refs_1_, bf16[512,512]{1,0:T(8,128)(2,1)S(1)} %copy-done.1, ...), custom_call_target="tpu_custom_call" | custom-call | flops 1024 | bytes 1024 | tf_op jit(solution)/shard_map/pallas_call | solution.py:51
  41.9 1.0 %shard_map.171 = bf16[2,256,256]{2,1,0:T(8,128)(2,1)S(1)} custom-call(bf16[12,16,512]{2,1,0:T(8,128)(2,1)S(1)} %get-tuple-element.89.low, bf16[12,16,512]{2,1,0:T(8,128)(2,1)S(1)} %get-tuple-element.90.high, bf16[12,256,256]{2,1,0:T(8,128)(2,1)S(1)} %get-tuple-element.120.grads.refs_1_, f32[768,256]{1,0:T(8,128)S(1)} %get-tuple-element.119.before, ...), custom_call_target="tpu_custom_call" | custom-call | flops 1024 | bytes 1024 | tf_op jit(solution)/shard_map/pallas_call | solution.py:51
  43.0 2.6 %shard_map.172 = (bf16[256,256]{1,0:T(8,128)(2,1)S(1)}, bf16[256,256]{1,0:T(8,128)(2,1)S(1)}, bf16[256,256]{1,0:T(8,128)(2,1)S(1)}) custom-call(bf16[12,16,512]{2,1,0:T(8,128)(2,1)S(1)} %get-tuple-element.89.low, bf16[12,16,512]{2,1,0:T(8,128)(2,1)S(1)} %get-tuple-element.90.high, bf16[12,256,256]{2,1,0:T(8,128)(2,1)S(1)} %get-tuple-element.129.refs_0_, ...), custom_call_target="tpu_custom_call" | custom-call | flops 1024 | bytes 1024 | tf_op jit(solution)/shard_map/pallas_call | solution.py:51
  46.2 1.9 %collective-permute-done.10.across = bf16[256,256]{1,0:T(8,128)(2,1)S(1)} collective-permute-done((bf16[256,256]{1,0:T(8,128)(2,1)S(1)}, bf16[256,256]{1,0:T(8,128)(2,1)S(1)}, u32[]{:S(2)}, u32[]{:S(2)}) %collective-permute-start.10) | collective-permute-done | bytes 131104 | tf_op jit(solution)/shard_map/ppermute | solution.py:558
  48.2 1.5 %collective-permute-start.13 = (bf16[256,256]{1,0:T(8,128)(2,1)S(1)}, bf16[256,256]{1,0:T(8,128)(2,1)S(1)}, u32[]{:S(2)}, u32[]{:S(2)}) collective-permute-start(bf16[256,256]{1,0:T(8,128)(2,1)S(1)} %get-tuple-element.128), channel_id=1, source_target_pairs={{4,0},{8,4},{12,8},{0,12},{5,1},{9,5},{13,9},{1,13},{6,2},{10,6},{... | collective-permute-start | bytes 393224 | tf_op jit(solution)/shard_map/ppermute | solution.py:26
  50.3 2.1 %shard_map.175 = (f32[512,256]{1,0:T(8,128)S(1)}, bf16[256,512]{1,0:T(8,128)(2,1)S(1)}) custom-call(bf16[12,16,512]{2,1,0:T(8,128)(2,1)S(1)} %get-tuple-element.89.low, bf16[12,16,512]{2,1,0:T(8,128)(2,1)S(1)} %get-tuple-element.90.high, bf16[12,256,256]{2,1,0:T(8,128)(2,1)S(1)} %get-tuple-element.129.refs_0_, ...), custom_call_target="tpu_custom_call" | custom-call | flops 1024 | bytes 1024 | tf_op jit(solution)/shard_map/pallas_call | solution.py:51
  52.3 1.2 %shard_map.176 = (bf16[256,512]{1,0:T(8,128)(2,1)}, f32[256,512]{1,0:T(8,128)S(1)}) custom-call(s32[1]{0:T(128)S(6)} %copy.17.tiles, bf16[256,512]{1,0:T(8,128)(2,1)S(1)} %get-tuple-element.82.refs_0_.feats, bf16[256,512]{1,0:T(8,128)(2,1)S(1)} %copy-done.2, bf16[256,512]{1,0:T(8,128)(2,1)S(1)} %get-tuple-element.83.w_out, bf16[256,512]{1,0:T(8,128)(2,1)S(1)} %copy-done.4, ...), custom_call_target="tpu_custom_call" | custom-call | flops 1024 | bytes 1024 | tf_op jit(solution)/shard_map/pallas_call | solution.py:51
  55.0 2.1 %collective-permute-done.14.refs_0_ = bf16[256,256]{1,0:T(8,128)(2,1)S(1)} collective-permute-done((bf16[256,256]{1,0:T(8,128)(2,1)S(1)}, bf16[256,256]{1,0:T(8,128)(2,1)S(1)}, u32[]{:S(2)}, u32[]{:S(2)}) %collective-permute-start.14) | collective-permute-done | bytes 131104 | tf_op jit(solution)/shard_map/ppermute | solution.py:26
  58.7 0.7 %collective-permute-done.17.refs_1_ = bf16[256,256]{1,0:T(8,128)(2,1)S(1)} collective-permute-done((bf16[256,256]{1,0:T(8,128)(2,1)S(1)}, bf16[256,256]{1,0:T(8,128)(2,1)S(1)}, u32[]{:S(2)}, u32[]{:S(2)}) %collective-permute-start.17) | collective-permute-done | bytes 131104 | tf_op jit(solution)/shard_map/ppermute | solution.py:26
  59.5 1.2 %collective-permute-start.18 = (bf16[2,64,256]{2,1,0:T(8,128)(2,1)S(1)}, bf16[2,64,256]{2,1,0:T(8,128)(2,1)S(1)}, u32[]{:S(2)}, u32[]{:S(2)}) collective-permute-start(bf16[2,64,256]{2,1,0:T(8,128)(2,1)S(1)} %get-tuple-element.158), channel_id=1, source_target_pairs={{0,8},{4,12},{8,0},{12,4},{1,9},{5,13},{9,1},{13,5},{2,10},{6,14},... | collective-permute-start | bytes 196616 | tf_op jit(solution)/shard_map/ppermute | solution.py:810
  60.6 4.2 %collective-permute-done.18.received = bf16[2,64,256]{2,1,0:T(8,128)(2,1)S(1)} collective-permute-done((bf16[2,64,256]{2,1,0:T(8,128)(2,1)S(1)}, bf16[2,64,256]{2,1,0:T(8,128)(2,1)S(1)}, u32[]{:S(2)}, u32[]{:S(2)}) %collective-permute-start.18) | collective-permute-done | bytes 65568 | tf_op jit(solution)/shard_map/ppermute | solution.py:810
  64.8 2.1 %collective-permute-start.19 = (bf16[1,64,256]{2,1,0:T(8,128)(2,1)S(1)}, bf16[1,64,256]{2,1,0:T(8,128)(2,1)S(1)}, u32[]{:S(2)}, u32[]{:S(2)}) collective-permute-start(bf16[1,64,256]{2,1,0:T(8,128)(2,1)S(1)} %get-tuple-element.160), channel_id=1, source_target_pairs={{0,4},{4,0},{8,12},{12,8},{1,5},{5,1},{9,13},{13,9},{2,6},{6,2},{1... | collective-permute-start | bytes 98312 | tf_op jit(solution)/shard_map/ppermute | solution.py:810
  67.7 1.2 %collective-permute-done.19.received = bf16[1,64,256]{2,1,0:T(8,128)(2,1)S(1)} collective-permute-done((bf16[1,64,256]{2,1,0:T(8,128)(2,1)S(1)}, bf16[1,64,256]{2,1,0:T(8,128)(2,1)S(1)}, u32[]{:S(2)}, u32[]{:S(2)}) %collective-permute-start.19) | collective-permute-done | bytes 32800 | tf_op jit(solution)/shard_map/ppermute | solution.py:810
  (57 shorter events, 9.6 us)
Async XLA Ops:
  0.6 9.5 %copy-start.9 = (s32[1,6,2]{1,2,0:T(2,128)S(1)}, s32[1,6,2]{1,2,0:T(2,128)}, u32[]{:S(2)}) copy-start(s32[1,6,2]{1,2,0:T(2,128)} %param.19) | copy-start | bytes 148
  0.6 14.7 %copy-start.7 = (f32[512]{0:T(512)S(1)}, f32[512]{0:T(512)}, u32[]{:S(2)}) copy-start(f32[512]{0:T(512)} %param.22) | copy-start | bytes 6148
  0.7 9.5 %collective-permute-start = (bf16[256,512]{1,0:T(8,128)(2,1)}, bf16[256,512]{1,0:T(8,128)(2,1)S(1)}, u32[]{:S(2)}, u32[]{:S(2)}) collective-permute-start(bf16[256,512]{1,0:T(8,128)(2,1)} %refs_2_.1), channel_id=1, source_target_pairs={{2,0},{0,2},{3,1},{1,3},{6,4},{4,6},{7,5},{5,7},{10,8},{8,10},{11,... | collective-permute-start | bytes 786440 | tf_op jit(solution)/shard_map/ppermute | solution.py:26
  6.9 8.8 %copy-start.2 = (bf16[256,512]{1,0:T(8,128)(2,1)S(1)}, bf16[256,512]{1,0:T(8,128)(2,1)}, u32[]{:S(2)}) copy-start(bf16[256,512]{1,0:T(8,128)(2,1)} %cots.1) | copy-start | bytes 786436
  6.9 10.5 %copy-start.5 = (s32[512]{0:T(512)S(1)}, s32[512]{0:T(512)}, u32[]{:S(2)}) copy-start(s32[512]{0:T(512)} %param.17) | copy-start | bytes 6148
  7.0 10.5 %copy-start.6 = (s32[12,512]{1,0:T(8,128)S(1)}, s32[12,512]{1,0:T(8,128)}, u32[]{:S(2)}) copy-start(s32[12,512]{1,0:T(8,128)} %senders) | copy-start | bytes 73732
  11.3 7.2 %collective-permute-start.3 = (bf16[272,256]{1,0:T(8,128)(2,1)S(1)}, bf16[272,256]{1,0:T(8,128)(2,1)S(1)}, u32[]{:S(2)}, u32[]{:S(2)}) collective-permute-start(bf16[272,256]{1,0:T(8,128)(2,1)S(1)} %get-tuple-element.97), channel_id=1, source_target_pairs={{1,0},{0,1},{3,2},{2,3},{5,4},{4,5},{7,6},{6,7},{9,8},{8,9},{11,10... | collective-permute-start | bytes 417800 | tf_op jit(solution)/shard_map/ppermute | solution.py:26
  11.3 10.1 %collective-permute-start.1 = (bf16[272,256]{1,0:T(8,128)(2,1)S(1)}, bf16[272,256]{1,0:T(8,128)(2,1)S(1)}, u32[]{:S(2)}, u32[]{:S(2)}) collective-permute-start(bf16[272,256]{1,0:T(8,128)(2,1)S(1)} %get-tuple-element.94), channel_id=1, source_target_pairs={{12,0},{0,4},{4,8},{8,12},{13,1},{1,5},{5,9},{9,13},{14,2},{2,6},{... | collective-permute-start | bytes 417800 | tf_op jit(solution)/shard_map/ppermute | solution.py:26
  13.2 8.7 %collective-permute-start.2 = (bf16[272,256]{1,0:T(8,128)(2,1)S(1)}, bf16[272,256]{1,0:T(8,128)(2,1)S(1)}, u32[]{:S(2)}, u32[]{:S(2)}) collective-permute-start(bf16[272,256]{1,0:T(8,128)(2,1)S(1)} %get-tuple-element.95), channel_id=1, source_target_pairs={{4,0},{8,4},{12,8},{0,12},{5,1},{9,5},{13,9},{1,13},{6,2},{10,6},{... | collective-permute-start | bytes 417800 | tf_op jit(solution)/shard_map/ppermute | solution.py:26
  15.7 8.4 %collective-permute-start.4 = (bf16[256,512]{1,0:T(8,128)(2,1)S(1)}, bf16[256,512]{1,0:T(8,128)(2,1)S(1)}, u32[]{:S(2)}, u32[]{:S(2)}) collective-permute-start(bf16[256,512]{1,0:T(8,128)(2,1)S(1)} %copy-done.2), channel_id=1, source_target_pairs={{2,0},{0,2},{3,1},{1,3},{6,4},{4,6},{7,5},{5,7},{10,8},{8,10},{11,... | collective-permute-start | bytes 786440 | tf_op jit(solution)/shard_map/ppermute | solution.py:26
  17.4 11.0 %collective-permute-start.5 = (bf16[272,256]{1,0:T(8,128)(2,1)S(1)}, bf16[272,256]{1,0:T(8,128)(2,1)S(1)}, u32[]{:S(2)}, u32[]{:S(2)}) collective-permute-start(bf16[272,256]{1,0:T(8,128)(2,1)S(1)} %get-tuple-element.105), channel_id=1, source_target_pairs={{0,9},{1,8},{4,13},{5,12},{8,1},{9,0},{12,5},{13,4},{2,11},{3,10},... | collective-permute-start | bytes 417800 | tf_op jit(solution)/shard_map/ppermute | solution.py:614
  18.5 5.6 %copy-start = (bf16[512,512]{1,0:T(8,128)(2,1)S(1)}, bf16[512,512]{1,0:T(8,128)(2,1)}, u32[]{:S(2)}) copy-start(bf16[512,512]{1,0:T(8,128)(2,1)} %refs_3_.3) | copy-start | bytes 1572868
  18.5 5.6 %copy-start.3 = (bf16[512,512]{1,0:T(8,128)(2,1)S(1)}, bf16[512,512]{1,0:T(8,128)(2,1)}, u32[]{:S(2)}) copy-start(bf16[512,512]{1,0:T(8,128)(2,1)} %get-tuple-element.100.refs_5_) | copy-start | bytes 1572868
  18.5 5.6 %copy-start.8 = (f32[512]{0:T(512)S(1)}, f32[512]{0:T(512)}, u32[]{:S(2)}) copy-start(f32[512]{0:T(512)} %param.26) | copy-start | bytes 6148
  21.9 6.5 %collective-permute-start.6 = (bf16[272,256]{1,0:T(8,128)(2,1)S(1)}, bf16[272,256]{1,0:T(8,128)(2,1)S(1)}, u32[]{:S(2)}, u32[]{:S(2)}) collective-permute-start(bf16[272,256]{1,0:T(8,128)(2,1)S(1)} %collective-permute-done.1.west.refs_2_), channel_id=1, source_target_pairs={{1,0},{0,1},{3,2},{2,3},{5,4},{4,5},{7,6},{6,7},{9,8},{8,9},{11,10... | collective-permute-start | bytes 417800 | tf_op jit(solution)/shard_map/ppermute | solution.py:26
  22.4 6.1 %collective-permute-start.7 = (bf16[272,256]{1,0:T(8,128)(2,1)S(1)}, bf16[272,256]{1,0:T(8,128)(2,1)S(1)}, u32[]{:S(2)}, u32[]{:S(2)}) collective-permute-start(bf16[272,256]{1,0:T(8,128)(2,1)S(1)} %collective-permute-done.2.east.refs_3_), channel_id=1, source_target_pairs={{1,0},{0,1},{3,2},{2,3},{5,4},{4,5},{7,6},{6,7},{9,8},{8,9},{11,10... | collective-permute-start | bytes 417800 | tf_op jit(solution)/shard_map/ppermute | solution.py:26
  30.9 5.6 %copy-start.1 = (bf16[512,512]{1,0:T(8,128)(2,1)S(1)}, bf16[512,512]{1,0:T(8,128)(2,1)}, u32[]{:S(2)}) copy-start(bf16[512,512]{1,0:T(8,128)(2,1)} %get-tuple-element.110.refs_2_) | copy-start | bytes 1572868
  30.9 5.6 %collective-permute-start.8 = (bf16[256,256]{1,0:T(8,128)(2,1)S(1)}, bf16[256,256]{1,0:T(8,128)(2,1)S(1)}, u32[]{:S(2)}, u32[]{:S(2)}) collective-permute-start(bf16[256,256]{1,0:T(8,128)(2,1)S(1)} %get-tuple-element.109.refs_0_), channel_id=1, source_target_pairs={{2,0},{0,2},{3,1},{1,3},{6,4},{4,6},{7,5},{5,7},{10,8},{8,10},{11,... | collective-permute-start | bytes 393224 | tf_op jit(solution)/shard_map/ppermute | solution.py:26
  34.9 5.3 %collective-permute-start.9 = (bf16[256,256]{1,0:T(8,128)(2,1)S(1)}, bf16[256,256]{1,0:T(8,128)(2,1)S(1)}, u32[]{:S(2)}, u32[]{:S(2)}) collective-permute-start(bf16[256,256]{1,0:T(8,128)(2,1)S(1)} %get-tuple-element.117.refs_0_), channel_id=1, source_target_pairs={{2,0},{0,2},{3,1},{1,3},{6,4},{4,6},{7,5},{5,7},{10,8},{8,10},{11,... | collective-permute-start | bytes 393224 | tf_op jit(solution)/shard_map/ppermute | solution.py:26
  41.7 6.3 %collective-permute-start.10 = (bf16[256,256]{1,0:T(8,128)(2,1)S(1)}, bf16[256,256]{1,0:T(8,128)(2,1)S(1)}, u32[]{:S(2)}, u32[]{:S(2)}) collective-permute-start(bf16[256,256]{1,0:T(8,128)(2,1)S(1)} %get-tuple-element.124), channel_id=1, source_target_pairs={{0,13},{1,4},{4,1},{5,8},{8,5},{9,12},{12,9},{13,0},{2,15},{3,6},{... | collective-permute-start | bytes 393224 | tf_op jit(solution)/shard_map/ppermute | solution.py:558
  42.9 5.2 %collective-permute-start.11 = (bf16[2,256,256]{2,1,0:T(8,128)(2,1)S(1)}, bf16[2,256,256]{2,1,0:T(8,128)(2,1)S(1)}, u32[]{:S(2)}, u32[]{:S(2)}) collective-permute-start(bf16[2,256,256]{2,1,0:T(8,128)(2,1)S(1)} %shard_map.171), channel_id=1, source_target_pairs={{1,0},{0,1},{3,2},{2,3},{5,4},{4,5},{7,6},{6,7},{9,8},{8,9},{11,10... | collective-permute-start | bytes 786440 | tf_op jit(solution)/shard_map/ppermute | solution.py:26
  45.6 7.9 %collective-permute-start.12 = (bf16[256,256]{1,0:T(8,128)(2,1)S(1)}, bf16[256,256]{1,0:T(8,128)(2,1)S(1)}, u32[]{:S(2)}, u32[]{:S(2)}) collective-permute-start(bf16[256,256]{1,0:T(8,128)(2,1)S(1)} %get-tuple-element.138), channel_id=1, source_target_pairs={{1,0},{0,1},{3,2},{2,3},{5,4},{4,5},{7,6},{6,7},{9,8},{8,9},{11,10... | collective-permute-start | bytes 393224 | tf_op jit(solution)/shard_map/ppermute | solution.py:26
  48.2 5.4 %collective-permute-start.13 = (bf16[256,256]{1,0:T(8,128)(2,1)S(1)}, bf16[256,256]{1,0:T(8,128)(2,1)S(1)}, u32[]{:S(2)}, u32[]{:S(2)}) collective-permute-start(bf16[256,256]{1,0:T(8,128)(2,1)S(1)} %get-tuple-element.128), channel_id=1, source_target_pairs={{4,0},{8,4},{12,8},{0,12},{5,1},{9,5},{13,9},{1,13},{6,2},{10,6},{... | collective-permute-start | bytes 393224 | tf_op jit(solution)/shard_map/ppermute | solution.py:26
  49.7 2.6 %copy-start.4 = (bf16[256,512]{1,0:T(8,128)(2,1)S(1)}, bf16[256,512]{1,0:T(8,128)(2,1)}, u32[]{:S(2)}) copy-start(bf16[256,512]{1,0:T(8,128)(2,1)} %get-tuple-element.84.w_node_v_t) | copy-start | bytes 786436
  49.7 7.4 %collective-permute-start.14 = (bf16[256,256]{1,0:T(8,128)(2,1)S(1)}, bf16[256,256]{1,0:T(8,128)(2,1)S(1)}, u32[]{:S(2)}, u32[]{:S(2)}) collective-permute-start(bf16[256,256]{1,0:T(8,128)(2,1)S(1)} %get-tuple-element.139), channel_id=1, source_target_pairs={{12,0},{0,4},{4,8},{8,12},{13,1},{1,5},{5,9},{9,13},{14,2},{2,6},{... | collective-permute-start | bytes 393224 | tf_op jit(solution)/shard_map/ppermute | solution.py:26
  54.3 5.1 %collective-permute-start.17 = (bf16[256,256]{1,0:T(8,128)(2,1)S(1)}, bf16[256,256]{1,0:T(8,128)(2,1)S(1)}, u32[]{:S(2)}, u32[]{:S(2)}) collective-permute-start(bf16[256,256]{1,0:T(8,128)(2,1)S(1)} %bitcast.16), channel_id=1, source_target_pairs={{2,0},{0,2},{3,1},{1,3},{6,4},{4,6},{7,5},{5,7},{10,8},{8,10},{11,... | collective-permute-start | bytes 393224 | tf_op jit(solution)/shard_map/ppermute | solution.py:26
  57.5 1.9 %collective-permute-start.16 = (bf16[4,64,256]{2,1,0:T(8,128)(2,1)S(1)}, bf16[4,64,256]{2,1,0:T(8,128)(2,1)S(1)}, u32[]{:S(2)}, u32[]{:S(2)}) collective-permute-start(bf16[4,64,256]{2,1,0:T(8,128)(2,1)S(1)} %get-tuple-element.151), channel_id=1, source_target_pairs={{1,0},{0,1},{3,2},{2,3},{5,4},{4,5},{7,6},{6,7},{9,8},{8,9},{11,10... | collective-permute-start | bytes 393224 | tf_op jit(solution)/shard_map/ppermute | solution.py:26
  58.0 8.9 %collective-permute-start.15 = (bf16[256,256]{1,0:T(8,128)(2,1)S(1)}, bf16[256,256]{1,0:T(8,128)(2,1)S(1)}, u32[]{:S(2)}, u32[]{:S(2)}) collective-permute-start(bf16[256,256]{1,0:T(8,128)(2,1)S(1)} %bitcast.15), channel_id=1, source_target_pairs={{2,0},{0,2},{3,1},{1,3},{6,4},{4,6},{7,5},{5,7},{10,8},{8,10},{11,... | collective-permute-start | bytes 393224 | tf_op jit(solution)/shard_map/ppermute | solution.py:26
  59.5 5.3 %collective-permute-start.18 = (bf16[2,64,256]{2,1,0:T(8,128)(2,1)S(1)}, bf16[2,64,256]{2,1,0:T(8,128)(2,1)S(1)}, u32[]{:S(2)}, u32[]{:S(2)}) collective-permute-start(bf16[2,64,256]{2,1,0:T(8,128)(2,1)S(1)} %get-tuple-element.158), channel_id=1, source_target_pairs={{0,8},{4,12},{8,0},{12,4},{1,9},{5,13},{9,1},{13,5},{2,10},{6,14},... | collective-permute-start | bytes 196616 | tf_op jit(solution)/shard_map/ppermute | solution.py:810
  64.8 4.0 %collective-permute-start.19 = (bf16[1,64,256]{2,1,0:T(8,128)(2,1)S(1)}, bf16[1,64,256]{2,1,0:T(8,128)(2,1)S(1)}, u32[]{:S(2)}, u32[]{:S(2)}) collective-permute-start(bf16[1,64,256]{2,1,0:T(8,128)(2,1)S(1)} %get-tuple-element.160), channel_id=1, source_target_pairs={{0,4},{4,0},{8,12},{12,8},{1,5},{5,1},{9,13},{13,9},{2,6},{6,2},{1... | collective-permute-start | bytes 98312 | tf_op jit(solution)/shard_map/ppermute | solution.py:810

commit v10 on v9

--- a/solution.py
+++ b/solution.py
@@ -14,6 +14,7 @@
 PACK = 16
 MIB = 1 << 20
 WEIGHTS_LIMIT = 52
+LINE_FLOPS = 10**9
 NO_CHUNK = 64
 SLOT_OF = ((3, 0), (1, 1), (4, 4), (2, 5), (0, 2), (5, 3))
 EARLY, LATE = (3, 4, 5), (1, 2, 0)
@@ -74,15 +75,15 @@
 
 
 def weights_kernel(*refs):
-    sources, refs = refs[:7], refs[7:]
-    w_send, w_recv, w_out, feats, w_send_t, w_recv_t, w_both_t, w_node_v_t, w_both, w_out_t = refs[:10]
-    w_msg, w_node_v, w_node_a, w_out_all, turned, sems = refs[10:]
+    sources, refs = refs[:6], refs[6:]
+    w_send, w_recv, w_out, w_send_t, w_recv_t, w_both_t, w_node_v_t, w_both, w_out_t = refs[:9]
+    w_msg, w_node_v, w_node_a, w_out_all, turned, sems = refs[9:]
     mine = lax.axis_index("ch")
     hid = w_send.shape[0]
-    targets = (w_msg, w_node_a, feats, w_send, w_recv, w_node_v, w_out_all)
+    targets = (w_msg, w_node_a, w_send, w_recv, w_node_v, w_out_all)
     copies = []
     for k, (source, target) in enumerate(zip(sources, targets)):
-        if k in (3, 4):
+        if k in (2, 3):
             source = source.at[pl.ds(pl.multiple_of(mine * hid, hid), hid), :]
         copies.append(pltpu.make_async_copy(source, target, sems.at[k]))
     for copy in copies:
@@ -127,27 +128,40 @@
             out[m] = spread[:, m * LANES : (m + 1) * LANES]
 
 
-def project_kernel(count, tiles, picks, *refs):
+def put_marks(picks, start, lift, out):
+    _, per_slot, slots = picks.shape
+    hid = out.shape[1]
+    spot = lax.broadcasted_iota(jnp.int32, (PACK, hid), 0)
+    marks = jnp.zeros((PACK, hid), jnp.float32)
+    for k in range(slots // 2 * per_slot):
+        rel = picks[0, k % per_slot, start + k // per_slot] - lift
+        marks = jnp.where(spot == k, rel.astype(jnp.float32), marks)
+    out[out.shape[0] - PACK :, :] = marks.astype(jnp.bfloat16)
+
+
+def project_half(blocks, w_send, feats, proj):
+    assemble(feats, blocks, lax.axis_index("ch"))
+    proj[...] = (0.5 * dot(w_send[...], feats[...]).T).astype(jnp.bfloat16)
+
+
+def lower_kernel(count, picks, *refs):
+    blocks, (w_send, feats, proj, lower) = refs[:count], refs[count:]
+    project_half(blocks, w_send, feats, proj)
+    lower[: proj.shape[0], :] = proj[...]
+    put_marks(picks, picks.shape[2] // 2, 0, lower)
+
+
+def upper_kernel(count, tiles, picks, *refs):
     blocks = refs[:count]
-    w_send, feats, proj, upper, lower, beside, cross = refs[count:]
-    mine, sub = lax.axis_index("ch"), lax.axis_index("sub")
+    w_send, below, lower, feats, proj, upper, beside, cross, both = refs[count:]
+    sub = lax.axis_index("sub")
     first = tiles[0] // 2
-    assemble(feats, blocks, mine)
-    whole = feats[...]
-    hid = proj.shape[1]
-    proj[...] = (0.5 * dot(w_send[...], whole).T).astype(jnp.bfloat16)
-    rows = upper.shape[0] - PACK
-    upper[:rows, :] = proj[pl.ds(pl.multiple_of(first * TILE, TILE), rows), :]
-    lower[:rows, :] = proj[:rows, :]
-    spot = lax.broadcasted_iota(jnp.int32, (PACK, hid), 0)
-    _, per_slot, slots = picks.shape
-    half = slots // 2
-    for start, out, lift in ((0, upper, first), (half, lower, 0)):
-        marks = jnp.zeros((PACK, hid), jnp.float32)
-        for k in range(half * per_slot):
-            rel = picks[0, k % per_slot, start + k // per_slot] - lift
-            marks = jnp.where(spot == k, rel.astype(jnp.float32), marks)
-        out[rows:, :] = marks.astype(jnp.bfloat16)
+    project_half(blocks, w_send, feats, proj)
+    rows = proj.shape[0]
+    both[:rows, :] = below[...]
+    both[rows:, :] = proj[...]
+    upper[:rows, :] = both[pl.ds(pl.multiple_of(first * TILE, TILE), rows), :]
+    put_marks(picks, 0, first, upper)
 
     @pl.when(sub == 0)
     def _():
@@ -160,22 +174,26 @@
         cross[...] = upper[...]
 
 
-def receive_kernel(bias, feats, w_recv, base):
+def receive_kernel(bias, below, above, w_recv, base):
     hid = base.shape[1]
     mine = lax.axis_index("ch")
     my_bias = jnp.zeros((1, hid), jnp.float32)
     for k in range(bias.shape[1] // hid):
         my_bias += jnp.where(mine == k, bias[:, k * hid : (k + 1) * hid], 0.0)
-    recv = dot(w_recv[...], feats[...]).T
-    base[...] = 0.5 * (recv.astype(jnp.bfloat16).astype(jnp.float32) + my_bias)
+    rows = below.shape[1]
+    for k, feats in enumerate((below, above)):
+        recv = dot(w_recv[...], feats[...]).T.astype(jnp.bfloat16).astype(jnp.float32)
+        base[k * rows : (k + 1) * rows, :] = 0.5 * (recv + my_bias)
 
 
 def prepare_kernel(count, tiles, *refs):
     blocks = refs[:count]
-    feats, w_node_v, bias, w_out_t, cots, pre, grad_hidden = refs[count:]
+    below, above, w_node_v, bias, w_out_t, cots, pre, grad_hidden = refs[count:]
     assemble(cots, blocks, lax.axis_index("ch"))
     column = jnp.broadcast_to(bias[...], (8, bias.shape[1])).T[:, :1]
-    pre[...] = dot(w_node_v[...], feats[...]) + column
+    rows = below.shape[1]
+    pre[:, :rows] = dot(w_node_v[...], below[...]) + column
+    pre[:, rows:] = dot(w_node_v[...], above[...]) + column
     lane = lax.broadcasted_iota(jnp.int32, (1, cots.shape[1]), 1)
     active = (lane < tiles[0] * TILE).astype(jnp.bfloat16)
     grad_hidden[...] = dot(w_out_t[...], cots[...] * active)
@@ -224,31 +242,34 @@
     return dot(picker, ext[...])
 
 
-def near_kernel(low, high, proj, beside, part, ext):
-    own = proj.shape[0]
-    ext[:own, :] = proj[...]
+def near_kernel(low, high, before, below, above, beside, part, ext):
+    rows = below.shape[0]
+    own = 2 * rows
+    ext[:rows, :] = below[...]
+    ext[rows:own, :] = above[...]
     fill(ext, own, beside, 0)
     first = own // CHUNK
     chunks = [jnp.bfloat16(chunk) for chunk in range(first)]
     chunks.append(chunk_of(0, first, low.shape[1:]))
 
     def step(m, carry):
-        part[m] = pick_rows(low[m], high[m], chunks, ext).astype(jnp.bfloat16)
-        return carry
-
-    lax.fori_loop(0, low.shape[0], step, 0, unroll=True)
-
-
-def line_kernel(low, high, before, west, east, part, ext):
-    first = low.shape[1] // CHUNK
-    chunks = []
-    for index, (place, block) in enumerate(((1, west), (2, east))):
-        fill(ext, index * CHUNK, block, place)
-        chunks.append(jnp.bfloat16(first + SLOT_OF[place][0]))
-
-    def step(m, carry):
         more = pick_rows(low[m], high[m], chunks, ext)
         part[m] = (before[m].astype(jnp.float32) + more).astype(jnp.bfloat16)
+        return carry
+
+    lax.fori_loop(0, low.shape[0], step, 0, unroll=True)
+
+
+def line_kernel(place, low, high, block, *refs):
+    *before, part, ext = refs
+    fill(ext, 0, block, place)
+    chunks = [jnp.bfloat16(low.shape[1] // CHUNK + SLOT_OF[place][0])]
+
+    def step(m, carry):
+        rows = pick_rows(low[m], high[m], chunks, ext)
+        for ref in before:
+            rows += ref[m].astype(jnp.float32)
+        part[m] = rows.astype(jnp.bfloat16)
         return carry
 
     lax.fori_loop(0, low.shape[0], step, 0, unroll=True)
@@ -457,7 +478,15 @@
     east[...] = (right[...] + more[1].astype(jnp.float32)).astype(jnp.bfloat16)
 
 
-def back_kernel(start, inv_root, tiles, own, beside, feats, upper, *refs):
+def band_bits(place, lons):
+    bits, weight = 0, 1
+    while weight < lons:
+        bits += weight if place * weight * 2 // lons % 2 else 0
+        weight *= 2
+    return bits
+
+
+def back_kernel(start, inv_root, tiles, feats, own, beside, upper, *refs):
     *refs, total = refs
     sub = lax.axis_index("sub")
     offset = pl.multiple_of(tiles[0] // 2 * TILE, TILE)
@@ -473,7 +502,7 @@
         total[: block.shape[0], :] += block
     rows = grad_send.shape[0]
     grad_send[...] = total[start : start + rows, :].astype(jnp.bfloat16)
-    terms = dot(feats[:, start : start + rows], grad_send[...])
+    terms = dot(feats[...], grad_send[...])
     if start:
         weight[...] = terms
         return
@@ -481,7 +510,7 @@
     lon = lax.axis_index("lon")
     lons, columns, _ = w_mine.shape
     for k in range(lons):
-        band = (lon ^ k) * 2
+        band = (lon ^ band_bits(k, lons)) * 2
         for out, core in ((w_mine, sub), (w_beside, 1 - sub)):
             spot = pl.multiple_of((band + core) * columns, columns)
             out[k] = weight[pl.ds(spot, columns), :].astype(out.dtype)
@@ -560,14 +589,15 @@
     picks = jnp.transpose(send_tiles, (0, 2, 1))
     sub = lax.axis_index("sub")
 
-    feat_blocks = gathered(features, "ch")
+    halves = 2
+    rows = nodes // halves
+    below_blocks = gathered(features[:, :rows], "ch")
 
     whole_w = pltpu.VMEM((chans_all, hidden_all), bf16)
     (
         w_send_my,
         w_recv_my,
         w_out_my,
-        features_held,
         w_send_t,
         w_recv_t,
         w_both_t,
@@ -580,7 +610,6 @@
             shape((hid, chans_all), bf16),
             shape((hid, chans_all), bf16),
             shape((chans, hidden_all), bf16),
-            shape((chans, nodes), bf16),
             shape((chans_all, hid), bf16),
             shape((chans_all, hid), bf16),
             shape((hid, hidden_all), bf16),
@@ -588,39 +617,24 @@
             shape((hidden_all, hidden_all), bf16),
             shape((hidden_all, chans_all), bf16),
         ),
-        [w_msg, w_node_a, features, w_send, w_recv, w_node_v, w_out],
-        away=7,
+        [w_msg, w_node_a, w_send, w_recv, w_node_v, w_out],
+        away=6,
         scalars=0,
-        scratch=[whole_w] * 5 + [pltpu.SemaphoreType.DMA((7,))],
+        scratch=[whole_w] * 5 + [pltpu.SemaphoreType.DMA((6,))],
         limit=WEIGHTS_LIMIT,
     )
-    feat_blocks[0] = features_held
-
     block = shape((slot_rows + PACK, hid), bf16)
-    feats, proj, upper, lower, beside, cross = call(
-        functools.partial(project_kernel, count),
-        (
-            shape((chans_all, nodes), bf16),
-            shape((nodes, hid), bf16),
-            block,
-            block,
-            block,
-            block,
-        ),
-        [tile_count, picks] + feat_blocks + [w_send_my],
-    )
-    west = shifted(upper, "lon", 1)
+    w_send_my, above = lax.optimization_barrier((w_send_my, features[:, rows:]))
+    above_blocks = gathered(above, "ch")
+    feat_shape, proj_shape = shape((chans_all, rows), bf16), shape((rows, hid), bf16)
+    feats_below, proj_below, lower = call(
+        functools.partial(lower_kernel, count),
+        (feat_shape, proj_shape, block),
+        [picks] + below_blocks + [w_send_my],
+        scalars=1,
+    )
     east = shifted(lower, "lon", -1)
-    cross = lax.ppermute(cross, cycle, far_route)
-    base = call(
-        receive_kernel,
-        shape((nodes, hid), f32),
-        [bias_edge[None, :], feats, w_recv_my],
-        scalars=0,
-    )
-    base, senders, cotangent_late = lax.optimization_barrier((base, senders, cotangent))
-    beside = shifted(beside, "sub", 1)
-    cot_blocks = gathered(cotangent_late, "ch")
+    proj_below, senders = lax.optimization_barrier((proj_below, senders))
     low_cols, high_cols, low_rows, high_rows = call(
         edges_kernel,
         (
@@ -632,6 +646,24 @@
         [tile_count, senders, degrees],
         scalars=1,
     )
+    above_blocks[-1], low_cols = lax.optimization_barrier((above_blocks[-1], low_cols))
+    feats_above, proj_above, upper, beside, cross = call(
+        functools.partial(upper_kernel, count),
+        (feat_shape, proj_shape, block, block, block),
+        [tile_count, picks] + above_blocks + [w_send_my, proj_below, lower],
+        scratch=[pltpu.VMEM((nodes, hid), bf16)],
+    )
+    west = shifted(upper, "lon", 1)
+    cross = lax.ppermute(cross, cycle, far_route)
+    base = call(
+        receive_kernel,
+        shape((nodes, hid), f32),
+        [bias_edge[None, :], feats_below, feats_above, w_recv_my],
+        scalars=0,
+    )
+    base, cotangent_late = lax.optimization_barrier((base, cotangent))
+    beside = shifted(beside, "sub", 1)
+    cot_blocks = gathered(cotangent_late, "ch")
     cots, pre, grad_hidden = call(
         functools.partial(prepare_kernel, count),
         (
@@ -639,35 +671,39 @@
             shape((hidden_all, nodes), f32),
             shape((hidden_all, nodes), f32),
         ),
-        [tile_count] + cot_blocks + [feats, w_node_v, bias_node[None, :], w_out_t],
+        [tile_count] + cot_blocks + [feats_below, feats_above, w_node_v, bias_node[None, :], w_out_t],
         scalars=1,
     )
 
     part_shape = shape((degree, nodes, hid), bf16)
+    def line(block, place, before, flops=1024):
+        return call(
+            functools.partial(line_kernel, place),
+            part_shape,
+            [low_cols, high_cols, block] + before,
+            scratch=[pltpu.VMEM((slot_rows, hid), bf16)],
+            scalars=0,
+            flops=flops,
+        )
+
+    east_too = shifted(east, "sub", 1)
+    part = line(east, 2, [], LINE_FLOPS)
+    part, beside = lax.optimization_barrier((part, beside))
     part = call(
         near_kernel,
         part_shape,
-        [low_cols, high_cols, proj, beside],
+        [low_cols, high_cols, part, proj_below, proj_above, beside],
         scratch=[pltpu.VMEM((nodes + slot_rows, hid), bf16)],
         scalars=0,
     )
-    west, east, part = lax.optimization_barrier((west, east, part))
+    west, part = lax.optimization_barrier((west, part))
     west_too = shifted(west, "sub", 1)
-    east_too = shifted(east, "sub", 1)
     part, pre = lax.optimization_barrier((part, pre))
-    part = call(
-        line_kernel,
-        part_shape,
-        [low_cols, high_cols, part, west, east],
-        scratch=[pltpu.VMEM((2 * slot_rows, hid), bf16)],
-        scalars=0,
-    )
+    part = line(west, 1, [part])
     part, cross = lax.optimization_barrier((part, cross))
     cross_rows = call(
         cross_rows_kernel, shape((slot_rows, hid), bf16), [cross], scalars=0
     )
-    halves = 2
-    rows = nodes // halves
     slopes, messages, hiddens, grad_pres, grads = [], [], [], [], []
     for k in range(halves):
         message, slope = call(
@@ -747,17 +783,18 @@
     updated, direct = call(
         output_kernel,
         (shape((chans, nodes), bf16), shape((chans, nodes), f32)),
-        [tile_count, features_held, cotangent, w_out_my, w_node_v_t] + hiddens + grad_pres,
+        [tile_count, features, cotangent, w_out_my, w_node_v_t] + hiddens + grad_pres,
         scalars=1,
     )
     columns = chans_all // shard_count
     inv_root = 1.0 / math.sqrt(total_nodes)
-    inputs = [tile_count, own, from_beside, feats, from_upper]
+    feats_of = [feats_below, feats_above]
     weight_shape = shape((chans_all, hid), f32)
     grad_shape = shape((rows, hid), bf16)
     finals = []
     for k in reversed(range(halves)):
         kernel = functools.partial(back_kernel, k * rows, inv_root)
+        inputs = [tile_count, feats_of[k], own, from_beside, from_upper]
         if k:
             grad_send, weight = call(
                 kernel,
@@ -807,7 +844,8 @@
             [w_mine, w_beside],
             scalars=0,
         )
-        w_beside = lax.ppermute(w_sent, "lon", [(i, i ^ span) for i in range(lons)])
+        apart = lons // span // 2
+        w_beside = lax.ppermute(w_sent, "lon", [(i, i ^ apart) for i in range(lons)])
     grad_w_send = call(
         weight_kernel, shape((columns, hid), f32), [w_mine, w_beside], scalars=0
     )

time: 69.6 us -> 70.9 us (1.019)
  waiting for transfers between devices: 17.7 us -> 15.4 us
  starting transfers between devices: 19 us -> 20.4 us
  Pallas kernels: 31 us -> 32.3 us
  local copies, waits for them, and re-layouts: 0.05 us -> 1.05 us
    ppermute x16 -> x17, waiting for transfers between devices: 9.91 us -> 6.8 us  [shifted(): return lax.ppermute(block, axis, route)]
    ppermute x1, waiting for transfers between devices: 0.66 us -> 2.01 us  [shards(): cross = lax.ppermute(cross, cycle, far_route)]
    pallas_call x29 -> x31, Pallas kernels: 31 us -> 32.3 us  [call(): pl.pallas_call(kernel, out_shape=out_shape, in_specs=[smem] * scalars + [...]
    slice x0 -> x1, local copies, waits for them, and re-layouts: none -> 0.99 us  [shards(): w_send_my, above = lax.optimization_barrier((w_send_my, features[:, rows:]))]
    ppermute x2, starting transfers between devices: 3.29 us -> 4.07 us  [shards(): lax.ppermute(w_sent, 'lon', [(i, i ^ apart) for i in range(lons)])]
    ppermute x16 -> x17, starting transfers between devices: 15.5 us -> 15.6 us  [shifted(): return lax.ppermute(block, axis, route)]
  transfers between devices with their start and end apart: 20 -> 21, of which waited for: 11 -> 12; matrix products, arithmetic and copies ran while one was open for 0% -> 0% of each run, Pallas kernels for 36% -> 39%
where the time goes in v10:
time: 70.9 us; the launch traced here: 70.8 us
  Pallas kernels  32.3 us (46%)
  starting transfers between devices  20.4 us (29%)
  waiting for transfers between devices  15.4 us (22%)
  between operations  1.68 us (2%)
  local copies, waits for them, and re-layouts  1.05 us (1%)
    pallas_call x31, Pallas kernels, call(): pl.pallas_call(kernel, out_shape=out_shape, in_specs=[smem] * scalars + [...  32.3 us
    ppermute x17, starting transfers between devices, shifted(): return lax.ppermute(block, axis, route)  15.6 us
    ppermute x17, waiting for transfers between devices, shifted(): return lax.ppermute(block, axis, route)  6.8 us
    ppermute x2, waiting for transfers between devices, shards(): lax.ppermute(w_sent, 'lon', [(i, i ^ apart) for i in range(lons)])  4.62 us
    ppermute x2, starting transfers between devices, shards(): lax.ppermute(w_sent, 'lon', [(i, i ^ apart) for i in range(lons)])  4.07 us
    ppermute x1, waiting for transfers between devices, shards(): cross = lax.ppermute(cross, cycle, far_route)  2.01 us
    ppermute x1, waiting for transfers between devices, shards(): across = lambda block: lax.ppermute(block, cycle, across_route)  1.93 us
  transfers between devices with their start and end apart: 21, of which 12 were waited for; matrix products, arithmetic and copies ran while one was open for 0% of the time, Pallas kernels for 39%

profile of v10, /device:TPU:0, one launch (start us, length us, event | category | flops | bytes accessed | tf_op | source)
XLA Modules:
  0.0 70.8 jit_solution(5390371369943595535)
XLA Ops:
  0.6 1.0 %fusion = (bf16[256,256]{1,0:T(8,128)(2,1)S(1)}, bf16[256,256]{1,0:T(8,128)(2,1)S(1)}) fusion(bf16[256,512]{1,0:T(8,128)(2,1)} %feats.1), kind=kLoop, calls=%fused_computation | loop fusion | bytes 524288 | tf_op jit(solution)/shard_map/slice | solution.py:627
  1.7 3.0 %collective-permute-start = (bf16[256,256]{1,0:T(8,128)(2,1)S(1)}, bf16[256,256]{1,0:T(8,128)(2,1)S(1)}, u32[]{:S(2)}, u32[]{:S(2)}) collective-permute-start(bf16[256,256]{1,0:T(8,128)(2,1)S(1)} %get-tuple-element.176.refs_0_), channel_id=1, source_target_pairs={{2,0},{0,2},{3,1},{1,3},{6,4},{4,6},{7,5},{5,7},{10,8},{8,10},{11,... | collective-permute-start | bytes 393224 | tf_op jit(solution)/shard_map/ppermute | solution.py:27
  4.7 3.2 %shard_map.157 = (bf16[256,512]{1,0:T(8,128)(2,1)S(1)}, bf16[256,512]{1,0:T(8,128)(2,1)S(1)}, bf16[256,512]{1,0:T(8,128)(2,1)S(1)}, bf16[512,256]{1,0:T(8,128)(2...) custom-call(bf16[512,512]{1,0:T(8,128)(2,1)} %refs_0_.1, ...), custom_call_target="tpu_custom_call" | custom-call | flops 1024 | bytes 1024 | tf_op jit(solution)/shard_map/pallas_call | solution.py:52
  8.2 0.9 %shard_map.158 = (bf16[512,256]{1,0:T(8,128)(2,1)S(1)}, bf16[256,256]{1,0:T(8,128)(2,1)S(1)}, bf16[272,256]{1,0:T(8,128)(2,1)S(1)}) custom-call(s32[1,2,6]{2,1,0:T(2,128)S(1)} %bitcast.12, bf16[256,256]{1,0:T(8,128)(2,1)S(1)} %get-tuple-element.176.refs_0_, bf16[256,256]{1,0:T(8,128)(2,1)S(1)} %collective-permute-done.refs_1_, ...), custom_call_target="tpu_custom_call" | custom-call | flops 1024 | bytes 1024 | tf_op jit(solution)/shard_map/pallas_call | solution.py:52
  9.1 3.9 %collective-permute-start.3 = (bf16[272,256]{1,0:T(8,128)(2,1)S(1)}, bf16[272,256]{1,0:T(8,128)(2,1)S(1)}, u32[]{:S(2)}, u32[]{:S(2)}) collective-permute-start(bf16[272,256]{1,0:T(8,128)(2,1)S(1)} %get-tuple-element.104.refs_4_), channel_id=1, source_target_pairs={{4,0},{8,4},{12,8},{0,12},{5,1},{9,5},{13,9},{1,13},{6,2},{10,6},{... | collective-permute-start | bytes 417800 | tf_op jit(solution)/shard_map/ppermute | solution.py:27
  13.7 1.0 %shard_map.159 = (bf16[12,512,128]{2,1,0:T(8,128)(2,1)S(1)}, bf16[12,512,128]{2,1,0:T(8,128)(2,1)S(1)}, bf16[12,16,512]{2,1,0:T(8,128)(2,1)S(1)}, bf16[12,16,512]{2,1,0:T(8,128)(2,1)S(1)}) custom-call(s32[1]{0:T(128)S(6)} %copy.17.tiles, s32[12,512]{1,0:T(8,128)S(1)} %copy-done.6, s32[1,512]{1,0:T(1,128)S(1)} %bitcast.7), custom_call_target="tpu_custom_call" | custom-call | flops 1024 | bytes 1024 | tf_op jit(solution)/shard_map/pallas_call | solution.py:52
  14.7 0.9 %shard_map.160 = (bf16[512,256]{1,0:T(8,128)(2,1)S(1)}, bf16[256,256]{1,0:T(8,128)(2,1)S(1)}, bf16[272,256]{1,0:T(8,128)(2,1)S(1)}, bf16[272,256]{1,0:T(8,128)(2,1)S(1)}, bf16[272,256]{1,0:T(8,128)(2,1)S(1)}) custom-call(s32[1]{0:T(128)S(6)} %copy.17.tiles, s32[1,2,6]{2,1,0:T(2,128)S(1)} %bitcast.13, bf16[256,256]{1,0:T(8,128)(2,1)S(1)} %get-tuple-element.97.refs_0_, ...), custom_call_target="tpu_custom_call" | custom-call | flops 1024 | bytes 1024 | tf_op jit(solution)/shard_map/pallas_call | solution.py:52
  16.4 1.5 %collective-permute-start.5 = (bf16[256,512]{1,0:T(8,128)(2,1)S(1)}, bf16[256,512]{1,0:T(8,128)(2,1)S(1)}, u32[]{:S(2)}, u32[]{:S(2)}) collective-permute-start(bf16[256,512]{1,0:T(8,128)(2,1)S(1)} %copy-done.3), channel_id=1, source_target_pairs={{2,0},{0,2},{3,1},{1,3},{6,4},{4,6},{7,5},{5,7},{10,8},{8,10},{11,... | collective-permute-start | bytes 786440 | tf_op jit(solution)/shard_map/ppermute | solution.py:27
  18.6 1.2 %shard_map.162.before = bf16[12,512,256]{2,1,0:T(8,128)(2,1)S(1)} custom-call(bf16[12,512,128]{2,1,0:T(8,128)(2,1)S(1)} %get-tuple-element.99.low, bf16[12,512,128]{2,1,0:T(8,128)(2,1)S(1)} %get-tuple-element.100.high, bf16[272,256]{1,0:T(8,128)(2,1)S(1)} %collective-permute-done.3.block.refs_3_), custom_call_target="tpu_custom_call" | custom-call | flops 1000000000 | bytes 1024 | tf_op jit(solution)/shard_map/pallas_call | solution.py:52
  19.8 3.3 %shard_map.163.refs_0_ = bf16[12,512,256]{2,1,0:T(8,128)(2,1)S(1)} custom-call(bf16[12,512,128]{2,1,0:T(8,128)(2,1)S(1)} %get-tuple-element.99.low, bf16[12,512,128]{2,1,0:T(8,128)(2,1)S(1)} %get-tuple-element.100.high, bf16[12,512,256]{2,1,0:T(8,128)(2,1)S(1)} %shard_map.162.before, bf16[256,256]{1,0:T(8,128)(2,1)S(1)} %get-tuple-element.103.refs_3_.below, ...), custom_call_target="tpu_custom_call" | custom-call | flops 1024 | bytes 1024 | tf_op jit(solution)/shard_map/pallas_call | solution.py:52
  23.2 1.2 %collective-permute-done.2.block.refs_2_ = bf16[272,256]{1,0:T(8,128)(2,1)S(1)} collective-permute-done((bf16[272,256]{1,0:T(8,128)(2,1)S(1)}, bf16[272,256]{1,0:T(8,128)(2,1)S(1)}, u32[]{:S(2)}, u32[]{:S(2)}) %collective-permute-start.2) | collective-permute-done | bytes 139296 | tf_op jit(solution)/shard_map/ppermute | solution.py:27
  24.9 1.1 %shard_map.164 = (bf16[512,512]{1,0:T(8,128)(2,1)}, f32[512,512]{1,0:T(8,128)S(1)}, f32[512,512]{1,0:T(8,128)S(1)}) custom-call(s32[1]{0:T(128)S(6)} %copy.17.tiles, bf16[256,512]{1,0:T(8,128)(2,1)S(1)} %copy-done.3, bf16[256,512]{1,0:T(8,128)(2,1)S(1)} %collective-permute-done.5.refs_1_, bf16[512,256]{1,0:T(8,128)(2,1)S(1)} %get-tuple-element.101.below.refs_2_.feats, ...), custom_call_target="tpu_custom_call" | custom-call | flops 1024 | bytes 1024 | tf_op jit(solution)/shard_map/pallas_call | solution.py:52
  26.0 1.5 %shard_map.165.part = bf16[12,512,256]{2,1,0:T(8,128)(2,1)S(1)} custom-call(bf16[12,512,128]{2,1,0:T(8,128)(2,1)S(1)} %get-tuple-element.99.low, bf16[12,512,128]{2,1,0:T(8,128)(2,1)S(1)} %get-tuple-element.100.high, bf16[272,256]{1,0:T(8,128)(2,1)S(1)} %collective-permute-done.2.block.refs_2_, bf16[12,512,256]{2,1,0:T(8,128)(2,1)S(1)} %shard_map.163.refs_0_), custom_call_target="tpu_custom_call" | custom-call | flops 1024 | bytes 1024 | tf_op jit(solution)/shard_map/pallas_call | solution.py:52
  27.5 2.0 %collective-permute-done.6.block.cross = bf16[272,256]{1,0:T(8,128)(2,1)S(1)} collective-permute-done((bf16[272,256]{1,0:T(8,128)(2,1)S(1)}, bf16[272,256]{1,0:T(8,128)(2,1)S(1)}, u32[]{:S(2)}, u32[]{:S(2)}) %collective-permute-start.6) | collective-permute-done | bytes 139296 | tf_op jit(solution)/shard_map/ppermute | solution.py:657
  29.6 2.5 %shard_map.167 = (bf16[256,256]{1,0:T(8,128)(2,1)S(1)}, bf16[12,256,256]{2,1,0:T(8,128)(2,1)S(1)}) custom-call(bf16[12,512,128]{2,1,0:T(8,128)(2,1)S(1)} %get-tuple-element.99.low, bf16[12,512,128]{2,1,0:T(8,128)(2,1)S(1)} %get-tuple-element.100.high, f32[512,256]{1,0:T(8,128)S(1)} %shard_map.161.base, s32[1,512]{1,0:T(1,128)S(1)} %bitcast.8, ...), custom_call_target="tpu_custom_call" | custom-call | flops 1024 | bytes 1024 | tf_op jit(solution)/shard_map/pallas_call | solution.py:52
  32.1 1.6 %collective-permute-start.9 = (bf16[256,256]{1,0:T(8,128)(2,1)S(1)}, bf16[256,256]{1,0:T(8,128)(2,1)S(1)}, u32[]{:S(2)}, u32[]{:S(2)}) collective-permute-start(bf16[256,256]{1,0:T(8,128)(2,1)S(1)} %get-tuple-element.123.refs_0_), channel_id=1, source_target_pairs={{2,0},{0,2},{3,1},{1,3},{6,4},{4,6},{7,5},{5,7},{10,8},{8,10},{11,... | collective-permute-start | bytes 393224 | tf_op jit(solution)/shard_map/ppermute | solution.py:27
  33.7 2.5 %shard_map.170 = (bf16[256,256]{1,0:T(8,128)(2,1)S(1)}, bf16[12,256,256]{2,1,0:T(8,128)(2,1)S(1)}) custom-call(bf16[12,512,128]{2,1,0:T(8,128)(2,1)S(1)} %get-tuple-element.99.low, bf16[12,512,128]{2,1,0:T(8,128)(2,1)S(1)} %get-tuple-element.100.high, f32[512,256]{1,0:T(8,128)S(1)} %shard_map.161.base, s32[1,512]{1,0:T(1,128)S(1)} %bitcast.9, ...), custom_call_target="tpu_custom_call" | custom-call | flops 1024 | bytes 1024 | tf_op jit(solution)/shard_map/pallas_call | solution.py:52
  36.8 0.9 %collective-permute-done.9.refs_1_ = bf16[256,256]{1,0:T(8,128)(2,1)S(1)} collective-permute-done((bf16[256,256]{1,0:T(8,128)(2,1)S(1)}, bf16[256,256]{1,0:T(8,128)(2,1)S(1)}, u32[]{:S(2)}, u32[]{:S(2)}) %collective-permute-start.9) | collective-permute-done | bytes 131104 | tf_op jit(solution)/shard_map/ppermute | solution.py:27
  37.7 1.0 %shard_map.168 = (bf16[512,256]{1,0:T(8,128)(2,1)S(1)}, bf16[512,256]{1,0:T(8,128)(2,1)S(1)}, f32[256,256]{1,0:T(8,128)S(1)}) custom-call(s32[1,512]{1,0:T(1,128)S(1)} %bitcast.10, bf16[256,256]{1,0:T(8,128)(2,1)S(1)} %get-tuple-element.123.refs_0_, bf16[256,256]{1,0:T(8,128)(2,1)S(1)} %collective-permute-done.9.refs_1_, bf16[512,512]{1,0:T(8,128)(2,1)S(1)} %copy-done.1, ...), custom_call_target="tpu_custom_call" | custom-call | flops 1024 | bytes 1024 | tf_op jit(solution)/shard_map/pallas_call | solution.py:52
  38.7 1.4 %shard_map.169 = (bf16[12,256,256]{2,1,0:T(8,128)(2,1)S(1)}, f32[768,256]{1,0:T(8,128)S(1)}) custom-call(bf16[12,16,512]{2,1,0:T(8,128)(2,1)S(1)} %get-tuple-element.95.low, bf16[12,16,512]{2,1,0:T(8,128)(2,1)S(1)} %get-tuple-element.96.high, bf16[12,256,256]{2,1,0:T(8,128)(2,1)S(1)} %get-tuple-element.122.slope, f32[256,256]{1,0:T(8,128)S(1)} %get-tuple-element.128.scale), custom_call_target="tpu_custom_call" | custom-call | flops 1024 | bytes 1024 | tf_op jit(solution)/shard_map/pallas_call | solution.py:52
  40.1 1.4 %collective-permute-done.10.refs_1_ = bf16[256,256]{1,0:T(8,128)(2,1)S(1)} collective-permute-done((bf16[256,256]{1,0:T(8,128)(2,1)S(1)}, bf16[256,256]{1,0:T(8,128)(2,1)S(1)}, u32[]{:S(2)}, u32[]{:S(2)}) %collective-permute-start.10) | collective-permute-done | bytes 131104 | tf_op jit(solution)/shard_map/ppermute | solution.py:27
  43.0 1.0 %shard_map.173 = bf16[2,256,256]{2,1,0:T(8,128)(2,1)S(1)} custom-call(bf16[12,16,512]{2,1,0:T(8,128)(2,1)S(1)} %get-tuple-element.95.low, bf16[12,16,512]{2,1,0:T(8,128)(2,1)S(1)} %get-tuple-element.96.high, bf16[12,256,256]{2,1,0:T(8,128)(2,1)S(1)} %get-tuple-element.134.grads.refs_1_, f32[768,256]{1,0:T(8,128)S(1)} %get-tuple-element.133.before, ...), custom_call_target="tpu_custom_call" | custom-call | flops 1024 | bytes 1024 | tf_op jit(solution)/shard_map/pallas_call | solution.py:52
  44.1 2.6 %shard_map.174 = (bf16[256,256]{1,0:T(8,128)(2,1)S(1)}, bf16[256,256]{1,0:T(8,128)(2,1)S(1)}, bf16[256,256]{1,0:T(8,128)(2,1)S(1)}) custom-call(bf16[12,16,512]{2,1,0:T(8,128)(2,1)S(1)} %get-tuple-element.95.low, bf16[12,16,512]{2,1,0:T(8,128)(2,1)S(1)} %get-tuple-element.96.high, bf16[12,256,256]{2,1,0:T(8,128)(2,1)S(1)} %get-tuple-element.143.refs_0_, ...), custom_call_target="tpu_custom_call" | custom-call | flops 1024 | bytes 1024 | tf_op jit(solution)/shard_map/pallas_call | solution.py:52
  47.3 1.9 %collective-permute-done.11.across = bf16[256,256]{1,0:T(8,128)(2,1)S(1)} collective-permute-done((bf16[256,256]{1,0:T(8,128)(2,1)S(1)}, bf16[256,256]{1,0:T(8,128)(2,1)S(1)}, u32[]{:S(2)}, u32[]{:S(2)}) %collective-permute-start.11) | collective-permute-done | bytes 131104 | tf_op jit(solution)/shard_map/ppermute | solution.py:587
  49.4 1.6 %collective-permute-start.14 = (bf16[256,256]{1,0:T(8,128)(2,1)S(1)}, bf16[256,256]{1,0:T(8,128)(2,1)S(1)}, u32[]{:S(2)}, u32[]{:S(2)}) collective-permute-start(bf16[256,256]{1,0:T(8,128)(2,1)S(1)} %get-tuple-element.142), channel_id=1, source_target_pairs={{4,0},{8,4},{12,8},{0,12},{5,1},{9,5},{13,9},{1,13},{6,2},{10,6},{... | collective-permute-start | bytes 393224 | tf_op jit(solution)/shard_map/ppermute | solution.py:27
  51.4 2.1 %shard_map.177 = (f32[512,256]{1,0:T(8,128)S(1)}, bf16[256,512]{1,0:T(8,128)(2,1)S(1)}) custom-call(bf16[12,16,512]{2,1,0:T(8,128)(2,1)S(1)} %get-tuple-element.95.low, bf16[12,16,512]{2,1,0:T(8,128)(2,1)S(1)} %get-tuple-element.96.high, bf16[12,256,256]{2,1,0:T(8,128)(2,1)S(1)} %get-tuple-element.143.refs_0_, ...), custom_call_target="tpu_custom_call" | custom-call | flops 1024 | bytes 1024 | tf_op jit(solution)/shard_map/pallas_call | solution.py:52
  53.5 1.1 %shard_map.178 = (bf16[256,512]{1,0:T(8,128)(2,1)}, f32[256,512]{1,0:T(8,128)S(1)}) custom-call(s32[1]{0:T(128)S(6)} %copy.17.tiles, bf16[256,512]{1,0:T(8,128)(2,1)S(1)} %copy-done.2, bf16[256,512]{1,0:T(8,128)(2,1)S(1)} %copy-done.3, bf16[256,512]{1,0:T(8,128)(2,1)S(1)} %get-tuple-element.89.w_out, bf16[256,512]{1,0:T(8,128)(2,1)S(1)} %get-tuple-element.90.w_node_v_t, ...), custom_call_target="tpu_custom_call" | custom-call | flops 1024 | bytes 1024 | tf_op jit(solution)/shard_map/pallas_call | solution.py:52
  56.2 2.2 %collective-permute-done.15.refs_0_ = bf16[256,256]{1,0:T(8,128)(2,1)S(1)} collective-permute-done((bf16[256,256]{1,0:T(8,128)(2,1)S(1)}, bf16[256,256]{1,0:T(8,128)(2,1)S(1)}, u32[]{:S(2)}, u32[]{:S(2)}) %collective-permute-start.15) | collective-permute-done | bytes 131104 | tf_op jit(solution)/shard_map/ppermute | solution.py:27
  60.7 0.9 %collective-permute-start.19 = (bf16[2,64,256]{2,1,0:T(8,128)(2,1)S(1)}, bf16[2,64,256]{2,1,0:T(8,128)(2,1)S(1)}, u32[]{:S(2)}, u32[]{:S(2)}) collective-permute-start(bf16[2,64,256]{2,1,0:T(8,128)(2,1)S(1)} %get-tuple-element.172), channel_id=1, source_target_pairs={{0,4},{4,0},{8,12},{12,8},{1,5},{5,1},{9,13},{13,9},{2,6},{6,2},{1... | collective-permute-start | bytes 196616 | tf_op jit(solution)/shard_map/ppermute | solution.py:848
  61.6 3.5 %collective-permute-done.19.received = bf16[2,64,256]{2,1,0:T(8,128)(2,1)S(1)} collective-permute-done((bf16[2,64,256]{2,1,0:T(8,128)(2,1)S(1)}, bf16[2,64,256]{2,1,0:T(8,128)(2,1)S(1)}, u32[]{:S(2)}, u32[]{:S(2)}) %collective-permute-start.19) | collective-permute-done | bytes 65568 | tf_op jit(solution)/shard_map/ppermute | solution.py:848
  65.0 3.2 %collective-permute-start.20 = (bf16[1,64,256]{2,1,0:T(8,128)(2,1)S(1)}, bf16[1,64,256]{2,1,0:T(8,128)(2,1)S(1)}, u32[]{:S(2)}, u32[]{:S(2)}) collective-permute-start(bf16[1,64,256]{2,1,0:T(8,128)(2,1)S(1)} %get-tuple-element.174), channel_id=1, source_target_pairs={{0,8},{4,12},{8,0},{12,4},{1,9},{5,13},{9,1},{13,5},{2,10},{6,14},... | collective-permute-start | bytes 98312 | tf_op jit(solution)/shard_map/ppermute | solution.py:848
  69.0 1.2 %collective-permute-done.20.received = bf16[1,64,256]{2,1,0:T(8,128)(2,1)S(1)} collective-permute-done((bf16[1,64,256]{2,1,0:T(8,128)(2,1)S(1)}, bf16[1,64,256]{2,1,0:T(8,128)(2,1)S(1)}, u32[]{:S(2)}, u32[]{:S(2)}) %collective-permute-start.20) | collective-permute-done | bytes 32800 | tf_op jit(solution)/shard_map/ppermute | solution.py:848
  (62 shorter events, 11.0 us)
Async XLA Ops:
  1.6 6.6 %copy-start.7 = (s32[1,6,2]{1,2,0:T(2,128)S(1)}, s32[1,6,2]{1,2,0:T(2,128)}, u32[]{:S(2)}) copy-start(s32[1,6,2]{1,2,0:T(2,128)} %param.19) | copy-start | bytes 148
  1.6 12.0 %copy-start.5 = (s32[512]{0:T(512)S(1)}, s32[512]{0:T(512)}, u32[]{:S(2)}) copy-start(s32[512]{0:T(512)} %param.17) | copy-start | bytes 6148
  1.6 12.0 %copy-start.6 = (s32[12,512]{1,0:T(8,128)S(1)}, s32[12,512]{1,0:T(8,128)}, u32[]{:S(2)}) copy-start(s32[12,512]{1,0:T(8,128)} %senders) | copy-start | bytes 73732
  1.7 14.3 %copy-start.8 = (f32[512]{0:T(512)S(1)}, f32[512]{0:T(512)}, u32[]{:S(2)}) copy-start(f32[512]{0:T(512)} %param.22) | copy-start | bytes 6148
  1.7 6.5 %collective-permute-start = (bf16[256,256]{1,0:T(8,128)(2,1)S(1)}, bf16[256,256]{1,0:T(8,128)(2,1)S(1)}, u32[]{:S(2)}, u32[]{:S(2)}) collective-permute-start(bf16[256,256]{1,0:T(8,128)(2,1)S(1)} %get-tuple-element.176.refs_0_), channel_id=1, source_target_pairs={{2,0},{0,2},{3,1},{1,3},{6,4},{4,6},{7,5},{5,7},{10,8},{8,10},{11,... | collective-permute-start | bytes 393224 | tf_op jit(solution)/shard_map/ppermute | solution.py:27
  7.8 8.6 %copy-start.3 = (bf16[256,512]{1,0:T(8,128)(2,1)S(1)}, bf16[256,512]{1,0:T(8,128)(2,1)}, u32[]{:S(2)}) copy-start(bf16[256,512]{1,0:T(8,128)(2,1)} %cots.1) | copy-start | bytes 786436
  7.9 6.9 %collective-permute-start.1 = (bf16[256,256]{1,0:T(8,128)(2,1)S(1)}, bf16[256,256]{1,0:T(8,128)(2,1)S(1)}, u32[]{:S(2)}, u32[]{:S(2)}) collective-permute-start(bf16[256,256]{1,0:T(8,128)(2,1)S(1)} %get-tuple-element.97.refs_0_), channel_id=1, source_target_pairs={{2,0},{0,2},{3,1},{1,3},{6,4},{4,6},{7,5},{5,7},{10,8},{8,10},{11,... | collective-permute-start | bytes 393224 | tf_op jit(solution)/shard_map/ppermute | solution.py:27
  9.1 9.6 %collective-permute-start.3 = (bf16[272,256]{1,0:T(8,128)(2,1)S(1)}, bf16[272,256]{1,0:T(8,128)(2,1)S(1)}, u32[]{:S(2)}, u32[]{:S(2)}) collective-permute-start(bf16[272,256]{1,0:T(8,128)(2,1)S(1)} %get-tuple-element.104.refs_4_), channel_id=1, source_target_pairs={{4,0},{8,4},{12,8},{0,12},{5,1},{9,5},{13,9},{1,13},{6,2},{10,6},{... | collective-permute-start | bytes 417800 | tf_op jit(solution)/shard_map/ppermute | solution.py:27
  15.7 4.2 %collective-permute-start.4 = (bf16[272,256]{1,0:T(8,128)(2,1)S(1)}, bf16[272,256]{1,0:T(8,128)(2,1)S(1)}, u32[]{:S(2)}, u32[]{:S(2)}) collective-permute-start(bf16[272,256]{1,0:T(8,128)(2,1)S(1)} %get-tuple-element.109), channel_id=1, source_target_pairs={{1,0},{0,1},{3,2},{2,3},{5,4},{4,5},{7,6},{6,7},{9,8},{8,9},{11,10... | collective-permute-start | bytes 417800 | tf_op jit(solution)/shard_map/ppermute | solution.py:27
  15.7 8.6 %collective-permute-start.2 = (bf16[272,256]{1,0:T(8,128)(2,1)S(1)}, bf16[272,256]{1,0:T(8,128)(2,1)S(1)}, u32[]{:S(2)}, u32[]{:S(2)}) collective-permute-start(bf16[272,256]{1,0:T(8,128)(2,1)S(1)} %get-tuple-element.108), channel_id=1, source_target_pairs={{12,0},{0,4},{4,8},{8,12},{13,1},{1,5},{5,9},{9,13},{14,2},{2,6},{... | collective-permute-start | bytes 417800 | tf_op jit(solution)/shard_map/ppermute | solution.py:27
  16.4 8.5 %collective-permute-start.5 = (bf16[256,512]{1,0:T(8,128)(2,1)S(1)}, bf16[256,512]{1,0:T(8,128)(2,1)S(1)}, u32[]{:S(2)}, u32[]{:S(2)}) collective-permute-start(bf16[256,512]{1,0:T(8,128)(2,1)S(1)} %copy-done.3), channel_id=1, source_target_pairs={{2,0},{0,2},{3,1},{1,3},{6,4},{4,6},{7,5},{5,7},{10,8},{8,10},{11,... | collective-permute-start | bytes 786440 | tf_op jit(solution)/shard_map/ppermute | solution.py:27
  18.0 11.6 %collective-permute-start.6 = (bf16[272,256]{1,0:T(8,128)(2,1)S(1)}, bf16[272,256]{1,0:T(8,128)(2,1)S(1)}, u32[]{:S(2)}, u32[]{:S(2)}) collective-permute-start(bf16[272,256]{1,0:T(8,128)(2,1)S(1)} %get-tuple-element.119), channel_id=1, source_target_pairs={{0,9},{1,8},{4,13},{5,12},{8,1},{9,0},{12,5},{13,4},{2,11},{3,10},... | collective-permute-start | bytes 417800 | tf_op jit(solution)/shard_map/ppermute | solution.py:657
  19.8 5.1 %copy-start = (bf16[512,512]{1,0:T(8,128)(2,1)S(1)}, bf16[512,512]{1,0:T(8,128)(2,1)}, u32[]{:S(2)}) copy-start(bf16[512,512]{1,0:T(8,128)(2,1)} %refs_4_.3) | copy-start | bytes 1572868
  19.8 5.1 %copy-start.4 = (bf16[512,512]{1,0:T(8,128)(2,1)S(1)}, bf16[512,512]{1,0:T(8,128)(2,1)}, u32[]{:S(2)}) copy-start(bf16[512,512]{1,0:T(8,128)(2,1)} %get-tuple-element.116.refs_6_) | copy-start | bytes 1572868
  19.8 5.1 %copy-start.9 = (f32[512]{0:T(512)S(1)}, f32[512]{0:T(512)}, u32[]{:S(2)}) copy-start(f32[512]{0:T(512)} %param.26) | copy-start | bytes 6148
  24.4 5.2 %collective-permute-start.8 = (bf16[272,256]{1,0:T(8,128)(2,1)S(1)}, bf16[272,256]{1,0:T(8,128)(2,1)S(1)}, u32[]{:S(2)}, u32[]{:S(2)}) collective-permute-start(bf16[272,256]{1,0:T(8,128)(2,1)S(1)} %collective-permute-done.3.block.refs_3_), channel_id=1, source_target_pairs={{1,0},{0,1},{3,2},{2,3},{5,4},{4,5},{7,6},{6,7},{9,8},{8,9},{11,10... | collective-permute-start | bytes 417800 | tf_op jit(solution)/shard_map/ppermute | solution.py:27
  24.4 5.2 %collective-permute-start.7 = (bf16[272,256]{1,0:T(8,128)(2,1)S(1)}, bf16[272,256]{1,0:T(8,128)(2,1)S(1)}, u32[]{:S(2)}, u32[]{:S(2)}) collective-permute-start(bf16[272,256]{1,0:T(8,128)(2,1)S(1)} %collective-permute-done.2.block.refs_2_), channel_id=1, source_target_pairs={{1,0},{0,1},{3,2},{2,3},{5,4},{4,5},{7,6},{6,7},{9,8},{8,9},{11,10... | collective-permute-start | bytes 417800 | tf_op jit(solution)/shard_map/ppermute | solution.py:27
  32.1 5.6 %copy-start.1 = (bf16[512,512]{1,0:T(8,128)(2,1)S(1)}, bf16[512,512]{1,0:T(8,128)(2,1)}, u32[]{:S(2)}) copy-start(bf16[512,512]{1,0:T(8,128)(2,1)} %get-tuple-element.124.refs_2_) | copy-start | bytes 1572868
  32.1 5.6 %collective-permute-start.9 = (bf16[256,256]{1,0:T(8,128)(2,1)S(1)}, bf16[256,256]{1,0:T(8,128)(2,1)S(1)}, u32[]{:S(2)}, u32[]{:S(2)}) collective-permute-start(bf16[256,256]{1,0:T(8,128)(2,1)S(1)} %get-tuple-element.123.refs_0_), channel_id=1, source_target_pairs={{2,0},{0,2},{3,1},{1,3},{6,4},{4,6},{7,5},{5,7},{10,8},{8,10},{11,... | collective-permute-start | bytes 393224 | tf_op jit(solution)/shard_map/ppermute | solution.py:27
  36.2 5.3 %collective-permute-start.10 = (bf16[256,256]{1,0:T(8,128)(2,1)S(1)}, bf16[256,256]{1,0:T(8,128)(2,1)S(1)}, u32[]{:S(2)}, u32[]{:S(2)}) collective-permute-start(bf16[256,256]{1,0:T(8,128)(2,1)S(1)} %get-tuple-element.131.refs_0_), channel_id=1, source_target_pairs={{2,0},{0,2},{3,1},{1,3},{6,4},{4,6},{7,5},{5,7},{10,8},{8,10},{11,... | collective-permute-start | bytes 393224 | tf_op jit(solution)/shard_map/ppermute | solution.py:27
  43.0 6.3 %collective-permute-start.11 = (bf16[256,256]{1,0:T(8,128)(2,1)S(1)}, bf16[256,256]{1,0:T(8,128)(2,1)S(1)}, u32[]{:S(2)}, u32[]{:S(2)}) collective-permute-start(bf16[256,256]{1,0:T(8,128)(2,1)S(1)} %get-tuple-element.138), channel_id=1, source_target_pairs={{0,13},{1,4},{4,1},{5,8},{8,5},{9,12},{12,9},{13,0},{2,15},{3,6},{... | collective-permute-start | bytes 393224 | tf_op jit(solution)/shard_map/ppermute | solution.py:587
  44.0 5.3 %collective-permute-start.12 = (bf16[2,256,256]{2,1,0:T(8,128)(2,1)S(1)}, bf16[2,256,256]{2,1,0:T(8,128)(2,1)S(1)}, u32[]{:S(2)}, u32[]{:S(2)}) collective-permute-start(bf16[2,256,256]{2,1,0:T(8,128)(2,1)S(1)} %shard_map.173), channel_id=1, source_target_pairs={{1,0},{0,1},{3,2},{2,3},{5,4},{4,5},{7,6},{6,7},{9,8},{8,9},{11,10... | collective-permute-start | bytes 786440 | tf_op jit(solution)/shard_map/ppermute | solution.py:27
  46.7 7.9 %collective-permute-start.13 = (bf16[256,256]{1,0:T(8,128)(2,1)S(1)}, bf16[256,256]{1,0:T(8,128)(2,1)S(1)}, u32[]{:S(2)}, u32[]{:S(2)}) collective-permute-start(bf16[256,256]{1,0:T(8,128)(2,1)S(1)} %get-tuple-element.152), channel_id=1, source_target_pairs={{1,0},{0,1},{3,2},{2,3},{5,4},{4,5},{7,6},{6,7},{9,8},{8,9},{11,10... | collective-permute-start | bytes 393224 | tf_op jit(solution)/shard_map/ppermute | solution.py:27
  49.4 5.4 %collective-permute-start.14 = (bf16[256,256]{1,0:T(8,128)(2,1)S(1)}, bf16[256,256]{1,0:T(8,128)(2,1)S(1)}, u32[]{:S(2)}, u32[]{:S(2)}) collective-permute-start(bf16[256,256]{1,0:T(8,128)(2,1)S(1)} %get-tuple-element.142), channel_id=1, source_target_pairs={{4,0},{8,4},{12,8},{0,12},{5,1},{9,5},{13,9},{1,13},{6,2},{10,6},{... | collective-permute-start | bytes 393224 | tf_op jit(solution)/shard_map/ppermute | solution.py:27
  50.9 2.6 %copy-start.2 = (bf16[256,512]{1,0:T(8,128)(2,1)S(1)}, bf16[256,512]{1,0:T(8,128)(2,1)}, u32[]{:S(2)}) copy-start(bf16[256,512]{1,0:T(8,128)(2,1)} %feats.1) | copy-start | bytes 786436
  50.9 7.4 %collective-permute-start.15 = (bf16[256,256]{1,0:T(8,128)(2,1)S(1)}, bf16[256,256]{1,0:T(8,128)(2,1)S(1)}, u32[]{:S(2)}, u32[]{:S(2)}) collective-permute-start(bf16[256,256]{1,0:T(8,128)(2,1)S(1)} %get-tuple-element.153), channel_id=1, source_target_pairs={{12,0},{0,4},{4,8},{8,12},{13,1},{1,5},{5,9},{9,13},{14,2},{2,6},{... | collective-permute-start | bytes 393224 | tf_op jit(solution)/shard_map/ppermute | solution.py:27
  55.6 5.1 %collective-permute-start.18 = (bf16[256,256]{1,0:T(8,128)(2,1)S(1)}, bf16[256,256]{1,0:T(8,128)(2,1)S(1)}, u32[]{:S(2)}, u32[]{:S(2)}) collective-permute-start(bf16[256,256]{1,0:T(8,128)(2,1)S(1)} %bitcast.17), channel_id=1, source_target_pairs={{2,0},{0,2},{3,1},{1,3},{6,4},{4,6},{7,5},{5,7},{10,8},{8,10},{11,... | collective-permute-start | bytes 393224 | tf_op jit(solution)/shard_map/ppermute | solution.py:27
  58.7 1.9 %collective-permute-start.17 = (bf16[4,64,256]{2,1,0:T(8,128)(2,1)S(1)}, bf16[4,64,256]{2,1,0:T(8,128)(2,1)S(1)}, u32[]{:S(2)}, u32[]{:S(2)}) collective-permute-start(bf16[4,64,256]{2,1,0:T(8,128)(2,1)S(1)} %get-tuple-element.165), channel_id=1, source_target_pairs={{1,0},{0,1},{3,2},{2,3},{5,4},{4,5},{7,6},{6,7},{9,8},{8,9},{11,10... | collective-permute-start | bytes 393224 | tf_op jit(solution)/shard_map/ppermute | solution.py:27
  59.3 9.0 %collective-permute-start.16 = (bf16[256,256]{1,0:T(8,128)(2,1)S(1)}, bf16[256,256]{1,0:T(8,128)(2,1)S(1)}, u32[]{:S(2)}, u32[]{:S(2)}) collective-permute-start(bf16[256,256]{1,0:T(8,128)(2,1)S(1)} %bitcast.16), channel_id=1, source_target_pairs={{2,0},{0,2},{3,1},{1,3},{6,4},{4,6},{7,5},{5,7},{10,8},{8,10},{11,... | collective-permute-start | bytes 393224 | tf_op jit(solution)/shard_map/ppermute | solution.py:27
  60.7 4.3 %collective-permute-start.19 = (bf16[2,64,256]{2,1,0:T(8,128)(2,1)S(1)}, bf16[2,64,256]{2,1,0:T(8,128)(2,1)S(1)}, u32[]{:S(2)}, u32[]{:S(2)}) collective-permute-start(bf16[2,64,256]{2,1,0:T(8,128)(2,1)S(1)} %get-tuple-element.172), channel_id=1, source_target_pairs={{0,4},{4,0},{8,12},{12,8},{1,5},{5,1},{9,13},{13,9},{2,6},{6,2},{1... | collective-permute-start | bytes 196616 | tf_op jit(solution)/shard_map/ppermute | solution.py:848
  65.0 5.1 %collective-permute-start.20 = (bf16[1,64,256]{2,1,0:T(8,128)(2,1)S(1)}, bf16[1,64,256]{2,1,0:T(8,128)(2,1)S(1)}, u32[]{:S(2)}, u32[]{:S(2)}) collective-permute-start(bf16[1,64,256]{2,1,0:T(8,128)(2,1)S(1)} %get-tuple-element.174), channel_id=1, source_target_pairs={{0,8},{4,12},{8,0},{12,4},{1,9},{5,13},{9,1},{13,5},{2,10},{6,14},... | collective-permute-start | bytes 98312 | tf_op jit(solution)/shard_map/ppermute | solution.py:848

commit v11 on v9

--- a/solution.py
+++ b/solution.py
@@ -14,6 +14,8 @@
 PACK = 16
 MIB = 1 << 20
 WEIGHTS_LIMIT = 52
+WEIGHT_FLOPS = 3 * 10**9
+CROSS_FLOPS = 2 * 10**9
 NO_CHUNK = 64
 SLOT_OF = ((3, 0), (1, 1), (4, 4), (2, 5), (0, 2), (5, 3))
 EARLY, LATE = (3, 4, 5), (1, 2, 0)
@@ -457,6 +459,14 @@
     east[...] = (right[...] + more[1].astype(jnp.float32)).astype(jnp.bfloat16)
 
 
+def band_bits(place, lons):
+    bits, weight = 0, 1
+    while weight < lons:
+        bits += weight if place * weight * 2 // lons % 2 else 0
+        weight *= 2
+    return bits
+
+
 def back_kernel(start, inv_root, tiles, own, beside, feats, upper, *refs):
     *refs, total = refs
     sub = lax.axis_index("sub")
@@ -481,7 +491,7 @@
     lon = lax.axis_index("lon")
     lons, columns, _ = w_mine.shape
     for k in range(lons):
-        band = (lon ^ k) * 2
+        band = (lon ^ band_bits(k, lons)) * 2
         for out, core in ((w_mine, sub), (w_beside, 1 - sub)):
             spot = pl.multiple_of((band + core) * columns, columns)
             out[k] = weight[pl.ds(spot, columns), :].astype(out.dtype)
@@ -618,9 +628,8 @@
         [bias_edge[None, :], feats, w_recv_my],
         scalars=0,
     )
-    base, senders, cotangent_late = lax.optimization_barrier((base, senders, cotangent))
+    base, senders = lax.optimization_barrier((base, senders))
     beside = shifted(beside, "sub", 1)
-    cot_blocks = gathered(cotangent_late, "ch")
     low_cols, high_cols, low_rows, high_rows = call(
         edges_kernel,
         (
@@ -632,17 +641,6 @@
         [tile_count, senders, degrees],
         scalars=1,
     )
-    cots, pre, grad_hidden = call(
-        functools.partial(prepare_kernel, count),
-        (
-            shape((chans_all, nodes), bf16),
-            shape((hidden_all, nodes), f32),
-            shape((hidden_all, nodes), f32),
-        ),
-        [tile_count] + cot_blocks + [feats, w_node_v, bias_node[None, :], w_out_t],
-        scalars=1,
-    )
-
     part_shape = shape((degree, nodes, hid), bf16)
     part = call(
         near_kernel,
@@ -654,7 +652,8 @@
     west, east, part = lax.optimization_barrier((west, east, part))
     west_too = shifted(west, "sub", 1)
     east_too = shifted(east, "sub", 1)
-    part, pre = lax.optimization_barrier((part, pre))
+    west, cotangent_late = lax.optimization_barrier((west, cotangent))
+    cot_blocks = gathered(cotangent_late, "ch")
     part = call(
         line_kernel,
         part_shape,
@@ -664,7 +663,7 @@
     )
     part, cross = lax.optimization_barrier((part, cross))
     cross_rows = call(
-        cross_rows_kernel, shape((slot_rows, hid), bf16), [cross], scalars=0
+        cross_rows_kernel, shape((slot_rows, hid), bf16), [cross], scalars=0, flops=CROSS_FLOPS
     )
     halves = 2
     rows = nodes // halves
@@ -677,8 +676,21 @@
             scratch=[pltpu.VMEM((3 * slot_rows, hid), bf16), pltpu.VMEM((rows, hid), f32)],
             scalars=0,
         )
+        if k == halves - 1:
+            message, cot_blocks[-1] = lax.optimization_barrier((message, cot_blocks[-1]))
         slopes.append(slope)
         messages.append(gathered(message, "ch"))
+
+    cots, pre, grad_hidden = call(
+        functools.partial(prepare_kernel, count),
+        (
+            shape((chans_all, nodes), bf16),
+            shape((hidden_all, nodes), f32),
+            shape((hidden_all, nodes), f32),
+        ),
+        [tile_count] + cot_blocks + [feats, w_node_v, bias_node[None, :], w_out_t],
+        scalars=1,
+    )
 
     block = shape((slot_rows, hid), bf16)
     sums = shape((len(EARLY) * slot_rows, hid), f32)
@@ -755,31 +767,7 @@
     inputs = [tile_count, own, from_beside, feats, from_upper]
     weight_shape = shape((chans_all, hid), f32)
     grad_shape = shape((rows, hid), bf16)
-    finals = []
-    for k in reversed(range(halves)):
-        kernel = functools.partial(back_kernel, k * rows, inv_root)
-        if k:
-            grad_send, weight = call(
-                kernel,
-                (grad_shape, weight_shape),
-                inputs,
-                scratch=[pltpu.VMEM((nodes, hid), f32)],
-                scalars=1,
-            )
-        else:
-            grad_send, w_mine, w_beside = call(
-                kernel,
-                (
-                    grad_shape,
-                    shape((lons, columns, hid), f32),
-                    shape((lons, columns, hid), bf16),
-                ),
-                inputs + [from_lower, weight],
-                scratch=[pltpu.VMEM(weight_shape.shape, f32), pltpu.VMEM((nodes, hid), f32)],
-                scalars=1,
-            )
-            w_beside = shifted(w_beside, "sub", 1)
-            w_beside, *finals = lax.optimization_barrier((w_beside, *finals))
+    def finish(k, grad_send, done):
         kept, sent = call(
             functools.partial(terms_kernel, k * rows),
             (shape((chans, rows), f32), shape((count - 1, chans, rows), bf16)),
@@ -787,17 +775,33 @@
             scratch=[pltpu.VMEM((chans_all, rows), f32)],
             scalars=0,
         )
-        if k:
-            weight, kept = lax.optimization_barrier((weight, kept))
         parts = [kept] + [shifted(sent[i - 1], "ch", i) for i in range(1, count)]
-        grad_features = call(
+        out = call(
             functools.partial(finish_kernel, count),
             shape((chans, nodes - k * rows), bf16),
-            parts + finals,
+            parts + done,
             scalars=0,
         )
-        finals = [grad_features]
-
+        return kept, out
+
+    grad_send, weight = call(
+        functools.partial(back_kernel, rows, inv_root),
+        (grad_shape, weight_shape),
+        inputs,
+        scratch=[pltpu.VMEM((nodes, hid), f32)],
+        scalars=1,
+    )
+    kept, upper_out = finish(1, grad_send, [])
+    weight, kept = lax.optimization_barrier((weight, kept))
+    grad_send, w_mine, w_beside = call(
+        functools.partial(back_kernel, 0, inv_root),
+        (grad_shape, shape((lons, columns, hid), f32), shape((lons, columns, hid), bf16)),
+        inputs + [from_lower, weight],
+        scratch=[pltpu.VMEM(weight_shape.shape, f32), pltpu.VMEM((nodes, hid), f32)],
+        scalars=1,
+    )
+    w_beside = shifted(w_beside, "sub", 1)
+    w_beside, upper_out = lax.optimization_barrier((w_beside, upper_out))
     span = lons
     while span > 1:
         span //= 2
@@ -807,10 +811,14 @@
             [w_mine, w_beside],
             scalars=0,
         )
-        w_beside = lax.ppermute(w_sent, "lon", [(i, i ^ span) for i in range(lons)])
+        if span == 1:
+            w_sent, grad_send = lax.optimization_barrier((w_sent, grad_send))
+        apart = lons // span // 2
+        w_beside = lax.ppermute(w_sent, "lon", [(i, i ^ apart) for i in range(lons)])
     grad_w_send = call(
-        weight_kernel, shape((columns, hid), f32), [w_mine, w_beside], scalars=0
-    )
+        weight_kernel, shape((columns, hid), f32), [w_mine, w_beside], scalars=0, flops=WEIGHT_FLOPS
+    )
+    _, grad_features = finish(0, grad_send, [upper_out])
     return (updated, grad_features, grad_w_send.T)
 
 

time: 69.6 us -> 73.2 us (1.052)
  waiting for transfers between devices: 17.7 us -> 20.4 us
  starting transfers between devices: 19 us -> 19.9 us
    ppermute x16, waiting for transfers between devices: 9.91 us -> 12.1 us  [shifted(): return lax.ppermute(block, axis, route)]
    ppermute x1, waiting for transfers between devices: 0.66 us -> 1.94 us  [shards(): cross = lax.ppermute(cross, cycle, far_route)]
    ppermute x2, waiting for transfers between devices: 5.32 us -> 4.43 us  [shards(): lax.ppermute(w_sent, 'lon', [(i, i ^ apart) for i in range(lons)])]
  transfers between devices with their start and end apart: 20 -> 20, of which waited for: 11 -> 11; matrix products, arithmetic and copies ran while one was open for 0% -> 0% of each run, Pallas kernels for 36% -> 38%
where the time goes in v11:
time: 73.2 us; the launch traced here: 73 us
  Pallas kernels  31 us (42%)
  waiting for transfers between devices  20.4 us (28%)
  starting transfers between devices  19.9 us (27%)
  between operations  1.65 us (2%)
    pallas_call x29, Pallas kernels, call(): pl.pallas_call(kernel, out_shape=out_shape, in_specs=[smem] * scalars + [...  31 us
    ppermute x16, starting transfers between devices, shifted(): return lax.ppermute(block, axis, route)  15.7 us
    ppermute x16, waiting for transfers between devices, shifted(): return lax.ppermute(block, axis, route)  12.1 us
    ppermute x2, waiting for transfers between devices, shards(): lax.ppermute(w_sent, 'lon', [(i, i ^ apart) for i in range(lons)])  4.43 us
    ppermute x2, starting transfers between devices, shards(): lax.ppermute(w_sent, 'lon', [(i, i ^ apart) for i in range(lons)])  3.72 us
    ppermute x1, waiting for transfers between devices, shards(): cross = lax.ppermute(cross, cycle, far_route)  1.94 us
    ppermute x1, waiting for transfers between devices, shards(): across = lambda block: lax.ppermute(block, cycle, across_route)  1.9 us
  transfers between devices with their start and end apart: 20, of which 11 were waited for; matrix products, arithmetic and copies ran while one was open for 0% of the time, Pallas kernels for 38%

profile of v11, /device:TPU:0, one launch (start us, length us, event | category | flops | bytes accessed | tf_op | source)
XLA Modules:
  0.0 73.0 jit_solution(11922297476605129181)
XLA Ops:
  0.7 3.0 %collective-permute-start = (bf16[256,512]{1,0:T(8,128)(2,1)}, bf16[256,512]{1,0:T(8,128)(2,1)S(1)}, u32[]{:S(2)}, u32[]{:S(2)}) collective-permute-start(bf16[256,512]{1,0:T(8,128)(2,1)} %refs_2_.1), channel_id=1, source_target_pairs={{2,0},{0,2},{3,1},{1,3},{6,4},{4,6},{7,5},{5,7},{10,8},{8,10},{11,... | collective-permute-start | bytes 786440 | tf_op jit(solution)/shard_map/ppermute | solution.py:28
  3.7 3.3 %shard_map.157 = (bf16[256,512]{1,0:T(8,128)(2,1)S(1)}, bf16[256,512]{1,0:T(8,128)(2,1)S(1)}, bf16[256,512]{1,0:T(8,128)(2,1)S(1)}, bf16[256,512]{1,0:T(8,128)(2...) custom-call(bf16[512,512]{1,0:T(8,128)(2,1)} %refs_0_.1, ...), custom_call_target="tpu_custom_call" | custom-call | flops 1024 | bytes 1024 | tf_op jit(solution)/shard_map/pallas_call | solution.py:53
  7.6 2.6 %collective-permute-done.refs_1_ = bf16[256,512]{1,0:T(8,128)(2,1)S(1)} collective-permute-done((bf16[256,512]{1,0:T(8,128)(2,1)}, bf16[256,512]{1,0:T(8,128)(2,1)S(1)}, u32[]{:S(2)}, u32[]{:S(2)}) %collective-permute-start) | collective-permute-done | bytes 262176 | tf_op jit(solution)/shard_map/ppermute | solution.py:28
  10.2 1.1 %shard_map.158 = (bf16[512,512]{1,0:T(8,128)(2,1)S(1)}, bf16[512,256]{1,0:T(8,128)(2,1)S(1)}, bf16[272,256]{1,0:T(8,128)(2,1)S(1)}, bf16[272,256]{1,0:T(8,128)(2...) custom-call(s32[1]{0:T(128)S(6)} %copy.17.tiles, s32[1,2,6]{2,1,0:T(2,128)S(1)} %bitcast.14, ...), custom_call_target="tpu_custom_call" | custom-call | flops 1024 | bytes 1024 | tf_op jit(solution)/shard_map/pallas_call | solution.py:53
  11.3 1.9 %collective-permute-start.1 = (bf16[272,256]{1,0:T(8,128)(2,1)S(1)}, bf16[272,256]{1,0:T(8,128)(2,1)S(1)}, u32[]{:S(2)}, u32[]{:S(2)}) collective-permute-start(bf16[272,256]{1,0:T(8,128)(2,1)S(1)} %get-tuple-element.96), channel_id=1, source_target_pairs={{12,0},{0,4},{4,8},{8,12},{13,1},{1,5},{5,9},{9,13},{14,2},{2,6},{... | collective-permute-start | bytes 417800 | tf_op jit(solution)/shard_map/ppermute | solution.py:28
  13.2 2.1 %collective-permute-start.2 = (bf16[272,256]{1,0:T(8,128)(2,1)S(1)}, bf16[272,256]{1,0:T(8,128)(2,1)S(1)}, u32[]{:S(2)}, u32[]{:S(2)}) collective-permute-start(bf16[272,256]{1,0:T(8,128)(2,1)S(1)} %get-tuple-element.97), channel_id=1, source_target_pairs={{4,0},{8,4},{12,8},{0,12},{5,1},{9,5},{13,9},{1,13},{6,2},{10,6},{... | collective-permute-start | bytes 417800 | tf_op jit(solution)/shard_map/ppermute | solution.py:28
  16.2 1.0 %shard_map.160 = (bf16[12,512,128]{2,1,0:T(8,128)(2,1)S(1)}, bf16[12,512,128]{2,1,0:T(8,128)(2,1)S(1)}, bf16[12,16,512]{2,1,0:T(8,128)(2,1)S(1)}, bf16[12,16,512]{2,1,0:T(8,128)(2,1)S(1)}) custom-call(s32[1]{0:T(128)S(6)} %copy.17.tiles, s32[12,512]{1,0:T(8,128)S(1)} %copy-done.6, s32[1,512]{1,0:T(1,128)S(1)} %bitcast.7), custom_call_target="tpu_custom_call" | custom-call | flops 1024 | bytes 1024 | tf_op jit(solution)/shard_map/pallas_call | solution.py:53
  17.2 2.8 %shard_map.161.before = bf16[12,512,256]{2,1,0:T(8,128)(2,1)S(1)} custom-call(bf16[12,512,128]{2,1,0:T(8,128)(2,1)S(1)} %get-tuple-element.93.low, bf16[12,512,128]{2,1,0:T(8,128)(2,1)S(1)} %get-tuple-element.94.high, bf16[512,256]{1,0:T(8,128)(2,1)S(1)} %get-tuple-element.98.proj, bf16[272,256]{1,0:T(8,128)(2,1)S(1)} %collective-permute-done.3.beside.refs_4_), custom_call_target="tpu_custom_call" | custom-call | flops 1024 | bytes 1024 | tf_op jit(solution)/shard_map/pallas_call | solution.py:53
  20.1 1.9 %collective-permute-done.2.east.refs_3_ = bf16[272,256]{1,0:T(8,128)(2,1)S(1)} collective-permute-done((bf16[272,256]{1,0:T(8,128)(2,1)S(1)}, bf16[272,256]{1,0:T(8,128)(2,1)S(1)}, u32[]{:S(2)}, u32[]{:S(2)}) %collective-permute-start.2) | collective-permute-done | bytes 139296 | tf_op jit(solution)/shard_map/ppermute | solution.py:28
  21.9 1.5 %collective-permute-start.8 = (bf16[256,512]{1,0:T(8,128)(2,1)S(1)}, bf16[256,512]{1,0:T(8,128)(2,1)S(1)}, u32[]{:S(2)}, u32[]{:S(2)}) collective-permute-start(bf16[256,512]{1,0:T(8,128)(2,1)S(1)} %copy-done.2), channel_id=1, source_target_pairs={{2,0},{0,2},{3,1},{1,3},{6,4},{4,6},{7,5},{5,7},{10,8},{8,10},{11,... | collective-permute-start | bytes 786440 | tf_op jit(solution)/shard_map/ppermute | solution.py:28
  23.9 2.5 %shard_map.162.part = bf16[12,512,256]{2,1,0:T(8,128)(2,1)S(1)} custom-call(bf16[12,512,128]{2,1,0:T(8,128)(2,1)S(1)} %get-tuple-element.93.low, bf16[12,512,128]{2,1,0:T(8,128)(2,1)S(1)} %get-tuple-element.94.high, bf16[12,512,256]{2,1,0:T(8,128)(2,1)S(1)} %shard_map.161.before, bf16[272,256]{1,0:T(8,128)(2,1)S(1)} %collective-permute-done.1.west.refs_2_, ...), custom_call_target="tpu_custom_call" | custom-call | flops 1024 | bytes 1024 | tf_op jit(solution)/shard_map/pallas_call | solution.py:53
  26.5 1.9 %collective-permute-done.4.block.cross = bf16[272,256]{1,0:T(8,128)(2,1)S(1)} collective-permute-done((bf16[272,256]{1,0:T(8,128)(2,1)S(1)}, bf16[272,256]{1,0:T(8,128)(2,1)S(1)}, u32[]{:S(2)}, u32[]{:S(2)}) %collective-permute-start.4) | collective-permute-done | bytes 139296 | tf_op jit(solution)/shard_map/ppermute | solution.py:624
  28.4 2.5 %shard_map.164 = (bf16[256,256]{1,0:T(8,128)(2,1)S(1)}, bf16[12,256,256]{2,1,0:T(8,128)(2,1)S(1)}) custom-call(bf16[12,512,128]{2,1,0:T(8,128)(2,1)S(1)} %get-tuple-element.93.low, bf16[12,512,128]{2,1,0:T(8,128)(2,1)S(1)} %get-tuple-element.94.high, f32[512,256]{1,0:T(8,128)S(1)} %shard_map.159.base, s32[1,512]{1,0:T(1,128)S(1)} %bitcast.8, ...), custom_call_target="tpu_custom_call" | custom-call | flops 1024 | bytes 1024 | tf_op jit(solution)/shard_map/pallas_call | solution.py:53
  30.9 1.6 %collective-permute-start.7 = (bf16[256,256]{1,0:T(8,128)(2,1)S(1)}, bf16[256,256]{1,0:T(8,128)(2,1)S(1)}, u32[]{:S(2)}, u32[]{:S(2)}) collective-permute-start(bf16[256,256]{1,0:T(8,128)(2,1)S(1)} %get-tuple-element.108.refs_0_), channel_id=1, source_target_pairs={{2,0},{0,2},{3,1},{1,3},{6,4},{4,6},{7,5},{5,7},{10,8},{8,10},{11,... | collective-permute-start | bytes 393224 | tf_op jit(solution)/shard_map/ppermute | solution.py:28
  32.5 2.5 %shard_map.165 = (bf16[256,256]{1,0:T(8,128)(2,1)S(1)}, bf16[12,256,256]{2,1,0:T(8,128)(2,1)S(1)}) custom-call(bf16[12,512,128]{2,1,0:T(8,128)(2,1)S(1)} %get-tuple-element.93.low, bf16[12,512,128]{2,1,0:T(8,128)(2,1)S(1)} %get-tuple-element.94.high, f32[512,256]{1,0:T(8,128)S(1)} %shard_map.159.base, s32[1,512]{1,0:T(1,128)S(1)} %bitcast.9, ...), custom_call_target="tpu_custom_call" | custom-call | flops 1024 | bytes 1024 | tf_op jit(solution)/shard_map/pallas_call | solution.py:53
  35.6 1.1 %shard_map.166 = (bf16[512,512]{1,0:T(8,128)(2,1)}, f32[512,512]{1,0:T(8,128)S(1)}, f32[512,512]{1,0:T(8,128)S(1)}) custom-call(s32[1]{0:T(128)S(6)} %copy.17.tiles, bf16[256,512]{1,0:T(8,128)(2,1)S(1)} %copy-done.2, bf16[256,512]{1,0:T(8,128)(2,1)S(1)} %collective-permute-done.8.refs_1_, bf16[512,512]{1,0:T(8,128)(2,1)S(1)} %get-tuple-element.88.feats.refs_2_, ...), custom_call_target="tpu_custom_call" | custom-call | flops 1024 | bytes 1024 | tf_op jit(solution)/shard_map/pallas_call | solution.py:53
  36.7 0.9 %shard_map.167 = (bf16[512,256]{1,0:T(8,128)(2,1)S(1)}, bf16[512,256]{1,0:T(8,128)(2,1)S(1)}, f32[256,256]{1,0:T(8,128)S(1)}) custom-call(s32[1,512]{1,0:T(1,128)S(1)} %bitcast.10, bf16[256,256]{1,0:T(8,128)(2,1)S(1)} %get-tuple-element.108.refs_0_, bf16[256,256]{1,0:T(8,128)(2,1)S(1)} %collective-permute-done.7.refs_1_, bf16[512,512]{1,0:T(8,128)(2,1)S(1)} %copy-done.1, ...), custom_call_target="tpu_custom_call" | custom-call | flops 1024 | bytes 1024 | tf_op jit(solution)/shard_map/pallas_call | solution.py:53
  37.6 1.4 %shard_map.168 = (bf16[12,256,256]{2,1,0:T(8,128)(2,1)S(1)}, f32[768,256]{1,0:T(8,128)S(1)}) custom-call(bf16[12,16,512]{2,1,0:T(8,128)(2,1)S(1)} %get-tuple-element.91.low, bf16[12,16,512]{2,1,0:T(8,128)(2,1)S(1)} %get-tuple-element.92.high, bf16[12,256,256]{2,1,0:T(8,128)(2,1)S(1)} %get-tuple-element.107.slope, f32[256,256]{1,0:T(8,128)S(1)} %get-tuple-element.117.scale), custom_call_target="tpu_custom_call" | custom-call | flops 1024 | bytes 1024 | tf_op jit(solution)/shard_map/pallas_call | solution.py:53
  39.1 1.2 %collective-permute-done.9.refs_1_ = bf16[256,256]{1,0:T(8,128)(2,1)S(1)} collective-permute-done((bf16[256,256]{1,0:T(8,128)(2,1)S(1)}, bf16[256,256]{1,0:T(8,128)(2,1)S(1)}, u32[]{:S(2)}, u32[]{:S(2)}) %collective-permute-start.9) | collective-permute-done | bytes 131104 | tf_op jit(solution)/shard_map/ppermute | solution.py:28
  41.9 1.0 %shard_map.171 = bf16[2,256,256]{2,1,0:T(8,128)(2,1)S(1)} custom-call(bf16[12,16,512]{2,1,0:T(8,128)(2,1)S(1)} %get-tuple-element.91.low, bf16[12,16,512]{2,1,0:T(8,128)(2,1)S(1)} %get-tuple-element.92.high, bf16[12,256,256]{2,1,0:T(8,128)(2,1)S(1)} %get-tuple-element.123.grads.refs_1_, f32[768,256]{1,0:T(8,128)S(1)} %get-tuple-element.122.before, ...), custom_call_target="tpu_custom_call" | custom-call | flops 1024 | bytes 1024 | tf_op jit(solution)/shard_map/pallas_call | solution.py:53
  43.0 2.6 %shard_map.172 = (bf16[256,256]{1,0:T(8,128)(2,1)S(1)}, bf16[256,256]{1,0:T(8,128)(2,1)S(1)}, bf16[256,256]{1,0:T(8,128)(2,1)S(1)}) custom-call(bf16[12,16,512]{2,1,0:T(8,128)(2,1)S(1)} %get-tuple-element.91.low, bf16[12,16,512]{2,1,0:T(8,128)(2,1)S(1)} %get-tuple-element.92.high, bf16[12,256,256]{2,1,0:T(8,128)(2,1)S(1)} %get-tuple-element.132.refs_0_, ...), custom_call_target="tpu_custom_call" | custom-call | flops 1024 | bytes 1024 | tf_op jit(solution)/shard_map/pallas_call | solution.py:53
  46.2 1.9 %collective-permute-done.10.across = bf16[256,256]{1,0:T(8,128)(2,1)S(1)} collective-permute-done((bf16[256,256]{1,0:T(8,128)(2,1)S(1)}, bf16[256,256]{1,0:T(8,128)(2,1)S(1)}, u32[]{:S(2)}, u32[]{:S(2)}) %collective-permute-start.10) | collective-permute-done | bytes 131104 | tf_op jit(solution)/shard_map/ppermute | solution.py:568
  48.2 1.5 %collective-permute-start.13 = (bf16[256,256]{1,0:T(8,128)(2,1)S(1)}, bf16[256,256]{1,0:T(8,128)(2,1)S(1)}, u32[]{:S(2)}, u32[]{:S(2)}) collective-permute-start(bf16[256,256]{1,0:T(8,128)(2,1)S(1)} %get-tuple-element.131), channel_id=1, source_target_pairs={{4,0},{8,4},{12,8},{0,12},{5,1},{9,5},{13,9},{1,13},{6,2},{10,6},{... | collective-permute-start | bytes 393224 | tf_op jit(solution)/shard_map/ppermute | solution.py:28
  50.3 2.1 %shard_map.175 = (f32[512,256]{1,0:T(8,128)S(1)}, bf16[256,512]{1,0:T(8,128)(2,1)S(1)}) custom-call(bf16[12,16,512]{2,1,0:T(8,128)(2,1)S(1)} %get-tuple-element.91.low, bf16[12,16,512]{2,1,0:T(8,128)(2,1)S(1)} %get-tuple-element.92.high, bf16[12,256,256]{2,1,0:T(8,128)(2,1)S(1)} %get-tuple-element.132.refs_0_, ...), custom_call_target="tpu_custom_call" | custom-call | flops 1024 | bytes 1024 | tf_op jit(solution)/shard_map/pallas_call | solution.py:53
  52.4 1.2 %shard_map.176 = (bf16[256,512]{1,0:T(8,128)(2,1)}, f32[256,512]{1,0:T(8,128)S(1)}) custom-call(s32[1]{0:T(128)S(6)} %copy.17.tiles, bf16[256,512]{1,0:T(8,128)(2,1)S(1)} %get-tuple-element.84.refs_0_.feats, bf16[256,512]{1,0:T(8,128)(2,1)S(1)} %copy-done.2, bf16[256,512]{1,0:T(8,128)(2,1)S(1)} %get-tuple-element.85.w_out, bf16[256,512]{1,0:T(8,128)(2,1)S(1)} %copy-done.4, ...), custom_call_target="tpu_custom_call" | custom-call | flops 1024 | bytes 1024 | tf_op jit(solution)/shard_map/pallas_call | solution.py:53
  54.4 1.1 %collective-permute-start.16 = (bf16[256,256]{1,0:T(8,128)(2,1)S(1)}, bf16[256,256]{1,0:T(8,128)(2,1)S(1)}, u32[]{:S(2)}, u32[]{:S(2)}) collective-permute-start(bf16[256,256]{1,0:T(8,128)(2,1)S(1)} %bitcast.15), channel_id=1, source_target_pairs={{2,0},{0,2},{3,1},{1,3},{6,4},{4,6},{7,5},{5,7},{10,8},{8,10},{11,... | collective-permute-start | bytes 393224 | tf_op jit(solution)/shard_map/ppermute | solution.py:28
  55.5 1.7 %collective-permute-done.14.refs_0_ = bf16[256,256]{1,0:T(8,128)(2,1)S(1)} collective-permute-done((bf16[256,256]{1,0:T(8,128)(2,1)S(1)}, bf16[256,256]{1,0:T(8,128)(2,1)S(1)}, u32[]{:S(2)}, u32[]{:S(2)}) %collective-permute-start.14) | collective-permute-done | bytes 131104 | tf_op jit(solution)/shard_map/ppermute | solution.py:28
  57.6 1.8 %collective-permute-done.16.refs_1_ = bf16[256,256]{1,0:T(8,128)(2,1)S(1)} collective-permute-done((bf16[256,256]{1,0:T(8,128)(2,1)S(1)}, bf16[256,256]{1,0:T(8,128)(2,1)S(1)}, u32[]{:S(2)}, u32[]{:S(2)}) %collective-permute-start.16) | collective-permute-done | bytes 131104 | tf_op jit(solution)/shard_map/ppermute | solution.py:28
  60.4 3.5 %collective-permute-done.17.received = bf16[2,64,256]{2,1,0:T(8,128)(2,1)S(1)} collective-permute-done((bf16[2,64,256]{2,1,0:T(8,128)(2,1)S(1)}, bf16[2,64,256]{2,1,0:T(8,128)(2,1)S(1)}, u32[]{:S(2)}, u32[]{:S(2)}) %collective-permute-start.17) | collective-permute-done | bytes 65568 | tf_op jit(solution)/shard_map/ppermute | solution.py:817
  63.9 2.9 %collective-permute-start.19 = (bf16[1,64,256]{2,1,0:T(8,128)(2,1)S(1)}, bf16[1,64,256]{2,1,0:T(8,128)(2,1)S(1)}, u32[]{:S(2)}, u32[]{:S(2)}) collective-permute-start(bf16[1,64,256]{2,1,0:T(8,128)(2,1)S(1)} %get-tuple-element.164), channel_id=1, source_target_pairs={{0,8},{4,12},{8,0},{12,4},{1,9},{5,13},{9,1},{13,5},{2,10},{6,14},... | collective-permute-start | bytes 98312 | tf_op jit(solution)/shard_map/ppermute | solution.py:817
  67.8 1.0 %collective-permute-done.19.received = bf16[1,64,256]{2,1,0:T(8,128)(2,1)S(1)} collective-permute-done((bf16[1,64,256]{2,1,0:T(8,128)(2,1)S(1)}, bf16[1,64,256]{2,1,0:T(8,128)(2,1)S(1)}, u32[]{:S(2)}, u32[]{:S(2)}) %collective-permute-start.19) | collective-permute-done | bytes 32800 | tf_op jit(solution)/shard_map/ppermute | solution.py:817
  69.4 2.8 %collective-permute-done.18.refs_1_ = bf16[256,256]{1,0:T(8,128)(2,1)S(1)} collective-permute-done((bf16[256,256]{1,0:T(8,128)(2,1)S(1)}, bf16[256,256]{1,0:T(8,128)(2,1)S(1)}, u32[]{:S(2)}, u32[]{:S(2)}) %collective-permute-start.18) | collective-permute-done | bytes 131104 | tf_op jit(solution)/shard_map/ppermute | solution.py:28
  (57 shorter events, 9.6 us)
Async XLA Ops:
  0.6 9.5 %copy-start.9 = (s32[1,6,2]{1,2,0:T(2,128)S(1)}, s32[1,6,2]{1,2,0:T(2,128)}, u32[]{:S(2)}) copy-start(s32[1,6,2]{1,2,0:T(2,128)} %param.19) | copy-start | bytes 148
  0.6 15.1 %copy-start.7 = (f32[512]{0:T(512)S(1)}, f32[512]{0:T(512)}, u32[]{:S(2)}) copy-start(f32[512]{0:T(512)} %param.22) | copy-start | bytes 6148
  0.7 9.5 %collective-permute-start = (bf16[256,512]{1,0:T(8,128)(2,1)}, bf16[256,512]{1,0:T(8,128)(2,1)S(1)}, u32[]{:S(2)}, u32[]{:S(2)}) collective-permute-start(bf16[256,512]{1,0:T(8,128)(2,1)} %refs_2_.1), channel_id=1, source_target_pairs={{2,0},{0,2},{3,1},{1,3},{6,4},{4,6},{7,5},{5,7},{10,8},{8,10},{11,... | collective-permute-start | bytes 786440 | tf_op jit(solution)/shard_map/ppermute | solution.py:28
  6.9 9.2 %copy-start.5 = (s32[512]{0:T(512)S(1)}, s32[512]{0:T(512)}, u32[]{:S(2)}) copy-start(s32[512]{0:T(512)} %param.17) | copy-start | bytes 6148
  6.9 9.2 %copy-start.6 = (s32[12,512]{1,0:T(8,128)S(1)}, s32[12,512]{1,0:T(8,128)}, u32[]{:S(2)}) copy-start(s32[12,512]{1,0:T(8,128)} %senders) | copy-start | bytes 73732
  11.3 5.9 %collective-permute-start.3 = (bf16[272,256]{1,0:T(8,128)(2,1)S(1)}, bf16[272,256]{1,0:T(8,128)(2,1)S(1)}, u32[]{:S(2)}, u32[]{:S(2)}) collective-permute-start(bf16[272,256]{1,0:T(8,128)(2,1)S(1)} %get-tuple-element.99), channel_id=1, source_target_pairs={{1,0},{0,1},{3,2},{2,3},{5,4},{4,5},{7,6},{6,7},{9,8},{8,9},{11,10... | collective-permute-start | bytes 417800 | tf_op jit(solution)/shard_map/ppermute | solution.py:28
  11.3 8.7 %collective-permute-start.1 = (bf16[272,256]{1,0:T(8,128)(2,1)S(1)}, bf16[272,256]{1,0:T(8,128)(2,1)S(1)}, u32[]{:S(2)}, u32[]{:S(2)}) collective-permute-start(bf16[272,256]{1,0:T(8,128)(2,1)S(1)} %get-tuple-element.96), channel_id=1, source_target_pairs={{12,0},{0,4},{4,8},{8,12},{13,1},{1,5},{5,9},{9,13},{14,2},{2,6},{... | collective-permute-start | bytes 417800 | tf_op jit(solution)/shard_map/ppermute | solution.py:28
  13.2 8.7 %collective-permute-start.2 = (bf16[272,256]{1,0:T(8,128)(2,1)S(1)}, bf16[272,256]{1,0:T(8,128)(2,1)S(1)}, u32[]{:S(2)}, u32[]{:S(2)}) collective-permute-start(bf16[272,256]{1,0:T(8,128)(2,1)S(1)} %get-tuple-element.97), channel_id=1, source_target_pairs={{4,0},{8,4},{12,8},{0,12},{5,1},{9,5},{13,9},{1,13},{6,2},{10,6},{... | collective-permute-start | bytes 417800 | tf_op jit(solution)/shard_map/ppermute | solution.py:28
  15.3 13.1 %collective-permute-start.4 = (bf16[272,256]{1,0:T(8,128)(2,1)S(1)}, bf16[272,256]{1,0:T(8,128)(2,1)S(1)}, u32[]{:S(2)}, u32[]{:S(2)}) collective-permute-start(bf16[272,256]{1,0:T(8,128)(2,1)S(1)} %get-tuple-element.104), channel_id=1, source_target_pairs={{0,9},{1,8},{4,13},{5,12},{8,1},{9,0},{12,5},{13,4},{2,11},{3,10},... | collective-permute-start | bytes 417800 | tf_op jit(solution)/shard_map/ppermute | solution.py:624
  17.2 4.7 %copy-start.2 = (bf16[256,512]{1,0:T(8,128)(2,1)S(1)}, bf16[256,512]{1,0:T(8,128)(2,1)}, u32[]{:S(2)}) copy-start(bf16[256,512]{1,0:T(8,128)(2,1)} %cots.1) | copy-start | bytes 786436
  21.9 13.1 %collective-permute-start.8 = (bf16[256,512]{1,0:T(8,128)(2,1)S(1)}, bf16[256,512]{1,0:T(8,128)(2,1)S(1)}, u32[]{:S(2)}, u32[]{:S(2)}) collective-permute-start(bf16[256,512]{1,0:T(8,128)(2,1)S(1)} %copy-done.2), channel_id=1, source_target_pairs={{2,0},{0,2},{3,1},{1,3},{6,4},{4,6},{7,5},{5,7},{10,8},{8,10},{11,... | collective-permute-start | bytes 786440 | tf_op jit(solution)/shard_map/ppermute | solution.py:28
  23.4 5.0 %collective-permute-start.5 = (bf16[272,256]{1,0:T(8,128)(2,1)S(1)}, bf16[272,256]{1,0:T(8,128)(2,1)S(1)}, u32[]{:S(2)}, u32[]{:S(2)}) collective-permute-start(bf16[272,256]{1,0:T(8,128)(2,1)S(1)} %collective-permute-done.1.west.refs_2_), channel_id=1, source_target_pairs={{1,0},{0,1},{3,2},{2,3},{5,4},{4,5},{7,6},{6,7},{9,8},{8,9},{11,10... | collective-permute-start | bytes 417800 | tf_op jit(solution)/shard_map/ppermute | solution.py:28
  23.4 5.0 %collective-permute-start.6 = (bf16[272,256]{1,0:T(8,128)(2,1)S(1)}, bf16[272,256]{1,0:T(8,128)(2,1)S(1)}, u32[]{:S(2)}, u32[]{:S(2)}) collective-permute-start(bf16[272,256]{1,0:T(8,128)(2,1)S(1)} %collective-permute-done.2.east.refs_3_), channel_id=1, source_target_pairs={{1,0},{0,1},{3,2},{2,3},{5,4},{4,5},{7,6},{6,7},{9,8},{8,9},{11,10... | collective-permute-start | bytes 417800 | tf_op jit(solution)/shard_map/ppermute | solution.py:28
  30.9 4.7 %copy-start = (bf16[512,512]{1,0:T(8,128)(2,1)S(1)}, bf16[512,512]{1,0:T(8,128)(2,1)}, u32[]{:S(2)}) copy-start(bf16[512,512]{1,0:T(8,128)(2,1)} %refs_3_.3) | copy-start | bytes 1572868
  30.9 4.7 %copy-start.3 = (bf16[512,512]{1,0:T(8,128)(2,1)S(1)}, bf16[512,512]{1,0:T(8,128)(2,1)}, u32[]{:S(2)}) copy-start(bf16[512,512]{1,0:T(8,128)(2,1)} %get-tuple-element.114.refs_5_) | copy-start | bytes 1572868
  30.9 4.7 %copy-start.8 = (f32[512]{0:T(512)S(1)}, f32[512]{0:T(512)}, u32[]{:S(2)}) copy-start(f32[512]{0:T(512)} %param.26) | copy-start | bytes 6148
  30.9 5.8 %collective-permute-start.7 = (bf16[256,256]{1,0:T(8,128)(2,1)S(1)}, bf16[256,256]{1,0:T(8,128)(2,1)S(1)}, u32[]{:S(2)}, u32[]{:S(2)}) collective-permute-start(bf16[256,256]{1,0:T(8,128)(2,1)S(1)} %get-tuple-element.108.refs_0_), channel_id=1, source_target_pairs={{2,0},{0,2},{3,1},{1,3},{6,4},{4,6},{7,5},{5,7},{10,8},{8,10},{11,... | collective-permute-start | bytes 393224 | tf_op jit(solution)/shard_map/ppermute | solution.py:28
  35.0 1.7 %copy-start.1 = (bf16[512,512]{1,0:T(8,128)(2,1)S(1)}, bf16[512,512]{1,0:T(8,128)(2,1)}, u32[]{:S(2)}) copy-start(bf16[512,512]{1,0:T(8,128)(2,1)} %get-tuple-element.109.refs_2_) | copy-start | bytes 1572868
  35.0 5.3 %collective-permute-start.9 = (bf16[256,256]{1,0:T(8,128)(2,1)S(1)}, bf16[256,256]{1,0:T(8,128)(2,1)S(1)}, u32[]{:S(2)}, u32[]{:S(2)}) collective-permute-start(bf16[256,256]{1,0:T(8,128)(2,1)S(1)} %get-tuple-element.120.refs_0_), channel_id=1, source_target_pairs={{2,0},{0,2},{3,1},{1,3},{6,4},{4,6},{7,5},{5,7},{10,8},{8,10},{11,... | collective-permute-start | bytes 393224 | tf_op jit(solution)/shard_map/ppermute | solution.py:28
  41.8 6.3 %collective-permute-start.10 = (bf16[256,256]{1,0:T(8,128)(2,1)S(1)}, bf16[256,256]{1,0:T(8,128)(2,1)S(1)}, u32[]{:S(2)}, u32[]{:S(2)}) collective-permute-start(bf16[256,256]{1,0:T(8,128)(2,1)S(1)} %get-tuple-element.127), channel_id=1, source_target_pairs={{0,13},{1,4},{4,1},{5,8},{8,5},{9,12},{12,9},{13,0},{2,15},{3,6},{... | collective-permute-start | bytes 393224 | tf_op jit(solution)/shard_map/ppermute | solution.py:568
  42.9 5.2 %collective-permute-start.11 = (bf16[2,256,256]{2,1,0:T(8,128)(2,1)S(1)}, bf16[2,256,256]{2,1,0:T(8,128)(2,1)S(1)}, u32[]{:S(2)}, u32[]{:S(2)}) collective-permute-start(bf16[2,256,256]{2,1,0:T(8,128)(2,1)S(1)} %shard_map.171), channel_id=1, source_target_pairs={{1,0},{0,1},{3,2},{2,3},{5,4},{4,5},{7,6},{6,7},{9,8},{8,9},{11,10... | collective-permute-start | bytes 786440 | tf_op jit(solution)/shard_map/ppermute | solution.py:28
  45.6 7.9 %collective-permute-start.12 = (bf16[256,256]{1,0:T(8,128)(2,1)S(1)}, bf16[256,256]{1,0:T(8,128)(2,1)S(1)}, u32[]{:S(2)}, u32[]{:S(2)}) collective-permute-start(bf16[256,256]{1,0:T(8,128)(2,1)S(1)} %get-tuple-element.141), channel_id=1, source_target_pairs={{1,0},{0,1},{3,2},{2,3},{5,4},{4,5},{7,6},{6,7},{9,8},{8,9},{11,10... | collective-permute-start | bytes 393224 | tf_op jit(solution)/shard_map/ppermute | solution.py:28
  48.2 5.4 %collective-permute-start.13 = (bf16[256,256]{1,0:T(8,128)(2,1)S(1)}, bf16[256,256]{1,0:T(8,128)(2,1)S(1)}, u32[]{:S(2)}, u32[]{:S(2)}) collective-permute-start(bf16[256,256]{1,0:T(8,128)(2,1)S(1)} %get-tuple-element.131), channel_id=1, source_target_pairs={{4,0},{8,4},{12,8},{0,12},{5,1},{9,5},{13,9},{1,13},{6,2},{10,6},{... | collective-permute-start | bytes 393224 | tf_op jit(solution)/shard_map/ppermute | solution.py:28
  49.8 2.6 %copy-start.4 = (bf16[256,512]{1,0:T(8,128)(2,1)S(1)}, bf16[256,512]{1,0:T(8,128)(2,1)}, u32[]{:S(2)}) copy-start(bf16[256,512]{1,0:T(8,128)(2,1)} %get-tuple-element.86.w_node_v_t) | copy-start | bytes 786436
  49.8 7.4 %collective-permute-start.14 = (bf16[256,256]{1,0:T(8,128)(2,1)S(1)}, bf16[256,256]{1,0:T(8,128)(2,1)S(1)}, u32[]{:S(2)}, u32[]{:S(2)}) collective-permute-start(bf16[256,256]{1,0:T(8,128)(2,1)S(1)} %get-tuple-element.142), channel_id=1, source_target_pairs={{12,0},{0,4},{4,8},{8,12},{13,1},{1,5},{5,9},{9,13},{14,2},{2,6},{... | collective-permute-start | bytes 393224 | tf_op jit(solution)/shard_map/ppermute | solution.py:28
  54.4 5.1 %collective-permute-start.16 = (bf16[256,256]{1,0:T(8,128)(2,1)S(1)}, bf16[256,256]{1,0:T(8,128)(2,1)S(1)}, u32[]{:S(2)}, u32[]{:S(2)}) collective-permute-start(bf16[256,256]{1,0:T(8,128)(2,1)S(1)} %bitcast.15), channel_id=1, source_target_pairs={{2,0},{0,2},{3,1},{1,3},{6,4},{4,6},{7,5},{5,7},{10,8},{8,10},{11,... | collective-permute-start | bytes 393224 | tf_op jit(solution)/shard_map/ppermute | solution.py:28
  57.5 1.9 %collective-permute-start.15 = (bf16[4,64,256]{2,1,0:T(8,128)(2,1)S(1)}, bf16[4,64,256]{2,1,0:T(8,128)(2,1)S(1)}, u32[]{:S(2)}, u32[]{:S(2)}) collective-permute-start(bf16[4,64,256]{2,1,0:T(8,128)(2,1)S(1)} %get-tuple-element.152), channel_id=1, source_target_pairs={{1,0},{0,1},{3,2},{2,3},{5,4},{4,5},{7,6},{6,7},{9,8},{8,9},{11,10... | collective-permute-start | bytes 393224 | tf_op jit(solution)/shard_map/ppermute | solution.py:28
  59.5 4.3 %collective-permute-start.17 = (bf16[2,64,256]{2,1,0:T(8,128)(2,1)S(1)}, bf16[2,64,256]{2,1,0:T(8,128)(2,1)S(1)}, u32[]{:S(2)}, u32[]{:S(2)}) collective-permute-start(bf16[2,64,256]{2,1,0:T(8,128)(2,1)S(1)} %get-tuple-element.156), channel_id=1, source_target_pairs={{0,4},{4,0},{8,12},{12,8},{1,5},{5,1},{9,13},{13,9},{2,6},{6,2},{1... | collective-permute-start | bytes 196616 | tf_op jit(solution)/shard_map/ppermute | solution.py:817
  63.9 4.9 %collective-permute-start.19 = (bf16[1,64,256]{2,1,0:T(8,128)(2,1)S(1)}, bf16[1,64,256]{2,1,0:T(8,128)(2,1)S(1)}, u32[]{:S(2)}, u32[]{:S(2)}) collective-permute-start(bf16[1,64,256]{2,1,0:T(8,128)(2,1)S(1)} %get-tuple-element.164), channel_id=1, source_target_pairs={{0,8},{4,12},{8,0},{12,4},{1,9},{5,13},{9,1},{13,5},{2,10},{6,14},... | collective-permute-start | bytes 98312 | tf_op jit(solution)/shard_map/ppermute | solution.py:817
  67.2 5.0 %collective-permute-start.18 = (bf16[256,256]{1,0:T(8,128)(2,1)S(1)}, bf16[256,256]{1,0:T(8,128)(2,1)S(1)}, u32[]{:S(2)}, u32[]{:S(2)}) collective-permute-start(bf16[256,256]{1,0:T(8,128)(2,1)S(1)} %bitcast.16), channel_id=1, source_target_pairs={{2,0},{0,2},{3,1},{1,3},{6,4},{4,6},{7,5},{5,7},{10,8},{8,10},{11,... | collective-permute-start | bytes 393224 | tf_op jit(solution)/shard_map/ppermute | solution.py:28

commit v12 on v8

--- a/solution.py
+++ b/solution.py
@@ -481,7 +481,7 @@
     lon = lax.axis_index("lon")
     lons, columns, _ = w_mine.shape
     for k in range(lons):
-        band = lax.rem(lon + k, lons) * 2
+        band = (lon ^ k) * 2
         for out, core in ((w_mine, sub), (w_beside, 1 - sub)):
             spot = pl.multiple_of((band + core) * columns, columns)
             out[k] = weight[pl.ds(spot, columns), :].astype(out.dtype)
@@ -512,17 +512,16 @@
         start += part.shape[1]
 
 
-def sum_kernel(w_mine, w_beside, near, sent):
-    near[...] = w_mine[0] + w_beside[0].astype(jnp.float32)
-    for k in range(sent.shape[0]):
-        sent[k] = (w_mine[k + 1] + w_beside[k + 1].astype(jnp.float32)).astype(jnp.bfloat16)
+def sum_kernel(held, received, near, sent):
+    near[...] = held[0] + received[0].astype(jnp.float32)
+    sent[...] = (held[1:] + received[1:].astype(jnp.float32)).astype(jnp.bfloat16)
 
 
 def weight_kernel(near, *refs):
-    out = refs[-1]
+    *terms, out = refs
     total = near[...]
-    for ref in refs[:-1]:
-        total += ref[...].astype(jnp.float32)
+    for term in terms:
+        total += term[...].astype(jnp.float32)
     out[...] = total
 
 
@@ -808,10 +807,11 @@
         [w_mine, w_beside],
         scalars=0,
     )
-    w_terms = [shifted(w_sent[k - 1], "lon", k) for k in range(1, lons)]
-    grad_w_send = call(
-        weight_kernel, shape((columns, hid), f32), [near] + w_terms, scalars=0
-    )
+    w_terms = [
+        lax.ppermute(w_sent[k - 1], "lon", [(i, i ^ k) for i in range(lons)])
+        for k in range(1, lons)
+    ]
+    grad_w_send = call(weight_kernel, shape((columns, hid), f32), [near] + w_terms, scalars=0)
     return (updated, grad_features, grad_w_send.T)
 
 

time: 70.6 us -> 69.7 us (0.987)
  waiting for transfers between devices: 16.8 us -> 15.9 us
    ppermute x0 -> x3, starting transfers between devices: none -> 5.24 us  [shards(): lax.ppermute(w_sent[k - 1], 'lon', [(i, i ^ k) for i in range(lons)])]
    ppermute x19 -> x16, starting transfers between devices: 20.7 us -> 15.5 us  [shifted(): return lax.ppermute(block, axis, route)]
    ppermute x19 -> x16, waiting for transfers between devices: 14.3 us -> 9.92 us  [shifted(): return lax.ppermute(block, axis, route)]
    ppermute x0 -> x3, waiting for transfers between devices: none -> 3.44 us  [shards(): lax.ppermute(w_sent[k - 1], 'lon', [(i, i ^ k) for i in range(lons)])]
  transfers between devices with their start and end apart: 21 -> 21, of which waited for: 12 -> 11; matrix products, arithmetic and copies ran while one was open for 0% -> 0% of each run, Pallas kernels for 36% -> 36%
where the time goes in v12:
time: 69.7 us; the launch traced here: 69.5 us
  Pallas kernels  31 us (44%)
  starting transfers between devices  21 us (30%)
  waiting for transfers between devices  15.9 us (23%)
  between operations  1.68 us (2%)
    pallas_call x28, Pallas kernels, call(): pl.pallas_call(kernel, out_shape=out_shape, in_specs=[smem] * scalars + [...  31 us
    ppermute x16, starting transfers between devices, shifted(): return lax.ppermute(block, axis, route)  15.5 us
    ppermute x16, waiting for transfers between devices, shifted(): return lax.ppermute(block, axis, route)  9.92 us
    ppermute x3, starting transfers between devices, shards(): lax.ppermute(w_sent[k - 1], 'lon', [(i, i ^ k) for i in range(lons)])  5.24 us
    ppermute x3, waiting for transfers between devices, shards(): lax.ppermute(w_sent[k - 1], 'lon', [(i, i ^ k) for i in range(lons)])  3.44 us
    ppermute x1, waiting for transfers between devices, shards(): across = lambda block: lax.ppermute(block, cycle, across_route)  1.85 us
  transfers between devices with their start and end apart: 21, of which 11 were waited for; matrix products, arithmetic and copies ran while one was open for 0% of the time, Pallas kernels for 36%

profile of v12, /device:TPU:0, one launch (start us, length us, event | category | flops | bytes accessed | tf_op | source)
XLA Modules:
  0.0 69.5 jit_solution(3047285829811345511)
XLA Ops:
  0.7 3.0 %collective-permute-start = (bf16[256,512]{1,0:T(8,128)(2,1)}, bf16[256,512]{1,0:T(8,128)(2,1)S(1)}, u32[]{:S(2)}, u32[]{:S(2)}) collective-permute-start(bf16[256,512]{1,0:T(8,128)(2,1)} %refs_2_.1), channel_id=1, source_target_pairs={{2,0},{0,2},{3,1},{1,3},{6,4},{4,6},{7,5},{5,7},{10,8},{8,10},{11,... | collective-permute-start | bytes 786440 | tf_op jit(solution)/shard_map/ppermute | solution.py:26
  3.7 3.3 %shard_map.157 = (bf16[256,512]{1,0:T(8,128)(2,1)S(1)}, bf16[256,512]{1,0:T(8,128)(2,1)S(1)}, bf16[256,512]{1,0:T(8,128)(2,1)S(1)}, bf16[256,512]{1,0:T(8,128)(2...) custom-call(bf16[512,512]{1,0:T(8,128)(2,1)} %refs_0_.1, ...), custom_call_target="tpu_custom_call" | custom-call | flops 1024 | bytes 1024 | tf_op jit(solution)/shard_map/pallas_call | solution.py:51
  7.6 2.5 %collective-permute-done.refs_1_ = bf16[256,512]{1,0:T(8,128)(2,1)S(1)} collective-permute-done((bf16[256,512]{1,0:T(8,128)(2,1)}, bf16[256,512]{1,0:T(8,128)(2,1)S(1)}, u32[]{:S(2)}, u32[]{:S(2)}) %collective-permute-start) | collective-permute-done | bytes 262176 | tf_op jit(solution)/shard_map/ppermute | solution.py:26
  10.2 1.1 %shard_map.158 = (bf16[512,512]{1,0:T(8,128)(2,1)S(1)}, bf16[512,256]{1,0:T(8,128)(2,1)S(1)}, bf16[272,256]{1,0:T(8,128)(2,1)S(1)}, bf16[272,256]{1,0:T(8,128)(2...) custom-call(s32[1]{0:T(128)S(6)} %copy.17.tiles, s32[1,2,6]{2,1,0:T(2,128)S(1)} %bitcast.20, ...), custom_call_target="tpu_custom_call" | custom-call | flops 1024 | bytes 1024 | tf_op jit(solution)/shard_map/pallas_call | solution.py:51
  11.3 1.9 %collective-permute-start.1 = (bf16[272,256]{1,0:T(8,128)(2,1)S(1)}, bf16[272,256]{1,0:T(8,128)(2,1)S(1)}, u32[]{:S(2)}, u32[]{:S(2)}) collective-permute-start(bf16[272,256]{1,0:T(8,128)(2,1)S(1)} %get-tuple-element.92), channel_id=1, source_target_pairs={{12,0},{0,4},{4,8},{8,12},{13,1},{1,5},{5,9},{9,13},{14,2},{2,6},{... | collective-permute-start | bytes 417800 | tf_op jit(solution)/shard_map/ppermute | solution.py:26
  13.2 2.1 %collective-permute-start.2 = (bf16[272,256]{1,0:T(8,128)(2,1)S(1)}, bf16[272,256]{1,0:T(8,128)(2,1)S(1)}, u32[]{:S(2)}, u32[]{:S(2)}) collective-permute-start(bf16[272,256]{1,0:T(8,128)(2,1)S(1)} %get-tuple-element.93), channel_id=1, source_target_pairs={{4,0},{8,4},{12,8},{0,12},{5,1},{9,5},{13,9},{1,13},{6,2},{10,6},{... | collective-permute-start | bytes 417800 | tf_op jit(solution)/shard_map/ppermute | solution.py:26
  15.7 1.7 %collective-permute-start.4 = (bf16[256,512]{1,0:T(8,128)(2,1)S(1)}, bf16[256,512]{1,0:T(8,128)(2,1)S(1)}, u32[]{:S(2)}, u32[]{:S(2)}) collective-permute-start(bf16[256,512]{1,0:T(8,128)(2,1)S(1)} %copy-done.2), channel_id=1, source_target_pairs={{2,0},{0,2},{3,1},{1,3},{6,4},{4,6},{7,5},{5,7},{10,8},{8,10},{11,... | collective-permute-start | bytes 786440 | tf_op jit(solution)/shard_map/ppermute | solution.py:26
  17.4 1.0 %shard_map.160 = (bf16[12,512,128]{2,1,0:T(8,128)(2,1)S(1)}, bf16[12,512,128]{2,1,0:T(8,128)(2,1)S(1)}, bf16[12,16,512]{2,1,0:T(8,128)(2,1)S(1)}, bf16[12,16,512]{2,1,0:T(8,128)(2,1)S(1)}) custom-call(s32[1]{0:T(128)S(6)} %copy.17.tiles, s32[12,512]{1,0:T(8,128)S(1)} %copy-done.6, s32[1,512]{1,0:T(1,128)S(1)} %bitcast.13), custom_call_target="tpu_custom_call" | custom-call | flops 1024 | bytes 1024 | tf_op jit(solution)/shard_map/pallas_call | solution.py:51
  18.5 2.9 %shard_map.161.before = bf16[12,512,256]{2,1,0:T(8,128)(2,1)S(1)} custom-call(bf16[12,512,128]{2,1,0:T(8,128)(2,1)S(1)} %get-tuple-element.89.low, bf16[12,512,128]{2,1,0:T(8,128)(2,1)S(1)} %get-tuple-element.90.high, bf16[512,256]{1,0:T(8,128)(2,1)S(1)} %get-tuple-element.94.proj, bf16[272,256]{1,0:T(8,128)(2,1)S(1)} %collective-permute-done.3.beside.refs_4_), custom_call_target="tpu_custom_call" | custom-call | flops 1024 | bytes 1024 | tf_op jit(solution)/shard_map/pallas_call | solution.py:51
  22.4 1.6 %collective-permute-done.4.refs_1_ = bf16[256,512]{1,0:T(8,128)(2,1)S(1)} collective-permute-done((bf16[256,512]{1,0:T(8,128)(2,1)S(1)}, bf16[256,512]{1,0:T(8,128)(2,1)S(1)}, u32[]{:S(2)}, u32[]{:S(2)}) %collective-permute-start.4) | collective-permute-done | bytes 262176 | tf_op jit(solution)/shard_map/ppermute | solution.py:26
  24.1 1.1 %shard_map.162 = (bf16[512,512]{1,0:T(8,128)(2,1)}, f32[512,512]{1,0:T(8,128)S(1)}, f32[512,512]{1,0:T(8,128)S(1)}) custom-call(s32[1]{0:T(128)S(6)} %copy.17.tiles, bf16[256,512]{1,0:T(8,128)(2,1)S(1)} %copy-done.2, bf16[256,512]{1,0:T(8,128)(2,1)S(1)} %collective-permute-done.4.refs_1_, bf16[512,512]{1,0:T(8,128)(2,1)S(1)} %get-tuple-element.84.feats.refs_2_, ...), custom_call_target="tpu_custom_call" | custom-call | flops 1024 | bytes 1024 | tf_op jit(solution)/shard_map/pallas_call | solution.py:51
  25.2 2.5 %shard_map.163.part = bf16[12,512,256]{2,1,0:T(8,128)(2,1)S(1)} custom-call(bf16[12,512,128]{2,1,0:T(8,128)(2,1)S(1)} %get-tuple-element.89.low, bf16[12,512,128]{2,1,0:T(8,128)(2,1)S(1)} %get-tuple-element.90.high, bf16[12,512,256]{2,1,0:T(8,128)(2,1)S(1)} %shard_map.161.before, bf16[272,256]{1,0:T(8,128)(2,1)S(1)} %collective-permute-done.1.west.refs_2_, ...), custom_call_target="tpu_custom_call" | custom-call | flops 1024 | bytes 1024 | tf_op jit(solution)/shard_map/pallas_call | solution.py:51
  28.4 2.5 %shard_map.165 = (bf16[256,256]{1,0:T(8,128)(2,1)S(1)}, bf16[12,256,256]{2,1,0:T(8,128)(2,1)S(1)}) custom-call(bf16[12,512,128]{2,1,0:T(8,128)(2,1)S(1)} %get-tuple-element.89.low, bf16[12,512,128]{2,1,0:T(8,128)(2,1)S(1)} %get-tuple-element.90.high, f32[512,256]{1,0:T(8,128)S(1)} %shard_map.159.base, s32[1,512]{1,0:T(1,128)S(1)} %bitcast.14, ...), custom_call_target="tpu_custom_call" | custom-call | flops 1024 | bytes 1024 | tf_op jit(solution)/shard_map/pallas_call | solution.py:51
  30.9 1.6 %collective-permute-start.8 = (bf16[256,256]{1,0:T(8,128)(2,1)S(1)}, bf16[256,256]{1,0:T(8,128)(2,1)S(1)}, u32[]{:S(2)}, u32[]{:S(2)}) collective-permute-start(bf16[256,256]{1,0:T(8,128)(2,1)S(1)} %get-tuple-element.107.refs_0_), channel_id=1, source_target_pairs={{2,0},{0,2},{3,1},{1,3},{6,4},{4,6},{7,5},{5,7},{10,8},{8,10},{11,... | collective-permute-start | bytes 393224 | tf_op jit(solution)/shard_map/ppermute | solution.py:26
  32.5 2.5 %shard_map.168 = (bf16[256,256]{1,0:T(8,128)(2,1)S(1)}, bf16[12,256,256]{2,1,0:T(8,128)(2,1)S(1)}) custom-call(bf16[12,512,128]{2,1,0:T(8,128)(2,1)S(1)} %get-tuple-element.89.low, bf16[12,512,128]{2,1,0:T(8,128)(2,1)S(1)} %get-tuple-element.90.high, f32[512,256]{1,0:T(8,128)S(1)} %shard_map.159.base, s32[1,512]{1,0:T(1,128)S(1)} %bitcast.15, ...), custom_call_target="tpu_custom_call" | custom-call | flops 1024 | bytes 1024 | tf_op jit(solution)/shard_map/pallas_call | solution.py:51
  35.5 1.0 %collective-permute-done.8.refs_1_ = bf16[256,256]{1,0:T(8,128)(2,1)S(1)} collective-permute-done((bf16[256,256]{1,0:T(8,128)(2,1)S(1)}, bf16[256,256]{1,0:T(8,128)(2,1)S(1)}, u32[]{:S(2)}, u32[]{:S(2)}) %collective-permute-start.8) | collective-permute-done | bytes 131104 | tf_op jit(solution)/shard_map/ppermute | solution.py:26
  36.5 0.9 %shard_map.166 = (bf16[512,256]{1,0:T(8,128)(2,1)S(1)}, bf16[512,256]{1,0:T(8,128)(2,1)S(1)}, f32[256,256]{1,0:T(8,128)S(1)}) custom-call(s32[1,512]{1,0:T(1,128)S(1)} %bitcast.16, bf16[256,256]{1,0:T(8,128)(2,1)S(1)} %get-tuple-element.107.refs_0_, bf16[256,256]{1,0:T(8,128)(2,1)S(1)} %collective-permute-done.8.refs_1_, bf16[512,512]{1,0:T(8,128)(2,1)S(1)} %copy-done.1, ...), custom_call_target="tpu_custom_call" | custom-call | flops 1024 | bytes 1024 | tf_op jit(solution)/shard_map/pallas_call | solution.py:51
  37.4 1.4 %shard_map.167 = (bf16[12,256,256]{2,1,0:T(8,128)(2,1)S(1)}, f32[768,256]{1,0:T(8,128)S(1)}) custom-call(bf16[12,16,512]{2,1,0:T(8,128)(2,1)S(1)} %get-tuple-element.87.low, bf16[12,16,512]{2,1,0:T(8,128)(2,1)S(1)} %get-tuple-element.88.high, bf16[12,256,256]{2,1,0:T(8,128)(2,1)S(1)} %get-tuple-element.106.slope, f32[256,256]{1,0:T(8,128)S(1)} %get-tuple-element.112.scale), custom_call_target="tpu_custom_call" | custom-call | flops 1024 | bytes 1024 | tf_op jit(solution)/shard_map/pallas_call | solution.py:51
  38.9 1.4 %collective-permute-done.9.refs_1_ = bf16[256,256]{1,0:T(8,128)(2,1)S(1)} collective-permute-done((bf16[256,256]{1,0:T(8,128)(2,1)S(1)}, bf16[256,256]{1,0:T(8,128)(2,1)S(1)}, u32[]{:S(2)}, u32[]{:S(2)}) %collective-permute-start.9) | collective-permute-done | bytes 131104 | tf_op jit(solution)/shard_map/ppermute | solution.py:26
  40.2 0.8 %shard_map.169 = (bf16[512,256]{1,0:T(8,128)(2,1)S(1)}, bf16[512,256]{1,0:T(8,128)(2,1)S(1)}, f32[256,256]{1,0:T(8,128)S(1)}) custom-call(s32[1,512]{1,0:T(1,128)S(1)} %bitcast.17, bf16[256,256]{1,0:T(8,128)(2,1)S(1)} %get-tuple-element.115.refs_0_, bf16[256,256]{1,0:T(8,128)(2,1)S(1)} %collective-permute-done.9.refs_1_, bf16[512,512]{1,0:T(8,128)(2,1)S(1)} %copy-done.1, ...), custom_call_target="tpu_custom_call" | custom-call | flops 1024 | bytes 1024 | tf_op jit(solution)/shard_map/pallas_call | solution.py:51
  41.0 0.7 %shard_map.170 = (bf16[256,256]{1,0:T(8,128)(2,1)S(1)}, bf16[12,256,256]{2,1,0:T(8,128)(2,1)S(1)}) custom-call(bf16[12,16,512]{2,1,0:T(8,128)(2,1)S(1)} %get-tuple-element.87.low, bf16[12,16,512]{2,1,0:T(8,128)(2,1)S(1)} %get-tuple-element.88.high, bf16[12,256,256]{2,1,0:T(8,128)(2,1)S(1)} %get-tuple-element.114.slope, ...), custom_call_target="tpu_custom_call" | custom-call | flops 1024 | bytes 1024 | tf_op jit(solution)/shard_map/pallas_call | solution.py:51
  41.9 1.0 %shard_map.171 = bf16[2,256,256]{2,1,0:T(8,128)(2,1)S(1)} custom-call(bf16[12,16,512]{2,1,0:T(8,128)(2,1)S(1)} %get-tuple-element.87.low, bf16[12,16,512]{2,1,0:T(8,128)(2,1)S(1)} %get-tuple-element.88.high, bf16[12,256,256]{2,1,0:T(8,128)(2,1)S(1)} %get-tuple-element.118.grads.refs_1_, f32[768,256]{1,0:T(8,128)S(1)} %get-tuple-element.117.before, ...), custom_call_target="tpu_custom_call" | custom-call | flops 1024 | bytes 1024 | tf_op jit(solution)/shard_map/pallas_call | solution.py:51
  43.0 2.6 %shard_map.172 = (bf16[256,256]{1,0:T(8,128)(2,1)S(1)}, bf16[256,256]{1,0:T(8,128)(2,1)S(1)}, bf16[256,256]{1,0:T(8,128)(2,1)S(1)}) custom-call(bf16[12,16,512]{2,1,0:T(8,128)(2,1)S(1)} %get-tuple-element.87.low, bf16[12,16,512]{2,1,0:T(8,128)(2,1)S(1)} %get-tuple-element.88.high, bf16[12,256,256]{2,1,0:T(8,128)(2,1)S(1)} %get-tuple-element.127.refs_0_, ...), custom_call_target="tpu_custom_call" | custom-call | flops 1024 | bytes 1024 | tf_op jit(solution)/shard_map/pallas_call | solution.py:51
  46.2 1.8 %collective-permute-done.10.across = bf16[256,256]{1,0:T(8,128)(2,1)S(1)} collective-permute-done((bf16[256,256]{1,0:T(8,128)(2,1)S(1)}, bf16[256,256]{1,0:T(8,128)(2,1)S(1)}, u32[]{:S(2)}, u32[]{:S(2)}) %collective-permute-start.10) | collective-permute-done | bytes 131104 | tf_op jit(solution)/shard_map/ppermute | solution.py:561
  48.2 1.5 %collective-permute-start.13 = (bf16[256,256]{1,0:T(8,128)(2,1)S(1)}, bf16[256,256]{1,0:T(8,128)(2,1)S(1)}, u32[]{:S(2)}, u32[]{:S(2)}) collective-permute-start(bf16[256,256]{1,0:T(8,128)(2,1)S(1)} %get-tuple-element.126), channel_id=1, source_target_pairs={{4,0},{8,4},{12,8},{0,12},{5,1},{9,5},{13,9},{1,13},{6,2},{10,6},{... | collective-permute-start | bytes 393224 | tf_op jit(solution)/shard_map/ppermute | solution.py:26
  50.3 2.1 %shard_map.175 = (f32[512,256]{1,0:T(8,128)S(1)}, bf16[256,512]{1,0:T(8,128)(2,1)S(1)}) custom-call(bf16[12,16,512]{2,1,0:T(8,128)(2,1)S(1)} %get-tuple-element.87.low, bf16[12,16,512]{2,1,0:T(8,128)(2,1)S(1)} %get-tuple-element.88.high, bf16[12,256,256]{2,1,0:T(8,128)(2,1)S(1)} %get-tuple-element.127.refs_0_, ...), custom_call_target="tpu_custom_call" | custom-call | flops 1024 | bytes 1024 | tf_op jit(solution)/shard_map/pallas_call | solution.py:51
  52.3 1.2 %shard_map.176 = (bf16[256,512]{1,0:T(8,128)(2,1)}, f32[256,512]{1,0:T(8,128)S(1)}) custom-call(s32[1]{0:T(128)S(6)} %copy.17.tiles, bf16[256,512]{1,0:T(8,128)(2,1)S(1)} %get-tuple-element.80.refs_0_.feats, bf16[256,512]{1,0:T(8,128)(2,1)S(1)} %copy-done.2, bf16[256,512]{1,0:T(8,128)(2,1)S(1)} %get-tuple-element.81.w_out, bf16[256,512]{1,0:T(8,128)(2,1)S(1)} %copy-done.4, ...), custom_call_target="tpu_custom_call" | custom-call | flops 1024 | bytes 1024 | tf_op jit(solution)/shard_map/pallas_call | solution.py:51
  55.0 2.1 %collective-permute-done.14.refs_0_ = bf16[256,256]{1,0:T(8,128)(2,1)S(1)} collective-permute-done((bf16[256,256]{1,0:T(8,128)(2,1)S(1)}, bf16[256,256]{1,0:T(8,128)(2,1)S(1)}, u32[]{:S(2)}, u32[]{:S(2)}) %collective-permute-start.14) | collective-permute-done | bytes 131104 | tf_op jit(solution)/shard_map/ppermute | solution.py:26
  58.6 0.7 %collective-permute-done.17.refs_1_ = bf16[256,256]{1,0:T(8,128)(2,1)S(1)} collective-permute-done((bf16[256,256]{1,0:T(8,128)(2,1)S(1)}, bf16[256,256]{1,0:T(8,128)(2,1)S(1)}, u32[]{:S(2)}, u32[]{:S(2)}) %collective-permute-start.17) | collective-permute-done | bytes 131104 | tf_op jit(solution)/shard_map/ppermute | solution.py:26
  59.5 4.6 %collective-permute-start.20 = (bf16[64,256]{1,0:T(8,128)(2,1)S(1)}, bf16[64,256]{1,0:T(8,128)(2,1)S(1)}, u32[]{:S(2)}, u32[]{:S(2)}) collective-permute-start(bf16[64,256]{1,0:T(8,128)(2,1)S(1)} %get-tuple-element.157), channel_id=1, source_target_pairs={{0,12},{4,8},{8,4},{12,0},{1,13},{5,9},{9,5},{13,1},{2,14},{6,10},... | collective-permute-start | bytes 98312 | tf_op jit(solution)/shard_map/ppermute | solution.py:811
  64.7 0.7 %shard_map.182 = bf16[256,512]{1,0:T(8,128)(2,1)} custom-call(f32[256,256]{1,0:T(8,128)S(1)} %get-tuple-element.147.refs_0_, bf16[256,256]{1,0:T(8,128)(2,1)S(1)} %collective-permute-done.15.refs_1_, bf16[256,256]{1,0:T(8,128)(2,1)S(1)} %shard_map.181.refs_2_), custom_call_target="tpu_custom_call" | custom-call | flops 1024 | bytes 1024 | tf_op jit(solution)/shard_map/pallas_call | solution.py:51
  66.0 2.9 %collective-permute-done.19.refs_1_ = bf16[64,256]{1,0:T(8,128)(2,1)S(1)} collective-permute-done((bf16[64,256]{1,0:T(8,128)(2,1)S(1)}, bf16[64,256]{1,0:T(8,128)(2,1)S(1)}, u32[]{:S(2)}, u32[]{:S(2)}) %collective-permute-start.19) | collective-permute-done | bytes 32800 | tf_op jit(solution)/shard_map/ppermute | solution.py:811
  (59 shorter events, 9.3 us)
Async XLA Ops:
  0.6 9.5 %copy-start.9 = (s32[1,6,2]{1,2,0:T(2,128)S(1)}, s32[1,6,2]{1,2,0:T(2,128)}, u32[]{:S(2)}) copy-start(s32[1,6,2]{1,2,0:T(2,128)} %param.19) | copy-start | bytes 148
  0.6 14.7 %copy-start.7 = (f32[512]{0:T(512)S(1)}, f32[512]{0:T(512)}, u32[]{:S(2)}) copy-start(f32[512]{0:T(512)} %param.22) | copy-start | bytes 6148
  0.7 9.5 %collective-permute-start = (bf16[256,512]{1,0:T(8,128)(2,1)}, bf16[256,512]{1,0:T(8,128)(2,1)S(1)}, u32[]{:S(2)}, u32[]{:S(2)}) collective-permute-start(bf16[256,512]{1,0:T(8,128)(2,1)} %refs_2_.1), channel_id=1, source_target_pairs={{2,0},{0,2},{3,1},{1,3},{6,4},{4,6},{7,5},{5,7},{10,8},{8,10},{11,... | collective-permute-start | bytes 786440 | tf_op jit(solution)/shard_map/ppermute | solution.py:26
  6.9 8.8 %copy-start.2 = (bf16[256,512]{1,0:T(8,128)(2,1)S(1)}, bf16[256,512]{1,0:T(8,128)(2,1)}, u32[]{:S(2)}) copy-start(bf16[256,512]{1,0:T(8,128)(2,1)} %cots.1) | copy-start | bytes 786436
  6.9 10.5 %copy-start.5 = (s32[512]{0:T(512)S(1)}, s32[512]{0:T(512)}, u32[]{:S(2)}) copy-start(s32[512]{0:T(512)} %param.17) | copy-start | bytes 6148
  7.0 10.5 %copy-start.6 = (s32[12,512]{1,0:T(8,128)S(1)}, s32[12,512]{1,0:T(8,128)}, u32[]{:S(2)}) copy-start(s32[12,512]{1,0:T(8,128)} %senders) | copy-start | bytes 73732
  11.3 7.2 %collective-permute-start.3 = (bf16[272,256]{1,0:T(8,128)(2,1)S(1)}, bf16[272,256]{1,0:T(8,128)(2,1)S(1)}, u32[]{:S(2)}, u32[]{:S(2)}) collective-permute-start(bf16[272,256]{1,0:T(8,128)(2,1)S(1)} %get-tuple-element.95), channel_id=1, source_target_pairs={{1,0},{0,1},{3,2},{2,3},{5,4},{4,5},{7,6},{6,7},{9,8},{8,9},{11,10... | collective-permute-start | bytes 417800 | tf_op jit(solution)/shard_map/ppermute | solution.py:26
  11.3 10.1 %collective-permute-start.1 = (bf16[272,256]{1,0:T(8,128)(2,1)S(1)}, bf16[272,256]{1,0:T(8,128)(2,1)S(1)}, u32[]{:S(2)}, u32[]{:S(2)}) collective-permute-start(bf16[272,256]{1,0:T(8,128)(2,1)S(1)} %get-tuple-element.92), channel_id=1, source_target_pairs={{12,0},{0,4},{4,8},{8,12},{13,1},{1,5},{5,9},{9,13},{14,2},{2,6},{... | collective-permute-start | bytes 417800 | tf_op jit(solution)/shard_map/ppermute | solution.py:26
  13.2 8.7 %collective-permute-start.2 = (bf16[272,256]{1,0:T(8,128)(2,1)S(1)}, bf16[272,256]{1,0:T(8,128)(2,1)S(1)}, u32[]{:S(2)}, u32[]{:S(2)}) collective-permute-start(bf16[272,256]{1,0:T(8,128)(2,1)S(1)} %get-tuple-element.93), channel_id=1, source_target_pairs={{4,0},{8,4},{12,8},{0,12},{5,1},{9,5},{13,9},{1,13},{6,2},{10,6},{... | collective-permute-start | bytes 417800 | tf_op jit(solution)/shard_map/ppermute | solution.py:26
  15.7 8.4 %collective-permute-start.4 = (bf16[256,512]{1,0:T(8,128)(2,1)S(1)}, bf16[256,512]{1,0:T(8,128)(2,1)S(1)}, u32[]{:S(2)}, u32[]{:S(2)}) collective-permute-start(bf16[256,512]{1,0:T(8,128)(2,1)S(1)} %copy-done.2), channel_id=1, source_target_pairs={{2,0},{0,2},{3,1},{1,3},{6,4},{4,6},{7,5},{5,7},{10,8},{8,10},{11,... | collective-permute-start | bytes 786440 | tf_op jit(solution)/shard_map/ppermute | solution.py:26
  17.4 11.0 %collective-permute-start.5 = (bf16[272,256]{1,0:T(8,128)(2,1)S(1)}, bf16[272,256]{1,0:T(8,128)(2,1)S(1)}, u32[]{:S(2)}, u32[]{:S(2)}) collective-permute-start(bf16[272,256]{1,0:T(8,128)(2,1)S(1)} %get-tuple-element.103), channel_id=1, source_target_pairs={{0,9},{1,8},{4,13},{5,12},{8,1},{9,0},{12,5},{13,4},{2,11},{3,10},... | collective-permute-start | bytes 417800 | tf_op jit(solution)/shard_map/ppermute | solution.py:617
  18.5 5.6 %copy-start = (bf16[512,512]{1,0:T(8,128)(2,1)S(1)}, bf16[512,512]{1,0:T(8,128)(2,1)}, u32[]{:S(2)}) copy-start(bf16[512,512]{1,0:T(8,128)(2,1)} %refs_3_.3) | copy-start | bytes 1572868
  18.5 5.6 %copy-start.3 = (bf16[512,512]{1,0:T(8,128)(2,1)S(1)}, bf16[512,512]{1,0:T(8,128)(2,1)}, u32[]{:S(2)}) copy-start(bf16[512,512]{1,0:T(8,128)(2,1)} %get-tuple-element.98.refs_5_) | copy-start | bytes 1572868
  18.5 5.6 %copy-start.8 = (f32[512]{0:T(512)S(1)}, f32[512]{0:T(512)}, u32[]{:S(2)}) copy-start(f32[512]{0:T(512)} %param.26) | copy-start | bytes 6148
  21.9 6.5 %collective-permute-start.6 = (bf16[272,256]{1,0:T(8,128)(2,1)S(1)}, bf16[272,256]{1,0:T(8,128)(2,1)S(1)}, u32[]{:S(2)}, u32[]{:S(2)}) collective-permute-start(bf16[272,256]{1,0:T(8,128)(2,1)S(1)} %collective-permute-done.1.west.refs_2_), channel_id=1, source_target_pairs={{1,0},{0,1},{3,2},{2,3},{5,4},{4,5},{7,6},{6,7},{9,8},{8,9},{11,10... | collective-permute-start | bytes 417800 | tf_op jit(solution)/shard_map/ppermute | solution.py:26
  22.4 6.1 %collective-permute-start.7 = (bf16[272,256]{1,0:T(8,128)(2,1)S(1)}, bf16[272,256]{1,0:T(8,128)(2,1)S(1)}, u32[]{:S(2)}, u32[]{:S(2)}) collective-permute-start(bf16[272,256]{1,0:T(8,128)(2,1)S(1)} %collective-permute-done.2.east.refs_3_), channel_id=1, source_target_pairs={{1,0},{0,1},{3,2},{2,3},{5,4},{4,5},{7,6},{6,7},{9,8},{8,9},{11,10... | collective-permute-start | bytes 417800 | tf_op jit(solution)/shard_map/ppermute | solution.py:26
  30.9 5.6 %copy-start.1 = (bf16[512,512]{1,0:T(8,128)(2,1)S(1)}, bf16[512,512]{1,0:T(8,128)(2,1)}, u32[]{:S(2)}) copy-start(bf16[512,512]{1,0:T(8,128)(2,1)} %get-tuple-element.108.refs_2_) | copy-start | bytes 1572868
  30.9 5.6 %collective-permute-start.8 = (bf16[256,256]{1,0:T(8,128)(2,1)S(1)}, bf16[256,256]{1,0:T(8,128)(2,1)S(1)}, u32[]{:S(2)}, u32[]{:S(2)}) collective-permute-start(bf16[256,256]{1,0:T(8,128)(2,1)S(1)} %get-tuple-element.107.refs_0_), channel_id=1, source_target_pairs={{2,0},{0,2},{3,1},{1,3},{6,4},{4,6},{7,5},{5,7},{10,8},{8,10},{11,... | collective-permute-start | bytes 393224 | tf_op jit(solution)/shard_map/ppermute | solution.py:26
  34.9 5.3 %collective-permute-start.9 = (bf16[256,256]{1,0:T(8,128)(2,1)S(1)}, bf16[256,256]{1,0:T(8,128)(2,1)S(1)}, u32[]{:S(2)}, u32[]{:S(2)}) collective-permute-start(bf16[256,256]{1,0:T(8,128)(2,1)S(1)} %get-tuple-element.115.refs_0_), channel_id=1, source_target_pairs={{2,0},{0,2},{3,1},{1,3},{6,4},{4,6},{7,5},{5,7},{10,8},{8,10},{11,... | collective-permute-start | bytes 393224 | tf_op jit(solution)/shard_map/ppermute | solution.py:26
  41.7 6.3 %collective-permute-start.10 = (bf16[256,256]{1,0:T(8,128)(2,1)S(1)}, bf16[256,256]{1,0:T(8,128)(2,1)S(1)}, u32[]{:S(2)}, u32[]{:S(2)}) collective-permute-start(bf16[256,256]{1,0:T(8,128)(2,1)S(1)} %get-tuple-element.122), channel_id=1, source_target_pairs={{0,13},{1,4},{4,1},{5,8},{8,5},{9,12},{12,9},{13,0},{2,15},{3,6},{... | collective-permute-start | bytes 393224 | tf_op jit(solution)/shard_map/ppermute | solution.py:561
  42.9 5.2 %collective-permute-start.11 = (bf16[2,256,256]{2,1,0:T(8,128)(2,1)S(1)}, bf16[2,256,256]{2,1,0:T(8,128)(2,1)S(1)}, u32[]{:S(2)}, u32[]{:S(2)}) collective-permute-start(bf16[2,256,256]{2,1,0:T(8,128)(2,1)S(1)} %shard_map.171), channel_id=1, source_target_pairs={{1,0},{0,1},{3,2},{2,3},{5,4},{4,5},{7,6},{6,7},{9,8},{8,9},{11,10... | collective-permute-start | bytes 786440 | tf_op jit(solution)/shard_map/ppermute | solution.py:26
  45.6 7.9 %collective-permute-start.12 = (bf16[256,256]{1,0:T(8,128)(2,1)S(1)}, bf16[256,256]{1,0:T(8,128)(2,1)S(1)}, u32[]{:S(2)}, u32[]{:S(2)}) collective-permute-start(bf16[256,256]{1,0:T(8,128)(2,1)S(1)} %get-tuple-element.136), channel_id=1, source_target_pairs={{1,0},{0,1},{3,2},{2,3},{5,4},{4,5},{7,6},{6,7},{9,8},{8,9},{11,10... | collective-permute-start | bytes 393224 | tf_op jit(solution)/shard_map/ppermute | solution.py:26
  48.2 5.4 %collective-permute-start.13 = (bf16[256,256]{1,0:T(8,128)(2,1)S(1)}, bf16[256,256]{1,0:T(8,128)(2,1)S(1)}, u32[]{:S(2)}, u32[]{:S(2)}) collective-permute-start(bf16[256,256]{1,0:T(8,128)(2,1)S(1)} %get-tuple-element.126), channel_id=1, source_target_pairs={{4,0},{8,4},{12,8},{0,12},{5,1},{9,5},{13,9},{1,13},{6,2},{10,6},{... | collective-permute-start | bytes 393224 | tf_op jit(solution)/shard_map/ppermute | solution.py:26
  49.7 2.6 %copy-start.4 = (bf16[256,512]{1,0:T(8,128)(2,1)S(1)}, bf16[256,512]{1,0:T(8,128)(2,1)}, u32[]{:S(2)}) copy-start(bf16[256,512]{1,0:T(8,128)(2,1)} %get-tuple-element.82.w_node_v_t) | copy-start | bytes 786436
  49.7 7.4 %collective-permute-start.14 = (bf16[256,256]{1,0:T(8,128)(2,1)S(1)}, bf16[256,256]{1,0:T(8,128)(2,1)S(1)}, u32[]{:S(2)}, u32[]{:S(2)}) collective-permute-start(bf16[256,256]{1,0:T(8,128)(2,1)S(1)} %get-tuple-element.137), channel_id=1, source_target_pairs={{12,0},{0,4},{4,8},{8,12},{13,1},{1,5},{5,9},{9,13},{14,2},{2,6},{... | collective-permute-start | bytes 393224 | tf_op jit(solution)/shard_map/ppermute | solution.py:26
  54.3 5.1 %collective-permute-start.17 = (bf16[256,256]{1,0:T(8,128)(2,1)S(1)}, bf16[256,256]{1,0:T(8,128)(2,1)S(1)}, u32[]{:S(2)}, u32[]{:S(2)}) collective-permute-start(bf16[256,256]{1,0:T(8,128)(2,1)S(1)} %bitcast.22), channel_id=1, source_target_pairs={{2,0},{0,2},{3,1},{1,3},{6,4},{4,6},{7,5},{5,7},{10,8},{8,10},{11,... | collective-permute-start | bytes 393224 | tf_op jit(solution)/shard_map/ppermute | solution.py:26
  57.5 1.9 %collective-permute-start.16 = (bf16[4,64,256]{2,1,0:T(8,128)(2,1)S(1)}, bf16[4,64,256]{2,1,0:T(8,128)(2,1)S(1)}, u32[]{:S(2)}, u32[]{:S(2)}) collective-permute-start(bf16[4,64,256]{2,1,0:T(8,128)(2,1)S(1)} %get-tuple-element.149), channel_id=1, source_target_pairs={{1,0},{0,1},{3,2},{2,3},{5,4},{4,5},{7,6},{6,7},{9,8},{8,9},{11,10... | collective-permute-start | bytes 393224 | tf_op jit(solution)/shard_map/ppermute | solution.py:26
  58.0 6.7 %collective-permute-start.15 = (bf16[256,256]{1,0:T(8,128)(2,1)S(1)}, bf16[256,256]{1,0:T(8,128)(2,1)S(1)}, u32[]{:S(2)}, u32[]{:S(2)}) collective-permute-start(bf16[256,256]{1,0:T(8,128)(2,1)S(1)} %bitcast.21), channel_id=1, source_target_pairs={{2,0},{0,2},{3,1},{1,3},{6,4},{4,6},{7,5},{5,7},{10,8},{8,10},{11,... | collective-permute-start | bytes 393224 | tf_op jit(solution)/shard_map/ppermute | solution.py:26
  59.5 6.5 %collective-permute-start.20 = (bf16[64,256]{1,0:T(8,128)(2,1)S(1)}, bf16[64,256]{1,0:T(8,128)(2,1)S(1)}, u32[]{:S(2)}, u32[]{:S(2)}) collective-permute-start(bf16[64,256]{1,0:T(8,128)(2,1)S(1)} %get-tuple-element.157), channel_id=1, source_target_pairs={{0,12},{4,8},{8,4},{12,0},{1,13},{5,9},{9,5},{13,1},{2,14},{6,10},... | collective-permute-start | bytes 98312 | tf_op jit(solution)/shard_map/ppermute | solution.py:811
  64.1 4.8 %collective-permute-start.19 = (bf16[64,256]{1,0:T(8,128)(2,1)S(1)}, bf16[64,256]{1,0:T(8,128)(2,1)S(1)}, u32[]{:S(2)}, u32[]{:S(2)}) collective-permute-start(bf16[64,256]{1,0:T(8,128)(2,1)S(1)} %get-tuple-element.158), channel_id=1, source_target_pairs={{0,8},{4,12},{8,0},{12,4},{1,9},{5,13},{9,1},{13,5},{2,10},{6,14},... | collective-permute-start | bytes 98312 | tf_op jit(solution)/shard_map/ppermute | solution.py:811
  64.1 4.8 %collective-permute-start.18 = (bf16[64,256]{1,0:T(8,128)(2,1)S(1)}, bf16[64,256]{1,0:T(8,128)(2,1)S(1)}, u32[]{:S(2)}, u32[]{:S(2)}) collective-permute-start(bf16[64,256]{1,0:T(8,128)(2,1)S(1)} %get-tuple-element.159), channel_id=1, source_target_pairs={{0,4},{4,0},{8,12},{12,8},{1,5},{5,1},{9,13},{13,9},{2,6},{6,2},{1... | collective-permute-start | bytes 98312 | tf_op jit(solution)/shard_map/ppermute | solution.py:811

commit v13 on v12

--- a/solution.py
+++ b/solution.py
@@ -14,6 +14,7 @@
 PACK = 16
 MIB = 1 << 20
 WEIGHTS_LIMIT = 52
+WEIGHT_FLOPS = 3 * 10**9
 NO_CHUNK = 64
 SLOT_OF = ((3, 0), (1, 1), (4, 4), (2, 5), (0, 2), (5, 3))
 EARLY, LATE = (3, 4, 5), (1, 2, 0)
@@ -758,31 +759,7 @@
     inputs = [tile_count, own, from_beside, feats, from_upper]
     weight_shape = shape((chans_all, hid), f32)
     grad_shape = shape((rows, hid), bf16)
-    finals = []
-    for k in reversed(range(halves)):
-        kernel = functools.partial(back_kernel, k * rows, inv_root)
-        if k:
-            grad_send, weight = call(
-                kernel,
-                (grad_shape, weight_shape),
-                inputs,
-                scratch=[pltpu.VMEM((nodes, hid), f32)],
-                scalars=1,
-            )
-        else:
-            grad_send, w_mine, w_beside = call(
-                kernel,
-                (
-                    grad_shape,
-                    shape((lons, columns, hid), f32),
-                    shape((lons, columns, hid), bf16),
-                ),
-                inputs + [from_lower, weight],
-                scratch=[pltpu.VMEM(weight_shape.shape, f32), pltpu.VMEM((nodes, hid), f32)],
-                scalars=1,
-            )
-            w_beside = shifted(w_beside, "sub", 1)
-            w_beside, *finals = lax.optimization_barrier((w_beside, *finals))
+    def finish(k, grad_send, done):
         kept, sent = call(
             functools.partial(terms_kernel, k * rows),
             (shape((chans, rows), f32), shape((count - 1, chans, rows), bf16)),
@@ -790,28 +767,52 @@
             scratch=[pltpu.VMEM((chans_all, rows), f32)],
             scalars=0,
         )
-        if k:
-            weight, kept = lax.optimization_barrier((weight, kept))
         parts = [kept] + [shifted(sent[i - 1], "ch", i) for i in range(1, count)]
-        grad_features = call(
+        out = call(
             functools.partial(finish_kernel, count),
             shape((chans, nodes - k * rows), bf16),
-            parts + finals,
+            parts + done,
             scalars=0,
         )
-        finals = [grad_features]
-
+        return kept, out
+
+    grad_send, weight = call(
+        functools.partial(back_kernel, rows, inv_root),
+        (grad_shape, weight_shape),
+        inputs,
+        scratch=[pltpu.VMEM((nodes, hid), f32)],
+        scalars=1,
+    )
+    kept, upper_out = finish(1, grad_send, [])
+    weight, kept = lax.optimization_barrier((weight, kept))
+    grad_send, w_mine, w_beside = call(
+        functools.partial(back_kernel, 0, inv_root),
+        (grad_shape, shape((lons, columns, hid), f32), shape((lons, columns, hid), bf16)),
+        inputs + [from_lower, weight],
+        scratch=[pltpu.VMEM(weight_shape.shape, f32), pltpu.VMEM((nodes, hid), f32)],
+        scalars=1,
+    )
+    w_beside = shifted(w_beside, "sub", 1)
+    w_beside, upper_out = lax.optimization_barrier((w_beside, upper_out))
     near, w_sent = call(
         sum_kernel,
         (shape((columns, hid), f32), shape((lons - 1, columns, hid), bf16)),
         [w_mine, w_beside],
         scalars=0,
     )
+    w_sent, grad_send = lax.optimization_barrier((w_sent, grad_send))
     w_terms = [
         lax.ppermute(w_sent[k - 1], "lon", [(i, i ^ k) for i in range(lons)])
         for k in range(1, lons)
     ]
-    grad_w_send = call(weight_kernel, shape((columns, hid), f32), [near] + w_terms, scalars=0)
+    grad_w_send = call(
+        weight_kernel,
+        shape((columns, hid), f32),
+        [near] + w_terms,
+        scalars=0,
+        flops=WEIGHT_FLOPS,
+    )
+    _, grad_features = finish(0, grad_send, [upper_out])
     return (updated, grad_features, grad_w_send.T)
 
 

time: 69.7 us -> 70.8 us (1.016)
  waiting for transfers between devices: 15.9 us -> 17.2 us
    ppermute x16, waiting for transfers between devices: 9.92 us -> 11.7 us  [shifted(): return lax.ppermute(block, axis, route)]
  transfers between devices with their start and end apart: 21 -> 21, of which waited for: 11 -> 12; matrix products, arithmetic and copies ran while one was open for 0% -> 0% of each run, Pallas kernels for 36% -> 36%
where the time goes in v13:
time: 70.8 us; the launch traced here: 70.7 us
  Pallas kernels  31 us (44%)
  starting transfers between devices  20.7 us (29%)
  waiting for transfers between devices  17.2 us (24%)
  between operations  1.68 us (2%)
    pallas_call x28, Pallas kernels, call(): pl.pallas_call(kernel, out_shape=out_shape, in_specs=[smem] * scalars + [...  31 us
    ppermute x16, starting transfers between devices, shifted(): return lax.ppermute(block, axis, route)  15.5 us
    ppermute x16, waiting for transfers between devices, shifted(): return lax.ppermute(block, axis, route)  11.7 us
    ppermute x3, starting transfers between devices, shards(): lax.ppermute(w_sent[k - 1], 'lon', [(i, i ^ k) for i in range(lons)])  4.97 us
    ppermute x3, waiting for transfers between devices, shards(): lax.ppermute(w_sent[k - 1], 'lon', [(i, i ^ k) for i in range(lons)])  3.05 us
    ppermute x1, waiting for transfers between devices, shards(): across = lambda block: lax.ppermute(block, cycle, across_route)  1.85 us
  transfers between devices with their start and end apart: 21, of which 12 were waited for; matrix products, arithmetic and copies ran while one was open for 0% of the time, Pallas kernels for 36%

profile of v13, /device:TPU:0, one launch (start us, length us, event | category | flops | bytes accessed | tf_op | source)
XLA Modules:
  0.0 70.7 jit_solution(18336626460735281376)
XLA Ops:
  0.7 3.0 %collective-permute-start = (bf16[256,512]{1,0:T(8,128)(2,1)}, bf16[256,512]{1,0:T(8,128)(2,1)S(1)}, u32[]{:S(2)}, u32[]{:S(2)}) collective-permute-start(bf16[256,512]{1,0:T(8,128)(2,1)} %refs_2_.1), channel_id=1, source_target_pairs={{2,0},{0,2},{3,1},{1,3},{6,4},{4,6},{7,5},{5,7},{10,8},{8,10},{11,... | collective-permute-start | bytes 786440 | tf_op jit(solution)/shard_map/ppermute | solution.py:27
  3.7 3.3 %shard_map.157 = (bf16[256,512]{1,0:T(8,128)(2,1)S(1)}, bf16[256,512]{1,0:T(8,128)(2,1)S(1)}, bf16[256,512]{1,0:T(8,128)(2,1)S(1)}, bf16[256,512]{1,0:T(8,128)(2...) custom-call(bf16[512,512]{1,0:T(8,128)(2,1)} %refs_0_.1, ...), custom_call_target="tpu_custom_call" | custom-call | flops 1024 | bytes 1024 | tf_op jit(solution)/shard_map/pallas_call | solution.py:52
  7.6 2.5 %collective-permute-done.refs_1_ = bf16[256,512]{1,0:T(8,128)(2,1)S(1)} collective-permute-done((bf16[256,512]{1,0:T(8,128)(2,1)}, bf16[256,512]{1,0:T(8,128)(2,1)S(1)}, u32[]{:S(2)}, u32[]{:S(2)}) %collective-permute-start) | collective-permute-done | bytes 262176 | tf_op jit(solution)/shard_map/ppermute | solution.py:27
  10.2 1.1 %shard_map.158 = (bf16[512,512]{1,0:T(8,128)(2,1)S(1)}, bf16[512,256]{1,0:T(8,128)(2,1)S(1)}, bf16[272,256]{1,0:T(8,128)(2,1)S(1)}, bf16[272,256]{1,0:T(8,128)(2...) custom-call(s32[1]{0:T(128)S(6)} %copy.17.tiles, s32[1,2,6]{2,1,0:T(2,128)S(1)} %bitcast.20, ...), custom_call_target="tpu_custom_call" | custom-call | flops 1024 | bytes 1024 | tf_op jit(solution)/shard_map/pallas_call | solution.py:52
  11.3 1.9 %collective-permute-start.1 = (bf16[272,256]{1,0:T(8,128)(2,1)S(1)}, bf16[272,256]{1,0:T(8,128)(2,1)S(1)}, u32[]{:S(2)}, u32[]{:S(2)}) collective-permute-start(bf16[272,256]{1,0:T(8,128)(2,1)S(1)} %get-tuple-element.93), channel_id=1, source_target_pairs={{12,0},{0,4},{4,8},{8,12},{13,1},{1,5},{5,9},{9,13},{14,2},{2,6},{... | collective-permute-start | bytes 417800 | tf_op jit(solution)/shard_map/ppermute | solution.py:27
  13.2 2.1 %collective-permute-start.2 = (bf16[272,256]{1,0:T(8,128)(2,1)S(1)}, bf16[272,256]{1,0:T(8,128)(2,1)S(1)}, u32[]{:S(2)}, u32[]{:S(2)}) collective-permute-start(bf16[272,256]{1,0:T(8,128)(2,1)S(1)} %get-tuple-element.94), channel_id=1, source_target_pairs={{4,0},{8,4},{12,8},{0,12},{5,1},{9,5},{13,9},{1,13},{6,2},{10,6},{... | collective-permute-start | bytes 417800 | tf_op jit(solution)/shard_map/ppermute | solution.py:27
  15.7 1.7 %collective-permute-start.4 = (bf16[256,512]{1,0:T(8,128)(2,1)S(1)}, bf16[256,512]{1,0:T(8,128)(2,1)S(1)}, u32[]{:S(2)}, u32[]{:S(2)}) collective-permute-start(bf16[256,512]{1,0:T(8,128)(2,1)S(1)} %copy-done.2), channel_id=1, source_target_pairs={{2,0},{0,2},{3,1},{1,3},{6,4},{4,6},{7,5},{5,7},{10,8},{8,10},{11,... | collective-permute-start | bytes 786440 | tf_op jit(solution)/shard_map/ppermute | solution.py:27
  17.4 1.0 %shard_map.160 = (bf16[12,512,128]{2,1,0:T(8,128)(2,1)S(1)}, bf16[12,512,128]{2,1,0:T(8,128)(2,1)S(1)}, bf16[12,16,512]{2,1,0:T(8,128)(2,1)S(1)}, bf16[12,16,512]{2,1,0:T(8,128)(2,1)S(1)}) custom-call(s32[1]{0:T(128)S(6)} %copy.17.tiles, s32[12,512]{1,0:T(8,128)S(1)} %copy-done.6, s32[1,512]{1,0:T(1,128)S(1)} %bitcast.13), custom_call_target="tpu_custom_call" | custom-call | flops 1024 | bytes 1024 | tf_op jit(solution)/shard_map/pallas_call | solution.py:52
  18.5 2.9 %shard_map.161.before = bf16[12,512,256]{2,1,0:T(8,128)(2,1)S(1)} custom-call(bf16[12,512,128]{2,1,0:T(8,128)(2,1)S(1)} %get-tuple-element.90.low, bf16[12,512,128]{2,1,0:T(8,128)(2,1)S(1)} %get-tuple-element.91.high, bf16[512,256]{1,0:T(8,128)(2,1)S(1)} %get-tuple-element.95.proj, bf16[272,256]{1,0:T(8,128)(2,1)S(1)} %collective-permute-done.3.beside.refs_4_), custom_call_target="tpu_custom_call" | custom-call | flops 1024 | bytes 1024 | tf_op jit(solution)/shard_map/pallas_call | solution.py:52
  22.4 1.6 %collective-permute-done.4.refs_1_ = bf16[256,512]{1,0:T(8,128)(2,1)S(1)} collective-permute-done((bf16[256,512]{1,0:T(8,128)(2,1)S(1)}, bf16[256,512]{1,0:T(8,128)(2,1)S(1)}, u32[]{:S(2)}, u32[]{:S(2)}) %collective-permute-start.4) | collective-permute-done | bytes 262176 | tf_op jit(solution)/shard_map/ppermute | solution.py:27
  24.1 1.1 %shard_map.162 = (bf16[512,512]{1,0:T(8,128)(2,1)}, f32[512,512]{1,0:T(8,128)S(1)}, f32[512,512]{1,0:T(8,128)S(1)}) custom-call(s32[1]{0:T(128)S(6)} %copy.17.tiles, bf16[256,512]{1,0:T(8,128)(2,1)S(1)} %copy-done.2, bf16[256,512]{1,0:T(8,128)(2,1)S(1)} %collective-permute-done.4.refs_1_, bf16[512,512]{1,0:T(8,128)(2,1)S(1)} %get-tuple-element.85.feats.refs_2_, ...), custom_call_target="tpu_custom_call" | custom-call | flops 1024 | bytes 1024 | tf_op jit(solution)/shard_map/pallas_call | solution.py:52
  25.2 2.5 %shard_map.163.part = bf16[12,512,256]{2,1,0:T(8,128)(2,1)S(1)} custom-call(bf16[12,512,128]{2,1,0:T(8,128)(2,1)S(1)} %get-tuple-element.90.low, bf16[12,512,128]{2,1,0:T(8,128)(2,1)S(1)} %get-tuple-element.91.high, bf16[12,512,256]{2,1,0:T(8,128)(2,1)S(1)} %shard_map.161.before, bf16[272,256]{1,0:T(8,128)(2,1)S(1)} %collective-permute-done.1.west.refs_2_, ...), custom_call_target="tpu_custom_call" | custom-call | flops 1024 | bytes 1024 | tf_op jit(solution)/shard_map/pallas_call | solution.py:52
  28.4 2.5 %shard_map.165 = (bf16[256,256]{1,0:T(8,128)(2,1)S(1)}, bf16[12,256,256]{2,1,0:T(8,128)(2,1)S(1)}) custom-call(bf16[12,512,128]{2,1,0:T(8,128)(2,1)S(1)} %get-tuple-element.90.low, bf16[12,512,128]{2,1,0:T(8,128)(2,1)S(1)} %get-tuple-element.91.high, f32[512,256]{1,0:T(8,128)S(1)} %shard_map.159.base, s32[1,512]{1,0:T(1,128)S(1)} %bitcast.14, ...), custom_call_target="tpu_custom_call" | custom-call | flops 1024 | bytes 1024 | tf_op jit(solution)/shard_map/pallas_call | solution.py:52
  30.9 1.6 %collective-permute-start.8 = (bf16[256,256]{1,0:T(8,128)(2,1)S(1)}, bf16[256,256]{1,0:T(8,128)(2,1)S(1)}, u32[]{:S(2)}, u32[]{:S(2)}) collective-permute-start(bf16[256,256]{1,0:T(8,128)(2,1)S(1)} %get-tuple-element.108.refs_0_), channel_id=1, source_target_pairs={{2,0},{0,2},{3,1},{1,3},{6,4},{4,6},{7,5},{5,7},{10,8},{8,10},{11,... | collective-permute-start | bytes 393224 | tf_op jit(solution)/shard_map/ppermute | solution.py:27
  32.5 2.5 %shard_map.168 = (bf16[256,256]{1,0:T(8,128)(2,1)S(1)}, bf16[12,256,256]{2,1,0:T(8,128)(2,1)S(1)}) custom-call(bf16[12,512,128]{2,1,0:T(8,128)(2,1)S(1)} %get-tuple-element.90.low, bf16[12,512,128]{2,1,0:T(8,128)(2,1)S(1)} %get-tuple-element.91.high, f32[512,256]{1,0:T(8,128)S(1)} %shard_map.159.base, s32[1,512]{1,0:T(1,128)S(1)} %bitcast.15, ...), custom_call_target="tpu_custom_call" | custom-call | flops 1024 | bytes 1024 | tf_op jit(solution)/shard_map/pallas_call | solution.py:52
  35.5 1.0 %collective-permute-done.8.refs_1_ = bf16[256,256]{1,0:T(8,128)(2,1)S(1)} collective-permute-done((bf16[256,256]{1,0:T(8,128)(2,1)S(1)}, bf16[256,256]{1,0:T(8,128)(2,1)S(1)}, u32[]{:S(2)}, u32[]{:S(2)}) %collective-permute-start.8) | collective-permute-done | bytes 131104 | tf_op jit(solution)/shard_map/ppermute | solution.py:27
  36.5 0.9 %shard_map.166 = (bf16[512,256]{1,0:T(8,128)(2,1)S(1)}, bf16[512,256]{1,0:T(8,128)(2,1)S(1)}, f32[256,256]{1,0:T(8,128)S(1)}) custom-call(s32[1,512]{1,0:T(1,128)S(1)} %bitcast.16, bf16[256,256]{1,0:T(8,128)(2,1)S(1)} %get-tuple-element.108.refs_0_, bf16[256,256]{1,0:T(8,128)(2,1)S(1)} %collective-permute-done.8.refs_1_, bf16[512,512]{1,0:T(8,128)(2,1)S(1)} %copy-done.1, ...), custom_call_target="tpu_custom_call" | custom-call | flops 1024 | bytes 1024 | tf_op jit(solution)/shard_map/pallas_call | solution.py:52
  37.4 1.4 %shard_map.167 = (bf16[12,256,256]{2,1,0:T(8,128)(2,1)S(1)}, f32[768,256]{1,0:T(8,128)S(1)}) custom-call(bf16[12,16,512]{2,1,0:T(8,128)(2,1)S(1)} %get-tuple-element.88.low, bf16[12,16,512]{2,1,0:T(8,128)(2,1)S(1)} %get-tuple-element.89.high, bf16[12,256,256]{2,1,0:T(8,128)(2,1)S(1)} %get-tuple-element.107.slope, f32[256,256]{1,0:T(8,128)S(1)} %get-tuple-element.113.scale), custom_call_target="tpu_custom_call" | custom-call | flops 1024 | bytes 1024 | tf_op jit(solution)/shard_map/pallas_call | solution.py:52
  38.9 1.4 %collective-permute-done.9.refs_1_ = bf16[256,256]{1,0:T(8,128)(2,1)S(1)} collective-permute-done((bf16[256,256]{1,0:T(8,128)(2,1)S(1)}, bf16[256,256]{1,0:T(8,128)(2,1)S(1)}, u32[]{:S(2)}, u32[]{:S(2)}) %collective-permute-start.9) | collective-permute-done | bytes 131104 | tf_op jit(solution)/shard_map/ppermute | solution.py:27
  40.2 0.8 %shard_map.169 = (bf16[512,256]{1,0:T(8,128)(2,1)S(1)}, bf16[512,256]{1,0:T(8,128)(2,1)S(1)}, f32[256,256]{1,0:T(8,128)S(1)}) custom-call(s32[1,512]{1,0:T(1,128)S(1)} %bitcast.17, bf16[256,256]{1,0:T(8,128)(2,1)S(1)} %get-tuple-element.116.refs_0_, bf16[256,256]{1,0:T(8,128)(2,1)S(1)} %collective-permute-done.9.refs_1_, bf16[512,512]{1,0:T(8,128)(2,1)S(1)} %copy-done.1, ...), custom_call_target="tpu_custom_call" | custom-call | flops 1024 | bytes 1024 | tf_op jit(solution)/shard_map/pallas_call | solution.py:52
  41.0 0.7 %shard_map.170 = (bf16[256,256]{1,0:T(8,128)(2,1)S(1)}, bf16[12,256,256]{2,1,0:T(8,128)(2,1)S(1)}) custom-call(bf16[12,16,512]{2,1,0:T(8,128)(2,1)S(1)} %get-tuple-element.88.low, bf16[12,16,512]{2,1,0:T(8,128)(2,1)S(1)} %get-tuple-element.89.high, bf16[12,256,256]{2,1,0:T(8,128)(2,1)S(1)} %get-tuple-element.115.slope, ...), custom_call_target="tpu_custom_call" | custom-call | flops 1024 | bytes 1024 | tf_op jit(solution)/shard_map/pallas_call | solution.py:52
  41.9 1.0 %shard_map.171 = bf16[2,256,256]{2,1,0:T(8,128)(2,1)S(1)} custom-call(bf16[12,16,512]{2,1,0:T(8,128)(2,1)S(1)} %get-tuple-element.88.low, bf16[12,16,512]{2,1,0:T(8,128)(2,1)S(1)} %get-tuple-element.89.high, bf16[12,256,256]{2,1,0:T(8,128)(2,1)S(1)} %get-tuple-element.119.grads.refs_1_, f32[768,256]{1,0:T(8,128)S(1)} %get-tuple-element.118.before, ...), custom_call_target="tpu_custom_call" | custom-call | flops 1024 | bytes 1024 | tf_op jit(solution)/shard_map/pallas_call | solution.py:52
  43.0 2.6 %shard_map.172 = (bf16[256,256]{1,0:T(8,128)(2,1)S(1)}, bf16[256,256]{1,0:T(8,128)(2,1)S(1)}, bf16[256,256]{1,0:T(8,128)(2,1)S(1)}) custom-call(bf16[12,16,512]{2,1,0:T(8,128)(2,1)S(1)} %get-tuple-element.88.low, bf16[12,16,512]{2,1,0:T(8,128)(2,1)S(1)} %get-tuple-element.89.high, bf16[12,256,256]{2,1,0:T(8,128)(2,1)S(1)} %get-tuple-element.128.refs_0_, ...), custom_call_target="tpu_custom_call" | custom-call | flops 1024 | bytes 1024 | tf_op jit(solution)/shard_map/pallas_call | solution.py:52
  46.2 1.8 %collective-permute-done.10.across = bf16[256,256]{1,0:T(8,128)(2,1)S(1)} collective-permute-done((bf16[256,256]{1,0:T(8,128)(2,1)S(1)}, bf16[256,256]{1,0:T(8,128)(2,1)S(1)}, u32[]{:S(2)}, u32[]{:S(2)}) %collective-permute-start.10) | collective-permute-done | bytes 131104 | tf_op jit(solution)/shard_map/ppermute | solution.py:562
  48.2 1.5 %collective-permute-start.13 = (bf16[256,256]{1,0:T(8,128)(2,1)S(1)}, bf16[256,256]{1,0:T(8,128)(2,1)S(1)}, u32[]{:S(2)}, u32[]{:S(2)}) collective-permute-start(bf16[256,256]{1,0:T(8,128)(2,1)S(1)} %get-tuple-element.127), channel_id=1, source_target_pairs={{4,0},{8,4},{12,8},{0,12},{5,1},{9,5},{13,9},{1,13},{6,2},{10,6},{... | collective-permute-start | bytes 393224 | tf_op jit(solution)/shard_map/ppermute | solution.py:27
  50.3 2.1 %shard_map.175 = (f32[512,256]{1,0:T(8,128)S(1)}, bf16[256,512]{1,0:T(8,128)(2,1)S(1)}) custom-call(bf16[12,16,512]{2,1,0:T(8,128)(2,1)S(1)} %get-tuple-element.88.low, bf16[12,16,512]{2,1,0:T(8,128)(2,1)S(1)} %get-tuple-element.89.high, bf16[12,256,256]{2,1,0:T(8,128)(2,1)S(1)} %get-tuple-element.128.refs_0_, ...), custom_call_target="tpu_custom_call" | custom-call | flops 1024 | bytes 1024 | tf_op jit(solution)/shard_map/pallas_call | solution.py:52
  52.3 1.2 %shard_map.176 = (bf16[256,512]{1,0:T(8,128)(2,1)}, f32[256,512]{1,0:T(8,128)S(1)}) custom-call(s32[1]{0:T(128)S(6)} %copy.17.tiles, bf16[256,512]{1,0:T(8,128)(2,1)S(1)} %get-tuple-element.81.refs_0_.feats, bf16[256,512]{1,0:T(8,128)(2,1)S(1)} %copy-done.2, bf16[256,512]{1,0:T(8,128)(2,1)S(1)} %get-tuple-element.82.w_out, bf16[256,512]{1,0:T(8,128)(2,1)S(1)} %copy-done.4, ...), custom_call_target="tpu_custom_call" | custom-call | flops 1024 | bytes 1024 | tf_op jit(solution)/shard_map/pallas_call | solution.py:52
  55.0 2.1 %collective-permute-done.14.refs_0_ = bf16[256,256]{1,0:T(8,128)(2,1)S(1)} collective-permute-done((bf16[256,256]{1,0:T(8,128)(2,1)S(1)}, bf16[256,256]{1,0:T(8,128)(2,1)S(1)}, u32[]{:S(2)}, u32[]{:S(2)}) %collective-permute-start.14) | collective-permute-done | bytes 131104 | tf_op jit(solution)/shard_map/ppermute | solution.py:27
  57.6 1.8 %collective-permute-done.16.refs_1_ = bf16[256,256]{1,0:T(8,128)(2,1)S(1)} collective-permute-done((bf16[256,256]{1,0:T(8,128)(2,1)S(1)}, bf16[256,256]{1,0:T(8,128)(2,1)S(1)}, u32[]{:S(2)}, u32[]{:S(2)}) %collective-permute-start.16) | collective-permute-done | bytes 131104 | tf_op jit(solution)/shard_map/ppermute | solution.py:27
  59.5 4.3 %collective-permute-start.20 = (bf16[64,256]{1,0:T(8,128)(2,1)S(1)}, bf16[64,256]{1,0:T(8,128)(2,1)S(1)}, u32[]{:S(2)}, u32[]{:S(2)}) collective-permute-start(bf16[64,256]{1,0:T(8,128)(2,1)S(1)} %get-tuple-element.159), channel_id=1, source_target_pairs={{0,12},{4,8},{8,4},{12,0},{1,13},{5,9},{9,5},{13,1},{2,14},{6,10},... | collective-permute-start | bytes 98312 | tf_op jit(solution)/shard_map/ppermute | solution.py:805
  65.8 2.8 %collective-permute-done.19.refs_1_ = bf16[64,256]{1,0:T(8,128)(2,1)S(1)} collective-permute-done((bf16[64,256]{1,0:T(8,128)(2,1)S(1)}, bf16[64,256]{1,0:T(8,128)(2,1)S(1)}, u32[]{:S(2)}, u32[]{:S(2)}) %collective-permute-start.19) | collective-permute-done | bytes 32800 | tf_op jit(solution)/shard_map/ppermute | solution.py:805
  69.9 0.7 %shard_map.183 = bf16[256,512]{1,0:T(8,128)(2,1)} custom-call(f32[256,256]{1,0:T(8,128)S(1)} %get-tuple-element.154.refs_0_, bf16[256,256]{1,0:T(8,128)(2,1)S(1)} %collective-permute-done.17.refs_1_, bf16[256,256]{1,0:T(8,128)(2,1)S(1)} %shard_map.180.refs_2_), custom_call_target="tpu_custom_call" | custom-call | flops 1024 | bytes 1024 | tf_op jit(solution)/shard_map/pallas_call | solution.py:52
  (59 shorter events, 9.7 us)
Async XLA Ops:
  0.6 9.5 %copy-start.9 = (s32[1,6,2]{1,2,0:T(2,128)S(1)}, s32[1,6,2]{1,2,0:T(2,128)}, u32[]{:S(2)}) copy-start(s32[1,6,2]{1,2,0:T(2,128)} %param.19) | copy-start | bytes 148
  0.6 14.7 %copy-start.7 = (f32[512]{0:T(512)S(1)}, f32[512]{0:T(512)}, u32[]{:S(2)}) copy-start(f32[512]{0:T(512)} %param.22) | copy-start | bytes 6148
  0.7 9.5 %collective-permute-start = (bf16[256,512]{1,0:T(8,128)(2,1)}, bf16[256,512]{1,0:T(8,128)(2,1)S(1)}, u32[]{:S(2)}, u32[]{:S(2)}) collective-permute-start(bf16[256,512]{1,0:T(8,128)(2,1)} %refs_2_.1), channel_id=1, source_target_pairs={{2,0},{0,2},{3,1},{1,3},{6,4},{4,6},{7,5},{5,7},{10,8},{8,10},{11,... | collective-permute-start | bytes 786440 | tf_op jit(solution)/shard_map/ppermute | solution.py:27
  6.9 8.8 %copy-start.2 = (bf16[256,512]{1,0:T(8,128)(2,1)S(1)}, bf16[256,512]{1,0:T(8,128)(2,1)}, u32[]{:S(2)}) copy-start(bf16[256,512]{1,0:T(8,128)(2,1)} %cots.1) | copy-start | bytes 786436
  6.9 10.5 %copy-start.5 = (s32[512]{0:T(512)S(1)}, s32[512]{0:T(512)}, u32[]{:S(2)}) copy-start(s32[512]{0:T(512)} %param.17) | copy-start | bytes 6148
  7.0 10.5 %copy-start.6 = (s32[12,512]{1,0:T(8,128)S(1)}, s32[12,512]{1,0:T(8,128)}, u32[]{:S(2)}) copy-start(s32[12,512]{1,0:T(8,128)} %senders) | copy-start | bytes 73732
  11.3 7.2 %collective-permute-start.3 = (bf16[272,256]{1,0:T(8,128)(2,1)S(1)}, bf16[272,256]{1,0:T(8,128)(2,1)S(1)}, u32[]{:S(2)}, u32[]{:S(2)}) collective-permute-start(bf16[272,256]{1,0:T(8,128)(2,1)S(1)} %get-tuple-element.96), channel_id=1, source_target_pairs={{1,0},{0,1},{3,2},{2,3},{5,4},{4,5},{7,6},{6,7},{9,8},{8,9},{11,10... | collective-permute-start | bytes 417800 | tf_op jit(solution)/shard_map/ppermute | solution.py:27
  11.3 10.1 %collective-permute-start.1 = (bf16[272,256]{1,0:T(8,128)(2,1)S(1)}, bf16[272,256]{1,0:T(8,128)(2,1)S(1)}, u32[]{:S(2)}, u32[]{:S(2)}) collective-permute-start(bf16[272,256]{1,0:T(8,128)(2,1)S(1)} %get-tuple-element.93), channel_id=1, source_target_pairs={{12,0},{0,4},{4,8},{8,12},{13,1},{1,5},{5,9},{9,13},{14,2},{2,6},{... | collective-permute-start | bytes 417800 | tf_op jit(solution)/shard_map/ppermute | solution.py:27
  13.2 8.7 %collective-permute-start.2 = (bf16[272,256]{1,0:T(8,128)(2,1)S(1)}, bf16[272,256]{1,0:T(8,128)(2,1)S(1)}, u32[]{:S(2)}, u32[]{:S(2)}) collective-permute-start(bf16[272,256]{1,0:T(8,128)(2,1)S(1)} %get-tuple-element.94), channel_id=1, source_target_pairs={{4,0},{8,4},{12,8},{0,12},{5,1},{9,5},{13,9},{1,13},{6,2},{10,6},{... | collective-permute-start | bytes 417800 | tf_op jit(solution)/shard_map/ppermute | solution.py:27
  15.7 8.4 %collective-permute-start.4 = (bf16[256,512]{1,0:T(8,128)(2,1)S(1)}, bf16[256,512]{1,0:T(8,128)(2,1)S(1)}, u32[]{:S(2)}, u32[]{:S(2)}) collective-permute-start(bf16[256,512]{1,0:T(8,128)(2,1)S(1)} %copy-done.2), channel_id=1, source_target_pairs={{2,0},{0,2},{3,1},{1,3},{6,4},{4,6},{7,5},{5,7},{10,8},{8,10},{11,... | collective-permute-start | bytes 786440 | tf_op jit(solution)/shard_map/ppermute | solution.py:27
  17.4 11.0 %collective-permute-start.5 = (bf16[272,256]{1,0:T(8,128)(2,1)S(1)}, bf16[272,256]{1,0:T(8,128)(2,1)S(1)}, u32[]{:S(2)}, u32[]{:S(2)}) collective-permute-start(bf16[272,256]{1,0:T(8,128)(2,1)S(1)} %get-tuple-element.104), channel_id=1, source_target_pairs={{0,9},{1,8},{4,13},{5,12},{8,1},{9,0},{12,5},{13,4},{2,11},{3,10},... | collective-permute-start | bytes 417800 | tf_op jit(solution)/shard_map/ppermute | solution.py:618
  18.5 5.6 %copy-start = (bf16[512,512]{1,0:T(8,128)(2,1)S(1)}, bf16[512,512]{1,0:T(8,128)(2,1)}, u32[]{:S(2)}) copy-start(bf16[512,512]{1,0:T(8,128)(2,1)} %refs_3_.3) | copy-start | bytes 1572868
  18.5 5.6 %copy-start.3 = (bf16[512,512]{1,0:T(8,128)(2,1)S(1)}, bf16[512,512]{1,0:T(8,128)(2,1)}, u32[]{:S(2)}) copy-start(bf16[512,512]{1,0:T(8,128)(2,1)} %get-tuple-element.99.refs_5_) | copy-start | bytes 1572868
  18.5 5.6 %copy-start.8 = (f32[512]{0:T(512)S(1)}, f32[512]{0:T(512)}, u32[]{:S(2)}) copy-start(f32[512]{0:T(512)} %param.26) | copy-start | bytes 6148
  21.9 6.5 %collective-permute-start.6 = (bf16[272,256]{1,0:T(8,128)(2,1)S(1)}, bf16[272,256]{1,0:T(8,128)(2,1)S(1)}, u32[]{:S(2)}, u32[]{:S(2)}) collective-permute-start(bf16[272,256]{1,0:T(8,128)(2,1)S(1)} %collective-permute-done.1.west.refs_2_), channel_id=1, source_target_pairs={{1,0},{0,1},{3,2},{2,3},{5,4},{4,5},{7,6},{6,7},{9,8},{8,9},{11,10... | collective-permute-start | bytes 417800 | tf_op jit(solution)/shard_map/ppermute | solution.py:27
  22.4 6.1 %collective-permute-start.7 = (bf16[272,256]{1,0:T(8,128)(2,1)S(1)}, bf16[272,256]{1,0:T(8,128)(2,1)S(1)}, u32[]{:S(2)}, u32[]{:S(2)}) collective-permute-start(bf16[272,256]{1,0:T(8,128)(2,1)S(1)} %collective-permute-done.2.east.refs_3_), channel_id=1, source_target_pairs={{1,0},{0,1},{3,2},{2,3},{5,4},{4,5},{7,6},{6,7},{9,8},{8,9},{11,10... | collective-permute-start | bytes 417800 | tf_op jit(solution)/shard_map/ppermute | solution.py:27
  30.9 5.6 %copy-start.1 = (bf16[512,512]{1,0:T(8,128)(2,1)S(1)}, bf16[512,512]{1,0:T(8,128)(2,1)}, u32[]{:S(2)}) copy-start(bf16[512,512]{1,0:T(8,128)(2,1)} %get-tuple-element.109.refs_2_) | copy-start | bytes 1572868
  30.9 5.6 %collective-permute-start.8 = (bf16[256,256]{1,0:T(8,128)(2,1)S(1)}, bf16[256,256]{1,0:T(8,128)(2,1)S(1)}, u32[]{:S(2)}, u32[]{:S(2)}) collective-permute-start(bf16[256,256]{1,0:T(8,128)(2,1)S(1)} %get-tuple-element.108.refs_0_), channel_id=1, source_target_pairs={{2,0},{0,2},{3,1},{1,3},{6,4},{4,6},{7,5},{5,7},{10,8},{8,10},{11,... | collective-permute-start | bytes 393224 | tf_op jit(solution)/shard_map/ppermute | solution.py:27
  34.9 5.3 %collective-permute-start.9 = (bf16[256,256]{1,0:T(8,128)(2,1)S(1)}, bf16[256,256]{1,0:T(8,128)(2,1)S(1)}, u32[]{:S(2)}, u32[]{:S(2)}) collective-permute-start(bf16[256,256]{1,0:T(8,128)(2,1)S(1)} %get-tuple-element.116.refs_0_), channel_id=1, source_target_pairs={{2,0},{0,2},{3,1},{1,3},{6,4},{4,6},{7,5},{5,7},{10,8},{8,10},{11,... | collective-permute-start | bytes 393224 | tf_op jit(solution)/shard_map/ppermute | solution.py:27
  41.7 6.3 %collective-permute-start.10 = (bf16[256,256]{1,0:T(8,128)(2,1)S(1)}, bf16[256,256]{1,0:T(8,128)(2,1)S(1)}, u32[]{:S(2)}, u32[]{:S(2)}) collective-permute-start(bf16[256,256]{1,0:T(8,128)(2,1)S(1)} %get-tuple-element.123), channel_id=1, source_target_pairs={{0,13},{1,4},{4,1},{5,8},{8,5},{9,12},{12,9},{13,0},{2,15},{3,6},{... | collective-permute-start | bytes 393224 | tf_op jit(solution)/shard_map/ppermute | solution.py:562
  42.9 5.2 %collective-permute-start.11 = (bf16[2,256,256]{2,1,0:T(8,128)(2,1)S(1)}, bf16[2,256,256]{2,1,0:T(8,128)(2,1)S(1)}, u32[]{:S(2)}, u32[]{:S(2)}) collective-permute-start(bf16[2,256,256]{2,1,0:T(8,128)(2,1)S(1)} %shard_map.171), channel_id=1, source_target_pairs={{1,0},{0,1},{3,2},{2,3},{5,4},{4,5},{7,6},{6,7},{9,8},{8,9},{11,10... | collective-permute-start | bytes 786440 | tf_op jit(solution)/shard_map/ppermute | solution.py:27
  45.6 7.9 %collective-permute-start.12 = (bf16[256,256]{1,0:T(8,128)(2,1)S(1)}, bf16[256,256]{1,0:T(8,128)(2,1)S(1)}, u32[]{:S(2)}, u32[]{:S(2)}) collective-permute-start(bf16[256,256]{1,0:T(8,128)(2,1)S(1)} %get-tuple-element.137), channel_id=1, source_target_pairs={{1,0},{0,1},{3,2},{2,3},{5,4},{4,5},{7,6},{6,7},{9,8},{8,9},{11,10... | collective-permute-start | bytes 393224 | tf_op jit(solution)/shard_map/ppermute | solution.py:27
  48.2 5.4 %collective-permute-start.13 = (bf16[256,256]{1,0:T(8,128)(2,1)S(1)}, bf16[256,256]{1,0:T(8,128)(2,1)S(1)}, u32[]{:S(2)}, u32[]{:S(2)}) collective-permute-start(bf16[256,256]{1,0:T(8,128)(2,1)S(1)} %get-tuple-element.127), channel_id=1, source_target_pairs={{4,0},{8,4},{12,8},{0,12},{5,1},{9,5},{13,9},{1,13},{6,2},{10,6},{... | collective-permute-start | bytes 393224 | tf_op jit(solution)/shard_map/ppermute | solution.py:27
  49.7 2.6 %copy-start.4 = (bf16[256,512]{1,0:T(8,128)(2,1)S(1)}, bf16[256,512]{1,0:T(8,128)(2,1)}, u32[]{:S(2)}) copy-start(bf16[256,512]{1,0:T(8,128)(2,1)} %get-tuple-element.83.w_node_v_t) | copy-start | bytes 786436
  49.7 7.4 %collective-permute-start.14 = (bf16[256,256]{1,0:T(8,128)(2,1)S(1)}, bf16[256,256]{1,0:T(8,128)(2,1)S(1)}, u32[]{:S(2)}, u32[]{:S(2)}) collective-permute-start(bf16[256,256]{1,0:T(8,128)(2,1)S(1)} %get-tuple-element.138), channel_id=1, source_target_pairs={{12,0},{0,4},{4,8},{8,12},{13,1},{1,5},{5,9},{9,13},{14,2},{2,6},{... | collective-permute-start | bytes 393224 | tf_op jit(solution)/shard_map/ppermute | solution.py:27
  54.3 5.1 %collective-permute-start.16 = (bf16[256,256]{1,0:T(8,128)(2,1)S(1)}, bf16[256,256]{1,0:T(8,128)(2,1)S(1)}, u32[]{:S(2)}, u32[]{:S(2)}) collective-permute-start(bf16[256,256]{1,0:T(8,128)(2,1)S(1)} %bitcast.22), channel_id=1, source_target_pairs={{2,0},{0,2},{3,1},{1,3},{6,4},{4,6},{7,5},{5,7},{10,8},{8,10},{11,... | collective-permute-start | bytes 393224 | tf_op jit(solution)/shard_map/ppermute | solution.py:27
  57.5 1.9 %collective-permute-start.15 = (bf16[4,64,256]{2,1,0:T(8,128)(2,1)S(1)}, bf16[4,64,256]{2,1,0:T(8,128)(2,1)S(1)}, u32[]{:S(2)}, u32[]{:S(2)}) collective-permute-start(bf16[4,64,256]{2,1,0:T(8,128)(2,1)S(1)} %get-tuple-element.148), channel_id=1, source_target_pairs={{1,0},{0,1},{3,2},{2,3},{5,4},{4,5},{7,6},{6,7},{9,8},{8,9},{11,10... | collective-permute-start | bytes 393224 | tf_op jit(solution)/shard_map/ppermute | solution.py:27
  59.5 6.3 %collective-permute-start.20 = (bf16[64,256]{1,0:T(8,128)(2,1)S(1)}, bf16[64,256]{1,0:T(8,128)(2,1)S(1)}, u32[]{:S(2)}, u32[]{:S(2)}) collective-permute-start(bf16[64,256]{1,0:T(8,128)(2,1)S(1)} %get-tuple-element.159), channel_id=1, source_target_pairs={{0,12},{4,8},{8,4},{12,0},{1,13},{5,9},{9,5},{13,1},{2,14},{6,10},... | collective-permute-start | bytes 98312 | tf_op jit(solution)/shard_map/ppermute | solution.py:805
  63.8 4.8 %collective-permute-start.19 = (bf16[64,256]{1,0:T(8,128)(2,1)S(1)}, bf16[64,256]{1,0:T(8,128)(2,1)S(1)}, u32[]{:S(2)}, u32[]{:S(2)}) collective-permute-start(bf16[64,256]{1,0:T(8,128)(2,1)S(1)} %get-tuple-element.160), channel_id=1, source_target_pairs={{0,8},{4,12},{8,0},{12,4},{1,9},{5,13},{9,1},{13,5},{2,10},{6,14},... | collective-permute-start | bytes 98312 | tf_op jit(solution)/shard_map/ppermute | solution.py:805
  63.8 4.8 %collective-permute-start.18 = (bf16[64,256]{1,0:T(8,128)(2,1)S(1)}, bf16[64,256]{1,0:T(8,128)(2,1)S(1)}, u32[]{:S(2)}, u32[]{:S(2)}) collective-permute-start(bf16[64,256]{1,0:T(8,128)(2,1)S(1)} %get-tuple-element.161), channel_id=1, source_target_pairs={{0,4},{4,0},{8,12},{12,8},{1,5},{5,1},{9,13},{13,9},{2,6},{6,2},{1... | collective-permute-start | bytes 98312 | tf_op jit(solution)/shard_map/ppermute | solution.py:805
  64.9 5.0 %collective-permute-start.17 = (bf16[256,256]{1,0:T(8,128)(2,1)S(1)}, bf16[256,256]{1,0:T(8,128)(2,1)S(1)}, u32[]{:S(2)}, u32[]{:S(2)}) collective-permute-start(bf16[256,256]{1,0:T(8,128)(2,1)S(1)} %bitcast.21), channel_id=1, source_target_pairs={{2,0},{0,2},{3,1},{1,3},{6,4},{4,6},{7,5},{5,7},{10,8},{8,10},{11,... | collective-permute-start | bytes 393224 | tf_op jit(solution)/shard_map/ppermute | solution.py:27

commit v14 on v9

--- a/solution.py
+++ b/solution.py
@@ -365,7 +365,7 @@
         grads[m] = (ref[m].astype(jnp.float32) * scale[...]).astype(jnp.bfloat16)
         return grads[m]
 
-    chunks = [chunk_of(place, nodes // CHUNK, (1, PACK, nodes)) for place in EARLY]
+    chunks = [chunk_of(place, nodes // CHUNK, (1, PACK, nodes)) for place in EARLY + LATE]
     total[...] = jnp.zeros_like(total)
     scatter(low, high, pairs(0, slope, nodes, grad_of), chunks, total)
 
@@ -386,7 +386,7 @@
 def other_kernel(start, low, high, grads, before, west, east, to_other, total):
     nodes = low.shape[2]
     chunks = [chunk_of(place, nodes // CHUNK, (1, PACK, nodes)) for place in EARLY[1:]]
-    total[...] = before[CHUNK:, :]
+    total[...] = before[CHUNK : len(EARLY) * CHUNK, :]
     scatter(low, high, pairs(start, grads, nodes, lambda ref, m: ref[m]), chunks, total)
     to_other[0] = fold(west, EARLY[1], 0, total)
     to_other[1] = fold(east, EARLY[2], 1, total)
@@ -400,13 +400,13 @@
     return steps
 
 
-def late_kernel(low, high, *refs):
-    *parts, west, east, beside, to_west, to_east, to_beside, total = refs
+def late_kernel(
+    start, low, high, grads, before, west, east, beside, to_west, to_east, to_beside, total
+):
     nodes = low.shape[2]
-    first = nodes // CHUNK
-    chunks = [chunk_of(place, first, (1, PACK, nodes)) for place in LATE]
-    total[...] = jnp.zeros_like(total)
-    scatter(low, high, all_pairs(parts, nodes), chunks, total)
+    chunks = [chunk_of(place, nodes // CHUNK, (1, PACK, nodes)) for place in LATE]
+    total[...] = before[len(EARLY) * CHUNK :, :]
+    scatter(low, high, pairs(start, grads, nodes, lambda ref, m: ref[m]), chunks, total)
     to_west[...] = fold(west, 1, 0, total)
     to_east[...] = fold(east, 2, 1, total)
     to_beside[...] = fold(beside, 0, 2, total)
@@ -681,7 +681,7 @@
         messages.append(gathered(message, "ch"))
 
     block = shape((slot_rows, hid), bf16)
-    sums = shape((len(EARLY) * slot_rows, hid), f32)
+    sums = shape((slots * slot_rows, hid), f32)
     grad_shape = shape((degree, rows, hid), bf16)
     for k in range(halves):
         hidden, grad_pre, scale = call(
@@ -717,13 +717,13 @@
             )
         grads.append(grad)
 
-    grads[0], to_other = lax.optimization_barrier((grads[0], to_other))
+    before, to_other = lax.optimization_barrier((before, to_other))
     from_other = shifted(to_other, "sub", 1)
     from_cross = across(to_cross)
     to_west, to_east, to_beside = call(
-        late_kernel,
+        functools.partial(late_kernel, nodes - rows),
         (block, block, block),
-        [low_rows, high_rows] + grads + [west, east, beside],
+        [low_rows, high_rows, grads[-1], before, west, east, beside],
         scratch=[pltpu.VMEM((len(LATE) * slot_rows, hid), f32)],
         scalars=0,
     )

time: 69.6 us -> 70.8 us (1.017)
  starting transfers between devices: 19 us -> 20.3 us
    ppermute x16, waiting for transfers between devices: 9.91 us -> 6.76 us  [shifted(): return lax.ppermute(block, axis, route)]
    ppermute x2, waiting for transfers between devices: 5.32 us -> 7.13 us  [shards(): w_beside = lax.ppermute(w_sent, 'lon', [(i, i ^ span) for i in range(lons)])]
    ppermute x16, starting transfers between devices: 15.5 us -> 17.3 us  [shifted(): return lax.ppermute(block, axis, route)]
    ppermute x1, waiting for transfers between devices: 1.86 us -> 2.95 us  [shards(): across = lambda block: lax.ppermute(block, cycle, across_route)]
    ppermute x2, starting transfers between devices: 3.29 us -> 2.54 us  [shards(): w_beside = lax.ppermute(w_sent, 'lon', [(i, i ^ span) for i in range(lons)])]
where the time goes in v14:
time: 70.8 us; the launch traced here: 70.6 us
  Pallas kernels  31.1 us (44%)
  starting transfers between devices  20.3 us (29%)
  waiting for transfers between devices  17.5 us (25%)
  between operations  1.67 us (2%)
    pallas_call x29, Pallas kernels, call(): pl.pallas_call(kernel, out_shape=out_shape, in_specs=[smem] * scalars + [...  31.1 us
    ppermute x16, starting transfers between devices, shifted(): return lax.ppermute(block, axis, route)  17.3 us
    ppermute x2, waiting for transfers between devices, shards(): w_beside = lax.ppermute(w_sent, 'lon', [(i, i ^ span) for i in range(lons)])  7.13 us
    ppermute x16, waiting for transfers between devices, shifted(): return lax.ppermute(block, axis, route)  6.76 us
    ppermute x1, waiting for transfers between devices, shards(): across = lambda block: lax.ppermute(block, cycle, across_route)  2.95 us
    ppermute x2, starting transfers between devices, shards(): w_beside = lax.ppermute(w_sent, 'lon', [(i, i ^ span) for i in range(lons)])  2.54 us
  transfers between devices with their start and end apart: 20, of which 11 were waited for; matrix products, arithmetic and copies ran while one was open for 0% of the time, Pallas kernels for 36%

profile of v14, /device:TPU:0, one launch (start us, length us, event | category | flops | bytes accessed | tf_op | source)
XLA Modules:
  0.0 70.6 jit_solution(4089727126859826143)
XLA Ops:
  0.7 3.0 %collective-permute-start = (bf16[256,512]{1,0:T(8,128)(2,1)}, bf16[256,512]{1,0:T(8,128)(2,1)S(1)}, u32[]{:S(2)}, u32[]{:S(2)}) collective-permute-start(bf16[256,512]{1,0:T(8,128)(2,1)} %refs_2_.1), channel_id=1, source_target_pairs={{2,0},{0,2},{3,1},{1,3},{6,4},{4,6},{7,5},{5,7},{10,8},{8,10},{11,... | collective-permute-start | bytes 786440 | tf_op jit(solution)/shard_map/ppermute | solution.py:26
  3.7 3.3 %shard_map.157 = (bf16[256,512]{1,0:T(8,128)(2,1)S(1)}, bf16[256,512]{1,0:T(8,128)(2,1)S(1)}, bf16[256,512]{1,0:T(8,128)(2,1)S(1)}, bf16[256,512]{1,0:T(8,128)(2...) custom-call(bf16[512,512]{1,0:T(8,128)(2,1)} %refs_0_.1, ...), custom_call_target="tpu_custom_call" | custom-call | flops 1024 | bytes 1024 | tf_op jit(solution)/shard_map/pallas_call | solution.py:51
  7.7 2.5 %collective-permute-done.refs_1_ = bf16[256,512]{1,0:T(8,128)(2,1)S(1)} collective-permute-done((bf16[256,512]{1,0:T(8,128)(2,1)}, bf16[256,512]{1,0:T(8,128)(2,1)S(1)}, u32[]{:S(2)}, u32[]{:S(2)}) %collective-permute-start) | collective-permute-done | bytes 262176 | tf_op jit(solution)/shard_map/ppermute | solution.py:26
  10.2 1.1 %shard_map.158 = (bf16[512,512]{1,0:T(8,128)(2,1)S(1)}, bf16[512,256]{1,0:T(8,128)(2,1)S(1)}, bf16[272,256]{1,0:T(8,128)(2,1)S(1)}, bf16[272,256]{1,0:T(8,128)(2...) custom-call(s32[1]{0:T(128)S(6)} %copy.17.tiles, s32[1,2,6]{2,1,0:T(2,128)S(1)} %bitcast.14, ...), custom_call_target="tpu_custom_call" | custom-call | flops 1024 | bytes 1024 | tf_op jit(solution)/shard_map/pallas_call | solution.py:51
  11.3 1.9 %collective-permute-start.1 = (bf16[272,256]{1,0:T(8,128)(2,1)S(1)}, bf16[272,256]{1,0:T(8,128)(2,1)S(1)}, u32[]{:S(2)}, u32[]{:S(2)}) collective-permute-start(bf16[272,256]{1,0:T(8,128)(2,1)S(1)} %get-tuple-element.94), channel_id=1, source_target_pairs={{12,0},{0,4},{4,8},{8,12},{13,1},{1,5},{5,9},{9,13},{14,2},{2,6},{... | collective-permute-start | bytes 417800 | tf_op jit(solution)/shard_map/ppermute | solution.py:26
  13.2 2.1 %collective-permute-start.2 = (bf16[272,256]{1,0:T(8,128)(2,1)S(1)}, bf16[272,256]{1,0:T(8,128)(2,1)S(1)}, u32[]{:S(2)}, u32[]{:S(2)}) collective-permute-start(bf16[272,256]{1,0:T(8,128)(2,1)S(1)} %get-tuple-element.95), channel_id=1, source_target_pairs={{4,0},{8,4},{12,8},{0,12},{5,1},{9,5},{13,9},{1,13},{6,2},{10,6},{... | collective-permute-start | bytes 417800 | tf_op jit(solution)/shard_map/ppermute | solution.py:26
  15.7 1.7 %collective-permute-start.4 = (bf16[256,512]{1,0:T(8,128)(2,1)S(1)}, bf16[256,512]{1,0:T(8,128)(2,1)S(1)}, u32[]{:S(2)}, u32[]{:S(2)}) collective-permute-start(bf16[256,512]{1,0:T(8,128)(2,1)S(1)} %copy-done.2), channel_id=1, source_target_pairs={{2,0},{0,2},{3,1},{1,3},{6,4},{4,6},{7,5},{5,7},{10,8},{8,10},{11,... | collective-permute-start | bytes 786440 | tf_op jit(solution)/shard_map/ppermute | solution.py:26
  17.4 1.0 %shard_map.160 = (bf16[12,512,128]{2,1,0:T(8,128)(2,1)S(1)}, bf16[12,512,128]{2,1,0:T(8,128)(2,1)S(1)}, bf16[12,16,512]{2,1,0:T(8,128)(2,1)S(1)}, bf16[12,16,512]{2,1,0:T(8,128)(2,1)S(1)}) custom-call(s32[1]{0:T(128)S(6)} %copy.17.tiles, s32[12,512]{1,0:T(8,128)S(1)} %copy-done.6, s32[1,512]{1,0:T(1,128)S(1)} %bitcast.7), custom_call_target="tpu_custom_call" | custom-call | flops 1024 | bytes 1024 | tf_op jit(solution)/shard_map/pallas_call | solution.py:51
  18.5 2.9 %shard_map.161.before = bf16[12,512,256]{2,1,0:T(8,128)(2,1)S(1)} custom-call(bf16[12,512,128]{2,1,0:T(8,128)(2,1)S(1)} %get-tuple-element.91.low, bf16[12,512,128]{2,1,0:T(8,128)(2,1)S(1)} %get-tuple-element.92.high, bf16[512,256]{1,0:T(8,128)(2,1)S(1)} %get-tuple-element.96.proj, bf16[272,256]{1,0:T(8,128)(2,1)S(1)} %collective-permute-done.3.beside), custom_call_target="tpu_custom_call" | custom-call | flops 1024 | bytes 1024 | tf_op jit(solution)/shard_map/pallas_call | solution.py:51
  22.4 1.6 %collective-permute-done.4.refs_1_ = bf16[256,512]{1,0:T(8,128)(2,1)S(1)} collective-permute-done((bf16[256,512]{1,0:T(8,128)(2,1)S(1)}, bf16[256,512]{1,0:T(8,128)(2,1)S(1)}, u32[]{:S(2)}, u32[]{:S(2)}) %collective-permute-start.4) | collective-permute-done | bytes 262176 | tf_op jit(solution)/shard_map/ppermute | solution.py:26
  24.1 1.1 %shard_map.162 = (bf16[512,512]{1,0:T(8,128)(2,1)}, f32[512,512]{1,0:T(8,128)S(1)}, f32[512,512]{1,0:T(8,128)S(1)}) custom-call(s32[1]{0:T(128)S(6)} %copy.17.tiles, bf16[256,512]{1,0:T(8,128)(2,1)S(1)} %copy-done.2, bf16[256,512]{1,0:T(8,128)(2,1)S(1)} %collective-permute-done.4.refs_1_, bf16[512,512]{1,0:T(8,128)(2,1)S(1)} %get-tuple-element.86.feats.refs_2_, ...), custom_call_target="tpu_custom_call" | custom-call | flops 1024 | bytes 1024 | tf_op jit(solution)/shard_map/pallas_call | solution.py:51
  25.2 2.5 %shard_map.163.part = bf16[12,512,256]{2,1,0:T(8,128)(2,1)S(1)} custom-call(bf16[12,512,128]{2,1,0:T(8,128)(2,1)S(1)} %get-tuple-element.91.low, bf16[12,512,128]{2,1,0:T(8,128)(2,1)S(1)} %get-tuple-element.92.high, bf16[12,512,256]{2,1,0:T(8,128)(2,1)S(1)} %shard_map.161.before, bf16[272,256]{1,0:T(8,128)(2,1)S(1)} %collective-permute-done.1.west, ...), custom_call_target="tpu_custom_call" | custom-call | flops 1024 | bytes 1024 | tf_op jit(solution)/shard_map/pallas_call | solution.py:51
  28.4 2.5 %shard_map.167 = (bf16[256,256]{1,0:T(8,128)(2,1)S(1)}, bf16[12,256,256]{2,1,0:T(8,128)(2,1)S(1)}) custom-call(bf16[12,512,128]{2,1,0:T(8,128)(2,1)S(1)} %get-tuple-element.91.low, bf16[12,512,128]{2,1,0:T(8,128)(2,1)S(1)} %get-tuple-element.92.high, f32[512,256]{1,0:T(8,128)S(1)} %shard_map.159.base, s32[1,512]{1,0:T(1,128)S(1)} %bitcast.8, ...), custom_call_target="tpu_custom_call" | custom-call | flops 1024 | bytes 1024 | tf_op jit(solution)/shard_map/pallas_call | solution.py:51
  30.9 1.6 %collective-permute-start.9 = (bf16[256,256]{1,0:T(8,128)(2,1)S(1)}, bf16[256,256]{1,0:T(8,128)(2,1)S(1)}, u32[]{:S(2)}, u32[]{:S(2)}) collective-permute-start(bf16[256,256]{1,0:T(8,128)(2,1)S(1)} %get-tuple-element.116.refs_0_), channel_id=1, source_target_pairs={{2,0},{0,2},{3,1},{1,3},{6,4},{4,6},{7,5},{5,7},{10,8},{8,10},{11,... | collective-permute-start | bytes 393224 | tf_op jit(solution)/shard_map/ppermute | solution.py:26
  32.5 2.5 %shard_map.165 = (bf16[256,256]{1,0:T(8,128)(2,1)S(1)}, bf16[12,256,256]{2,1,0:T(8,128)(2,1)S(1)}) custom-call(bf16[12,512,128]{2,1,0:T(8,128)(2,1)S(1)} %get-tuple-element.91.low, bf16[12,512,128]{2,1,0:T(8,128)(2,1)S(1)} %get-tuple-element.92.high, f32[512,256]{1,0:T(8,128)S(1)} %shard_map.159.base, s32[1,512]{1,0:T(1,128)S(1)} %bitcast.9, ...), custom_call_target="tpu_custom_call" | custom-call | flops 1024 | bytes 1024 | tf_op jit(solution)/shard_map/pallas_call | solution.py:51
  35.5 1.0 %collective-permute-done.9.refs_1_ = bf16[256,256]{1,0:T(8,128)(2,1)S(1)} collective-permute-done((bf16[256,256]{1,0:T(8,128)(2,1)S(1)}, bf16[256,256]{1,0:T(8,128)(2,1)S(1)}, u32[]{:S(2)}, u32[]{:S(2)}) %collective-permute-start.9) | collective-permute-done | bytes 131104 | tf_op jit(solution)/shard_map/ppermute | solution.py:26
  36.5 0.9 %shard_map.168 = (bf16[512,256]{1,0:T(8,128)(2,1)S(1)}, bf16[512,256]{1,0:T(8,128)(2,1)S(1)}, f32[256,256]{1,0:T(8,128)S(1)}) custom-call(s32[1,512]{1,0:T(1,128)S(1)} %bitcast.10, bf16[256,256]{1,0:T(8,128)(2,1)S(1)} %get-tuple-element.116.refs_0_, bf16[256,256]{1,0:T(8,128)(2,1)S(1)} %collective-permute-done.9.refs_1_, bf16[512,512]{1,0:T(8,128)(2,1)S(1)} %copy-done.1, ...), custom_call_target="tpu_custom_call" | custom-call | flops 1024 | bytes 1024 | tf_op jit(solution)/shard_map/pallas_call | solution.py:51
  37.4 2.7 %shard_map.169 = (bf16[12,256,256]{2,1,0:T(8,128)(2,1)S(1)}, f32[1536,256]{1,0:T(8,128)S(1)}) custom-call(bf16[12,16,512]{2,1,0:T(8,128)(2,1)S(1)} %get-tuple-element.89.low, bf16[12,16,512]{2,1,0:T(8,128)(2,1)S(1)} %get-tuple-element.90.high, bf16[12,256,256]{2,1,0:T(8,128)(2,1)S(1)} %get-tuple-element.115.slope, f32[256,256]{1,0:T(8,128)S(1)} %get-tuple-element.117.scale), custom_call_target="tpu_custom_call" | custom-call | flops 1024 | bytes 1024 | tf_op jit(solution)/shard_map/pallas_call | solution.py:51
  40.3 0.7 %shard_map.166 = (bf16[512,256]{1,0:T(8,128)(2,1)S(1)}, bf16[512,256]{1,0:T(8,128)(2,1)S(1)}, f32[256,256]{1,0:T(8,128)S(1)}) custom-call(s32[1,512]{1,0:T(1,128)S(1)} %bitcast.11, bf16[256,256]{1,0:T(8,128)(2,1)S(1)} %get-tuple-element.109.refs_0_, bf16[256,256]{1,0:T(8,128)(2,1)S(1)} %collective-permute-done.8.refs_1_, bf16[512,512]{1,0:T(8,128)(2,1)S(1)} %copy-done.1, ...), custom_call_target="tpu_custom_call" | custom-call | flops 1024 | bytes 1024 | tf_op jit(solution)/shard_map/pallas_call | solution.py:51
  42.2 1.0 %shard_map.171 = bf16[2,256,256]{2,1,0:T(8,128)(2,1)S(1)} custom-call(bf16[12,16,512]{2,1,0:T(8,128)(2,1)S(1)} %get-tuple-element.89.low, bf16[12,16,512]{2,1,0:T(8,128)(2,1)S(1)} %get-tuple-element.90.high, bf16[12,256,256]{2,1,0:T(8,128)(2,1)S(1)} %get-tuple-element.119.grads.refs_1_, f32[1536,256]{1,0:T(8,128)S(1)} %get-tuple-element.120.before, ...), custom_call_target="tpu_custom_call" | custom-call | flops 1024 | bytes 1024 | tf_op jit(solution)/shard_map/pallas_call | solution.py:51
  43.3 1.4 %shard_map.172 = (bf16[256,256]{1,0:T(8,128)(2,1)S(1)}, bf16[256,256]{1,0:T(8,128)(2,1)S(1)}, bf16[256,256]{1,0:T(8,128)(2,1)S(1)}) custom-call(bf16[12,16,512]{2,1,0:T(8,128)(2,1)S(1)} %get-tuple-element.89.low, bf16[12,16,512]{2,1,0:T(8,128)(2,1)S(1)} %get-tuple-element.90.high, bf16[12,256,256]{2,1,0:T(8,128)(2,1)S(1)} %get-tuple-element.119.grads.refs_1_, ...), custom_call_target="tpu_custom_call" | custom-call | flops 1024 | bytes 1024 | tf_op jit(solution)/shard_map/pallas_call | solution.py:51
  45.2 2.9 %collective-permute-done.10.across = bf16[256,256]{1,0:T(8,128)(2,1)S(1)} collective-permute-done((bf16[256,256]{1,0:T(8,128)(2,1)S(1)}, bf16[256,256]{1,0:T(8,128)(2,1)S(1)}, u32[]{:S(2)}, u32[]{:S(2)}) %collective-permute-start.10) | collective-permute-done | bytes 131104 | tf_op jit(solution)/shard_map/ppermute | solution.py:558
  48.3 1.1 %collective-permute-start.13 = (bf16[256,256]{1,0:T(8,128)(2,1)S(1)}, bf16[256,256]{1,0:T(8,128)(2,1)S(1)}, u32[]{:S(2)}, u32[]{:S(2)}) collective-permute-start(bf16[256,256]{1,0:T(8,128)(2,1)S(1)} %get-tuple-element.127), channel_id=1, source_target_pairs={{4,0},{8,4},{12,8},{0,12},{5,1},{9,5},{13,9},{1,13},{6,2},{10,6},{... | collective-permute-start | bytes 393224 | tf_op jit(solution)/shard_map/ppermute | solution.py:26
  49.4 1.0 %collective-permute-start.14 = (bf16[256,256]{1,0:T(8,128)(2,1)S(1)}, bf16[256,256]{1,0:T(8,128)(2,1)S(1)}, u32[]{:S(2)}, u32[]{:S(2)}) collective-permute-start(bf16[256,256]{1,0:T(8,128)(2,1)S(1)} %get-tuple-element.139), channel_id=1, source_target_pairs={{12,0},{0,4},{4,8},{8,12},{13,1},{1,5},{5,9},{9,13},{14,2},{2,6},{... | collective-permute-start | bytes 393224 | tf_op jit(solution)/shard_map/ppermute | solution.py:26
  50.4 2.1 %shard_map.175 = (f32[512,256]{1,0:T(8,128)S(1)}, bf16[256,512]{1,0:T(8,128)(2,1)S(1)}) custom-call(bf16[12,16,512]{2,1,0:T(8,128)(2,1)S(1)} %get-tuple-element.89.low, bf16[12,16,512]{2,1,0:T(8,128)(2,1)S(1)} %get-tuple-element.90.high, bf16[12,256,256]{2,1,0:T(8,128)(2,1)S(1)} %get-tuple-element.129.refs_0_, ...), custom_call_target="tpu_custom_call" | custom-call | flops 1024 | bytes 1024 | tf_op jit(solution)/shard_map/pallas_call | solution.py:51
  52.5 1.2 %shard_map.176 = (bf16[256,512]{1,0:T(8,128)(2,1)}, f32[256,512]{1,0:T(8,128)S(1)}) custom-call(s32[1]{0:T(128)S(6)} %copy.17.tiles, bf16[256,512]{1,0:T(8,128)(2,1)S(1)} %get-tuple-element.82.refs_0_.feats, bf16[256,512]{1,0:T(8,128)(2,1)S(1)} %copy-done.2, bf16[256,512]{1,0:T(8,128)(2,1)S(1)} %get-tuple-element.83.w_out, bf16[256,512]{1,0:T(8,128)(2,1)S(1)} %copy-done.4, ...), custom_call_target="tpu_custom_call" | custom-call | flops 1024 | bytes 1024 | tf_op jit(solution)/shard_map/pallas_call | solution.py:51
  54.4 1.6 %collective-permute-start.17 = (bf16[256,256]{1,0:T(8,128)(2,1)S(1)}, bf16[256,256]{1,0:T(8,128)(2,1)S(1)}, u32[]{:S(2)}, u32[]{:S(2)}) collective-permute-start(bf16[256,256]{1,0:T(8,128)(2,1)S(1)} %bitcast.16), channel_id=1, source_target_pairs={{2,0},{0,2},{3,1},{1,3},{6,4},{4,6},{7,5},{5,7},{10,8},{8,10},{11,... | collective-permute-start | bytes 393224 | tf_op jit(solution)/shard_map/ppermute | solution.py:26
  56.0 0.8 %collective-permute-done.14.refs_0_ = bf16[256,256]{1,0:T(8,128)(2,1)S(1)} collective-permute-done((bf16[256,256]{1,0:T(8,128)(2,1)S(1)}, bf16[256,256]{1,0:T(8,128)(2,1)S(1)}, u32[]{:S(2)}, u32[]{:S(2)}) %collective-permute-start.14) | collective-permute-done | bytes 131104 | tf_op jit(solution)/shard_map/ppermute | solution.py:26
  57.8 1.5 %collective-permute-start.15 = (bf16[256,256]{1,0:T(8,128)(2,1)S(1)}, bf16[256,256]{1,0:T(8,128)(2,1)S(1)}, u32[]{:S(2)}, u32[]{:S(2)}) collective-permute-start(bf16[256,256]{1,0:T(8,128)(2,1)S(1)} %bitcast.15), channel_id=1, source_target_pairs={{2,0},{0,2},{3,1},{1,3},{6,4},{4,6},{7,5},{5,7},{10,8},{8,10},{11,... | collective-permute-start | bytes 393224 | tf_op jit(solution)/shard_map/ppermute | solution.py:26
  59.5 1.9 %collective-permute-start.18 = (bf16[2,64,256]{2,1,0:T(8,128)(2,1)S(1)}, bf16[2,64,256]{2,1,0:T(8,128)(2,1)S(1)}, u32[]{:S(2)}, u32[]{:S(2)}) collective-permute-start(bf16[2,64,256]{2,1,0:T(8,128)(2,1)S(1)} %get-tuple-element.158), channel_id=1, source_target_pairs={{0,8},{4,12},{8,0},{12,4},{1,9},{5,13},{9,1},{13,5},{2,10},{6,14},... | collective-permute-start | bytes 196616 | tf_op jit(solution)/shard_map/ppermute | solution.py:810
  61.5 4.5 %collective-permute-done.18.received = bf16[2,64,256]{2,1,0:T(8,128)(2,1)S(1)} collective-permute-done((bf16[2,64,256]{2,1,0:T(8,128)(2,1)S(1)}, bf16[2,64,256]{2,1,0:T(8,128)(2,1)S(1)}, u32[]{:S(2)}, u32[]{:S(2)}) %collective-permute-start.18) | collective-permute-done | bytes 65568 | tf_op jit(solution)/shard_map/ppermute | solution.py:810
  67.3 2.6 %collective-permute-done.19.received = bf16[1,64,256]{2,1,0:T(8,128)(2,1)S(1)} collective-permute-done((bf16[1,64,256]{2,1,0:T(8,128)(2,1)S(1)}, bf16[1,64,256]{2,1,0:T(8,128)(2,1)S(1)}, u32[]{:S(2)}, u32[]{:S(2)}) %collective-permute-start.19) | collective-permute-done | bytes 32800 | tf_op jit(solution)/shard_map/ppermute | solution.py:810
  (57 shorter events, 8.7 us)
Async XLA Ops:
  0.6 9.5 %copy-start.9 = (s32[1,6,2]{1,2,0:T(2,128)S(1)}, s32[1,6,2]{1,2,0:T(2,128)}, u32[]{:S(2)}) copy-start(s32[1,6,2]{1,2,0:T(2,128)} %param.19) | copy-start | bytes 148
  0.6 14.7 %copy-start.7 = (f32[512]{0:T(512)S(1)}, f32[512]{0:T(512)}, u32[]{:S(2)}) copy-start(f32[512]{0:T(512)} %param.22) | copy-start | bytes 6148
  0.7 9.5 %collective-permute-start = (bf16[256,512]{1,0:T(8,128)(2,1)}, bf16[256,512]{1,0:T(8,128)(2,1)S(1)}, u32[]{:S(2)}, u32[]{:S(2)}) collective-permute-start(bf16[256,512]{1,0:T(8,128)(2,1)} %refs_2_.1), channel_id=1, source_target_pairs={{2,0},{0,2},{3,1},{1,3},{6,4},{4,6},{7,5},{5,7},{10,8},{8,10},{11,... | collective-permute-start | bytes 786440 | tf_op jit(solution)/shard_map/ppermute | solution.py:26
  6.9 8.8 %copy-start.2 = (bf16[256,512]{1,0:T(8,128)(2,1)S(1)}, bf16[256,512]{1,0:T(8,128)(2,1)}, u32[]{:S(2)}) copy-start(bf16[256,512]{1,0:T(8,128)(2,1)} %cots.1) | copy-start | bytes 786436
  6.9 10.5 %copy-start.5 = (s32[512]{0:T(512)S(1)}, s32[512]{0:T(512)}, u32[]{:S(2)}) copy-start(s32[512]{0:T(512)} %param.17) | copy-start | bytes 6148
  7.0 10.5 %copy-start.6 = (s32[12,512]{1,0:T(8,128)S(1)}, s32[12,512]{1,0:T(8,128)}, u32[]{:S(2)}) copy-start(s32[12,512]{1,0:T(8,128)} %senders) | copy-start | bytes 73732
  11.3 7.2 %collective-permute-start.3 = (bf16[272,256]{1,0:T(8,128)(2,1)S(1)}, bf16[272,256]{1,0:T(8,128)(2,1)S(1)}, u32[]{:S(2)}, u32[]{:S(2)}) collective-permute-start(bf16[272,256]{1,0:T(8,128)(2,1)S(1)} %get-tuple-element.97), channel_id=1, source_target_pairs={{1,0},{0,1},{3,2},{2,3},{5,4},{4,5},{7,6},{6,7},{9,8},{8,9},{11,10... | collective-permute-start | bytes 417800 | tf_op jit(solution)/shard_map/ppermute | solution.py:26
  11.3 10.1 %collective-permute-start.1 = (bf16[272,256]{1,0:T(8,128)(2,1)S(1)}, bf16[272,256]{1,0:T(8,128)(2,1)S(1)}, u32[]{:S(2)}, u32[]{:S(2)}) collective-permute-start(bf16[272,256]{1,0:T(8,128)(2,1)S(1)} %get-tuple-element.94), channel_id=1, source_target_pairs={{12,0},{0,4},{4,8},{8,12},{13,1},{1,5},{5,9},{9,13},{14,2},{2,6},{... | collective-permute-start | bytes 417800 | tf_op jit(solution)/shard_map/ppermute | solution.py:26
  13.2 8.7 %collective-permute-start.2 = (bf16[272,256]{1,0:T(8,128)(2,1)S(1)}, bf16[272,256]{1,0:T(8,128)(2,1)S(1)}, u32[]{:S(2)}, u32[]{:S(2)}) collective-permute-start(bf16[272,256]{1,0:T(8,128)(2,1)S(1)} %get-tuple-element.95), channel_id=1, source_target_pairs={{4,0},{8,4},{12,8},{0,12},{5,1},{9,5},{13,9},{1,13},{6,2},{10,6},{... | collective-permute-start | bytes 417800 | tf_op jit(solution)/shard_map/ppermute | solution.py:26
  15.7 8.4 %collective-permute-start.4 = (bf16[256,512]{1,0:T(8,128)(2,1)S(1)}, bf16[256,512]{1,0:T(8,128)(2,1)S(1)}, u32[]{:S(2)}, u32[]{:S(2)}) collective-permute-start(bf16[256,512]{1,0:T(8,128)(2,1)S(1)} %copy-done.2), channel_id=1, source_target_pairs={{2,0},{0,2},{3,1},{1,3},{6,4},{4,6},{7,5},{5,7},{10,8},{8,10},{11,... | collective-permute-start | bytes 786440 | tf_op jit(solution)/shard_map/ppermute | solution.py:26
  17.4 11.0 %collective-permute-start.5 = (bf16[272,256]{1,0:T(8,128)(2,1)S(1)}, bf16[272,256]{1,0:T(8,128)(2,1)S(1)}, u32[]{:S(2)}, u32[]{:S(2)}) collective-permute-start(bf16[272,256]{1,0:T(8,128)(2,1)S(1)} %get-tuple-element.105), channel_id=1, source_target_pairs={{0,9},{1,8},{4,13},{5,12},{8,1},{9,0},{12,5},{13,4},{2,11},{3,10},... | collective-permute-start | bytes 417800 | tf_op jit(solution)/shard_map/ppermute | solution.py:614
  18.5 5.6 %copy-start = (bf16[512,512]{1,0:T(8,128)(2,1)S(1)}, bf16[512,512]{1,0:T(8,128)(2,1)}, u32[]{:S(2)}) copy-start(bf16[512,512]{1,0:T(8,128)(2,1)} %refs_3_.3) | copy-start | bytes 1572868
  18.5 5.6 %copy-start.3 = (bf16[512,512]{1,0:T(8,128)(2,1)S(1)}, bf16[512,512]{1,0:T(8,128)(2,1)}, u32[]{:S(2)}) copy-start(bf16[512,512]{1,0:T(8,128)(2,1)} %get-tuple-element.100.refs_5_) | copy-start | bytes 1572868
  18.5 5.6 %copy-start.8 = (f32[512]{0:T(512)S(1)}, f32[512]{0:T(512)}, u32[]{:S(2)}) copy-start(f32[512]{0:T(512)} %param.26) | copy-start | bytes 6148
  21.9 6.5 %collective-permute-start.6 = (bf16[272,256]{1,0:T(8,128)(2,1)S(1)}, bf16[272,256]{1,0:T(8,128)(2,1)S(1)}, u32[]{:S(2)}, u32[]{:S(2)}) collective-permute-start(bf16[272,256]{1,0:T(8,128)(2,1)S(1)} %collective-permute-done.1.west), channel_id=1, source_target_pairs={{1,0},{0,1},{3,2},{2,3},{5,4},{4,5},{7,6},{6,7},{9,8},{8,9},{11,10... | collective-permute-start | bytes 417800 | tf_op jit(solution)/shard_map/ppermute | solution.py:26
  22.4 6.1 %collective-permute-start.7 = (bf16[272,256]{1,0:T(8,128)(2,1)S(1)}, bf16[272,256]{1,0:T(8,128)(2,1)S(1)}, u32[]{:S(2)}, u32[]{:S(2)}) collective-permute-start(bf16[272,256]{1,0:T(8,128)(2,1)S(1)} %collective-permute-done.2.east), channel_id=1, source_target_pairs={{1,0},{0,1},{3,2},{2,3},{5,4},{4,5},{7,6},{6,7},{9,8},{8,9},{11,10... | collective-permute-start | bytes 417800 | tf_op jit(solution)/shard_map/ppermute | solution.py:26
  30.9 5.6 %copy-start.1 = (bf16[512,512]{1,0:T(8,128)(2,1)S(1)}, bf16[512,512]{1,0:T(8,128)(2,1)}, u32[]{:S(2)}) copy-start(bf16[512,512]{1,0:T(8,128)(2,1)} %get-tuple-element.110.refs_2_) | copy-start | bytes 1572868
  30.9 5.6 %collective-permute-start.9 = (bf16[256,256]{1,0:T(8,128)(2,1)S(1)}, bf16[256,256]{1,0:T(8,128)(2,1)S(1)}, u32[]{:S(2)}, u32[]{:S(2)}) collective-permute-start(bf16[256,256]{1,0:T(8,128)(2,1)S(1)} %get-tuple-element.116.refs_0_), channel_id=1, source_target_pairs={{2,0},{0,2},{3,1},{1,3},{6,4},{4,6},{7,5},{5,7},{10,8},{8,10},{11,... | collective-permute-start | bytes 393224 | tf_op jit(solution)/shard_map/ppermute | solution.py:26
  35.0 5.3 %collective-permute-start.8 = (bf16[256,256]{1,0:T(8,128)(2,1)S(1)}, bf16[256,256]{1,0:T(8,128)(2,1)S(1)}, u32[]{:S(2)}, u32[]{:S(2)}) collective-permute-start(bf16[256,256]{1,0:T(8,128)(2,1)S(1)} %get-tuple-element.109.refs_0_), channel_id=1, source_target_pairs={{2,0},{0,2},{3,1},{1,3},{6,4},{4,6},{7,5},{5,7},{10,8},{8,10},{11,... | collective-permute-start | bytes 393224 | tf_op jit(solution)/shard_map/ppermute | solution.py:26
  41.7 6.5 %collective-permute-start.10 = (bf16[256,256]{1,0:T(8,128)(2,1)S(1)}, bf16[256,256]{1,0:T(8,128)(2,1)S(1)}, u32[]{:S(2)}, u32[]{:S(2)}) collective-permute-start(bf16[256,256]{1,0:T(8,128)(2,1)S(1)} %get-tuple-element.123), channel_id=1, source_target_pairs={{0,13},{1,4},{4,1},{5,8},{8,5},{9,12},{12,9},{13,0},{2,15},{3,6},{... | collective-permute-start | bytes 393224 | tf_op jit(solution)/shard_map/ppermute | solution.py:558
  43.2 5.1 %collective-permute-start.11 = (bf16[2,256,256]{2,1,0:T(8,128)(2,1)S(1)}, bf16[2,256,256]{2,1,0:T(8,128)(2,1)S(1)}, u32[]{:S(2)}, u32[]{:S(2)}) collective-permute-start(bf16[2,256,256]{2,1,0:T(8,128)(2,1)S(1)} %shard_map.171), channel_id=1, source_target_pairs={{1,0},{0,1},{3,2},{2,3},{5,4},{4,5},{7,6},{6,7},{9,8},{8,9},{11,10... | collective-permute-start | bytes 786440 | tf_op jit(solution)/shard_map/ppermute | solution.py:26
  44.7 9.0 %collective-permute-start.12 = (bf16[256,256]{1,0:T(8,128)(2,1)S(1)}, bf16[256,256]{1,0:T(8,128)(2,1)S(1)}, u32[]{:S(2)}, u32[]{:S(2)}) collective-permute-start(bf16[256,256]{1,0:T(8,128)(2,1)S(1)} %get-tuple-element.138), channel_id=1, source_target_pairs={{1,0},{0,1},{3,2},{2,3},{5,4},{4,5},{7,6},{6,7},{9,8},{8,9},{11,10... | collective-permute-start | bytes 393224 | tf_op jit(solution)/shard_map/ppermute | solution.py:26
  48.3 5.3 %collective-permute-start.13 = (bf16[256,256]{1,0:T(8,128)(2,1)S(1)}, bf16[256,256]{1,0:T(8,128)(2,1)S(1)}, u32[]{:S(2)}, u32[]{:S(2)}) collective-permute-start(bf16[256,256]{1,0:T(8,128)(2,1)S(1)} %get-tuple-element.127), channel_id=1, source_target_pairs={{4,0},{8,4},{12,8},{0,12},{5,1},{9,5},{13,9},{1,13},{6,2},{10,6},{... | collective-permute-start | bytes 393224 | tf_op jit(solution)/shard_map/ppermute | solution.py:26
  49.4 7.4 %collective-permute-start.14 = (bf16[256,256]{1,0:T(8,128)(2,1)S(1)}, bf16[256,256]{1,0:T(8,128)(2,1)S(1)}, u32[]{:S(2)}, u32[]{:S(2)}) collective-permute-start(bf16[256,256]{1,0:T(8,128)(2,1)S(1)} %get-tuple-element.139), channel_id=1, source_target_pairs={{12,0},{0,4},{4,8},{8,12},{13,1},{1,5},{5,9},{9,13},{14,2},{2,6},{... | collective-permute-start | bytes 393224 | tf_op jit(solution)/shard_map/ppermute | solution.py:26
  50.4 2.1 %copy-start.4 = (bf16[256,512]{1,0:T(8,128)(2,1)S(1)}, bf16[256,512]{1,0:T(8,128)(2,1)}, u32[]{:S(2)}) copy-start(bf16[256,512]{1,0:T(8,128)(2,1)} %get-tuple-element.84.w_node_v_t) | copy-start | bytes 786436
  54.4 5.0 %collective-permute-start.17 = (bf16[256,256]{1,0:T(8,128)(2,1)S(1)}, bf16[256,256]{1,0:T(8,128)(2,1)S(1)}, u32[]{:S(2)}, u32[]{:S(2)}) collective-permute-start(bf16[256,256]{1,0:T(8,128)(2,1)S(1)} %bitcast.16), channel_id=1, source_target_pairs={{2,0},{0,2},{3,1},{1,3},{6,4},{4,6},{7,5},{5,7},{10,8},{8,10},{11,... | collective-permute-start | bytes 393224 | tf_op jit(solution)/shard_map/ppermute | solution.py:26
  57.3 2.2 %collective-permute-start.16 = (bf16[4,64,256]{2,1,0:T(8,128)(2,1)S(1)}, bf16[4,64,256]{2,1,0:T(8,128)(2,1)S(1)}, u32[]{:S(2)}, u32[]{:S(2)}) collective-permute-start(bf16[4,64,256]{2,1,0:T(8,128)(2,1)S(1)} %get-tuple-element.151), channel_id=1, source_target_pairs={{1,0},{0,1},{3,2},{2,3},{5,4},{4,5},{7,6},{6,7},{9,8},{8,9},{11,10... | collective-permute-start | bytes 393224 | tf_op jit(solution)/shard_map/ppermute | solution.py:26
  57.8 8.8 %collective-permute-start.15 = (bf16[256,256]{1,0:T(8,128)(2,1)S(1)}, bf16[256,256]{1,0:T(8,128)(2,1)S(1)}, u32[]{:S(2)}, u32[]{:S(2)}) collective-permute-start(bf16[256,256]{1,0:T(8,128)(2,1)S(1)} %bitcast.15), channel_id=1, source_target_pairs={{2,0},{0,2},{3,1},{1,3},{6,4},{4,6},{7,5},{5,7},{10,8},{8,10},{11,... | collective-permute-start | bytes 393224 | tf_op jit(solution)/shard_map/ppermute | solution.py:26
  59.5 6.4 %collective-permute-start.18 = (bf16[2,64,256]{2,1,0:T(8,128)(2,1)S(1)}, bf16[2,64,256]{2,1,0:T(8,128)(2,1)S(1)}, u32[]{:S(2)}, u32[]{:S(2)}) collective-permute-start(bf16[2,64,256]{2,1,0:T(8,128)(2,1)S(1)} %get-tuple-element.158), channel_id=1, source_target_pairs={{0,8},{4,12},{8,0},{12,4},{1,9},{5,13},{9,1},{13,5},{2,10},{6,14},... | collective-permute-start | bytes 196616 | tf_op jit(solution)/shard_map/ppermute | solution.py:810
  66.0 4.0 %collective-permute-start.19 = (bf16[1,64,256]{2,1,0:T(8,128)(2,1)S(1)}, bf16[1,64,256]{2,1,0:T(8,128)(2,1)S(1)}, u32[]{:S(2)}, u32[]{:S(2)}) collective-permute-start(bf16[1,64,256]{2,1,0:T(8,128)(2,1)S(1)} %get-tuple-element.160), channel_id=1, source_target_pairs={{0,4},{4,0},{8,12},{12,8},{1,5},{5,1},{9,13},{13,9},{2,6},{6,2},{1... | collective-permute-start | bytes 98312 | tf_op jit(solution)/shard_map/ppermute | solution.py:810

commit v15 on v14

--- a/solution.py
+++ b/solution.py
@@ -443,33 +443,30 @@
         direct[:, span] = cots[:, span].astype(jnp.float32) + dot(w_node_v_t[...], grad_pre[...])
 
 
-def across_kernel(left, right, across, west, east):
-    sub = lax.axis_index("sub")
-    other = across[...].astype(jnp.float32)
-    to_west = left[...].astype(jnp.float32) + jnp.where(sub == 0, 0.0, other)
-    to_east = right[...].astype(jnp.float32) + jnp.where(sub == 0, other, 0.0)
-    west[...] = to_west.astype(west.dtype)
-    east[...] = to_east.astype(east.dtype)
+def pass_kernel(block, out):
+    out[...] = block[...]
 
 
 def add_kernel(left, right, more, west, east):
-    west[...] = (left[...] + more[0].astype(jnp.float32)).astype(jnp.bfloat16)
-    east[...] = (right[...] + more[1].astype(jnp.float32)).astype(jnp.bfloat16)
-
-
-def back_kernel(start, inv_root, tiles, own, beside, feats, upper, *refs):
+    to_west = left[...].astype(jnp.float32) + more[0].astype(jnp.float32)
+    to_east = right[...].astype(jnp.float32) + more[1].astype(jnp.float32)
+    west[...] = to_west.astype(jnp.bfloat16)
+    east[...] = to_east.astype(jnp.bfloat16)
+
+
+def back_kernel(start, inv_root, tiles, own, beside, across, feats, upper, *refs):
     *refs, total = refs
     sub = lax.axis_index("sub")
     offset = pl.multiple_of(tiles[0] // 2 * TILE, TILE)
     total[...] = own[...]
-    near = beside[...].astype(jnp.float32)
-    block = upper[...].astype(jnp.float32) + jnp.where(sub == 0, near, 0.0)
+    near, far = beside[...].astype(jnp.float32), across[...].astype(jnp.float32)
+    block = upper[...].astype(jnp.float32) + jnp.where(sub == 0, near, far)
     total[pl.ds(offset, block.shape[0]), :] += block
     if start:
         grad_send, weight = refs
     else:
         lower, before, grad_send, w_mine, w_beside, weight = refs
-        block = lower[...].astype(jnp.float32) + jnp.where(sub == 0, 0.0, near)
+        block = lower[...].astype(jnp.float32) + jnp.where(sub == 0, far, near)
         total[: block.shape[0], :] += block
     rows = grad_send.shape[0]
     grad_send[...] = total[start : start + rows, :].astype(jnp.bfloat16)
@@ -719,7 +716,7 @@
 
     before, to_other = lax.optimization_barrier((before, to_other))
     from_other = shifted(to_other, "sub", 1)
-    from_cross = across(to_cross)
+    from_cross = lax.ppermute(to_cross, cycle, far_route)
     to_west, to_east, to_beside = call(
         functools.partial(late_kernel, nodes - rows),
         (block, block, block),
@@ -727,10 +724,6 @@
         scratch=[pltpu.VMEM((len(LATE) * slot_rows, hid), f32)],
         scalars=0,
     )
-    wide = shape((slot_rows, hid), f32)
-    to_west, to_east = call(
-        across_kernel, (wide, wide), [to_west, to_east, from_cross], scalars=0, flops=15 * 10**8
-    )
     to_west, to_east = call(add_kernel, (block, block), [to_west, to_east, from_other], scalars=0)
     from_upper = shifted(to_west, "lon", -1)
     from_lower = shifted(to_east, "lon", 1)
@@ -750,9 +743,11 @@
         [tile_count, features_held, cotangent, w_out_my, w_node_v_t] + hiddens + grad_pres,
         scalars=1,
     )
+    direct, from_cross = lax.optimization_barrier((direct, from_cross))
+    from_cross = call(pass_kernel, block, [from_cross], scalars=0, flops=10**9)
     columns = chans_all // shard_count
     inv_root = 1.0 / math.sqrt(total_nodes)
-    inputs = [tile_count, own, from_beside, feats, from_upper]
+    inputs = [tile_count, own, from_beside, from_cross, feats, from_upper]
     weight_shape = shape((chans_all, hid), f32)
     grad_shape = shape((rows, hid), bf16)
     finals = []

time: 70.8 us -> 74.2 us (1.048)
  waiting for transfers between devices: 17.5 us -> 23.1 us
  starting transfers between devices: 20.3 us -> 18.1 us
    ppermute x16, waiting for transfers between devices: 6.76 us -> 13.4 us  [shifted(): return lax.ppermute(block, axis, route)]
    ppermute x1, waiting for transfers between devices: 2.95 us -> 0.01 us  [shards(): from_cross = lax.ppermute(to_cross, cycle, far_route)]
    ppermute x2, starting transfers between devices: 2.54 us -> 0.14 us  [shards(): w_beside = lax.ppermute(w_sent, 'lon', [(i, i ^ span) for i in range(lons)])]
    ppermute x2, waiting for transfers between devices: 7.13 us -> 9.01 us  [shards(): w_beside = lax.ppermute(w_sent, 'lon', [(i, i ^ span) for i in range(lons)])]
    ppermute x1, starting transfers between devices: 0.47 us -> 2.02 us  [shards(): from_cross = lax.ppermute(to_cross, cycle, far_route)]
    ppermute x16, starting transfers between devices: 17.3 us -> 15.9 us  [shifted(): return lax.ppermute(block, axis, route)]
  transfers between devices with their start and end apart: 20 -> 20, of which waited for: 11 -> 10; matrix products, arithmetic and copies ran while one was open for 0% -> 0% of each run, Pallas kernels for 36% -> 33%
where the time goes in v15:
time: 74.2 us; the launch traced here: 74 us
  Pallas kernels  31 us (42%)
  waiting for transfers between devices  23.1 us (31%)
  starting transfers between devices  18.1 us (24%)
  between operations  1.69 us (2%)
    pallas_call x29, Pallas kernels, call(): pl.pallas_call(kernel, out_shape=out_shape, in_specs=[smem] * scalars + [...  31 us
    ppermute x16, starting transfers between devices, shifted(): return lax.ppermute(block, axis, route)  15.9 us
    ppermute x16, waiting for transfers between devices, shifted(): return lax.ppermute(block, axis, route)  13.4 us
    ppermute x2, waiting for transfers between devices, shards(): w_beside = lax.ppermute(w_sent, 'lon', [(i, i ^ span) for i in range(lons)])  9.01 us
    ppermute x1, starting transfers between devices, shards(): from_cross = lax.ppermute(to_cross, cycle, far_route)  2.02 us
  transfers between devices with their start and end apart: 20, of which 10 were waited for; matrix products, arithmetic and copies ran while one was open for 0% of the time, Pallas kernels for 33%

profile of v15, /device:TPU:0, one launch (start us, length us, event | category | flops | bytes accessed | tf_op | source)
XLA Modules:
  0.0 74.0 jit_solution(1625751912363149357)
XLA Ops:
  0.7 3.0 %collective-permute-start = (bf16[256,512]{1,0:T(8,128)(2,1)}, bf16[256,512]{1,0:T(8,128)(2,1)S(1)}, u32[]{:S(2)}, u32[]{:S(2)}) collective-permute-start(bf16[256,512]{1,0:T(8,128)(2,1)} %refs_2_.1), channel_id=1, source_target_pairs={{2,0},{0,2},{3,1},{1,3},{6,4},{4,6},{7,5},{5,7},{10,8},{8,10},{11,... | collective-permute-start | bytes 786440 | tf_op jit(solution)/shard_map/ppermute | solution.py:26
  3.7 3.3 %shard_map.157 = (bf16[256,512]{1,0:T(8,128)(2,1)S(1)}, bf16[256,512]{1,0:T(8,128)(2,1)S(1)}, bf16[256,512]{1,0:T(8,128)(2,1)S(1)}, bf16[256,512]{1,0:T(8,128)(2...) custom-call(bf16[512,512]{1,0:T(8,128)(2,1)} %refs_0_.1, ...), custom_call_target="tpu_custom_call" | custom-call | flops 1024 | bytes 1024 | tf_op jit(solution)/shard_map/pallas_call | solution.py:51
  7.7 2.5 %collective-permute-done.refs_1_ = bf16[256,512]{1,0:T(8,128)(2,1)S(1)} collective-permute-done((bf16[256,512]{1,0:T(8,128)(2,1)}, bf16[256,512]{1,0:T(8,128)(2,1)S(1)}, u32[]{:S(2)}, u32[]{:S(2)}) %collective-permute-start) | collective-permute-done | bytes 262176 | tf_op jit(solution)/shard_map/ppermute | solution.py:26
  10.2 1.1 %shard_map.158 = (bf16[512,512]{1,0:T(8,128)(2,1)S(1)}, bf16[512,256]{1,0:T(8,128)(2,1)S(1)}, bf16[272,256]{1,0:T(8,128)(2,1)S(1)}, bf16[272,256]{1,0:T(8,128)(2...) custom-call(s32[1]{0:T(128)S(6)} %copy.17.tiles, s32[1,2,6]{2,1,0:T(2,128)S(1)} %bitcast.14, ...), custom_call_target="tpu_custom_call" | custom-call | flops 1024 | bytes 1024 | tf_op jit(solution)/shard_map/pallas_call | solution.py:51
  11.3 1.9 %collective-permute-start.1 = (bf16[272,256]{1,0:T(8,128)(2,1)S(1)}, bf16[272,256]{1,0:T(8,128)(2,1)S(1)}, u32[]{:S(2)}, u32[]{:S(2)}) collective-permute-start(bf16[272,256]{1,0:T(8,128)(2,1)S(1)} %get-tuple-element.94), channel_id=1, source_target_pairs={{12,0},{0,4},{4,8},{8,12},{13,1},{1,5},{5,9},{9,13},{14,2},{2,6},{... | collective-permute-start | bytes 417800 | tf_op jit(solution)/shard_map/ppermute | solution.py:26
  13.2 2.1 %collective-permute-start.2 = (bf16[272,256]{1,0:T(8,128)(2,1)S(1)}, bf16[272,256]{1,0:T(8,128)(2,1)S(1)}, u32[]{:S(2)}, u32[]{:S(2)}) collective-permute-start(bf16[272,256]{1,0:T(8,128)(2,1)S(1)} %get-tuple-element.95), channel_id=1, source_target_pairs={{4,0},{8,4},{12,8},{0,12},{5,1},{9,5},{13,9},{1,13},{6,2},{10,6},{... | collective-permute-start | bytes 417800 | tf_op jit(solution)/shard_map/ppermute | solution.py:26
  15.7 1.7 %collective-permute-start.4 = (bf16[256,512]{1,0:T(8,128)(2,1)S(1)}, bf16[256,512]{1,0:T(8,128)(2,1)S(1)}, u32[]{:S(2)}, u32[]{:S(2)}) collective-permute-start(bf16[256,512]{1,0:T(8,128)(2,1)S(1)} %copy-done.2), channel_id=1, source_target_pairs={{2,0},{0,2},{3,1},{1,3},{6,4},{4,6},{7,5},{5,7},{10,8},{8,10},{11,... | collective-permute-start | bytes 786440 | tf_op jit(solution)/shard_map/ppermute | solution.py:26
  17.4 1.0 %shard_map.160 = (bf16[12,512,128]{2,1,0:T(8,128)(2,1)S(1)}, bf16[12,512,128]{2,1,0:T(8,128)(2,1)S(1)}, bf16[12,16,512]{2,1,0:T(8,128)(2,1)S(1)}, bf16[12,16,512]{2,1,0:T(8,128)(2,1)S(1)}) custom-call(s32[1]{0:T(128)S(6)} %copy.17.tiles, s32[12,512]{1,0:T(8,128)S(1)} %copy-done.6, s32[1,512]{1,0:T(1,128)S(1)} %bitcast.7), custom_call_target="tpu_custom_call" | custom-call | flops 1024 | bytes 1024 | tf_op jit(solution)/shard_map/pallas_call | solution.py:51
  18.5 2.9 %shard_map.161.before = bf16[12,512,256]{2,1,0:T(8,128)(2,1)S(1)} custom-call(bf16[12,512,128]{2,1,0:T(8,128)(2,1)S(1)} %get-tuple-element.91.low, bf16[12,512,128]{2,1,0:T(8,128)(2,1)S(1)} %get-tuple-element.92.high, bf16[512,256]{1,0:T(8,128)(2,1)S(1)} %get-tuple-element.96.proj, bf16[272,256]{1,0:T(8,128)(2,1)S(1)} %collective-permute-done.3.beside), custom_call_target="tpu_custom_call" | custom-call | flops 1024 | bytes 1024 | tf_op jit(solution)/shard_map/pallas_call | solution.py:51
  22.4 1.6 %collective-permute-done.4.refs_1_ = bf16[256,512]{1,0:T(8,128)(2,1)S(1)} collective-permute-done((bf16[256,512]{1,0:T(8,128)(2,1)S(1)}, bf16[256,512]{1,0:T(8,128)(2,1)S(1)}, u32[]{:S(2)}, u32[]{:S(2)}) %collective-permute-start.4) | collective-permute-done | bytes 262176 | tf_op jit(solution)/shard_map/ppermute | solution.py:26
  24.1 1.1 %shard_map.162 = (bf16[512,512]{1,0:T(8,128)(2,1)}, f32[512,512]{1,0:T(8,128)S(1)}, f32[512,512]{1,0:T(8,128)S(1)}) custom-call(s32[1]{0:T(128)S(6)} %copy.17.tiles, bf16[256,512]{1,0:T(8,128)(2,1)S(1)} %copy-done.2, bf16[256,512]{1,0:T(8,128)(2,1)S(1)} %collective-permute-done.4.refs_1_, bf16[512,512]{1,0:T(8,128)(2,1)S(1)} %get-tuple-element.86.feats.refs_2_, ...), custom_call_target="tpu_custom_call" | custom-call | flops 1024 | bytes 1024 | tf_op jit(solution)/shard_map/pallas_call | solution.py:51
  25.2 2.5 %shard_map.163.part = bf16[12,512,256]{2,1,0:T(8,128)(2,1)S(1)} custom-call(bf16[12,512,128]{2,1,0:T(8,128)(2,1)S(1)} %get-tuple-element.91.low, bf16[12,512,128]{2,1,0:T(8,128)(2,1)S(1)} %get-tuple-element.92.high, bf16[12,512,256]{2,1,0:T(8,128)(2,1)S(1)} %shard_map.161.before, bf16[272,256]{1,0:T(8,128)(2,1)S(1)} %collective-permute-done.1.west, ...), custom_call_target="tpu_custom_call" | custom-call | flops 1024 | bytes 1024 | tf_op jit(solution)/shard_map/pallas_call | solution.py:51
  28.4 2.5 %shard_map.167 = (bf16[256,256]{1,0:T(8,128)(2,1)S(1)}, bf16[12,256,256]{2,1,0:T(8,128)(2,1)S(1)}) custom-call(bf16[12,512,128]{2,1,0:T(8,128)(2,1)S(1)} %get-tuple-element.91.low, bf16[12,512,128]{2,1,0:T(8,128)(2,1)S(1)} %get-tuple-element.92.high, f32[512,256]{1,0:T(8,128)S(1)} %shard_map.159.base, s32[1,512]{1,0:T(1,128)S(1)} %bitcast.8, ...), custom_call_target="tpu_custom_call" | custom-call | flops 1024 | bytes 1024 | tf_op jit(solution)/shard_map/pallas_call | solution.py:51
  30.9 1.6 %collective-permute-start.9 = (bf16[256,256]{1,0:T(8,128)(2,1)S(1)}, bf16[256,256]{1,0:T(8,128)(2,1)S(1)}, u32[]{:S(2)}, u32[]{:S(2)}) collective-permute-start(bf16[256,256]{1,0:T(8,128)(2,1)S(1)} %get-tuple-element.116.refs_0_), channel_id=1, source_target_pairs={{2,0},{0,2},{3,1},{1,3},{6,4},{4,6},{7,5},{5,7},{10,8},{8,10},{11,... | collective-permute-start | bytes 393224 | tf_op jit(solution)/shard_map/ppermute | solution.py:26
  32.5 2.5 %shard_map.165 = (bf16[256,256]{1,0:T(8,128)(2,1)S(1)}, bf16[12,256,256]{2,1,0:T(8,128)(2,1)S(1)}) custom-call(bf16[12,512,128]{2,1,0:T(8,128)(2,1)S(1)} %get-tuple-element.91.low, bf16[12,512,128]{2,1,0:T(8,128)(2,1)S(1)} %get-tuple-element.92.high, f32[512,256]{1,0:T(8,128)S(1)} %shard_map.159.base, s32[1,512]{1,0:T(1,128)S(1)} %bitcast.9, ...), custom_call_target="tpu_custom_call" | custom-call | flops 1024 | bytes 1024 | tf_op jit(solution)/shard_map/pallas_call | solution.py:51
  35.5 1.0 %collective-permute-done.9.refs_1_ = bf16[256,256]{1,0:T(8,128)(2,1)S(1)} collective-permute-done((bf16[256,256]{1,0:T(8,128)(2,1)S(1)}, bf16[256,256]{1,0:T(8,128)(2,1)S(1)}, u32[]{:S(2)}, u32[]{:S(2)}) %collective-permute-start.9) | collective-permute-done | bytes 131104 | tf_op jit(solution)/shard_map/ppermute | solution.py:26
  36.5 0.9 %shard_map.168 = (bf16[512,256]{1,0:T(8,128)(2,1)S(1)}, bf16[512,256]{1,0:T(8,128)(2,1)S(1)}, f32[256,256]{1,0:T(8,128)S(1)}) custom-call(s32[1,512]{1,0:T(1,128)S(1)} %bitcast.10, bf16[256,256]{1,0:T(8,128)(2,1)S(1)} %get-tuple-element.116.refs_0_, bf16[256,256]{1,0:T(8,128)(2,1)S(1)} %collective-permute-done.9.refs_1_, bf16[512,512]{1,0:T(8,128)(2,1)S(1)} %copy-done.1, ...), custom_call_target="tpu_custom_call" | custom-call | flops 1024 | bytes 1024 | tf_op jit(solution)/shard_map/pallas_call | solution.py:51
  37.4 2.7 %shard_map.169 = (bf16[12,256,256]{2,1,0:T(8,128)(2,1)S(1)}, f32[1536,256]{1,0:T(8,128)S(1)}) custom-call(bf16[12,16,512]{2,1,0:T(8,128)(2,1)S(1)} %get-tuple-element.89.low, bf16[12,16,512]{2,1,0:T(8,128)(2,1)S(1)} %get-tuple-element.90.high, bf16[12,256,256]{2,1,0:T(8,128)(2,1)S(1)} %get-tuple-element.115.slope, f32[256,256]{1,0:T(8,128)S(1)} %get-tuple-element.117.scale), custom_call_target="tpu_custom_call" | custom-call | flops 1024 | bytes 1024 | tf_op jit(solution)/shard_map/pallas_call | solution.py:51
  40.3 0.7 %shard_map.166 = (bf16[512,256]{1,0:T(8,128)(2,1)S(1)}, bf16[512,256]{1,0:T(8,128)(2,1)S(1)}, f32[256,256]{1,0:T(8,128)S(1)}) custom-call(s32[1,512]{1,0:T(1,128)S(1)} %bitcast.11, bf16[256,256]{1,0:T(8,128)(2,1)S(1)} %get-tuple-element.109.refs_0_, bf16[256,256]{1,0:T(8,128)(2,1)S(1)} %collective-permute-done.8.refs_1_, bf16[512,512]{1,0:T(8,128)(2,1)S(1)} %copy-done.1, ...), custom_call_target="tpu_custom_call" | custom-call | flops 1024 | bytes 1024 | tf_op jit(solution)/shard_map/pallas_call | solution.py:51
  41.0 0.7 shard_map.170
  41.7 1.0 %shard_map.171 = bf16[2,256,256]{2,1,0:T(8,128)(2,1)S(1)} custom-call(bf16[12,16,512]{2,1,0:T(8,128)(2,1)S(1)} %get-tuple-element.89.low, bf16[12,16,512]{2,1,0:T(8,128)(2,1)S(1)} %get-tuple-element.90.high, bf16[12,256,256]{2,1,0:T(8,128)(2,1)S(1)} %get-tuple-element.119.grads.refs_1_, f32[1536,256]{1,0:T(8,128)S(1)} %get-tuple-element.120.before, ...), custom_call_target="tpu_custom_call" | custom-call | flops 1024 | bytes 1024 | tf_op jit(solution)/shard_map/pallas_call | solution.py:51
  42.8 2.0 %collective-permute-start.12 = (bf16[256,256]{1,0:T(8,128)(2,1)S(1)}, bf16[256,256]{1,0:T(8,128)(2,1)S(1)}, u32[]{:S(2)}, u32[]{:S(2)}) collective-permute-start(bf16[256,256]{1,0:T(8,128)(2,1)S(1)} %get-tuple-element.137), channel_id=1, source_target_pairs={{0,9},{1,8},{4,13},{5,12},{8,1},{9,0},{12,5},{13,4},{2,11},{3,10},... | collective-permute-start | bytes 393224 | tf_op jit(solution)/shard_map/ppermute | solution.py:719
  44.8 1.4 %shard_map.172 = (bf16[256,256]{1,0:T(8,128)(2,1)S(1)}, bf16[256,256]{1,0:T(8,128)(2,1)S(1)}, bf16[256,256]{1,0:T(8,128)(2,1)S(1)}) custom-call(bf16[12,16,512]{2,1,0:T(8,128)(2,1)S(1)} %get-tuple-element.89.low, bf16[12,16,512]{2,1,0:T(8,128)(2,1)S(1)} %get-tuple-element.90.high, bf16[12,256,256]{2,1,0:T(8,128)(2,1)S(1)} %get-tuple-element.119.grads.refs_1_, ...), custom_call_target="tpu_custom_call" | custom-call | flops 1024 | bytes 1024 | tf_op jit(solution)/shard_map/pallas_call | solution.py:51
  46.6 1.9 %collective-permute-start.14 = (bf16[256,256]{1,0:T(8,128)(2,1)S(1)}, bf16[256,256]{1,0:T(8,128)(2,1)S(1)}, u32[]{:S(2)}, u32[]{:S(2)}) collective-permute-start(bf16[256,256]{1,0:T(8,128)(2,1)S(1)} %get-tuple-element.139), channel_id=1, source_target_pairs={{12,0},{0,4},{4,8},{8,12},{13,1},{1,5},{5,9},{9,13},{14,2},{2,6},{... | collective-permute-start | bytes 393224 | tf_op jit(solution)/shard_map/ppermute | solution.py:26
  48.5 2.1 %shard_map.174 = (f32[512,256]{1,0:T(8,128)S(1)}, bf16[256,512]{1,0:T(8,128)(2,1)S(1)}) custom-call(bf16[12,16,512]{2,1,0:T(8,128)(2,1)S(1)} %get-tuple-element.89.low, bf16[12,16,512]{2,1,0:T(8,128)(2,1)S(1)} %get-tuple-element.90.high, bf16[12,256,256]{2,1,0:T(8,128)(2,1)S(1)} %get-tuple-element.126.refs_0_, ...), custom_call_target="tpu_custom_call" | custom-call | flops 1024 | bytes 1024 | tf_op jit(solution)/shard_map/pallas_call | solution.py:51
  50.6 1.2 %shard_map.175 = (bf16[256,512]{1,0:T(8,128)(2,1)}, f32[256,512]{1,0:T(8,128)S(1)}) custom-call(s32[1]{0:T(128)S(6)} %copy.17.tiles, bf16[256,512]{1,0:T(8,128)(2,1)S(1)} %get-tuple-element.82.refs_0_.feats, bf16[256,512]{1,0:T(8,128)(2,1)S(1)} %copy-done.2, bf16[256,512]{1,0:T(8,128)(2,1)S(1)} %get-tuple-element.83.w_out, bf16[256,512]{1,0:T(8,128)(2,1)S(1)} %copy-done.4, ...), custom_call_target="tpu_custom_call" | custom-call | flops 1024 | bytes 1024 | tf_op jit(solution)/shard_map/pallas_call | solution.py:51
  51.8 5.3 %collective-permute-done.13.upper = bf16[256,256]{1,0:T(8,128)(2,1)S(1)} collective-permute-done((bf16[256,256]{1,0:T(8,128)(2,1)S(1)}, bf16[256,256]{1,0:T(8,128)(2,1)S(1)}, u32[]{:S(2)}, u32[]{:S(2)}) %collective-permute-start.13) | collective-permute-done | bytes 131104 | tf_op jit(solution)/shard_map/ppermute | solution.py:26
  57.8 1.5 %collective-permute-start.17 = (bf16[256,256]{1,0:T(8,128)(2,1)S(1)}, bf16[256,256]{1,0:T(8,128)(2,1)S(1)}, u32[]{:S(2)}, u32[]{:S(2)}) collective-permute-start(bf16[256,256]{1,0:T(8,128)(2,1)S(1)} %bitcast.16), channel_id=1, source_target_pairs={{2,0},{0,2},{3,1},{1,3},{6,4},{4,6},{7,5},{5,7},{10,8},{8,10},{11,... | collective-permute-start | bytes 393224 | tf_op jit(solution)/shard_map/ppermute | solution.py:26
  60.9 2.4 %collective-permute-done.17.refs_1_ = bf16[256,256]{1,0:T(8,128)(2,1)S(1)} collective-permute-done((bf16[256,256]{1,0:T(8,128)(2,1)S(1)}, bf16[256,256]{1,0:T(8,128)(2,1)S(1)}, u32[]{:S(2)}, u32[]{:S(2)}) %collective-permute-start.17) | collective-permute-done | bytes 131104 | tf_op jit(solution)/shard_map/ppermute | solution.py:26
  63.5 5.9 %collective-permute-done.18.received = bf16[2,64,256]{2,1,0:T(8,128)(2,1)S(1)} collective-permute-done((bf16[2,64,256]{2,1,0:T(8,128)(2,1)S(1)}, bf16[2,64,256]{2,1,0:T(8,128)(2,1)S(1)}, u32[]{:S(2)}, u32[]{:S(2)}) %collective-permute-start.18) | collective-permute-done | bytes 65568 | tf_op jit(solution)/shard_map/ppermute | solution.py:805
  69.5 0.7 shard_map.182
  70.2 3.2 %collective-permute-done.19.received = bf16[1,64,256]{2,1,0:T(8,128)(2,1)S(1)} collective-permute-done((bf16[1,64,256]{2,1,0:T(8,128)(2,1)S(1)}, bf16[1,64,256]{2,1,0:T(8,128)(2,1)S(1)}, u32[]{:S(2)}, u32[]{:S(2)}) %collective-permute-start.19) | collective-permute-done | bytes 32800 | tf_op jit(solution)/shard_map/ppermute | solution.py:805
  (57 shorter events, 6.6 us)
Async XLA Ops:
  0.6 9.5 %copy-start.9 = (s32[1,6,2]{1,2,0:T(2,128)S(1)}, s32[1,6,2]{1,2,0:T(2,128)}, u32[]{:S(2)}) copy-start(s32[1,6,2]{1,2,0:T(2,128)} %param.19) | copy-start | bytes 148
  0.6 14.7 %copy-start.7 = (f32[512]{0:T(512)S(1)}, f32[512]{0:T(512)}, u32[]{:S(2)}) copy-start(f32[512]{0:T(512)} %param.22) | copy-start | bytes 6148
  0.7 9.5 %collective-permute-start = (bf16[256,512]{1,0:T(8,128)(2,1)}, bf16[256,512]{1,0:T(8,128)(2,1)S(1)}, u32[]{:S(2)}, u32[]{:S(2)}) collective-permute-start(bf16[256,512]{1,0:T(8,128)(2,1)} %refs_2_.1), channel_id=1, source_target_pairs={{2,0},{0,2},{3,1},{1,3},{6,4},{4,6},{7,5},{5,7},{10,8},{8,10},{11,... | collective-permute-start | bytes 786440 | tf_op jit(solution)/shard_map/ppermute | solution.py:26
  6.9 8.8 %copy-start.2 = (bf16[256,512]{1,0:T(8,128)(2,1)S(1)}, bf16[256,512]{1,0:T(8,128)(2,1)}, u32[]{:S(2)}) copy-start(bf16[256,512]{1,0:T(8,128)(2,1)} %cots.1) | copy-start | bytes 786436
  6.9 10.5 %copy-start.5 = (s32[512]{0:T(512)S(1)}, s32[512]{0:T(512)}, u32[]{:S(2)}) copy-start(s32[512]{0:T(512)} %param.17) | copy-start | bytes 6148
  7.0 10.5 %copy-start.6 = (s32[12,512]{1,0:T(8,128)S(1)}, s32[12,512]{1,0:T(8,128)}, u32[]{:S(2)}) copy-start(s32[12,512]{1,0:T(8,128)} %senders) | copy-start | bytes 73732
  11.3 7.2 %collective-permute-start.3 = (bf16[272,256]{1,0:T(8,128)(2,1)S(1)}, bf16[272,256]{1,0:T(8,128)(2,1)S(1)}, u32[]{:S(2)}, u32[]{:S(2)}) collective-permute-start(bf16[272,256]{1,0:T(8,128)(2,1)S(1)} %get-tuple-element.97), channel_id=1, source_target_pairs={{1,0},{0,1},{3,2},{2,3},{5,4},{4,5},{7,6},{6,7},{9,8},{8,9},{11,10... | collective-permute-start | bytes 417800 | tf_op jit(solution)/shard_map/ppermute | solution.py:26
  11.3 10.1 %collective-permute-start.1 = (bf16[272,256]{1,0:T(8,128)(2,1)S(1)}, bf16[272,256]{1,0:T(8,128)(2,1)S(1)}, u32[]{:S(2)}, u32[]{:S(2)}) collective-permute-start(bf16[272,256]{1,0:T(8,128)(2,1)S(1)} %get-tuple-element.94), channel_id=1, source_target_pairs={{12,0},{0,4},{4,8},{8,12},{13,1},{1,5},{5,9},{9,13},{14,2},{2,6},{... | collective-permute-start | bytes 417800 | tf_op jit(solution)/shard_map/ppermute | solution.py:26
  13.2 8.7 %collective-permute-start.2 = (bf16[272,256]{1,0:T(8,128)(2,1)S(1)}, bf16[272,256]{1,0:T(8,128)(2,1)S(1)}, u32[]{:S(2)}, u32[]{:S(2)}) collective-permute-start(bf16[272,256]{1,0:T(8,128)(2,1)S(1)} %get-tuple-element.95), channel_id=1, source_target_pairs={{4,0},{8,4},{12,8},{0,12},{5,1},{9,5},{13,9},{1,13},{6,2},{10,6},{... | collective-permute-start | bytes 417800 | tf_op jit(solution)/shard_map/ppermute | solution.py:26
  15.7 8.4 %collective-permute-start.4 = (bf16[256,512]{1,0:T(8,128)(2,1)S(1)}, bf16[256,512]{1,0:T(8,128)(2,1)S(1)}, u32[]{:S(2)}, u32[]{:S(2)}) collective-permute-start(bf16[256,512]{1,0:T(8,128)(2,1)S(1)} %copy-done.2), channel_id=1, source_target_pairs={{2,0},{0,2},{3,1},{1,3},{6,4},{4,6},{7,5},{5,7},{10,8},{8,10},{11,... | collective-permute-start | bytes 786440 | tf_op jit(solution)/shard_map/ppermute | solution.py:26
  17.4 11.0 %collective-permute-start.5 = (bf16[272,256]{1,0:T(8,128)(2,1)S(1)}, bf16[272,256]{1,0:T(8,128)(2,1)S(1)}, u32[]{:S(2)}, u32[]{:S(2)}) collective-permute-start(bf16[272,256]{1,0:T(8,128)(2,1)S(1)} %get-tuple-element.105), channel_id=1, source_target_pairs={{0,9},{1,8},{4,13},{5,12},{8,1},{9,0},{12,5},{13,4},{2,11},{3,10},... | collective-permute-start | bytes 417800 | tf_op jit(solution)/shard_map/ppermute | solution.py:611
  18.5 5.6 %copy-start = (bf16[512,512]{1,0:T(8,128)(2,1)S(1)}, bf16[512,512]{1,0:T(8,128)(2,1)}, u32[]{:S(2)}) copy-start(bf16[512,512]{1,0:T(8,128)(2,1)} %refs_3_.3) | copy-start | bytes 1572868
  18.5 5.6 %copy-start.3 = (bf16[512,512]{1,0:T(8,128)(2,1)S(1)}, bf16[512,512]{1,0:T(8,128)(2,1)}, u32[]{:S(2)}) copy-start(bf16[512,512]{1,0:T(8,128)(2,1)} %get-tuple-element.100.refs_5_) | copy-start | bytes 1572868
  18.5 5.6 %copy-start.8 = (f32[512]{0:T(512)S(1)}, f32[512]{0:T(512)}, u32[]{:S(2)}) copy-start(f32[512]{0:T(512)} %param.26) | copy-start | bytes 6148
  21.9 6.5 %collective-permute-start.6 = (bf16[272,256]{1,0:T(8,128)(2,1)S(1)}, bf16[272,256]{1,0:T(8,128)(2,1)S(1)}, u32[]{:S(2)}, u32[]{:S(2)}) collective-permute-start(bf16[272,256]{1,0:T(8,128)(2,1)S(1)} %collective-permute-done.1.west), channel_id=1, source_target_pairs={{1,0},{0,1},{3,2},{2,3},{5,4},{4,5},{7,6},{6,7},{9,8},{8,9},{11,10... | collective-permute-start | bytes 417800 | tf_op jit(solution)/shard_map/ppermute | solution.py:26
  22.4 6.1 %collective-permute-start.7 = (bf16[272,256]{1,0:T(8,128)(2,1)S(1)}, bf16[272,256]{1,0:T(8,128)(2,1)S(1)}, u32[]{:S(2)}, u32[]{:S(2)}) collective-permute-start(bf16[272,256]{1,0:T(8,128)(2,1)S(1)} %collective-permute-done.2.east), channel_id=1, source_target_pairs={{1,0},{0,1},{3,2},{2,3},{5,4},{4,5},{7,6},{6,7},{9,8},{8,9},{11,10... | collective-permute-start | bytes 417800 | tf_op jit(solution)/shard_map/ppermute | solution.py:26
  30.9 5.6 %copy-start.1 = (bf16[512,512]{1,0:T(8,128)(2,1)S(1)}, bf16[512,512]{1,0:T(8,128)(2,1)}, u32[]{:S(2)}) copy-start(bf16[512,512]{1,0:T(8,128)(2,1)} %get-tuple-element.110.refs_2_) | copy-start | bytes 1572868
  30.9 5.6 %collective-permute-start.9 = (bf16[256,256]{1,0:T(8,128)(2,1)S(1)}, bf16[256,256]{1,0:T(8,128)(2,1)S(1)}, u32[]{:S(2)}, u32[]{:S(2)}) collective-permute-start(bf16[256,256]{1,0:T(8,128)(2,1)S(1)} %get-tuple-element.116.refs_0_), channel_id=1, source_target_pairs={{2,0},{0,2},{3,1},{1,3},{6,4},{4,6},{7,5},{5,7},{10,8},{8,10},{11,... | collective-permute-start | bytes 393224 | tf_op jit(solution)/shard_map/ppermute | solution.py:26
  35.0 5.3 %collective-permute-start.8 = (bf16[256,256]{1,0:T(8,128)(2,1)S(1)}, bf16[256,256]{1,0:T(8,128)(2,1)S(1)}, u32[]{:S(2)}, u32[]{:S(2)}) collective-permute-start(bf16[256,256]{1,0:T(8,128)(2,1)S(1)} %get-tuple-element.109.refs_0_), channel_id=1, source_target_pairs={{2,0},{0,2},{3,1},{1,3},{6,4},{4,6},{7,5},{5,7},{10,8},{8,10},{11,... | collective-permute-start | bytes 393224 | tf_op jit(solution)/shard_map/ppermute | solution.py:26
  42.7 3.6 %collective-permute-start.10 = (bf16[2,256,256]{2,1,0:T(8,128)(2,1)S(1)}, bf16[2,256,256]{2,1,0:T(8,128)(2,1)S(1)}, u32[]{:S(2)}, u32[]{:S(2)}) collective-permute-start(bf16[2,256,256]{2,1,0:T(8,128)(2,1)S(1)} %shard_map.171), channel_id=1, source_target_pairs={{1,0},{0,1},{3,2},{2,3},{5,4},{4,5},{7,6},{6,7},{9,8},{8,9},{11,10... | collective-permute-start | bytes 786440 | tf_op jit(solution)/shard_map/ppermute | solution.py:26
  42.8 9.0 %collective-permute-start.12 = (bf16[256,256]{1,0:T(8,128)(2,1)S(1)}, bf16[256,256]{1,0:T(8,128)(2,1)S(1)}, u32[]{:S(2)}, u32[]{:S(2)}) collective-permute-start(bf16[256,256]{1,0:T(8,128)(2,1)S(1)} %get-tuple-element.137), channel_id=1, source_target_pairs={{0,9},{1,8},{4,13},{5,12},{8,1},{9,0},{12,5},{13,4},{2,11},{3,10},... | collective-permute-start | bytes 393224 | tf_op jit(solution)/shard_map/ppermute | solution.py:719
  46.2 5.5 %collective-permute-start.11 = (bf16[256,256]{1,0:T(8,128)(2,1)S(1)}, bf16[256,256]{1,0:T(8,128)(2,1)S(1)}, u32[]{:S(2)}, u32[]{:S(2)}) collective-permute-start(bf16[256,256]{1,0:T(8,128)(2,1)S(1)} %get-tuple-element.135), channel_id=1, source_target_pairs={{1,0},{0,1},{3,2},{2,3},{5,4},{4,5},{7,6},{6,7},{9,8},{8,9},{11,10... | collective-permute-start | bytes 393224 | tf_op jit(solution)/shard_map/ppermute | solution.py:26
  46.4 10.6 %collective-permute-start.13 = (bf16[256,256]{1,0:T(8,128)(2,1)S(1)}, bf16[256,256]{1,0:T(8,128)(2,1)S(1)}, u32[]{:S(2)}, u32[]{:S(2)}) collective-permute-start(bf16[256,256]{1,0:T(8,128)(2,1)S(1)} %get-tuple-element.124), channel_id=1, source_target_pairs={{4,0},{8,4},{12,8},{0,12},{5,1},{9,5},{13,9},{1,13},{6,2},{10,6},{... | collective-permute-start | bytes 393224 | tf_op jit(solution)/shard_map/ppermute | solution.py:26
  46.6 12.8 %collective-permute-start.14 = (bf16[256,256]{1,0:T(8,128)(2,1)S(1)}, bf16[256,256]{1,0:T(8,128)(2,1)S(1)}, u32[]{:S(2)}, u32[]{:S(2)}) collective-permute-start(bf16[256,256]{1,0:T(8,128)(2,1)S(1)} %get-tuple-element.139), channel_id=1, source_target_pairs={{12,0},{0,4},{4,8},{8,12},{13,1},{1,5},{5,9},{9,13},{14,2},{2,6},{... | collective-permute-start | bytes 393224 | tf_op jit(solution)/shard_map/ppermute | solution.py:26
  48.5 2.1 %copy-start.4 = (bf16[256,512]{1,0:T(8,128)(2,1)S(1)}, bf16[256,512]{1,0:T(8,128)(2,1)}, u32[]{:S(2)}) copy-start(bf16[256,512]{1,0:T(8,128)(2,1)} %get-tuple-element.84.w_node_v_t) | copy-start | bytes 786436
  57.8 5.5 %collective-permute-start.17 = (bf16[256,256]{1,0:T(8,128)(2,1)S(1)}, bf16[256,256]{1,0:T(8,128)(2,1)S(1)}, u32[]{:S(2)}, u32[]{:S(2)}) collective-permute-start(bf16[256,256]{1,0:T(8,128)(2,1)S(1)} %bitcast.16), channel_id=1, source_target_pairs={{2,0},{0,2},{3,1},{1,3},{6,4},{4,6},{7,5},{5,7},{10,8},{8,10},{11,... | collective-permute-start | bytes 393224 | tf_op jit(solution)/shard_map/ppermute | solution.py:26
  59.8 3.6 %collective-permute-start.16 = (bf16[4,64,256]{2,1,0:T(8,128)(2,1)S(1)}, bf16[4,64,256]{2,1,0:T(8,128)(2,1)S(1)}, u32[]{:S(2)}, u32[]{:S(2)}) collective-permute-start(bf16[4,64,256]{2,1,0:T(8,128)(2,1)S(1)} %get-tuple-element.151), channel_id=1, source_target_pairs={{1,0},{0,1},{3,2},{2,3},{5,4},{4,5},{7,6},{6,7},{9,8},{8,9},{11,10... | collective-permute-start | bytes 393224 | tf_op jit(solution)/shard_map/ppermute | solution.py:26
  60.3 9.2 %collective-permute-start.15 = (bf16[256,256]{1,0:T(8,128)(2,1)S(1)}, bf16[256,256]{1,0:T(8,128)(2,1)S(1)}, u32[]{:S(2)}, u32[]{:S(2)}) collective-permute-start(bf16[256,256]{1,0:T(8,128)(2,1)S(1)} %bitcast.15), channel_id=1, source_target_pairs={{2,0},{0,2},{3,1},{1,3},{6,4},{4,6},{7,5},{5,7},{10,8},{8,10},{11,... | collective-permute-start | bytes 393224 | tf_op jit(solution)/shard_map/ppermute | solution.py:26
  63.4 5.9 %collective-permute-start.18 = (bf16[2,64,256]{2,1,0:T(8,128)(2,1)S(1)}, bf16[2,64,256]{2,1,0:T(8,128)(2,1)S(1)}, u32[]{:S(2)}, u32[]{:S(2)}) collective-permute-start(bf16[2,64,256]{2,1,0:T(8,128)(2,1)S(1)} %get-tuple-element.158), channel_id=1, source_target_pairs={{0,8},{4,12},{8,0},{12,4},{1,9},{5,13},{9,1},{13,5},{2,10},{6,14},... | collective-permute-start | bytes 196616 | tf_op jit(solution)/shard_map/ppermute | solution.py:805
  69.4 4.0 %collective-permute-start.19 = (bf16[1,64,256]{2,1,0:T(8,128)(2,1)S(1)}, bf16[1,64,256]{2,1,0:T(8,128)(2,1)S(1)}, u32[]{:S(2)}, u32[]{:S(2)}) collective-permute-start(bf16[1,64,256]{2,1,0:T(8,128)(2,1)S(1)} %get-tuple-element.160), channel_id=1, source_target_pairs={{0,4},{4,0},{8,12},{12,8},{1,5},{5,1},{9,13},{13,9},{2,6},{6,2},{1... | collective-permute-start | bytes 98312 | tf_op jit(solution)/shard_map/ppermute | solution.py:805

commit v16 on v9

--- a/solution.py
+++ b/solution.py
@@ -457,6 +457,14 @@
     east[...] = (right[...] + more[1].astype(jnp.float32)).astype(jnp.bfloat16)
 
 
+def band_bits(place, lons):
+    bits, weight = 0, 1
+    while weight < lons:
+        bits += weight if place * weight * 2 // lons % 2 else 0
+        weight *= 2
+    return bits
+
+
 def back_kernel(start, inv_root, tiles, own, beside, feats, upper, *refs):
     *refs, total = refs
     sub = lax.axis_index("sub")
@@ -481,7 +489,7 @@
     lon = lax.axis_index("lon")
     lons, columns, _ = w_mine.shape
     for k in range(lons):
-        band = (lon ^ k) * 2
+        band = (lon ^ band_bits(k, lons)) * 2
         for out, core in ((w_mine, sub), (w_beside, 1 - sub)):
             spot = pl.multiple_of((band + core) * columns, columns)
             out[k] = weight[pl.ds(spot, columns), :].astype(out.dtype)
@@ -807,7 +815,8 @@
             [w_mine, w_beside],
             scalars=0,
         )
-        w_beside = lax.ppermute(w_sent, "lon", [(i, i ^ span) for i in range(lons)])
+        apart = lons // span // 2
+        w_beside = lax.ppermute(w_sent, "lon", [(i, i ^ apart) for i in range(lons)])
     grad_w_send = call(
         weight_kernel, shape((columns, hid), f32), [w_mine, w_beside], scalars=0
     )

time: 69.6 us -> 69.6 us (level)
  starting transfers between devices: 19 us -> 19.7 us
where the time goes in v16:
time: 69.6 us; the launch traced here: 69.5 us
  Pallas kernels  31 us (45%)
  starting transfers between devices  19.7 us (28%)
  waiting for transfers between devices  17.1 us (25%)
  between operations  1.67 us (2%)
    pallas_call x29, Pallas kernels, call(): pl.pallas_call(kernel, out_shape=out_shape, in_specs=[smem] * scalars + [...  31 us
    ppermute x16, starting transfers between devices, shifted(): return lax.ppermute(block, axis, route)  15.5 us
    ppermute x16, waiting for transfers between devices, shifted(): return lax.ppermute(block, axis, route)  9.91 us
    ppermute x2, waiting for transfers between devices, shards(): lax.ppermute(w_sent, 'lon', [(i, i ^ apart) for i in range(lons)])  4.63 us
    ppermute x2, starting transfers between devices, shards(): lax.ppermute(w_sent, 'lon', [(i, i ^ apart) for i in range(lons)])  3.97 us
    ppermute x1, waiting for transfers between devices, shards(): across = lambda block: lax.ppermute(block, cycle, across_route)  1.86 us
  transfers between devices with their start and end apart: 20, of which 11 were waited for; matrix products, arithmetic and copies ran while one was open for 0% of the time, Pallas kernels for 36%

profile of v16, /device:TPU:0, one launch (start us, length us, event | category | flops | bytes accessed | tf_op | source)
XLA Modules:
  0.0 69.5 jit_solution(3581523807780599056)
XLA Ops:
  0.7 3.0 %collective-permute-start = (bf16[256,512]{1,0:T(8,128)(2,1)}, bf16[256,512]{1,0:T(8,128)(2,1)S(1)}, u32[]{:S(2)}, u32[]{:S(2)}) collective-permute-start(bf16[256,512]{1,0:T(8,128)(2,1)} %refs_2_.1), channel_id=1, source_target_pairs={{2,0},{0,2},{3,1},{1,3},{6,4},{4,6},{7,5},{5,7},{10,8},{8,10},{11,... | collective-permute-start | bytes 786440 | tf_op jit(solution)/shard_map/ppermute | solution.py:26
  3.7 3.3 %shard_map.157 = (bf16[256,512]{1,0:T(8,128)(2,1)S(1)}, bf16[256,512]{1,0:T(8,128)(2,1)S(1)}, bf16[256,512]{1,0:T(8,128)(2,1)S(1)}, bf16[256,512]{1,0:T(8,128)(2...) custom-call(bf16[512,512]{1,0:T(8,128)(2,1)} %refs_0_.1, ...), custom_call_target="tpu_custom_call" | custom-call | flops 1024 | bytes 1024 | tf_op jit(solution)/shard_map/pallas_call | solution.py:51
  7.7 2.5 %collective-permute-done.refs_1_ = bf16[256,512]{1,0:T(8,128)(2,1)S(1)} collective-permute-done((bf16[256,512]{1,0:T(8,128)(2,1)}, bf16[256,512]{1,0:T(8,128)(2,1)S(1)}, u32[]{:S(2)}, u32[]{:S(2)}) %collective-permute-start) | collective-permute-done | bytes 262176 | tf_op jit(solution)/shard_map/ppermute | solution.py:26
  10.2 1.1 %shard_map.158 = (bf16[512,512]{1,0:T(8,128)(2,1)S(1)}, bf16[512,256]{1,0:T(8,128)(2,1)S(1)}, bf16[272,256]{1,0:T(8,128)(2,1)S(1)}, bf16[272,256]{1,0:T(8,128)(2...) custom-call(s32[1]{0:T(128)S(6)} %copy.17.tiles, s32[1,2,6]{2,1,0:T(2,128)S(1)} %bitcast.14, ...), custom_call_target="tpu_custom_call" | custom-call | flops 1024 | bytes 1024 | tf_op jit(solution)/shard_map/pallas_call | solution.py:51
  11.3 1.9 %collective-permute-start.1 = (bf16[272,256]{1,0:T(8,128)(2,1)S(1)}, bf16[272,256]{1,0:T(8,128)(2,1)S(1)}, u32[]{:S(2)}, u32[]{:S(2)}) collective-permute-start(bf16[272,256]{1,0:T(8,128)(2,1)S(1)} %get-tuple-element.94), channel_id=1, source_target_pairs={{12,0},{0,4},{4,8},{8,12},{13,1},{1,5},{5,9},{9,13},{14,2},{2,6},{... | collective-permute-start | bytes 417800 | tf_op jit(solution)/shard_map/ppermute | solution.py:26
  13.2 2.1 %collective-permute-start.2 = (bf16[272,256]{1,0:T(8,128)(2,1)S(1)}, bf16[272,256]{1,0:T(8,128)(2,1)S(1)}, u32[]{:S(2)}, u32[]{:S(2)}) collective-permute-start(bf16[272,256]{1,0:T(8,128)(2,1)S(1)} %get-tuple-element.95), channel_id=1, source_target_pairs={{4,0},{8,4},{12,8},{0,12},{5,1},{9,5},{13,9},{1,13},{6,2},{10,6},{... | collective-permute-start | bytes 417800 | tf_op jit(solution)/shard_map/ppermute | solution.py:26
  15.7 1.7 %collective-permute-start.4 = (bf16[256,512]{1,0:T(8,128)(2,1)S(1)}, bf16[256,512]{1,0:T(8,128)(2,1)S(1)}, u32[]{:S(2)}, u32[]{:S(2)}) collective-permute-start(bf16[256,512]{1,0:T(8,128)(2,1)S(1)} %copy-done.2), channel_id=1, source_target_pairs={{2,0},{0,2},{3,1},{1,3},{6,4},{4,6},{7,5},{5,7},{10,8},{8,10},{11,... | collective-permute-start | bytes 786440 | tf_op jit(solution)/shard_map/ppermute | solution.py:26
  17.4 1.0 %shard_map.160 = (bf16[12,512,128]{2,1,0:T(8,128)(2,1)S(1)}, bf16[12,512,128]{2,1,0:T(8,128)(2,1)S(1)}, bf16[12,16,512]{2,1,0:T(8,128)(2,1)S(1)}, bf16[12,16,512]{2,1,0:T(8,128)(2,1)S(1)}) custom-call(s32[1]{0:T(128)S(6)} %copy.17.tiles, s32[12,512]{1,0:T(8,128)S(1)} %copy-done.6, s32[1,512]{1,0:T(1,128)S(1)} %bitcast.7), custom_call_target="tpu_custom_call" | custom-call | flops 1024 | bytes 1024 | tf_op jit(solution)/shard_map/pallas_call | solution.py:51
  18.5 2.9 %shard_map.161.before = bf16[12,512,256]{2,1,0:T(8,128)(2,1)S(1)} custom-call(bf16[12,512,128]{2,1,0:T(8,128)(2,1)S(1)} %get-tuple-element.91.low, bf16[12,512,128]{2,1,0:T(8,128)(2,1)S(1)} %get-tuple-element.92.high, bf16[512,256]{1,0:T(8,128)(2,1)S(1)} %get-tuple-element.96.proj, bf16[272,256]{1,0:T(8,128)(2,1)S(1)} %collective-permute-done.3.beside.refs_4_), custom_call_target="tpu_custom_call" | custom-call | flops 1024 | bytes 1024 | tf_op jit(solution)/shard_map/pallas_call | solution.py:51
  22.4 1.6 %collective-permute-done.4.refs_1_ = bf16[256,512]{1,0:T(8,128)(2,1)S(1)} collective-permute-done((bf16[256,512]{1,0:T(8,128)(2,1)S(1)}, bf16[256,512]{1,0:T(8,128)(2,1)S(1)}, u32[]{:S(2)}, u32[]{:S(2)}) %collective-permute-start.4) | collective-permute-done | bytes 262176 | tf_op jit(solution)/shard_map/ppermute | solution.py:26
  24.1 1.1 %shard_map.162 = (bf16[512,512]{1,0:T(8,128)(2,1)}, f32[512,512]{1,0:T(8,128)S(1)}, f32[512,512]{1,0:T(8,128)S(1)}) custom-call(s32[1]{0:T(128)S(6)} %copy.17.tiles, bf16[256,512]{1,0:T(8,128)(2,1)S(1)} %copy-done.2, bf16[256,512]{1,0:T(8,128)(2,1)S(1)} %collective-permute-done.4.refs_1_, bf16[512,512]{1,0:T(8,128)(2,1)S(1)} %get-tuple-element.86.feats.refs_2_, ...), custom_call_target="tpu_custom_call" | custom-call | flops 1024 | bytes 1024 | tf_op jit(solution)/shard_map/pallas_call | solution.py:51
  25.2 2.5 %shard_map.163.part = bf16[12,512,256]{2,1,0:T(8,128)(2,1)S(1)} custom-call(bf16[12,512,128]{2,1,0:T(8,128)(2,1)S(1)} %get-tuple-element.91.low, bf16[12,512,128]{2,1,0:T(8,128)(2,1)S(1)} %get-tuple-element.92.high, bf16[12,512,256]{2,1,0:T(8,128)(2,1)S(1)} %shard_map.161.before, bf16[272,256]{1,0:T(8,128)(2,1)S(1)} %collective-permute-done.1.west.refs_2_, ...), custom_call_target="tpu_custom_call" | custom-call | flops 1024 | bytes 1024 | tf_op jit(solution)/shard_map/pallas_call | solution.py:51
  28.4 2.5 %shard_map.165 = (bf16[256,256]{1,0:T(8,128)(2,1)S(1)}, bf16[12,256,256]{2,1,0:T(8,128)(2,1)S(1)}) custom-call(bf16[12,512,128]{2,1,0:T(8,128)(2,1)S(1)} %get-tuple-element.91.low, bf16[12,512,128]{2,1,0:T(8,128)(2,1)S(1)} %get-tuple-element.92.high, f32[512,256]{1,0:T(8,128)S(1)} %shard_map.159.base, s32[1,512]{1,0:T(1,128)S(1)} %bitcast.8, ...), custom_call_target="tpu_custom_call" | custom-call | flops 1024 | bytes 1024 | tf_op jit(solution)/shard_map/pallas_call | solution.py:51
  30.9 1.6 %collective-permute-start.8 = (bf16[256,256]{1,0:T(8,128)(2,1)S(1)}, bf16[256,256]{1,0:T(8,128)(2,1)S(1)}, u32[]{:S(2)}, u32[]{:S(2)}) collective-permute-start(bf16[256,256]{1,0:T(8,128)(2,1)S(1)} %get-tuple-element.109.refs_0_), channel_id=1, source_target_pairs={{2,0},{0,2},{3,1},{1,3},{6,4},{4,6},{7,5},{5,7},{10,8},{8,10},{11,... | collective-permute-start | bytes 393224 | tf_op jit(solution)/shard_map/ppermute | solution.py:26
  32.5 2.5 %shard_map.168 = (bf16[256,256]{1,0:T(8,128)(2,1)S(1)}, bf16[12,256,256]{2,1,0:T(8,128)(2,1)S(1)}) custom-call(bf16[12,512,128]{2,1,0:T(8,128)(2,1)S(1)} %get-tuple-element.91.low, bf16[12,512,128]{2,1,0:T(8,128)(2,1)S(1)} %get-tuple-element.92.high, f32[512,256]{1,0:T(8,128)S(1)} %shard_map.159.base, s32[1,512]{1,0:T(1,128)S(1)} %bitcast.9, ...), custom_call_target="tpu_custom_call" | custom-call | flops 1024 | bytes 1024 | tf_op jit(solution)/shard_map/pallas_call | solution.py:51
  35.5 1.0 %collective-permute-done.8.refs_1_ = bf16[256,256]{1,0:T(8,128)(2,1)S(1)} collective-permute-done((bf16[256,256]{1,0:T(8,128)(2,1)S(1)}, bf16[256,256]{1,0:T(8,128)(2,1)S(1)}, u32[]{:S(2)}, u32[]{:S(2)}) %collective-permute-start.8) | collective-permute-done | bytes 131104 | tf_op jit(solution)/shard_map/ppermute | solution.py:26
  36.5 0.9 %shard_map.166 = (bf16[512,256]{1,0:T(8,128)(2,1)S(1)}, bf16[512,256]{1,0:T(8,128)(2,1)S(1)}, f32[256,256]{1,0:T(8,128)S(1)}) custom-call(s32[1,512]{1,0:T(1,128)S(1)} %bitcast.10, bf16[256,256]{1,0:T(8,128)(2,1)S(1)} %get-tuple-element.109.refs_0_, bf16[256,256]{1,0:T(8,128)(2,1)S(1)} %collective-permute-done.8.refs_1_, bf16[512,512]{1,0:T(8,128)(2,1)S(1)} %copy-done.1, ...), custom_call_target="tpu_custom_call" | custom-call | flops 1024 | bytes 1024 | tf_op jit(solution)/shard_map/pallas_call | solution.py:51
  37.4 1.4 %shard_map.167 = (bf16[12,256,256]{2,1,0:T(8,128)(2,1)S(1)}, f32[768,256]{1,0:T(8,128)S(1)}) custom-call(bf16[12,16,512]{2,1,0:T(8,128)(2,1)S(1)} %get-tuple-element.89.low, bf16[12,16,512]{2,1,0:T(8,128)(2,1)S(1)} %get-tuple-element.90.high, bf16[12,256,256]{2,1,0:T(8,128)(2,1)S(1)} %get-tuple-element.108.slope, f32[256,256]{1,0:T(8,128)S(1)} %get-tuple-element.114.scale), custom_call_target="tpu_custom_call" | custom-call | flops 1024 | bytes 1024 | tf_op jit(solution)/shard_map/pallas_call | solution.py:51
  38.9 1.4 %collective-permute-done.9.refs_1_ = bf16[256,256]{1,0:T(8,128)(2,1)S(1)} collective-permute-done((bf16[256,256]{1,0:T(8,128)(2,1)S(1)}, bf16[256,256]{1,0:T(8,128)(2,1)S(1)}, u32[]{:S(2)}, u32[]{:S(2)}) %collective-permute-start.9) | collective-permute-done | bytes 131104 | tf_op jit(solution)/shard_map/ppermute | solution.py:26
  40.3 0.8 %shard_map.169 = (bf16[512,256]{1,0:T(8,128)(2,1)S(1)}, bf16[512,256]{1,0:T(8,128)(2,1)S(1)}, f32[256,256]{1,0:T(8,128)S(1)}) custom-call(s32[1,512]{1,0:T(1,128)S(1)} %bitcast.11, bf16[256,256]{1,0:T(8,128)(2,1)S(1)} %get-tuple-element.117.refs_0_, bf16[256,256]{1,0:T(8,128)(2,1)S(1)} %collective-permute-done.9.refs_1_, bf16[512,512]{1,0:T(8,128)(2,1)S(1)} %copy-done.1, ...), custom_call_target="tpu_custom_call" | custom-call | flops 1024 | bytes 1024 | tf_op jit(solution)/shard_map/pallas_call | solution.py:51
  41.9 1.0 %shard_map.171 = bf16[2,256,256]{2,1,0:T(8,128)(2,1)S(1)} custom-call(bf16[12,16,512]{2,1,0:T(8,128)(2,1)S(1)} %get-tuple-element.89.low, bf16[12,16,512]{2,1,0:T(8,128)(2,1)S(1)} %get-tuple-element.90.high, bf16[12,256,256]{2,1,0:T(8,128)(2,1)S(1)} %get-tuple-element.120.grads.refs_1_, f32[768,256]{1,0:T(8,128)S(1)} %get-tuple-element.119.before, ...), custom_call_target="tpu_custom_call" | custom-call | flops 1024 | bytes 1024 | tf_op jit(solution)/shard_map/pallas_call | solution.py:51
  43.0 2.6 %shard_map.172 = (bf16[256,256]{1,0:T(8,128)(2,1)S(1)}, bf16[256,256]{1,0:T(8,128)(2,1)S(1)}, bf16[256,256]{1,0:T(8,128)(2,1)S(1)}) custom-call(bf16[12,16,512]{2,1,0:T(8,128)(2,1)S(1)} %get-tuple-element.89.low, bf16[12,16,512]{2,1,0:T(8,128)(2,1)S(1)} %get-tuple-element.90.high, bf16[12,256,256]{2,1,0:T(8,128)(2,1)S(1)} %get-tuple-element.129.refs_0_, ...), custom_call_target="tpu_custom_call" | custom-call | flops 1024 | bytes 1024 | tf_op jit(solution)/shard_map/pallas_call | solution.py:51
  46.2 1.9 %collective-permute-done.10.across = bf16[256,256]{1,0:T(8,128)(2,1)S(1)} collective-permute-done((bf16[256,256]{1,0:T(8,128)(2,1)S(1)}, bf16[256,256]{1,0:T(8,128)(2,1)S(1)}, u32[]{:S(2)}, u32[]{:S(2)}) %collective-permute-start.10) | collective-permute-done | bytes 131104 | tf_op jit(solution)/shard_map/ppermute | solution.py:566
  48.2 1.5 %collective-permute-start.13 = (bf16[256,256]{1,0:T(8,128)(2,1)S(1)}, bf16[256,256]{1,0:T(8,128)(2,1)S(1)}, u32[]{:S(2)}, u32[]{:S(2)}) collective-permute-start(bf16[256,256]{1,0:T(8,128)(2,1)S(1)} %get-tuple-element.128), channel_id=1, source_target_pairs={{4,0},{8,4},{12,8},{0,12},{5,1},{9,5},{13,9},{1,13},{6,2},{10,6},{... | collective-permute-start | bytes 393224 | tf_op jit(solution)/shard_map/ppermute | solution.py:26
  50.3 2.1 %shard_map.175 = (f32[512,256]{1,0:T(8,128)S(1)}, bf16[256,512]{1,0:T(8,128)(2,1)S(1)}) custom-call(bf16[12,16,512]{2,1,0:T(8,128)(2,1)S(1)} %get-tuple-element.89.low, bf16[12,16,512]{2,1,0:T(8,128)(2,1)S(1)} %get-tuple-element.90.high, bf16[12,256,256]{2,1,0:T(8,128)(2,1)S(1)} %get-tuple-element.129.refs_0_, ...), custom_call_target="tpu_custom_call" | custom-call | flops 1024 | bytes 1024 | tf_op jit(solution)/shard_map/pallas_call | solution.py:51
  52.3 1.2 %shard_map.176 = (bf16[256,512]{1,0:T(8,128)(2,1)}, f32[256,512]{1,0:T(8,128)S(1)}) custom-call(s32[1]{0:T(128)S(6)} %copy.17.tiles, bf16[256,512]{1,0:T(8,128)(2,1)S(1)} %get-tuple-element.82.refs_0_.feats, bf16[256,512]{1,0:T(8,128)(2,1)S(1)} %copy-done.2, bf16[256,512]{1,0:T(8,128)(2,1)S(1)} %get-tuple-element.83.w_out, bf16[256,512]{1,0:T(8,128)(2,1)S(1)} %copy-done.4, ...), custom_call_target="tpu_custom_call" | custom-call | flops 1024 | bytes 1024 | tf_op jit(solution)/shard_map/pallas_call | solution.py:51
  55.0 2.1 %collective-permute-done.14.refs_0_ = bf16[256,256]{1,0:T(8,128)(2,1)S(1)} collective-permute-done((bf16[256,256]{1,0:T(8,128)(2,1)S(1)}, bf16[256,256]{1,0:T(8,128)(2,1)S(1)}, u32[]{:S(2)}, u32[]{:S(2)}) %collective-permute-start.14) | collective-permute-done | bytes 131104 | tf_op jit(solution)/shard_map/ppermute | solution.py:26
  58.7 0.7 %collective-permute-done.17.refs_1_ = bf16[256,256]{1,0:T(8,128)(2,1)S(1)} collective-permute-done((bf16[256,256]{1,0:T(8,128)(2,1)S(1)}, bf16[256,256]{1,0:T(8,128)(2,1)S(1)}, u32[]{:S(2)}, u32[]{:S(2)}) %collective-permute-start.17) | collective-permute-done | bytes 131104 | tf_op jit(solution)/shard_map/ppermute | solution.py:26
  59.5 0.9 %collective-permute-start.18 = (bf16[2,64,256]{2,1,0:T(8,128)(2,1)S(1)}, bf16[2,64,256]{2,1,0:T(8,128)(2,1)S(1)}, u32[]{:S(2)}, u32[]{:S(2)}) collective-permute-start(bf16[2,64,256]{2,1,0:T(8,128)(2,1)S(1)} %get-tuple-element.158), channel_id=1, source_target_pairs={{0,4},{4,0},{8,12},{12,8},{1,5},{5,1},{9,13},{13,9},{2,6},{6,2},{1... | collective-permute-start | bytes 196616 | tf_op jit(solution)/shard_map/ppermute | solution.py:819
  60.3 3.5 %collective-permute-done.18.received = bf16[2,64,256]{2,1,0:T(8,128)(2,1)S(1)} collective-permute-done((bf16[2,64,256]{2,1,0:T(8,128)(2,1)S(1)}, bf16[2,64,256]{2,1,0:T(8,128)(2,1)S(1)}, u32[]{:S(2)}, u32[]{:S(2)}) %collective-permute-start.18) | collective-permute-done | bytes 65568 | tf_op jit(solution)/shard_map/ppermute | solution.py:819
  63.8 3.1 %collective-permute-start.19 = (bf16[1,64,256]{2,1,0:T(8,128)(2,1)S(1)}, bf16[1,64,256]{2,1,0:T(8,128)(2,1)S(1)}, u32[]{:S(2)}, u32[]{:S(2)}) collective-permute-start(bf16[1,64,256]{2,1,0:T(8,128)(2,1)S(1)} %get-tuple-element.160), channel_id=1, source_target_pairs={{0,8},{4,12},{8,0},{12,4},{1,9},{5,13},{9,1},{13,5},{2,10},{6,14},... | collective-permute-start | bytes 98312 | tf_op jit(solution)/shard_map/ppermute | solution.py:819
  67.7 1.2 %collective-permute-done.19.received = bf16[1,64,256]{2,1,0:T(8,128)(2,1)S(1)} collective-permute-done((bf16[1,64,256]{2,1,0:T(8,128)(2,1)S(1)}, bf16[1,64,256]{2,1,0:T(8,128)(2,1)S(1)}, u32[]{:S(2)}, u32[]{:S(2)}) %collective-permute-start.19) | collective-permute-done | bytes 32800 | tf_op jit(solution)/shard_map/ppermute | solution.py:819
  (57 shorter events, 9.6 us)
Async XLA Ops:
  0.6 9.5 %copy-start.9 = (s32[1,6,2]{1,2,0:T(2,128)S(1)}, s32[1,6,2]{1,2,0:T(2,128)}, u32[]{:S(2)}) copy-start(s32[1,6,2]{1,2,0:T(2,128)} %param.19) | copy-start | bytes 148
  0.6 14.7 %copy-start.7 = (f32[512]{0:T(512)S(1)}, f32[512]{0:T(512)}, u32[]{:S(2)}) copy-start(f32[512]{0:T(512)} %param.22) | copy-start | bytes 6148
  0.7 9.5 %collective-permute-start = (bf16[256,512]{1,0:T(8,128)(2,1)}, bf16[256,512]{1,0:T(8,128)(2,1)S(1)}, u32[]{:S(2)}, u32[]{:S(2)}) collective-permute-start(bf16[256,512]{1,0:T(8,128)(2,1)} %refs_2_.1), channel_id=1, source_target_pairs={{2,0},{0,2},{3,1},{1,3},{6,4},{4,6},{7,5},{5,7},{10,8},{8,10},{11,... | collective-permute-start | bytes 786440 | tf_op jit(solution)/shard_map/ppermute | solution.py:26
  6.9 8.8 %copy-start.2 = (bf16[256,512]{1,0:T(8,128)(2,1)S(1)}, bf16[256,512]{1,0:T(8,128)(2,1)}, u32[]{:S(2)}) copy-start(bf16[256,512]{1,0:T(8,128)(2,1)} %cots.1) | copy-start | bytes 786436
  6.9 10.5 %copy-start.5 = (s32[512]{0:T(512)S(1)}, s32[512]{0:T(512)}, u32[]{:S(2)}) copy-start(s32[512]{0:T(512)} %param.17) | copy-start | bytes 6148
  7.0 10.5 %copy-start.6 = (s32[12,512]{1,0:T(8,128)S(1)}, s32[12,512]{1,0:T(8,128)}, u32[]{:S(2)}) copy-start(s32[12,512]{1,0:T(8,128)} %senders) | copy-start | bytes 73732
  11.3 7.2 %collective-permute-start.3 = (bf16[272,256]{1,0:T(8,128)(2,1)S(1)}, bf16[272,256]{1,0:T(8,128)(2,1)S(1)}, u32[]{:S(2)}, u32[]{:S(2)}) collective-permute-start(bf16[272,256]{1,0:T(8,128)(2,1)S(1)} %get-tuple-element.97), channel_id=1, source_target_pairs={{1,0},{0,1},{3,2},{2,3},{5,4},{4,5},{7,6},{6,7},{9,8},{8,9},{11,10... | collective-permute-start | bytes 417800 | tf_op jit(solution)/shard_map/ppermute | solution.py:26
  11.3 10.1 %collective-permute-start.1 = (bf16[272,256]{1,0:T(8,128)(2,1)S(1)}, bf16[272,256]{1,0:T(8,128)(2,1)S(1)}, u32[]{:S(2)}, u32[]{:S(2)}) collective-permute-start(bf16[272,256]{1,0:T(8,128)(2,1)S(1)} %get-tuple-element.94), channel_id=1, source_target_pairs={{12,0},{0,4},{4,8},{8,12},{13,1},{1,5},{5,9},{9,13},{14,2},{2,6},{... | collective-permute-start | bytes 417800 | tf_op jit(solution)/shard_map/ppermute | solution.py:26
  13.2 8.7 %collective-permute-start.2 = (bf16[272,256]{1,0:T(8,128)(2,1)S(1)}, bf16[272,256]{1,0:T(8,128)(2,1)S(1)}, u32[]{:S(2)}, u32[]{:S(2)}) collective-permute-start(bf16[272,256]{1,0:T(8,128)(2,1)S(1)} %get-tuple-element.95), channel_id=1, source_target_pairs={{4,0},{8,4},{12,8},{0,12},{5,1},{9,5},{13,9},{1,13},{6,2},{10,6},{... | collective-permute-start | bytes 417800 | tf_op jit(solution)/shard_map/ppermute | solution.py:26
  15.7 8.4 %collective-permute-start.4 = (bf16[256,512]{1,0:T(8,128)(2,1)S(1)}, bf16[256,512]{1,0:T(8,128)(2,1)S(1)}, u32[]{:S(2)}, u32[]{:S(2)}) collective-permute-start(bf16[256,512]{1,0:T(8,128)(2,1)S(1)} %copy-done.2), channel_id=1, source_target_pairs={{2,0},{0,2},{3,1},{1,3},{6,4},{4,6},{7,5},{5,7},{10,8},{8,10},{11,... | collective-permute-start | bytes 786440 | tf_op jit(solution)/shard_map/ppermute | solution.py:26
  17.4 11.0 %collective-permute-start.5 = (bf16[272,256]{1,0:T(8,128)(2,1)S(1)}, bf16[272,256]{1,0:T(8,128)(2,1)S(1)}, u32[]{:S(2)}, u32[]{:S(2)}) collective-permute-start(bf16[272,256]{1,0:T(8,128)(2,1)S(1)} %get-tuple-element.105), channel_id=1, source_target_pairs={{0,9},{1,8},{4,13},{5,12},{8,1},{9,0},{12,5},{13,4},{2,11},{3,10},... | collective-permute-start | bytes 417800 | tf_op jit(solution)/shard_map/ppermute | solution.py:622
  18.5 5.6 %copy-start = (bf16[512,512]{1,0:T(8,128)(2,1)S(1)}, bf16[512,512]{1,0:T(8,128)(2,1)}, u32[]{:S(2)}) copy-start(bf16[512,512]{1,0:T(8,128)(2,1)} %refs_3_.3) | copy-start | bytes 1572868
  18.5 5.6 %copy-start.3 = (bf16[512,512]{1,0:T(8,128)(2,1)S(1)}, bf16[512,512]{1,0:T(8,128)(2,1)}, u32[]{:S(2)}) copy-start(bf16[512,512]{1,0:T(8,128)(2,1)} %get-tuple-element.100.refs_5_) | copy-start | bytes 1572868
  18.5 5.6 %copy-start.8 = (f32[512]{0:T(512)S(1)}, f32[512]{0:T(512)}, u32[]{:S(2)}) copy-start(f32[512]{0:T(512)} %param.26) | copy-start | bytes 6148
  21.9 6.5 %collective-permute-start.6 = (bf16[272,256]{1,0:T(8,128)(2,1)S(1)}, bf16[272,256]{1,0:T(8,128)(2,1)S(1)}, u32[]{:S(2)}, u32[]{:S(2)}) collective-permute-start(bf16[272,256]{1,0:T(8,128)(2,1)S(1)} %collective-permute-done.1.west.refs_2_), channel_id=1, source_target_pairs={{1,0},{0,1},{3,2},{2,3},{5,4},{4,5},{7,6},{6,7},{9,8},{8,9},{11,10... | collective-permute-start | bytes 417800 | tf_op jit(solution)/shard_map/ppermute | solution.py:26
  22.4 6.1 %collective-permute-start.7 = (bf16[272,256]{1,0:T(8,128)(2,1)S(1)}, bf16[272,256]{1,0:T(8,128)(2,1)S(1)}, u32[]{:S(2)}, u32[]{:S(2)}) collective-permute-start(bf16[272,256]{1,0:T(8,128)(2,1)S(1)} %collective-permute-done.2.east.refs_3_), channel_id=1, source_target_pairs={{1,0},{0,1},{3,2},{2,3},{5,4},{4,5},{7,6},{6,7},{9,8},{8,9},{11,10... | collective-permute-start | bytes 417800 | tf_op jit(solution)/shard_map/ppermute | solution.py:26
  30.9 5.6 %copy-start.1 = (bf16[512,512]{1,0:T(8,128)(2,1)S(1)}, bf16[512,512]{1,0:T(8,128)(2,1)}, u32[]{:S(2)}) copy-start(bf16[512,512]{1,0:T(8,128)(2,1)} %get-tuple-element.110.refs_2_) | copy-start | bytes 1572868
  30.9 5.6 %collective-permute-start.8 = (bf16[256,256]{1,0:T(8,128)(2,1)S(1)}, bf16[256,256]{1,0:T(8,128)(2,1)S(1)}, u32[]{:S(2)}, u32[]{:S(2)}) collective-permute-start(bf16[256,256]{1,0:T(8,128)(2,1)S(1)} %get-tuple-element.109.refs_0_), channel_id=1, source_target_pairs={{2,0},{0,2},{3,1},{1,3},{6,4},{4,6},{7,5},{5,7},{10,8},{8,10},{11,... | collective-permute-start | bytes 393224 | tf_op jit(solution)/shard_map/ppermute | solution.py:26
  34.9 5.3 %collective-permute-start.9 = (bf16[256,256]{1,0:T(8,128)(2,1)S(1)}, bf16[256,256]{1,0:T(8,128)(2,1)S(1)}, u32[]{:S(2)}, u32[]{:S(2)}) collective-permute-start(bf16[256,256]{1,0:T(8,128)(2,1)S(1)} %get-tuple-element.117.refs_0_), channel_id=1, source_target_pairs={{2,0},{0,2},{3,1},{1,3},{6,4},{4,6},{7,5},{5,7},{10,8},{8,10},{11,... | collective-permute-start | bytes 393224 | tf_op jit(solution)/shard_map/ppermute | solution.py:26
  41.7 6.3 %collective-permute-start.10 = (bf16[256,256]{1,0:T(8,128)(2,1)S(1)}, bf16[256,256]{1,0:T(8,128)(2,1)S(1)}, u32[]{:S(2)}, u32[]{:S(2)}) collective-permute-start(bf16[256,256]{1,0:T(8,128)(2,1)S(1)} %get-tuple-element.124), channel_id=1, source_target_pairs={{0,13},{1,4},{4,1},{5,8},{8,5},{9,12},{12,9},{13,0},{2,15},{3,6},{... | collective-permute-start | bytes 393224 | tf_op jit(solution)/shard_map/ppermute | solution.py:566
  42.9 5.2 %collective-permute-start.11 = (bf16[2,256,256]{2,1,0:T(8,128)(2,1)S(1)}, bf16[2,256,256]{2,1,0:T(8,128)(2,1)S(1)}, u32[]{:S(2)}, u32[]{:S(2)}) collective-permute-start(bf16[2,256,256]{2,1,0:T(8,128)(2,1)S(1)} %shard_map.171), channel_id=1, source_target_pairs={{1,0},{0,1},{3,2},{2,3},{5,4},{4,5},{7,6},{6,7},{9,8},{8,9},{11,10... | collective-permute-start | bytes 786440 | tf_op jit(solution)/shard_map/ppermute | solution.py:26
  45.6 7.9 %collective-permute-start.12 = (bf16[256,256]{1,0:T(8,128)(2,1)S(1)}, bf16[256,256]{1,0:T(8,128)(2,1)S(1)}, u32[]{:S(2)}, u32[]{:S(2)}) collective-permute-start(bf16[256,256]{1,0:T(8,128)(2,1)S(1)} %get-tuple-element.138), channel_id=1, source_target_pairs={{1,0},{0,1},{3,2},{2,3},{5,4},{4,5},{7,6},{6,7},{9,8},{8,9},{11,10... | collective-permute-start | bytes 393224 | tf_op jit(solution)/shard_map/ppermute | solution.py:26
  48.2 5.4 %collective-permute-start.13 = (bf16[256,256]{1,0:T(8,128)(2,1)S(1)}, bf16[256,256]{1,0:T(8,128)(2,1)S(1)}, u32[]{:S(2)}, u32[]{:S(2)}) collective-permute-start(bf16[256,256]{1,0:T(8,128)(2,1)S(1)} %get-tuple-element.128), channel_id=1, source_target_pairs={{4,0},{8,4},{12,8},{0,12},{5,1},{9,5},{13,9},{1,13},{6,2},{10,6},{... | collective-permute-start | bytes 393224 | tf_op jit(solution)/shard_map/ppermute | solution.py:26
  49.7 2.6 %copy-start.4 = (bf16[256,512]{1,0:T(8,128)(2,1)S(1)}, bf16[256,512]{1,0:T(8,128)(2,1)}, u32[]{:S(2)}) copy-start(bf16[256,512]{1,0:T(8,128)(2,1)} %get-tuple-element.84.w_node_v_t) | copy-start | bytes 786436
  49.7 7.4 %collective-permute-start.14 = (bf16[256,256]{1,0:T(8,128)(2,1)S(1)}, bf16[256,256]{1,0:T(8,128)(2,1)S(1)}, u32[]{:S(2)}, u32[]{:S(2)}) collective-permute-start(bf16[256,256]{1,0:T(8,128)(2,1)S(1)} %get-tuple-element.139), channel_id=1, source_target_pairs={{12,0},{0,4},{4,8},{8,12},{13,1},{1,5},{5,9},{9,13},{14,2},{2,6},{... | collective-permute-start | bytes 393224 | tf_op jit(solution)/shard_map/ppermute | solution.py:26
  54.3 5.1 %collective-permute-start.17 = (bf16[256,256]{1,0:T(8,128)(2,1)S(1)}, bf16[256,256]{1,0:T(8,128)(2,1)S(1)}, u32[]{:S(2)}, u32[]{:S(2)}) collective-permute-start(bf16[256,256]{1,0:T(8,128)(2,1)S(1)} %bitcast.16), channel_id=1, source_target_pairs={{2,0},{0,2},{3,1},{1,3},{6,4},{4,6},{7,5},{5,7},{10,8},{8,10},{11,... | collective-permute-start | bytes 393224 | tf_op jit(solution)/shard_map/ppermute | solution.py:26
  57.5 1.9 %collective-permute-start.16 = (bf16[4,64,256]{2,1,0:T(8,128)(2,1)S(1)}, bf16[4,64,256]{2,1,0:T(8,128)(2,1)S(1)}, u32[]{:S(2)}, u32[]{:S(2)}) collective-permute-start(bf16[4,64,256]{2,1,0:T(8,128)(2,1)S(1)} %get-tuple-element.151), channel_id=1, source_target_pairs={{1,0},{0,1},{3,2},{2,3},{5,4},{4,5},{7,6},{6,7},{9,8},{8,9},{11,10... | collective-permute-start | bytes 393224 | tf_op jit(solution)/shard_map/ppermute | solution.py:26
  58.0 8.9 %collective-permute-start.15 = (bf16[256,256]{1,0:T(8,128)(2,1)S(1)}, bf16[256,256]{1,0:T(8,128)(2,1)S(1)}, u32[]{:S(2)}, u32[]{:S(2)}) collective-permute-start(bf16[256,256]{1,0:T(8,128)(2,1)S(1)} %bitcast.15), channel_id=1, source_target_pairs={{2,0},{0,2},{3,1},{1,3},{6,4},{4,6},{7,5},{5,7},{10,8},{8,10},{11,... | collective-permute-start | bytes 393224 | tf_op jit(solution)/shard_map/ppermute | solution.py:26
  59.5 4.3 %collective-permute-start.18 = (bf16[2,64,256]{2,1,0:T(8,128)(2,1)S(1)}, bf16[2,64,256]{2,1,0:T(8,128)(2,1)S(1)}, u32[]{:S(2)}, u32[]{:S(2)}) collective-permute-start(bf16[2,64,256]{2,1,0:T(8,128)(2,1)S(1)} %get-tuple-element.158), channel_id=1, source_target_pairs={{0,4},{4,0},{8,12},{12,8},{1,5},{5,1},{9,13},{13,9},{2,6},{6,2},{1... | collective-permute-start | bytes 196616 | tf_op jit(solution)/shard_map/ppermute | solution.py:819
  63.8 5.0 %collective-permute-start.19 = (bf16[1,64,256]{2,1,0:T(8,128)(2,1)S(1)}, bf16[1,64,256]{2,1,0:T(8,128)(2,1)S(1)}, u32[]{:S(2)}, u32[]{:S(2)}) collective-permute-start(bf16[1,64,256]{2,1,0:T(8,128)(2,1)S(1)} %get-tuple-element.160), channel_id=1, source_target_pairs={{0,8},{4,12},{8,0},{12,4},{1,9},{5,13},{9,1},{13,5},{2,10},{6,14},... | collective-permute-start | bytes 98312 | tf_op jit(solution)/shard_map/ppermute | solution.py:819
